TPU v7x, 32 devices: a whole 2x2x4 slice. The times are simulated.
32 devices in a mesh: grp: 2 (over y), blk: 4 (over z), term: 2 (over x), sub: 2 (over core).
Axes of the slice: x: 2, y: 2, z: 4, core: 2. Of those that a mesh axis runs over, the one named last changes fastest.
Arguments:
- amplitudes: float32 [128, 128, 3, 128], P(('grp', 'blk'), 'sub'), parts along dimension 0, may hold values from -6 to 6
- left_operators: float32 [32, 64, 128, 128], P(('grp', 'term'), 'blk', 'sub'), parts along dimension 0, may hold values from -0.125 to 0.125
- right_operators: float32 [32, 64, 128, 128], P(('grp', 'term'), 'blk'), parts along dimension 0, may hold values from -0.5 to 0.5
- term_kind: int32 [32], P(('grp', 'term')), parts along dimension 0, may hold values 0 or 1
- partner: int32 [128], P(('grp', 'blk')), parts along dimension 0, may hold values from 0 to 63, as said below
- left_diag: float32 [128, 128], P(('grp', 'blk'), 'sub'), parts along dimension 0, may hold values from 0.5 to 8
- right_diag: float32 [128, 128], P(('grp', 'blk')), parts along dimension 0, may hold values from 0.5 to 8
Outputs:
- sigma_second: float32 [128, 128, 3, 128], P(('grp', 'blk'), 'sub'), parts along dimension 0
- correction: float32 [128, 128, 3, 128], P(('grp', 'blk'), 'sub'), parts along dimension 0
There are 2 independent parts, one for each index of `grp`. A program takes and returns all parts, laid end to end along the dimension named above; each array names one. Nothing has to cross between parts.
Inputs may be any that keep to these rules, and one draw needn't show every extreme that they name: partner is a permutation of the sectors. Sector 16 p + j goes to sector 16 ((p + c_j) mod 4) + pi_j, where c and pi (a permutation of 0 to 15) are the same for every p, and each value of c_j mod 4 occurs exactly 16 / 4 times.
All inputs are finite; a program needn't handle non-finite values. No bound on the sum of `term_kind` on one device may be relied on, other than what follows from the above.
Results may differ from a plain program's by a relative error of at most 0.0003.
Values sent between devices are 32-bit elements; how exact they have to be, the bound alone decides.
No kernel may reach another device: no remote copies, remote signals or barrier semaphores. Data moves between devices by JAX's collectives and lax.ppermute only.
A program may use at most 64 MiB of HBM per device.

v0:
```python
import jax
import jax.numpy as jnp
from jax import lax
from jax.sharding import PartitionSpec as P


def route_tables(partner, device, devices):
    count = partner.shape[0]
    per_peer = count // devices
    slots = jnp.arange(count, dtype=jnp.int32)
    offset = (partner // count - device) % devices
    target = partner % count
    before = (offset[None, :] == offset[:, None]) & (slots[None, :] < slots[:, None])
    order = jnp.sum(before.astype(jnp.int32), axis=1)
    offsets = jnp.arange(devices, dtype=jnp.int32)
    places = jnp.arange(per_peer, dtype=jnp.int32)
    match = (offset[None, None, :] == offsets[:, None, None]) & (
        order[None, None, :] == places[None, :, None]
    )
    table = jnp.sum(jnp.where(match, slots[None, None, :], 0), axis=2)
    send_index = table[(offsets - device) % devices].reshape(-1)
    source = jnp.sum(jnp.where(target[None, :] == slots[:, None], slots[None, :], 0), axis=1)
    receive_index = (device - offset[source]) % devices * per_peer + order[source]
    return (send_index, receive_index)


def correct(sigma, vector, diag_sum, correlation, weight):
    theta = (correlation / weight)[None, None, :, None]
    return (sigma - theta * vector) / jnp.maximum(jnp.abs(diag_sum - theta), 1.0)


def shards(amplitudes, left_operators, right_operators, term_kind, partner, left_diag, right_diag):
    devices = lax.axis_size("blk")
    send_index, receive_index = route_tables(partner, lax.axis_index("blk"), devices)
    diag_sum = left_diag[:, :, None, None] + right_diag[:, None, None, :]
    count = (
        amplitudes.shape[0]
        * devices
        * amplitudes.shape[1]
        * lax.axis_size("sub")
        * amplitudes.shape[3]
    )

    def partials(vector_half):
        full = lax.all_gather(vector_half, "sub", axis=1, tiled=True)

        def one_term(carry, inputs):
            left_block, right_block, kind = inputs
            middle = jnp.einsum("soi,sirc->sorc", left_block, full, precision=lax.Precision.HIGHEST)
            result = jnp.einsum(
                "sorc,sdc->sord", middle, right_block, precision=lax.Precision.HIGHEST
            )
            moving = (kind == 1).astype(jnp.float32)
            return ((carry[0] + (1.0 - moving) * result, carry[1] + moving * result), None)

        start = jnp.zeros(vector_half.shape, jnp.float32)
        (kept, moved), _ = lax.scan(
            one_term, (start, start), (left_operators, right_operators, term_kind)
        )
        return (kept, moved)

    def relay(moved):
        outgoing = jnp.take(moved, send_index, axis=0).reshape((devices, -1) + moved.shape[1:])
        incoming = lax.all_to_all(outgoing, "blk", split_axis=0, concat_axis=0, tiled=True)
        return jnp.take(incoming.reshape(moved.shape), receive_index, axis=0)

    def sigma_whole(vector_half):
        kept, moved = partials(vector_half)
        total = lax.psum(kept + relay(moved), "term")
        return total + diag_sum * vector_half

    sigma_first = sigma_whole(amplitudes)
    correlation, weight = lax.psum(
        (
            jnp.sum(amplitudes * sigma_first, axis=(0, 1, 3)),
            jnp.sum(amplitudes * amplitudes, axis=(0, 1, 3)),
        ),
        ("blk", "sub"),
    )
    raw = correct(sigma_first, amplitudes, diag_sum, correlation, weight)
    squares = lax.psum(jnp.sum(raw * raw, axis=(0, 1, 3)), ("blk", "sub"))
    correction = raw * lax.rsqrt(squares / count + 1e-06)[None, None, :, None]
    sigma_second = sigma_whole(correction)
    return (sigma_second, correction)


def solution(mesh):
    return jax.shard_map(
        shards,
        mesh=mesh,
        in_specs=(
            P(("grp", "blk"), "sub", None, None),
            P(("grp", "term"), "blk", "sub", None),
            P(("grp", "term"), "blk", None, None),
            P(("grp", "term")),
            P(("grp", "blk")),
            P(("grp", "blk"), "sub"),
            P(("grp", "blk"), None),
        ),
        out_specs=(P(("grp", "blk"), "sub", None, None), P(("grp", "blk"), "sub", None, None)),
        check_vma=False,
    )
```

profile of v0, /device:TPU:0, one launch (start us, length us, event | category | flops | bytes accessed | tf_op | source)
XLA Modules:
  0.0 451.5 jit_solution(211118016285526785)
XLA Ops:
  9.0 15.4 %all-gather.3.cloned.1.call-done = f32[16,128,3,128]{3,1,2,0:T(8,128)} async-done(((f32[16,64,3,128]{3,1,2,0:T(8,128)}), f32[16,128,3,128]{3,1,2,0:T(8,128)}) %all-gather.3.cloned.1.call-update) | async-done | bytes 3145744 | tf_op jit(solution)/shard_map/all_gather | solution.py:45
  24.4 88.2 %while.26 = (s32[]{:T(128)}, f32[16,64,3,128]{3,1,2,0:T(8,128)}, f32[16,64,3,128]{3,1,2,0:T(8,128)S(1)}, s32[8]{0:T(128)S(1)}, f32[8,16,64,128]{3,2,1,0:T(8,128)...) while((s32[]{:T(128)}, f32[16,64,3,128]{3,1,2,0:T(8,128)}, ...), condition=%wide.region_1.2_spmd.clone, body=%wide.region_0.1_spmd.clone.sunk | while | flops 1210318848 | bytes 14157473 | solution.py:57
  25.7 4.3 fusion.39
  30.0 5.0 %select_add_fusion.8 = (f32[16,64,3,128]{3,1,2,0:T(8,128)S(1)}, f32[16,64,3,128]{3,1,2,0:T(8,128)}) fusion(f32[16,64,3,128]{3,1,2,0:T(8,128)S(1)} %get-tuple-element.296, f32[]{:T(128)} %bitcast.58, pred[]{:T(512)S(6)} %compare.18, f32[]{:T(128)S(6)} %sub.74, f32[16,64,3,128]{3,1,2,0:T(8,128)} %get-tuple-element.295, ...), kind=kOutput, calls=%fused_computation.7.clone.1 | convolution fusion | flops 606339072 | bytes 8913925 | tf_op jit(solution)/shard_map/while/body/eval_jaxpr/sorc,sdc->sord/dot_general | solution.py:50
  36.3 4.3 fusion.39
  40.6 5.5 %select_add_fusion.8 = (f32[16,64,3,128]{3,1,2,0:T(8,128)S(1)}, f32[16,64,3,128]{3,1,2,0:T(8,128)}) fusion(f32[16,64,3,128]{3,1,2,0:T(8,128)S(1)} %get-tuple-element.296, f32[]{:T(128)} %bitcast.58, pred[]{:T(512)S(6)} %compare.18, f32[]{:T(128)S(6)} %sub.74, f32[16,64,3,128]{3,1,2,0:T(8,128)} %get-tuple-element.295, ...), kind=kOutput, calls=%fused_computation.7.clone.1 | convolution fusion | flops 606339072 | bytes 8913925 | tf_op jit(solution)/shard_map/while/body/eval_jaxpr/sorc,sdc->sord/dot_general | solution.py:50
  47.4 4.3 fusion.39
  51.7 5.5 %select_add_fusion.8 = (f32[16,64,3,128]{3,1,2,0:T(8,128)S(1)}, f32[16,64,3,128]{3,1,2,0:T(8,128)}) fusion(f32[16,64,3,128]{3,1,2,0:T(8,128)S(1)} %get-tuple-element.296, f32[]{:T(128)} %bitcast.58, pred[]{:T(512)S(6)} %compare.18, f32[]{:T(128)S(6)} %sub.74, f32[16,64,3,128]{3,1,2,0:T(8,128)} %get-tuple-element.295, ...), kind=kOutput, calls=%fused_computation.7.clone.1 | convolution fusion | flops 606339072 | bytes 8913925 | tf_op jit(solution)/shard_map/while/body/eval_jaxpr/sorc,sdc->sord/dot_general | solution.py:50
  58.5 4.3 fusion.39
  62.8 5.5 %select_add_fusion.8 = (f32[16,64,3,128]{3,1,2,0:T(8,128)S(1)}, f32[16,64,3,128]{3,1,2,0:T(8,128)}) fusion(f32[16,64,3,128]{3,1,2,0:T(8,128)S(1)} %get-tuple-element.296, f32[]{:T(128)} %bitcast.58, pred[]{:T(512)S(6)} %compare.18, f32[]{:T(128)S(6)} %sub.74, f32[16,64,3,128]{3,1,2,0:T(8,128)} %get-tuple-element.295, ...), kind=kOutput, calls=%fused_computation.7.clone.1 | convolution fusion | flops 606339072 | bytes 8913925 | tf_op jit(solution)/shard_map/while/body/eval_jaxpr/sorc,sdc->sord/dot_general | solution.py:50
  69.6 4.3 fusion.39
  73.9 5.5 %select_add_fusion.8 = (f32[16,64,3,128]{3,1,2,0:T(8,128)S(1)}, f32[16,64,3,128]{3,1,2,0:T(8,128)}) fusion(f32[16,64,3,128]{3,1,2,0:T(8,128)S(1)} %get-tuple-element.296, f32[]{:T(128)} %bitcast.58, pred[]{:T(512)S(6)} %compare.18, f32[]{:T(128)S(6)} %sub.74, f32[16,64,3,128]{3,1,2,0:T(8,128)} %get-tuple-element.295, ...), kind=kOutput, calls=%fused_computation.7.clone.1 | convolution fusion | flops 606339072 | bytes 8913925 | tf_op jit(solution)/shard_map/while/body/eval_jaxpr/sorc,sdc->sord/dot_general | solution.py:50
  80.7 4.3 fusion.39
  85.0 5.5 %select_add_fusion.8 = (f32[16,64,3,128]{3,1,2,0:T(8,128)S(1)}, f32[16,64,3,128]{3,1,2,0:T(8,128)}) fusion(f32[16,64,3,128]{3,1,2,0:T(8,128)S(1)} %get-tuple-element.296, f32[]{:T(128)} %bitcast.58, pred[]{:T(512)S(6)} %compare.18, f32[]{:T(128)S(6)} %sub.74, f32[16,64,3,128]{3,1,2,0:T(8,128)} %get-tuple-element.295, ...), kind=kOutput, calls=%fused_computation.7.clone.1 | convolution fusion | flops 606339072 | bytes 8913925 | tf_op jit(solution)/shard_map/while/body/eval_jaxpr/sorc,sdc->sord/dot_general | solution.py:50
  91.8 4.3 fusion.39
  96.1 5.5 %select_add_fusion.8 = (f32[16,64,3,128]{3,1,2,0:T(8,128)S(1)}, f32[16,64,3,128]{3,1,2,0:T(8,128)}) fusion(f32[16,64,3,128]{3,1,2,0:T(8,128)S(1)} %get-tuple-element.296, f32[]{:T(128)} %bitcast.58, pred[]{:T(512)S(6)} %compare.18, f32[]{:T(128)S(6)} %sub.74, f32[16,64,3,128]{3,1,2,0:T(8,128)} %get-tuple-element.295, ...), kind=kOutput, calls=%fused_computation.7.clone.1 | convolution fusion | flops 606339072 | bytes 8913925 | tf_op jit(solution)/shard_map/while/body/eval_jaxpr/sorc,sdc->sord/dot_general | solution.py:50
  102.9 4.3 fusion.39
  107.2 5.5 %select_add_fusion.8 = (f32[16,64,3,128]{3,1,2,0:T(8,128)S(1)}, f32[16,64,3,128]{3,1,2,0:T(8,128)}) fusion(f32[16,64,3,128]{3,1,2,0:T(8,128)S(1)} %get-tuple-element.296, f32[]{:T(128)} %bitcast.58, pred[]{:T(512)S(6)} %compare.18, f32[]{:T(128)S(6)} %sub.74, f32[16,64,3,128]{3,1,2,0:T(8,128)} %get-tuple-element.295, ...), kind=kOutput, calls=%fused_computation.7.clone.1 | convolution fusion | flops 606339072 | bytes 8913925 | tf_op jit(solution)/shard_map/while/body/eval_jaxpr/sorc,sdc->sord/dot_general | solution.py:50
  114.6 4.9 %all-to-all-start = ((f32[4,4,64,3,128]{4,2,3,1,0:T(8,128)}), f32[4,4,64,3,128]{4,2,3,1,0:T(8,128)S(1)}, u32[]{:S(2)}, u32[]{:S(2)}) async-start(f32[4,4,64,3,128]{4,2,3,1,0:T(8,128)} %bitcast.66), calls=%async_computation | async-start | bytes 3145728 | tf_op jit(solution)/shard_map/all_to_all | solution.py:64
  120.9 36.0 %all-to-all-done = f32[4,4,64,3,128]{4,2,3,1,0:T(8,128)S(1)} async-done(((f32[4,4,64,3,128]{4,2,3,1,0:T(8,128)}), f32[4,4,64,3,128]{4,2,3,1,0:T(8,128)S(1)}, u32[]{:S(2)}, u32[]{:S(2)}) %all-to-all-start) | async-done | bytes 1572896 | tf_op jit(solution)/shard_map/all_to_all | solution.py:64
  158.7 2.9 select_add_fusion.5
  162.0 50.4 %all-reduce.4.cloned.1.call-done = f32[16,64,3,128]{3,1,2,0:T(8,128)} async-done(((f32[16,64,3,128]{3,1,2,0:T(8,128)}), f32[16,64,3,128]{3,1,2,0:T(8,128)}) %all-reduce.4.cloned.1.call-update) | async-done | bytes 1572880 | tf_op jit(solution)/shard_map/psum | solution.py:69
  212.4 1.9 multiply_reduce_fusion.1
  214.3 16.3 %all-reduce = (f32[3]{0:T(128)S(1)}, f32[3]{0:T(128)S(1)}) all-reduce(f32[3]{0:T(128)S(1)} %get-tuple-element.146, f32[3]{0:T(128)S(1)} %get-tuple-element.145), channel_id=1, replica_groups=mesh['grp'=2,'blk'=4,'term'=2,'sub'=2] {'blk','sub'}, use_global_device_ids=true, to_apply=%region_7.9 | all-reduce | flops 6 | bytes 48 | tf_op jit(solution)/shard_map/psum | solution.py:73
  230.6 2.2 multiply_reduce_fusion
  232.8 13.6 %psum.38 = f32[3]{0:T(128)S(1)} all-reduce(f32[3]{0:T(128)S(1)} %get-tuple-element.177), channel_id=1, replica_groups=mesh['grp'=2,'blk'=4,'term'=2,'sub'=2] {'blk','sub'}, use_global_device_ids=true, to_apply=%region_11.13 | all-reduce | flops 3 | bytes 24 | tf_op jit(solution)/shard_map/psum | solution.py:81
  248.1 9.3 %all-gather.5.cloned.1.call-done = f32[16,128,3,128]{3,1,2,0:T(8,128)} async-done(((f32[16,64,3,128]{3,1,2,0:T(8,128)}), f32[16,128,3,128]{3,1,2,0:T(8,128)}) %all-gather.5.cloned.1.call-update) | async-done | bytes 3145744 | tf_op jit(solution)/shard_map/all_gather | solution.py:45
  257.4 87.0 %while.27 = (s32[]{:T(128)}, f32[16,64,3,128]{3,1,2,0:T(8,128)}, f32[16,64,3,128]{3,1,2,0:T(8,128)S(1)}, s32[8]{0:T(128)S(1)}, f32[8,16,64,128]{3,2,1,0:T(8,128)...) while((s32[]{:T(128)}, f32[16,64,3,128]{3,1,2,0:T(8,128)}, ...), condition=%wide.region_13.15_spmd.clone, body=%wide.region_12.14_spmd.clone.sunk | while | flops 1210318848 | bytes 14157473 | solution.py:57
  258.6 4.3 fusion.43
  262.9 4.9 %select_add_fusion.9 = (f32[16,64,3,128]{3,1,2,0:T(8,128)S(1)}, f32[16,64,3,128]{3,1,2,0:T(8,128)}) fusion(f32[16,64,3,128]{3,1,2,0:T(8,128)S(1)} %get-tuple-element.329, f32[]{:T(128)} %bitcast.63, pred[]{:T(512)S(6)} %compare.19, f32[]{:T(128)S(6)} %sub.75, f32[16,64,3,128]{3,1,2,0:T(8,128)} %get-tuple-element.328, ...), kind=kOutput, calls=%fused_computation.17.clone.1 | convolution fusion | flops 606339072 | bytes 8913925 | tf_op jit(solution)/shard_map/while/body/eval_jaxpr/sorc,sdc->sord/dot_general | solution.py:50
  269.0 4.3 fusion.43
  273.3 5.4 %select_add_fusion.9 = (f32[16,64,3,128]{3,1,2,0:T(8,128)S(1)}, f32[16,64,3,128]{3,1,2,0:T(8,128)}) fusion(f32[16,64,3,128]{3,1,2,0:T(8,128)S(1)} %get-tuple-element.329, f32[]{:T(128)} %bitcast.63, pred[]{:T(512)S(6)} %compare.19, f32[]{:T(128)S(6)} %sub.75, f32[16,64,3,128]{3,1,2,0:T(8,128)} %get-tuple-element.328, ...), kind=kOutput, calls=%fused_computation.17.clone.1 | convolution fusion | flops 606339072 | bytes 8913925 | tf_op jit(solution)/shard_map/while/body/eval_jaxpr/sorc,sdc->sord/dot_general | solution.py:50
  280.0 4.3 fusion.43
  284.2 5.4 %select_add_fusion.9 = (f32[16,64,3,128]{3,1,2,0:T(8,128)S(1)}, f32[16,64,3,128]{3,1,2,0:T(8,128)}) fusion(f32[16,64,3,128]{3,1,2,0:T(8,128)S(1)} %get-tuple-element.329, f32[]{:T(128)} %bitcast.63, pred[]{:T(512)S(6)} %compare.19, f32[]{:T(128)S(6)} %sub.75, f32[16,64,3,128]{3,1,2,0:T(8,128)} %get-tuple-element.328, ...), kind=kOutput, calls=%fused_computation.17.clone.1 | convolution fusion | flops 606339072 | bytes 8913925 | tf_op jit(solution)/shard_map/while/body/eval_jaxpr/sorc,sdc->sord/dot_general | solution.py:50
  290.9 4.3 fusion.43
  295.2 5.4 %select_add_fusion.9 = (f32[16,64,3,128]{3,1,2,0:T(8,128)S(1)}, f32[16,64,3,128]{3,1,2,0:T(8,128)}) fusion(f32[16,64,3,128]{3,1,2,0:T(8,128)S(1)} %get-tuple-element.329, f32[]{:T(128)} %bitcast.63, pred[]{:T(512)S(6)} %compare.19, f32[]{:T(128)S(6)} %sub.75, f32[16,64,3,128]{3,1,2,0:T(8,128)} %get-tuple-element.328, ...), kind=kOutput, calls=%fused_computation.17.clone.1 | convolution fusion | flops 606339072 | bytes 8913925 | tf_op jit(solution)/shard_map/while/body/eval_jaxpr/sorc,sdc->sord/dot_general | solution.py:50
  301.8 4.3 fusion.43
  306.1 5.4 %select_add_fusion.9 = (f32[16,64,3,128]{3,1,2,0:T(8,128)S(1)}, f32[16,64,3,128]{3,1,2,0:T(8,128)}) fusion(f32[16,64,3,128]{3,1,2,0:T(8,128)S(1)} %get-tuple-element.329, f32[]{:T(128)} %bitcast.63, pred[]{:T(512)S(6)} %compare.19, f32[]{:T(128)S(6)} %sub.75, f32[16,64,3,128]{3,1,2,0:T(8,128)} %get-tuple-element.328, ...), kind=kOutput, calls=%fused_computation.17.clone.1 | convolution fusion | flops 606339072 | bytes 8913925 | tf_op jit(solution)/shard_map/while/body/eval_jaxpr/sorc,sdc->sord/dot_general | solution.py:50
  312.8 4.3 fusion.43
  317.1 5.4 %select_add_fusion.9 = (f32[16,64,3,128]{3,1,2,0:T(8,128)S(1)}, f32[16,64,3,128]{3,1,2,0:T(8,128)}) fusion(f32[16,64,3,128]{3,1,2,0:T(8,128)S(1)} %get-tuple-element.329, f32[]{:T(128)} %bitcast.63, pred[]{:T(512)S(6)} %compare.19, f32[]{:T(128)S(6)} %sub.75, f32[16,64,3,128]{3,1,2,0:T(8,128)} %get-tuple-element.328, ...), kind=kOutput, calls=%fused_computation.17.clone.1 | convolution fusion | flops 606339072 | bytes 8913925 | tf_op jit(solution)/shard_map/while/body/eval_jaxpr/sorc,sdc->sord/dot_general | solution.py:50
  323.7 4.3 fusion.43
  328.0 5.4 %select_add_fusion.9 = (f32[16,64,3,128]{3,1,2,0:T(8,128)S(1)}, f32[16,64,3,128]{3,1,2,0:T(8,128)}) fusion(f32[16,64,3,128]{3,1,2,0:T(8,128)S(1)} %get-tuple-element.329, f32[]{:T(128)} %bitcast.63, pred[]{:T(512)S(6)} %compare.19, f32[]{:T(128)S(6)} %sub.75, f32[16,64,3,128]{3,1,2,0:T(8,128)} %get-tuple-element.328, ...), kind=kOutput, calls=%fused_computation.17.clone.1 | convolution fusion | flops 606339072 | bytes 8913925 | tf_op jit(solution)/shard_map/while/body/eval_jaxpr/sorc,sdc->sord/dot_general | solution.py:50
  334.7 4.3 fusion.43
  338.9 5.4 %select_add_fusion.9 = (f32[16,64,3,128]{3,1,2,0:T(8,128)S(1)}, f32[16,64,3,128]{3,1,2,0:T(8,128)}) fusion(f32[16,64,3,128]{3,1,2,0:T(8,128)S(1)} %get-tuple-element.329, f32[]{:T(128)} %bitcast.63, pred[]{:T(512)S(6)} %compare.19, f32[]{:T(128)S(6)} %sub.75, f32[16,64,3,128]{3,1,2,0:T(8,128)} %get-tuple-element.328, ...), kind=kOutput, calls=%fused_computation.17.clone.1 | convolution fusion | flops 606339072 | bytes 8913925 | tf_op jit(solution)/shard_map/while/body/eval_jaxpr/sorc,sdc->sord/dot_general | solution.py:50
  345.2 42.2 %all_to_all.10 = f32[4,4,64,3,128]{4,2,3,1,0:T(8,128)} all-to-all(f32[4,4,64,3,128]{4,2,3,1,0:T(8,128)S(1)} %bitcast.67), channel_id=1, replica_groups=mesh['grp'=2,'blk'=4,'term'=2,'sub'=2] {'blk'}, dimensions={0} | all-to-all | bytes 3145728 | tf_op jit(solution)/shard_map/all_to_all | solution.py:64
  387.4 2.2 gather_fusion.6
  391.2 50.7 %all-reduce.6.cloned.1.call-done = f32[16,64,3,128]{3,1,2,0:T(8,128)} async-done(((f32[16,64,3,128]{3,1,2,0:T(8,128)}), f32[16,64,3,128]{3,1,2,0:T(8,128)}) %all-reduce.6.cloned.1.call-update) | async-done | bytes 1572880 | tf_op jit(solution)/shard_map/psum | solution.py:69
  441.8 3.1 multiply_add_fusion
  (76 shorter events, 21.1 us)
Async XLA Ops:
  7.2 0.8 copy-start.8
  7.2 17.2 %copy-start.9 = (s32[8]{0:T(128)S(1)}, s32[8]{0:T(128)}, u32[]{:S(2)}) copy-start(s32[8]{0:T(128)} %param.16) | copy-start | bytes 100
  7.2 17.2 %all-gather.3.cloned.1.call-start = ((), (), s32[]{:S(2)}) async-start(), calls=%async_computation.2 | async-start | bytes 4718592 | tf_op jit(solution)/shard_map/all_gather | solution.py:45
  114.6 42.3 %all-to-all-start = ((f32[4,4,64,3,128]{4,2,3,1,0:T(8,128)}), f32[4,4,64,3,128]{4,2,3,1,0:T(8,128)S(1)}, u32[]{:S(2)}, u32[]{:S(2)}) async-start(f32[4,4,64,3,128]{4,2,3,1,0:T(8,128)} %bitcast.66), calls=%async_computation | async-start | bytes 3145728 | tf_op jit(solution)/shard_map/all_to_all | solution.py:64
  119.5 92.9 %all-reduce.4.cloned.1.call-start = ((), (), s32[]{:S(2)}) async-start(), calls=%async_computation.3 | async-start | bytes 3145728 | tf_op jit(solution)/shard_map/psum | solution.py:69
  156.9 1.8 copy-start
  158.7 3.0 copy-start.6
  158.7 3.0 copy-start.7
  161.7 50.7 %copy-start.2 = (f32[16,64,3,128]{3,1,2,0:T(8,128)S(1)}, f32[16,64,3,128]{3,1,2,0:T(8,128)}, u32[]{:S(2)}) copy-start(f32[16,64,3,128]{3,1,2,0:T(8,128)} %param.13) | copy-start | bytes 4718596
  161.7 95.7 %all-gather.5.cloned.1.call-start = ((), (), s32[]{:S(2)}) async-start(), calls=%async_computation.4 | async-start | bytes 4718592 | tf_op jit(solution)/shard_map/all_gather | solution.py:45
  162.0 52.3 %copy-start.5 = (f32[16,64,128]{2,1,0:T(8,128)}, f32[16,64,128]{2,1,0:T(8,128)S(1)}, u32[]{:S(2)}) copy-start(f32[16,64,128]{2,1,0:T(8,128)S(1)} %broadcast_add_fusion) | copy-start | bytes 1572868
  232.8 15.0 %copy-start.3 = (f32[16,64,3,128]{3,1,2,0:T(8,128)}, f32[16,64,3,128]{3,1,2,0:T(8,128)S(1)}, u32[]{:S(2)}) copy-start(f32[16,64,3,128]{3,1,2,0:T(8,128)S(1)} %get-tuple-element.178) | copy-start | bytes 4718596
  247.9 194.0 %all-reduce.6.cloned.1.call-start = ((), (), s32[]{:S(2)}) async-start(), calls=%async_computation.5 | async-start | bytes 3145728 | tf_op jit(solution)/shard_map/psum | solution.py:69
  387.4 2.2 copy-start.1
  391.1 50.7 %copy-start.4 = (f32[16,64,3,128]{3,1,2,0:T(8,128)S(1)}, f32[16,64,3,128]{3,1,2,0:T(8,128)}, u32[]{:S(2)}) copy-start(f32[16,64,3,128]{3,1,2,0:T(8,128)} %copy-done.3) | copy-start | bytes 4718596
Sparse Core Ops, SparseCore 0:
  9.6 14.8 all-gather.2
  161.8 50.5 all-reduce.3
  248.0 9.3 all-gather.4
  391.3 50.5 all-reduce.5
where the time goes:
time: 453 us; the launch traced here: 451 us
  waiting for transfers between devices  162 us (36%)
  matrix products  155 us (34%)
  blocking collectives  72.1 us (16%)
  local copies, waits for them, and re-layouts  17.2 us (4%)
  other arithmetic  15.3 us (3%)
  between operations  14 us (3%)
  loops' own time  10.7 us (2%)
  starting transfers between devices  5.16 us (1%)
    psum x2, waiting for transfers between devices, sigma_whole(): total = lax.psum(kept + relay(moved), 'term')  101 us
    dot_general x16, matrix products, one_term(): jnp.einsum('sorc,sdc->sord', middle, right_block, precision=lax.Precision...  86.3 us
    dot_general x16, matrix products, one_term(): jnp.einsum('soi,sirc->sorc', left_block, full, precision=lax.Precision.HI...  68.3 us
    all_to_all x1, blocking collectives, relay(): lax.all_to_all(outgoing, 'blk', split_axis=0, concat_axis=0, tiled=True)  42.2 us
    all_to_all x1, waiting for transfers between devices, relay(): lax.all_to_all(outgoing, 'blk', split_axis=0, concat_axis=0, tiled=True)  36 us
    all_gather x2, waiting for transfers between devices, partials(): full = lax.all_gather(vector_half, 'sub', axis=1, tiled=True)  24.7 us
    psum x1, blocking collectives, shards(): lax.psum((jnp.sum(amplitudes * sigma_first, axis=(0, 1, 3)), jnp.sum(ampl...  16.3 us
    psum x1, blocking collectives, shards(): squares = lax.psum(jnp.sum(raw * raw, axis=(0, 1, 3)), ('blk', 'sub'))  13.6 us
  transfers between devices with their start and end apart: 5, of which 5 were waited for; matrix products, arithmetic and copies ran while one was open for 1% of the time, Pallas kernels for 0%

commit v1 on v0

v1 whole, which is shorter than its diff:
```python
import functools

import jax
import jax.numpy as jnp
from jax import lax
from jax.experimental import pallas as pl
from jax.experimental.pallas import tpu as pltpu
from jax.sharding import PartitionSpec as P

LIMIT = 48 * 1024 * 1024
WHOLE = pl.BlockSpec(memory_space=pltpu.VMEM)
SCALARS = pl.BlockSpec(memory_space=pltpu.SMEM)
ANY = pl.BlockSpec(memory_space=pl.ANY)


def power_of_two(size):
    return size & (size - 1) == 0


def flip(value, axis, bit):
    size = lax.axis_size(axis)
    return lax.ppermute(value, axis, [(i, i ^ bit) for i in range(size)])


def small_sum(value, axis):
    size = lax.axis_size(axis)
    if not power_of_two(size):
        return lax.psum(value, axis)
    if size == 4:
        one, two, three = (flip(value, axis, bit) for bit in (1, 2, 3))
        return (value + one) + (two + three)
    bit = 1
    while bit < size:
        value = value + flip(value, axis, bit)
        bit *= 2
    return value


def halves(value):
    high = value.astype(jnp.bfloat16)
    low = (value - high.astype(jnp.float32)).astype(jnp.bfloat16)
    return high, low


def table_kernel(devices, partner_ref, kind_ref, table_ref, used):
    count, terms = partner_ref.shape[0], kind_ref.shape[0]
    per = count // devices
    me = lax.axis_index("blk")
    for c in range(devices):
        used[c] = 0

    def place(j, carry):
        where_to = partner_ref[j]
        owner = lax.div(where_to, count)
        offset = lax.rem(owner - me + devices, devices)
        at = offset * per + used[offset]
        used[offset] = used[offset] + 1
        table_ref[at] = j
        table_ref[count + at] = where_to - owner * count
        table_ref[2 * count + j] = at
        return carry

    lax.fori_loop(0, count, place, 0)
    for k in range(terms):
        table_ref[3 * count + k] = kind_ref[k]
    table_ref[3 * count + terms] = lax.axis_index("sub")


def make_table(partner, term_kind):
    devices = lax.axis_size("blk")
    length = 3 * partner.shape[0] + term_kind.shape[0] + 1
    return pl.pallas_call(
        functools.partial(table_kernel, devices),
        out_shape=jax.ShapeDtypeStruct((length,), jnp.int32),
        in_specs=[SCALARS, SCALARS],
        out_specs=SCALARS,
        scratch_shapes=[pltpu.SMEM((devices,), jnp.int32)],
    )(partner, term_kind)


def sector_kernel(count, terms, table, l_ref, r_ref, own_ref, other_ref, *rest):
    moved_ref, kept_ref, lhs, high_rhs, low_rhs = rest[-5:]
    roots, rows, width = own_ref.shape[1:]
    first = table[3 * count + terms] == 0
    own, other = own_ref[0], other_ref[0]
    top = jnp.where(first, own, other)
    bottom = jnp.where(first, other, own)
    vector = jnp.concatenate(
        [jnp.concatenate([half[r] for r in range(roots)], axis=1) for half in (top, bottom)], axis=0
    )
    wide = jnp.concatenate(halves(vector), axis=1)
    left = l_ref[:, 0].reshape(terms * rows, 2 * rows)
    both = jnp.dot(
        jnp.concatenate(halves(left), axis=1),
        jnp.concatenate([wide, wide], axis=0),
        preferred_element_type=jnp.float32,
    )
    span = roots * width
    middle_high, middle_low = halves(both[:, :span] + both[:, span:])
    for k in range(terms):
        lanes = slice(k * width, (k + 1) * width)
        for r in range(roots):
            part = (slice(k * rows, (k + 1) * rows), slice(r * width, (r + 1) * width))
            lhs[r * rows : (r + 1) * rows, lanes] = middle_high[part]
            lhs[(roots + r) * rows : (roots + r + 1) * rows, lanes] = middle_low[part]
    blank = jnp.zeros((width, width), jnp.bfloat16)
    for k in range(terms):
        lanes = slice(k * width, (k + 1) * width)
        kind = table[3 * count + k]
        used = pl.ds(pl.multiple_of((1 - kind) * width, width), width)
        unused = pl.ds(pl.multiple_of(kind * width, width), width)
        high, low = halves(r_ref[k, 0])
        high_rhs[used, lanes] = high
        high_rhs[unused, lanes] = blank
        low_rhs[used, lanes] = low
        low_rhs[unused, lanes] = blank
    dims = (((1,), (1,)), ((), ()))
    tall = lax.dot_general(lhs[...], high_rhs[...], dims, preferred_element_type=jnp.float32)
    short = lax.dot_general(
        lhs[: roots * rows], low_rhs[...], dims, preferred_element_type=jnp.float32
    )
    result = tall[: roots * rows] + tall[roots * rows :] + short
    moved_ref[0] = result[:, :width].reshape(roots, rows, width)
    kept_ref[0] = result[:, width:].reshape(roots, rows, width)


def sectors(table, base, size, left, right, own, other, kept, ordered):
    terms, count, rows, _ = left.shape
    roots, width = own.shape[1], own.shape[3]

    def source(i, table):
        return table[base + i]

    def held(i, table):
        return base + i if ordered else table[base + i]

    def vector_at(i, table):
        return (held(i, table), 0, 0, 0)

    block = (1, roots, rows, width)
    in_specs = [
        pl.BlockSpec((terms, 1, rows, 2 * rows), lambda i, t: (0, source(i, t), 0, 0)),
        pl.BlockSpec((terms, 1, width, width), lambda i, t: (0, source(i, t), 0, 0)),
        pl.BlockSpec(block, vector_at),
        pl.BlockSpec(block, vector_at),
    ]
    args = [left, right, own, other]
    aliases = {}
    if kept is not None:
        in_specs.append(ANY)
        args.append(kept)
        aliases = {5: 1}
    flops = size * terms * rows * width * roots * width * 4 * 3
    return pl.pallas_call(
        functools.partial(sector_kernel, count, terms),
        out_shape=[
            jax.ShapeDtypeStruct((size,) + block[1:], jnp.float32),
            jax.ShapeDtypeStruct((count,) + block[1:], jnp.float32),
        ],
        grid_spec=pltpu.PrefetchScalarGridSpec(
            num_scalar_prefetch=1,
            grid=(size,),
            in_specs=in_specs,
            out_specs=[
                pl.BlockSpec(block, lambda i, t: (i, 0, 0, 0)),
                pl.BlockSpec(block, lambda i, t: (source(i, t), 0, 0, 0)),
            ],
            scratch_shapes=[
                pltpu.VMEM((2 * roots * rows, terms * width), jnp.bfloat16),
                pltpu.VMEM((2 * width, terms * width), jnp.bfloat16),
                pltpu.VMEM((2 * width, terms * width), jnp.bfloat16),
            ],
        ),
        input_output_aliases=aliases,
        compiler_params=pltpu.CompilerParams(vmem_limit_bytes=LIMIT),
        cost_estimate=pl.CostEstimate(
            flops=flops, bytes_accessed=size * terms * 3 * rows * width * 4, transcendentals=0
        ),
        name="sectors",
    )(table, *args)


def gather_kernel(share, with_inner, table, kept_ref, arrived_ref, vector_ref, diag_ref, sum_ref, *rest):
    vector = vector_ref[0]
    total = kept_ref[0] + arrived_ref[0] + (share * diag_ref[0])[None] * vector
    sum_ref[0] = total
    if with_inner:
        inner_ref = rest[0]

        @pl.when(pl.program_id(0) == 0)
        def _():
            inner_ref[...] = jnp.zeros_like(inner_ref)

        for r in range(vector.shape[0]):
            inner_ref[r : r + 1] += jnp.sum(vector[r] * total[r], axis=0, keepdims=True)


def combine(table, base, size, kept, arrived, vector, diag, share, ordered, with_inner):
    count, roots, rows, width = kept.shape
    block = (1, roots, rows, width)

    def slot(i, table):
        return table[count + base + i]

    def held(i, table):
        return table[2 * count + slot(i, table)] if ordered else slot(i, table)

    out_shape = [jax.ShapeDtypeStruct((size,) + block[1:], jnp.float32)]
    out_specs = [pl.BlockSpec(block, lambda i, t: (i, 0, 0, 0))]
    if with_inner:
        out_shape.append(jax.ShapeDtypeStruct((8, width), jnp.float32))
        out_specs.append(pl.BlockSpec((8, width), lambda i, t: (0, 0)))
    out = pl.pallas_call(
        functools.partial(gather_kernel, share, with_inner),
        out_shape=out_shape,
        grid_spec=pltpu.PrefetchScalarGridSpec(
            num_scalar_prefetch=1,
            grid=(size,),
            in_specs=[
                pl.BlockSpec(block, lambda i, t: (slot(i, t), 0, 0, 0)),
                pl.BlockSpec(block, lambda i, t: (i, 0, 0, 0)),
                pl.BlockSpec(block, lambda i, t: (held(i, t), 0, 0, 0)),
                pl.BlockSpec((1, rows, width), lambda i, t: (slot(i, t), 0, 0)),
            ],
            out_specs=out_specs,
        ),
        compiler_params=pltpu.CompilerParams(vmem_limit_bytes=LIMIT),
        cost_estimate=pl.CostEstimate(
            flops=size * roots * rows * width * 4,
            bytes_accessed=size * roots * rows * width * 16,
            transcendentals=0,
        ),
        name="combine",
    )(table, kept, arrived, vector, diag)
    return out if with_inner else (out[0], None)


def correct_kernel(pieces, table, weight_ref, inner_ref, vector_ref, diag_ref, *rest):
    parts, (raw_ref, squares_ref) = rest[:-2], rest[-2:]
    count, roots, rows, width = vector_ref.shape
    theta = jnp.sum(inner_ref[...], axis=1, keepdims=True) / jnp.sum(
        weight_ref[...], axis=1, keepdims=True
    )
    squares = [jnp.zeros((1, width), jnp.float32) for _ in range(roots)]
    for piece, (base, size) in enumerate(pieces):
        mine, theirs = parts[2 * piece], parts[2 * piece + 1]
        for i in range(size):
            slot = table[count + base + i]
            place = table[2 * count + slot]
            diag = diag_ref[slot]
            for r in range(roots):
                shift = theta[r : r + 1]
                sigma = mine[i, r] + theirs[i, r]
                raw = (sigma - shift * vector_ref[slot, r]) / jnp.maximum(jnp.abs(diag - shift), 1.0)
                raw_ref[place, r] = raw
                squares[r] = squares[r] + jnp.sum(raw * raw, axis=0, keepdims=True)
    squares_ref[...] = jnp.zeros_like(squares_ref)
    for r in range(roots):
        squares_ref[r : r + 1] = squares[r]


def correct(table, pieces, weight, inner, vector, diag, parts):
    return pl.pallas_call(
        functools.partial(correct_kernel, pieces),
        out_shape=[
            jax.ShapeDtypeStruct(vector.shape, jnp.float32),
            jax.ShapeDtypeStruct(weight.shape, jnp.float32),
        ],
        in_specs=[SCALARS] + [WHOLE] * (4 + len(parts)),
        out_specs=[WHOLE, WHOLE],
        compiler_params=pltpu.CompilerParams(vmem_limit_bytes=LIMIT),
        name="correct",
    )(table, weight, inner, vector, diag, *parts)


def scale_of(squares_ref, count):
    return lax.rsqrt(jnp.sum(squares_ref[...], axis=1, keepdims=True) / count + 1e-06)


def scaled_kernel(count, table, squares_ref, raw_ref, out_ref):
    scale = scale_of(squares_ref, count)
    for r in range(raw_ref.shape[1]):
        out_ref[0, r] = raw_ref[0, r] * scale[r : r + 1]


def scaled(table, squares, raw, count):
    slots, roots, rows, width = raw.shape
    block = (1, roots, rows, width)
    return pl.pallas_call(
        functools.partial(scaled_kernel, count),
        out_shape=jax.ShapeDtypeStruct(raw.shape, jnp.float32),
        grid_spec=pltpu.PrefetchScalarGridSpec(
            num_scalar_prefetch=1,
            grid=(slots,),
            in_specs=[
                pl.BlockSpec(squares.shape, lambda i, t: (0, 0)),
                pl.BlockSpec(block, lambda i, t: (t[2 * slots + i], 0, 0, 0)),
            ],
            out_specs=pl.BlockSpec(block, lambda i, t: (i, 0, 0, 0)),
        ),
        compiler_params=pltpu.CompilerParams(vmem_limit_bytes=LIMIT),
        name="scaled",
    )(table, squares, raw)


def finish_kernel(count, table, squares_ref, mine_ref, theirs_ref, *rest):
    out_ref = rest[-1]
    scale = scale_of(squares_ref, count)
    for r in range(mine_ref.shape[1]):
        out_ref[0, r] = (mine_ref[0, r] + theirs_ref[0, r]) * scale[r : r + 1]


def finish(table, base, squares, mine, theirs, out, slots, count):
    size, roots, rows, width = mine.shape
    block = (1, roots, rows, width)
    in_specs = [
        pl.BlockSpec(squares.shape, lambda i, t: (0, 0)),
        pl.BlockSpec(block, lambda i, t: (i, 0, 0, 0)),
        pl.BlockSpec(block, lambda i, t: (i, 0, 0, 0)),
    ]
    args, aliases = [squares, mine, theirs], {}
    if out is not None:
        in_specs.append(ANY)
        args.append(out)
        aliases = {4: 0}
    return pl.pallas_call(
        functools.partial(finish_kernel, count),
        out_shape=jax.ShapeDtypeStruct((slots,) + block[1:], jnp.float32),
        grid_spec=pltpu.PrefetchScalarGridSpec(
            num_scalar_prefetch=1,
            grid=(size,),
            in_specs=in_specs,
            out_specs=pl.BlockSpec(block, lambda i, t: (t[slots + base + i], 0, 0, 0)),
        ),
        input_output_aliases=aliases,
        compiler_params=pltpu.CompilerParams(vmem_limit_bytes=LIMIT),
        name="finish",
    )(table, *args)


def add_over_term(value):
    size = lax.axis_size("term")
    if size == 1 or not power_of_two(size):
        return lax.psum(value, "term"), jnp.zeros_like(value)
    bit = 1
    while 2 * bit < size:
        value = value + flip(value, "term", bit)
        bit *= 2
    return value, flip(value, "term", bit)


def shards(amplitudes, left, right, term_kind, partner, left_diag, right_diag):
    devices, terms_over = lax.axis_size("blk"), lax.axis_size("term")
    vector = jnp.transpose(amplitudes, (0, 2, 1, 3))
    slots, roots, rows, width = vector.shape
    per = slots // devices
    count = slots * devices * rows * lax.axis_size("sub") * width
    table = make_table(partner, term_kind)
    diag = left_diag[:, :, None] + right_diag[:, None, :]

    moving = [c for c in range(1, devices) if 2 * c != devices]
    moving.sort(key=lambda c: min(c, devices - c))
    moving = [(c, c * per, per) for c in moving]
    if devices % 2 == 0:
        c, cut = devices // 2, (per + 1) // 2
        moving.append((c, c * per, cut))
        if per > cut:
            moving.append((c, c * per + cut, per - cut))
    staying = (0, 0, per)
    order = [staying] + moving
    spans = [(base, size) for _, base, size in order]

    def sub_pair(value):
        return lax.ppermute(value, "sub", [(0, 1), (1, 0)])

    def partials(own, ordered, with_inner):
        other = sub_pair(own)
        kept, outgoing = None, {}
        for piece in moving + [staying]:
            outgoing[piece], kept = sectors(
                table, piece[1], piece[2], left, right, own, other, kept, ordered
            )
        sums, inners, arrivals = [], [], []
        for at, piece in enumerate(order):
            c, base, size = piece
            arrived = outgoing[piece]
            if c:
                if len(arrivals) >= 2:
                    arrived, _ = lax.optimization_barrier((arrived, arrivals[-2]))
                arrived = lax.ppermute(
                    arrived, "blk", [(p, (p + c) % devices) for p in range(devices)]
                )
                arrivals.append(arrived)
            mine, inner = combine(
                table, base, size, kept, arrived, own, diag, 1.0 / terms_over, ordered, with_inner
            )
            sums += list(add_over_term(mine))
            inners.append(inner)
        return sums, inners

    weight = jnp.sum(vector * vector, axis=(0, 2))
    weight = jnp.pad(weight, ((0, 8 - roots), (0, 0)), constant_values=1.0)
    weight = small_sum(small_sum(weight, "sub"), "blk")
    sums, inners = partials(vector, False, True)
    inner = sum(inners[1:], inners[0])
    for axis in ("sub", "term", "blk"):
        inner = small_sum(inner, axis)
    raw, squares = correct(table, spans, weight, inner, vector, diag, sums)
    for axis in ("sub", "blk"):
        squares = small_sum(squares, axis)
    sums, _ = partials(raw, True, False)
    correction = scaled(table, squares, raw, count)
    sigma = None
    for piece, (base, size) in enumerate(spans):
        sigma = finish(
            table, base, squares, sums[2 * piece], sums[2 * piece + 1], sigma, slots, count
        )
    return jnp.transpose(sigma, (0, 2, 1, 3)), jnp.transpose(correction, (0, 2, 1, 3))


def solution(mesh):
    return jax.shard_map(
        shards,
        mesh=mesh,
        in_specs=(
            P(("grp", "blk"), "sub", None, None),
            P(("grp", "term"), "blk", "sub", None),
            P(("grp", "term"), "blk", None, None),
            P(("grp", "term")),
            P(("grp", "blk")),
            P(("grp", "blk"), "sub"),
            P(("grp", "blk"), None),
        ),
        out_specs=(P(("grp", "blk"), "sub", None, None), P(("grp", "blk"), "sub", None, None)),
        check_vma=False,
    )
```

time: 453 us -> 192 us (0.42)
  matrix products: 155 us -> 0 us
  waiting for transfers between devices: 162 us -> 67.4 us
  Pallas kernels: 0 us -> 86.5 us
  blocking collectives: 72.1 us -> 0 us
  starting transfers between devices: 5.16 us -> 34.5 us
  local copies, waits for them, and re-layouts: 17.2 us -> 2.08 us
  other arithmetic: 15.3 us -> 0.4 us
  between operations: 14 us -> 0.91 us
  loops' own time: 10.7 us -> 0 us
    dot_general x32 -> x0, matrix products: 155 us -> none  [the longest x16 86.3 us: one_term(): jnp.einsum('sorc,sdc->sord', middle, right_block, precision=lax.Precision...]
    psum x2 -> x0, waiting for transfers between devices: 101 us -> none  [sigma_whole(): total = lax.psum(kept + relay(moved), 'term')]
    pallas_call x0 -> x28, Pallas kernels: none -> 86.5 us  [the longest x10 60.3 us: sectors(): pl.pallas_call(functools.partial(sector_kernel, count, terms), out_shape=...]
    ppermute x0 -> x33, waiting for transfers between devices: none -> 67.4 us  [the longest x23 41.4 us: flip(): return lax.ppermute(value, axis, [(i, i ^ bit) for i in range(size)])]
    all_to_all x1 -> x0, blocking collectives: 42.2 us -> none  [relay(): lax.all_to_all(outgoing, 'blk', split_axis=0, concat_axis=0, tiled=True)]
    all_to_all x1 -> x0, waiting for transfers between devices: 36 us -> none  [relay(): lax.all_to_all(outgoing, 'blk', split_axis=0, concat_axis=0, tiled=True)]
    ppermute x0 -> x33, starting transfers between devices: none -> 34.5 us  [the longest x23 21.5 us: flip(): return lax.ppermute(value, axis, [(i, i ^ bit) for i in range(size)])]
    psum x2 -> x0, blocking collectives: 29.9 us -> none  [the longest x1 16.3 us: shards(): lax.psum((jnp.sum(amplitudes * sigma_first, axis=(0, 1, 3)), jnp.sum(ampl...]
  transfers between devices with their start and end apart: 5 -> 33, of which waited for: 5 -> 20; matrix products, arithmetic and copies ran while one was open for 1% -> 0% of each run, Pallas kernels for 0% -> 28%
where the time goes in v1:
time: 192 us
  Pallas kernels  86.5 us (45%)
  waiting for transfers between devices  67.4 us (35%)
  starting transfers between devices  34.5 us (18%)
  local copies, waits for them, and re-layouts  2.08 us (1%)
    pallas_call x10, Pallas kernels, sectors(): pl.pallas_call(functools.partial(sector_kernel, count, terms), out_shape=...  60.3 us
    ppermute x23, waiting for transfers between devices, flip(): return lax.ppermute(value, axis, [(i, i ^ bit) for i in range(size)])  41.4 us
    ppermute x23, starting transfers between devices, flip(): return lax.ppermute(value, axis, [(i, i ^ bit) for i in range(size)])  21.5 us
    ppermute x8, waiting for transfers between devices, partials(): lax.ppermute(arrived, 'blk', [(p, (p + c) % devices) for p in range(devic...  20.9 us
    ppermute x8, starting transfers between devices, partials(): lax.ppermute(arrived, 'blk', [(p, (p + c) % devices) for p in range(devic...  12.4 us
    pallas_call x5, Pallas kernels, finish(): pl.pallas_call(functools.partial(finish_kernel, count), out_shape=jax.Sha...  9.14 us
    pallas_call x10, Pallas kernels, combine(): pl.pallas_call(functools.partial(gather_kernel, share, with_inner), out_s...  6.92 us
    pallas_call x1, Pallas kernels, scaled(): pl.pallas_call(functools.partial(scaled_kernel, count), out_shape=jax.Sha...  6.5 us
  transfers between devices with their start and end apart: 33, of which 20 were waited for; matrix products, arithmetic and copies ran while one was open for 0% of the time, Pallas kernels for 28%

profile of v1, /device:TPU:0, one launch (start us, length us, event | category | flops | bytes accessed | tf_op | source)
XLA Modules:
  0.0 191.8 jit_solution(13264494801123831405)
XLA Ops:
  1.1 1.5 shard_map.86.table
  2.7 1.7 collective-permute-done.4.other_ref
  4.4 1.4 copy-done
  6.5 7.1 %sectors.10 = (f32[4,3,64,128]{3,2,1,0:T(8,128)S(1)}, f32[16,3,64,128]{3,2,1,0:T(8,128)S(1)}) custom-call(s32[57]{0:T(128)S(1)} %copy-done.1, f32[8,16,64,128]{3,2,1,0:T(8,128)} %l_ref.19, f32[8,16,128,128]{3,2,1,0:T(8,128)} %r_ref.19, f32[16,3,64,128]{3,2,1,0:T(8,128)S(1)} %bitcast.6, f32[16,3,64,128]{3,2,1,0:T(8,128)S(1)} %collective-permute-done.4.other_ref), custom_call_target="tpu_custom_call" | custom-call | flops 1207959552 | bytes 3145728 | tf_op jit(solution)/shard_map/sectors/pallas_call | solution.py:154
  13.6 7.1 %sectors.11 = (f32[4,3,64,128]{3,2,1,0:T(8,128)S(1)}, f32[16,3,64,128]{3,2,1,0:T(8,128)S(1)}) custom-call(s32[57]{0:T(128)S(1)} %copy-done.1, f32[8,16,64,128]{3,2,1,0:T(8,128)} %l_ref.19, f32[8,16,128,128]{3,2,1,0:T(8,128)} %r_ref.19, f32[16,3,64,128]{3,2,1,0:T(8,128)S(1)} %bitcast.7, ...), custom_call_target="tpu_custom_call", output_to_operand_aliasing={{1}: (5, {})} | custom-call | flops 1207959552 | bytes 3145728 | tf_op jit(solution)/shard_map/sectors/pallas_call | solution.py:154
  20.7 5.0 %collective-permute-start.6 = (f32[4,3,64,128]{3,2,1,0:T(8,128)S(1)}, f32[4,3,64,128]{3,2,1,0:T(8,128)S(1)}, u32[]{:S(2)}, u32[]{:S(2)}) collective-permute-start(f32[4,3,64,128]{3,2,1,0:T(8,128)S(1)} %get-tuple-element.47), channel_id=1, source_target_pairs={{0,12},{4,0},{8,4},{12,8},{1,13},{5,1},{9,5},{13,9},{2,14},{6,2},{... | collective-permute-start | bytes 1179656 | tf_op jit(solution)/shard_map/ppermute | solution.py:390
  26.0 4.4 %sectors.12 = (f32[2,3,64,128]{3,2,1,0:T(8,128)S(1)}, f32[16,3,64,128]{3,2,1,0:T(8,128)S(1)}) custom-call(s32[57]{0:T(128)S(1)} %copy-done.1, f32[8,16,64,128]{3,2,1,0:T(8,128)} %l_ref.19, f32[8,16,128,128]{3,2,1,0:T(8,128)} %r_ref.19, f32[16,3,64,128]{3,2,1,0:T(8,128)S(1)} %bitcast.8, ...), custom_call_target="tpu_custom_call", output_to_operand_aliasing={{1}: (5, {})} | custom-call | flops 603979776 | bytes 1572864 | tf_op jit(solution)/shard_map/sectors/pallas_call | solution.py:154
  30.4 4.4 %sectors.13 = (f32[2,3,64,128]{3,2,1,0:T(8,128)S(1)}, f32[16,3,64,128]{3,2,1,0:T(8,128)S(1)}) custom-call(s32[57]{0:T(128)S(1)} %copy-done.1, f32[8,16,64,128]{3,2,1,0:T(8,128)} %l_ref.19, f32[8,16,128,128]{3,2,1,0:T(8,128)} %r_ref.19, f32[16,3,64,128]{3,2,1,0:T(8,128)S(1)} %bitcast.9, ...), custom_call_target="tpu_custom_call", output_to_operand_aliasing={{1}: (5, {})} | custom-call | flops 603979776 | bytes 1572864 | tf_op jit(solution)/shard_map/sectors/pallas_call | solution.py:154
  35.3 1.4 collective-permute-start.8
  36.7 8.0 %collective-permute-done.5.arrived_ref = f32[4,3,64,128]{3,2,1,0:T(8,128)S(1)} collective-permute-done((f32[4,3,64,128]{3,2,1,0:T(8,128)S(1)}, f32[4,3,64,128]{3,2,1,0:T(8,128)S(1)}, u32[]{:S(2)}, u32[]{:S(2)}) %collective-permute-start.5) | collective-permute-done | bytes 393248 | tf_op jit(solution)/shard_map/ppermute | solution.py:390
  45.9 7.1 %sectors.14 = (f32[4,3,64,128]{3,2,1,0:T(8,128)S(1)}, f32[16,3,64,128]{3,2,1,0:T(8,128)S(1)}) custom-call(s32[57]{0:T(128)S(1)} %copy-done.1, f32[8,16,64,128]{3,2,1,0:T(8,128)} %l_ref.19, f32[8,16,128,128]{3,2,1,0:T(8,128)} %r_ref.19, f32[16,3,64,128]{3,2,1,0:T(8,128)S(1)} %bitcast.10, ...), custom_call_target="tpu_custom_call", output_to_operand_aliasing={{1}: (5, {})} | custom-call | flops 1207959552 | bytes 3145728 | tf_op jit(solution)/shard_map/sectors/pallas_call | solution.py:154
  57.2 3.5 %collective-permute-done.7.arrived_ref = f32[2,3,64,128]{3,2,1,0:T(8,128)S(1)} collective-permute-done((f32[2,3,64,128]{3,2,1,0:T(8,128)S(1)}, f32[2,3,64,128]{3,2,1,0:T(8,128)S(1)}, u32[]{:S(2)}, u32[]{:S(2)}) %collective-permute-start.7) | collective-permute-done | bytes 196640 | tf_op jit(solution)/shard_map/ppermute | solution.py:390
  62.5 1.5 collective-permute-start.10
  64.1 1.7 collective-permute-start.3
  65.8 1.8 collective-permute-start.1
  69.1 1.5 collective-permute-start.15
  71.1 1.6 collective-permute-start.13
  73.7 2.9 %collective-permute-done.13 = f32[8,128]{1,0:T(8,128)S(1)} collective-permute-done((f32[8,128]{1,0:T(8,128)S(1)}, f32[8,128]{1,0:T(8,128)S(1)}, u32[]{:S(2)}, u32[]{:S(2)}) %collective-permute-start.13) | collective-permute-done | bytes 4128 | tf_op jit(solution)/shard_map/ppermute | solution.py:22
  76.5 1.5 collective-permute-start.17
  78.6 2.0 %collective-permute-done.14.rest_1_ = f32[4,3,64,128]{3,2,1,0:T(8,128)S(1)} collective-permute-done((f32[4,3,64,128]{3,2,1,0:T(8,128)S(1)}, f32[4,3,64,128]{3,2,1,0:T(8,128)S(1)}, u32[]{:S(2)}, u32[]{:S(2)}) %collective-permute-start.14) | collective-permute-done | bytes 393248 | tf_op jit(solution)/shard_map/ppermute | solution.py:22
  80.6 8.4 %collective-permute-done.15.rest_3_ = f32[4,3,64,128]{3,2,1,0:T(8,128)S(1)} collective-permute-done((f32[4,3,64,128]{3,2,1,0:T(8,128)S(1)}, f32[4,3,64,128]{3,2,1,0:T(8,128)S(1)}, u32[]{:S(2)}, u32[]{:S(2)}) %collective-permute-start.15) | collective-permute-done | bytes 393248 | tf_op jit(solution)/shard_map/ppermute | solution.py:22
  89.1 8.4 %collective-permute-done.16.rest_5_ = f32[4,3,64,128]{3,2,1,0:T(8,128)S(1)} collective-permute-done((f32[4,3,64,128]{3,2,1,0:T(8,128)S(1)}, f32[4,3,64,128]{3,2,1,0:T(8,128)S(1)}, u32[]{:S(2)}, u32[]{:S(2)}) %collective-permute-start.16) | collective-permute-done | bytes 393248 | tf_op jit(solution)/shard_map/ppermute | solution.py:22
  97.5 4.2 %collective-permute-done.17.rest_7_ = f32[2,3,64,128]{3,2,1,0:T(8,128)S(1)} collective-permute-done((f32[2,3,64,128]{3,2,1,0:T(8,128)S(1)}, f32[2,3,64,128]{3,2,1,0:T(8,128)S(1)}, u32[]{:S(2)}, u32[]{:S(2)}) %collective-permute-start.17) | collective-permute-done | bytes 196640 | tf_op jit(solution)/shard_map/ppermute | solution.py:22
  101.7 2.2 %collective-permute-done.18.rest_9_ = f32[2,3,64,128]{3,2,1,0:T(8,128)S(1)} collective-permute-done((f32[2,3,64,128]{3,2,1,0:T(8,128)S(1)}, f32[2,3,64,128]{3,2,1,0:T(8,128)S(1)}, u32[]{:S(2)}, u32[]{:S(2)}) %collective-permute-start.18) | collective-permute-done | bytes 196640 | tf_op jit(solution)/shard_map/ppermute | solution.py:22
  103.9 2.1 %correct.1 = (f32[16,3,64,128]{3,2,1,0:T(8,128)S(1)}, f32[8,128]{1,0:T(8,128)S(1)}) custom-call(s32[57]{0:T(128)S(1)} %copy-done.1, f32[8,128]{1,0:T(8,128)S(1)} %add_add_fusion.3.weight_ref, f32[8,128]{1,0:T(8,128)S(1)} %add_add_fusion.1.inner_ref, f32[16,3,64,128]{3,2,1,0:T(8,128)} %bitcast.5, f32[16,64,128]{2,1,0:T(8,128)S(1)} %broadcast_add_fusion.diag_ref, ...), custom_call_target="tpu_custom_call" | custom-call | tf_op jit(solution)/shard_map/correct/pallas_call | solution.py:263
  106.1 3.4 %collective-permute-done.23.other_ref = f32[16,3,64,128]{3,2,1,0:T(8,128)S(1)} collective-permute-done((f32[16,3,64,128]{3,2,1,0:T(8,128)S(1)}, f32[16,3,64,128]{3,2,1,0:T(8,128)S(1)}, u32[]{:S(2)}, u32[]{:S(2)}) %collective-permute-start.23) | collective-permute-done | bytes 1572896 | tf_op jit(solution)/shard_map/ppermute | solution.py:374
  109.5 7.1 %sectors.15 = (f32[4,3,64,128]{3,2,1,0:T(8,128)S(1)}, f32[16,3,64,128]{3,2,1,0:T(8,128)S(1)}) custom-call(s32[57]{0:T(128)S(1)} %copy-done.1, f32[8,16,64,128]{3,2,1,0:T(8,128)} %l_ref.19, f32[8,16,128,128]{3,2,1,0:T(8,128)} %r_ref.19, f32[16,3,64,128]{3,2,1,0:T(8,128)S(1)} %get-tuple-element.61.own_ref.vector_ref.raw_ref, ...), custom_call_target="tpu_custom_call" | custom-call | flops 1207959552 | bytes 3145728 | tf_op jit(solution)/shard_map/sectors/pallas_call | solution.py:154
  116.6 7.1 %sectors.16 = (f32[4,3,64,128]{3,2,1,0:T(8,128)S(1)}, f32[16,3,64,128]{3,2,1,0:T(8,128)S(1)}) custom-call(s32[57]{0:T(128)S(1)} %copy-done.1, f32[8,16,64,128]{3,2,1,0:T(8,128)} %l_ref.19, f32[8,16,128,128]{3,2,1,0:T(8,128)} %r_ref.19, f32[16,3,64,128]{3,2,1,0:T(8,128)S(1)} %get-tuple-element.61.own_ref.vector_ref.raw_ref, ...), custom_call_target="tpu_custom_call", output_to_operand_aliasing={{1}: (5, {})} | custom-call | flops 1207959552 | bytes 3145728 | tf_op jit(solution)/shard_map/sectors/pallas_call | solution.py:154
  123.8 1.7 collective-permute-start.24
  127.0 1.7 collective-permute-start.21
  128.7 4.4 %sectors.17 = (f32[2,3,64,128]{3,2,1,0:T(8,128)S(1)}, f32[16,3,64,128]{3,2,1,0:T(8,128)S(1)}) custom-call(s32[57]{0:T(128)S(1)} %copy-done.1, f32[8,16,64,128]{3,2,1,0:T(8,128)} %l_ref.19, f32[8,16,128,128]{3,2,1,0:T(8,128)} %r_ref.19, f32[16,3,64,128]{3,2,1,0:T(8,128)S(1)} %get-tuple-element.61.own_ref.vector_ref.raw_ref, ...), custom_call_target="tpu_custom_call", output_to_operand_aliasing={{1}: (5, {})} | custom-call | flops 603979776 | bytes 1572864 | tf_op jit(solution)/shard_map/sectors/pallas_call | solution.py:154
  133.1 4.4 %sectors.18 = (f32[2,3,64,128]{3,2,1,0:T(8,128)S(1)}, f32[16,3,64,128]{3,2,1,0:T(8,128)S(1)}) custom-call(s32[57]{0:T(128)S(1)} %copy-done.1, f32[8,16,64,128]{3,2,1,0:T(8,128)} %l_ref.19, f32[8,16,128,128]{3,2,1,0:T(8,128)} %r_ref.19, f32[16,3,64,128]{3,2,1,0:T(8,128)S(1)} %get-tuple-element.61.own_ref.vector_ref.raw_ref, ...), custom_call_target="tpu_custom_call", output_to_operand_aliasing={{1}: (5, {})} | custom-call | flops 603979776 | bytes 1572864 | tf_op jit(solution)/shard_map/sectors/pallas_call | solution.py:154
  137.5 1.3 collective-permute-start.25
  138.8 6.6 %collective-permute-done.27.arrived_ref = f32[4,3,64,128]{3,2,1,0:T(8,128)S(1)} collective-permute-done((f32[4,3,64,128]{3,2,1,0:T(8,128)S(1)}, f32[4,3,64,128]{3,2,1,0:T(8,128)S(1)}, u32[]{:S(2)}, u32[]{:S(2)}) %collective-permute-start.27) | collective-permute-done | bytes 393248 | tf_op jit(solution)/shard_map/ppermute | solution.py:390
  145.4 1.4 collective-permute-start.28
  146.8 7.1 %sectors.19 = (f32[4,3,64,128]{3,2,1,0:T(8,128)S(1)}, f32[16,3,64,128]{3,2,1,0:T(8,128)S(1)}) custom-call(s32[57]{0:T(128)S(1)} %copy-done.1, f32[8,16,64,128]{3,2,1,0:T(8,128)} %l_ref.19, f32[8,16,128,128]{3,2,1,0:T(8,128)} %r_ref.19, f32[16,3,64,128]{3,2,1,0:T(8,128)S(1)} %get-tuple-element.61.own_ref.vector_ref.raw_ref, ...), custom_call_target="tpu_custom_call", output_to_operand_aliasing={{1}: (5, {})} | custom-call | flops 1207959552 | bytes 3145728 | tf_op jit(solution)/shard_map/sectors/pallas_call | solution.py:154
  156.0 1.5 collective-permute-start.31
  158.9 1.4 collective-permute-start.22
  162.8 1.5 collective-permute-done.22
  164.3 1.5 collective-permute-start.26
  166.3 6.5 %scaled.1 = f32[16,3,64,128]{3,2,1,0:T(8,128)} custom-call(s32[57]{0:T(128)S(1)} %copy-done.1, f32[8,128]{1,0:T(8,128)S(1)} %add_add_fusion.squares_ref, f32[16,3,64,128]{3,2,1,0:T(8,128)S(1)} %get-tuple-element.61.own_ref.vector_ref.raw_ref), custom_call_target="tpu_custom_call" | custom-call | tf_op jit(solution)/shard_map/scaled/pallas_call | solution.py:289
  172.8 2.1 %finish.5.rest_0_ = f32[16,3,64,128]{3,2,1,0:T(8,128)} custom-call(s32[57]{0:T(128)S(1)} %copy-done.1, f32[8,128]{1,0:T(8,128)S(1)} %add_add_fusion.squares_ref, f32[4,3,64,128]{3,2,1,0:T(8,128)S(1)} %combine.19.mine_ref, f32[4,3,64,128]{3,2,1,0:T(8,128)S(1)} %collective-permute-done.32.theirs_ref), custom_call_target="tpu_custom_call" | custom-call | tf_op jit(solution)/shard_map/finish/pallas_call | solution.py:326
  175.2 2.1 %finish.6.rest_0_ = f32[16,3,64,128]{3,2,1,0:T(8,128)} custom-call(s32[57]{0:T(128)S(1)} %copy-done.1, f32[8,128]{1,0:T(8,128)S(1)} %add_add_fusion.squares_ref, f32[4,3,64,128]{3,2,1,0:T(8,128)S(1)} %combine.18.mine_ref, f32[4,3,64,128]{3,2,1,0:T(8,128)S(1)} %collective-permute-done.31.theirs_ref, ...), custom_call_target="tpu_custom_call", output_to_operand_aliasing={{}: (4, {})} | custom-call | tf_op jit(solution)/shard_map/finish/pallas_call | solution.py:326
  177.3 6.3 %collective-permute-done.30.theirs_ref = f32[4,3,64,128]{3,2,1,0:T(8,128)S(1)} collective-permute-done((f32[4,3,64,128]{3,2,1,0:T(8,128)S(1)}, f32[4,3,64,128]{3,2,1,0:T(8,128)S(1)}, u32[]{:S(2)}, u32[]{:S(2)}) %collective-permute-start.30) | collective-permute-done | bytes 393248 | tf_op jit(solution)/shard_map/ppermute | solution.py:22
  183.6 2.1 %finish.7.rest_0_ = f32[16,3,64,128]{3,2,1,0:T(8,128)} custom-call(s32[57]{0:T(128)S(1)} %copy-done.1, f32[8,128]{1,0:T(8,128)S(1)} %add_add_fusion.squares_ref, f32[4,3,64,128]{3,2,1,0:T(8,128)S(1)} %combine.17.mine_ref, f32[4,3,64,128]{3,2,1,0:T(8,128)S(1)} %collective-permute-done.30.theirs_ref, ...), custom_call_target="tpu_custom_call", output_to_operand_aliasing={{}: (4, {})} | custom-call | tf_op jit(solution)/shard_map/finish/pallas_call | solution.py:326
  185.8 3.3 %collective-permute-done.29.theirs_ref = f32[2,3,64,128]{3,2,1,0:T(8,128)S(1)} collective-permute-done((f32[2,3,64,128]{3,2,1,0:T(8,128)S(1)}, f32[2,3,64,128]{3,2,1,0:T(8,128)S(1)}, u32[]{:S(2)}, u32[]{:S(2)}) %collective-permute-start.29) | collective-permute-done | bytes 196640 | tf_op jit(solution)/shard_map/ppermute | solution.py:22
  189.0 1.4 finish.8.rest_0_
  190.4 1.4 finish.9
  (65 shorter events, 21.0 us)
Async XLA Ops:
  0.6 3.8 %collective-permute-start.4 = (f32[16,3,64,128]{3,2,1,0:T(8,128)}, f32[16,3,64,128]{3,2,1,0:T(8,128)S(1)}, u32[]{:S(2)}, u32[]{:S(2)}) collective-permute-start(f32[16,3,64,128]{3,2,1,0:T(8,128)} %bitcast.4), channel_id=1, source_target_pairs={{0,1},{1,0},{2,3},{3,2},{4,5},{5,4},{6,7},{7,6},{8,9},{9,8},{10,11... | collective-permute-start | bytes 4718600 | tf_op jit(solution)/shard_map/ppermute | solution.py:374
  4.4 1.4 copy-start
  5.8 0.7 copy-start.1
  13.6 12.2 %copy-start.2 = (f32[16,128]{1,0:T(8,128)S(1)}, f32[16,128]{1,0:T(8,128)}, u32[]{:S(2)}) copy-start(f32[16,128]{1,0:T(8,128)} %param.13) | copy-start | bytes 24580
  13.6 12.2 %copy-start.3 = (f32[16,64]{1,0:T(8,128)S(1)}, f32[16,64]{1,0:T(8,128)}, u32[]{:S(2)}) copy-start(f32[16,64]{1,0:T(8,128)} %param.12) | copy-start | bytes 12292
  20.7 14.5 %collective-permute-start.6 = (f32[4,3,64,128]{3,2,1,0:T(8,128)S(1)}, f32[4,3,64,128]{3,2,1,0:T(8,128)S(1)}, u32[]{:S(2)}, u32[]{:S(2)}) collective-permute-start(f32[4,3,64,128]{3,2,1,0:T(8,128)S(1)} %get-tuple-element.47), channel_id=1, source_target_pairs={{0,12},{4,0},{8,4},{12,8},{1,13},{5,1},{9,5},{13,9},{2,14},{6,2},{... | collective-permute-start | bytes 1179656 | tf_op jit(solution)/shard_map/ppermute | solution.py:390
  25.8 18.9 %collective-permute-start.5 = (f32[4,3,64,128]{3,2,1,0:T(8,128)S(1)}, f32[4,3,64,128]{3,2,1,0:T(8,128)S(1)}, u32[]{:S(2)}, u32[]{:S(2)}) collective-permute-start(f32[4,3,64,128]{3,2,1,0:T(8,128)S(1)} %get-tuple-element.45), channel_id=1, source_target_pairs={{0,4},{4,8},{8,12},{12,0},{1,5},{5,9},{9,13},{13,1},{2,6},{6,10},{... | collective-permute-start | bytes 1179656 | tf_op jit(solution)/shard_map/ppermute | solution.py:390
  35.3 21.2 %collective-permute-start.8 = (f32[2,3,64,128]{3,2,1,0:T(8,128)S(1)}, f32[2,3,64,128]{3,2,1,0:T(8,128)S(1)}, u32[]{:S(2)}, u32[]{:S(2)}) collective-permute-start(f32[2,3,64,128]{3,2,1,0:T(8,128)S(1)} %get-tuple-element.53), channel_id=1, source_target_pairs={{0,8},{4,12},{8,0},{12,4},{1,9},{5,13},{9,1},{13,5},{2,10},{6,14},... | collective-permute-start | bytes 589832 | tf_op jit(solution)/shard_map/ppermute | solution.py:390
  44.7 15.9 %collective-permute-start.7 = (f32[2,3,64,128]{3,2,1,0:T(8,128)S(1)}, f32[2,3,64,128]{3,2,1,0:T(8,128)S(1)}, u32[]{:S(2)}, u32[]{:S(2)}) collective-permute-start(f32[2,3,64,128]{3,2,1,0:T(8,128)S(1)} %get-tuple-element.50), channel_id=1, source_target_pairs={{0,8},{4,12},{8,0},{12,4},{1,9},{5,13},{9,1},{13,5},{2,10},{6,14},... | collective-permute-start | bytes 589832 | tf_op jit(solution)/shard_map/ppermute | solution.py:390
  61.3 1.2 collective-permute-start.9
  61.4 2.6 %collective-permute-start = (f32[8,128]{1,0:T(8,128)S(1)}, f32[8,128]{1,0:T(8,128)S(1)}, u32[]{:S(2)}, u32[]{:S(2)}) collective-permute-start(f32[8,128]{1,0:T(8,128)S(1)} %pad.4), channel_id=1, source_target_pairs={{0,1},{1,0},{2,3},{3,2},{4,5},{5,4},{6,7},{7,6},{8,9},{9,8},{10,11... | collective-permute-start | bytes 12296 | tf_op jit(solution)/shard_map/ppermute | solution.py:22
  62.5 5.1 %collective-permute-start.10 = (f32[8,128]{1,0:T(8,128)S(1)}, f32[8,128]{1,0:T(8,128)S(1)}, u32[]{:S(2)}, u32[]{:S(2)}) collective-permute-start(f32[8,128]{1,0:T(8,128)S(1)} %add.77), channel_id=1, source_target_pairs={{0,2},{2,0},{1,3},{3,1},{4,6},{6,4},{5,7},{7,5},{8,10},{10,8},{9,1... | collective-permute-start | bytes 12296 | tf_op jit(solution)/shard_map/ppermute | solution.py:22
  64.0 5.1 %collective-permute-start.2 = (f32[8,128]{1,0:T(8,128)S(1)}, f32[8,128]{1,0:T(8,128)S(1)}, u32[]{:S(2)}, u32[]{:S(2)}) collective-permute-start(f32[8,128]{1,0:T(8,128)S(1)} %pad_add_fusion), channel_id=1, source_target_pairs={{0,8},{4,12},{8,0},{12,4},{1,9},{5,13},{9,1},{13,5},{2,10},{6,14},... | collective-permute-start | bytes 12296 | tf_op jit(solution)/shard_map/ppermute | solution.py:22
  64.1 6.5 %collective-permute-start.3 = (f32[8,128]{1,0:T(8,128)S(1)}, f32[8,128]{1,0:T(8,128)S(1)}, u32[]{:S(2)}, u32[]{:S(2)}) collective-permute-start(f32[8,128]{1,0:T(8,128)S(1)} %pad_add_fusion), channel_id=1, source_target_pairs={{0,12},{4,8},{8,4},{12,0},{1,13},{5,9},{9,5},{13,1},{2,14},{6,10},... | collective-permute-start | bytes 12296 | tf_op jit(solution)/shard_map/ppermute | solution.py:22
  65.8 5.3 %collective-permute-start.1 = (f32[8,128]{1,0:T(8,128)S(1)}, f32[8,128]{1,0:T(8,128)S(1)}, u32[]{:S(2)}, u32[]{:S(2)}) collective-permute-start(f32[8,128]{1,0:T(8,128)S(1)} %pad_add_fusion), channel_id=1, source_target_pairs={{0,4},{4,0},{8,12},{12,8},{1,5},{5,1},{9,13},{13,9},{2,6},{6,2},{1... | collective-permute-start | bytes 12296 | tf_op jit(solution)/shard_map/ppermute | solution.py:22
  67.6 5.2 %collective-permute-start.12 = (f32[8,128]{1,0:T(8,128)S(1)}, f32[8,128]{1,0:T(8,128)S(1)}, u32[]{:S(2)}, u32[]{:S(2)}) collective-permute-start(f32[8,128]{1,0:T(8,128)S(1)} %add.78), channel_id=1, source_target_pairs={{0,8},{4,12},{8,0},{12,4},{1,9},{5,13},{9,1},{13,5},{2,10},{6,14},... | collective-permute-start | bytes 12296 | tf_op jit(solution)/shard_map/ppermute | solution.py:22
  68.6 12.1 %collective-permute-start.14 = (f32[4,3,64,128]{3,2,1,0:T(8,128)S(1)}, f32[4,3,64,128]{3,2,1,0:T(8,128)S(1)}, u32[]{:S(2)}, u32[]{:S(2)}) collective-permute-start(f32[4,3,64,128]{3,2,1,0:T(8,128)S(1)} %get-tuple-element.55.rest_0_), channel_id=1, source_target_pairs={{0,2},{2,0},{1,3},{3,1},{4,6},{6,4},{5,7},{7,5},{8,10},{10,8},{9,1... | collective-permute-start | bytes 1179656 | tf_op jit(solution)/shard_map/ppermute | solution.py:22
  69.1 19.9 %collective-permute-start.15 = (f32[4,3,64,128]{3,2,1,0:T(8,128)S(1)}, f32[4,3,64,128]{3,2,1,0:T(8,128)S(1)}, u32[]{:S(2)}, u32[]{:S(2)}) collective-permute-start(f32[4,3,64,128]{3,2,1,0:T(8,128)S(1)} %get-tuple-element.56.rest_2_), channel_id=1, source_target_pairs={{0,2},{2,0},{1,3},{3,1},{4,6},{6,4},{5,7},{7,5},{8,10},{10,8},{9,1... | collective-permute-start | bytes 1179656 | tf_op jit(solution)/shard_map/ppermute | solution.py:22
  70.6 26.9 %collective-permute-start.16 = (f32[4,3,64,128]{3,2,1,0:T(8,128)S(1)}, f32[4,3,64,128]{3,2,1,0:T(8,128)S(1)}, u32[]{:S(2)}, u32[]{:S(2)}) collective-permute-start(f32[4,3,64,128]{3,2,1,0:T(8,128)S(1)} %get-tuple-element.57.rest_4_), channel_id=1, source_target_pairs={{0,2},{2,0},{1,3},{3,1},{4,6},{6,4},{5,7},{7,5},{8,10},{10,8},{9,1... | collective-permute-start | bytes 1179656 | tf_op jit(solution)/shard_map/ppermute | solution.py:22
  71.1 5.4 %collective-permute-start.13 = (f32[8,128]{1,0:T(8,128)S(1)}, f32[8,128]{1,0:T(8,128)S(1)}, u32[]{:S(2)}, u32[]{:S(2)}) collective-permute-start(f32[8,128]{1,0:T(8,128)S(1)} %add.78), channel_id=1, source_target_pairs={{0,12},{4,8},{8,4},{12,0},{1,13},{5,9},{9,5},{13,1},{2,14},{6,10},... | collective-permute-start | bytes 12296 | tf_op jit(solution)/shard_map/ppermute | solution.py:22
  72.8 5.3 %collective-permute-start.11 = (f32[8,128]{1,0:T(8,128)S(1)}, f32[8,128]{1,0:T(8,128)S(1)}, u32[]{:S(2)}, u32[]{:S(2)}) collective-permute-start(f32[8,128]{1,0:T(8,128)S(1)} %add.78), channel_id=1, source_target_pairs={{0,4},{4,0},{8,12},{12,8},{1,5},{5,1},{9,13},{13,9},{2,6},{6,2},{1... | collective-permute-start | bytes 12296 | tf_op jit(solution)/shard_map/ppermute | solution.py:22
  76.5 25.1 %collective-permute-start.17 = (f32[2,3,64,128]{3,2,1,0:T(8,128)S(1)}, f32[2,3,64,128]{3,2,1,0:T(8,128)S(1)}, u32[]{:S(2)}, u32[]{:S(2)}) collective-permute-start(f32[2,3,64,128]{3,2,1,0:T(8,128)S(1)} %get-tuple-element.58.rest_6_), channel_id=1, source_target_pairs={{0,2},{2,0},{1,3},{3,1},{4,6},{6,4},{5,7},{7,5},{8,10},{10,8},{9,1... | collective-permute-start | bytes 589832 | tf_op jit(solution)/shard_map/ppermute | solution.py:22
  78.0 25.9 %collective-permute-start.18 = (f32[2,3,64,128]{3,2,1,0:T(8,128)S(1)}, f32[2,3,64,128]{3,2,1,0:T(8,128)S(1)}, u32[]{:S(2)}, u32[]{:S(2)}) collective-permute-start(f32[2,3,64,128]{3,2,1,0:T(8,128)S(1)} %get-tuple-element.59.rest_8_), channel_id=1, source_target_pairs={{0,2},{2,0},{1,3},{3,1},{4,6},{6,4},{5,7},{7,5},{8,10},{10,8},{9,1... | collective-permute-start | bytes 589832 | tf_op jit(solution)/shard_map/ppermute | solution.py:22
  106.0 3.5 %collective-permute-start.23 = (f32[16,3,64,128]{3,2,1,0:T(8,128)S(1)}, f32[16,3,64,128]{3,2,1,0:T(8,128)S(1)}, u32[]{:S(2)}, u32[]{:S(2)}) collective-permute-start(f32[16,3,64,128]{3,2,1,0:T(8,128)S(1)} %get-tuple-element.61.own_ref.vector_ref.raw_ref), channel_id=1, source_target_pairs={{0,1},{1,0},{2,3},{3,2},{4,5},{5,4},{6,7},{7,6},{8,9},{9,8},{10,11... | collective-permute-start | bytes 4718600 | tf_op jit(solution)/shard_map/ppermute | solution.py:374
  123.8 13.7 %collective-permute-start.24 = (f32[4,3,64,128]{3,2,1,0:T(8,128)S(1)}, f32[4,3,64,128]{3,2,1,0:T(8,128)S(1)}, u32[]{:S(2)}, u32[]{:S(2)}) collective-permute-start(f32[4,3,64,128]{3,2,1,0:T(8,128)S(1)} %get-tuple-element.68), channel_id=1, source_target_pairs={{0,12},{4,0},{8,4},{12,8},{1,13},{5,1},{9,5},{13,9},{2,14},{6,2},{... | collective-permute-start | bytes 1179656 | tf_op jit(solution)/shard_map/ppermute | solution.py:390
  125.4 20.0 %collective-permute-start.27 = (f32[4,3,64,128]{3,2,1,0:T(8,128)S(1)}, f32[4,3,64,128]{3,2,1,0:T(8,128)S(1)}, u32[]{:S(2)}, u32[]{:S(2)}) collective-permute-start(f32[4,3,64,128]{3,2,1,0:T(8,128)S(1)} %get-tuple-element.71), channel_id=1, source_target_pairs={{0,4},{4,8},{8,12},{12,0},{1,5},{5,9},{9,13},{13,1},{2,6},{6,10},{... | collective-permute-start | bytes 1179656 | tf_op jit(solution)/shard_map/ppermute | solution.py:390
  125.8 1.2 collective-permute-start.19
  127.0 31.2 %collective-permute-start.21 = (f32[8,128]{1,0:T(8,128)S(1)}, f32[8,128]{1,0:T(8,128)S(1)}, u32[]{:S(2)}, u32[]{:S(2)}) collective-permute-start(f32[8,128]{1,0:T(8,128)S(1)} %add.82), channel_id=1, source_target_pairs={{0,8},{4,12},{8,0},{12,4},{1,9},{5,13},{9,1},{13,5},{2,10},{6,14},... | collective-permute-start | bytes 12296 | tf_op jit(solution)/shard_map/ppermute | solution.py:22
  137.5 21.4 %collective-permute-start.25 = (f32[2,3,64,128]{3,2,1,0:T(8,128)S(1)}, f32[2,3,64,128]{3,2,1,0:T(8,128)S(1)}, u32[]{:S(2)}, u32[]{:S(2)}) collective-permute-start(f32[2,3,64,128]{3,2,1,0:T(8,128)S(1)} %get-tuple-element.69), channel_id=1, source_target_pairs={{0,8},{4,12},{8,0},{12,4},{1,9},{5,13},{9,1},{13,5},{2,10},{6,14},... | collective-permute-start | bytes 589832 | tf_op jit(solution)/shard_map/ppermute | solution.py:390
  145.4 16.1 %collective-permute-start.28 = (f32[2,3,64,128]{3,2,1,0:T(8,128)S(1)}, f32[2,3,64,128]{3,2,1,0:T(8,128)S(1)}, u32[]{:S(2)}, u32[]{:S(2)}) collective-permute-start(f32[2,3,64,128]{3,2,1,0:T(8,128)S(1)} %get-tuple-element.72), channel_id=1, source_target_pairs={{0,8},{4,12},{8,0},{12,4},{1,9},{5,13},{9,1},{13,5},{2,10},{6,14},... | collective-permute-start | bytes 589832 | tf_op jit(solution)/shard_map/ppermute | solution.py:390
  154.7 18.1 %collective-permute-start.32 = (f32[4,3,64,128]{3,2,1,0:T(8,128)S(1)}, f32[4,3,64,128]{3,2,1,0:T(8,128)S(1)}, u32[]{:S(2)}, u32[]{:S(2)}) collective-permute-start(f32[4,3,64,128]{3,2,1,0:T(8,128)S(1)} %combine.19.mine_ref), channel_id=1, source_target_pairs={{0,2},{2,0},{1,3},{3,1},{4,6},{6,4},{5,7},{7,5},{8,10},{10,8},{9,1... | collective-permute-start | bytes 1179656 | tf_op jit(solution)/shard_map/ppermute | solution.py:22
  156.0 19.2 %collective-permute-start.31 = (f32[4,3,64,128]{3,2,1,0:T(8,128)S(1)}, f32[4,3,64,128]{3,2,1,0:T(8,128)S(1)}, u32[]{:S(2)}, u32[]{:S(2)}) collective-permute-start(f32[4,3,64,128]{3,2,1,0:T(8,128)S(1)} %combine.18.mine_ref), channel_id=1, source_target_pairs={{0,2},{2,0},{1,3},{3,1},{4,6},{6,4},{5,7},{7,5},{8,10},{10,8},{9,1... | collective-permute-start | bytes 1179656 | tf_op jit(solution)/shard_map/ppermute | solution.py:22
  158.2 25.4 %collective-permute-start.30 = (f32[4,3,64,128]{3,2,1,0:T(8,128)S(1)}, f32[4,3,64,128]{3,2,1,0:T(8,128)S(1)}, u32[]{:S(2)}, u32[]{:S(2)}) collective-permute-start(f32[4,3,64,128]{3,2,1,0:T(8,128)S(1)} %combine.17.mine_ref), channel_id=1, source_target_pairs={{0,2},{2,0},{1,3},{3,1},{4,6},{6,4},{5,7},{7,5},{8,10},{10,8},{9,1... | collective-permute-start | bytes 1179656 | tf_op jit(solution)/shard_map/ppermute | solution.py:22
  158.9 5.4 %collective-permute-start.22 = (f32[8,128]{1,0:T(8,128)S(1)}, f32[8,128]{1,0:T(8,128)S(1)}, u32[]{:S(2)}, u32[]{:S(2)}) collective-permute-start(f32[8,128]{1,0:T(8,128)S(1)} %add.82), channel_id=1, source_target_pairs={{0,12},{4,8},{8,4},{12,0},{1,13},{5,9},{9,5},{13,1},{2,14},{6,10},... | collective-permute-start | bytes 12296 | tf_op jit(solution)/shard_map/ppermute | solution.py:22
  161.5 4.2 %collective-permute-start.20 = (f32[8,128]{1,0:T(8,128)S(1)}, f32[8,128]{1,0:T(8,128)S(1)}, u32[]{:S(2)}, u32[]{:S(2)}) collective-permute-start(f32[8,128]{1,0:T(8,128)S(1)} %add.82), channel_id=1, source_target_pairs={{0,4},{4,0},{8,12},{12,8},{1,5},{5,1},{9,13},{13,9},{2,6},{6,2},{1... | collective-permute-start | bytes 12296 | tf_op jit(solution)/shard_map/ppermute | solution.py:22
  164.3 26.2 %collective-permute-start.26 = (f32[2,3,64,128]{3,2,1,0:T(8,128)S(1)}, f32[2,3,64,128]{3,2,1,0:T(8,128)S(1)}, u32[]{:S(2)}, u32[]{:S(2)}) collective-permute-start(f32[2,3,64,128]{3,2,1,0:T(8,128)S(1)} %combine.15.mine_ref), channel_id=1, source_target_pairs={{0,2},{2,0},{1,3},{3,1},{4,6},{6,4},{5,7},{7,5},{8,10},{10,8},{9,1... | collective-permute-start | bytes 589832 | tf_op jit(solution)/shard_map/ppermute | solution.py:22
  165.7 23.3 %collective-permute-start.29 = (f32[2,3,64,128]{3,2,1,0:T(8,128)S(1)}, f32[2,3,64,128]{3,2,1,0:T(8,128)S(1)}, u32[]{:S(2)}, u32[]{:S(2)}) collective-permute-start(f32[2,3,64,128]{3,2,1,0:T(8,128)S(1)} %combine.16.mine_ref), channel_id=1, source_target_pairs={{0,2},{2,0},{1,3},{3,1},{4,6},{6,4},{5,7},{7,5},{8,10},{10,8},{9,1... | collective-permute-start | bytes 589832 | tf_op jit(solution)/shard_map/ppermute | solution.py:22

commit v2 on v1

v2 whole, which is shorter than its diff:
```python
import functools

import jax
import jax.numpy as jnp
from jax import lax
from jax.experimental import pallas as pl
from jax.experimental.pallas import tpu as pltpu
from jax.sharding import PartitionSpec as P

LIMIT = 48 * 1024 * 1024
SMALL = 24 * 1024 * 1024
FREE = pl.CostEstimate(flops=0, bytes_accessed=0, transcendentals=0)
WHOLE = pl.BlockSpec(memory_space=pltpu.VMEM)
SCALARS = pl.BlockSpec(memory_space=pltpu.SMEM)
ANY = pl.BlockSpec(memory_space=pl.ANY)


def power_of_two(size):
    return size & (size - 1) == 0


def flip(value, axis, bit):
    size = lax.axis_size(axis)
    return lax.ppermute(value, axis, [(i, i ^ bit) for i in range(size)])


def small_sum(value, axis):
    size = lax.axis_size(axis)
    if not power_of_two(size):
        return lax.psum(value, axis)
    if size == 4:
        one, two, three = (flip(value, axis, bit) for bit in (1, 2, 3))
        return (value + one) + (two + three)
    bit = 1
    while bit < size:
        value = value + flip(value, axis, bit)
        bit *= 2
    return value


def halves(value):
    high = value.astype(jnp.bfloat16)
    low = (value - high.astype(jnp.float32)).astype(jnp.bfloat16)
    return high, low


def table_kernel(devices, partner_ref, kind_ref, table_ref, used):
    count, terms = partner_ref.shape[0], kind_ref.shape[0]
    per = count // devices
    me = lax.axis_index("blk")
    for c in range(devices):
        used[c] = 0

    def place(j, carry):
        where_to = partner_ref[j]
        owner = lax.div(where_to, count)
        offset = lax.rem(owner - me + devices, devices)
        at = offset * per + used[offset]
        used[offset] = used[offset] + 1
        table_ref[at] = j
        table_ref[count + at] = where_to - owner * count
        table_ref[2 * count + j] = at
        return carry

    lax.fori_loop(0, count, place, 0)
    for k in range(terms):
        table_ref[3 * count + k] = kind_ref[k]
    table_ref[3 * count + terms] = lax.axis_index("sub")


def make_table(partner, term_kind):
    devices = lax.axis_size("blk")
    length = 3 * partner.shape[0] + term_kind.shape[0] + 1
    return pl.pallas_call(
        functools.partial(table_kernel, devices),
        out_shape=jax.ShapeDtypeStruct((length,), jnp.int32),
        in_specs=[SCALARS, SCALARS],
        out_specs=SCALARS,
        scratch_shapes=[pltpu.SMEM((devices,), jnp.int32)],
    )(partner, term_kind)


def sector(table, count, terms, l_ref, r_ref, own_ref, other_ref, lhs, high_rhs, low_rhs):
    roots, rows, width = own_ref.shape[1:]
    first = table[3 * count + terms] == 0
    own, other = own_ref[0], other_ref[0]
    top = jnp.where(first, own, other)
    bottom = jnp.where(first, other, own)
    left = l_ref[:, 0].reshape(terms * rows, 2 * rows)
    left = jnp.concatenate(halves(left), axis=1)
    for r in range(roots):
        wide = jnp.concatenate(halves(jnp.concatenate([top[r], bottom[r]], axis=0)), axis=1)
        both = jnp.dot(
            left, jnp.concatenate([wide, wide], axis=0), preferred_element_type=jnp.float32
        )
        high, low = halves(both[:, :width] + both[:, width:])
        for k in range(terms):
            lanes = slice(k * width, (k + 1) * width)
            part = slice(k * rows, (k + 1) * rows)
            lhs[r * rows : (r + 1) * rows, lanes] = high[part]
            lhs[(roots + r) * rows : (roots + r + 1) * rows, lanes] = low[part]
    for k in range(terms):
        lanes = slice(k * width, (k + 1) * width)
        kind = table[3 * count + k]
        used = pl.ds(pl.multiple_of((1 - kind) * width, width), width)
        high, low = halves(r_ref[k, 0])
        high_rhs[used, lanes] = high
        low_rhs[used, lanes] = low
    dims = (((1,), (1,)), ((), ()))
    tall = lax.dot_general(lhs[...], high_rhs[...], dims, preferred_element_type=jnp.float32)
    short = lax.dot_general(
        lhs[: roots * rows], low_rhs[...], dims, preferred_element_type=jnp.float32
    )
    result = tall[: roots * rows] + tall[roots * rows :] + short
    return result.reshape(roots, rows, 2 * width)


def sector_kernel(count, terms, unroll, starts, table, *refs):
    inputs, scratch = refs[: 4 * unroll], refs[-3 * unroll :]
    outputs = refs[-3 * unroll - len(starts) : -3 * unroll]
    moved_refs, kept_ref = outputs[:-1], outputs[-1]
    width = kept_ref.shape[3]
    step = pl.program_id(0)

    @pl.when(step == 0)
    def _():
        for ref in scratch:
            if ref.shape[0] == 2 * width:
                ref[...] = jnp.zeros_like(ref)

    results = [
        sector(table, count, terms, *inputs[4 * u : 4 * u + 4], *scratch[3 * u : 3 * u + 3])
        for u in range(unroll)
    ]
    for u in range(unroll):
        kept_ref[u] = results[u][:, :, width:]
    for ref, begin, end in zip(moved_refs, starts, starts[1:]):

        @pl.when((step >= begin) & (step < end))
        def _(ref=ref):
            for u in range(unroll):
                ref[u] = results[u][:, :, :width]


def sectors(table, pieces, left, right, own, other, kept, ordered):
    terms, count, rows, _ = left.shape
    roots, width = own.shape[1], own.shape[3]
    unroll = 2 if all(base % 2 == 0 and size % 2 == 0 for base, size in pieces) else 1
    starts = [0]
    for _, size in pieces:
        starts.append(starts[-1] + size // unroll)

    def place(i):
        at = pieces[0][0] // unroll + i
        for begin, (base, _) in zip(starts[1:], pieces[1:]):
            at = jnp.where(i >= begin, base // unroll + i - begin, at)
        return at

    def specs(u):
        def source(i, table):
            return table[unroll * place(i) + u]

        def held(i, table):
            return (unroll * place(i) + u if ordered else source(i, table), 0, 0, 0)

        return [
            pl.BlockSpec((terms, 1, rows, 2 * rows), lambda i, t: (0, source(i, t), 0, 0)),
            pl.BlockSpec((terms, 1, width, width), lambda i, t: (0, source(i, t), 0, 0)),
            pl.BlockSpec((1, roots, rows, width), held),
            pl.BlockSpec((1, roots, rows, width), held),
        ]

    def moved_spec(begin, end):
        return pl.BlockSpec(block, lambda i, t: (jnp.clip(i - begin, 0, end - begin - 1), 0, 0, 0))

    block = (unroll, roots, rows, width)
    in_specs = [spec for u in range(unroll) for spec in specs(u)]
    args = [left, right, own, other] * unroll
    aliases = {}
    if kept is not None:
        in_specs.append(ANY)
        args.append(kept)
        aliases = {4 * unroll + 1: len(pieces)}
    out = pl.pallas_call(
        functools.partial(sector_kernel, count, terms, unroll, starts),
        out_shape=[
            jax.ShapeDtypeStruct((size,) + block[1:], jnp.float32)
            for size in [size for _, size in pieces] + [count]
        ],
        grid_spec=pltpu.PrefetchScalarGridSpec(
            num_scalar_prefetch=1,
            grid=(starts[-1],),
            in_specs=in_specs,
            out_specs=[moved_spec(begin, end) for begin, end in zip(starts, starts[1:])]
            + [pl.BlockSpec(block, lambda i, t: (place(i), 0, 0, 0))],
            scratch_shapes=[
                pltpu.VMEM((2 * roots * rows, terms * width), jnp.bfloat16),
                pltpu.VMEM((2 * width, terms * width), jnp.bfloat16),
                pltpu.VMEM((2 * width, terms * width), jnp.bfloat16),
            ]
            * unroll,
        ),
        input_output_aliases=aliases,
        compiler_params=pltpu.CompilerParams(vmem_limit_bytes=LIMIT),
        cost_estimate=FREE,
        name="sectors",
    )(table, *args)
    return out[:-1], out[-1]


def gather_kernel(share, with_inner, table, kept_ref, arrived_ref, vector_ref, diag_ref, sum_ref, *rest):
    vector = vector_ref[0]
    total = kept_ref[0] + arrived_ref[0] + (share * diag_ref[0])[None] * vector
    sum_ref[0] = total
    if with_inner:
        inner_ref = rest[0]
        roots = vector.shape[0]

        @pl.when(pl.program_id(0) == 0)
        def _():
            inner_ref[...] = jnp.zeros_like(inner_ref)

        for r in range(roots):
            inner_ref[r : r + 1] += jnp.sum(vector[r] * total[r], axis=0, keepdims=True)
            inner_ref[roots + r : roots + r + 1] += share * jnp.sum(
                vector[r] * vector[r], axis=0, keepdims=True
            )


def combine(table, base, size, kept, arrived, vector, diag, share, ordered, with_inner):
    count, roots, rows, width = kept.shape
    block = (1, roots, rows, width)

    def slot(i, table):
        return table[count + base + i]

    def place(i, table):
        return table[2 * count + slot(i, table)]

    def held(i, table):
        return place(i, table) if ordered else slot(i, table)

    out_shape = [jax.ShapeDtypeStruct((size,) + block[1:], jnp.float32)]
    out_specs = [pl.BlockSpec(block, lambda i, t: (i, 0, 0, 0))]
    if with_inner:
        out_shape.append(jax.ShapeDtypeStruct((8, width), jnp.float32))
        out_specs.append(pl.BlockSpec((8, width), lambda i, t: (0, 0)))
    out = pl.pallas_call(
        functools.partial(gather_kernel, share, with_inner),
        out_shape=out_shape,
        grid_spec=pltpu.PrefetchScalarGridSpec(
            num_scalar_prefetch=1,
            grid=(size,),
            in_specs=[
                pl.BlockSpec(block, lambda i, t: (place(i, t), 0, 0, 0)),
                pl.BlockSpec(block, lambda i, t: (i, 0, 0, 0)),
                pl.BlockSpec(block, lambda i, t: (held(i, t), 0, 0, 0)),
                pl.BlockSpec((1, rows, width), lambda i, t: (slot(i, t), 0, 0)),
            ],
            out_specs=out_specs,
        ),
        compiler_params=pltpu.CompilerParams(vmem_limit_bytes=SMALL),
        cost_estimate=FREE,
        name="combine",
    )(table, kept, arrived, vector, diag)
    return out if with_inner else (out[0], None)


def correct_kernel(pieces, table, inner_ref, vector_ref, diag_ref, *rest):
    parts, (raw_ref, squares_ref) = rest[:-2], rest[-2:]
    count, roots, rows, width = vector_ref.shape
    inner = jnp.sum(inner_ref[...], axis=1, keepdims=True)
    theta = inner[:roots] / inner[roots : 2 * roots]
    squares = [jnp.zeros((1, width), jnp.float32) for _ in range(roots)]
    for piece, (base, size) in enumerate(pieces):
        mine, theirs = parts[2 * piece], parts[2 * piece + 1]
        for i in range(size):
            slot = table[count + base + i]
            place = table[2 * count + slot]
            diag = diag_ref[slot]
            for r in range(roots):
                shift = theta[r : r + 1]
                sigma = mine[i, r] + theirs[i, r]
                raw = (sigma - shift * vector_ref[slot, r]) / jnp.maximum(jnp.abs(diag - shift), 1.0)
                raw_ref[place, r] = raw
                squares[r] = squares[r] + jnp.sum(raw * raw, axis=0, keepdims=True)
    squares_ref[...] = jnp.zeros_like(squares_ref)
    for r in range(roots):
        squares_ref[r : r + 1] = squares[r]


def correct(table, pieces, inner, vector, diag, parts):
    return pl.pallas_call(
        functools.partial(correct_kernel, pieces),
        out_shape=[
            jax.ShapeDtypeStruct(vector.shape, jnp.float32),
            jax.ShapeDtypeStruct(inner.shape, jnp.float32),
        ],
        in_specs=[SCALARS] + [WHOLE] * (3 + len(parts)),
        out_specs=[WHOLE, WHOLE],
        compiler_params=pltpu.CompilerParams(vmem_limit_bytes=SMALL),
        cost_estimate=FREE,
        name="correct",
    )(table, inner, vector, diag, *parts)


def scaled_kernel(table, scale_ref, raw_ref, out_ref):
    for r in range(raw_ref.shape[1]):
        out_ref[0, r] = raw_ref[0, r] * scale_ref[r : r + 1]


def scaled(table, scale, raw):
    slots, roots, rows, width = raw.shape
    block = (1, roots, rows, width)
    return pl.pallas_call(
        scaled_kernel,
        out_shape=jax.ShapeDtypeStruct(raw.shape, jnp.float32),
        grid_spec=pltpu.PrefetchScalarGridSpec(
            num_scalar_prefetch=1,
            grid=(slots,),
            in_specs=[
                pl.BlockSpec(scale.shape, lambda i, t: (0, 0)),
                pl.BlockSpec(block, lambda i, t: (t[2 * slots + i], 0, 0, 0)),
            ],
            out_specs=pl.BlockSpec(block, lambda i, t: (i, 0, 0, 0)),
        ),
        compiler_params=pltpu.CompilerParams(vmem_limit_bytes=SMALL),
        cost_estimate=FREE,
        name="scaled",
    )(table, scale, raw)


def finish_kernel(table, scale_ref, mine_ref, theirs_ref, *rest):
    out_ref = rest[-1]
    for r in range(mine_ref.shape[1]):
        out_ref[0, r] = (mine_ref[0, r] + theirs_ref[0, r]) * scale_ref[r : r + 1]


def finish(table, base, scale, mine, theirs, out, slots):
    size, roots, rows, width = mine.shape
    block = (1, roots, rows, width)
    in_specs = [
        pl.BlockSpec(scale.shape, lambda i, t: (0, 0)),
        pl.BlockSpec(block, lambda i, t: (i, 0, 0, 0)),
        pl.BlockSpec(block, lambda i, t: (i, 0, 0, 0)),
    ]
    args, aliases = [scale, mine, theirs], {}
    if out is not None:
        in_specs.append(ANY)
        args.append(out)
        aliases = {4: 0}
    return pl.pallas_call(
        finish_kernel,
        out_shape=jax.ShapeDtypeStruct((slots,) + block[1:], jnp.float32),
        grid_spec=pltpu.PrefetchScalarGridSpec(
            num_scalar_prefetch=1,
            grid=(size,),
            in_specs=in_specs,
            out_specs=pl.BlockSpec(block, lambda i, t: (t[slots + base + i], 0, 0, 0)),
        ),
        input_output_aliases=aliases,
        compiler_params=pltpu.CompilerParams(vmem_limit_bytes=SMALL),
        cost_estimate=FREE,
        name="finish",
    )(table, *args)


def add_over_term(value):
    size = lax.axis_size("term")
    if size == 1 or not power_of_two(size):
        return lax.psum(value, "term"), jnp.zeros_like(value)
    bit = 1
    while 2 * bit < size:
        value = value + flip(value, "term", bit)
        bit *= 2
    return value, flip(value, "term", bit)


def shards(amplitudes, left, right, term_kind, partner, left_diag, right_diag):
    devices, terms_over = lax.axis_size("blk"), lax.axis_size("term")
    vector = jnp.transpose(amplitudes, (0, 2, 1, 3))
    slots, roots, rows, width = vector.shape
    per = slots // devices
    count = slots * devices * rows * lax.axis_size("sub") * width
    table = make_table(partner, term_kind)
    diag = left_diag[:, :, None] + right_diag[:, None, :]

    cuts = [(0, per // 2), (per // 2, per - per // 2)] if per > 1 else [(0, per)]
    moving = []
    for c in range(1, (devices + 1) // 2):
        for start, size in cuts:
            moving += [(c, c * per + start, size), (devices - c, (devices - c) * per + start, size)]
    if devices % 2 == 0 and devices > 1:
        c = devices // 2
        moving += [(c, c * per + start, size) for start, size in cuts]
    order = [(0, 0, per)] + moving
    spans = [(base, size) for _, base, size in order]
    batches = [order[1:3], order[3:] + order[:1]]

    def after(value, *others):
        return lax.optimization_barrier((value,) + others)[0]

    def relay(value, c):
        return lax.ppermute(value, "blk", [(p, (p + c) % devices) for p in range(devices)])

    def partials(own, ordered, with_inner):
        other = lax.ppermute(own, "sub", [(0, 1), (1, 0)])
        kept, outgoing = None, {}
        for batch in batches:
            if batch:
                parts, kept = sectors(
                    table, [piece[1:] for piece in batch], left, right, own, other, kept, ordered
                )
                outgoing.update(zip(batch, parts))
        sums, inners, arrivals, exchanged = [], [], [], []
        for piece in order:
            c, base, size = piece
            arrived = outgoing[piece]
            if not c:
                early = []
                for first in batches[0]:
                    early.append(relay(outgoing[first], first[0]))
                arrived = after(arrived, *early)
                arrivals += early
            elif piece not in batches[0]:
                arrived = relay(after(arrived, arrivals[-2]), c)
                arrivals.append(arrived)
            else:
                arrived = arrivals[batches[0].index(piece)]
            mine, inner = combine(
                table, base, size, kept, arrived, own, diag, 1.0 / terms_over, ordered, with_inner
            )
            if len(exchanged) >= 2:
                mine = after(mine, exchanged[-2])
            mine, theirs = add_over_term(mine)
            sums += [mine, theirs]
            exchanged.append(theirs)
            inners.append(inner)
        return sums, inners, kept, exchanged

    sums, inners, _, exchanged = partials(vector, False, True)
    inner = sum(inners[1:], inners[0])
    if len(exchanged) >= 4:
        inner = after(inner, exchanged[-3])
    inner = small_sum(small_sum(inner, ("term", "sub")), "blk")
    raw, squares = correct(table, spans, inner, vector, diag, sums)
    sums, _, kept, _ = partials(raw, True, False)
    squares = small_sum(small_sum(after(squares, kept), "sub"), "blk")
    scale = lax.rsqrt(jnp.sum(squares, axis=1, keepdims=True) / count + 1e-06)
    scale = jnp.broadcast_to(scale, squares.shape)
    correction = scaled(table, scale, raw)
    sigma = None
    for piece, (base, size) in enumerate(spans):
        sigma = finish(
            table, base, scale, sums[2 * piece], sums[2 * piece + 1], sigma, slots
        )
    return jnp.transpose(sigma, (0, 2, 1, 3)), jnp.transpose(correction, (0, 2, 1, 3))


def solution(mesh):
    return jax.shard_map(
        shards,
        mesh=mesh,
        in_specs=(
            P(("grp", "blk"), "sub", None, None),
            P(("grp", "term"), "blk", "sub", None),
            P(("grp", "term"), "blk", None, None),
            P(("grp", "term")),
            P(("grp", "blk")),
            P(("grp", "blk"), "sub"),
            P(("grp", "blk"), None),
        ),
        out_specs=(P(("grp", "blk"), "sub", None, None), P(("grp", "blk"), "sub", None, None)),
        check_vma=False,
    )
```

time: 192 us -> 170 us (0.89)
  Pallas kernels: 86.5 us -> 61.7 us
  starting transfers between devices: 34.5 us -> 56.8 us
  waiting for transfers between devices: 67.4 us -> 48.4 us
    pallas_call x16 -> x12, Pallas kernels: 75.9 us -> 49.6 us  [the longest x4 34.4 us: sectors(): pl.pallas_call(functools.partial(sector_kernel, count, terms, unroll, sta...]
    ppermute x23 -> x24, waiting for transfers between devices: 41.4 us -> 28.2 us  [flip(): return lax.ppermute(value, axis, [(i, i ^ bit) for i in range(size)])]
    ppermute x23 -> x24, starting transfers between devices: 21.5 us -> 33.9 us  [flip(): return lax.ppermute(value, axis, [(i, i ^ bit) for i in range(size)])]
    ppermute x10 -> x14, starting transfers between devices: 13 us -> 22.9 us  [the longest x12 22.3 us: relay(): lax.ppermute(value, 'blk', [(p, (p + c) % devices) for p in range(devices)])]
    ppermute x10 -> x14, waiting for transfers between devices: 26 us -> 20.2 us  [the longest x12 15 us: relay(): lax.ppermute(value, 'blk', [(p, (p + c) % devices) for p in range(devices)])]
    pallas_call x10 -> x14, Pallas kernels: 6.92 us -> 9.3 us  [combine(): pl.pallas_call(functools.partial(gather_kernel, share, with_inner), out_s...]
  transfers between devices with their start and end apart: 33 -> 38, of which waited for: 20 -> 20; matrix products, arithmetic and copies ran while one was open for 0% -> 0% of each run, Pallas kernels for 28% -> 28%
where the time goes in v2:
time: 170 us
  Pallas kernels  61.7 us (36%)
  starting transfers between devices  56.8 us (33%)
  waiting for transfers between devices  48.4 us (28%)
  local copies, waits for them, and re-layouts  2.14 us (1%)
    pallas_call x4, Pallas kernels, sectors(): pl.pallas_call(functools.partial(sector_kernel, count, terms, unroll, sta...  34.4 us
    ppermute x24, starting transfers between devices, flip(): return lax.ppermute(value, axis, [(i, i ^ bit) for i in range(size)])  33.9 us
    ppermute x24, waiting for transfers between devices, flip(): return lax.ppermute(value, axis, [(i, i ^ bit) for i in range(size)])  28.2 us
    ppermute x12, starting transfers between devices, relay(): lax.ppermute(value, 'blk', [(p, (p + c) % devices) for p in range(devices)])  22.3 us
    ppermute x12, waiting for transfers between devices, relay(): lax.ppermute(value, 'blk', [(p, (p + c) % devices) for p in range(devices)])  15 us
    pallas_call x7, Pallas kernels, finish(): pl.pallas_call(finish_kernel, out_shape=jax.ShapeDtypeStruct((slots,) + b...  9.42 us
    pallas_call x14, Pallas kernels, combine(): pl.pallas_call(functools.partial(gather_kernel, share, with_inner), out_s...  9.3 us
    pallas_call x1, Pallas kernels, scaled(): pl.pallas_call(scaled_kernel, out_shape=jax.ShapeDtypeStruct(raw.shape, j...  5.78 us
  transfers between devices with their start and end apart: 38, of which 20 were waited for; matrix products, arithmetic and copies ran while one was open for 0% of the time, Pallas kernels for 28%

profile of v2, /device:TPU:0, one launch (start us, length us, event | category | flops | bytes accessed | tf_op | source)
XLA Modules:
  0.0 170.2 jit_solution(16223601799443559145)
XLA Ops:
  1.1 1.5 shard_map.86.table
  2.7 1.7 %collective-permute-done.refs_3_.refs_7_ = f32[16,3,64,128]{3,2,1,0:T(8,128)S(1)} collective-permute-done((f32[16,3,64,128]{3,2,1,0:T(8,128)}, f32[16,3,64,128]{3,2,1,0:T(8,128)S(1)}, u32[]{:S(2)}, u32[]{:S(2)}) %collective-permute-start) | collective-permute-done | bytes 1572896 | tf_op jit(solution)/shard_map/ppermute | solution.py:407
  4.4 1.4 copy-done
  6.5 5.3 %sectors.4 = (f32[2,3,64,128]{3,2,1,0:T(8,128)S(1)}, f32[2,3,64,128]{3,2,1,0:T(8,128)S(1)}, f32[16,3,64,128]{3,2,1,0:T(8,128)S(1)}) custom-call(s32[57]{0:T(128)S(1)} %copy-done.1, f32[8,16,64,128]{3,2,1,0:T(8,128)} %refs_4_.7, f32[8,16,128,128]{3,2,1,0:T(8,128)} %refs_5_.7, f32[16,3,64,128]{3,2,1,0:T(8,128)S(1)} %bitcast.4, ...), custom_call_target="tpu_custom_call" | custom-call | tf_op jit(solution)/shard_map/sectors/pallas_call | solution.py:184
  11.7 3.0 %collective-permute-start.1 = (f32[2,3,64,128]{3,2,1,0:T(8,128)S(1)}, f32[2,3,64,128]{3,2,1,0:T(8,128)S(1)}, u32[]{:S(2)}, u32[]{:S(2)}) collective-permute-start(f32[2,3,64,128]{3,2,1,0:T(8,128)S(1)} %get-tuple-element.61), channel_id=1, source_target_pairs={{0,4},{4,8},{8,12},{12,0},{1,5},{5,9},{9,13},{13,1},{2,6},{6,10},{... | collective-permute-start | bytes 589832 | tf_op jit(solution)/shard_map/ppermute | solution.py:404
  14.7 2.1 %collective-permute-start.2 = (f32[2,3,64,128]{3,2,1,0:T(8,128)S(1)}, f32[2,3,64,128]{3,2,1,0:T(8,128)S(1)}, u32[]{:S(2)}, u32[]{:S(2)}) collective-permute-start(f32[2,3,64,128]{3,2,1,0:T(8,128)S(1)} %get-tuple-element.62), channel_id=1, source_target_pairs={{0,12},{4,0},{8,4},{12,8},{1,13},{5,1},{9,5},{13,9},{2,14},{6,2},{... | collective-permute-start | bytes 589832 | tf_op jit(solution)/shard_map/ppermute | solution.py:404
  17.0 12.0 %sectors.5 = (f32[2,3,64,128]{3,2,1,0:T(8,128)S(1)}, f32[2,3,64,128]{3,2,1,0:T(8,128)S(1)}, f32[2,3,64,128]{3,2,1,0:T(8,128)S(1)}, f32[2,3,64,128]{3,2,1,0:T(8,1...) custom-call(s32[57]{0:T(128)S(1)} %copy-done.1, ...), custom_call_target="tpu_custom_call", output_to_operand_aliasing={{5}: (9, {})} | custom-call | tf_op jit(solution)/shard_map/sectors/pallas_call | solution.py:184
  29.8 1.7 %collective-permute-start.7 = (f32[4,3,64,128]{3,2,1,0:T(8,128)S(1)}, f32[4,3,64,128]{3,2,1,0:T(8,128)S(1)}, u32[]{:S(2)}, u32[]{:S(2)}) collective-permute-start(f32[4,3,64,128]{3,2,1,0:T(8,128)S(1)} %get-tuple-element.81.rest_0_), channel_id=1, source_target_pairs={{0,2},{2,0},{1,3},{3,1},{4,6},{6,4},{5,7},{7,5},{8,10},{10,8},{9,1... | collective-permute-start | bytes 1179656 | tf_op jit(solution)/shard_map/ppermute | solution.py:24
  31.6 3.8 %collective-permute-start.4 = (f32[2,3,64,128]{3,2,1,0:T(8,128)S(1)}, f32[2,3,64,128]{3,2,1,0:T(8,128)S(1)}, u32[]{:S(2)}, u32[]{:S(2)}) collective-permute-start(f32[2,3,64,128]{3,2,1,0:T(8,128)S(1)} %get-tuple-element.71), channel_id=1, source_target_pairs={{0,12},{4,0},{8,4},{12,8},{1,13},{5,1},{9,5},{13,9},{2,14},{6,2},{... | collective-permute-start | bytes 589832 | tf_op jit(solution)/shard_map/ppermute | solution.py:404
  36.1 5.1 %collective-permute-done.3.arrived_ref = f32[2,3,64,128]{3,2,1,0:T(8,128)S(1)} collective-permute-done((f32[2,3,64,128]{3,2,1,0:T(8,128)S(1)}, f32[2,3,64,128]{3,2,1,0:T(8,128)S(1)}, u32[]{:S(2)}, u32[]{:S(2)}) %collective-permute-start.3) | collective-permute-done | bytes 196640 | tf_op jit(solution)/shard_map/ppermute | solution.py:404
  42.3 3.7 %collective-permute-start.6 = (f32[2,3,64,128]{3,2,1,0:T(8,128)S(1)}, f32[2,3,64,128]{3,2,1,0:T(8,128)S(1)}, u32[]{:S(2)}, u32[]{:S(2)}) collective-permute-start(f32[2,3,64,128]{3,2,1,0:T(8,128)S(1)} %get-tuple-element.77), channel_id=1, source_target_pairs={{0,8},{4,12},{8,0},{12,4},{1,9},{5,13},{9,1},{13,5},{2,10},{6,14},... | collective-permute-start | bytes 589832 | tf_op jit(solution)/shard_map/ppermute | solution.py:404
  47.0 1.7 %collective-permute-start.16 = (f32[2,3,64,128]{3,2,1,0:T(8,128)S(1)}, f32[2,3,64,128]{3,2,1,0:T(8,128)S(1)}, u32[]{:S(2)}, u32[]{:S(2)}) collective-permute-start(f32[2,3,64,128]{3,2,1,0:T(8,128)S(1)} %get-tuple-element.85.rest_2_), channel_id=1, source_target_pairs={{0,2},{2,0},{1,3},{3,1},{4,6},{6,4},{5,7},{7,5},{8,10},{10,8},{9,1... | collective-permute-start | bytes 589832 | tf_op jit(solution)/shard_map/ppermute | solution.py:24
  50.1 6.5 %collective-permute-done.5.arrived_ref = f32[2,3,64,128]{3,2,1,0:T(8,128)S(1)} collective-permute-done((f32[2,3,64,128]{3,2,1,0:T(8,128)S(1)}, f32[2,3,64,128]{3,2,1,0:T(8,128)S(1)}, u32[]{:S(2)}, u32[]{:S(2)}) %collective-permute-start.5) | collective-permute-done | bytes 196640 | tf_op jit(solution)/shard_map/ppermute | solution.py:404
  57.3 1.9 %collective-permute-done.6.arrived_ref = f32[2,3,64,128]{3,2,1,0:T(8,128)S(1)} collective-permute-done((f32[2,3,64,128]{3,2,1,0:T(8,128)S(1)}, f32[2,3,64,128]{3,2,1,0:T(8,128)S(1)}, u32[]{:S(2)}, u32[]{:S(2)}) %collective-permute-start.6) | collective-permute-done | bytes 196640 | tf_op jit(solution)/shard_map/ppermute | solution.py:404
  60.5 5.1 %collective-permute-done.9.rest_9_ = f32[2,3,64,128]{3,2,1,0:T(8,128)S(1)} collective-permute-done((f32[2,3,64,128]{3,2,1,0:T(8,128)S(1)}, f32[2,3,64,128]{3,2,1,0:T(8,128)S(1)}, u32[]{:S(2)}, u32[]{:S(2)}) %collective-permute-start.9) | collective-permute-done | bytes 196640 | tf_op jit(solution)/shard_map/ppermute | solution.py:24
  66.2 1.3 collective-permute-start.10
  69.3 2.9 %collective-permute-start.15 = (f32[8,128]{1,0:T(8,128)S(1)}, f32[8,128]{1,0:T(8,128)S(1)}, u32[]{:S(2)}, u32[]{:S(2)}) collective-permute-start(f32[8,128]{1,0:T(8,128)S(1)} %add_add_fusion.1), channel_id=1, source_target_pairs={{0,12},{4,8},{8,4},{12,0},{1,13},{5,9},{9,5},{13,1},{2,14},{6,10},... | collective-permute-start | bytes 12296 | tf_op jit(solution)/shard_map/ppermute | solution.py:24
  72.2 1.5 collective-permute-start.13
  75.0 1.3 collective-permute-start.19
  76.7 5.4 %collective-permute-done.18.rest_11_ = f32[2,3,64,128]{3,2,1,0:T(8,128)S(1)} collective-permute-done((f32[2,3,64,128]{3,2,1,0:T(8,128)S(1)}, f32[2,3,64,128]{3,2,1,0:T(8,128)S(1)}, u32[]{:S(2)}, u32[]{:S(2)}) %collective-permute-start.18) | collective-permute-done | bytes 196640 | tf_op jit(solution)/shard_map/ppermute | solution.py:24
  82.2 2.3 %collective-permute-done.19.rest_13_ = f32[2,3,64,128]{3,2,1,0:T(8,128)S(1)} collective-permute-done((f32[2,3,64,128]{3,2,1,0:T(8,128)S(1)}, f32[2,3,64,128]{3,2,1,0:T(8,128)S(1)}, u32[]{:S(2)}, u32[]{:S(2)}) %collective-permute-start.19) | collective-permute-done | bytes 196640 | tf_op jit(solution)/shard_map/ppermute | solution.py:24
  84.5 1.2 correct.1
  85.8 3.4 %collective-permute-done.20.refs_3_.refs_7_ = f32[16,3,64,128]{3,2,1,0:T(8,128)S(1)} collective-permute-done((f32[16,3,64,128]{3,2,1,0:T(8,128)S(1)}, f32[16,3,64,128]{3,2,1,0:T(8,128)S(1)}, u32[]{:S(2)}, u32[]{:S(2)}) %collective-permute-start.20) | collective-permute-done | bytes 1572896 | tf_op jit(solution)/shard_map/ppermute | solution.py:407
  89.2 5.2 %sectors.6 = (f32[2,3,64,128]{3,2,1,0:T(8,128)S(1)}, f32[2,3,64,128]{3,2,1,0:T(8,128)S(1)}, f32[16,3,64,128]{3,2,1,0:T(8,128)S(1)}) custom-call(s32[57]{0:T(128)S(1)} %copy-done.1, f32[8,16,64,128]{3,2,1,0:T(8,128)} %refs_4_.7, f32[8,16,128,128]{3,2,1,0:T(8,128)} %refs_5_.7, f32[16,3,64,128]{3,2,1,0:T(8,128)S(1)} %get-tuple-element.93.refs_2_.refs_6_.vector_ref.raw_ref, ...), custom_call_target="tpu_custom_call" | custom-call | tf_op jit(solution)/shard_map/sectors/pallas_call | solution.py:184
  94.5 2.9 %collective-permute-start.25 = (f32[2,3,64,128]{3,2,1,0:T(8,128)S(1)}, f32[2,3,64,128]{3,2,1,0:T(8,128)S(1)}, u32[]{:S(2)}, u32[]{:S(2)}) collective-permute-start(f32[2,3,64,128]{3,2,1,0:T(8,128)S(1)} %get-tuple-element.99), channel_id=1, source_target_pairs={{0,12},{4,0},{8,4},{12,8},{1,13},{5,1},{9,5},{13,9},{2,14},{6,2},{... | collective-permute-start | bytes 589832 | tf_op jit(solution)/shard_map/ppermute | solution.py:404
  97.4 11.9 %sectors.7 = (f32[2,3,64,128]{3,2,1,0:T(8,128)S(1)}, f32[2,3,64,128]{3,2,1,0:T(8,128)S(1)}, f32[2,3,64,128]{3,2,1,0:T(8,128)S(1)}, f32[2,3,64,128]{3,2,1,0:T(8,1...) custom-call(s32[57]{0:T(128)S(1)} %copy-done.1, ...), custom_call_target="tpu_custom_call", output_to_operand_aliasing={{5}: (9, {})} | custom-call | tf_op jit(solution)/shard_map/sectors/pallas_call | solution.py:184
  111.0 3.8 %collective-permute-start.26 = (f32[2,3,64,128]{3,2,1,0:T(8,128)S(1)}, f32[2,3,64,128]{3,2,1,0:T(8,128)S(1)}, u32[]{:S(2)}, u32[]{:S(2)}) collective-permute-start(f32[2,3,64,128]{3,2,1,0:T(8,128)S(1)} %get-tuple-element.100), channel_id=1, source_target_pairs={{0,12},{4,0},{8,4},{12,8},{1,13},{5,1},{9,5},{13,9},{2,14},{6,2},{... | collective-permute-start | bytes 589832 | tf_op jit(solution)/shard_map/ppermute | solution.py:404
  115.5 1.2 collective-permute-start.35
  117.3 4.8 %collective-permute-done.29.theirs_ref = f32[4,3,64,128]{3,2,1,0:T(8,128)S(1)} collective-permute-done((f32[4,3,64,128]{3,2,1,0:T(8,128)S(1)}, f32[4,3,64,128]{3,2,1,0:T(8,128)S(1)}, u32[]{:S(2)}, u32[]{:S(2)}) %collective-permute-start.29) | collective-permute-done | bytes 393248 | tf_op jit(solution)/shard_map/ppermute | solution.py:24
  124.0 2.3 %collective-permute-done.35.theirs_ref = f32[2,3,64,128]{3,2,1,0:T(8,128)S(1)} collective-permute-done((f32[2,3,64,128]{3,2,1,0:T(8,128)S(1)}, f32[2,3,64,128]{3,2,1,0:T(8,128)S(1)}, u32[]{:S(2)}, u32[]{:S(2)}) %collective-permute-start.35) | collective-permute-done | bytes 196640 | tf_op jit(solution)/shard_map/ppermute | solution.py:24
  127.8 2.3 %collective-permute-start.27 = (f32[2,3,64,128]{3,2,1,0:T(8,128)S(1)}, f32[2,3,64,128]{3,2,1,0:T(8,128)S(1)}, u32[]{:S(2)}, u32[]{:S(2)}) collective-permute-start(f32[2,3,64,128]{3,2,1,0:T(8,128)S(1)} %get-tuple-element.101), channel_id=1, source_target_pairs={{0,8},{4,12},{8,0},{12,4},{1,9},{5,13},{9,1},{13,5},{2,10},{6,14},... | collective-permute-start | bytes 589832 | tf_op jit(solution)/shard_map/ppermute | solution.py:404
  130.8 1.2 collective-permute-start.31
  132.0 1.2 collective-permute-done.21
  133.1 3.9 %collective-permute-start.24 = (f32[8,128]{1,0:T(8,128)S(1)}, f32[8,128]{1,0:T(8,128)S(1)}, u32[]{:S(2)}, u32[]{:S(2)}) collective-permute-start(f32[8,128]{1,0:T(8,128)S(1)} %add.84), channel_id=1, source_target_pairs={{0,12},{4,8},{8,4},{12,0},{1,13},{5,9},{9,5},{13,1},{2,14},{6,10},... | collective-permute-start | bytes 12296 | tf_op jit(solution)/shard_map/ppermute | solution.py:24
  137.0 1.7 collective-permute-done.24
  138.7 6.6 %collective-permute-start.23 = (f32[8,128]{1,0:T(8,128)S(1)}, f32[8,128]{1,0:T(8,128)S(1)}, u32[]{:S(2)}, u32[]{:S(2)}) collective-permute-start(f32[8,128]{1,0:T(8,128)S(1)} %add.84), channel_id=1, source_target_pairs={{0,8},{4,12},{8,0},{12,4},{1,9},{5,13},{9,1},{13,5},{2,10},{6,14},... | collective-permute-start | bytes 12296 | tf_op jit(solution)/shard_map/ppermute | solution.py:24
  145.3 1.6 collective-permute-done.23
  146.9 2.9 %collective-permute-start.22 = (f32[8,128]{1,0:T(8,128)S(1)}, f32[8,128]{1,0:T(8,128)S(1)}, u32[]{:S(2)}, u32[]{:S(2)}) collective-permute-start(f32[8,128]{1,0:T(8,128)S(1)} %add.84), channel_id=1, source_target_pairs={{0,4},{4,0},{8,12},{12,8},{1,5},{5,1},{9,13},{13,9},{2,6},{6,2},{1... | collective-permute-start | bytes 12296 | tf_op jit(solution)/shard_map/ppermute | solution.py:24
  149.8 1.6 collective-permute-done.22
  153.7 1.2 collective-permute-start.32
  155.0 5.8 %scaled.1 = f32[16,3,64,128]{3,2,1,0:T(8,128)} custom-call(s32[57]{0:T(128)S(1)} %copy-done.1, f32[8,128]{1,0:T(8,128)S(1)} %broadcast_in_dim.2.scale_ref, f32[16,3,64,128]{3,2,1,0:T(8,128)S(1)} %get-tuple-element.93.refs_2_.refs_6_.vector_ref.raw_ref), custom_call_target="tpu_custom_call" | custom-call | tf_op jit(solution)/shard_map/scaled/pallas_call | solution.py:315
  160.8 1.9 %finish.7.rest_0_ = f32[16,3,64,128]{3,2,1,0:T(8,128)} custom-call(s32[57]{0:T(128)S(1)} %copy-done.1, f32[8,128]{1,0:T(8,128)S(1)} %broadcast_in_dim.2.scale_ref, f32[4,3,64,128]{3,2,1,0:T(8,128)S(1)} %combine.24.mine_ref, f32[4,3,64,128]{3,2,1,0:T(8,128)S(1)} %collective-permute-done.29.theirs_ref), custom_call_target="tpu_custom_call" | custom-call | tf_op jit(solution)/shard_map/finish/pallas_call | solution.py:352
  162.7 1.3 finish.8.rest_0_
  164.0 1.3 finish.9.rest_0_
  165.2 1.3 finish.10.rest_0_
  166.5 1.3 finish.11.rest_0_
  167.7 1.3 finish.12.rest_0_
  169.0 1.3 finish.13
  (72 shorter events, 21.8 us)
Async XLA Ops:
  0.6 3.8 %collective-permute-start = (f32[16,3,64,128]{3,2,1,0:T(8,128)}, f32[16,3,64,128]{3,2,1,0:T(8,128)S(1)}, u32[]{:S(2)}, u32[]{:S(2)}) collective-permute-start(f32[16,3,64,128]{3,2,1,0:T(8,128)} %bitcast.3), channel_id=1, source_target_pairs={{0,1},{1,0},{2,3},{3,2},{4,5},{5,4},{6,7},{7,6},{8,9},{9,8},{10,11... | collective-permute-start | bytes 4718600 | tf_op jit(solution)/shard_map/ppermute | solution.py:407
  4.4 1.4 copy-start
  5.8 0.7 copy-start.1
  6.5 10.4 %copy-start.2 = (f32[16,128]{1,0:T(8,128)S(1)}, f32[16,128]{1,0:T(8,128)}, u32[]{:S(2)}) copy-start(f32[16,128]{1,0:T(8,128)} %param.13) | copy-start | bytes 24580
  6.5 10.4 %copy-start.3 = (f32[16,64]{1,0:T(8,128)S(1)}, f32[16,64]{1,0:T(8,128)}, u32[]{:S(2)}) copy-start(f32[16,64]{1,0:T(8,128)} %param.12) | copy-start | bytes 12292
  11.7 17.3 %collective-permute-start.1 = (f32[2,3,64,128]{3,2,1,0:T(8,128)S(1)}, f32[2,3,64,128]{3,2,1,0:T(8,128)S(1)}, u32[]{:S(2)}, u32[]{:S(2)}) collective-permute-start(f32[2,3,64,128]{3,2,1,0:T(8,128)S(1)} %get-tuple-element.61), channel_id=1, source_target_pairs={{0,4},{4,8},{8,12},{12,0},{1,5},{5,9},{9,13},{13,1},{2,6},{6,10},{... | collective-permute-start | bytes 589832 | tf_op jit(solution)/shard_map/ppermute | solution.py:404
  14.7 14.3 %collective-permute-start.2 = (f32[2,3,64,128]{3,2,1,0:T(8,128)S(1)}, f32[2,3,64,128]{3,2,1,0:T(8,128)S(1)}, u32[]{:S(2)}, u32[]{:S(2)}) collective-permute-start(f32[2,3,64,128]{3,2,1,0:T(8,128)S(1)} %get-tuple-element.62), channel_id=1, source_target_pairs={{0,12},{4,0},{8,4},{12,8},{1,13},{5,1},{9,5},{13,9},{2,14},{6,2},{... | collective-permute-start | bytes 589832 | tf_op jit(solution)/shard_map/ppermute | solution.py:404
  29.8 16.1 %collective-permute-start.7 = (f32[4,3,64,128]{3,2,1,0:T(8,128)S(1)}, f32[4,3,64,128]{3,2,1,0:T(8,128)S(1)}, u32[]{:S(2)}, u32[]{:S(2)}) collective-permute-start(f32[4,3,64,128]{3,2,1,0:T(8,128)S(1)} %get-tuple-element.81.rest_0_), channel_id=1, source_target_pairs={{0,2},{2,0},{1,3},{3,1},{4,6},{6,4},{5,7},{7,5},{8,10},{10,8},{9,1... | collective-permute-start | bytes 1179656 | tf_op jit(solution)/shard_map/ppermute | solution.py:24
  31.6 9.6 %collective-permute-start.3 = (f32[2,3,64,128]{3,2,1,0:T(8,128)S(1)}, f32[2,3,64,128]{3,2,1,0:T(8,128)S(1)}, u32[]{:S(2)}, u32[]{:S(2)}) collective-permute-start(f32[2,3,64,128]{3,2,1,0:T(8,128)S(1)} %get-tuple-element.68), channel_id=1, source_target_pairs={{0,4},{4,8},{8,12},{12,0},{1,5},{5,9},{9,13},{13,1},{2,6},{6,10},{... | collective-permute-start | bytes 589832 | tf_op jit(solution)/shard_map/ppermute | solution.py:404
  31.6 10.7 %collective-permute-start.4 = (f32[2,3,64,128]{3,2,1,0:T(8,128)S(1)}, f32[2,3,64,128]{3,2,1,0:T(8,128)S(1)}, u32[]{:S(2)}, u32[]{:S(2)}) collective-permute-start(f32[2,3,64,128]{3,2,1,0:T(8,128)S(1)} %get-tuple-element.71), channel_id=1, source_target_pairs={{0,12},{4,0},{8,4},{12,8},{1,13},{5,1},{9,5},{13,9},{2,14},{6,2},{... | collective-permute-start | bytes 589832 | tf_op jit(solution)/shard_map/ppermute | solution.py:404
  41.2 15.4 %collective-permute-start.5 = (f32[2,3,64,128]{3,2,1,0:T(8,128)S(1)}, f32[2,3,64,128]{3,2,1,0:T(8,128)S(1)}, u32[]{:S(2)}, u32[]{:S(2)}) collective-permute-start(f32[2,3,64,128]{3,2,1,0:T(8,128)S(1)} %get-tuple-element.74), channel_id=1, source_target_pairs={{0,8},{4,12},{8,0},{12,4},{1,9},{5,13},{9,1},{13,5},{2,10},{6,14},... | collective-permute-start | bytes 589832 | tf_op jit(solution)/shard_map/ppermute | solution.py:404
  42.3 17.0 %collective-permute-start.6 = (f32[2,3,64,128]{3,2,1,0:T(8,128)S(1)}, f32[2,3,64,128]{3,2,1,0:T(8,128)S(1)}, u32[]{:S(2)}, u32[]{:S(2)}) collective-permute-start(f32[2,3,64,128]{3,2,1,0:T(8,128)S(1)} %get-tuple-element.77), channel_id=1, source_target_pairs={{0,8},{4,12},{8,0},{12,4},{1,9},{5,13},{9,1},{13,5},{2,10},{6,14},... | collective-permute-start | bytes 589832 | tf_op jit(solution)/shard_map/ppermute | solution.py:404
  46.0 13.9 %collective-permute-start.8 = (f32[2,3,64,128]{3,2,1,0:T(8,128)S(1)}, f32[2,3,64,128]{3,2,1,0:T(8,128)S(1)}, u32[]{:S(2)}, u32[]{:S(2)}) collective-permute-start(f32[2,3,64,128]{3,2,1,0:T(8,128)S(1)} %get-tuple-element.82.rest_4_), channel_id=1, source_target_pairs={{0,2},{2,0},{1,3},{3,1},{4,6},{6,4},{5,7},{7,5},{8,10},{10,8},{9,1... | collective-permute-start | bytes 589832 | tf_op jit(solution)/shard_map/ppermute | solution.py:24
  47.0 20.5 %collective-permute-start.16 = (f32[2,3,64,128]{3,2,1,0:T(8,128)S(1)}, f32[2,3,64,128]{3,2,1,0:T(8,128)S(1)}, u32[]{:S(2)}, u32[]{:S(2)}) collective-permute-start(f32[2,3,64,128]{3,2,1,0:T(8,128)S(1)} %get-tuple-element.85.rest_2_), channel_id=1, source_target_pairs={{0,2},{2,0},{1,3},{3,1},{4,6},{6,4},{5,7},{7,5},{8,10},{10,8},{9,1... | collective-permute-start | bytes 589832 | tf_op jit(solution)/shard_map/ppermute | solution.py:24
  59.9 5.7 %collective-permute-start.9 = (f32[2,3,64,128]{3,2,1,0:T(8,128)S(1)}, f32[2,3,64,128]{3,2,1,0:T(8,128)S(1)}, u32[]{:S(2)}, u32[]{:S(2)}) collective-permute-start(f32[2,3,64,128]{3,2,1,0:T(8,128)S(1)} %get-tuple-element.83.rest_8_), channel_id=1, source_target_pairs={{0,2},{2,0},{1,3},{3,1},{4,6},{6,4},{5,7},{7,5},{8,10},{10,8},{9,1... | collective-permute-start | bytes 589832 | tf_op jit(solution)/shard_map/ppermute | solution.py:24
  65.7 3.0 %collective-permute-start.12 = (f32[8,128]{1,0:T(8,128)S(1)}, f32[8,128]{1,0:T(8,128)S(1)}, u32[]{:S(2)}, u32[]{:S(2)}) collective-permute-start(f32[8,128]{1,0:T(8,128)S(1)} %add_add_fusion.2), channel_id=1, source_target_pairs={{0,3},{1,2},{2,1},{3,0},{4,7},{5,6},{6,5},{7,4},{8,11},{9,10},{10,... | collective-permute-start | bytes 12296 | tf_op jit(solution)/shard_map/ppermute | solution.py:24
  65.7 3.6 %collective-permute-start.11 = (f32[8,128]{1,0:T(8,128)S(1)}, f32[8,128]{1,0:T(8,128)S(1)}, u32[]{:S(2)}, u32[]{:S(2)}) collective-permute-start(f32[8,128]{1,0:T(8,128)S(1)} %add_add_fusion.2), channel_id=1, source_target_pairs={{0,2},{1,3},{2,0},{3,1},{4,6},{5,7},{6,4},{7,5},{8,10},{9,11},{10,... | collective-permute-start | bytes 12296 | tf_op jit(solution)/shard_map/ppermute | solution.py:24
  66.2 3.1 %collective-permute-start.10 = (f32[8,128]{1,0:T(8,128)S(1)}, f32[8,128]{1,0:T(8,128)S(1)}, u32[]{:S(2)}, u32[]{:S(2)}) collective-permute-start(f32[8,128]{1,0:T(8,128)S(1)} %add_add_fusion.2), channel_id=1, source_target_pairs={{0,1},{1,0},{2,3},{3,2},{4,5},{5,4},{6,7},{7,6},{8,9},{9,8},{10,11... | collective-permute-start | bytes 12296 | tf_op jit(solution)/shard_map/ppermute | solution.py:24
  67.5 6.8 %collective-permute-start.17 = (f32[2,3,64,128]{3,2,1,0:T(8,128)S(1)}, f32[2,3,64,128]{3,2,1,0:T(8,128)S(1)}, u32[]{:S(2)}, u32[]{:S(2)}) collective-permute-start(f32[2,3,64,128]{3,2,1,0:T(8,128)S(1)} %get-tuple-element.87.rest_6_), channel_id=1, source_target_pairs={{0,2},{2,0},{1,3},{3,1},{4,6},{6,4},{5,7},{7,5},{8,10},{10,8},{9,1... | collective-permute-start | bytes 589832 | tf_op jit(solution)/shard_map/ppermute | solution.py:24
  69.3 7.1 %collective-permute-start.15 = (f32[8,128]{1,0:T(8,128)S(1)}, f32[8,128]{1,0:T(8,128)S(1)}, u32[]{:S(2)}, u32[]{:S(2)}) collective-permute-start(f32[8,128]{1,0:T(8,128)S(1)} %add_add_fusion.1), channel_id=1, source_target_pairs={{0,12},{4,8},{8,4},{12,0},{1,13},{5,9},{9,5},{13,1},{2,14},{6,10},... | collective-permute-start | bytes 12296 | tf_op jit(solution)/shard_map/ppermute | solution.py:24
  72.2 4.5 %collective-permute-start.14 = (f32[8,128]{1,0:T(8,128)S(1)}, f32[8,128]{1,0:T(8,128)S(1)}, u32[]{:S(2)}, u32[]{:S(2)}) collective-permute-start(f32[8,128]{1,0:T(8,128)S(1)} %add_add_fusion.1), channel_id=1, source_target_pairs={{0,8},{4,12},{8,0},{12,4},{1,9},{5,13},{9,1},{13,5},{2,10},{6,14},... | collective-permute-start | bytes 12296 | tf_op jit(solution)/shard_map/ppermute | solution.py:24
  72.2 4.5 %collective-permute-start.13 = (f32[8,128]{1,0:T(8,128)S(1)}, f32[8,128]{1,0:T(8,128)S(1)}, u32[]{:S(2)}, u32[]{:S(2)}) collective-permute-start(f32[8,128]{1,0:T(8,128)S(1)} %add_add_fusion.1), channel_id=1, source_target_pairs={{0,4},{4,0},{8,12},{12,8},{1,5},{5,1},{9,13},{13,9},{2,6},{6,2},{1... | collective-permute-start | bytes 12296 | tf_op jit(solution)/shard_map/ppermute | solution.py:24
  74.3 7.8 %collective-permute-start.18 = (f32[2,3,64,128]{3,2,1,0:T(8,128)S(1)}, f32[2,3,64,128]{3,2,1,0:T(8,128)S(1)}, u32[]{:S(2)}, u32[]{:S(2)}) collective-permute-start(f32[2,3,64,128]{3,2,1,0:T(8,128)S(1)} %get-tuple-element.89.rest_10_), channel_id=1, source_target_pairs={{0,2},{2,0},{1,3},{3,1},{4,6},{6,4},{5,7},{7,5},{8,10},{10,8},{9,1... | collective-permute-start | bytes 589832 | tf_op jit(solution)/shard_map/ppermute | solution.py:24
  75.0 9.5 %collective-permute-start.19 = (f32[2,3,64,128]{3,2,1,0:T(8,128)S(1)}, f32[2,3,64,128]{3,2,1,0:T(8,128)S(1)}, u32[]{:S(2)}, u32[]{:S(2)}) collective-permute-start(f32[2,3,64,128]{3,2,1,0:T(8,128)S(1)} %get-tuple-element.91.rest_12_), channel_id=1, source_target_pairs={{0,2},{2,0},{1,3},{3,1},{4,6},{6,4},{5,7},{7,5},{8,10},{10,8},{9,1... | collective-permute-start | bytes 589832 | tf_op jit(solution)/shard_map/ppermute | solution.py:24
  85.7 3.5 %collective-permute-start.20 = (f32[16,3,64,128]{3,2,1,0:T(8,128)S(1)}, f32[16,3,64,128]{3,2,1,0:T(8,128)S(1)}, u32[]{:S(2)}, u32[]{:S(2)}) collective-permute-start(f32[16,3,64,128]{3,2,1,0:T(8,128)S(1)} %get-tuple-element.93.refs_2_.refs_6_.vector_ref.raw_ref), channel_id=1, source_target_pairs={{0,1},{1,0},{2,3},{3,2},{4,5},{5,4},{6,7},{7,6},{8,9},{9,8},{10,11... | collective-permute-start | bytes 4718600 | tf_op jit(solution)/shard_map/ppermute | solution.py:407
  94.5 14.8 %collective-permute-start.25 = (f32[2,3,64,128]{3,2,1,0:T(8,128)S(1)}, f32[2,3,64,128]{3,2,1,0:T(8,128)S(1)}, u32[]{:S(2)}, u32[]{:S(2)}) collective-permute-start(f32[2,3,64,128]{3,2,1,0:T(8,128)S(1)} %get-tuple-element.99), channel_id=1, source_target_pairs={{0,12},{4,0},{8,4},{12,8},{1,13},{5,1},{9,5},{13,9},{2,14},{6,2},{... | collective-permute-start | bytes 589832 | tf_op jit(solution)/shard_map/ppermute | solution.py:404
  97.4 12.0 %collective-permute-start.28 = (f32[2,3,64,128]{3,2,1,0:T(8,128)S(1)}, f32[2,3,64,128]{3,2,1,0:T(8,128)S(1)}, u32[]{:S(2)}, u32[]{:S(2)}) collective-permute-start(f32[2,3,64,128]{3,2,1,0:T(8,128)S(1)} %get-tuple-element.103), channel_id=1, source_target_pairs={{0,4},{4,8},{8,12},{12,0},{1,5},{5,9},{9,13},{13,1},{2,6},{6,10},{... | collective-permute-start | bytes 589832 | tf_op jit(solution)/shard_map/ppermute | solution.py:404
  110.0 12.1 %collective-permute-start.29 = (f32[4,3,64,128]{3,2,1,0:T(8,128)S(1)}, f32[4,3,64,128]{3,2,1,0:T(8,128)S(1)}, u32[]{:S(2)}, u32[]{:S(2)}) collective-permute-start(f32[4,3,64,128]{3,2,1,0:T(8,128)S(1)} %combine.24.mine_ref), channel_id=1, source_target_pairs={{0,2},{2,0},{1,3},{3,1},{4,6},{6,4},{5,7},{7,5},{8,10},{10,8},{9,1... | collective-permute-start | bytes 1179656 | tf_op jit(solution)/shard_map/ppermute | solution.py:24
  111.0 12.0 %collective-permute-start.26 = (f32[2,3,64,128]{3,2,1,0:T(8,128)S(1)}, f32[2,3,64,128]{3,2,1,0:T(8,128)S(1)}, u32[]{:S(2)}, u32[]{:S(2)}) collective-permute-start(f32[2,3,64,128]{3,2,1,0:T(8,128)S(1)} %get-tuple-element.100), channel_id=1, source_target_pairs={{0,12},{4,0},{8,4},{12,8},{1,13},{5,1},{9,5},{13,9},{2,14},{6,2},{... | collective-permute-start | bytes 589832 | tf_op jit(solution)/shard_map/ppermute | solution.py:404
  114.8 8.6 %collective-permute-start.33 = (f32[2,3,64,128]{3,2,1,0:T(8,128)S(1)}, f32[2,3,64,128]{3,2,1,0:T(8,128)S(1)}, u32[]{:S(2)}, u32[]{:S(2)}) collective-permute-start(f32[2,3,64,128]{3,2,1,0:T(8,128)S(1)} %get-tuple-element.110), channel_id=1, source_target_pairs={{0,4},{4,8},{8,12},{12,0},{1,5},{5,9},{9,13},{13,1},{2,6},{6,10},{... | collective-permute-start | bytes 589832 | tf_op jit(solution)/shard_map/ppermute | solution.py:404
  115.5 10.9 %collective-permute-start.35 = (f32[2,3,64,128]{3,2,1,0:T(8,128)S(1)}, f32[2,3,64,128]{3,2,1,0:T(8,128)S(1)}, u32[]{:S(2)}, u32[]{:S(2)}) collective-permute-start(f32[2,3,64,128]{3,2,1,0:T(8,128)S(1)} %combine.27.mine_ref), channel_id=1, source_target_pairs={{0,2},{2,0},{1,3},{3,1},{4,6},{6,4},{5,7},{7,5},{8,10},{10,8},{9,1... | collective-permute-start | bytes 589832 | tf_op jit(solution)/shard_map/ppermute | solution.py:24
  122.1 8.7 %collective-permute-start.30 = (f32[2,3,64,128]{3,2,1,0:T(8,128)S(1)}, f32[2,3,64,128]{3,2,1,0:T(8,128)S(1)}, u32[]{:S(2)}, u32[]{:S(2)}) collective-permute-start(f32[2,3,64,128]{3,2,1,0:T(8,128)S(1)} %combine.23.mine_ref), channel_id=1, source_target_pairs={{0,2},{2,0},{1,3},{3,1},{4,6},{6,4},{5,7},{7,5},{8,10},{10,8},{9,1... | collective-permute-start | bytes 589832 | tf_op jit(solution)/shard_map/ppermute | solution.py:24
  126.3 25.2 %collective-permute-start.34 = (f32[2,3,64,128]{3,2,1,0:T(8,128)S(1)}, f32[2,3,64,128]{3,2,1,0:T(8,128)S(1)}, u32[]{:S(2)}, u32[]{:S(2)}) collective-permute-start(f32[2,3,64,128]{3,2,1,0:T(8,128)S(1)} %get-tuple-element.111), channel_id=1, source_target_pairs={{0,8},{4,12},{8,0},{12,4},{1,9},{5,13},{9,1},{13,5},{2,10},{6,14},... | collective-permute-start | bytes 589832 | tf_op jit(solution)/shard_map/ppermute | solution.py:404
  126.9 25.2 %collective-permute-start.36 = (f32[2,3,64,128]{3,2,1,0:T(8,128)S(1)}, f32[2,3,64,128]{3,2,1,0:T(8,128)S(1)}, u32[]{:S(2)}, u32[]{:S(2)}) collective-permute-start(f32[2,3,64,128]{3,2,1,0:T(8,128)S(1)} %combine.26.mine_ref), channel_id=1, source_target_pairs={{0,2},{2,0},{1,3},{3,1},{4,6},{6,4},{5,7},{7,5},{8,10},{10,8},{9,1... | collective-permute-start | bytes 589832 | tf_op jit(solution)/shard_map/ppermute | solution.py:24
  127.8 25.2 %collective-permute-start.27 = (f32[2,3,64,128]{3,2,1,0:T(8,128)S(1)}, f32[2,3,64,128]{3,2,1,0:T(8,128)S(1)}, u32[]{:S(2)}, u32[]{:S(2)}) collective-permute-start(f32[2,3,64,128]{3,2,1,0:T(8,128)S(1)} %get-tuple-element.101), channel_id=1, source_target_pairs={{0,8},{4,12},{8,0},{12,4},{1,9},{5,13},{9,1},{13,5},{2,10},{6,14},... | collective-permute-start | bytes 589832 | tf_op jit(solution)/shard_map/ppermute | solution.py:404
  130.8 22.9 %collective-permute-start.31 = (f32[2,3,64,128]{3,2,1,0:T(8,128)S(1)}, f32[2,3,64,128]{3,2,1,0:T(8,128)S(1)}, u32[]{:S(2)}, u32[]{:S(2)}) collective-permute-start(f32[2,3,64,128]{3,2,1,0:T(8,128)S(1)} %combine.22.mine_ref), channel_id=1, source_target_pairs={{0,2},{2,0},{1,3},{3,1},{4,6},{6,4},{5,7},{7,5},{8,10},{10,8},{9,1... | collective-permute-start | bytes 589832 | tf_op jit(solution)/shard_map/ppermute | solution.py:24
  132.0 1.2 collective-permute-start.21
  133.1 5.5 %collective-permute-start.24 = (f32[8,128]{1,0:T(8,128)S(1)}, f32[8,128]{1,0:T(8,128)S(1)}, u32[]{:S(2)}, u32[]{:S(2)}) collective-permute-start(f32[8,128]{1,0:T(8,128)S(1)} %add.84), channel_id=1, source_target_pairs={{0,12},{4,8},{8,4},{12,0},{1,13},{5,9},{9,5},{13,1},{2,14},{6,10},... | collective-permute-start | bytes 12296 | tf_op jit(solution)/shard_map/ppermute | solution.py:24
  138.7 8.2 %collective-permute-start.23 = (f32[8,128]{1,0:T(8,128)S(1)}, f32[8,128]{1,0:T(8,128)S(1)}, u32[]{:S(2)}, u32[]{:S(2)}) collective-permute-start(f32[8,128]{1,0:T(8,128)S(1)} %add.84), channel_id=1, source_target_pairs={{0,8},{4,12},{8,0},{12,4},{1,9},{5,13},{9,1},{13,5},{2,10},{6,14},... | collective-permute-start | bytes 12296 | tf_op jit(solution)/shard_map/ppermute | solution.py:24
  146.9 4.5 %collective-permute-start.22 = (f32[8,128]{1,0:T(8,128)S(1)}, f32[8,128]{1,0:T(8,128)S(1)}, u32[]{:S(2)}, u32[]{:S(2)}) collective-permute-start(f32[8,128]{1,0:T(8,128)S(1)} %add.84), channel_id=1, source_target_pairs={{0,4},{4,0},{8,12},{12,8},{1,5},{5,1},{9,13},{13,9},{2,6},{6,2},{1... | collective-permute-start | bytes 12296 | tf_op jit(solution)/shard_map/ppermute | solution.py:24
  152.1 15.6 %collective-permute-start.37 = (f32[2,3,64,128]{3,2,1,0:T(8,128)S(1)}, f32[2,3,64,128]{3,2,1,0:T(8,128)S(1)}, u32[]{:S(2)}, u32[]{:S(2)}) collective-permute-start(f32[2,3,64,128]{3,2,1,0:T(8,128)S(1)} %combine.25.mine_ref), channel_id=1, source_target_pairs={{0,2},{2,0},{1,3},{3,1},{4,6},{6,4},{5,7},{7,5},{8,10},{10,8},{9,1... | collective-permute-start | bytes 589832 | tf_op jit(solution)/shard_map/ppermute | solution.py:24
  153.7 15.2 %collective-permute-start.32 = (f32[2,3,64,128]{3,2,1,0:T(8,128)S(1)}, f32[2,3,64,128]{3,2,1,0:T(8,128)S(1)}, u32[]{:S(2)}, u32[]{:S(2)}) collective-permute-start(f32[2,3,64,128]{3,2,1,0:T(8,128)S(1)} %combine.21.mine_ref), channel_id=1, source_target_pairs={{0,2},{2,0},{1,3},{3,1},{4,6},{6,4},{5,7},{7,5},{8,10},{10,8},{9,1... | collective-permute-start | bytes 589832 | tf_op jit(solution)/shard_map/ppermute | solution.py:24

commit v3 on v2

v3 whole, which is shorter than its diff:
```python
import functools

import jax
import jax.numpy as jnp
from jax import lax
from jax.experimental import pallas as pl
from jax.experimental.pallas import tpu as pltpu
from jax.sharding import PartitionSpec as P

TAG = 8
LIMIT = 48 * 1024 * 1024
SMALL = 24 * 1024 * 1024
FREE = pl.CostEstimate(flops=0, bytes_accessed=0, transcendentals=0)
WHOLE = pl.BlockSpec(memory_space=pltpu.VMEM)
SCALARS = pl.BlockSpec(memory_space=pltpu.SMEM)
ANY = pl.BlockSpec(memory_space=pl.ANY)


def power_of_two(size):
    return size & (size - 1) == 0


def flip(value, axis, bit):
    size = lax.axis_size(axis)
    return lax.ppermute(value, axis, [(i, i ^ bit) for i in range(size)])


def small_sum(value, axis):
    size = lax.axis_size(axis)
    if not power_of_two(size):
        return lax.psum(value, axis)
    if size == 4:
        one, two, three = (flip(value, axis, bit) for bit in (1, 2, 3))
        return (value + one) + (two + three)
    bit = 1
    while bit < size:
        value = value + flip(value, axis, bit)
        bit *= 2
    return value


def halves(value):
    high = value.astype(jnp.bfloat16)
    low = (value - high.astype(jnp.float32)).astype(jnp.bfloat16)
    return high, low


def table_kernel(devices, partner_ref, kind_ref, table_ref, used):
    count, terms = partner_ref.shape[0], kind_ref.shape[0]
    per = count // devices
    me = lax.axis_index("blk")
    for c in range(devices):
        used[c] = 0

    def place(j, carry):
        where_to = partner_ref[j]
        owner = lax.div(where_to, count)
        offset = lax.rem(owner - me + devices, devices)
        at = offset * per + used[offset]
        used[offset] = used[offset] + 1
        table_ref[at] = j
        table_ref[count + at] = where_to - owner * count
        table_ref[2 * count + j] = at
        return carry

    lax.fori_loop(0, count, place, 0)
    for k in range(terms):
        table_ref[3 * count + k] = kind_ref[k]
    table_ref[3 * count + terms] = lax.axis_index("sub")


def make_table(partner, term_kind):
    devices = lax.axis_size("blk")
    length = 3 * partner.shape[0] + term_kind.shape[0] + 1
    return pl.pallas_call(
        functools.partial(table_kernel, devices),
        out_shape=jax.ShapeDtypeStruct((length,), jnp.int32),
        in_specs=[SCALARS, SCALARS],
        out_specs=SCALARS,
        scratch_shapes=[pltpu.SMEM((devices,), jnp.int32)],
    )(partner, term_kind)


def sector(table, count, terms, l_ref, r_ref, own_ref, other_ref, lhs, high_rhs, low_rhs):
    rows, width = l_ref.shape[2], r_ref.shape[3]
    roots = own_ref.shape[0] // rows
    first = table[3 * count + terms] == 0
    own, other = own_ref[...], other_ref[...]
    top = jnp.where(first, own, other)
    bottom = jnp.where(first, other, own)
    left = l_ref[:, 0].reshape(terms * rows, 2 * rows)
    left = jnp.concatenate(halves(left), axis=1)
    for r in range(roots):
        at = slice(r * rows, (r + 1) * rows)
        wide = jnp.concatenate(halves(jnp.concatenate([top[at], bottom[at]], axis=0)), axis=1)
        both = jnp.dot(
            left, jnp.concatenate([wide, wide], axis=0), preferred_element_type=jnp.float32
        )
        high, low = halves(both[:, :width] + both[:, width:])
        for k in range(terms):
            lanes = slice(k * width, (k + 1) * width)
            part = slice(k * rows, (k + 1) * rows)
            lhs[r * rows : (r + 1) * rows, lanes] = high[part]
            lhs[(roots + r) * rows : (roots + r + 1) * rows, lanes] = low[part]
    for k in range(terms):
        lanes = slice(k * width, (k + 1) * width)
        kind = table[3 * count + k]
        used = pl.ds(pl.multiple_of((1 - kind) * width, width), width)
        high, low = halves(r_ref[k, 0])
        high_rhs[used, lanes] = high
        low_rhs[used, lanes] = low
    dims = (((1,), (1,)), ((), ()))
    tall = lax.dot_general(lhs[...], high_rhs[...], dims, preferred_element_type=jnp.float32)
    short = lax.dot_general(
        lhs[: roots * rows], low_rhs[...], dims, preferred_element_type=jnp.float32
    )
    return tall[: roots * rows] + tall[roots * rows :] + short


def sector_kernel(count, terms, unroll, starts, tags, table, *refs):
    inputs, scratch = refs[: 4 * unroll], refs[-3 * unroll :]
    outputs = refs[-3 * unroll - len(starts) : -3 * unroll]
    tag_refs = refs[4 * unroll : 4 * unroll + 2]
    moved_refs, kept_ref = outputs[:-1], outputs[-1]
    width = kept_ref.shape[1]
    height = kept_ref.shape[0] // unroll
    step = pl.program_id(0)

    @pl.when(step == 0)
    def _():
        for ref in scratch:
            if ref.shape[0] == 2 * width:
                ref[...] = jnp.zeros_like(ref)
        if any(tags):
            tag = tag_refs[0][...] + tag_refs[1][...]
            for ref, begin, end, tagged in zip(moved_refs, starts, starts[1:], tags):
                if tagged:
                    ref[(end - begin) * unroll * height :] = tag

    results = [
        sector(table, count, terms, *inputs[4 * u : 4 * u + 4], *scratch[3 * u : 3 * u + 3])
        for u in range(unroll)
    ]
    for u in range(unroll):
        kept_ref[u * height : (u + 1) * height] = results[u][:, width:]
    for ref, begin, end in zip(moved_refs, starts, starts[1:]):

        @pl.when((step >= begin) & (step < end))
        def _(ref=ref, begin=begin):
            for u in range(unroll):
                at = pl.multiple_of(((step - begin) * unroll + u) * height, height)
                ref[pl.ds(at, height)] = results[u][:, :width]


def place_of(i, pieces):
    at, begin = pieces[0][0] + i, 0
    for (_, size), (base, _) in zip(pieces, pieces[1:]):
        begin += size
        at = jnp.where(i >= begin, base + i - begin, at)
    return at


def sectors(table, pieces, tags, left, right, own, other, kept, ordered):
    terms, count, rows, width = left.shape
    height = own.shape[0] // TAG * TAG // count // rows * rows
    roots = height // rows
    unroll = 2 if all(base % 2 == 0 and size % 2 == 0 for base, size in pieces) else 1
    units = [(base // unroll, size // unroll) for base, size in pieces]
    starts = [0]
    for _, size in units:
        starts.append(starts[-1] + size)

    def specs(u):
        def source(i, table):
            return table[unroll * place_of(i, units) + u]

        def held(i, table):
            return (unroll * place_of(i, units) + u if ordered else source(i, table), 0)

        return [
            pl.BlockSpec((terms, 1, rows, width), lambda i, t: (0, source(i, t), 0, 0)),
            pl.BlockSpec((terms, 1, width, width), lambda i, t: (0, source(i, t), 0, 0)),
            pl.BlockSpec((height, width), held),
            pl.BlockSpec((height, width), held),
        ]

    in_specs = [spec for u in range(unroll) for spec in specs(u)]
    args = [left, right, own, other] * unroll
    if any(tags):
        in_specs += [pl.BlockSpec((TAG, width), lambda i, t: (count * height // TAG, 0))] * 2
        args += [own, other]
    aliases = {}
    if kept is not None:
        in_specs.append(ANY)
        args.append(kept)
        aliases = {len(args): len(pieces)}
    shapes = [(size * height + TAG * tagged, width) for (_, size), tagged in zip(pieces, tags)]
    out = pl.pallas_call(
        functools.partial(sector_kernel, count, terms, unroll, starts, tags),
        out_shape=[
            jax.ShapeDtypeStruct(shape, jnp.float32)
            for shape in shapes + [(count * height, width)]
        ],
        grid_spec=pltpu.PrefetchScalarGridSpec(
            num_scalar_prefetch=1,
            grid=(starts[-1],),
            in_specs=in_specs,
            out_specs=[pl.BlockSpec(shape, lambda i, t: (0, 0)) for shape in shapes]
            + [pl.BlockSpec((unroll * height, width), lambda i, t: (place_of(i, units), 0))],
            scratch_shapes=[
                pltpu.VMEM((2 * height, terms * width), jnp.bfloat16),
                pltpu.VMEM((2 * width, terms * width), jnp.bfloat16),
                pltpu.VMEM((2 * width, terms * width), jnp.bfloat16),
            ]
            * unroll,
        ),
        input_output_aliases=aliases,
        compiler_params=pltpu.CompilerParams(vmem_limit_bytes=LIMIT),
        cost_estimate=FREE,
        name="sectors",
    )(table, *args)
    return out[:-1], out[-1]


def combine_kernel(share, starts, with_inner, table, kept_ref, vector_ref, diag_ref, *refs):
    arrived_refs, sum_ref = refs[: len(starts)], refs[len(starts)]
    rows = diag_ref.shape[1]
    roots = vector_ref.shape[0] // rows
    step = pl.program_id(0)
    arrived = arrived_refs[0][...]
    for ref, begin in zip(arrived_refs[1:], starts[1:]):
        arrived = jnp.where(step >= begin, ref[...], arrived)
    diag = share * diag_ref[0]
    if with_inner:
        inner_ref = refs[-1]

        @pl.when(step == 0)
        def _():
            inner_ref[...] = jnp.zeros_like(inner_ref)

    for r in range(roots):
        at = slice(r * rows, (r + 1) * rows)
        vector = vector_ref[at]
        total = kept_ref[at] + arrived[at] + diag * vector
        sum_ref[at] = total
        if with_inner:
            inner_ref[r : r + 1] += jnp.sum(vector * total, axis=0, keepdims=True)
            inner_ref[roots + r : roots + r + 1] += share * jnp.sum(
                vector * vector, axis=0, keepdims=True
            )


def combine(table, pieces, kept, arrived, vector, diag, share, ordered, with_inner):
    count, rows, width = diag.shape
    height = kept.shape[0] // count
    starts = [0]
    for _, size in pieces:
        starts.append(starts[-1] + size)

    def slot(i, table):
        return table[count + place_of(i, pieces)]

    def place(i, table):
        return table[2 * count + slot(i, table)]

    def held(i, table):
        return (place(i, table) if ordered else slot(i, table), 0)

    def arrived_spec(begin, end):
        return pl.BlockSpec((height, width), lambda i, t: (jnp.clip(i - begin, 0, end - begin - 1), 0))

    block = (height, width)
    out_shape = [jax.ShapeDtypeStruct((starts[-1] * height, width), jnp.float32)]
    out_specs = [pl.BlockSpec(block, lambda i, t: (i, 0))]
    if with_inner:
        out_shape.append(jax.ShapeDtypeStruct((TAG, width), jnp.float32))
        out_specs.append(pl.BlockSpec((TAG, width), lambda i, t: (0, 0)))
    out = pl.pallas_call(
        functools.partial(combine_kernel, share, starts[:-1], with_inner),
        out_shape=out_shape,
        grid_spec=pltpu.PrefetchScalarGridSpec(
            num_scalar_prefetch=1,
            grid=(starts[-1],),
            in_specs=[
                pl.BlockSpec(block, lambda i, t: (place(i, t), 0)),
                pl.BlockSpec(block, held),
                pl.BlockSpec((1, rows, width), lambda i, t: (slot(i, t), 0, 0)),
            ]
            + [arrived_spec(begin, end) for begin, end in zip(starts, starts[1:])],
            out_specs=out_specs,
        ),
        compiler_params=pltpu.CompilerParams(vmem_limit_bytes=SMALL),
        cost_estimate=FREE,
        name="combine",
    )(table, kept, vector, diag, *arrived)
    return out if with_inner else (out[0], None)


def correct_kernel(groups, table, inner_ref, vector_ref, diag_ref, *rest):
    parts, raw_ref = rest[:-1], rest[-1]
    count, rows, width = diag_ref.shape
    height = vector_ref.shape[0] // count
    roots = height // rows
    inner = jnp.sum(inner_ref[...], axis=1, keepdims=True)
    theta = inner[:roots] / inner[roots : 2 * roots]
    squares = [jnp.zeros((1, width), jnp.float32) for _ in range(roots)]
    for at, pieces in enumerate(groups):
        mine, theirs = parts[2 * at], parts[2 * at + 1]
        row = 0
        for base, size in pieces:
            for i in range(size):
                slot = table[count + base + i]
                held = slot * height
                place = table[2 * count + slot] * height
                diag = diag_ref[slot]
                for r in range(roots):
                    shift = theta[r : r + 1]
                    sigma = mine[row : row + rows] + theirs[row : row + rows]
                    vector = vector_ref[pl.ds(pl.multiple_of(held + r * rows, rows), rows)]
                    raw = (sigma - shift * vector) / jnp.maximum(jnp.abs(diag - shift), 1.0)
                    raw_ref[pl.ds(pl.multiple_of(place + r * rows, rows), rows)] = raw
                    squares[r] = squares[r] + jnp.sum(raw * raw, axis=0, keepdims=True)
                    row += rows
    raw_ref[count * height :] = jnp.concatenate(
        squares + [jnp.zeros((TAG - roots, width), jnp.float32)], axis=0
    )


def correct(table, groups, inner, vector, diag, parts):
    return pl.pallas_call(
        functools.partial(correct_kernel, groups),
        out_shape=jax.ShapeDtypeStruct((vector.shape[0] + TAG, vector.shape[1]), jnp.float32),
        in_specs=[SCALARS] + [WHOLE] * (3 + len(parts)),
        out_specs=WHOLE,
        compiler_params=pltpu.CompilerParams(vmem_limit_bytes=SMALL),
        cost_estimate=FREE,
        name="correct",
    )(table, inner, vector, diag, *parts)


def scaled_kernel(rows, table, scale_ref, raw_ref, out_ref):
    for r in range(raw_ref.shape[0] // rows):
        at = slice(r * rows, (r + 1) * rows)
        out_ref[at] = raw_ref[at] * scale_ref[r : r + 1]


def scaled(table, scale, raw, count, rows):
    height, width = raw.shape[0] // count // rows * rows, raw.shape[1]
    return pl.pallas_call(
        functools.partial(scaled_kernel, rows),
        out_shape=jax.ShapeDtypeStruct((count * height, width), jnp.float32),
        grid_spec=pltpu.PrefetchScalarGridSpec(
            num_scalar_prefetch=1,
            grid=(count,),
            in_specs=[
                pl.BlockSpec(scale.shape, lambda i, t: (0, 0)),
                pl.BlockSpec((height, width), lambda i, t: (t[2 * count + i], 0)),
            ],
            out_specs=pl.BlockSpec((height, width), lambda i, t: (i, 0)),
        ),
        compiler_params=pltpu.CompilerParams(vmem_limit_bytes=SMALL),
        cost_estimate=FREE,
        name="scaled",
    )(table, scale, raw)


def finish_kernel(rows, table, scale_ref, mine_ref, theirs_ref, *rest):
    out_ref = rest[-1]
    for r in range(mine_ref.shape[0] // rows):
        at = slice(r * rows, (r + 1) * rows)
        out_ref[at] = (mine_ref[at] + theirs_ref[at]) * scale_ref[r : r + 1]


def finish(table, pieces, scale, mine, theirs, out, count, rows):
    size = sum(size for _, size in pieces)
    height, width = mine.shape[0] // size, mine.shape[1]
    block = (height, width)
    in_specs = [
        pl.BlockSpec(scale.shape, lambda i, t: (0, 0)),
        pl.BlockSpec(block, lambda i, t: (i, 0)),
        pl.BlockSpec(block, lambda i, t: (i, 0)),
    ]
    args, aliases = [scale, mine, theirs], {}
    if out is not None:
        in_specs.append(ANY)
        args.append(out)
        aliases = {4: 0}
    return pl.pallas_call(
        functools.partial(finish_kernel, rows),
        out_shape=jax.ShapeDtypeStruct((count * height, width), jnp.float32),
        grid_spec=pltpu.PrefetchScalarGridSpec(
            num_scalar_prefetch=1,
            grid=(size,),
            in_specs=in_specs,
            out_specs=pl.BlockSpec(block, lambda i, t: (t[count + place_of(i, pieces)], 0)),
        ),
        input_output_aliases=aliases,
        compiler_params=pltpu.CompilerParams(vmem_limit_bytes=SMALL),
        cost_estimate=FREE,
        name="finish",
    )(table, *args)


def add_over_term(value):
    size = lax.axis_size("term")
    if size == 1 or not power_of_two(size):
        return lax.psum(value, "term"), jnp.zeros_like(value)
    bit = 1
    while 2 * bit < size:
        value = value + flip(value, "term", bit)
        bit *= 2
    return value, flip(value, "term", bit)


def after(value, *others):
    return lax.optimization_barrier((value,) + others)[0]


def shards(amplitudes, left, right, term_kind, partner, left_diag, right_diag):
    devices, terms_over = lax.axis_size("blk"), lax.axis_size("term")
    slots, rows, roots, width = amplitudes.shape
    per = slots // devices
    elements = slots * devices * rows * lax.axis_size("sub") * width
    vector = jnp.transpose(amplitudes, (0, 2, 1, 3)).reshape(slots * roots * rows, width)
    table = make_table(partner, term_kind)
    diag = left_diag[:, :, None] + right_diag[:, None, :]

    cuts = [(0, per // 2), (per // 2, per - per // 2)] if per > 1 else [(0, per)]
    staying, moving = (0, 0, per), []
    for c in range(1, (devices + 1) // 2):
        for start, size in cuts:
            moving += [(c, c * per + start, size), (devices - c, (devices - c) * per + start, size)]
    groups = [[staying] + moving[:2]] + [moving[i : i + 2] for i in range(2, len(moving), 2)]
    if devices % 2 == 0:
        c = devices // 2
        opposite = [(c, c * per + start, size) for start, size in cuts]
        groups += [[piece] for piece in opposite]
        moving += opposite
    batches = [moving[:2], moving[2:] + [staying]]

    def spans(pieces):
        return [piece[1:] for piece in pieces]

    def relay(value, c):
        return lax.ppermute(value, "blk", [(p, (p + c) % devices) for p in range(devices)])

    def partials(own, second):
        other = lax.ppermute(own, "sub", [(0, 1), (1, 0)])
        kept, outgoing = None, {}
        for batch in batches:
            parts, kept = sectors(
                table,
                spans(batch),
                [second and piece[0] > 0 for piece in batch],
                left,
                right,
                own,
                other,
                kept,
                second,
            )
            outgoing.update(zip(batch, parts))
        arrived, sums, inners = {}, [], []
        for at, piece in enumerate(moving):
            value = outgoing[piece]
            if at >= 2:
                value = after(value, arrived[moving[at - 2]])
            arrived[piece] = relay(value, piece[0])
        arrived[staying] = after(outgoing[staying], *[arrived[piece] for piece in moving[:2]])
        for group in groups:
            mine, inner = combine(
                table,
                spans(group),
                kept,
                [arrived[piece] for piece in group],
                own,
                diag,
                1.0 / terms_over,
                second,
                not second,
            )
            if len(sums) >= 4:
                mine = after(mine, sums[-3])
            sums += add_over_term(mine)
            inners.append(inner)
        return sums, inners, arrived, other

    sums, inners, _, _ = partials(vector, False)
    inner = sum(inners[1:], inners[0])
    for axis in ("sub", "blk", "term"):
        inner = small_sum(inner, axis)
    raw = correct(table, [spans(group) for group in groups], inner, vector, diag, sums)
    sums, _, arrived, other = partials(raw, True)
    squares = raw[-TAG:] + other[-TAG:]
    seen = set()
    for piece in moving:
        if piece[0] not in seen:
            seen.add(piece[0])
            squares = squares + arrived[piece][-TAG:]
    scale = lax.rsqrt(jnp.sum(squares, axis=1, keepdims=True) / elements + 1e-06)
    scale = jnp.broadcast_to(scale, squares.shape)
    correction = scaled(table, scale, raw, slots, rows)
    sigma = None
    for at, group in enumerate(groups):
        sigma = finish(
            table, spans(group), scale, sums[2 * at], sums[2 * at + 1], sigma, slots, rows
        )
    return tuple(
        jnp.transpose(value.reshape(slots, roots, rows, width), (0, 2, 1, 3))
        for value in (sigma, correction)
    )


def solution(mesh):
    return jax.shard_map(
        shards,
        mesh=mesh,
        in_specs=(
            P(("grp", "blk"), "sub", None, None),
            P(("grp", "term"), "blk", "sub", None),
            P(("grp", "term"), "blk", None, None),
            P(("grp", "term")),
            P(("grp", "blk")),
            P(("grp", "blk"), "sub"),
            P(("grp", "blk"), None),
        ),
        out_specs=(P(("grp", "blk"), "sub", None, None), P(("grp", "blk"), "sub", None, None)),
        check_vma=False,
    )
```

time: 170 us -> 152 us (0.89)
  starting transfers between devices: 56.8 us -> 35.5 us
  waiting for transfers between devices: 48.4 us -> 56.1 us
  Pallas kernels: 61.7 us -> 57 us
    ppermute x12, waiting for transfers between devices: 15 us -> 42.1 us  [relay(): lax.ppermute(value, 'blk', [(p, (p + c) % devices) for p in range(devices)])]
    ppermute x24 -> x13, starting transfers between devices: 33.9 us -> 13.5 us  [flip(): return lax.ppermute(value, axis, [(i, i ^ bit) for i in range(size)])]
    ppermute x24 -> x13, waiting for transfers between devices: 28.2 us -> 8.94 us  [flip(): return lax.ppermute(value, axis, [(i, i ^ bit) for i in range(size)])]
    pallas_call x23 -> x14, Pallas kernels: 25.7 us -> 21 us  [the longest x4 7.64 us: finish(): pl.pallas_call(functools.partial(finish_kernel, rows), out_shape=jax.Shap...]
  transfers between devices with their start and end apart: 38 -> 27, of which waited for: 20 -> 11; matrix products, arithmetic and copies ran while one was open for 0% -> 0% of each run, Pallas kernels for 28% -> 28%
where the time goes in v3:
time: 152 us
  Pallas kernels  57 us (38%)
  waiting for transfers between devices  56.1 us (37%)
  starting transfers between devices  35.5 us (23%)
  local copies, waits for them, and re-layouts  2.14 us (1%)
    ppermute x12, waiting for transfers between devices, relay(): lax.ppermute(value, 'blk', [(p, (p + c) % devices) for p in range(devices)])  42.1 us
    pallas_call x4, Pallas kernels, sectors(): pl.pallas_call(functools.partial(sector_kernel, count, terms, unroll, sta...  34.5 us
    ppermute x12, starting transfers between devices, relay(): lax.ppermute(value, 'blk', [(p, (p + c) % devices) for p in range(devices)])  21.4 us
    ppermute x13, starting transfers between devices, flip(): return lax.ppermute(value, axis, [(i, i ^ bit) for i in range(size)])  13.5 us
    ppermute x13, waiting for transfers between devices, flip(): return lax.ppermute(value, axis, [(i, i ^ bit) for i in range(size)])  8.94 us
    pallas_call x4, Pallas kernels, finish(): pl.pallas_call(functools.partial(finish_kernel, rows), out_shape=jax.Shap...  7.64 us
    pallas_call x8, Pallas kernels, combine(): pl.pallas_call(functools.partial(combine_kernel, share, starts[:-1], with...  6.3 us
    pallas_call x1, Pallas kernels, scaled(): pl.pallas_call(functools.partial(scaled_kernel, rows), out_shape=jax.Shap...  5.79 us
  transfers between devices with their start and end apart: 27, of which 11 were waited for; matrix products, arithmetic and copies ran while one was open for 0% of the time, Pallas kernels for 28%

profile of v3, /device:TPU:0, one launch (start us, length us, event | category | flops | bytes accessed | tf_op | source)
XLA Modules:
  0.0 151.9 jit_solution(14996881920276238977)
XLA Ops:
  1.1 1.5 %shard_map.86.table = s32[57]{0:T(128)} custom-call(s32[16]{0:T(128)} %partner_ref.1, s32[8]{0:T(128)} %kind_ref.1), custom_call_target="tpu_custom_call" | custom-call | tf_op jit(solution)/shard_map/pallas_call | solution.py:75
  2.7 1.7 %collective-permute-done.refs_3_.refs_7_ = f32[3072,128]{1,0:T(8,128)S(1)} collective-permute-done((f32[3072,128]{1,0:T(8,128)}, f32[3072,128]{1,0:T(8,128)S(1)}, u32[]{:S(2)}, u32[]{:S(2)}) %collective-permute-start) | collective-permute-done | bytes 1572896 | tf_op jit(solution)/shard_map/ppermute | solution.py:448
  4.4 1.4 copy-done
  5.8 0.7 copy-done.1
  6.5 5.3 %sectors.4 = (f32[384,128]{1,0:T(8,128)S(1)}, f32[384,128]{1,0:T(8,128)S(1)}, f32[3072,128]{1,0:T(8,128)S(1)}) custom-call(s32[57]{0:T(128)S(1)} %copy-done.1, f32[8,16,64,128]{3,2,1,0:T(8,128)} %refs_4_.7, f32[8,16,128,128]{3,2,1,0:T(8,128)} %refs_5_.7, f32[3072,128]{1,0:T(8,128)S(1)} %bitcast.10, f32[3072,128]{1,0:T(8,128)S(1)} %collective-permute-done.refs_3_.refs_7_, ...), custom_call_target="tpu_custom_call" | custom-call | tf_op jit(solution)/shard_map/sectors/pallas_call | solution.py:198
  11.7 3.0 %collective-permute-start.1 = (f32[384,128]{1,0:T(8,128)S(1)}, f32[384,128]{1,0:T(8,128)S(1)}, u32[]{:S(2)}, u32[]{:S(2)}) collective-permute-start(f32[384,128]{1,0:T(8,128)S(1)} %get-tuple-element.45), channel_id=1, source_target_pairs={{0,4},{4,8},{8,12},{12,0},{1,5},{5,9},{9,13},{13,1},{2,6},{6,10},{... | collective-permute-start | bytes 589832 | tf_op jit(solution)/shard_map/ppermute | solution.py:445
  14.7 2.1 %collective-permute-start.2 = (f32[384,128]{1,0:T(8,128)S(1)}, f32[384,128]{1,0:T(8,128)S(1)}, u32[]{:S(2)}, u32[]{:S(2)}) collective-permute-start(f32[384,128]{1,0:T(8,128)S(1)} %get-tuple-element.46), channel_id=1, source_target_pairs={{0,12},{4,0},{8,4},{12,8},{1,13},{5,1},{9,5},{13,9},{2,14},{6,2},{... | collective-permute-start | bytes 589832 | tf_op jit(solution)/shard_map/ppermute | solution.py:445
  17.0 12.0 %sectors.5 = (f32[384,128]{1,0:T(8,128)S(1)}, f32[384,128]{1,0:T(8,128)S(1)}, f32[384,128]{1,0:T(8,128)S(1)}, f32[384,128]{1,0:T(8,128)S(1)}, f32[768,128]{1,0:T(8,128)S(1)}, /*index=5*/f32[3072,128]{1,0:T(8,128)S(1)}) custom-call(s32[57]{0:T(128)S(1)} %copy-done.1, f32[8,16,64,128]{3,2,1,0:T(8,128)} %refs_4_.7, ...), custom_call_target="tpu_custom_call", output_to_operand_aliasing={{5}: (9, {})} | custom-call | tf_op jit(solution)/shard_map/sectors/pallas_call | solution.py:198
  29.1 1.2 combine.8
  30.2 1.7 %collective-permute-start.12 = (f32[1536,128]{1,0:T(8,128)S(1)}, f32[1536,128]{1,0:T(8,128)S(1)}, u32[]{:S(2)}, u32[]{:S(2)}) collective-permute-start(f32[1536,128]{1,0:T(8,128)S(1)} %get-tuple-element.60.rest_0_), channel_id=1, source_target_pairs={{0,2},{2,0},{1,3},{3,1},{4,6},{6,4},{5,7},{7,5},{8,10},{10,8},{9,1... | collective-permute-start | bytes 2359304 | tf_op jit(solution)/shard_map/ppermute | solution.py:25
  31.9 3.8 %collective-permute-start.4 = (f32[384,128]{1,0:T(8,128)S(1)}, f32[384,128]{1,0:T(8,128)S(1)}, u32[]{:S(2)}, u32[]{:S(2)}) collective-permute-start(f32[384,128]{1,0:T(8,128)S(1)} %get-tuple-element.52), channel_id=1, source_target_pairs={{0,12},{4,0},{8,4},{12,8},{1,13},{5,1},{9,5},{13,9},{2,14},{6,2},{... | collective-permute-start | bytes 589832 | tf_op jit(solution)/shard_map/ppermute | solution.py:445
  35.8 5.8 %collective-permute-done.3.refs_0_ = f32[384,128]{1,0:T(8,128)S(1)} collective-permute-done((f32[384,128]{1,0:T(8,128)S(1)}, f32[384,128]{1,0:T(8,128)S(1)}, u32[]{:S(2)}, u32[]{:S(2)}) %collective-permute-start.3) | collective-permute-done | bytes 196640 | tf_op jit(solution)/shard_map/ppermute | solution.py:445
  41.6 1.1 collective-permute-done.4.refs_1_
  42.7 3.7 %collective-permute-start.6 = (f32[384,128]{1,0:T(8,128)S(1)}, f32[384,128]{1,0:T(8,128)S(1)}, u32[]{:S(2)}, u32[]{:S(2)}) collective-permute-start(f32[384,128]{1,0:T(8,128)S(1)} %get-tuple-element.58), channel_id=1, source_target_pairs={{0,8},{4,12},{8,0},{12,4},{1,9},{5,13},{9,1},{13,5},{2,10},{6,14},... | collective-permute-start | bytes 589832 | tf_op jit(solution)/shard_map/ppermute | solution.py:445
  46.4 0.8 combine.9
  47.6 9.4 %collective-permute-done.5.refs_0_ = f32[384,128]{1,0:T(8,128)S(1)} collective-permute-done((f32[384,128]{1,0:T(8,128)S(1)}, f32[384,128]{1,0:T(8,128)S(1)}, u32[]{:S(2)}, u32[]{:S(2)}) %collective-permute-start.5) | collective-permute-done | bytes 196640 | tf_op jit(solution)/shard_map/ppermute | solution.py:445
  57.0 0.7 combine.10
  57.7 1.9 %collective-permute-done.6.refs_0_ = f32[384,128]{1,0:T(8,128)S(1)} collective-permute-done((f32[384,128]{1,0:T(8,128)S(1)}, f32[384,128]{1,0:T(8,128)S(1)}, u32[]{:S(2)}, u32[]{:S(2)}) %collective-permute-start.6) | collective-permute-done | bytes 196640 | tf_op jit(solution)/shard_map/ppermute | solution.py:445
  59.6 0.7 combine.11
  60.4 1.2 collective-permute-done.7
  61.6 1.7 %collective-permute-start.10 = (f32[8,128]{1,0:T(8,128)S(1)}, f32[8,128]{1,0:T(8,128)S(1)}, u32[]{:S(2)}, u32[]{:S(2)}) collective-permute-start(f32[8,128]{1,0:T(8,128)S(1)} %add.63), channel_id=1, source_target_pairs={{0,12},{4,8},{8,4},{12,0},{1,13},{5,9},{9,5},{13,1},{2,14},{6,10},... | collective-permute-start | bytes 12296 | tf_op jit(solution)/shard_map/ppermute | solution.py:25
  63.3 2.7 %collective-permute-start.8 = (f32[8,128]{1,0:T(8,128)S(1)}, f32[8,128]{1,0:T(8,128)S(1)}, u32[]{:S(2)}, u32[]{:S(2)}) collective-permute-start(f32[8,128]{1,0:T(8,128)S(1)} %add.63), channel_id=1, source_target_pairs={{0,4},{4,0},{8,12},{12,8},{1,5},{5,1},{9,13},{13,9},{2,6},{6,2},{1... | collective-permute-start | bytes 12296 | tf_op jit(solution)/shard_map/ppermute | solution.py:25
  66.5 1.5 collective-permute-start.14
  68.0 0.6 collective-permute-start.11
  68.6 7.8 %collective-permute-done.11 = f32[8,128]{1,0:T(8,128)S(1)} collective-permute-done((f32[8,128]{1,0:T(8,128)S(1)}, f32[8,128]{1,0:T(8,128)S(1)}, u32[]{:S(2)}, u32[]{:S(2)}) %collective-permute-start.11) | collective-permute-done | bytes 4128 | tf_op jit(solution)/shard_map/ppermute | solution.py:25
  76.4 1.2 correct.1.refs_2_.refs_6_.refs_8_.vector_ref.raw_ref
  77.7 3.4 %collective-permute-done.16.refs_3_.refs_7_.refs_9_ = f32[3080,128]{1,0:T(8,128)S(1)} collective-permute-done((f32[3080,128]{1,0:T(8,128)S(1)}, f32[3080,128]{1,0:T(8,128)S(1)}, u32[]{:S(2)}, u32[]{:S(2)}) %collective-permute-start.16) | collective-permute-done | bytes 1576992 | tf_op jit(solution)/shard_map/ppermute | solution.py:448
  81.1 5.3 %sectors.6 = (f32[392,128]{1,0:T(8,128)S(1)}, f32[392,128]{1,0:T(8,128)S(1)}, f32[3072,128]{1,0:T(8,128)S(1)}) custom-call(s32[57]{0:T(128)S(1)} %copy-done.1, f32[8,16,64,128]{3,2,1,0:T(8,128)} %refs_4_.7, f32[8,16,128,128]{3,2,1,0:T(8,128)} %refs_5_.7, f32[3080,128]{1,0:T(8,128)S(1)} %correct.1.refs_2_.refs_6_.refs_8_.vector_ref.raw_ref, ...), custom_call_target="tpu_custom_call" | custom-call | tf_op jit(solution)/shard_map/sectors/pallas_call | solution.py:198
  86.7 3.5 %collective-permute-start.18 = (f32[392,128]{1,0:T(8,128)S(1)}, f32[392,128]{1,0:T(8,128)S(1)}, u32[]{:S(2)}, u32[]{:S(2)}) collective-permute-start(f32[392,128]{1,0:T(8,128)S(1)} %get-tuple-element.67), channel_id=1, source_target_pairs={{0,12},{4,0},{8,4},{12,8},{1,13},{5,1},{9,5},{13,9},{2,14},{6,2},{... | collective-permute-start | bytes 602120 | tf_op jit(solution)/shard_map/ppermute | solution.py:445
  90.3 12.0 %sectors.7 = (f32[392,128]{1,0:T(8,128)S(1)}, f32[392,128]{1,0:T(8,128)S(1)}, f32[392,128]{1,0:T(8,128)S(1)}, f32[392,128]{1,0:T(8,128)S(1)}, f32[768,128]{1,0:T(8,128)S(1)}, /*index=5*/f32[3072,128]{1,0:T(8,128)S(1)}) custom-call(s32[57]{0:T(128)S(1)} %copy-done.1, f32[8,16,64,128]{3,2,1,0:T(8,128)} %refs_4_.7, ...), custom_call_target="tpu_custom_call", output_to_operand_aliasing={{5}: (11, {})} | custom-call | tf_op jit(solution)/shard_map/sectors/pallas_call | solution.py:198
  102.3 0.9 combine.15.mine_ref
  103.8 2.0 %collective-permute-start.19 = (f32[392,128]{1,0:T(8,128)S(1)}, f32[392,128]{1,0:T(8,128)S(1)}, u32[]{:S(2)}, u32[]{:S(2)}) collective-permute-start(f32[392,128]{1,0:T(8,128)S(1)} %get-tuple-element.71), channel_id=1, source_target_pairs={{0,4},{4,8},{8,12},{12,0},{1,5},{5,9},{9,13},{13,1},{2,6},{6,10},{... | collective-permute-start | bytes 602120 | tf_op jit(solution)/shard_map/ppermute | solution.py:445
  105.8 8.5 %collective-permute-done.21.refs_1_ = f32[392,128]{1,0:T(8,128)S(1)} collective-permute-done((f32[392,128]{1,0:T(8,128)S(1)}, f32[392,128]{1,0:T(8,128)S(1)}, u32[]{:S(2)}, u32[]{:S(2)}) %collective-permute-start.21) | collective-permute-done | bytes 200736 | tf_op jit(solution)/shard_map/ppermute | solution.py:445
  114.3 0.7 combine.13.mine_ref
  115.1 1.6 %collective-permute-start.23 = (f32[768,128]{1,0:T(8,128)S(1)}, f32[768,128]{1,0:T(8,128)S(1)}, u32[]{:S(2)}, u32[]{:S(2)}) collective-permute-start(f32[768,128]{1,0:T(8,128)S(1)} %combine.13.mine_ref), channel_id=1, source_target_pairs={{0,2},{2,0},{1,3},{3,1},{4,6},{6,4},{5,7},{7,5},{8,10},{10,8},{9,1... | collective-permute-start | bytes 1179656 | tf_op jit(solution)/shard_map/ppermute | solution.py:25
  116.6 1.2 collective-permute-start.22
  117.8 1.7 %collective-permute-start.20 = (f32[392,128]{1,0:T(8,128)S(1)}, f32[392,128]{1,0:T(8,128)S(1)}, u32[]{:S(2)}, u32[]{:S(2)}) collective-permute-start(f32[392,128]{1,0:T(8,128)S(1)} %get-tuple-element.72), channel_id=1, source_target_pairs={{0,8},{4,12},{8,0},{12,4},{1,9},{5,13},{9,1},{13,5},{2,10},{6,14},... | collective-permute-start | bytes 602120 | tf_op jit(solution)/shard_map/ppermute | solution.py:445
  119.5 12.0 %collective-permute-done.22.refs_0_ = f32[392,128]{1,0:T(8,128)S(1)} collective-permute-done((f32[392,128]{1,0:T(8,128)S(1)}, f32[392,128]{1,0:T(8,128)S(1)}, u32[]{:S(2)}, u32[]{:S(2)}) %collective-permute-start.22) | collective-permute-done | bytes 200736 | tf_op jit(solution)/shard_map/ppermute | solution.py:445
  131.5 0.6 combine.12.mine_ref
  132.2 3.4 %collective-permute-done.20.refs_0_ = f32[392,128]{1,0:T(8,128)S(1)} collective-permute-done((f32[392,128]{1,0:T(8,128)S(1)}, f32[392,128]{1,0:T(8,128)S(1)}, u32[]{:S(2)}, u32[]{:S(2)}) %collective-permute-start.20) | collective-permute-done | bytes 200736 | tf_op jit(solution)/shard_map/ppermute | solution.py:445
  135.6 0.6 combine.14.mine_ref
  136.3 0.6 collective-permute-start.24
  136.9 1.5 collective-permute-start.26
  138.5 5.8 %scaled.1 = f32[3072,128]{1,0:T(8,128)} custom-call(s32[57]{0:T(128)S(1)} %copy-done.1, f32[8,128]{1,0:T(8,128)S(1)} %broadcast_in_dim.2.scale_ref, f32[3080,128]{1,0:T(8,128)S(1)} %correct.1.refs_2_.refs_6_.refs_8_.vector_ref.raw_ref), custom_call_target="tpu_custom_call" | custom-call | tf_op jit(solution)/shard_map/scaled/pallas_call | solution.py:349
  144.3 3.2 %finish.4.rest_0_ = f32[3072,128]{1,0:T(8,128)} custom-call(s32[57]{0:T(128)S(1)} %copy-done.1, f32[8,128]{1,0:T(8,128)S(1)} %broadcast_in_dim.2.scale_ref, f32[1536,128]{1,0:T(8,128)S(1)} %combine.15.mine_ref, f32[1536,128]{1,0:T(8,128)S(1)} %collective-permute-done.25.theirs_ref), custom_call_target="tpu_custom_call" | custom-call | tf_op jit(solution)/shard_map/finish/pallas_call | solution.py:388
  147.5 1.9 %finish.5.rest_0_ = f32[3072,128]{1,0:T(8,128)} custom-call(s32[57]{0:T(128)S(1)} %copy-done.1, f32[8,128]{1,0:T(8,128)S(1)} %broadcast_in_dim.2.scale_ref, f32[768,128]{1,0:T(8,128)S(1)} %combine.13.mine_ref, f32[768,128]{1,0:T(8,128)S(1)} %collective-permute-done.23.theirs_ref, f32[3072,128]{1,0:T(8,128)} %finish.4.rest_0_), custom_call_target="tpu_custom_call", output_to_operand_aliasing={{}: (4, {})} | custom-call | tf_op jit(solution)/shard_map/finish/pallas_call | solution.py:388
  149.4 1.3 finish.6.rest_0_
  150.7 1.3 finish.7
  (41 shorter events, 3.0 us)
Async XLA Ops:
  0.6 3.8 %collective-permute-start = (f32[3072,128]{1,0:T(8,128)}, f32[3072,128]{1,0:T(8,128)S(1)}, u32[]{:S(2)}, u32[]{:S(2)}) collective-permute-start(f32[3072,128]{1,0:T(8,128)} %bitcast.9), channel_id=1, source_target_pairs={{0,1},{1,0},{2,3},{3,2},{4,5},{5,4},{6,7},{7,6},{8,9},{9,8},{10,11... | collective-permute-start | bytes 4718600 | tf_op jit(solution)/shard_map/ppermute | solution.py:448
  4.4 1.4 copy-start
  5.8 0.7 copy-start.1
  6.5 10.4 %copy-start.2 = (f32[16,128]{1,0:T(8,128)S(1)}, f32[16,128]{1,0:T(8,128)}, u32[]{:S(2)}) copy-start(f32[16,128]{1,0:T(8,128)} %param.13) | copy-start | bytes 24580
  6.5 10.4 %copy-start.3 = (f32[16,64]{1,0:T(8,128)S(1)}, f32[16,64]{1,0:T(8,128)}, u32[]{:S(2)}) copy-start(f32[16,64]{1,0:T(8,128)} %param.12) | copy-start | bytes 12292
  11.7 17.3 %collective-permute-start.1 = (f32[384,128]{1,0:T(8,128)S(1)}, f32[384,128]{1,0:T(8,128)S(1)}, u32[]{:S(2)}, u32[]{:S(2)}) collective-permute-start(f32[384,128]{1,0:T(8,128)S(1)} %get-tuple-element.45), channel_id=1, source_target_pairs={{0,4},{4,8},{8,12},{12,0},{1,5},{5,9},{9,13},{13,1},{2,6},{6,10},{... | collective-permute-start | bytes 589832 | tf_op jit(solution)/shard_map/ppermute | solution.py:445
  14.7 14.3 %collective-permute-start.2 = (f32[384,128]{1,0:T(8,128)S(1)}, f32[384,128]{1,0:T(8,128)S(1)}, u32[]{:S(2)}, u32[]{:S(2)}) collective-permute-start(f32[384,128]{1,0:T(8,128)S(1)} %get-tuple-element.46), channel_id=1, source_target_pairs={{0,12},{4,0},{8,4},{12,8},{1,13},{5,1},{9,5},{13,9},{2,14},{6,2},{... | collective-permute-start | bytes 589832 | tf_op jit(solution)/shard_map/ppermute | solution.py:445
  30.2 36.3 %collective-permute-start.12 = (f32[1536,128]{1,0:T(8,128)S(1)}, f32[1536,128]{1,0:T(8,128)S(1)}, u32[]{:S(2)}, u32[]{:S(2)}) collective-permute-start(f32[1536,128]{1,0:T(8,128)S(1)} %get-tuple-element.60.rest_0_), channel_id=1, source_target_pairs={{0,2},{2,0},{1,3},{3,1},{4,6},{6,4},{5,7},{7,5},{8,10},{10,8},{9,1... | collective-permute-start | bytes 2359304 | tf_op jit(solution)/shard_map/ppermute | solution.py:25
  31.9 9.6 %collective-permute-start.3 = (f32[384,128]{1,0:T(8,128)S(1)}, f32[384,128]{1,0:T(8,128)S(1)}, u32[]{:S(2)}, u32[]{:S(2)}) collective-permute-start(f32[384,128]{1,0:T(8,128)S(1)} %get-tuple-element.50), channel_id=1, source_target_pairs={{0,4},{4,8},{8,12},{12,0},{1,5},{5,9},{9,13},{13,1},{2,6},{6,10},{... | collective-permute-start | bytes 589832 | tf_op jit(solution)/shard_map/ppermute | solution.py:445
  31.9 10.7 %collective-permute-start.4 = (f32[384,128]{1,0:T(8,128)S(1)}, f32[384,128]{1,0:T(8,128)S(1)}, u32[]{:S(2)}, u32[]{:S(2)}) collective-permute-start(f32[384,128]{1,0:T(8,128)S(1)} %get-tuple-element.52), channel_id=1, source_target_pairs={{0,12},{4,0},{8,4},{12,8},{1,13},{5,1},{9,5},{13,9},{2,14},{6,2},{... | collective-permute-start | bytes 589832 | tf_op jit(solution)/shard_map/ppermute | solution.py:445
  41.6 15.4 %collective-permute-start.5 = (f32[384,128]{1,0:T(8,128)S(1)}, f32[384,128]{1,0:T(8,128)S(1)}, u32[]{:S(2)}, u32[]{:S(2)}) collective-permute-start(f32[384,128]{1,0:T(8,128)S(1)} %get-tuple-element.55), channel_id=1, source_target_pairs={{0,8},{4,12},{8,0},{12,4},{1,9},{5,13},{9,1},{13,5},{2,10},{6,14},... | collective-permute-start | bytes 589832 | tf_op jit(solution)/shard_map/ppermute | solution.py:445
  42.7 17.0 %collective-permute-start.6 = (f32[384,128]{1,0:T(8,128)S(1)}, f32[384,128]{1,0:T(8,128)S(1)}, u32[]{:S(2)}, u32[]{:S(2)}) collective-permute-start(f32[384,128]{1,0:T(8,128)S(1)} %get-tuple-element.58), channel_id=1, source_target_pairs={{0,8},{4,12},{8,0},{12,4},{1,9},{5,13},{9,1},{13,5},{2,10},{6,14},... | collective-permute-start | bytes 589832 | tf_op jit(solution)/shard_map/ppermute | solution.py:445
  47.2 18.8 %collective-permute-start.13 = (f32[768,128]{1,0:T(8,128)S(1)}, f32[768,128]{1,0:T(8,128)S(1)}, u32[]{:S(2)}, u32[]{:S(2)}) collective-permute-start(f32[768,128]{1,0:T(8,128)S(1)} %get-tuple-element.61.rest_2_), channel_id=1, source_target_pairs={{0,2},{2,0},{1,3},{3,1},{4,6},{6,4},{5,7},{7,5},{8,10},{10,8},{9,1... | collective-permute-start | bytes 1179656 | tf_op jit(solution)/shard_map/ppermute | solution.py:25
  60.3 1.2 collective-permute-start.7
  61.6 6.4 %collective-permute-start.10 = (f32[8,128]{1,0:T(8,128)S(1)}, f32[8,128]{1,0:T(8,128)S(1)}, u32[]{:S(2)}, u32[]{:S(2)}) collective-permute-start(f32[8,128]{1,0:T(8,128)S(1)} %add.63), channel_id=1, source_target_pairs={{0,12},{4,8},{8,4},{12,0},{1,13},{5,9},{9,5},{13,1},{2,14},{6,10},... | collective-permute-start | bytes 12296 | tf_op jit(solution)/shard_map/ppermute | solution.py:25
  63.3 4.7 %collective-permute-start.9 = (f32[8,128]{1,0:T(8,128)S(1)}, f32[8,128]{1,0:T(8,128)S(1)}, u32[]{:S(2)}, u32[]{:S(2)}) collective-permute-start(f32[8,128]{1,0:T(8,128)S(1)} %add.63), channel_id=1, source_target_pairs={{0,8},{4,12},{8,0},{12,4},{1,9},{5,13},{9,1},{13,5},{2,10},{6,14},... | collective-permute-start | bytes 12296 | tf_op jit(solution)/shard_map/ppermute | solution.py:25
  63.3 4.7 %collective-permute-start.8 = (f32[8,128]{1,0:T(8,128)S(1)}, f32[8,128]{1,0:T(8,128)S(1)}, u32[]{:S(2)}, u32[]{:S(2)}) collective-permute-start(f32[8,128]{1,0:T(8,128)S(1)} %add.63), channel_id=1, source_target_pairs={{0,4},{4,0},{8,12},{12,8},{1,5},{5,1},{9,13},{13,9},{2,6},{6,2},{1... | collective-permute-start | bytes 12296 | tf_op jit(solution)/shard_map/ppermute | solution.py:25
  66.0 10.4 %collective-permute-start.15 = (f32[384,128]{1,0:T(8,128)S(1)}, f32[384,128]{1,0:T(8,128)S(1)}, u32[]{:S(2)}, u32[]{:S(2)}) collective-permute-start(f32[384,128]{1,0:T(8,128)S(1)} %get-tuple-element.65.rest_6_), channel_id=1, source_target_pairs={{0,2},{2,0},{1,3},{3,1},{4,6},{6,4},{5,7},{7,5},{8,10},{10,8},{9,1... | collective-permute-start | bytes 589832 | tf_op jit(solution)/shard_map/ppermute | solution.py:25
  66.5 9.9 %collective-permute-start.14 = (f32[384,128]{1,0:T(8,128)S(1)}, f32[384,128]{1,0:T(8,128)S(1)}, u32[]{:S(2)}, u32[]{:S(2)}) collective-permute-start(f32[384,128]{1,0:T(8,128)S(1)} %get-tuple-element.63.rest_4_), channel_id=1, source_target_pairs={{0,2},{2,0},{1,3},{3,1},{4,6},{6,4},{5,7},{7,5},{8,10},{10,8},{9,1... | collective-permute-start | bytes 589832 | tf_op jit(solution)/shard_map/ppermute | solution.py:25
  68.0 8.4 %collective-permute-start.11 = (f32[8,128]{1,0:T(8,128)S(1)}, f32[8,128]{1,0:T(8,128)S(1)}, u32[]{:S(2)}, u32[]{:S(2)}) collective-permute-start(f32[8,128]{1,0:T(8,128)S(1)} %add_add_fusion), channel_id=1, source_target_pairs={{0,2},{2,0},{1,3},{3,1},{4,6},{6,4},{5,7},{7,5},{8,10},{10,8},{9,1... | collective-permute-start | bytes 12296 | tf_op jit(solution)/shard_map/ppermute | solution.py:25
  77.6 3.5 %collective-permute-start.16 = (f32[3080,128]{1,0:T(8,128)S(1)}, f32[3080,128]{1,0:T(8,128)S(1)}, u32[]{:S(2)}, u32[]{:S(2)}) collective-permute-start(f32[3080,128]{1,0:T(8,128)S(1)} %correct.1.refs_2_.refs_6_.refs_8_.vector_ref.raw_ref), channel_id=1, source_target_pairs={{0,1},{1,0},{2,3},{3,2},{4,5},{5,4},{6,7},{7,6},{8,9},{9,8},{10,11... | collective-permute-start | bytes 4730888 | tf_op jit(solution)/shard_map/ppermute | solution.py:448
  86.4 15.8 %collective-permute-start.17 = (f32[392,128]{1,0:T(8,128)S(1)}, f32[392,128]{1,0:T(8,128)S(1)}, u32[]{:S(2)}, u32[]{:S(2)}) collective-permute-start(f32[392,128]{1,0:T(8,128)S(1)} %get-tuple-element.66), channel_id=1, source_target_pairs={{0,4},{4,8},{8,12},{12,0},{1,5},{5,9},{9,13},{13,1},{2,6},{6,10},{... | collective-permute-start | bytes 602120 | tf_op jit(solution)/shard_map/ppermute | solution.py:445
  86.7 15.5 %collective-permute-start.18 = (f32[392,128]{1,0:T(8,128)S(1)}, f32[392,128]{1,0:T(8,128)S(1)}, u32[]{:S(2)}, u32[]{:S(2)}) collective-permute-start(f32[392,128]{1,0:T(8,128)S(1)} %get-tuple-element.67), channel_id=1, source_target_pairs={{0,12},{4,0},{8,4},{12,8},{1,13},{5,1},{9,5},{13,9},{2,14},{6,2},{... | collective-permute-start | bytes 602120 | tf_op jit(solution)/shard_map/ppermute | solution.py:445
  103.2 33.7 %collective-permute-start.25 = (f32[1536,128]{1,0:T(8,128)S(1)}, f32[1536,128]{1,0:T(8,128)S(1)}, u32[]{:S(2)}, u32[]{:S(2)}) collective-permute-start(f32[1536,128]{1,0:T(8,128)S(1)} %combine.15.mine_ref), channel_id=1, source_target_pairs={{0,2},{2,0},{1,3},{3,1},{4,6},{6,4},{5,7},{7,5},{8,10},{10,8},{9,1... | collective-permute-start | bytes 2359304 | tf_op jit(solution)/shard_map/ppermute | solution.py:25
  103.8 10.5 %collective-permute-start.21 = (f32[392,128]{1,0:T(8,128)S(1)}, f32[392,128]{1,0:T(8,128)S(1)}, u32[]{:S(2)}, u32[]{:S(2)}) collective-permute-start(f32[392,128]{1,0:T(8,128)S(1)} %get-tuple-element.76), channel_id=1, source_target_pairs={{0,12},{4,0},{8,4},{12,8},{1,13},{5,1},{9,5},{13,9},{2,14},{6,2},{... | collective-permute-start | bytes 602120 | tf_op jit(solution)/shard_map/ppermute | solution.py:445
  103.8 10.5 %collective-permute-start.19 = (f32[392,128]{1,0:T(8,128)S(1)}, f32[392,128]{1,0:T(8,128)S(1)}, u32[]{:S(2)}, u32[]{:S(2)}) collective-permute-start(f32[392,128]{1,0:T(8,128)S(1)} %get-tuple-element.71), channel_id=1, source_target_pairs={{0,4},{4,8},{8,12},{12,0},{1,5},{5,9},{9,13},{13,1},{2,6},{6,10},{... | collective-permute-start | bytes 602120 | tf_op jit(solution)/shard_map/ppermute | solution.py:445
  115.1 21.3 %collective-permute-start.23 = (f32[768,128]{1,0:T(8,128)S(1)}, f32[768,128]{1,0:T(8,128)S(1)}, u32[]{:S(2)}, u32[]{:S(2)}) collective-permute-start(f32[768,128]{1,0:T(8,128)S(1)} %combine.13.mine_ref), channel_id=1, source_target_pairs={{0,2},{2,0},{1,3},{3,1},{4,6},{6,4},{5,7},{7,5},{8,10},{10,8},{9,1... | collective-permute-start | bytes 1179656 | tf_op jit(solution)/shard_map/ppermute | solution.py:25
  116.6 14.9 %collective-permute-start.22 = (f32[392,128]{1,0:T(8,128)S(1)}, f32[392,128]{1,0:T(8,128)S(1)}, u32[]{:S(2)}, u32[]{:S(2)}) collective-permute-start(f32[392,128]{1,0:T(8,128)S(1)} %get-tuple-element.77), channel_id=1, source_target_pairs={{0,8},{4,12},{8,0},{12,4},{1,9},{5,13},{9,1},{13,5},{2,10},{6,14},... | collective-permute-start | bytes 602120 | tf_op jit(solution)/shard_map/ppermute | solution.py:445
  117.8 17.8 %collective-permute-start.20 = (f32[392,128]{1,0:T(8,128)S(1)}, f32[392,128]{1,0:T(8,128)S(1)}, u32[]{:S(2)}, u32[]{:S(2)}) collective-permute-start(f32[392,128]{1,0:T(8,128)S(1)} %get-tuple-element.72), channel_id=1, source_target_pairs={{0,8},{4,12},{8,0},{12,4},{1,9},{5,13},{9,1},{13,5},{2,10},{6,14},... | collective-permute-start | bytes 602120 | tf_op jit(solution)/shard_map/ppermute | solution.py:445
  136.3 14.4 %collective-permute-start.24 = (f32[384,128]{1,0:T(8,128)S(1)}, f32[384,128]{1,0:T(8,128)S(1)}, u32[]{:S(2)}, u32[]{:S(2)}) collective-permute-start(f32[384,128]{1,0:T(8,128)S(1)} %combine.12.mine_ref), channel_id=1, source_target_pairs={{0,2},{2,0},{1,3},{3,1},{4,6},{6,4},{5,7},{7,5},{8,10},{10,8},{9,1... | collective-permute-start | bytes 589832 | tf_op jit(solution)/shard_map/ppermute | solution.py:25
  136.9 12.5 %collective-permute-start.26 = (f32[384,128]{1,0:T(8,128)S(1)}, f32[384,128]{1,0:T(8,128)S(1)}, u32[]{:S(2)}, u32[]{:S(2)}) collective-permute-start(f32[384,128]{1,0:T(8,128)S(1)} %combine.14.mine_ref), channel_id=1, source_target_pairs={{0,2},{2,0},{1,3},{3,1},{4,6},{6,4},{5,7},{7,5},{8,10},{10,8},{9,1... | collective-permute-start | bytes 589832 | tf_op jit(solution)/shard_map/ppermute | solution.py:25

commit v4 on v3

--- a/solution.py
+++ b/solution.py
@@ -81,7 +81,7 @@
     )(partner, term_kind)
 
 
-def sector(table, count, terms, l_ref, r_ref, own_ref, other_ref, lhs, high_rhs, low_rhs):
+def sector(table, count, terms, joined, l_ref, r_ref, own_ref, other_ref, lhs, high_rhs, low_rhs):
     rows, width = l_ref.shape[2], r_ref.shape[3]
     roots = own_ref.shape[0] // rows
     first = table[3 * count + terms] == 0
@@ -90,12 +90,18 @@
     bottom = jnp.where(first, other, own)
     left = l_ref[:, 0].reshape(terms * rows, 2 * rows)
     left = jnp.concatenate(halves(left), axis=1)
+    wide = []
     for r in range(roots):
         at = slice(r * rows, (r + 1) * rows)
-        wide = jnp.concatenate(halves(jnp.concatenate([top[at], bottom[at]], axis=0)), axis=1)
-        both = jnp.dot(
-            left, jnp.concatenate([wide, wide], axis=0), preferred_element_type=jnp.float32
-        )
+        one = jnp.concatenate(halves(jnp.concatenate([top[at], bottom[at]], axis=0)), axis=1)
+        wide.append(jnp.concatenate([one, one], axis=0))
+    if joined:
+        every = jnp.dot(left, jnp.concatenate(wide, axis=1), preferred_element_type=jnp.float32)
+    for r in range(roots):
+        if joined:
+            both = every[:, 2 * r * width : 2 * (r + 1) * width]
+        else:
+            both = jnp.dot(left, wide[r], preferred_element_type=jnp.float32)
         high, low = halves(both[:, :width] + both[:, width:])
         for k in range(terms):
             lanes = slice(k * width, (k + 1) * width)
@@ -117,7 +123,7 @@
     return tall[: roots * rows] + tall[roots * rows :] + short
 
 
-def sector_kernel(count, terms, unroll, starts, tags, table, *refs):
+def sector_kernel(count, terms, unroll, joined, starts, tags, table, *refs):
     inputs, scratch = refs[: 4 * unroll], refs[-3 * unroll :]
     outputs = refs[-3 * unroll - len(starts) : -3 * unroll]
     tag_refs = refs[4 * unroll : 4 * unroll + 2]
@@ -138,7 +144,7 @@
                     ref[(end - begin) * unroll * height :] = tag
 
     results = [
-        sector(table, count, terms, *inputs[4 * u : 4 * u + 4], *scratch[3 * u : 3 * u + 3])
+        sector(table, count, terms, joined, *inputs[4 * u : 4 * u + 4], *scratch[3 * u : 3 * u + 3])
         for u in range(unroll)
     ]
     for u in range(unroll):
@@ -196,7 +202,7 @@
         aliases = {len(args): len(pieces)}
     shapes = [(size * height + TAG * tagged, width) for (_, size), tagged in zip(pieces, tags)]
     out = pl.pallas_call(
-        functools.partial(sector_kernel, count, terms, unroll, starts, tags),
+        functools.partial(sector_kernel, count, terms, unroll, not ordered, starts, tags),
         out_shape=[
             jax.ShapeDtypeStruct(shape, jnp.float32)
             for shape in shapes + [(count * height, width)]
@@ -223,7 +229,9 @@
 
 
 def combine_kernel(share, starts, with_inner, table, kept_ref, vector_ref, diag_ref, *refs):
-    arrived_refs, sum_ref = refs[: len(starts)], refs[len(starts)]
+    arrived_refs, sum_ref = refs[: len(starts)], refs[-2 if with_inner else -1]
+    height = vector_ref.shape[0]
+    before = refs[len(starts) : -2] if with_inner else ()
     rows = diag_ref.shape[1]
     roots = vector_ref.shape[0] // rows
     step = pl.program_id(0)
@@ -236,21 +244,26 @@
 
         @pl.when(step == 0)
         def _():
-            inner_ref[...] = jnp.zeros_like(inner_ref)
+            inner_ref[...] = sum((ref[...] for ref in before), jnp.zeros_like(inner_ref))
 
     for r in range(roots):
         at = slice(r * rows, (r + 1) * rows)
         vector = vector_ref[at]
         total = kept_ref[at] + arrived[at] + diag * vector
-        sum_ref[at] = total
+        if before:
+            sum_ref[pl.ds(pl.multiple_of(step * height + r * rows, rows), rows)] = total
+        else:
+            sum_ref[at] = total
         if with_inner:
             inner_ref[r : r + 1] += jnp.sum(vector * total, axis=0, keepdims=True)
             inner_ref[roots + r : roots + r + 1] += share * jnp.sum(
                 vector * vector, axis=0, keepdims=True
             )
-
-
-def combine(table, pieces, kept, arrived, vector, diag, share, ordered, with_inner):
+    if before:
+        sum_ref[sum_ref.shape[0] - TAG :] = inner_ref[...]
+
+
+def combine(table, pieces, kept, arrived, vector, diag, share, ordered, with_inner, before):
     count, rows, width = diag.shape
     height = kept.shape[0] // count
     starts = [0]
@@ -270,8 +283,9 @@
         return pl.BlockSpec((height, width), lambda i, t: (jnp.clip(i - begin, 0, end - begin - 1), 0))
 
     block = (height, width)
-    out_shape = [jax.ShapeDtypeStruct((starts[-1] * height, width), jnp.float32)]
-    out_specs = [pl.BlockSpec(block, lambda i, t: (i, 0))]
+    whole = (starts[-1] * height + TAG * bool(before), width)
+    out_shape = [jax.ShapeDtypeStruct(whole, jnp.float32)]
+    out_specs = [pl.BlockSpec(whole if before else block, lambda i, t: (0 if before else i, 0))]
     if with_inner:
         out_shape.append(jax.ShapeDtypeStruct((TAG, width), jnp.float32))
         out_specs.append(pl.BlockSpec((TAG, width), lambda i, t: (0, 0)))
@@ -286,13 +300,14 @@
                 pl.BlockSpec(block, held),
                 pl.BlockSpec((1, rows, width), lambda i, t: (slot(i, t), 0, 0)),
             ]
-            + [arrived_spec(begin, end) for begin, end in zip(starts, starts[1:])],
+            + [arrived_spec(begin, end) for begin, end in zip(starts, starts[1:])]
+            + [pl.BlockSpec((TAG, width), lambda i, t: (0, 0))] * len(before),
             out_specs=out_specs,
         ),
         compiler_params=pltpu.CompilerParams(vmem_limit_bytes=SMALL),
         cost_estimate=FREE,
         name="combine",
-    )(table, kept, vector, diag, *arrived)
+    )(table, kept, vector, diag, *arrived, *before)
     return out if with_inner else (out[0], None)
 
 
@@ -338,67 +353,88 @@
     )(table, inner, vector, diag, *parts)
 
 
-def scaled_kernel(rows, table, scale_ref, raw_ref, out_ref):
-    for r in range(raw_ref.shape[0] // rows):
-        at = slice(r * rows, (r + 1) * rows)
-        out_ref[at] = raw_ref[at] * scale_ref[r : r + 1]
+def scatter(held, out_ref, sems, rows_of):
+    height = held.shape[0] // len(rows_of)
+    copies = []
+    for i, make in enumerate(rows_of):
+        at = slice(i * height, (i + 1) * height)
+        row = make(at)
+        copies.append(
+            pltpu.make_async_copy(
+                held.at[at], out_ref.at[pl.ds(pl.multiple_of(row, height), height)], sems.at[i]
+            )
+        )
+        copies[-1].start()
+    for copy in copies:
+        copy.wait()
+
+
+def scaled_kernel(count, rows, table, scale_ref, raw_ref, out_ref, held, sems):
+    height = held.shape[0] // count
+
+    def make(i, at):
+        place = pl.multiple_of(table[2 * count + i] * height, height)
+        for r in range(height // rows):
+            part = raw_ref[pl.ds(place + r * rows, rows)]
+            held[at.start + r * rows : at.start + (r + 1) * rows] = part * scale_ref[r : r + 1]
+        return i * height
+
+    scatter(held, out_ref, sems, [functools.partial(make, i) for i in range(count)])
 
 
 def scaled(table, scale, raw, count, rows):
     height, width = raw.shape[0] // count // rows * rows, raw.shape[1]
     return pl.pallas_call(
-        functools.partial(scaled_kernel, rows),
+        functools.partial(scaled_kernel, count, rows),
         out_shape=jax.ShapeDtypeStruct((count * height, width), jnp.float32),
-        grid_spec=pltpu.PrefetchScalarGridSpec(
-            num_scalar_prefetch=1,
-            grid=(count,),
-            in_specs=[
-                pl.BlockSpec(scale.shape, lambda i, t: (0, 0)),
-                pl.BlockSpec((height, width), lambda i, t: (t[2 * count + i], 0)),
-            ],
-            out_specs=pl.BlockSpec((height, width), lambda i, t: (i, 0)),
-        ),
+        in_specs=[SCALARS, WHOLE, WHOLE],
+        out_specs=ANY,
+        scratch_shapes=[
+            pltpu.VMEM((count * height, width), jnp.float32),
+            pltpu.SemaphoreType.DMA((count,)),
+        ],
         compiler_params=pltpu.CompilerParams(vmem_limit_bytes=SMALL),
         cost_estimate=FREE,
         name="scaled",
     )(table, scale, raw)
 
 
-def finish_kernel(rows, table, scale_ref, mine_ref, theirs_ref, *rest):
-    out_ref = rest[-1]
-    for r in range(mine_ref.shape[0] // rows):
-        at = slice(r * rows, (r + 1) * rows)
-        out_ref[at] = (mine_ref[at] + theirs_ref[at]) * scale_ref[r : r + 1]
+def finish_kernel(count, rows, places, table, scale_ref, mine_ref, theirs_ref, *rest):
+    out_ref, held, sems = rest[-3:]
+    height = held.shape[0] // len(places)
+
+    def make(place, at):
+        for r in range(height // rows):
+            part = slice(at.start + r * rows, at.start + (r + 1) * rows)
+            held[part] = (mine_ref[part] + theirs_ref[part]) * scale_ref[r : r + 1]
+        return table[count + place] * height
+
+    scatter(held, out_ref, sems, [functools.partial(make, place) for place in places])
 
 
 def finish(table, pieces, scale, mine, theirs, out, count, rows):
-    size = sum(size for _, size in pieces)
-    height, width = mine.shape[0] // size, mine.shape[1]
-    block = (height, width)
-    in_specs = [
-        pl.BlockSpec(scale.shape, lambda i, t: (0, 0)),
-        pl.BlockSpec(block, lambda i, t: (i, 0)),
-        pl.BlockSpec(block, lambda i, t: (i, 0)),
-    ]
-    args, aliases = [scale, mine, theirs], {}
+    places = [base + i for base, size in pieces for i in range(size)]
+    height, width = mine.shape[0] // len(places), mine.shape[1]
+    in_specs = [SCALARS, WHOLE, WHOLE, WHOLE]
+    args, aliases = [table, scale, mine, theirs], {}
     if out is not None:
         in_specs.append(ANY)
         args.append(out)
         aliases = {4: 0}
     return pl.pallas_call(
-        functools.partial(finish_kernel, rows),
+        functools.partial(finish_kernel, count, rows, places),
         out_shape=jax.ShapeDtypeStruct((count * height, width), jnp.float32),
-        grid_spec=pltpu.PrefetchScalarGridSpec(
-            num_scalar_prefetch=1,
-            grid=(size,),
-            in_specs=in_specs,
-            out_specs=pl.BlockSpec(block, lambda i, t: (t[count + place_of(i, pieces)], 0)),
-        ),
+        in_specs=in_specs,
+        out_specs=ANY,
+        scratch_shapes=[
+            pltpu.VMEM(mine.shape, jnp.float32),
+            pltpu.SemaphoreType.DMA((len(places),)),
+        ],
         input_output_aliases=aliases,
         compiler_params=pltpu.CompilerParams(vmem_limit_bytes=SMALL),
         cost_estimate=FREE,
         name="finish",
-    )(table, *args)
+    )(*args)
 
 
 def add_over_term(value):
@@ -412,8 +448,8 @@
     return value, flip(value, "term", bit)
 
 
-def after(value, *others):
-    return lax.optimization_barrier((value,) + others)[0]
+def after(*values):
+    return lax.optimization_barrier(values)
 
 
 def shards(amplitudes, left, right, term_kind, partner, left_diag, right_diag):
@@ -437,6 +473,7 @@
         groups += [[piece] for piece in opposite]
         moving += opposite
     batches = [moving[:2], moving[2:] + [staying]]
+    late = len(groups) > 2 and per > 1 and devices % 2 == 0
 
     def spans(pieces):
         return [piece[1:] for piece in pieces]
@@ -444,7 +481,7 @@
     def relay(value, c):
         return lax.ppermute(value, "blk", [(p, (p + c) % devices) for p in range(devices)])
 
-    def partials(own, second):
+    def partials(own, second, between):
         other = lax.ppermute(own, "sub", [(0, 1), (1, 0)])
         kept, outgoing = None, {}
         for batch in batches:
@@ -460,51 +497,71 @@
                 second,
             )
             outgoing.update(zip(batch, parts))
-        arrived, sums, inners = {}, [], []
-        for at, piece in enumerate(moving):
+        arrived, sums, inners, done = {}, [], [], ()
+        for at, piece in enumerate(moving[:-1] if late else moving):
             value = outgoing[piece]
             if at >= 2:
-                value = after(value, arrived[moving[at - 2]])
+                value = after(value, arrived[moving[at - 2]])[0]
+                if 2 * piece[0] == devices:
+                    value = after(value, arrived[moving[at - 1]])[0]
             arrived[piece] = relay(value, piece[0])
-        arrived[staying] = after(outgoing[staying], *[arrived[piece] for piece in moving[:2]])
+        arrived[staying] = after(outgoing[staying], *[arrived[piece] for piece in moving[:2]])[0]
         for group in groups:
+            if late and group == groups[-1]:
+                piece = group[0]
+                arrived[piece] = relay(after(outgoing[piece], sums[-2])[0], piece[0])
+                if between:
+                    arrived[piece], *done = after(arrived[piece], *between(sums, arrived, other))
+            first, *others = [arrived[piece] for piece in group]
+            if sums:
+                first = after(first, sums[-2])[0]
+            last = group == groups[-1] and len(groups) > 1
             mine, inner = combine(
                 table,
                 spans(group),
                 kept,
-                [arrived[piece] for piece in group],
+                [first] + others,
                 own,
                 diag,
                 1.0 / terms_over,
                 second,
                 not second,
+                inners if last and not second else (),
             )
             if len(sums) >= 4:
-                mine = after(mine, sums[-3])
+                mine = after(mine, sums[-1 if last else -3])[0]
             sums += add_over_term(mine)
             inners.append(inner)
-        return sums, inners, arrived, other
-
-    sums, inners, _, _ = partials(vector, False)
-    inner = sum(inners[1:], inners[0])
-    for axis in ("sub", "blk", "term"):
+        if between and not late:
+            done = between(sums, arrived, other)
+        return sums, inners, done
+
+    sums, inners, _ = partials(vector, False, None)
+    if len(groups) > 1:
+        inner = sums[-2][-TAG:] + sums[-1][-TAG:]
+    else:
+        inner = small_sum(inners[0], "term")
+    for axis in ("sub", "blk"):
         inner = small_sum(inner, axis)
     raw = correct(table, [spans(group) for group in groups], inner, vector, diag, sums)
-    sums, _, arrived, other = partials(raw, True)
-    squares = raw[-TAG:] + other[-TAG:]
-    seen = set()
-    for piece in moving:
-        if piece[0] not in seen:
-            seen.add(piece[0])
-            squares = squares + arrived[piece][-TAG:]
-    scale = lax.rsqrt(jnp.sum(squares, axis=1, keepdims=True) / elements + 1e-06)
-    scale = jnp.broadcast_to(scale, squares.shape)
-    correction = scaled(table, scale, raw, slots, rows)
-    sigma = None
-    for at, group in enumerate(groups):
-        sigma = finish(
-            table, spans(group), scale, sums[2 * at], sums[2 * at + 1], sigma, slots, rows
+
+    def add_finished(sigma, scale, sums, at):
+        return finish(
+            table, spans(groups[at]), scale, sums[2 * at], sums[2 * at + 1], sigma, slots, rows
         )
+
+    def correction_and_more(sums, arrived, other):
+        squares = raw[-TAG:] + other[-TAG:]
+        first_of = {piece[0]: piece for piece in reversed(moving)}
+        for c in sorted(first_of):
+            squares = squares + arrived[first_of[c]][-TAG:]
+        scale = lax.rsqrt(jnp.sum(squares, axis=1, keepdims=True) / elements + 1e-06)
+        scale = jnp.broadcast_to(scale, squares.shape)
+        return scaled(table, scale, raw, slots, rows), scale, add_finished(None, scale, sums, 0)
+
+    sums, _, (correction, scale, sigma) = partials(raw, True, correction_and_more)
+    for at in range(1, len(groups)):
+        sigma = add_finished(sigma, scale, sums, at)
     return tuple(
         jnp.transpose(value.reshape(slots, roots, rows, width), (0, 2, 1, 3))
         for value in (sigma, correction)

time: 152 us -> 152 us (level)
  Pallas kernels: 57 us -> 51.3 us
  waiting for transfers between devices: 56.1 us -> 61.6 us
    pallas_call x9, Pallas kernels: 47.9 us -> 41.6 us  [the longest x4 34.5 us: sectors(): pl.pallas_call(functools.partial(sector_kernel, count, terms, unroll, not...]
    ppermute x13 -> x12, waiting for transfers between devices: 8.94 us -> 11.8 us  [flip(): return lax.ppermute(value, axis, [(i, i ^ bit) for i in range(size)])]
    ppermute x12, waiting for transfers between devices: 42.1 us -> 44.7 us  [relay(): lax.ppermute(value, 'blk', [(p, (p + c) % devices) for p in range(devices)])]
    ppermute x13 -> x12, starting transfers between devices: 13.5 us -> 13.3 us  [flip(): return lax.ppermute(value, axis, [(i, i ^ bit) for i in range(size)])]
  transfers between devices with their start and end apart: 27 -> 26, of which waited for: 11 -> 17; matrix products, arithmetic and copies ran while one was open for 0% -> 0% of each run, Pallas kernels for 28% -> 24%
where the time goes in v4:
time: 152 us
  waiting for transfers between devices  61.6 us (41%)
  Pallas kernels  51.3 us (34%)
  starting transfers between devices  35.3 us (23%)
  local copies, waits for them, and re-layouts  2.14 us (1%)
    ppermute x12, waiting for transfers between devices, relay(): lax.ppermute(value, 'blk', [(p, (p + c) % devices) for p in range(devices)])  44.7 us
    pallas_call x4, Pallas kernels, sectors(): pl.pallas_call(functools.partial(sector_kernel, count, terms, unroll, not...  34.5 us
    ppermute x12, starting transfers between devices, relay(): lax.ppermute(value, 'blk', [(p, (p + c) % devices) for p in range(devices)])  21.5 us
    ppermute x12, starting transfers between devices, flip(): return lax.ppermute(value, axis, [(i, i ^ bit) for i in range(size)])  13.3 us
    ppermute x12, waiting for transfers between devices, flip(): return lax.ppermute(value, axis, [(i, i ^ bit) for i in range(size)])  11.8 us
    pallas_call x8, Pallas kernels, combine(): pl.pallas_call(functools.partial(combine_kernel, share, starts[:-1], with...  6.89 us
    pallas_call x4, Pallas kernels, finish(): pl.pallas_call(functools.partial(finish_kernel, count, rows, places), out...  5.32 us
    ppermute x2, waiting for transfers between devices, partials(): other = lax.ppermute(own, 'sub', [(0, 1), (1, 0)])  5.12 us
  transfers between devices with their start and end apart: 26, of which 17 were waited for; matrix products, arithmetic and copies ran while one was open for 0% of the time, Pallas kernels for 24%

profile of v4, /device:TPU:0, one launch (start us, length us, event | category | flops | bytes accessed | tf_op | source)
XLA Modules:
  0.0 151.6 jit_solution(16906196403013544338)
XLA Ops:
  1.1 1.5 %shard_map.86.table = s32[57]{0:T(128)} custom-call(s32[16]{0:T(128)} %partner_ref.1, s32[8]{0:T(128)} %kind_ref.1), custom_call_target="tpu_custom_call" | custom-call | tf_op jit(solution)/shard_map/pallas_call | solution.py:75
  2.7 1.7 %collective-permute-done.refs_3_.refs_7_ = f32[3072,128]{1,0:T(8,128)S(1)} collective-permute-done((f32[3072,128]{1,0:T(8,128)}, f32[3072,128]{1,0:T(8,128)S(1)}, u32[]{:S(2)}, u32[]{:S(2)}) %collective-permute-start) | collective-permute-done | bytes 1572896 | tf_op jit(solution)/shard_map/ppermute | solution.py:485
  4.4 1.4 copy-done
  6.5 5.3 %sectors.4 = (f32[384,128]{1,0:T(8,128)S(1)}, f32[384,128]{1,0:T(8,128)S(1)}, f32[3072,128]{1,0:T(8,128)S(1)}) custom-call(s32[57]{0:T(128)S(1)} %copy-done.1, f32[8,16,64,128]{3,2,1,0:T(8,128)} %refs_4_.7, f32[8,16,128,128]{3,2,1,0:T(8,128)} %refs_5_.7, f32[3072,128]{1,0:T(8,128)S(1)} %bitcast.10, f32[3072,128]{1,0:T(8,128)S(1)} %collective-permute-done.refs_3_.refs_7_, ...), custom_call_target="tpu_custom_call" | custom-call | tf_op jit(solution)/shard_map/sectors/pallas_call | solution.py:204
  11.7 3.0 %collective-permute-start.1 = (f32[384,128]{1,0:T(8,128)S(1)}, f32[384,128]{1,0:T(8,128)S(1)}, u32[]{:S(2)}, u32[]{:S(2)}) collective-permute-start(f32[384,128]{1,0:T(8,128)S(1)} %get-tuple-element.58), channel_id=1, source_target_pairs={{0,4},{4,8},{8,12},{12,0},{1,5},{5,9},{9,13},{13,1},{2,6},{6,10},{... | collective-permute-start | bytes 589832 | tf_op jit(solution)/shard_map/ppermute | solution.py:482
  14.7 2.1 %collective-permute-start.3 = (f32[384,128]{1,0:T(8,128)S(1)}, f32[384,128]{1,0:T(8,128)S(1)}, u32[]{:S(2)}, u32[]{:S(2)}) collective-permute-start(f32[384,128]{1,0:T(8,128)S(1)} %get-tuple-element.62), channel_id=1, source_target_pairs={{0,12},{4,0},{8,4},{12,8},{1,13},{5,1},{9,5},{13,9},{2,14},{6,2},{... | collective-permute-start | bytes 589832 | tf_op jit(solution)/shard_map/ppermute | solution.py:482
  17.0 12.0 %sectors.5 = (f32[384,128]{1,0:T(8,128)S(1)}, f32[384,128]{1,0:T(8,128)S(1)}, f32[384,128]{1,0:T(8,128)S(1)}, f32[384,128]{1,0:T(8,128)S(1)}, f32[768,128]{1,0:T(8,128)S(1)}, /*index=5*/f32[3072,128]{1,0:T(8,128)S(1)}) custom-call(s32[57]{0:T(128)S(1)} %copy-done.1, f32[8,16,64,128]{3,2,1,0:T(8,128)} %refs_4_.7, ...), custom_call_target="tpu_custom_call", output_to_operand_aliasing={{5}: (9, {})} | custom-call | tf_op jit(solution)/shard_map/sectors/pallas_call | solution.py:204
  29.1 1.2 combine.8
  30.2 1.7 %collective-permute-start.6 = (f32[1536,128]{1,0:T(8,128)S(1)}, f32[1536,128]{1,0:T(8,128)S(1)}, u32[]{:S(2)}, u32[]{:S(2)}) collective-permute-start(f32[1536,128]{1,0:T(8,128)S(1)} %get-tuple-element.67.rest_0_), channel_id=1, source_target_pairs={{0,2},{2,0},{1,3},{3,1},{4,6},{6,4},{5,7},{7,5},{8,10},{10,8},{9,1... | collective-permute-start | bytes 2359304 | tf_op jit(solution)/shard_map/ppermute | solution.py:25
  31.9 3.8 %collective-permute-start.4 = (f32[384,128]{1,0:T(8,128)S(1)}, f32[384,128]{1,0:T(8,128)S(1)}, u32[]{:S(2)}, u32[]{:S(2)}) collective-permute-start(f32[384,128]{1,0:T(8,128)S(1)} %get-tuple-element.63), channel_id=1, source_target_pairs={{0,12},{4,0},{8,4},{12,8},{1,13},{5,1},{9,5},{13,9},{2,14},{6,2},{... | collective-permute-start | bytes 589832 | tf_op jit(solution)/shard_map/ppermute | solution.py:482
  35.8 5.8 %collective-permute-done.2.refs_0_ = f32[384,128]{1,0:T(8,128)S(1)} collective-permute-done((f32[384,128]{1,0:T(8,128)S(1)}, f32[384,128]{1,0:T(8,128)S(1)}, u32[]{:S(2)}, u32[]{:S(2)}) %collective-permute-start.2) | collective-permute-done | bytes 196640 | tf_op jit(solution)/shard_map/ppermute | solution.py:482
  41.6 0.8 collective-permute-done.4.refs_1_
  42.4 2.4 %collective-permute-start.5 = (f32[384,128]{1,0:T(8,128)S(1)}, f32[384,128]{1,0:T(8,128)S(1)}, u32[]{:S(2)}, u32[]{:S(2)}) collective-permute-start(f32[384,128]{1,0:T(8,128)S(1)} %get-tuple-element.64), channel_id=1, source_target_pairs={{0,8},{4,12},{8,0},{12,4},{1,9},{5,13},{9,1},{13,5},{2,10},{6,14},... | collective-permute-start | bytes 589832 | tf_op jit(solution)/shard_map/ppermute | solution.py:482
  44.8 0.8 combine.9
  45.6 7.0 %collective-permute-done.5.refs_0_ = f32[384,128]{1,0:T(8,128)S(1)} collective-permute-done((f32[384,128]{1,0:T(8,128)S(1)}, f32[384,128]{1,0:T(8,128)S(1)}, u32[]{:S(2)}, u32[]{:S(2)}) %collective-permute-start.5) | collective-permute-done | bytes 196640 | tf_op jit(solution)/shard_map/ppermute | solution.py:482
  53.4 0.8 collective-permute-start.8
  54.2 10.6 %collective-permute-done.7.refs_0_ = f32[384,128]{1,0:T(8,128)S(1)} collective-permute-done((f32[384,128]{1,0:T(8,128)S(1)}, f32[384,128]{1,0:T(8,128)S(1)}, u32[]{:S(2)}, u32[]{:S(2)}) %collective-permute-start.7) | collective-permute-done | bytes 196640 | tf_op jit(solution)/shard_map/ppermute | solution.py:482
  64.8 1.3 combine.11
  66.7 1.4 collective-permute-start.14
  68.1 5.9 %collective-permute-done.9.rest_7_ = f32[392,128]{1,0:T(8,128)S(1)} collective-permute-done((f32[392,128]{1,0:T(8,128)S(1)}, f32[392,128]{1,0:T(8,128)S(1)}, u32[]{:S(2)}, u32[]{:S(2)}) %collective-permute-start.9) | collective-permute-done | bytes 200736 | tf_op jit(solution)/shard_map/ppermute | solution.py:25
  74.0 1.2 collective-permute-done.10
  75.1 1.1 collective-permute-start.13
  76.3 3.3 %collective-permute-start.11 = (f32[8,128]{1,0:T(8,128)S(1)}, f32[8,128]{1,0:T(8,128)S(1)}, u32[]{:S(2)}, u32[]{:S(2)}) collective-permute-start(f32[8,128]{1,0:T(8,128)S(1)} %add.52), channel_id=1, source_target_pairs={{0,4},{4,0},{8,12},{12,8},{1,5},{5,1},{9,13},{13,9},{2,6},{6,2},{1... | collective-permute-start | bytes 12296 | tf_op jit(solution)/shard_map/ppermute | solution.py:25
  79.5 1.0 collective-permute-done.13
  81.2 1.2 correct.1.refs_2_.refs_6_.refs_8_.vector_ref.raw_ref
  82.5 3.4 %collective-permute-done.15.refs_3_.refs_7_.refs_9_ = f32[3080,128]{1,0:T(8,128)S(1)} collective-permute-done((f32[3080,128]{1,0:T(8,128)S(1)}, f32[3080,128]{1,0:T(8,128)S(1)}, u32[]{:S(2)}, u32[]{:S(2)}) %collective-permute-start.15) | collective-permute-done | bytes 1576992 | tf_op jit(solution)/shard_map/ppermute | solution.py:485
  85.9 5.3 %sectors.6 = (f32[392,128]{1,0:T(8,128)S(1)}, f32[392,128]{1,0:T(8,128)S(1)}, f32[3072,128]{1,0:T(8,128)S(1)}) custom-call(s32[57]{0:T(128)S(1)} %copy-done.1, f32[8,16,64,128]{3,2,1,0:T(8,128)} %refs_4_.7, f32[8,16,128,128]{3,2,1,0:T(8,128)} %refs_5_.7, f32[3080,128]{1,0:T(8,128)S(1)} %correct.1.refs_2_.refs_6_.refs_8_.vector_ref.raw_ref, ...), custom_call_target="tpu_custom_call" | custom-call | tf_op jit(solution)/shard_map/sectors/pallas_call | solution.py:204
  91.2 2.0 %collective-permute-start.16 = (f32[392,128]{1,0:T(8,128)S(1)}, f32[392,128]{1,0:T(8,128)S(1)}, u32[]{:S(2)}, u32[]{:S(2)}) collective-permute-start(f32[392,128]{1,0:T(8,128)S(1)} %get-tuple-element.85), channel_id=1, source_target_pairs={{0,4},{4,8},{8,12},{12,0},{1,5},{5,9},{9,13},{13,1},{2,6},{6,10},{... | collective-permute-start | bytes 602120 | tf_op jit(solution)/shard_map/ppermute | solution.py:482
  93.2 1.9 %collective-permute-start.18 = (f32[392,128]{1,0:T(8,128)S(1)}, f32[392,128]{1,0:T(8,128)S(1)}, u32[]{:S(2)}, u32[]{:S(2)}) collective-permute-start(f32[392,128]{1,0:T(8,128)S(1)} %get-tuple-element.89), channel_id=1, source_target_pairs={{0,12},{4,0},{8,4},{12,8},{1,13},{5,1},{9,5},{13,9},{2,14},{6,2},{... | collective-permute-start | bytes 602120 | tf_op jit(solution)/shard_map/ppermute | solution.py:482
  95.1 12.0 %sectors.7 = (f32[392,128]{1,0:T(8,128)S(1)}, f32[392,128]{1,0:T(8,128)S(1)}, f32[392,128]{1,0:T(8,128)S(1)}, f32[392,128]{1,0:T(8,128)S(1)}, f32[768,128]{1,0:T(8,128)S(1)}, /*index=5*/f32[3072,128]{1,0:T(8,128)S(1)}) custom-call(s32[57]{0:T(128)S(1)} %copy-done.1, f32[8,16,64,128]{3,2,1,0:T(8,128)} %refs_4_.7, ...), custom_call_target="tpu_custom_call", output_to_operand_aliasing={{5}: (11, {})} | custom-call | tf_op jit(solution)/shard_map/sectors/pallas_call | solution.py:204
  107.1 0.9 combine.12.mine_ref
  108.0 0.9 collective-permute-start.21
  108.9 3.8 %collective-permute-start.19 = (f32[392,128]{1,0:T(8,128)S(1)}, f32[392,128]{1,0:T(8,128)S(1)}, u32[]{:S(2)}, u32[]{:S(2)}) collective-permute-start(f32[392,128]{1,0:T(8,128)S(1)} %get-tuple-element.90), channel_id=1, source_target_pairs={{0,12},{4,0},{8,4},{12,8},{1,13},{5,1},{9,5},{13,9},{2,14},{6,2},{... | collective-permute-start | bytes 602120 | tf_op jit(solution)/shard_map/ppermute | solution.py:482
  112.7 5.9 %collective-permute-done.17.refs_0_ = f32[392,128]{1,0:T(8,128)S(1)} collective-permute-done((f32[392,128]{1,0:T(8,128)S(1)}, f32[392,128]{1,0:T(8,128)S(1)}, u32[]{:S(2)}, u32[]{:S(2)}) %collective-permute-start.17) | collective-permute-done | bytes 200736 | tf_op jit(solution)/shard_map/ppermute | solution.py:482
  118.6 0.8 collective-permute-done.19.refs_1_
  119.4 2.4 %collective-permute-start.20 = (f32[392,128]{1,0:T(8,128)S(1)}, f32[392,128]{1,0:T(8,128)S(1)}, u32[]{:S(2)}, u32[]{:S(2)}) collective-permute-start(f32[392,128]{1,0:T(8,128)S(1)} %get-tuple-element.91), channel_id=1, source_target_pairs={{0,8},{4,12},{8,0},{12,4},{1,9},{5,13},{9,1},{13,5},{2,10},{6,14},... | collective-permute-start | bytes 602120 | tf_op jit(solution)/shard_map/ppermute | solution.py:482
  121.8 0.7 combine.13.mine_ref
  122.5 1.3 collective-permute-start.25
  123.8 5.9 %collective-permute-done.20.refs_0_ = f32[392,128]{1,0:T(8,128)S(1)} collective-permute-done((f32[392,128]{1,0:T(8,128)S(1)}, f32[392,128]{1,0:T(8,128)S(1)}, u32[]{:S(2)}, u32[]{:S(2)}) %collective-permute-start.20) | collective-permute-done | bytes 200736 | tf_op jit(solution)/shard_map/ppermute | solution.py:482
  130.4 1.3 collective-permute-start.23
  131.8 1.8 %scaled.1 = f32[3072,128]{1,0:T(8,128)} custom-call(s32[57]{0:T(128)S(1)} %copy-done.1, f32[8,128]{1,0:T(8,128)S(1)} %broadcast_in_dim.2.scale_ref, f32[3080,128]{1,0:T(8,128)S(1)} %correct.1.refs_2_.refs_6_.refs_8_.vector_ref.raw_ref), custom_call_target="tpu_custom_call" | custom-call | tf_op jit(solution)/shard_map/scaled/pallas_call | solution.py:387
  133.6 1.5 finish.4.rest_0_
  135.1 8.0 %collective-permute-done.22.refs_0_ = f32[392,128]{1,0:T(8,128)S(1)} collective-permute-done((f32[392,128]{1,0:T(8,128)S(1)}, f32[392,128]{1,0:T(8,128)S(1)}, u32[]{:S(2)}, u32[]{:S(2)}) %collective-permute-start.22) | collective-permute-done | bytes 200736 | tf_op jit(solution)/shard_map/ppermute | solution.py:482
  143.7 0.9 collective-permute-start.24
  144.6 1.3 finish.5.rest_0_
  146.0 1.2 finish.6.rest_0_
  147.2 3.1 %collective-permute-done.24.theirs_ref = f32[384,128]{1,0:T(8,128)S(1)} collective-permute-done((f32[384,128]{1,0:T(8,128)S(1)}, f32[384,128]{1,0:T(8,128)S(1)}, u32[]{:S(2)}, u32[]{:S(2)}) %collective-permute-start.24) | collective-permute-done | bytes 196640 | tf_op jit(solution)/shard_map/ppermute | solution.py:25
  150.3 1.2 finish.7
  (38 shorter events, 5.0 us)
Async XLA Ops:
  0.6 3.8 %collective-permute-start = (f32[3072,128]{1,0:T(8,128)}, f32[3072,128]{1,0:T(8,128)S(1)}, u32[]{:S(2)}, u32[]{:S(2)}) collective-permute-start(f32[3072,128]{1,0:T(8,128)} %bitcast.9), channel_id=1, source_target_pairs={{0,1},{1,0},{2,3},{3,2},{4,5},{5,4},{6,7},{7,6},{8,9},{9,8},{10,11... | collective-permute-start | bytes 4718600 | tf_op jit(solution)/shard_map/ppermute | solution.py:485
  4.4 1.4 copy-start
  5.8 0.7 copy-start.1
  6.5 10.4 %copy-start.2 = (f32[16,128]{1,0:T(8,128)S(1)}, f32[16,128]{1,0:T(8,128)}, u32[]{:S(2)}) copy-start(f32[16,128]{1,0:T(8,128)} %param.13) | copy-start | bytes 24580
  6.5 10.4 %copy-start.3 = (f32[16,64]{1,0:T(8,128)S(1)}, f32[16,64]{1,0:T(8,128)}, u32[]{:S(2)}) copy-start(f32[16,64]{1,0:T(8,128)} %param.12) | copy-start | bytes 12292
  11.7 17.3 %collective-permute-start.1 = (f32[384,128]{1,0:T(8,128)S(1)}, f32[384,128]{1,0:T(8,128)S(1)}, u32[]{:S(2)}, u32[]{:S(2)}) collective-permute-start(f32[384,128]{1,0:T(8,128)S(1)} %get-tuple-element.58), channel_id=1, source_target_pairs={{0,4},{4,8},{8,12},{12,0},{1,5},{5,9},{9,13},{13,1},{2,6},{6,10},{... | collective-permute-start | bytes 589832 | tf_op jit(solution)/shard_map/ppermute | solution.py:482
  14.7 14.3 %collective-permute-start.3 = (f32[384,128]{1,0:T(8,128)S(1)}, f32[384,128]{1,0:T(8,128)S(1)}, u32[]{:S(2)}, u32[]{:S(2)}) collective-permute-start(f32[384,128]{1,0:T(8,128)S(1)} %get-tuple-element.62), channel_id=1, source_target_pairs={{0,12},{4,0},{8,4},{12,8},{1,13},{5,1},{9,5},{13,9},{2,14},{6,2},{... | collective-permute-start | bytes 589832 | tf_op jit(solution)/shard_map/ppermute | solution.py:482
  30.2 23.1 %collective-permute-start.6 = (f32[1536,128]{1,0:T(8,128)S(1)}, f32[1536,128]{1,0:T(8,128)S(1)}, u32[]{:S(2)}, u32[]{:S(2)}) collective-permute-start(f32[1536,128]{1,0:T(8,128)S(1)} %get-tuple-element.67.rest_0_), channel_id=1, source_target_pairs={{0,2},{2,0},{1,3},{3,1},{4,6},{6,4},{5,7},{7,5},{8,10},{10,8},{9,1... | collective-permute-start | bytes 2359304 | tf_op jit(solution)/shard_map/ppermute | solution.py:25
  31.9 9.6 %collective-permute-start.2 = (f32[384,128]{1,0:T(8,128)S(1)}, f32[384,128]{1,0:T(8,128)S(1)}, u32[]{:S(2)}, u32[]{:S(2)}) collective-permute-start(f32[384,128]{1,0:T(8,128)S(1)} %get-tuple-element.59), channel_id=1, source_target_pairs={{0,4},{4,8},{8,12},{12,0},{1,5},{5,9},{9,13},{13,1},{2,6},{6,10},{... | collective-permute-start | bytes 589832 | tf_op jit(solution)/shard_map/ppermute | solution.py:482
  31.9 10.4 %collective-permute-start.4 = (f32[384,128]{1,0:T(8,128)S(1)}, f32[384,128]{1,0:T(8,128)S(1)}, u32[]{:S(2)}, u32[]{:S(2)}) collective-permute-start(f32[384,128]{1,0:T(8,128)S(1)} %get-tuple-element.63), channel_id=1, source_target_pairs={{0,12},{4,0},{8,4},{12,8},{1,13},{5,1},{9,5},{13,9},{2,14},{6,2},{... | collective-permute-start | bytes 589832 | tf_op jit(solution)/shard_map/ppermute | solution.py:482
  42.4 10.2 %collective-permute-start.5 = (f32[384,128]{1,0:T(8,128)S(1)}, f32[384,128]{1,0:T(8,128)S(1)}, u32[]{:S(2)}, u32[]{:S(2)}) collective-permute-start(f32[384,128]{1,0:T(8,128)S(1)} %get-tuple-element.64), channel_id=1, source_target_pairs={{0,8},{4,12},{8,0},{12,4},{1,9},{5,13},{9,1},{13,5},{2,10},{6,14},... | collective-permute-start | bytes 589832 | tf_op jit(solution)/shard_map/ppermute | solution.py:482
  53.3 11.5 %collective-permute-start.7 = (f32[384,128]{1,0:T(8,128)S(1)}, f32[384,128]{1,0:T(8,128)S(1)}, u32[]{:S(2)}, u32[]{:S(2)}) collective-permute-start(f32[384,128]{1,0:T(8,128)S(1)} %get-tuple-element.73), channel_id=1, source_target_pairs={{0,8},{4,12},{8,0},{12,4},{1,9},{5,13},{9,1},{13,5},{2,10},{6,14},... | collective-permute-start | bytes 589832 | tf_op jit(solution)/shard_map/ppermute | solution.py:482
  53.4 12.7 %collective-permute-start.8 = (f32[384,128]{1,0:T(8,128)S(1)}, f32[384,128]{1,0:T(8,128)S(1)}, u32[]{:S(2)}, u32[]{:S(2)}) collective-permute-start(f32[384,128]{1,0:T(8,128)S(1)} %get-tuple-element.72.rest_4_), channel_id=1, source_target_pairs={{0,2},{2,0},{1,3},{3,1},{4,6},{6,4},{5,7},{7,5},{8,10},{10,8},{9,1... | collective-permute-start | bytes 589832 | tf_op jit(solution)/shard_map/ppermute | solution.py:25
  66.0 7.9 %collective-permute-start.9 = (f32[392,128]{1,0:T(8,128)S(1)}, f32[392,128]{1,0:T(8,128)S(1)}, u32[]{:S(2)}, u32[]{:S(2)}) collective-permute-start(f32[392,128]{1,0:T(8,128)S(1)} %get-tuple-element.79.rest_6_), channel_id=1, source_target_pairs={{0,2},{2,0},{1,3},{3,1},{4,6},{6,4},{5,7},{7,5},{8,10},{10,8},{9,1... | collective-permute-start | bytes 602120 | tf_op jit(solution)/shard_map/ppermute | solution.py:25
  66.7 14.5 %collective-permute-start.14 = (f32[768,128]{1,0:T(8,128)S(1)}, f32[768,128]{1,0:T(8,128)S(1)}, u32[]{:S(2)}, u32[]{:S(2)}) collective-permute-start(f32[768,128]{1,0:T(8,128)S(1)} %get-tuple-element.69.rest_2_), channel_id=1, source_target_pairs={{0,2},{2,0},{1,3},{3,1},{4,6},{6,4},{5,7},{7,5},{8,10},{10,8},{9,1... | collective-permute-start | bytes 1179656 | tf_op jit(solution)/shard_map/ppermute | solution.py:25
  74.0 1.2 collective-permute-start.10
  75.1 5.4 %collective-permute-start.13 = (f32[8,128]{1,0:T(8,128)S(1)}, f32[8,128]{1,0:T(8,128)S(1)}, u32[]{:S(2)}, u32[]{:S(2)}) collective-permute-start(f32[8,128]{1,0:T(8,128)S(1)} %add.52), channel_id=1, source_target_pairs={{0,12},{4,8},{8,4},{12,0},{1,13},{5,9},{9,5},{13,1},{2,14},{6,10},... | collective-permute-start | bytes 12296 | tf_op jit(solution)/shard_map/ppermute | solution.py:25
  76.3 4.5 %collective-permute-start.12 = (f32[8,128]{1,0:T(8,128)S(1)}, f32[8,128]{1,0:T(8,128)S(1)}, u32[]{:S(2)}, u32[]{:S(2)}) collective-permute-start(f32[8,128]{1,0:T(8,128)S(1)} %add.52), channel_id=1, source_target_pairs={{0,8},{4,12},{8,0},{12,4},{1,9},{5,13},{9,1},{13,5},{2,10},{6,14},... | collective-permute-start | bytes 12296 | tf_op jit(solution)/shard_map/ppermute | solution.py:25
  76.3 4.8 %collective-permute-start.11 = (f32[8,128]{1,0:T(8,128)S(1)}, f32[8,128]{1,0:T(8,128)S(1)}, u32[]{:S(2)}, u32[]{:S(2)}) collective-permute-start(f32[8,128]{1,0:T(8,128)S(1)} %add.52), channel_id=1, source_target_pairs={{0,4},{4,0},{8,12},{12,8},{1,5},{5,1},{9,13},{13,9},{2,6},{6,2},{1... | collective-permute-start | bytes 12296 | tf_op jit(solution)/shard_map/ppermute | solution.py:25
  82.5 3.5 %collective-permute-start.15 = (f32[3080,128]{1,0:T(8,128)S(1)}, f32[3080,128]{1,0:T(8,128)S(1)}, u32[]{:S(2)}, u32[]{:S(2)}) collective-permute-start(f32[3080,128]{1,0:T(8,128)S(1)} %correct.1.refs_2_.refs_6_.refs_8_.vector_ref.raw_ref), channel_id=1, source_target_pairs={{0,1},{1,0},{2,3},{3,2},{4,5},{5,4},{6,7},{7,6},{8,9},{9,8},{10,11... | collective-permute-start | bytes 4730888 | tf_op jit(solution)/shard_map/ppermute | solution.py:485
  91.2 15.9 %collective-permute-start.16 = (f32[392,128]{1,0:T(8,128)S(1)}, f32[392,128]{1,0:T(8,128)S(1)}, u32[]{:S(2)}, u32[]{:S(2)}) collective-permute-start(f32[392,128]{1,0:T(8,128)S(1)} %get-tuple-element.85), channel_id=1, source_target_pairs={{0,4},{4,8},{8,12},{12,0},{1,5},{5,9},{9,13},{13,1},{2,6},{6,10},{... | collective-permute-start | bytes 602120 | tf_op jit(solution)/shard_map/ppermute | solution.py:482
  93.2 13.9 %collective-permute-start.18 = (f32[392,128]{1,0:T(8,128)S(1)}, f32[392,128]{1,0:T(8,128)S(1)}, u32[]{:S(2)}, u32[]{:S(2)}) collective-permute-start(f32[392,128]{1,0:T(8,128)S(1)} %get-tuple-element.89), channel_id=1, source_target_pairs={{0,12},{4,0},{8,4},{12,8},{1,13},{5,1},{9,5},{13,9},{2,14},{6,2},{... | collective-permute-start | bytes 602120 | tf_op jit(solution)/shard_map/ppermute | solution.py:482
  108.0 22.4 %collective-permute-start.21 = (f32[1536,128]{1,0:T(8,128)S(1)}, f32[1536,128]{1,0:T(8,128)S(1)}, u32[]{:S(2)}, u32[]{:S(2)}) collective-permute-start(f32[1536,128]{1,0:T(8,128)S(1)} %combine.12.mine_ref), channel_id=1, source_target_pairs={{0,2},{2,0},{1,3},{3,1},{4,6},{6,4},{5,7},{7,5},{8,10},{10,8},{9,1... | collective-permute-start | bytes 2359304 | tf_op jit(solution)/shard_map/ppermute | solution.py:25
  108.9 9.7 %collective-permute-start.17 = (f32[392,128]{1,0:T(8,128)S(1)}, f32[392,128]{1,0:T(8,128)S(1)}, u32[]{:S(2)}, u32[]{:S(2)}) collective-permute-start(f32[392,128]{1,0:T(8,128)S(1)} %get-tuple-element.86), channel_id=1, source_target_pairs={{0,4},{4,8},{8,12},{12,0},{1,5},{5,9},{9,13},{13,1},{2,6},{6,10},{... | collective-permute-start | bytes 602120 | tf_op jit(solution)/shard_map/ppermute | solution.py:482
  108.9 10.5 %collective-permute-start.19 = (f32[392,128]{1,0:T(8,128)S(1)}, f32[392,128]{1,0:T(8,128)S(1)}, u32[]{:S(2)}, u32[]{:S(2)}) collective-permute-start(f32[392,128]{1,0:T(8,128)S(1)} %get-tuple-element.90), channel_id=1, source_target_pairs={{0,12},{4,0},{8,4},{12,8},{1,13},{5,1},{9,5},{13,9},{2,14},{6,2},{... | collective-permute-start | bytes 602120 | tf_op jit(solution)/shard_map/ppermute | solution.py:482
  119.4 10.3 %collective-permute-start.20 = (f32[392,128]{1,0:T(8,128)S(1)}, f32[392,128]{1,0:T(8,128)S(1)}, u32[]{:S(2)}, u32[]{:S(2)}) collective-permute-start(f32[392,128]{1,0:T(8,128)S(1)} %get-tuple-element.91), channel_id=1, source_target_pairs={{0,8},{4,12},{8,0},{12,4},{1,9},{5,13},{9,1},{13,5},{2,10},{6,14},... | collective-permute-start | bytes 602120 | tf_op jit(solution)/shard_map/ppermute | solution.py:482
  122.5 22.1 %collective-permute-start.25 = (f32[768,128]{1,0:T(8,128)S(1)}, f32[768,128]{1,0:T(8,128)S(1)}, u32[]{:S(2)}, u32[]{:S(2)}) collective-permute-start(f32[768,128]{1,0:T(8,128)S(1)} %combine.13.mine_ref), channel_id=1, source_target_pairs={{0,2},{2,0},{1,3},{3,1},{4,6},{6,4},{5,7},{7,5},{8,10},{10,8},{9,1... | collective-permute-start | bytes 1179656 | tf_op jit(solution)/shard_map/ppermute | solution.py:25
  130.4 13.3 %collective-permute-start.23 = (f32[384,128]{1,0:T(8,128)S(1)}, f32[384,128]{1,0:T(8,128)S(1)}, u32[]{:S(2)}, u32[]{:S(2)}) collective-permute-start(f32[384,128]{1,0:T(8,128)S(1)} %combine.14.mine_ref), channel_id=1, source_target_pairs={{0,2},{2,0},{1,3},{3,1},{4,6},{6,4},{5,7},{7,5},{8,10},{10,8},{9,1... | collective-permute-start | bytes 589832 | tf_op jit(solution)/shard_map/ppermute | solution.py:25
  131.7 11.4 %collective-permute-start.22 = (f32[392,128]{1,0:T(8,128)S(1)}, f32[392,128]{1,0:T(8,128)S(1)}, u32[]{:S(2)}, u32[]{:S(2)}) collective-permute-start(f32[392,128]{1,0:T(8,128)S(1)} %get-tuple-element.97), channel_id=1, source_target_pairs={{0,8},{4,12},{8,0},{12,4},{1,9},{5,13},{9,1},{13,5},{2,10},{6,14},... | collective-permute-start | bytes 602120 | tf_op jit(solution)/shard_map/ppermute | solution.py:482
  143.7 6.6 %collective-permute-start.24 = (f32[384,128]{1,0:T(8,128)S(1)}, f32[384,128]{1,0:T(8,128)S(1)}, u32[]{:S(2)}, u32[]{:S(2)}) collective-permute-start(f32[384,128]{1,0:T(8,128)S(1)} %combine.15.mine_ref), channel_id=1, source_target_pairs={{0,2},{2,0},{1,3},{3,1},{4,6},{6,4},{5,7},{7,5},{8,10},{10,8},{9,1... | collective-permute-start | bytes 589832 | tf_op jit(solution)/shard_map/ppermute | solution.py:25

commit v5 on v4

--- a/solution.py
+++ b/solution.py
@@ -81,7 +81,7 @@
     )(partner, term_kind)
 
 
-def sector(table, count, terms, joined, l_ref, r_ref, own_ref, other_ref, lhs, high_rhs, low_rhs):
+def sector(table, count, terms, turned, l_ref, r_ref, own_ref, other_ref, lhs, high_rhs, low_rhs):
     rows, width = l_ref.shape[2], r_ref.shape[3]
     roots = own_ref.shape[0] // rows
     first = table[3 * count + terms] == 0
@@ -95,13 +95,8 @@
         at = slice(r * rows, (r + 1) * rows)
         one = jnp.concatenate(halves(jnp.concatenate([top[at], bottom[at]], axis=0)), axis=1)
         wide.append(jnp.concatenate([one, one], axis=0))
-    if joined:
-        every = jnp.dot(left, jnp.concatenate(wide, axis=1), preferred_element_type=jnp.float32)
     for r in range(roots):
-        if joined:
-            both = every[:, 2 * r * width : 2 * (r + 1) * width]
-        else:
-            both = jnp.dot(left, wide[r], preferred_element_type=jnp.float32)
+        both = jnp.dot(left, wide[r], preferred_element_type=jnp.float32)
         high, low = halves(both[:, :width] + both[:, width:])
         for k in range(terms):
             lanes = slice(k * width, (k + 1) * width)
@@ -112,10 +107,11 @@
         lanes = slice(k * width, (k + 1) * width)
         kind = table[3 * count + k]
         used = pl.ds(pl.multiple_of((1 - kind) * width, width), width)
-        high, low = halves(r_ref[k, 0])
-        high_rhs[used, lanes] = high
-        low_rhs[used, lanes] = low
-    dims = (((1,), (1,)), ((), ()))
+        high, low = halves(r_ref[k, 0].T if turned else r_ref[k, 0])
+        to = (lanes, used) if turned else (used, lanes)
+        high_rhs[to] = high
+        low_rhs[to] = low
+    dims = (((1,), (0 if turned else 1,)), ((), ()))
     tall = lax.dot_general(lhs[...], high_rhs[...], dims, preferred_element_type=jnp.float32)
     short = lax.dot_general(
         lhs[: roots * rows], low_rhs[...], dims, preferred_element_type=jnp.float32
@@ -123,7 +119,7 @@
     return tall[: roots * rows] + tall[roots * rows :] + short
 
 
-def sector_kernel(count, terms, unroll, joined, starts, tags, table, *refs):
+def sector_kernel(count, terms, unroll, turned, starts, tags, table, *refs):
     inputs, scratch = refs[: 4 * unroll], refs[-3 * unroll :]
     outputs = refs[-3 * unroll - len(starts) : -3 * unroll]
     tag_refs = refs[4 * unroll : 4 * unroll + 2]
@@ -134,8 +130,8 @@
 
     @pl.when(step == 0)
     def _():
-        for ref in scratch:
-            if ref.shape[0] == 2 * width:
+        for at, ref in enumerate(scratch):
+            if at % 3:
                 ref[...] = jnp.zeros_like(ref)
         if any(tags):
             tag = tag_refs[0][...] + tag_refs[1][...]
@@ -144,7 +140,7 @@
                     ref[(end - begin) * unroll * height :] = tag
 
     results = [
-        sector(table, count, terms, joined, *inputs[4 * u : 4 * u + 4], *scratch[3 * u : 3 * u + 3])
+        sector(table, count, terms, turned, *inputs[4 * u : 4 * u + 4], *scratch[3 * u : 3 * u + 3])
         for u in range(unroll)
     ]
     for u in range(unroll):
@@ -200,9 +196,10 @@
         in_specs.append(ANY)
         args.append(kept)
         aliases = {len(args): len(pieces)}
+    rhs = (terms * width, 2 * width) if ordered else (2 * width, terms * width)
     shapes = [(size * height + TAG * tagged, width) for (_, size), tagged in zip(pieces, tags)]
     out = pl.pallas_call(
-        functools.partial(sector_kernel, count, terms, unroll, not ordered, starts, tags),
+        functools.partial(sector_kernel, count, terms, unroll, ordered, starts, tags),
         out_shape=[
             jax.ShapeDtypeStruct(shape, jnp.float32)
             for shape in shapes + [(count * height, width)]
@@ -215,8 +212,8 @@
             + [pl.BlockSpec((unroll * height, width), lambda i, t: (place_of(i, units), 0))],
             scratch_shapes=[
                 pltpu.VMEM((2 * height, terms * width), jnp.bfloat16),
-                pltpu.VMEM((2 * width, terms * width), jnp.bfloat16),
-                pltpu.VMEM((2 * width, terms * width), jnp.bfloat16),
+                pltpu.VMEM(rhs, jnp.bfloat16),
+                pltpu.VMEM(rhs, jnp.bfloat16),
             ]
             * unroll,
         ),
@@ -461,19 +458,20 @@
     table = make_table(partner, term_kind)
     diag = left_diag[:, :, None] + right_diag[:, None, :]
 
-    cuts = [(0, per // 2), (per // 2, per - per // 2)] if per > 1 else [(0, per)]
-    staying, moving = (0, 0, per), []
-    for c in range(1, (devices + 1) // 2):
-        for start, size in cuts:
-            moving += [(c, c * per + start, size), (devices - c, (devices - c) * per + start, size)]
-    groups = [[staying] + moving[:2]] + [moving[i : i + 2] for i in range(2, len(moving), 2)]
+    staying = (0, 0, per)
+    pairs = [
+        [(c, c * per, per), (devices - c, (devices - c) * per, per)]
+        for c in range(1, (devices + 1) // 2)
+    ]
+    opposite = []
     if devices % 2 == 0:
         c = devices // 2
+        cuts = [(0, per // 2), (per // 2, per - per // 2)] if per > 1 else [(0, per)]
         opposite = [(c, c * per + start, size) for start, size in cuts]
-        groups += [[piece] for piece in opposite]
-        moving += opposite
+    groups = [[staying]] + pairs + [[piece] for piece in opposite]
+    moving = [piece for group in groups[1:] for piece in group]
     batches = [moving[:2], moving[2:] + [staying]]
-    late = len(groups) > 2 and per > 1 and devices % 2 == 0
+    late = len(opposite) == 2 and len(pairs) > 0
 
     def spans(pieces):
         return [piece[1:] for piece in pieces]
@@ -501,11 +499,9 @@
         for at, piece in enumerate(moving[:-1] if late else moving):
             value = outgoing[piece]
             if at >= 2:
-                value = after(value, arrived[moving[at - 2]])[0]
-                if 2 * piece[0] == devices:
-                    value = after(value, arrived[moving[at - 1]])[0]
+                value = after(value, arrived[moving[at - 2]], arrived[moving[at - 1]])[0]
             arrived[piece] = relay(value, piece[0])
-        arrived[staying] = after(outgoing[staying], *[arrived[piece] for piece in moving[:2]])[0]
+        arrived[staying] = outgoing[staying]
         for group in groups:
             if late and group == groups[-1]:
                 piece = group[0]
@@ -528,8 +524,8 @@
                 not second,
                 inners if last and not second else (),
             )
-            if len(sums) >= 4:
-                mine = after(mine, sums[-1 if last else -3])[0]
+            if len(sums) == 2 or last:
+                mine = after(mine, *sums[1::2][-2:])[0]
             sums += add_over_term(mine)
             inners.append(inner)
         if between and not late:

time: 152 us -> 147 us (0.967)
  starting transfers between devices: 35.3 us -> 21.7 us
  waiting for transfers between devices: 61.6 us -> 70.9 us
    ppermute x12 -> x8, starting transfers between devices: 21.5 us -> 9.93 us  [relay(): lax.ppermute(value, 'blk', [(p, (p + c) % devices) for p in range(devices)])]
    ppermute x12, waiting for transfers between devices: 11.8 us -> 17.8 us  [flip(): return lax.ppermute(value, axis, [(i, i ^ bit) for i in range(size)])]
    ppermute x12 -> x8, waiting for transfers between devices: 44.7 us -> 48.9 us  [relay(): lax.ppermute(value, 'blk', [(p, (p + c) % devices) for p in range(devices)])]
    ppermute x12, starting transfers between devices: 13.3 us -> 11.2 us  [flip(): return lax.ppermute(value, axis, [(i, i ^ bit) for i in range(size)])]
  transfers between devices with their start and end apart: 26 -> 22, of which waited for: 17 -> 17; matrix products, arithmetic and copies ran while one was open for 0% -> 1% of each run, Pallas kernels for 24% -> 21%
where the time goes in v5:
time: 147 us
  waiting for transfers between devices  70.9 us (48%)
  Pallas kernels  50 us (34%)
  starting transfers between devices  21.7 us (15%)
  local copies, waits for them, and re-layouts  2.13 us (1%)
    ppermute x8, waiting for transfers between devices, relay(): lax.ppermute(value, 'blk', [(p, (p + c) % devices) for p in range(devices)])  48.9 us
    pallas_call x4, Pallas kernels, sectors(): pl.pallas_call(functools.partial(sector_kernel, count, terms, unroll, ord...  33.4 us
    ppermute x12, waiting for transfers between devices, flip(): return lax.ppermute(value, axis, [(i, i ^ bit) for i in range(size)])  17.8 us
    ppermute x12, starting transfers between devices, flip(): return lax.ppermute(value, axis, [(i, i ^ bit) for i in range(size)])  11.2 us
    ppermute x8, starting transfers between devices, relay(): lax.ppermute(value, 'blk', [(p, (p + c) % devices) for p in range(devices)])  9.93 us
    pallas_call x8, Pallas kernels, combine(): pl.pallas_call(functools.partial(combine_kernel, share, starts[:-1], with...  6.73 us
    pallas_call x4, Pallas kernels, finish(): pl.pallas_call(functools.partial(finish_kernel, count, rows, places), out...  5.31 us
    ppermute x2, waiting for transfers between devices, partials(): other = lax.ppermute(own, 'sub', [(0, 1), (1, 0)])  4.2 us
  transfers between devices with their start and end apart: 22, of which 17 were waited for; matrix products, arithmetic and copies ran while one was open for 1% of the time, Pallas kernels for 21%

profile of v5, /device:TPU:0, one launch (start us, length us, event | category | flops | bytes accessed | tf_op | source)
XLA Modules:
  0.0 146.5 jit_solution(17187428747361841119)
XLA Ops:
  1.1 1.5 %shard_map.86.table = s32[57]{0:T(128)} custom-call(s32[16]{0:T(128)} %partner_ref.1, s32[8]{0:T(128)} %kind_ref.1), custom_call_target="tpu_custom_call" | custom-call | tf_op jit(solution)/shard_map/pallas_call | solution.py:75
  2.7 0.9 broadcast_add_fusion.diag_ref
  3.6 0.8 collective-permute-done.refs_3_.refs_7_
  4.4 1.4 copy-done
  5.8 0.7 copy-done.1
  6.5 8.5 %sectors.4 = (f32[768,128]{1,0:T(8,128)S(1)}, f32[768,128]{1,0:T(8,128)S(1)}, f32[3072,128]{1,0:T(8,128)S(1)}) custom-call(s32[57]{0:T(128)S(1)} %copy-done.1, f32[8,16,64,128]{3,2,1,0:T(8,128)} %refs_4_.7, f32[8,16,128,128]{3,2,1,0:T(8,128)} %refs_5_.7, f32[3072,128]{1,0:T(8,128)S(1)} %bitcast.10, f32[3072,128]{1,0:T(8,128)S(1)} %collective-permute-done.refs_3_.refs_7_, ...), custom_call_target="tpu_custom_call" | custom-call | tf_op jit(solution)/shard_map/sectors/pallas_call | solution.py:201
  15.0 3.0 %collective-permute-start.1 = (f32[768,128]{1,0:T(8,128)S(1)}, f32[768,128]{1,0:T(8,128)S(1)}, u32[]{:S(2)}, u32[]{:S(2)}) collective-permute-start(f32[768,128]{1,0:T(8,128)S(1)} %get-tuple-element.45), channel_id=1, source_target_pairs={{0,4},{4,8},{8,12},{12,0},{1,5},{5,9},{9,13},{13,1},{2,6},{6,10},{... | collective-permute-start | bytes 1179656 | tf_op jit(solution)/shard_map/ppermute | solution.py:480
  18.0 2.1 %collective-permute-start.2 = (f32[768,128]{1,0:T(8,128)S(1)}, f32[768,128]{1,0:T(8,128)S(1)}, u32[]{:S(2)}, u32[]{:S(2)}) collective-permute-start(f32[768,128]{1,0:T(8,128)S(1)} %get-tuple-element.46), channel_id=1, source_target_pairs={{0,12},{4,0},{8,4},{12,8},{1,13},{5,1},{9,5},{13,9},{2,14},{6,2},{... | collective-permute-start | bytes 1179656 | tf_op jit(solution)/shard_map/ppermute | solution.py:480
  20.1 8.6 %sectors.5 = (f32[384,128]{1,0:T(8,128)S(1)}, f32[384,128]{1,0:T(8,128)S(1)}, f32[768,128]{1,0:T(8,128)S(1)}, f32[3072,128]{1,0:T(8,128)S(1)}) custom-call(s32[57]{0:T(128)S(1)} %copy-done.1, f32[8,16,64,128]{3,2,1,0:T(8,128)} %refs_4_.7, f32[8,16,128,128]{3,2,1,0:T(8,128)} %refs_5_.7, f32[3072,128]{1,0:T(8,128)S(1)} %bitcast.12, ...), custom_call_target="tpu_custom_call", output_to_operand_aliasing={{3}: (9, {})} | custom-call | tf_op jit(solution)/shard_map/sectors/pallas_call | solution.py:201
  28.7 0.8 combine.8
  29.5 1.7 %collective-permute-start.4 = (f32[768,128]{1,0:T(8,128)S(1)}, f32[768,128]{1,0:T(8,128)S(1)}, u32[]{:S(2)}, u32[]{:S(2)}) collective-permute-start(f32[768,128]{1,0:T(8,128)S(1)} %get-tuple-element.49.rest_0_), channel_id=1, source_target_pairs={{0,2},{2,0},{1,3},{3,1},{4,6},{6,4},{5,7},{7,5},{8,10},{10,8},{9,1... | collective-permute-start | bytes 1179656 | tf_op jit(solution)/shard_map/ppermute | solution.py:25
  31.2 6.1 %collective-permute-done.2.refs_1_ = f32[768,128]{1,0:T(8,128)S(1)} collective-permute-done((f32[768,128]{1,0:T(8,128)S(1)}, f32[768,128]{1,0:T(8,128)S(1)}, u32[]{:S(2)}, u32[]{:S(2)}) %collective-permute-start.2) | collective-permute-done | bytes 393248 | tf_op jit(solution)/shard_map/ppermute | solution.py:480
  37.3 1.1 combine.9
  38.4 2.0 %collective-permute-done.4.rest_1_ = f32[768,128]{1,0:T(8,128)S(1)} collective-permute-done((f32[768,128]{1,0:T(8,128)S(1)}, f32[768,128]{1,0:T(8,128)S(1)}, u32[]{:S(2)}, u32[]{:S(2)}) %collective-permute-start.4) | collective-permute-done | bytes 393248 | tf_op jit(solution)/shard_map/ppermute | solution.py:25
  40.4 1.5 %collective-permute-start.6 = (f32[1536,128]{1,0:T(8,128)S(1)}, f32[1536,128]{1,0:T(8,128)S(1)}, u32[]{:S(2)}, u32[]{:S(2)}) collective-permute-start(f32[1536,128]{1,0:T(8,128)S(1)} %get-tuple-element.52.rest_2_), channel_id=1, source_target_pairs={{0,2},{2,0},{1,3},{3,1},{4,6},{6,4},{5,7},{7,5},{8,10},{10,8},{9,1... | collective-permute-start | bytes 2359304 | tf_op jit(solution)/shard_map/ppermute | solution.py:25
  41.9 0.7 collective-permute-start.3
  42.6 9.6 %collective-permute-done.3.refs_0_ = f32[384,128]{1,0:T(8,128)S(1)} collective-permute-done((f32[384,128]{1,0:T(8,128)S(1)}, f32[384,128]{1,0:T(8,128)S(1)}, u32[]{:S(2)}, u32[]{:S(2)}) %collective-permute-start.3) | collective-permute-done | bytes 196640 | tf_op jit(solution)/shard_map/ppermute | solution.py:480
  52.2 0.7 combine.10
  53.6 9.8 %collective-permute-done.5.refs_0_ = f32[384,128]{1,0:T(8,128)S(1)} collective-permute-done((f32[384,128]{1,0:T(8,128)S(1)}, f32[384,128]{1,0:T(8,128)S(1)}, u32[]{:S(2)}, u32[]{:S(2)}) %collective-permute-start.5) | collective-permute-done | bytes 196640 | tf_op jit(solution)/shard_map/ppermute | solution.py:480
  63.4 1.3 combine.11
  65.2 6.4 %collective-permute-done.8.rest_7_ = f32[392,128]{1,0:T(8,128)S(1)} collective-permute-done((f32[392,128]{1,0:T(8,128)S(1)}, f32[392,128]{1,0:T(8,128)S(1)}, u32[]{:S(2)}, u32[]{:S(2)}) %collective-permute-start.8) | collective-permute-done | bytes 200736 | tf_op jit(solution)/shard_map/ppermute | solution.py:25
  71.6 1.2 collective-permute-done.9
  72.7 2.6 %collective-permute-start.12 = (f32[8,128]{1,0:T(8,128)S(1)}, f32[8,128]{1,0:T(8,128)S(1)}, u32[]{:S(2)}, u32[]{:S(2)}) collective-permute-start(f32[8,128]{1,0:T(8,128)S(1)} %add.52), channel_id=1, source_target_pairs={{0,12},{4,8},{8,4},{12,0},{1,13},{5,9},{9,5},{13,1},{2,14},{6,10},... | collective-permute-start | bytes 12296 | tf_op jit(solution)/shard_map/ppermute | solution.py:25
  75.3 0.9 collective-permute-start.10
  76.2 1.0 collective-permute-done.11
  77.2 0.9 collective-permute-done.12
  78.1 0.8 collective-permute-done.10
  78.9 1.2 correct.1.refs_2_.refs_6_.refs_8_.vector_ref.raw_ref
  80.2 3.4 %collective-permute-done.13.refs_3_.refs_7_.refs_9_ = f32[3080,128]{1,0:T(8,128)S(1)} collective-permute-done((f32[3080,128]{1,0:T(8,128)S(1)}, f32[3080,128]{1,0:T(8,128)S(1)}, u32[]{:S(2)}, u32[]{:S(2)}) %collective-permute-start.13) | collective-permute-done | bytes 1576992 | tf_op jit(solution)/shard_map/ppermute | solution.py:483
  83.6 8.1 %sectors.6 = (f32[776,128]{1,0:T(8,128)S(1)}, f32[776,128]{1,0:T(8,128)S(1)}, f32[3072,128]{1,0:T(8,128)S(1)}) custom-call(s32[57]{0:T(128)S(1)} %copy-done.1, f32[8,16,64,128]{3,2,1,0:T(8,128)} %refs_4_.7, f32[8,16,128,128]{3,2,1,0:T(8,128)} %refs_5_.7, f32[3080,128]{1,0:T(8,128)S(1)} %correct.1.refs_2_.refs_6_.refs_8_.vector_ref.raw_ref, ...), custom_call_target="tpu_custom_call" | custom-call | tf_op jit(solution)/shard_map/sectors/pallas_call | solution.py:201
  91.7 1.0 collective-permute-start.14
  92.7 2.9 %collective-permute-start.15 = (f32[776,128]{1,0:T(8,128)S(1)}, f32[776,128]{1,0:T(8,128)S(1)}, u32[]{:S(2)}, u32[]{:S(2)}) collective-permute-start(f32[776,128]{1,0:T(8,128)S(1)} %get-tuple-element.67), channel_id=1, source_target_pairs={{0,12},{4,0},{8,4},{12,8},{1,13},{5,1},{9,5},{13,9},{2,14},{6,2},{... | collective-permute-start | bytes 1191944 | tf_op jit(solution)/shard_map/ppermute | solution.py:480
  95.6 8.1 %sectors.7 = (f32[392,128]{1,0:T(8,128)S(1)}, f32[392,128]{1,0:T(8,128)S(1)}, f32[768,128]{1,0:T(8,128)S(1)}, f32[3072,128]{1,0:T(8,128)S(1)}) custom-call(s32[57]{0:T(128)S(1)} %copy-done.1, f32[8,16,64,128]{3,2,1,0:T(8,128)} %refs_4_.7, f32[8,16,128,128]{3,2,1,0:T(8,128)} %refs_5_.7, ...), custom_call_target="tpu_custom_call", output_to_operand_aliasing={{3}: (11, {})} | custom-call | tf_op jit(solution)/shard_map/sectors/pallas_call | solution.py:201
  103.8 0.7 combine.12.mine_ref
  105.7 6.5 %collective-permute-done.15.refs_1_ = f32[776,128]{1,0:T(8,128)S(1)} collective-permute-done((f32[776,128]{1,0:T(8,128)S(1)}, f32[776,128]{1,0:T(8,128)S(1)}, u32[]{:S(2)}, u32[]{:S(2)}) %collective-permute-start.15) | collective-permute-done | bytes 397344 | tf_op jit(solution)/shard_map/ppermute | solution.py:480
  112.2 0.9 combine.13.mine_ref
  113.1 2.0 %collective-permute-done.17.theirs_ref = f32[768,128]{1,0:T(8,128)S(1)} collective-permute-done((f32[768,128]{1,0:T(8,128)S(1)}, f32[768,128]{1,0:T(8,128)S(1)}, u32[]{:S(2)}, u32[]{:S(2)}) %collective-permute-start.17) | collective-permute-done | bytes 393248 | tf_op jit(solution)/shard_map/ppermute | solution.py:25
  115.9 10.2 %collective-permute-done.16.refs_0_ = f32[392,128]{1,0:T(8,128)S(1)} collective-permute-done((f32[392,128]{1,0:T(8,128)S(1)}, f32[392,128]{1,0:T(8,128)S(1)}, u32[]{:S(2)}, u32[]{:S(2)}) %collective-permute-start.16) | collective-permute-done | bytes 200736 | tf_op jit(solution)/shard_map/ppermute | solution.py:480
  126.2 0.6 combine.14.mine_ref
  126.8 1.5 %collective-permute-start.20 = (f32[384,128]{1,0:T(8,128)S(1)}, f32[384,128]{1,0:T(8,128)S(1)}, u32[]{:S(2)}, u32[]{:S(2)}) collective-permute-start(f32[384,128]{1,0:T(8,128)S(1)} %combine.14.mine_ref), channel_id=1, source_target_pairs={{0,2},{2,0},{1,3},{3,1},{4,6},{6,4},{5,7},{7,5},{8,10},{10,8},{9,1... | collective-permute-start | bytes 589832 | tf_op jit(solution)/shard_map/ppermute | solution.py:25
  128.6 1.8 %scaled.1 = f32[3072,128]{1,0:T(8,128)} custom-call(s32[57]{0:T(128)S(1)} %copy-done.1, f32[8,128]{1,0:T(8,128)S(1)} %broadcast_in_dim.2.scale_ref, f32[3080,128]{1,0:T(8,128)S(1)} %correct.1.refs_2_.refs_6_.refs_8_.vector_ref.raw_ref), custom_call_target="tpu_custom_call" | custom-call | tf_op jit(solution)/shard_map/scaled/pallas_call | solution.py:384
  130.4 1.3 finish.4.rest_0_
  131.7 6.0 %collective-permute-done.18.refs_0_ = f32[392,128]{1,0:T(8,128)S(1)} collective-permute-done((f32[392,128]{1,0:T(8,128)S(1)}, f32[392,128]{1,0:T(8,128)S(1)}, u32[]{:S(2)}, u32[]{:S(2)}) %collective-permute-start.18) | collective-permute-done | bytes 200736 | tf_op jit(solution)/shard_map/ppermute | solution.py:480
  137.7 0.6 combine.15.mine_ref
  139.0 1.5 %finish.5.rest_0_ = f32[3072,128]{1,0:T(8,128)} custom-call(s32[57]{0:T(128)S(1)} %copy-done.1, f32[8,128]{1,0:T(8,128)S(1)} %broadcast_in_dim.2.scale_ref, f32[1536,128]{1,0:T(8,128)S(1)} %combine.13.mine_ref, f32[1536,128]{1,0:T(8,128)S(1)} %collective-permute-done.19.theirs_ref, f32[3072,128]{1,0:T(8,128)} %finish.4.rest_0_), custom_call_target="tpu_custom_call", output_to_operand_aliasing={{}: (4, {})} | custom-call | tf_op jit(solution)/shard_map/finish/pallas_call | solution.py:421
  140.5 1.3 finish.6.rest_0_
  141.8 3.5 %collective-permute-done.21.theirs_ref = f32[384,128]{1,0:T(8,128)S(1)} collective-permute-done((f32[384,128]{1,0:T(8,128)S(1)}, f32[384,128]{1,0:T(8,128)S(1)}, u32[]{:S(2)}, u32[]{:S(2)}) %collective-permute-start.21) | collective-permute-done | bytes 196640 | tf_op jit(solution)/shard_map/ppermute | solution.py:25
  145.3 1.2 finish.7
  (26 shorter events, 4.6 us)
Async XLA Ops:
  0.6 3.8 %collective-permute-start = (f32[3072,128]{1,0:T(8,128)}, f32[3072,128]{1,0:T(8,128)S(1)}, u32[]{:S(2)}, u32[]{:S(2)}) collective-permute-start(f32[3072,128]{1,0:T(8,128)} %bitcast.9), channel_id=1, source_target_pairs={{0,1},{1,0},{2,3},{3,2},{4,5},{5,4},{6,7},{7,6},{8,9},{9,8},{10,11... | collective-permute-start | bytes 4718600 | tf_op jit(solution)/shard_map/ppermute | solution.py:483
  4.4 1.4 copy-start
  5.8 0.7 copy-start.1
  15.0 16.2 %collective-permute-start.1 = (f32[768,128]{1,0:T(8,128)S(1)}, f32[768,128]{1,0:T(8,128)S(1)}, u32[]{:S(2)}, u32[]{:S(2)}) collective-permute-start(f32[768,128]{1,0:T(8,128)S(1)} %get-tuple-element.45), channel_id=1, source_target_pairs={{0,4},{4,8},{8,12},{12,0},{1,5},{5,9},{9,13},{13,1},{2,6},{6,10},{... | collective-permute-start | bytes 1179656 | tf_op jit(solution)/shard_map/ppermute | solution.py:480
  18.0 19.3 %collective-permute-start.2 = (f32[768,128]{1,0:T(8,128)S(1)}, f32[768,128]{1,0:T(8,128)S(1)}, u32[]{:S(2)}, u32[]{:S(2)}) collective-permute-start(f32[768,128]{1,0:T(8,128)S(1)} %get-tuple-element.46), channel_id=1, source_target_pairs={{0,12},{4,0},{8,4},{12,8},{1,13},{5,1},{9,5},{13,9},{2,14},{6,2},{... | collective-permute-start | bytes 1179656 | tf_op jit(solution)/shard_map/ppermute | solution.py:480
  29.5 10.9 %collective-permute-start.4 = (f32[768,128]{1,0:T(8,128)S(1)}, f32[768,128]{1,0:T(8,128)S(1)}, u32[]{:S(2)}, u32[]{:S(2)}) collective-permute-start(f32[768,128]{1,0:T(8,128)S(1)} %get-tuple-element.49.rest_0_), channel_id=1, source_target_pairs={{0,2},{2,0},{1,3},{3,1},{4,6},{6,4},{5,7},{7,5},{8,10},{10,8},{9,1... | collective-permute-start | bytes 1179656 | tf_op jit(solution)/shard_map/ppermute | solution.py:25
  40.4 24.2 %collective-permute-start.6 = (f32[1536,128]{1,0:T(8,128)S(1)}, f32[1536,128]{1,0:T(8,128)S(1)}, u32[]{:S(2)}, u32[]{:S(2)}) collective-permute-start(f32[1536,128]{1,0:T(8,128)S(1)} %get-tuple-element.52.rest_2_), channel_id=1, source_target_pairs={{0,2},{2,0},{1,3},{3,1},{4,6},{6,4},{5,7},{7,5},{8,10},{10,8},{9,1... | collective-permute-start | bytes 2359304 | tf_op jit(solution)/shard_map/ppermute | solution.py:25
  41.9 10.3 %collective-permute-start.3 = (f32[384,128]{1,0:T(8,128)S(1)}, f32[384,128]{1,0:T(8,128)S(1)}, u32[]{:S(2)}, u32[]{:S(2)}) collective-permute-start(f32[384,128]{1,0:T(8,128)S(1)} %get-tuple-element.47), channel_id=1, source_target_pairs={{0,8},{4,12},{8,0},{12,4},{1,9},{5,13},{9,1},{13,5},{2,10},{6,14},... | collective-permute-start | bytes 589832 | tf_op jit(solution)/shard_map/ppermute | solution.py:480
  52.9 10.5 %collective-permute-start.5 = (f32[384,128]{1,0:T(8,128)S(1)}, f32[384,128]{1,0:T(8,128)S(1)}, u32[]{:S(2)}, u32[]{:S(2)}) collective-permute-start(f32[384,128]{1,0:T(8,128)S(1)} %get-tuple-element.55), channel_id=1, source_target_pairs={{0,8},{4,12},{8,0},{12,4},{1,9},{5,13},{9,1},{13,5},{2,10},{6,14},... | collective-permute-start | bytes 589832 | tf_op jit(solution)/shard_map/ppermute | solution.py:480
  53.0 11.7 %collective-permute-start.7 = (f32[384,128]{1,0:T(8,128)S(1)}, f32[384,128]{1,0:T(8,128)S(1)}, u32[]{:S(2)}, u32[]{:S(2)}) collective-permute-start(f32[384,128]{1,0:T(8,128)S(1)} %get-tuple-element.54.rest_4_), channel_id=1, source_target_pairs={{0,2},{2,0},{1,3},{3,1},{4,6},{6,4},{5,7},{7,5},{8,10},{10,8},{9,1... | collective-permute-start | bytes 589832 | tf_op jit(solution)/shard_map/ppermute | solution.py:25
  64.6 6.9 %collective-permute-start.8 = (f32[392,128]{1,0:T(8,128)S(1)}, f32[392,128]{1,0:T(8,128)S(1)}, u32[]{:S(2)}, u32[]{:S(2)}) collective-permute-start(f32[392,128]{1,0:T(8,128)S(1)} %get-tuple-element.61.rest_6_), channel_id=1, source_target_pairs={{0,2},{2,0},{1,3},{3,1},{4,6},{6,4},{5,7},{7,5},{8,10},{10,8},{9,1... | collective-permute-start | bytes 602120 | tf_op jit(solution)/shard_map/ppermute | solution.py:25
  71.6 1.2 collective-permute-start.9
  72.7 4.5 %collective-permute-start.11 = (f32[8,128]{1,0:T(8,128)S(1)}, f32[8,128]{1,0:T(8,128)S(1)}, u32[]{:S(2)}, u32[]{:S(2)}) collective-permute-start(f32[8,128]{1,0:T(8,128)S(1)} %add.52), channel_id=1, source_target_pairs={{0,8},{4,12},{8,0},{12,4},{1,9},{5,13},{9,1},{13,5},{2,10},{6,14},... | collective-permute-start | bytes 12296 | tf_op jit(solution)/shard_map/ppermute | solution.py:25
  72.7 5.4 %collective-permute-start.12 = (f32[8,128]{1,0:T(8,128)S(1)}, f32[8,128]{1,0:T(8,128)S(1)}, u32[]{:S(2)}, u32[]{:S(2)}) collective-permute-start(f32[8,128]{1,0:T(8,128)S(1)} %add.52), channel_id=1, source_target_pairs={{0,12},{4,8},{8,4},{12,0},{1,13},{5,9},{9,5},{13,1},{2,14},{6,10},... | collective-permute-start | bytes 12296 | tf_op jit(solution)/shard_map/ppermute | solution.py:25
  75.3 3.6 %collective-permute-start.10 = (f32[8,128]{1,0:T(8,128)S(1)}, f32[8,128]{1,0:T(8,128)S(1)}, u32[]{:S(2)}, u32[]{:S(2)}) collective-permute-start(f32[8,128]{1,0:T(8,128)S(1)} %add.52), channel_id=1, source_target_pairs={{0,4},{4,0},{8,12},{12,8},{1,5},{5,1},{9,13},{13,9},{2,6},{6,2},{1... | collective-permute-start | bytes 12296 | tf_op jit(solution)/shard_map/ppermute | solution.py:25
  80.2 3.5 %collective-permute-start.13 = (f32[3080,128]{1,0:T(8,128)S(1)}, f32[3080,128]{1,0:T(8,128)S(1)}, u32[]{:S(2)}, u32[]{:S(2)}) collective-permute-start(f32[3080,128]{1,0:T(8,128)S(1)} %correct.1.refs_2_.refs_6_.refs_8_.vector_ref.raw_ref), channel_id=1, source_target_pairs={{0,1},{1,0},{2,3},{3,2},{4,5},{5,4},{6,7},{7,6},{8,9},{9,8},{10,11... | collective-permute-start | bytes 4730888 | tf_op jit(solution)/shard_map/ppermute | solution.py:483
  91.7 13.9 %collective-permute-start.14 = (f32[776,128]{1,0:T(8,128)S(1)}, f32[776,128]{1,0:T(8,128)S(1)}, u32[]{:S(2)}, u32[]{:S(2)}) collective-permute-start(f32[776,128]{1,0:T(8,128)S(1)} %get-tuple-element.66), channel_id=1, source_target_pairs={{0,4},{4,8},{8,12},{12,0},{1,5},{5,9},{9,13},{13,1},{2,6},{6,10},{... | collective-permute-start | bytes 1191944 | tf_op jit(solution)/shard_map/ppermute | solution.py:480
  92.7 19.5 %collective-permute-start.15 = (f32[776,128]{1,0:T(8,128)S(1)}, f32[776,128]{1,0:T(8,128)S(1)}, u32[]{:S(2)}, u32[]{:S(2)}) collective-permute-start(f32[776,128]{1,0:T(8,128)S(1)} %get-tuple-element.67), channel_id=1, source_target_pairs={{0,12},{4,0},{8,4},{12,8},{1,13},{5,1},{9,5},{13,9},{2,14},{6,2},{... | collective-permute-start | bytes 1191944 | tf_op jit(solution)/shard_map/ppermute | solution.py:480
  104.5 10.7 %collective-permute-start.17 = (f32[768,128]{1,0:T(8,128)S(1)}, f32[768,128]{1,0:T(8,128)S(1)}, u32[]{:S(2)}, u32[]{:S(2)}) collective-permute-start(f32[768,128]{1,0:T(8,128)S(1)} %combine.12.mine_ref), channel_id=1, source_target_pairs={{0,2},{2,0},{1,3},{3,1},{4,6},{6,4},{5,7},{7,5},{8,10},{10,8},{9,1... | collective-permute-start | bytes 1179656 | tf_op jit(solution)/shard_map/ppermute | solution.py:25
  115.2 23.2 %collective-permute-start.19 = (f32[1536,128]{1,0:T(8,128)S(1)}, f32[1536,128]{1,0:T(8,128)S(1)}, u32[]{:S(2)}, u32[]{:S(2)}) collective-permute-start(f32[1536,128]{1,0:T(8,128)S(1)} %combine.13.mine_ref), channel_id=1, source_target_pairs={{0,2},{2,0},{1,3},{3,1},{4,6},{6,4},{5,7},{7,5},{8,10},{10,8},{9,1... | collective-permute-start | bytes 2359304 | tf_op jit(solution)/shard_map/ppermute | solution.py:25
  115.7 10.5 %collective-permute-start.16 = (f32[392,128]{1,0:T(8,128)S(1)}, f32[392,128]{1,0:T(8,128)S(1)}, u32[]{:S(2)}, u32[]{:S(2)}) collective-permute-start(f32[392,128]{1,0:T(8,128)S(1)} %get-tuple-element.68), channel_id=1, source_target_pairs={{0,8},{4,12},{8,0},{12,4},{1,9},{5,13},{9,1},{13,5},{2,10},{6,14},... | collective-permute-start | bytes 602120 | tf_op jit(solution)/shard_map/ppermute | solution.py:480
  126.8 11.5 %collective-permute-start.20 = (f32[384,128]{1,0:T(8,128)S(1)}, f32[384,128]{1,0:T(8,128)S(1)}, u32[]{:S(2)}, u32[]{:S(2)}) collective-permute-start(f32[384,128]{1,0:T(8,128)S(1)} %combine.14.mine_ref), channel_id=1, source_target_pairs={{0,2},{2,0},{1,3},{3,1},{4,6},{6,4},{5,7},{7,5},{8,10},{10,8},{9,1... | collective-permute-start | bytes 589832 | tf_op jit(solution)/shard_map/ppermute | solution.py:25
  128.4 9.4 %collective-permute-start.18 = (f32[392,128]{1,0:T(8,128)S(1)}, f32[392,128]{1,0:T(8,128)S(1)}, u32[]{:S(2)}, u32[]{:S(2)}) collective-permute-start(f32[392,128]{1,0:T(8,128)S(1)} %get-tuple-element.73), channel_id=1, source_target_pairs={{0,8},{4,12},{8,0},{12,4},{1,9},{5,13},{9,1},{13,5},{2,10},{6,14},... | collective-permute-start | bytes 602120 | tf_op jit(solution)/shard_map/ppermute | solution.py:480
  138.4 6.9 %collective-permute-start.21 = (f32[384,128]{1,0:T(8,128)S(1)}, f32[384,128]{1,0:T(8,128)S(1)}, u32[]{:S(2)}, u32[]{:S(2)}) collective-permute-start(f32[384,128]{1,0:T(8,128)S(1)} %combine.15.mine_ref), channel_id=1, source_target_pairs={{0,2},{2,0},{1,3},{3,1},{4,6},{6,4},{5,7},{7,5},{8,10},{10,8},{9,1... | collective-permute-start | bytes 589832 | tf_op jit(solution)/shard_map/ppermute | solution.py:25

commit v6 on v5

--- a/solution.py
+++ b/solution.py
@@ -29,9 +29,6 @@
     size = lax.axis_size(axis)
     if not power_of_two(size):
         return lax.psum(value, axis)
-    if size == 4:
-        one, two, three = (flip(value, axis, bit) for bit in (1, 2, 3))
-        return (value + one) + (two + three)
     bit = 1
     while bit < size:
         value = value + flip(value, axis, bit)
@@ -45,7 +42,9 @@
     return high, low
 
 
-def table_kernel(devices, partner_ref, kind_ref, table_ref, used):
+def table_kernel(devices, partner_ref, kind_ref, vector_ref, table_ref, copied_ref, used, sem):
+    copy = pltpu.make_async_copy(vector_ref, copied_ref, sem)
+    copy.start()
     count, terms = partner_ref.shape[0], kind_ref.shape[0]
     per = count // devices
     me = lax.axis_index("blk")
@@ -67,21 +66,26 @@
     for k in range(terms):
         table_ref[3 * count + k] = kind_ref[k]
     table_ref[3 * count + terms] = lax.axis_index("sub")
-
-
-def make_table(partner, term_kind):
+    copy.wait()
+
+
+def make_table(partner, term_kind, vector):
     devices = lax.axis_size("blk")
     length = 3 * partner.shape[0] + term_kind.shape[0] + 1
     return pl.pallas_call(
         functools.partial(table_kernel, devices),
-        out_shape=jax.ShapeDtypeStruct((length,), jnp.int32),
-        in_specs=[SCALARS, SCALARS],
-        out_specs=SCALARS,
-        scratch_shapes=[pltpu.SMEM((devices,), jnp.int32)],
-    )(partner, term_kind)
-
-
-def sector(table, count, terms, turned, l_ref, r_ref, own_ref, other_ref, lhs, high_rhs, low_rhs):
+        out_shape=[
+            jax.ShapeDtypeStruct((length,), jnp.int32),
+            jax.ShapeDtypeStruct(vector.shape, vector.dtype),
+        ],
+        in_specs=[SCALARS, SCALARS, ANY],
+        out_specs=[SCALARS, ANY],
+        scratch_shapes=[pltpu.SMEM((devices,), jnp.int32), pltpu.SemaphoreType.DMA],
+        name="table",
+    )(partner, term_kind, vector)
+
+
+def sector(table, count, terms, l_ref, r_ref, own_ref, other_ref, lhs, high_rhs, low_rhs):
     rows, width = l_ref.shape[2], r_ref.shape[3]
     roots = own_ref.shape[0] // rows
     first = table[3 * count + terms] == 0
@@ -107,19 +111,15 @@
         lanes = slice(k * width, (k + 1) * width)
         kind = table[3 * count + k]
         used = pl.ds(pl.multiple_of((1 - kind) * width, width), width)
-        high, low = halves(r_ref[k, 0].T if turned else r_ref[k, 0])
-        to = (lanes, used) if turned else (used, lanes)
-        high_rhs[to] = high
-        low_rhs[to] = low
-    dims = (((1,), (0 if turned else 1,)), ((), ()))
-    tall = lax.dot_general(lhs[...], high_rhs[...], dims, preferred_element_type=jnp.float32)
-    short = lax.dot_general(
-        lhs[: roots * rows], low_rhs[...], dims, preferred_element_type=jnp.float32
-    )
+        high, low = halves(r_ref[k, 0].T)
+        high_rhs[lanes, used] = high
+        low_rhs[lanes, used] = low
+    tall = jnp.dot(lhs[...], high_rhs[...], preferred_element_type=jnp.float32)
+    short = jnp.dot(lhs[: roots * rows], low_rhs[...], preferred_element_type=jnp.float32)
     return tall[: roots * rows] + tall[roots * rows :] + short
 
 
-def sector_kernel(count, terms, unroll, turned, starts, tags, table, *refs):
+def sector_kernel(count, terms, unroll, starts, tags, table, *refs):
     inputs, scratch = refs[: 4 * unroll], refs[-3 * unroll :]
     outputs = refs[-3 * unroll - len(starts) : -3 * unroll]
     tag_refs = refs[4 * unroll : 4 * unroll + 2]
@@ -137,21 +137,21 @@
             tag = tag_refs[0][...] + tag_refs[1][...]
             for ref, begin, end, tagged in zip(moved_refs, starts, starts[1:], tags):
                 if tagged:
-                    ref[(end - begin) * unroll * height :] = tag
+                    ref[(end - begin) * height :] = tag
 
     results = [
-        sector(table, count, terms, turned, *inputs[4 * u : 4 * u + 4], *scratch[3 * u : 3 * u + 3])
+        sector(table, count, terms, *inputs[4 * u : 4 * u + 4], *scratch[3 * u : 3 * u + 3])
         for u in range(unroll)
     ]
     for u in range(unroll):
         kept_ref[u * height : (u + 1) * height] = results[u][:, width:]
     for ref, begin, end in zip(moved_refs, starts, starts[1:]):
-
-        @pl.when((step >= begin) & (step < end))
-        def _(ref=ref, begin=begin):
-            for u in range(unroll):
-                at = pl.multiple_of(((step - begin) * unroll + u) * height, height)
-                ref[pl.ds(at, height)] = results[u][:, :width]
+        for u in range(unroll):
+            at = step * unroll + u - begin
+
+            @pl.when((at >= 0) & (at < end - begin))
+            def _(ref=ref, u=u, at=at):
+                ref[pl.ds(pl.multiple_of(at * height, height), height)] = results[u][:, :width]
 
 
 def place_of(i, pieces):
@@ -166,18 +166,27 @@
     terms, count, rows, width = left.shape
     height = own.shape[0] // TAG * TAG // count // rows * rows
     roots = height // rows
-    unroll = 2 if all(base % 2 == 0 and size % 2 == 0 for base, size in pieces) else 1
-    units = [(base // unroll, size // unroll) for base, size in pieces]
     starts = [0]
-    for _, size in units:
+    for _, size in pieces:
         starts.append(starts[-1] + size)
+    places = [base + i for base, size in pieces for i in range(size)]
+
+    def fits(unroll):
+        return len(places) % unroll == 0 and all(
+            places[i] % unroll == 0
+            and places[i : i + unroll] == list(range(places[i], places[i] + unroll))
+            for i in range(0, len(places), unroll)
+        )
+
+    choices = (2, 1) if ordered or len(places) < 8 else (4, 2, 1)
+    unroll = next(unroll for unroll in choices if fits(unroll))
 
     def specs(u):
         def source(i, table):
-            return table[unroll * place_of(i, units) + u]
+            return table[place_of(unroll * i + u, pieces)]
 
         def held(i, table):
-            return (unroll * place_of(i, units) + u if ordered else source(i, table), 0)
+            return (place_of(unroll * i + u, pieces) if ordered else source(i, table), 0)
 
         return [
             pl.BlockSpec((terms, 1, rows, width), lambda i, t: (0, source(i, t), 0, 0)),
@@ -196,20 +205,25 @@
         in_specs.append(ANY)
         args.append(kept)
         aliases = {len(args): len(pieces)}
-    rhs = (terms * width, 2 * width) if ordered else (2 * width, terms * width)
+    rhs = (terms * width, 2 * width)
     shapes = [(size * height + TAG * tagged, width) for (_, size), tagged in zip(pieces, tags)]
     out = pl.pallas_call(
-        functools.partial(sector_kernel, count, terms, unroll, ordered, starts, tags),
+        functools.partial(sector_kernel, count, terms, unroll, starts, tags),
         out_shape=[
             jax.ShapeDtypeStruct(shape, jnp.float32)
             for shape in shapes + [(count * height, width)]
         ],
         grid_spec=pltpu.PrefetchScalarGridSpec(
             num_scalar_prefetch=1,
-            grid=(starts[-1],),
+            grid=(starts[-1] // unroll,),
             in_specs=in_specs,
             out_specs=[pl.BlockSpec(shape, lambda i, t: (0, 0)) for shape in shapes]
-            + [pl.BlockSpec((unroll * height, width), lambda i, t: (place_of(i, units), 0))],
+            + [
+                pl.BlockSpec(
+                    (unroll * height, width),
+                    lambda i, t: (lax.div(place_of(unroll * i, pieces), unroll), 0),
+                )
+            ],
             scratch_shapes=[
                 pltpu.VMEM((2 * height, terms * width), jnp.bfloat16),
                 pltpu.VMEM(rhs, jnp.bfloat16),
@@ -455,7 +469,8 @@
     per = slots // devices
     elements = slots * devices * rows * lax.axis_size("sub") * width
     vector = jnp.transpose(amplitudes, (0, 2, 1, 3)).reshape(slots * roots * rows, width)
-    table = make_table(partner, term_kind)
+    arriving = lax.ppermute(vector, "sub", [(0, 1), (1, 0)])
+    table, vector = make_table(partner, term_kind, vector)
     diag = left_diag[:, :, None] + right_diag[:, None, :]
 
     staying = (0, 0, per)
@@ -468,9 +483,9 @@
         c = devices // 2
         cuts = [(0, per // 2), (per // 2, per - per // 2)] if per > 1 else [(0, per)]
         opposite = [(c, c * per + start, size) for start, size in cuts]
-    groups = [[staying]] + pairs + [[piece] for piece in opposite]
-    moving = [piece for group in groups[1:] for piece in group]
-    batches = [moving[:2], moving[2:] + [staying]]
+    moving = [piece for pair in pairs for piece in pair] + opposite
+    groups = [[piece] for piece in [staying] + moving]
+    batches = [moving[:1], moving[1:] + [staying]]
     late = len(opposite) == 2 and len(pairs) > 0
 
     def spans(pieces):
@@ -480,7 +495,7 @@
         return lax.ppermute(value, "blk", [(p, (p + c) % devices) for p in range(devices)])
 
     def partials(own, second, between):
-        other = lax.ppermute(own, "sub", [(0, 1), (1, 0)])
+        other = lax.ppermute(own, "sub", [(0, 1), (1, 0)]) if second else arriving
         kept, outgoing = None, {}
         for batch in batches:
             parts, kept = sectors(
@@ -496,18 +511,16 @@
             )
             outgoing.update(zip(batch, parts))
         arrived, sums, inners, done = {}, [], [], ()
-        for at, piece in enumerate(moving[:-1] if late else moving):
+        for at, piece in enumerate(moving):
             value = outgoing[piece]
-            if at >= 2:
-                value = after(value, arrived[moving[at - 2]], arrived[moving[at - 1]])[0]
+            if at >= 1:
+                value = after(value, arrived[moving[at - 1]])[0]
             arrived[piece] = relay(value, piece[0])
-        arrived[staying] = outgoing[staying]
+        arrived[staying] = after(outgoing[staying], arrived[moving[0]])[0]
         for group in groups:
-            if late and group == groups[-1]:
+            if late and group == groups[-1] and between:
                 piece = group[0]
-                arrived[piece] = relay(after(outgoing[piece], sums[-2])[0], piece[0])
-                if between:
-                    arrived[piece], *done = after(arrived[piece], *between(sums, arrived, other))
+                arrived[piece], *done = after(arrived[piece], *between(sums, arrived, other))
             first, *others = [arrived[piece] for piece in group]
             if sums:
                 first = after(first, sums[-2])[0]
@@ -524,8 +537,10 @@
                 not second,
                 inners if last and not second else (),
             )
-            if len(sums) == 2 or last:
+            if last:
                 mine = after(mine, *sums[1::2][-2:])[0]
+            elif len(sums) >= 4:
+                mine = after(mine, sums[-3])[0]
             sums += add_over_term(mine)
             inners.append(inner)
         if between and not late:

time: 147 us -> 189 us (1.29)
  Pallas kernels: 50 us -> 100 us
  waiting for transfers between devices: 70.9 us -> 53.9 us
  starting transfers between devices: 21.7 us -> 30.7 us
    pallas_call x5, Pallas kernels: 34.9 us -> 83.2 us  [the longest x1 49.9 us: make_table(): pl.pallas_call(functools.partial(table_kernel, devices), out_shape=[jax.S...]
    ppermute x8, waiting for transfers between devices: 48.9 us -> 36.3 us  [relay(): lax.ppermute(value, 'blk', [(p, (p + c) % devices) for p in range(devices)])]
    ppermute x12 -> x13, starting transfers between devices: 11.2 us -> 17.2 us  [flip(): return lax.ppermute(value, axis, [(i, i ^ bit) for i in range(size)])]
    ppermute x12 -> x13, waiting for transfers between devices: 17.8 us -> 14.2 us  [flip(): return lax.ppermute(value, axis, [(i, i ^ bit) for i in range(size)])]
    ppermute x8, starting transfers between devices: 9.93 us -> 12.9 us  [relay(): lax.ppermute(value, 'blk', [(p, (p + c) % devices) for p in range(devices)])]
    pallas_call x4 -> x5, Pallas kernels: 5.31 us -> 6.48 us  [finish(): pl.pallas_call(functools.partial(finish_kernel, count, rows, places), out...]
    pallas_call x8 -> x10, Pallas kernels: 6.73 us -> 7.73 us  [combine(): pl.pallas_call(functools.partial(combine_kernel, share, starts[:-1], with...]
  transfers between devices with their start and end apart: 22 -> 23, of which waited for: 17 -> 19; matrix products, arithmetic and copies ran while one was open for 1% -> 0% of each run, Pallas kernels for 21% -> 47%
where the time goes in v6:
time: 189 us; the launch traced here: 188 us
  Pallas kernels  100 us (53%)
  waiting for transfers between devices  53.9 us (29%)
  starting transfers between devices  30.7 us (16%)
  local copies, waits for them, and re-layouts  2.14 us (1%)
    pallas_call x1, Pallas kernels, make_table(): pl.pallas_call(functools.partial(table_kernel, devices), out_shape=[jax.S...  49.9 us
    ppermute x8, waiting for transfers between devices, relay(): lax.ppermute(value, 'blk', [(p, (p + c) % devices) for p in range(devices)])  36.3 us
    pallas_call x4, Pallas kernels, sectors(): pl.pallas_call(functools.partial(sector_kernel, count, terms, unroll, sta...  33.3 us
    ppermute x13, starting transfers between devices, flip(): return lax.ppermute(value, axis, [(i, i ^ bit) for i in range(size)])  17.2 us
    ppermute x13, waiting for transfers between devices, flip(): return lax.ppermute(value, axis, [(i, i ^ bit) for i in range(size)])  14.2 us
    ppermute x8, starting transfers between devices, relay(): lax.ppermute(value, 'blk', [(p, (p + c) % devices) for p in range(devices)])  12.9 us
    pallas_call x10, Pallas kernels, combine(): pl.pallas_call(functools.partial(combine_kernel, share, starts[:-1], with...  7.73 us
    pallas_call x5, Pallas kernels, finish(): pl.pallas_call(functools.partial(finish_kernel, count, rows, places), out...  6.48 us
  transfers between devices with their start and end apart: 23, of which 19 were waited for; matrix products, arithmetic and copies ran while one was open for 0% of the time, Pallas kernels for 47%

profile of v6, /device:TPU:0, one launch (start us, length us, event | category | flops | bytes accessed | tf_op | source)
XLA Modules:
  0.0 188.4 jit_solution(14539605555763474286)
XLA Ops:
  1.1 49.9 %table.1 = (s32[57]{0:T(128)}, f32[3072,128]{1,0:T(8,128)}) custom-call(s32[16]{0:T(128)} %partner_ref.1, s32[8]{0:T(128)} %kind_ref.1, f32[3072,128]{1,0:T(8,128)} %bitcast.11), custom_call_target="tpu_custom_call" | custom-call | tf_op jit(solution)/shard_map/table/pallas_call | solution.py:75
  51.1 1.4 copy-done
  53.2 5.0 %sectors.4 = (f32[768,128]{1,0:T(8,128)S(1)}, f32[3072,128]{1,0:T(8,128)S(1)}) custom-call(s32[57]{0:T(128)S(1)} %copy-done.1, f32[8,16,64,128]{3,2,1,0:T(8,128)} %refs_4_.7, f32[8,16,128,128]{3,2,1,0:T(8,128)} %refs_5_.7, f32[3072,128]{1,0:T(8,128)S(1)} %copy-done, f32[3072,128]{1,0:T(8,128)S(1)} %collective-permute-done.refs_3_.refs_7_.refs_11_.refs_15_, ...), custom_call_target="tpu_custom_call" | custom-call | tf_op jit(solution)/shard_map/sectors/pallas_call | solution.py:210
  58.2 2.6 %collective-permute-start.1 = (f32[768,128]{1,0:T(8,128)S(1)}, f32[768,128]{1,0:T(8,128)S(1)}, u32[]{:S(2)}, u32[]{:S(2)}) collective-permute-start(f32[768,128]{1,0:T(8,128)S(1)} %get-tuple-element.60), channel_id=1, source_target_pairs={{0,4},{4,8},{8,12},{12,0},{1,5},{5,9},{9,13},{13,1},{2,6},{6,10},{... | collective-permute-start | bytes 1179656 | tf_op jit(solution)/shard_map/ppermute | solution.py:495
  60.9 11.7 %sectors.5 = (f32[768,128]{1,0:T(8,128)S(1)}, f32[384,128]{1,0:T(8,128)S(1)}, f32[384,128]{1,0:T(8,128)S(1)}, f32[768,128]{1,0:T(8,128)S(1)}, f32[3072,128]{1,0:T(8,128)S(1)}) custom-call(s32[57]{0:T(128)S(1)} %copy-done.1, f32[8,16,64,128]{3,2,1,0:T(8,128)} %refs_4_.7, f32[8,16,128,128]{3,2,1,0:T(8,128)} %refs_5_.7, ...), custom_call_target="tpu_custom_call", output_to_operand_aliasing={{4}: (17, {})} | custom-call | tf_op jit(solution)/shard_map/sectors/pallas_call | solution.py:210
  72.7 2.0 %collective-permute-start.2 = (f32[768,128]{1,0:T(8,128)S(1)}, f32[768,128]{1,0:T(8,128)S(1)}, u32[]{:S(2)}, u32[]{:S(2)}) collective-permute-start(f32[768,128]{1,0:T(8,128)S(1)} %get-tuple-element.61), channel_id=1, source_target_pairs={{0,12},{4,0},{8,4},{12,8},{1,13},{5,1},{9,5},{13,9},{2,14},{6,2},{... | collective-permute-start | bytes 1179656 | tf_op jit(solution)/shard_map/ppermute | solution.py:495
  74.9 0.8 combine.10
  75.7 1.7 collective-permute-start.5
  77.4 0.8 combine.11
  78.7 5.2 %collective-permute-done.2.refs_0_ = f32[768,128]{1,0:T(8,128)S(1)} collective-permute-done((f32[768,128]{1,0:T(8,128)S(1)}, f32[768,128]{1,0:T(8,128)S(1)}, u32[]{:S(2)}, u32[]{:S(2)}) %collective-permute-start.2) | collective-permute-done | bytes 393248 | tf_op jit(solution)/shard_map/ppermute | solution.py:495
  83.8 2.6 %collective-permute-start.3 = (f32[384,128]{1,0:T(8,128)S(1)}, f32[384,128]{1,0:T(8,128)S(1)}, u32[]{:S(2)}, u32[]{:S(2)}) collective-permute-start(f32[384,128]{1,0:T(8,128)S(1)} %get-tuple-element.62), channel_id=1, source_target_pairs={{0,8},{4,12},{8,0},{12,4},{1,9},{5,13},{9,1},{13,5},{2,10},{6,14},... | collective-permute-start | bytes 589832 | tf_op jit(solution)/shard_map/ppermute | solution.py:495
  86.4 0.8 combine.12
  87.7 1.7 collective-permute-start.7
  89.4 6.0 %collective-permute-done.3.refs_0_ = f32[384,128]{1,0:T(8,128)S(1)} collective-permute-done((f32[384,128]{1,0:T(8,128)S(1)}, f32[384,128]{1,0:T(8,128)S(1)}, u32[]{:S(2)}, u32[]{:S(2)}) %collective-permute-start.3) | collective-permute-done | bytes 196640 | tf_op jit(solution)/shard_map/ppermute | solution.py:495
  96.1 1.7 collective-permute-start.8
  97.8 8.1 %collective-permute-done.4.refs_0_ = f32[384,128]{1,0:T(8,128)S(1)} collective-permute-done((f32[384,128]{1,0:T(8,128)S(1)}, f32[384,128]{1,0:T(8,128)S(1)}, u32[]{:S(2)}, u32[]{:S(2)}) %collective-permute-start.4) | collective-permute-done | bytes 196640 | tf_op jit(solution)/shard_map/ppermute | solution.py:495
  106.0 1.3 combine.14
  107.2 0.8 collective-permute-done.8.rest_7_
  108.1 1.5 collective-permute-start.9
  109.6 4.8 %collective-permute-done.9.rest_9_ = f32[392,128]{1,0:T(8,128)S(1)} collective-permute-done((f32[392,128]{1,0:T(8,128)S(1)}, f32[392,128]{1,0:T(8,128)S(1)}, u32[]{:S(2)}, u32[]{:S(2)}) %collective-permute-start.9) | collective-permute-done | bytes 200736 | tf_op jit(solution)/shard_map/ppermute | solution.py:25
  114.4 1.2 collective-permute-done.10
  115.5 2.2 %collective-permute-start.11 = (f32[8,128]{1,0:T(8,128)S(1)}, f32[8,128]{1,0:T(8,128)S(1)}, u32[]{:S(2)}, u32[]{:S(2)}) collective-permute-start(f32[8,128]{1,0:T(8,128)S(1)} %add.49), channel_id=1, source_target_pairs={{0,4},{4,0},{8,12},{12,8},{1,5},{5,1},{9,13},{13,9},{2,6},{6,2},{1... | collective-permute-start | bytes 12296 | tf_op jit(solution)/shard_map/ppermute | solution.py:25
  117.7 1.6 collective-permute-done.11
  119.3 1.7 collective-permute-start.12
  121.0 2.8 %collective-permute-done.12 = f32[8,128]{1,0:T(8,128)S(1)} collective-permute-done((f32[8,128]{1,0:T(8,128)S(1)}, f32[8,128]{1,0:T(8,128)S(1)}, u32[]{:S(2)}, u32[]{:S(2)}) %collective-permute-start.12) | collective-permute-done | bytes 4128 | tf_op jit(solution)/shard_map/ppermute | solution.py:25
  123.8 1.2 correct.1.refs_2_.refs_6_.refs_8_.raw_ref.vector_ref
  125.1 3.4 %collective-permute-done.13.refs_3_.refs_7_.refs_9_ = f32[3080,128]{1,0:T(8,128)S(1)} collective-permute-done((f32[3080,128]{1,0:T(8,128)S(1)}, f32[3080,128]{1,0:T(8,128)S(1)}, u32[]{:S(2)}, u32[]{:S(2)}) %collective-permute-start.13) | collective-permute-done | bytes 1576992 | tf_op jit(solution)/shard_map/ppermute | solution.py:498
  128.5 5.1 %sectors.6 = (f32[776,128]{1,0:T(8,128)S(1)}, f32[3072,128]{1,0:T(8,128)S(1)}) custom-call(s32[57]{0:T(128)S(1)} %copy-done.1, f32[8,16,64,128]{3,2,1,0:T(8,128)} %refs_4_.7, f32[8,16,128,128]{3,2,1,0:T(8,128)} %refs_5_.7, f32[3080,128]{1,0:T(8,128)S(1)} %correct.1.refs_2_.refs_6_.refs_8_.raw_ref.vector_ref, ...), custom_call_target="tpu_custom_call" | custom-call | tf_op jit(solution)/shard_map/sectors/pallas_call | solution.py:210
  133.6 2.1 %collective-permute-start.14 = (f32[776,128]{1,0:T(8,128)S(1)}, f32[776,128]{1,0:T(8,128)S(1)}, u32[]{:S(2)}, u32[]{:S(2)}) collective-permute-start(f32[776,128]{1,0:T(8,128)S(1)} %get-tuple-element.86), channel_id=1, source_target_pairs={{0,4},{4,8},{8,12},{12,0},{1,5},{5,9},{9,13},{13,1},{2,6},{6,10},{... | collective-permute-start | bytes 1191944 | tf_op jit(solution)/shard_map/ppermute | solution.py:495
  135.6 11.5 %sectors.7 = (f32[776,128]{1,0:T(8,128)S(1)}, f32[392,128]{1,0:T(8,128)S(1)}, f32[392,128]{1,0:T(8,128)S(1)}, f32[768,128]{1,0:T(8,128)S(1)}, f32[3072,128]{1,0:T(8,128)S(1)}) custom-call(s32[57]{0:T(128)S(1)} %copy-done.1, f32[8,16,64,128]{3,2,1,0:T(8,128)} %refs_4_.7, f32[8,16,128,128]{3,2,1,0:T(8,128)} %refs_5_.7, ...), custom_call_target="tpu_custom_call", output_to_operand_aliasing={{4}: (11, {})} | custom-call | tf_op jit(solution)/shard_map/sectors/pallas_call | solution.py:210
  147.2 1.9 collective-permute-start.15
  149.0 0.7 combine.15.mine_ref
  149.8 1.5 collective-permute-start.18
  151.2 0.7 combine.16.mine_ref
  152.6 5.6 %collective-permute-done.15.refs_0_ = f32[776,128]{1,0:T(8,128)S(1)} collective-permute-done((f32[776,128]{1,0:T(8,128)S(1)}, f32[776,128]{1,0:T(8,128)S(1)}, u32[]{:S(2)}, u32[]{:S(2)}) %collective-permute-start.15) | collective-permute-done | bytes 397344 | tf_op jit(solution)/shard_map/ppermute | solution.py:495
  158.2 1.7 collective-permute-start.16
  160.6 1.3 collective-permute-done.18.theirs_ref
  161.9 1.4 collective-permute-start.20
  163.3 6.0 %collective-permute-done.16.refs_0_ = f32[392,128]{1,0:T(8,128)S(1)} collective-permute-done((f32[392,128]{1,0:T(8,128)S(1)}, f32[392,128]{1,0:T(8,128)S(1)}, u32[]{:S(2)}, u32[]{:S(2)}) %collective-permute-start.16) | collective-permute-done | bytes 200736 | tf_op jit(solution)/shard_map/ppermute | solution.py:495
  170.3 1.4 collective-permute-start.21
  171.9 1.8 scaled.1
  173.7 1.3 finish.5.rest_0_
  175.1 5.3 %collective-permute-done.17.refs_0_ = f32[392,128]{1,0:T(8,128)S(1)} collective-permute-done((f32[392,128]{1,0:T(8,128)S(1)}, f32[392,128]{1,0:T(8,128)S(1)}, u32[]{:S(2)}, u32[]{:S(2)}) %collective-permute-start.17) | collective-permute-done | bytes 200736 | tf_op jit(solution)/shard_map/ppermute | solution.py:495
  181.5 1.4 collective-permute-start.22
  182.9 1.3 finish.6.rest_0_
  184.2 1.3 finish.7.rest_0_
  185.6 1.2 finish.8.rest_0_
  187.2 1.2 finish.9
  (36 shorter events, 7.3 us)
Async XLA Ops:
  0.6 50.5 %collective-permute-start = (f32[3072,128]{1,0:T(8,128)}, f32[3072,128]{1,0:T(8,128)S(1)}, u32[]{:S(2)}, u32[]{:S(2)}) collective-permute-start(f32[3072,128]{1,0:T(8,128)} %bitcast.10), channel_id=1, source_target_pairs={{0,1},{1,0},{2,3},{3,2},{4,5},{5,4},{6,7},{7,6},{8,9},{9,8},{10,11... | collective-permute-start | bytes 4718600 | tf_op jit(solution)/shard_map/ppermute | solution.py:472
  51.1 1.4 copy-start
  52.5 0.7 copy-start.1
  58.2 14.4 %collective-permute-start.1 = (f32[768,128]{1,0:T(8,128)S(1)}, f32[768,128]{1,0:T(8,128)S(1)}, u32[]{:S(2)}, u32[]{:S(2)}) collective-permute-start(f32[768,128]{1,0:T(8,128)S(1)} %get-tuple-element.60), channel_id=1, source_target_pairs={{0,4},{4,8},{8,12},{12,0},{1,5},{5,9},{9,13},{13,1},{2,6},{6,10},{... | collective-permute-start | bytes 1179656 | tf_op jit(solution)/shard_map/ppermute | solution.py:495
  60.9 13.8 %copy-start.2 = (f32[16,128]{1,0:T(8,128)S(1)}, f32[16,128]{1,0:T(8,128)}, u32[]{:S(2)}) copy-start(f32[16,128]{1,0:T(8,128)} %param.13) | copy-start | bytes 24580
  60.9 13.8 %copy-start.3 = (f32[16,64]{1,0:T(8,128)S(1)}, f32[16,64]{1,0:T(8,128)}, u32[]{:S(2)}) copy-start(f32[16,64]{1,0:T(8,128)} %param.12) | copy-start | bytes 12292
  72.7 11.2 %collective-permute-start.2 = (f32[768,128]{1,0:T(8,128)S(1)}, f32[768,128]{1,0:T(8,128)S(1)}, u32[]{:S(2)}, u32[]{:S(2)}) collective-permute-start(f32[768,128]{1,0:T(8,128)S(1)} %get-tuple-element.61), channel_id=1, source_target_pairs={{0,12},{4,0},{8,4},{12,8},{1,13},{5,1},{9,5},{13,9},{2,14},{6,2},{... | collective-permute-start | bytes 1179656 | tf_op jit(solution)/shard_map/ppermute | solution.py:495
  75.7 12.0 %collective-permute-start.5 = (f32[768,128]{1,0:T(8,128)S(1)}, f32[768,128]{1,0:T(8,128)S(1)}, u32[]{:S(2)}, u32[]{:S(2)}) collective-permute-start(f32[768,128]{1,0:T(8,128)S(1)} %get-tuple-element.66.rest_0_), channel_id=1, source_target_pairs={{0,2},{2,0},{1,3},{3,1},{4,6},{6,4},{5,7},{7,5},{8,10},{10,8},{9,1... | collective-permute-start | bytes 1179656 | tf_op jit(solution)/shard_map/ppermute | solution.py:25
  78.2 17.9 %collective-permute-start.6 = (f32[768,128]{1,0:T(8,128)S(1)}, f32[768,128]{1,0:T(8,128)S(1)}, u32[]{:S(2)}, u32[]{:S(2)}) collective-permute-start(f32[768,128]{1,0:T(8,128)S(1)} %get-tuple-element.68.rest_2_), channel_id=1, source_target_pairs={{0,2},{2,0},{1,3},{3,1},{4,6},{6,4},{5,7},{7,5},{8,10},{10,8},{9,1... | collective-permute-start | bytes 1179656 | tf_op jit(solution)/shard_map/ppermute | solution.py:25
  83.8 11.5 %collective-permute-start.3 = (f32[384,128]{1,0:T(8,128)S(1)}, f32[384,128]{1,0:T(8,128)S(1)}, u32[]{:S(2)}, u32[]{:S(2)}) collective-permute-start(f32[384,128]{1,0:T(8,128)S(1)} %get-tuple-element.62), channel_id=1, source_target_pairs={{0,8},{4,12},{8,0},{12,4},{1,9},{5,13},{9,1},{13,5},{2,10},{6,14},... | collective-permute-start | bytes 589832 | tf_op jit(solution)/shard_map/ppermute | solution.py:495
  87.7 19.5 %collective-permute-start.7 = (f32[768,128]{1,0:T(8,128)S(1)}, f32[768,128]{1,0:T(8,128)S(1)}, u32[]{:S(2)}, u32[]{:S(2)}) collective-permute-start(f32[768,128]{1,0:T(8,128)S(1)} %get-tuple-element.71.rest_4_), channel_id=1, source_target_pairs={{0,2},{2,0},{1,3},{3,1},{4,6},{6,4},{5,7},{7,5},{8,10},{10,8},{9,1... | collective-permute-start | bytes 1179656 | tf_op jit(solution)/shard_map/ppermute | solution.py:25
  95.4 10.6 %collective-permute-start.4 = (f32[384,128]{1,0:T(8,128)S(1)}, f32[384,128]{1,0:T(8,128)S(1)}, u32[]{:S(2)}, u32[]{:S(2)}) collective-permute-start(f32[384,128]{1,0:T(8,128)S(1)} %get-tuple-element.63), channel_id=1, source_target_pairs={{0,8},{4,12},{8,0},{12,4},{1,9},{5,13},{9,1},{13,5},{2,10},{6,14},... | collective-permute-start | bytes 589832 | tf_op jit(solution)/shard_map/ppermute | solution.py:495
  96.1 11.9 %collective-permute-start.8 = (f32[384,128]{1,0:T(8,128)S(1)}, f32[384,128]{1,0:T(8,128)S(1)}, u32[]{:S(2)}, u32[]{:S(2)}) collective-permute-start(f32[384,128]{1,0:T(8,128)S(1)} %get-tuple-element.74.rest_6_), channel_id=1, source_target_pairs={{0,2},{2,0},{1,3},{3,1},{4,6},{6,4},{5,7},{7,5},{8,10},{10,8},{9,1... | collective-permute-start | bytes 589832 | tf_op jit(solution)/shard_map/ppermute | solution.py:25
  108.1 6.3 %collective-permute-start.9 = (f32[392,128]{1,0:T(8,128)S(1)}, f32[392,128]{1,0:T(8,128)S(1)}, u32[]{:S(2)}, u32[]{:S(2)}) collective-permute-start(f32[392,128]{1,0:T(8,128)S(1)} %get-tuple-element.81.rest_8_), channel_id=1, source_target_pairs={{0,2},{2,0},{1,3},{3,1},{4,6},{6,4},{5,7},{7,5},{8,10},{10,8},{9,1... | collective-permute-start | bytes 602120 | tf_op jit(solution)/shard_map/ppermute | solution.py:25
  114.4 1.2 collective-permute-start.10
  115.5 3.7 %collective-permute-start.11 = (f32[8,128]{1,0:T(8,128)S(1)}, f32[8,128]{1,0:T(8,128)S(1)}, u32[]{:S(2)}, u32[]{:S(2)}) collective-permute-start(f32[8,128]{1,0:T(8,128)S(1)} %add.49), channel_id=1, source_target_pairs={{0,4},{4,0},{8,12},{12,8},{1,5},{5,1},{9,13},{13,9},{2,6},{6,2},{1... | collective-permute-start | bytes 12296 | tf_op jit(solution)/shard_map/ppermute | solution.py:25
  119.3 4.5 %collective-permute-start.12 = (f32[8,128]{1,0:T(8,128)S(1)}, f32[8,128]{1,0:T(8,128)S(1)}, u32[]{:S(2)}, u32[]{:S(2)}) collective-permute-start(f32[8,128]{1,0:T(8,128)S(1)} %add.50), channel_id=1, source_target_pairs={{0,8},{4,12},{8,0},{12,4},{1,9},{5,13},{9,1},{13,5},{2,10},{6,14},... | collective-permute-start | bytes 12296 | tf_op jit(solution)/shard_map/ppermute | solution.py:25
  125.0 3.5 %collective-permute-start.13 = (f32[3080,128]{1,0:T(8,128)S(1)}, f32[3080,128]{1,0:T(8,128)S(1)}, u32[]{:S(2)}, u32[]{:S(2)}) collective-permute-start(f32[3080,128]{1,0:T(8,128)S(1)} %correct.1.refs_2_.refs_6_.refs_8_.raw_ref.vector_ref), channel_id=1, source_target_pairs={{0,1},{1,0},{2,3},{3,2},{4,5},{5,4},{6,7},{7,6},{8,9},{9,8},{10,11... | collective-permute-start | bytes 4730888 | tf_op jit(solution)/shard_map/ppermute | solution.py:498
  133.6 13.6 %collective-permute-start.14 = (f32[776,128]{1,0:T(8,128)S(1)}, f32[776,128]{1,0:T(8,128)S(1)}, u32[]{:S(2)}, u32[]{:S(2)}) collective-permute-start(f32[776,128]{1,0:T(8,128)S(1)} %get-tuple-element.86), channel_id=1, source_target_pairs={{0,4},{4,8},{8,12},{12,0},{1,5},{5,9},{9,13},{13,1},{2,6},{6,10},{... | collective-permute-start | bytes 1191944 | tf_op jit(solution)/shard_map/ppermute | solution.py:495
  147.2 11.0 %collective-permute-start.15 = (f32[776,128]{1,0:T(8,128)S(1)}, f32[776,128]{1,0:T(8,128)S(1)}, u32[]{:S(2)}, u32[]{:S(2)}) collective-permute-start(f32[776,128]{1,0:T(8,128)S(1)} %get-tuple-element.87), channel_id=1, source_target_pairs={{0,12},{4,0},{8,4},{12,8},{1,13},{5,1},{9,5},{13,9},{2,14},{6,2},{... | collective-permute-start | bytes 1191944 | tf_op jit(solution)/shard_map/ppermute | solution.py:495
  149.8 12.1 %collective-permute-start.18 = (f32[768,128]{1,0:T(8,128)S(1)}, f32[768,128]{1,0:T(8,128)S(1)}, u32[]{:S(2)}, u32[]{:S(2)}) collective-permute-start(f32[768,128]{1,0:T(8,128)S(1)} %combine.15.mine_ref), channel_id=1, source_target_pairs={{0,2},{2,0},{1,3},{3,1},{4,6},{6,4},{5,7},{7,5},{8,10},{10,8},{9,1... | collective-permute-start | bytes 1179656 | tf_op jit(solution)/shard_map/ppermute | solution.py:25
  151.9 18.3 %collective-permute-start.19 = (f32[768,128]{1,0:T(8,128)S(1)}, f32[768,128]{1,0:T(8,128)S(1)}, u32[]{:S(2)}, u32[]{:S(2)}) collective-permute-start(f32[768,128]{1,0:T(8,128)S(1)} %combine.16.mine_ref), channel_id=1, source_target_pairs={{0,2},{2,0},{1,3},{3,1},{4,6},{6,4},{5,7},{7,5},{8,10},{10,8},{9,1... | collective-permute-start | bytes 1179656 | tf_op jit(solution)/shard_map/ppermute | solution.py:25
  158.2 11.1 %collective-permute-start.16 = (f32[392,128]{1,0:T(8,128)S(1)}, f32[392,128]{1,0:T(8,128)S(1)}, u32[]{:S(2)}, u32[]{:S(2)}) collective-permute-start(f32[392,128]{1,0:T(8,128)S(1)} %get-tuple-element.88), channel_id=1, source_target_pairs={{0,8},{4,12},{8,0},{12,4},{1,9},{5,13},{9,1},{13,5},{2,10},{6,14},... | collective-permute-start | bytes 602120 | tf_op jit(solution)/shard_map/ppermute | solution.py:495
  161.9 19.2 %collective-permute-start.20 = (f32[768,128]{1,0:T(8,128)S(1)}, f32[768,128]{1,0:T(8,128)S(1)}, u32[]{:S(2)}, u32[]{:S(2)}) collective-permute-start(f32[768,128]{1,0:T(8,128)S(1)} %combine.17.mine_ref), channel_id=1, source_target_pairs={{0,2},{2,0},{1,3},{3,1},{4,6},{6,4},{5,7},{7,5},{8,10},{10,8},{9,1... | collective-permute-start | bytes 1179656 | tf_op jit(solution)/shard_map/ppermute | solution.py:25
  169.3 11.1 %collective-permute-start.17 = (f32[392,128]{1,0:T(8,128)S(1)}, f32[392,128]{1,0:T(8,128)S(1)}, u32[]{:S(2)}, u32[]{:S(2)}) collective-permute-start(f32[392,128]{1,0:T(8,128)S(1)} %get-tuple-element.89), channel_id=1, source_target_pairs={{0,8},{4,12},{8,0},{12,4},{1,9},{5,13},{9,1},{13,5},{2,10},{6,14},... | collective-permute-start | bytes 602120 | tf_op jit(solution)/shard_map/ppermute | solution.py:495
  170.3 11.2 %collective-permute-start.21 = (f32[384,128]{1,0:T(8,128)S(1)}, f32[384,128]{1,0:T(8,128)S(1)}, u32[]{:S(2)}, u32[]{:S(2)}) collective-permute-start(f32[384,128]{1,0:T(8,128)S(1)} %combine.18.mine_ref), channel_id=1, source_target_pairs={{0,2},{2,0},{1,3},{3,1},{4,6},{6,4},{5,7},{7,5},{8,10},{10,8},{9,1... | collective-permute-start | bytes 589832 | tf_op jit(solution)/shard_map/ppermute | solution.py:25
  181.5 5.7 %collective-permute-start.22 = (f32[384,128]{1,0:T(8,128)S(1)}, f32[384,128]{1,0:T(8,128)S(1)}, u32[]{:S(2)}, u32[]{:S(2)}) collective-permute-start(f32[384,128]{1,0:T(8,128)S(1)} %combine.19.mine_ref), channel_id=1, source_target_pairs={{0,2},{2,0},{1,3},{3,1},{4,6},{6,4},{5,7},{7,5},{8,10},{10,8},{9,1... | collective-permute-start | bytes 589832 | tf_op jit(solution)/shard_map/ppermute | solution.py:25

commit v7 on v6

--- a/solution.py
+++ b/solution.py
@@ -42,9 +42,7 @@
     return high, low
 
 
-def table_kernel(devices, partner_ref, kind_ref, vector_ref, table_ref, copied_ref, used, sem):
-    copy = pltpu.make_async_copy(vector_ref, copied_ref, sem)
-    copy.start()
+def table_kernel(devices, partner_ref, kind_ref, _, table_ref, used):
     count, terms = partner_ref.shape[0], kind_ref.shape[0]
     per = count // devices
     me = lax.axis_index("blk")
@@ -63,29 +61,45 @@
         return carry
 
     lax.fori_loop(0, count, place, 0)
+    moving = sum(kind_ref[k] for k in range(terms))
+    moving_pairs = lax.div(moving + 1, 2)
+    before = (jnp.int32(0), 2 * moving_pairs)
     for k in range(terms):
-        table_ref[3 * count + k] = kind_ref[k]
-    table_ref[3 * count + terms] = lax.axis_index("sub")
-    copy.wait()
+        moves = kind_ref[k] == 1
+        table_ref[3 * count + k] = jnp.where(moves, before[0], before[1])
+        before = (jnp.where(moves, before[0] + 1, before[0]), jnp.where(moves, before[1], before[1] + 1))
+    at = 3 * count + terms
+    table_ref[at] = lax.axis_index("sub")
+    table_ref[at + 1] = moving_pairs
+    table_ref[at + 2] = moving_pairs + lax.div(terms - moving + 1, 2)
+    table_ref[at + 3] = moving
 
 
 def make_table(partner, term_kind, vector):
     devices = lax.axis_size("blk")
-    length = 3 * partner.shape[0] + term_kind.shape[0] + 1
+    length = 3 * partner.shape[0] + term_kind.shape[0] + 4
     return pl.pallas_call(
         functools.partial(table_kernel, devices),
-        out_shape=[
-            jax.ShapeDtypeStruct((length,), jnp.int32),
-            jax.ShapeDtypeStruct(vector.shape, vector.dtype),
-        ],
-        in_specs=[SCALARS, SCALARS, ANY],
-        out_specs=[SCALARS, ANY],
-        scratch_shapes=[pltpu.SMEM((devices,), jnp.int32), pltpu.SemaphoreType.DMA],
+        out_shape=jax.ShapeDtypeStruct((length,), jnp.int32),
+        in_specs=[SCALARS, SCALARS, WHOLE],
+        out_specs=SCALARS,
+        scratch_shapes=[pltpu.SMEM((devices,), jnp.int32)],
+        compiler_params=pltpu.CompilerParams(vmem_limit_bytes=SMALL),
         name="table",
     )(partner, term_kind, vector)
 
 
-def sector(table, count, terms, l_ref, r_ref, own_ref, other_ref, lhs, high_rhs, low_rhs):
+def add_pair(table, at, pair, lhs, rhs, total):
+    height, width = total.shape[0] // 2, total.shape[1]
+    deep = slice(2 * pair * width, 2 * (pair + 1) * width)
+    both = jnp.dot(lhs[:, deep], rhs[deep], preferred_element_type=jnp.float32)
+    result = both[:height, :width] + both[:height, width:] + both[height:, :width]
+    kept = jnp.where(pair < table[at + 1], 0, height)
+    into = pl.ds(pl.multiple_of(kept, height), height)
+    total[into] = total[into] + result
+
+
+def sector(table, count, terms, l_ref, r_ref, own_ref, other_ref, lhs, rhs, total):
     rows, width = l_ref.shape[2], r_ref.shape[3]
     roots = own_ref.shape[0] // rows
     first = table[3 * count + terms] == 0
@@ -94,29 +108,28 @@
     bottom = jnp.where(first, other, own)
     left = l_ref[:, 0].reshape(terms * rows, 2 * rows)
     left = jnp.concatenate(halves(left), axis=1)
-    wide = []
+
+    def lanes_of(k):
+        return pl.ds(pl.multiple_of(table[3 * count + k] * width, width), width)
+
     for r in range(roots):
         at = slice(r * rows, (r + 1) * rows)
-        one = jnp.concatenate(halves(jnp.concatenate([top[at], bottom[at]], axis=0)), axis=1)
-        wide.append(jnp.concatenate([one, one], axis=0))
-    for r in range(roots):
-        both = jnp.dot(left, wide[r], preferred_element_type=jnp.float32)
+        wide = jnp.concatenate(halves(jnp.concatenate([top[at], bottom[at]], axis=0)), axis=1)
+        both = jnp.dot(
+            left, jnp.concatenate([wide, wide], axis=0), preferred_element_type=jnp.float32
+        )
         high, low = halves(both[:, :width] + both[:, width:])
         for k in range(terms):
-            lanes = slice(k * width, (k + 1) * width)
             part = slice(k * rows, (k + 1) * rows)
-            lhs[r * rows : (r + 1) * rows, lanes] = high[part]
-            lhs[(roots + r) * rows : (roots + r + 1) * rows, lanes] = low[part]
+            lhs[r * rows : (r + 1) * rows, lanes_of(k)] = high[part]
+            lhs[(roots + r) * rows : (roots + r + 1) * rows, lanes_of(k)] = low[part]
     for k in range(terms):
-        lanes = slice(k * width, (k + 1) * width)
-        kind = table[3 * count + k]
-        used = pl.ds(pl.multiple_of((1 - kind) * width, width), width)
         high, low = halves(r_ref[k, 0].T)
-        high_rhs[lanes, used] = high
-        low_rhs[lanes, used] = low
-    tall = jnp.dot(lhs[...], high_rhs[...], preferred_element_type=jnp.float32)
-    short = jnp.dot(lhs[: roots * rows], low_rhs[...], preferred_element_type=jnp.float32)
-    return tall[: roots * rows] + tall[roots * rows :] + short
+        rhs[lanes_of(k), :width] = high
+        rhs[lanes_of(k), width:] = low
+    total[...] = jnp.zeros_like(total)
+    for pair in range((terms + 1) // 2):
+        add_pair(table, 3 * count + terms, pair, lhs, rhs, total)
 
 
 def sector_kernel(count, terms, unroll, starts, tags, table, *refs):
@@ -127,31 +140,46 @@
     width = kept_ref.shape[1]
     height = kept_ref.shape[0] // unroll
     step = pl.program_id(0)
+    at = 3 * count + terms
 
     @pl.when(step == 0)
     def _():
-        for at, ref in enumerate(scratch):
-            if at % 3:
-                ref[...] = jnp.zeros_like(ref)
         if any(tags):
             tag = tag_refs[0][...] + tag_refs[1][...]
             for ref, begin, end, tagged in zip(moved_refs, starts, starts[1:], tags):
                 if tagged:
                     ref[(end - begin) * height :] = tag
 
-    results = [
+    @pl.when((step == 0) & (lax.rem(table[at + 3], 2) + terms % 2 > 0))
+    def _():
+        empty = [jnp.where(lax.rem(table[at + 3], 2) == 1, table[at + 3], terms)]
+        empty += range(terms, scratch[0].shape[1] // width)
+        for u in range(unroll):
+            lhs, rhs, _ = scratch[3 * u : 3 * u + 3]
+            for one in empty:
+                lanes = pl.ds(pl.multiple_of(one * width, width), width)
+                lhs[:, lanes] = jnp.zeros((lhs.shape[0], width), lhs.dtype)
+                rhs[lanes] = jnp.zeros((width, rhs.shape[1]), rhs.dtype)
+
+    for u in range(unroll):
         sector(table, count, terms, *inputs[4 * u : 4 * u + 4], *scratch[3 * u : 3 * u + 3])
-        for u in range(unroll)
-    ]
+    if terms % 2 == 0:
+
+        @pl.when(table[at + 2] > terms // 2)
+        def _():
+            for u in range(unroll):
+                add_pair(table, at, terms // 2, *scratch[3 * u : 3 * u + 3])
+
     for u in range(unroll):
-        kept_ref[u * height : (u + 1) * height] = results[u][:, width:]
+        kept_ref[u * height : (u + 1) * height] = scratch[3 * u + 2][height:]
     for ref, begin, end in zip(moved_refs, starts, starts[1:]):
         for u in range(unroll):
-            at = step * unroll + u - begin
-
-            @pl.when((at >= 0) & (at < end - begin))
-            def _(ref=ref, u=u, at=at):
-                ref[pl.ds(pl.multiple_of(at * height, height), height)] = results[u][:, :width]
+            to = step * unroll + u - begin
+
+            @pl.when((to >= 0) & (to < end - begin))
+            def _(ref=ref, u=u, to=to):
+                into = pl.ds(pl.multiple_of(to * height, height), height)
+                ref[into] = scratch[3 * u + 2][:height]
 
 
 def place_of(i, pieces):
@@ -162,10 +190,9 @@
     return at
 
 
-def sectors(table, pieces, tags, left, right, own, other, kept, ordered):
+def sectors(table, pieces, tags, left, right, own, other, kept, origin, roots):
     terms, count, rows, width = left.shape
-    height = own.shape[0] // TAG * TAG // count // rows * rows
-    roots = height // rows
+    height = roots * rows
     starts = [0]
     for _, size in pieces:
         starts.append(starts[-1] + size)
@@ -178,15 +205,15 @@
             for i in range(0, len(places), unroll)
         )
 
-    choices = (2, 1) if ordered or len(places) < 8 else (4, 2, 1)
-    unroll = next(unroll for unroll in choices if fits(unroll))
+    unroll = next(unroll for unroll in (2, 1) if fits(unroll))
 
     def specs(u):
         def source(i, table):
             return table[place_of(unroll * i + u, pieces)]
 
         def held(i, table):
-            return (place_of(unroll * i + u, pieces) if ordered else source(i, table), 0)
+            at = source(i, table) if origin is None else place_of(unroll * i + u, pieces) - origin
+            return (at, 0)
 
         return [
             pl.BlockSpec((terms, 1, rows, width), lambda i, t: (0, source(i, t), 0, 0)),
@@ -198,14 +225,14 @@
     in_specs = [spec for u in range(unroll) for spec in specs(u)]
     args = [left, right, own, other] * unroll
     if any(tags):
-        in_specs += [pl.BlockSpec((TAG, width), lambda i, t: (count * height // TAG, 0))] * 2
+        in_specs += [pl.BlockSpec((TAG, width), lambda i, t: (own.shape[0] // TAG - 1, 0))] * 2
         args += [own, other]
     aliases = {}
     if kept is not None:
         in_specs.append(ANY)
         args.append(kept)
         aliases = {len(args): len(pieces)}
-    rhs = (terms * width, 2 * width)
+    deep = (terms + 2 - terms % 2) * width
     shapes = [(size * height + TAG * tagged, width) for (_, size), tagged in zip(pieces, tags)]
     out = pl.pallas_call(
         functools.partial(sector_kernel, count, terms, unroll, starts, tags),
@@ -225,9 +252,9 @@
                 )
             ],
             scratch_shapes=[
-                pltpu.VMEM((2 * height, terms * width), jnp.bfloat16),
-                pltpu.VMEM(rhs, jnp.bfloat16),
-                pltpu.VMEM(rhs, jnp.bfloat16),
+                pltpu.VMEM((2 * height, deep), jnp.bfloat16),
+                pltpu.VMEM((deep, 2 * width), jnp.bfloat16),
+                pltpu.VMEM((2 * height, width), jnp.float32),
             ]
             * unroll,
         ),
@@ -322,8 +349,8 @@
     return out if with_inner else (out[0], None)
 
 
-def correct_kernel(groups, table, inner_ref, vector_ref, diag_ref, *rest):
-    parts, raw_ref = rest[:-1], rest[-1]
+def correct_kernel(groups, ahead, table, inner_ref, vector_ref, diag_ref, *rest):
+    parts, (raw_ref, ahead_ref) = rest[:-2], rest[-2:]
     count, rows, width = diag_ref.shape
     height = vector_ref.shape[0] // count
     roots = height // rows
@@ -350,14 +377,20 @@
     raw_ref[count * height :] = jnp.concatenate(
         squares + [jnp.zeros((TAG - roots, width), jnp.float32)], axis=0
     )
-
-
-def correct(table, groups, inner, vector, diag, parts):
+    ahead_ref[: ahead[1] * height] = raw_ref[ahead[0] * height : (ahead[0] + ahead[1]) * height]
+    ahead_ref[ahead[1] * height :] = raw_ref[count * height :]
+
+
+def correct(table, groups, ahead, inner, vector, diag, parts):
+    height, width = vector.shape[0] // diag.shape[0], vector.shape[1]
     return pl.pallas_call(
-        functools.partial(correct_kernel, groups),
-        out_shape=jax.ShapeDtypeStruct((vector.shape[0] + TAG, vector.shape[1]), jnp.float32),
+        functools.partial(correct_kernel, groups, ahead),
+        out_shape=[
+            jax.ShapeDtypeStruct((vector.shape[0] + TAG, width), jnp.float32),
+            jax.ShapeDtypeStruct((ahead[1] * height + TAG, width), jnp.float32),
+        ],
         in_specs=[SCALARS] + [WHOLE] * (3 + len(parts)),
-        out_specs=WHOLE,
+        out_specs=[WHOLE, WHOLE],
         compiler_params=pltpu.CompilerParams(vmem_limit_bytes=SMALL),
         cost_estimate=FREE,
         name="correct",
@@ -469,8 +502,7 @@
     per = slots // devices
     elements = slots * devices * rows * lax.axis_size("sub") * width
     vector = jnp.transpose(amplitudes, (0, 2, 1, 3)).reshape(slots * roots * rows, width)
-    arriving = lax.ppermute(vector, "sub", [(0, 1), (1, 0)])
-    table, vector = make_table(partner, term_kind, vector)
+    table = make_table(partner, term_kind, vector)
     diag = left_diag[:, :, None] + right_diag[:, None, :]
 
     staying = (0, 0, per)
@@ -494,20 +526,29 @@
     def relay(value, c):
         return lax.ppermute(value, "blk", [(p, (p + c) % devices) for p in range(devices)])
 
+    def swap(value):
+        return lax.ppermute(value, "sub", [(0, 1), (1, 0)])
+
     def partials(own, second, between):
-        other = lax.ppermute(own, "sub", [(0, 1), (1, 0)]) if second else arriving
+        if second:
+            early = (ahead, swap(ahead))
+            other = swap(after(own, early[1])[0])
+        else:
+            other = swap(own)
         kept, outgoing = None, {}
         for batch in batches:
+            early_now = second and batch is batches[0]
+            pair = early if early_now else (own, other)
             parts, kept = sectors(
                 table,
                 spans(batch),
                 [second and piece[0] > 0 for piece in batch],
                 left,
                 right,
-                own,
-                other,
+                *pair,
                 kept,
-                second,
+                (batch[0][1] if early_now else 0) if second else None,
+                roots,
             )
             outgoing.update(zip(batch, parts))
         arrived, sums, inners, done = {}, [], [], ()
@@ -535,7 +576,7 @@
                 1.0 / terms_over,
                 second,
                 not second,
-                inners if last and not second else (),
+                (),
             )
             if last:
                 mine = after(mine, *sums[1::2][-2:])[0]
@@ -548,13 +589,12 @@
         return sums, inners, done
 
     sums, inners, _ = partials(vector, False, None)
-    if len(groups) > 1:
-        inner = sums[-2][-TAG:] + sums[-1][-TAG:]
-    else:
-        inner = small_sum(inners[0], "term")
-    for axis in ("sub", "blk"):
-        inner = small_sum(inner, axis)
-    raw = correct(table, [spans(group) for group in groups], inner, vector, diag, sums)
+    inner = small_sum(small_sum(sum(inners[1:], inners[0]), "sub"), "blk")
+    inner = small_sum(after(inner, sums[-1])[0], "term")
+    first = spans(batches[0])[0]
+    raw, ahead = correct(
+        table, [spans(group) for group in groups], first, inner, vector, diag, sums
+    )
 
     def add_finished(sigma, scale, sums, at):
         return finish(

time: 189 us -> 146 us (0.77)
  Pallas kernels: 100 us -> 54.8 us
  starting transfers between devices: 30.7 us -> 36.1 us
  waiting for transfers between devices: 53.9 us -> 50.9 us
    pallas_call x2, Pallas kernels: 51.2 us -> 2.75 us  [the longest x1 1.48 us: make_table(): pl.pallas_call(functools.partial(table_kernel, devices), out_shape=jax.Sh...]
    ppermute x8, waiting for transfers between devices: 36.3 us -> 28 us  [relay(): lax.ppermute(value, 'blk', [(p, (p + c) % devices) for p in range(devices)])]
    ppermute x13 -> x14, waiting for transfers between devices: 14.2 us -> 21.2 us  [flip(): return lax.ppermute(value, axis, [(i, i ^ bit) for i in range(size)])]
    ppermute x13 -> x14, starting transfers between devices: 17.2 us -> 22.9 us  [flip(): return lax.ppermute(value, axis, [(i, i ^ bit) for i in range(size)])]
    pallas_call x4, Pallas kernels: 33.3 us -> 36.6 us  [sectors(): pl.pallas_call(functools.partial(sector_kernel, count, terms, unroll, sta...]
  transfers between devices with their start and end apart: 23 -> 25, of which waited for: 19 -> 18; matrix products, arithmetic and copies ran while one was open for 0% -> 0% of each run, Pallas kernels for 47% -> 32%
where the time goes in v7:
time: 146 us
  Pallas kernels  54.8 us (38%)
  waiting for transfers between devices  50.9 us (35%)
  starting transfers between devices  36.1 us (25%)
  local copies, waits for them, and re-layouts  2.8 us (2%)
    pallas_call x4, Pallas kernels, sectors(): pl.pallas_call(functools.partial(sector_kernel, count, terms, unroll, sta...  36.6 us
    ppermute x8, waiting for transfers between devices, relay(): lax.ppermute(value, 'blk', [(p, (p + c) % devices) for p in range(devices)])  28 us
    ppermute x14, starting transfers between devices, flip(): return lax.ppermute(value, axis, [(i, i ^ bit) for i in range(size)])  22.9 us
    ppermute x14, waiting for transfers between devices, flip(): return lax.ppermute(value, axis, [(i, i ^ bit) for i in range(size)])  21.2 us
    ppermute x8, starting transfers between devices, relay(): lax.ppermute(value, 'blk', [(p, (p + c) % devices) for p in range(devices)])  12.5 us
    pallas_call x10, Pallas kernels, combine(): pl.pallas_call(functools.partial(combine_kernel, share, starts[:-1], with...  7.14 us
    pallas_call x5, Pallas kernels, finish(): pl.pallas_call(functools.partial(finish_kernel, count, rows, places), out...  6.47 us
  transfers between devices with their start and end apart: 25, of which 18 were waited for; matrix products, arithmetic and copies ran while one was open for 0% of the time, Pallas kernels for 32%

profile of v7, /device:TPU:0, one launch (start us, length us, event | category | flops | bytes accessed | tf_op | source)
XLA Modules:
  0.0 145.8 jit_solution(11368361948751959169)
XLA Ops:
  1.1 1.4 copy-done
  3.9 1.5 %table.1 = s32[60]{0:T(128)S(1)} custom-call(s32[16]{0:T(128)S(1)} %copy-done.2, s32[8]{0:T(128)S(1)} %copy-done.3, f32[3072,128]{1,0:T(8,128)S(1)} %bitcast.10), custom_call_target="tpu_custom_call" | custom-call | tf_op jit(solution)/shard_map/table/pallas_call | solution.py:81
  5.4 5.4 %sectors.4 = (f32[768,128]{1,0:T(8,128)S(1)}, f32[3072,128]{1,0:T(8,128)S(1)}) custom-call(s32[60]{0:T(128)S(1)} %table.1, f32[8,16,64,128]{3,2,1,0:T(8,128)} %refs_4_.7, f32[8,16,128,128]{3,2,1,0:T(8,128)} %refs_5_.7, f32[3072,128]{1,0:T(8,128)S(1)} %bitcast.11, f32[3072,128]{1,0:T(8,128)S(1)} %collective-permute-done.refs_3_.refs_7_, ...), custom_call_target="tpu_custom_call" | custom-call | tf_op jit(solution)/shard_map/sectors/pallas_call | solution.py:237
  10.8 2.6 %collective-permute-start.1 = (f32[768,128]{1,0:T(8,128)S(1)}, f32[768,128]{1,0:T(8,128)S(1)}, u32[]{:S(2)}, u32[]{:S(2)}) collective-permute-start(f32[768,128]{1,0:T(8,128)S(1)} %get-tuple-element.59), channel_id=1, source_target_pairs={{0,4},{4,8},{8,12},{12,0},{1,5},{5,9},{9,13},{13,1},{2,6},{6,10},{... | collective-permute-start | bytes 1179656 | tf_op jit(solution)/shard_map/ppermute | solution.py:527
  13.5 12.9 %sectors.5 = (f32[768,128]{1,0:T(8,128)S(1)}, f32[384,128]{1,0:T(8,128)S(1)}, f32[384,128]{1,0:T(8,128)S(1)}, f32[768,128]{1,0:T(8,128)S(1)}, f32[3072,128]{1,0:T(8,128)S(1)}) custom-call(s32[60]{0:T(128)S(1)} %table.1, f32[8,16,64,128]{3,2,1,0:T(8,128)} %refs_4_.7, f32[8,16,128,128]{3,2,1,0:T(8,128)} %refs_5_.7, ...), custom_call_target="tpu_custom_call", output_to_operand_aliasing={{4}: (9, {})} | custom-call | tf_op jit(solution)/shard_map/sectors/pallas_call | solution.py:237
  26.3 2.1 %collective-permute-start.2 = (f32[768,128]{1,0:T(8,128)S(1)}, f32[768,128]{1,0:T(8,128)S(1)}, u32[]{:S(2)}, u32[]{:S(2)}) collective-permute-start(f32[768,128]{1,0:T(8,128)S(1)} %get-tuple-element.66), channel_id=1, source_target_pairs={{0,12},{4,0},{8,4},{12,8},{1,13},{5,1},{9,5},{13,9},{2,14},{6,2},{... | collective-permute-start | bytes 1179656 | tf_op jit(solution)/shard_map/ppermute | solution.py:527
  28.7 0.8 combine.10
  29.5 4.0 %collective-permute-start.4 = (f32[768,128]{1,0:T(8,128)S(1)}, f32[768,128]{1,0:T(8,128)S(1)}, u32[]{:S(2)}, u32[]{:S(2)}) collective-permute-start(f32[768,128]{1,0:T(8,128)S(1)} %get-tuple-element.62.rest_0_), channel_id=1, source_target_pairs={{0,2},{2,0},{1,3},{3,1},{4,6},{6,4},{5,7},{7,5},{8,10},{10,8},{9,1... | collective-permute-start | bytes 1179656 | tf_op jit(solution)/shard_map/ppermute | solution.py:25
  33.5 0.8 combine.11
  34.4 3.3 %collective-permute-done.2.refs_0_ = f32[768,128]{1,0:T(8,128)S(1)} collective-permute-done((f32[768,128]{1,0:T(8,128)S(1)}, f32[768,128]{1,0:T(8,128)S(1)}, u32[]{:S(2)}, u32[]{:S(2)}) %collective-permute-start.2) | collective-permute-done | bytes 393248 | tf_op jit(solution)/shard_map/ppermute | solution.py:527
  37.6 2.6 %collective-permute-start.3 = (f32[384,128]{1,0:T(8,128)S(1)}, f32[384,128]{1,0:T(8,128)S(1)}, u32[]{:S(2)}, u32[]{:S(2)}) collective-permute-start(f32[384,128]{1,0:T(8,128)S(1)} %get-tuple-element.71), channel_id=1, source_target_pairs={{0,8},{4,12},{8,0},{12,4},{1,9},{5,13},{9,1},{13,5},{2,10},{6,14},... | collective-permute-start | bytes 589832 | tf_op jit(solution)/shard_map/ppermute | solution.py:527
  40.2 0.8 combine.12
  41.0 2.4 %collective-permute-done.4.rest_1_ = f32[768,128]{1,0:T(8,128)S(1)} collective-permute-done((f32[768,128]{1,0:T(8,128)S(1)}, f32[768,128]{1,0:T(8,128)S(1)}, u32[]{:S(2)}, u32[]{:S(2)}) %collective-permute-start.4) | collective-permute-done | bytes 393248 | tf_op jit(solution)/shard_map/ppermute | solution.py:25
  43.4 2.1 %collective-permute-start.10 = (f32[768,128]{1,0:T(8,128)S(1)}, f32[768,128]{1,0:T(8,128)S(1)}, u32[]{:S(2)}, u32[]{:S(2)}) collective-permute-start(f32[768,128]{1,0:T(8,128)S(1)} %get-tuple-element.73.rest_4_), channel_id=1, source_target_pairs={{0,2},{2,0},{1,3},{3,1},{4,6},{6,4},{5,7},{7,5},{8,10},{10,8},{9,1... | collective-permute-start | bytes 1179656 | tf_op jit(solution)/shard_map/ppermute | solution.py:25
  45.5 3.7 %collective-permute-done.3.refs_0_ = f32[384,128]{1,0:T(8,128)S(1)} collective-permute-done((f32[384,128]{1,0:T(8,128)S(1)}, f32[384,128]{1,0:T(8,128)S(1)}, u32[]{:S(2)}, u32[]{:S(2)}) %collective-permute-start.3) | collective-permute-done | bytes 196640 | tf_op jit(solution)/shard_map/ppermute | solution.py:527
  49.8 2.0 %collective-permute-done.6.rest_3_ = f32[768,128]{1,0:T(8,128)S(1)} collective-permute-done((f32[768,128]{1,0:T(8,128)S(1)}, f32[768,128]{1,0:T(8,128)S(1)}, u32[]{:S(2)}, u32[]{:S(2)}) %collective-permute-start.6) | collective-permute-done | bytes 393248 | tf_op jit(solution)/shard_map/ppermute | solution.py:25
  51.8 2.1 %collective-permute-start.11 = (f32[384,128]{1,0:T(8,128)S(1)}, f32[384,128]{1,0:T(8,128)S(1)}, u32[]{:S(2)}, u32[]{:S(2)}) collective-permute-start(f32[384,128]{1,0:T(8,128)S(1)} %get-tuple-element.79.rest_6_), channel_id=1, source_target_pairs={{0,2},{2,0},{1,3},{3,1},{4,6},{6,4},{5,7},{7,5},{8,10},{10,8},{9,1... | collective-permute-start | bytes 589832 | tf_op jit(solution)/shard_map/ppermute | solution.py:25
  53.9 5.8 %collective-permute-done.5.refs_0_ = f32[384,128]{1,0:T(8,128)S(1)} collective-permute-done((f32[384,128]{1,0:T(8,128)S(1)}, f32[384,128]{1,0:T(8,128)S(1)}, u32[]{:S(2)}, u32[]{:S(2)}) %collective-permute-start.5) | collective-permute-done | bytes 196640 | tf_op jit(solution)/shard_map/ppermute | solution.py:527
  60.4 3.4 %collective-permute-done.11.rest_7_ = f32[384,128]{1,0:T(8,128)S(1)} collective-permute-done((f32[384,128]{1,0:T(8,128)S(1)}, f32[384,128]{1,0:T(8,128)S(1)}, u32[]{:S(2)}, u32[]{:S(2)}) %collective-permute-start.11) | collective-permute-done | bytes 196640 | tf_op jit(solution)/shard_map/ppermute | solution.py:25
  63.9 1.7 %collective-permute-start.12 = (f32[384,128]{1,0:T(8,128)S(1)}, f32[384,128]{1,0:T(8,128)S(1)}, u32[]{:S(2)}, u32[]{:S(2)}) collective-permute-start(f32[384,128]{1,0:T(8,128)S(1)} %get-tuple-element.83.rest_8_), channel_id=1, source_target_pairs={{0,2},{2,0},{1,3},{3,1},{4,6},{6,4},{5,7},{7,5},{8,10},{10,8},{9,1... | collective-permute-start | bytes 589832 | tf_op jit(solution)/shard_map/ppermute | solution.py:25
  65.6 1.2 collective-permute-done.7
  66.8 2.7 %collective-permute-start.8 = (f32[8,128]{1,0:T(8,128)S(1)}, f32[8,128]{1,0:T(8,128)S(1)}, u32[]{:S(2)}, u32[]{:S(2)}) collective-permute-start(f32[8,128]{1,0:T(8,128)S(1)} %add.64), channel_id=1, source_target_pairs={{0,4},{4,0},{8,12},{12,8},{1,5},{5,1},{9,13},{13,9},{2,6},{6,2},{1... | collective-permute-start | bytes 12296 | tf_op jit(solution)/shard_map/ppermute | solution.py:25
  69.5 1.6 %collective-permute-done.8 = f32[8,128]{1,0:T(8,128)S(1)} collective-permute-done((f32[8,128]{1,0:T(8,128)S(1)}, f32[8,128]{1,0:T(8,128)S(1)}, u32[]{:S(2)}, u32[]{:S(2)}) %collective-permute-start.8) | collective-permute-done | bytes 4128 | tf_op jit(solution)/shard_map/ppermute | solution.py:25
  71.0 1.2 collective-permute-start.9
  72.2 3.3 %collective-permute-done.9 = f32[8,128]{1,0:T(8,128)S(1)} collective-permute-done((f32[8,128]{1,0:T(8,128)S(1)}, f32[8,128]{1,0:T(8,128)S(1)}, u32[]{:S(2)}, u32[]{:S(2)}) %collective-permute-start.9) | collective-permute-done | bytes 4128 | tf_op jit(solution)/shard_map/ppermute | solution.py:25
  75.8 3.3 %collective-permute-done.13 = f32[8,128]{1,0:T(8,128)S(1)} collective-permute-done((f32[8,128]{1,0:T(8,128)S(1)}, f32[8,128]{1,0:T(8,128)S(1)}, u32[]{:S(2)}, u32[]{:S(2)}) %collective-permute-start.13) | collective-permute-done | bytes 4128 | tf_op jit(solution)/shard_map/ppermute | solution.py:25
  79.2 1.3 correct.1
  80.5 1.7 %collective-permute-done.14.refs_3_.refs_7_.refs_9_ = f32[776,128]{1,0:T(8,128)S(1)} collective-permute-done((f32[776,128]{1,0:T(8,128)S(1)}, f32[776,128]{1,0:T(8,128)S(1)}, u32[]{:S(2)}, u32[]{:S(2)}) %collective-permute-start.14) | collective-permute-done | bytes 397344 | tf_op jit(solution)/shard_map/ppermute | solution.py:530
  82.4 5.4 %sectors.6 = (f32[776,128]{1,0:T(8,128)S(1)}, f32[3072,128]{1,0:T(8,128)S(1)}) custom-call(s32[60]{0:T(128)S(1)} %table.1, f32[8,16,64,128]{3,2,1,0:T(8,128)} %refs_4_.7, f32[8,16,128,128]{3,2,1,0:T(8,128)} %refs_5_.7, f32[776,128]{1,0:T(8,128)S(1)} %get-tuple-element.86.refs_2_.refs_6_.refs_8_, ...), custom_call_target="tpu_custom_call" | custom-call | tf_op jit(solution)/shard_map/sectors/pallas_call | solution.py:237
  87.8 2.1 %collective-permute-start.16 = (f32[776,128]{1,0:T(8,128)S(1)}, f32[776,128]{1,0:T(8,128)S(1)}, u32[]{:S(2)}, u32[]{:S(2)}) collective-permute-start(f32[776,128]{1,0:T(8,128)S(1)} %get-tuple-element.92), channel_id=1, source_target_pairs={{0,4},{4,8},{8,12},{12,0},{1,5},{5,9},{9,13},{13,1},{2,6},{6,10},{... | collective-permute-start | bytes 1191944 | tf_op jit(solution)/shard_map/ppermute | solution.py:527
  89.9 12.9 %sectors.7 = (f32[776,128]{1,0:T(8,128)S(1)}, f32[392,128]{1,0:T(8,128)S(1)}, f32[392,128]{1,0:T(8,128)S(1)}, f32[768,128]{1,0:T(8,128)S(1)}, f32[3072,128]{1,0:T(8,128)S(1)}) custom-call(s32[60]{0:T(128)S(1)} %table.1, f32[8,16,64,128]{3,2,1,0:T(8,128)} %refs_4_.7, f32[8,16,128,128]{3,2,1,0:T(8,128)} %refs_5_.7, ...), custom_call_target="tpu_custom_call", output_to_operand_aliasing={{4}: (11, {})} | custom-call | tf_op jit(solution)/shard_map/sectors/pallas_call | solution.py:237
  102.8 1.9 %collective-permute-start.17 = (f32[776,128]{1,0:T(8,128)S(1)}, f32[776,128]{1,0:T(8,128)S(1)}, u32[]{:S(2)}, u32[]{:S(2)}) collective-permute-start(f32[776,128]{1,0:T(8,128)S(1)} %get-tuple-element.93), channel_id=1, source_target_pairs={{0,12},{4,0},{8,4},{12,8},{1,13},{5,1},{9,5},{13,9},{2,14},{6,2},{... | collective-permute-start | bytes 1191944 | tf_op jit(solution)/shard_map/ppermute | solution.py:527
  105.4 2.6 %collective-permute-start.20 = (f32[768,128]{1,0:T(8,128)S(1)}, f32[768,128]{1,0:T(8,128)S(1)}, u32[]{:S(2)}, u32[]{:S(2)}) collective-permute-start(f32[768,128]{1,0:T(8,128)S(1)} %combine.15.mine_ref), channel_id=1, source_target_pairs={{0,2},{2,0},{1,3},{3,1},{4,6},{6,4},{5,7},{7,5},{8,10},{10,8},{9,1... | collective-permute-start | bytes 1179656 | tf_op jit(solution)/shard_map/ppermute | solution.py:25
  108.7 5.3 %collective-permute-done.17.refs_0_ = f32[776,128]{1,0:T(8,128)S(1)} collective-permute-done((f32[776,128]{1,0:T(8,128)S(1)}, f32[776,128]{1,0:T(8,128)S(1)}, u32[]{:S(2)}, u32[]{:S(2)}) %collective-permute-start.17) | collective-permute-done | bytes 397344 | tf_op jit(solution)/shard_map/ppermute | solution.py:527
  114.0 1.2 collective-permute-start.18
  115.9 2.0 %collective-permute-done.20.theirs_ref = f32[768,128]{1,0:T(8,128)S(1)} collective-permute-done((f32[768,128]{1,0:T(8,128)S(1)}, f32[768,128]{1,0:T(8,128)S(1)}, u32[]{:S(2)}, u32[]{:S(2)}) %collective-permute-start.20) | collective-permute-done | bytes 393248 | tf_op jit(solution)/shard_map/ppermute | solution.py:25
  117.9 2.1 %collective-permute-start.22 = (f32[768,128]{1,0:T(8,128)S(1)}, f32[768,128]{1,0:T(8,128)S(1)}, u32[]{:S(2)}, u32[]{:S(2)}) collective-permute-start(f32[768,128]{1,0:T(8,128)S(1)} %combine.17.mine_ref), channel_id=1, source_target_pairs={{0,2},{2,0},{1,3},{3,1},{4,6},{6,4},{5,7},{7,5},{8,10},{10,8},{9,1... | collective-permute-start | bytes 1179656 | tf_op jit(solution)/shard_map/ppermute | solution.py:25
  120.0 5.4 %collective-permute-done.18.refs_0_ = f32[392,128]{1,0:T(8,128)S(1)} collective-permute-done((f32[392,128]{1,0:T(8,128)S(1)}, f32[392,128]{1,0:T(8,128)S(1)}, u32[]{:S(2)}, u32[]{:S(2)}) %collective-permute-start.18) | collective-permute-done | bytes 200736 | tf_op jit(solution)/shard_map/ppermute | solution.py:527
  126.3 2.3 %collective-permute-start.23 = (f32[384,128]{1,0:T(8,128)S(1)}, f32[384,128]{1,0:T(8,128)S(1)}, u32[]{:S(2)}, u32[]{:S(2)}) collective-permute-start(f32[384,128]{1,0:T(8,128)S(1)} %combine.18.mine_ref), channel_id=1, source_target_pairs={{0,2},{2,0},{1,3},{3,1},{4,6},{6,4},{5,7},{7,5},{8,10},{10,8},{9,1... | collective-permute-start | bytes 589832 | tf_op jit(solution)/shard_map/ppermute | solution.py:25
  128.8 1.8 %scaled.1 = f32[3072,128]{1,0:T(8,128)} custom-call(s32[60]{0:T(128)S(1)} %table.1, f32[8,128]{1,0:T(8,128)S(1)} %broadcast_in_dim.2.scale_ref, f32[3080,128]{1,0:T(8,128)S(1)} %get-tuple-element.87.refs_2_.refs_6_.refs_8_.raw_ref.vector_ref), custom_call_target="tpu_custom_call" | custom-call | tf_op jit(solution)/shard_map/scaled/pallas_call | solution.py:431
  130.7 1.3 finish.5.rest_0_
  132.0 4.5 %collective-permute-done.19.refs_0_ = f32[392,128]{1,0:T(8,128)S(1)} collective-permute-done((f32[392,128]{1,0:T(8,128)S(1)}, f32[392,128]{1,0:T(8,128)S(1)}, u32[]{:S(2)}, u32[]{:S(2)}) %collective-permute-start.19) | collective-permute-done | bytes 200736 | tf_op jit(solution)/shard_map/ppermute | solution.py:527
  137.2 0.9 collective-permute-done.23.theirs_ref
  138.1 1.7 %collective-permute-start.24 = (f32[384,128]{1,0:T(8,128)S(1)}, f32[384,128]{1,0:T(8,128)S(1)}, u32[]{:S(2)}, u32[]{:S(2)}) collective-permute-start(f32[384,128]{1,0:T(8,128)S(1)} %combine.19.mine_ref), channel_id=1, source_target_pairs={{0,2},{2,0},{1,3},{3,1},{4,6},{6,4},{5,7},{7,5},{8,10},{10,8},{9,1... | collective-permute-start | bytes 589832 | tf_op jit(solution)/shard_map/ppermute | solution.py:25
  139.8 1.3 finish.6.rest_0_
  141.2 1.3 finish.7.rest_0_
  142.5 1.3 finish.8.rest_0_
  144.5 1.2 finish.9
  (45 shorter events, 8.7 us)
Async XLA Ops:
  0.6 4.7 %collective-permute-start = (f32[3072,128]{1,0:T(8,128)}, f32[3072,128]{1,0:T(8,128)S(1)}, u32[]{:S(2)}, u32[]{:S(2)}) collective-permute-start(f32[3072,128]{1,0:T(8,128)} %bitcast.9), channel_id=1, source_target_pairs={{0,1},{1,0},{2,3},{3,2},{4,5},{5,4},{6,7},{7,6},{8,9},{9,8},{10,11... | collective-permute-start | bytes 4718600 | tf_op jit(solution)/shard_map/ppermute | solution.py:530
  1.1 1.4 copy-start
  2.6 0.7 copy-start.2
  3.2 0.7 copy-start.3
  3.9 1.5 %copy-start.1 = (f32[16,64,3,128]{3,1,2,0:T(8,128)S(1)}, f32[16,64,3,128]{3,1,2,0:T(8,128)}, u32[]{:S(2)}) copy-start(f32[16,64,3,128]{3,1,2,0:T(8,128)} %param.7) | copy-start | bytes 4718596
  10.8 15.5 %collective-permute-start.1 = (f32[768,128]{1,0:T(8,128)S(1)}, f32[768,128]{1,0:T(8,128)S(1)}, u32[]{:S(2)}, u32[]{:S(2)}) collective-permute-start(f32[768,128]{1,0:T(8,128)S(1)} %get-tuple-element.59), channel_id=1, source_target_pairs={{0,4},{4,8},{8,12},{12,0},{1,5},{5,9},{9,13},{13,1},{2,6},{6,10},{... | collective-permute-start | bytes 1179656 | tf_op jit(solution)/shard_map/ppermute | solution.py:527
  13.5 15.0 %copy-start.4 = (f32[16,128]{1,0:T(8,128)S(1)}, f32[16,128]{1,0:T(8,128)}, u32[]{:S(2)}) copy-start(f32[16,128]{1,0:T(8,128)} %param.13) | copy-start | bytes 24580
  13.5 15.0 %copy-start.5 = (f32[16,64]{1,0:T(8,128)S(1)}, f32[16,64]{1,0:T(8,128)}, u32[]{:S(2)}) copy-start(f32[16,64]{1,0:T(8,128)} %param.12) | copy-start | bytes 12292
  26.3 11.3 %collective-permute-start.2 = (f32[768,128]{1,0:T(8,128)S(1)}, f32[768,128]{1,0:T(8,128)S(1)}, u32[]{:S(2)}, u32[]{:S(2)}) collective-permute-start(f32[768,128]{1,0:T(8,128)S(1)} %get-tuple-element.66), channel_id=1, source_target_pairs={{0,12},{4,0},{8,4},{12,8},{1,13},{5,1},{9,5},{13,9},{2,14},{6,2},{... | collective-permute-start | bytes 1179656 | tf_op jit(solution)/shard_map/ppermute | solution.py:527
  29.5 13.9 %collective-permute-start.4 = (f32[768,128]{1,0:T(8,128)S(1)}, f32[768,128]{1,0:T(8,128)S(1)}, u32[]{:S(2)}, u32[]{:S(2)}) collective-permute-start(f32[768,128]{1,0:T(8,128)S(1)} %get-tuple-element.62.rest_0_), channel_id=1, source_target_pairs={{0,2},{2,0},{1,3},{3,1},{4,6},{6,4},{5,7},{7,5},{8,10},{10,8},{9,1... | collective-permute-start | bytes 1179656 | tf_op jit(solution)/shard_map/ppermute | solution.py:25
  34.3 17.5 %collective-permute-start.6 = (f32[768,128]{1,0:T(8,128)S(1)}, f32[768,128]{1,0:T(8,128)S(1)}, u32[]{:S(2)}, u32[]{:S(2)}) collective-permute-start(f32[768,128]{1,0:T(8,128)S(1)} %get-tuple-element.67.rest_2_), channel_id=1, source_target_pairs={{0,2},{2,0},{1,3},{3,1},{4,6},{6,4},{5,7},{7,5},{8,10},{10,8},{9,1... | collective-permute-start | bytes 1179656 | tf_op jit(solution)/shard_map/ppermute | solution.py:25
  37.6 11.5 %collective-permute-start.3 = (f32[384,128]{1,0:T(8,128)S(1)}, f32[384,128]{1,0:T(8,128)S(1)}, u32[]{:S(2)}, u32[]{:S(2)}) collective-permute-start(f32[384,128]{1,0:T(8,128)S(1)} %get-tuple-element.71), channel_id=1, source_target_pairs={{0,8},{4,12},{8,0},{12,4},{1,9},{5,13},{9,1},{13,5},{2,10},{6,14},... | collective-permute-start | bytes 589832 | tf_op jit(solution)/shard_map/ppermute | solution.py:527
  43.4 17.0 %collective-permute-start.10 = (f32[768,128]{1,0:T(8,128)S(1)}, f32[768,128]{1,0:T(8,128)S(1)}, u32[]{:S(2)}, u32[]{:S(2)}) collective-permute-start(f32[768,128]{1,0:T(8,128)S(1)} %get-tuple-element.73.rest_4_), channel_id=1, source_target_pairs={{0,2},{2,0},{1,3},{3,1},{4,6},{6,4},{5,7},{7,5},{8,10},{10,8},{9,1... | collective-permute-start | bytes 1179656 | tf_op jit(solution)/shard_map/ppermute | solution.py:25
  49.1 10.6 %collective-permute-start.5 = (f32[384,128]{1,0:T(8,128)S(1)}, f32[384,128]{1,0:T(8,128)S(1)}, u32[]{:S(2)}, u32[]{:S(2)}) collective-permute-start(f32[384,128]{1,0:T(8,128)S(1)} %get-tuple-element.77), channel_id=1, source_target_pairs={{0,8},{4,12},{8,0},{12,4},{1,9},{5,13},{9,1},{13,5},{2,10},{6,14},... | collective-permute-start | bytes 589832 | tf_op jit(solution)/shard_map/ppermute | solution.py:527
  51.8 12.0 %collective-permute-start.11 = (f32[384,128]{1,0:T(8,128)S(1)}, f32[384,128]{1,0:T(8,128)S(1)}, u32[]{:S(2)}, u32[]{:S(2)}) collective-permute-start(f32[384,128]{1,0:T(8,128)S(1)} %get-tuple-element.79.rest_6_), channel_id=1, source_target_pairs={{0,2},{2,0},{1,3},{3,1},{4,6},{6,4},{5,7},{7,5},{8,10},{10,8},{9,1... | collective-permute-start | bytes 589832 | tf_op jit(solution)/shard_map/ppermute | solution.py:25
  63.9 11.7 %collective-permute-start.12 = (f32[384,128]{1,0:T(8,128)S(1)}, f32[384,128]{1,0:T(8,128)S(1)}, u32[]{:S(2)}, u32[]{:S(2)}) collective-permute-start(f32[384,128]{1,0:T(8,128)S(1)} %get-tuple-element.83.rest_8_), channel_id=1, source_target_pairs={{0,2},{2,0},{1,3},{3,1},{4,6},{6,4},{5,7},{7,5},{8,10},{10,8},{9,1... | collective-permute-start | bytes 589832 | tf_op jit(solution)/shard_map/ppermute | solution.py:25
  65.6 1.2 collective-permute-start.7
  66.8 4.3 %collective-permute-start.8 = (f32[8,128]{1,0:T(8,128)S(1)}, f32[8,128]{1,0:T(8,128)S(1)}, u32[]{:S(2)}, u32[]{:S(2)}) collective-permute-start(f32[8,128]{1,0:T(8,128)S(1)} %add.64), channel_id=1, source_target_pairs={{0,4},{4,0},{8,12},{12,8},{1,5},{5,1},{9,13},{13,9},{2,6},{6,2},{1... | collective-permute-start | bytes 12296 | tf_op jit(solution)/shard_map/ppermute | solution.py:25
  71.0 4.5 %collective-permute-start.9 = (f32[8,128]{1,0:T(8,128)S(1)}, f32[8,128]{1,0:T(8,128)S(1)}, u32[]{:S(2)}, u32[]{:S(2)}) collective-permute-start(f32[8,128]{1,0:T(8,128)S(1)} %add.65), channel_id=1, source_target_pairs={{0,8},{4,12},{8,0},{12,4},{1,9},{5,13},{9,1},{13,5},{2,10},{6,14},... | collective-permute-start | bytes 12296 | tf_op jit(solution)/shard_map/ppermute | solution.py:25
  75.6 3.6 %collective-permute-start.13 = (f32[8,128]{1,0:T(8,128)S(1)}, f32[8,128]{1,0:T(8,128)S(1)}, u32[]{:S(2)}, u32[]{:S(2)}) collective-permute-start(f32[8,128]{1,0:T(8,128)S(1)} %add.66), channel_id=1, source_target_pairs={{0,2},{2,0},{1,3},{3,1},{4,6},{6,4},{5,7},{7,5},{8,10},{10,8},{9,1... | collective-permute-start | bytes 12296 | tf_op jit(solution)/shard_map/ppermute | solution.py:25
  80.4 1.8 %collective-permute-start.14 = (f32[776,128]{1,0:T(8,128)S(1)}, f32[776,128]{1,0:T(8,128)S(1)}, u32[]{:S(2)}, u32[]{:S(2)}) collective-permute-start(f32[776,128]{1,0:T(8,128)S(1)} %get-tuple-element.86.refs_2_.refs_6_.refs_8_), channel_id=1, source_target_pairs={{0,1},{1,0},{2,3},{3,2},{4,5},{5,4},{6,7},{7,6},{8,9},{9,8},{10,11... | collective-permute-start | bytes 1191944 | tf_op jit(solution)/shard_map/ppermute | solution.py:530
  82.2 7.7 %collective-permute-start.15 = (f32[3080,128]{1,0:T(8,128)S(1)}, f32[3080,128]{1,0:T(8,128)S(1)}, u32[]{:S(2)}, u32[]{:S(2)}) collective-permute-start(f32[3080,128]{1,0:T(8,128)S(1)} %get-tuple-element.87.refs_2_.refs_6_.refs_8_.raw_ref.vector_ref), channel_id=1, source_target_pairs={{0,1},{1,0},{2,3},{3,2},{4,5},{5,4},{6,7},{7,6},{8,9},{9,8},{10,11... | collective-permute-start | bytes 4730888 | tf_op jit(solution)/shard_map/ppermute | solution.py:530
  87.8 15.0 %collective-permute-start.16 = (f32[776,128]{1,0:T(8,128)S(1)}, f32[776,128]{1,0:T(8,128)S(1)}, u32[]{:S(2)}, u32[]{:S(2)}) collective-permute-start(f32[776,128]{1,0:T(8,128)S(1)} %get-tuple-element.92), channel_id=1, source_target_pairs={{0,4},{4,8},{8,12},{12,0},{1,5},{5,9},{9,13},{13,1},{2,6},{6,10},{... | collective-permute-start | bytes 1191944 | tf_op jit(solution)/shard_map/ppermute | solution.py:527
  102.8 11.3 %collective-permute-start.17 = (f32[776,128]{1,0:T(8,128)S(1)}, f32[776,128]{1,0:T(8,128)S(1)}, u32[]{:S(2)}, u32[]{:S(2)}) collective-permute-start(f32[776,128]{1,0:T(8,128)S(1)} %get-tuple-element.93), channel_id=1, source_target_pairs={{0,12},{4,0},{8,4},{12,8},{1,13},{5,1},{9,5},{13,9},{2,14},{6,2},{... | collective-permute-start | bytes 1191944 | tf_op jit(solution)/shard_map/ppermute | solution.py:527
  105.4 12.5 %collective-permute-start.20 = (f32[768,128]{1,0:T(8,128)S(1)}, f32[768,128]{1,0:T(8,128)S(1)}, u32[]{:S(2)}, u32[]{:S(2)}) collective-permute-start(f32[768,128]{1,0:T(8,128)S(1)} %combine.15.mine_ref), channel_id=1, source_target_pairs={{0,2},{2,0},{1,3},{3,1},{4,6},{6,4},{5,7},{7,5},{8,10},{10,8},{9,1... | collective-permute-start | bytes 1179656 | tf_op jit(solution)/shard_map/ppermute | solution.py:25
  108.7 17.7 %collective-permute-start.21 = (f32[768,128]{1,0:T(8,128)S(1)}, f32[768,128]{1,0:T(8,128)S(1)}, u32[]{:S(2)}, u32[]{:S(2)}) collective-permute-start(f32[768,128]{1,0:T(8,128)S(1)} %combine.16.mine_ref), channel_id=1, source_target_pairs={{0,2},{2,0},{1,3},{3,1},{4,6},{6,4},{5,7},{7,5},{8,10},{10,8},{9,1... | collective-permute-start | bytes 1179656 | tf_op jit(solution)/shard_map/ppermute | solution.py:25
  114.0 11.4 %collective-permute-start.18 = (f32[392,128]{1,0:T(8,128)S(1)}, f32[392,128]{1,0:T(8,128)S(1)}, u32[]{:S(2)}, u32[]{:S(2)}) collective-permute-start(f32[392,128]{1,0:T(8,128)S(1)} %get-tuple-element.94), channel_id=1, source_target_pairs={{0,8},{4,12},{8,0},{12,4},{1,9},{5,13},{9,1},{13,5},{2,10},{6,14},... | collective-permute-start | bytes 602120 | tf_op jit(solution)/shard_map/ppermute | solution.py:527
  117.9 19.3 %collective-permute-start.22 = (f32[768,128]{1,0:T(8,128)S(1)}, f32[768,128]{1,0:T(8,128)S(1)}, u32[]{:S(2)}, u32[]{:S(2)}) collective-permute-start(f32[768,128]{1,0:T(8,128)S(1)} %combine.17.mine_ref), channel_id=1, source_target_pairs={{0,2},{2,0},{1,3},{3,1},{4,6},{6,4},{5,7},{7,5},{8,10},{10,8},{9,1... | collective-permute-start | bytes 1179656 | tf_op jit(solution)/shard_map/ppermute | solution.py:25
  125.4 11.1 %collective-permute-start.19 = (f32[392,128]{1,0:T(8,128)S(1)}, f32[392,128]{1,0:T(8,128)S(1)}, u32[]{:S(2)}, u32[]{:S(2)}) collective-permute-start(f32[392,128]{1,0:T(8,128)S(1)} %get-tuple-element.95), channel_id=1, source_target_pairs={{0,8},{4,12},{8,0},{12,4},{1,9},{5,13},{9,1},{13,5},{2,10},{6,14},... | collective-permute-start | bytes 602120 | tf_op jit(solution)/shard_map/ppermute | solution.py:527
  126.3 11.8 %collective-permute-start.23 = (f32[384,128]{1,0:T(8,128)S(1)}, f32[384,128]{1,0:T(8,128)S(1)}, u32[]{:S(2)}, u32[]{:S(2)}) collective-permute-start(f32[384,128]{1,0:T(8,128)S(1)} %combine.18.mine_ref), channel_id=1, source_target_pairs={{0,2},{2,0},{1,3},{3,1},{4,6},{6,4},{5,7},{7,5},{8,10},{10,8},{9,1... | collective-permute-start | bytes 589832 | tf_op jit(solution)/shard_map/ppermute | solution.py:25
  138.1 6.4 %collective-permute-start.24 = (f32[384,128]{1,0:T(8,128)S(1)}, f32[384,128]{1,0:T(8,128)S(1)}, u32[]{:S(2)}, u32[]{:S(2)}) collective-permute-start(f32[384,128]{1,0:T(8,128)S(1)} %combine.19.mine_ref), channel_id=1, source_target_pairs={{0,2},{2,0},{1,3},{3,1},{4,6},{6,4},{5,7},{7,5},{8,10},{10,8},{9,1... | collective-permute-start | bytes 589832 | tf_op jit(solution)/shard_map/ppermute | solution.py:25

commit v8 on v7

--- a/solution.py
+++ b/solution.py
@@ -61,23 +61,14 @@
         return carry
 
     lax.fori_loop(0, count, place, 0)
-    moving = sum(kind_ref[k] for k in range(terms))
-    moving_pairs = lax.div(moving + 1, 2)
-    before = (jnp.int32(0), 2 * moving_pairs)
     for k in range(terms):
-        moves = kind_ref[k] == 1
-        table_ref[3 * count + k] = jnp.where(moves, before[0], before[1])
-        before = (jnp.where(moves, before[0] + 1, before[0]), jnp.where(moves, before[1], before[1] + 1))
-    at = 3 * count + terms
-    table_ref[at] = lax.axis_index("sub")
-    table_ref[at + 1] = moving_pairs
-    table_ref[at + 2] = moving_pairs + lax.div(terms - moving + 1, 2)
-    table_ref[at + 3] = moving
+        table_ref[3 * count + k] = kind_ref[k]
+    table_ref[3 * count + terms] = lax.axis_index("sub")
 
 
 def make_table(partner, term_kind, vector):
     devices = lax.axis_size("blk")
-    length = 3 * partner.shape[0] + term_kind.shape[0] + 4
+    length = 3 * partner.shape[0] + term_kind.shape[0] + 1
     return pl.pallas_call(
         functools.partial(table_kernel, devices),
         out_shape=jax.ShapeDtypeStruct((length,), jnp.int32),
@@ -89,50 +80,56 @@
     )(partner, term_kind, vector)
 
 
-def add_pair(table, at, pair, lhs, rhs, total):
-    height, width = total.shape[0] // 2, total.shape[1]
-    deep = slice(2 * pair * width, 2 * (pair + 1) * width)
-    both = jnp.dot(lhs[:, deep], rhs[deep], preferred_element_type=jnp.float32)
-    result = both[:height, :width] + both[:height, width:] + both[height:, :width]
-    kept = jnp.where(pair < table[at + 1], 0, height)
-    into = pl.ds(pl.multiple_of(kept, height), height)
-    total[into] = total[into] + result
-
-
-def sector(table, count, terms, l_ref, r_ref, own_ref, other_ref, lhs, rhs, total):
+def sector(table, count, terms, deep, l_ref, r_ref, own_ref, other_ref, lhs, high_rhs, low_rhs):
     rows, width = l_ref.shape[2], r_ref.shape[3]
-    roots = own_ref.shape[0] // rows
+    height = own_ref.shape[0]
+    roots = height // rows
     first = table[3 * count + terms] == 0
     own, other = own_ref[...], other_ref[...]
     top = jnp.where(first, own, other)
     bottom = jnp.where(first, other, own)
+    vector = jnp.concatenate(
+        [
+            jnp.concatenate([half[r * rows : (r + 1) * rows] for r in range(roots)], axis=1)
+            for half in (top, bottom)
+        ],
+        axis=0,
+    )
+    high, low = halves(vector)
     left = l_ref[:, 0].reshape(terms * rows, 2 * rows)
-    left = jnp.concatenate(halves(left), axis=1)
-
-    def lanes_of(k):
-        return pl.ds(pl.multiple_of(table[3 * count + k] * width, width), width)
-
-    for r in range(roots):
-        at = slice(r * rows, (r + 1) * rows)
-        wide = jnp.concatenate(halves(jnp.concatenate([top[at], bottom[at]], axis=0)), axis=1)
-        both = jnp.dot(
-            left, jnp.concatenate([wide, wide], axis=0), preferred_element_type=jnp.float32
+    left = jnp.concatenate(halves(left) * 2, axis=1)
+    middle = jnp.dot(
+        left,
+        jnp.concatenate([high, high, low, low], axis=0),
+        preferred_element_type=jnp.float32,
+    )
+    high, low = halves(middle)
+    for k in range(terms):
+        lanes = slice(k * width, (k + 1) * width)
+        for r in range(roots):
+            part = (slice(k * rows, (k + 1) * rows), slice(r * width, (r + 1) * width))
+            lhs[r * rows : (r + 1) * rows, lanes] = high[part]
+            lhs[(roots + r) * rows : (roots + r + 1) * rows, lanes] = low[part]
+    for k in range(terms):
+        lanes = slice(k * width, (k + 1) * width)
+        kind = table[3 * count + k]
+        used = pl.ds(pl.multiple_of((1 - kind) * width, width), width)
+        high, low = halves(r_ref[k, 0].T)
+        high_rhs[lanes, used] = high
+        low_rhs[lanes, used] = low
+    if deep:
+        high, low = lhs[:height], lhs[height:]
+        return jnp.dot(
+            jnp.concatenate([high, low, high], axis=1),
+            jnp.concatenate([high_rhs[...], high_rhs[...], low_rhs[...]], axis=0),
+            preferred_element_type=jnp.float32,
         )
-        high, low = halves(both[:, :width] + both[:, width:])
-        for k in range(terms):
-            part = slice(k * rows, (k + 1) * rows)
-            lhs[r * rows : (r + 1) * rows, lanes_of(k)] = high[part]
-            lhs[(roots + r) * rows : (roots + r + 1) * rows, lanes_of(k)] = low[part]
-    for k in range(terms):
-        high, low = halves(r_ref[k, 0].T)
-        rhs[lanes_of(k), :width] = high
-        rhs[lanes_of(k), width:] = low
-    total[...] = jnp.zeros_like(total)
-    for pair in range((terms + 1) // 2):
-        add_pair(table, 3 * count + terms, pair, lhs, rhs, total)
-
-
-def sector_kernel(count, terms, unroll, starts, tags, table, *refs):
+    tall = jnp.dot(lhs[...], high_rhs[...], preferred_element_type=jnp.float32)
+    short = jnp.dot(lhs[:height], low_rhs[...], preferred_element_type=jnp.float32)
+    return tall[:height] + tall[height:] + short
+
+
+def sector_kernel(count, terms, unroll, deep, starts, tags, table, *refs):
     inputs, scratch = refs[: 4 * unroll], refs[-3 * unroll :]
     outputs = refs[-3 * unroll - len(starts) : -3 * unroll]
     tag_refs = refs[4 * unroll : 4 * unroll + 2]
@@ -140,46 +137,31 @@
     width = kept_ref.shape[1]
     height = kept_ref.shape[0] // unroll
     step = pl.program_id(0)
-    at = 3 * count + terms
 
     @pl.when(step == 0)
     def _():
+        for at, ref in enumerate(scratch):
+            if at % 3:
+                ref[...] = jnp.zeros_like(ref)
         if any(tags):
             tag = tag_refs[0][...] + tag_refs[1][...]
             for ref, begin, end, tagged in zip(moved_refs, starts, starts[1:], tags):
                 if tagged:
                     ref[(end - begin) * height :] = tag
 
-    @pl.when((step == 0) & (lax.rem(table[at + 3], 2) + terms % 2 > 0))
-    def _():
-        empty = [jnp.where(lax.rem(table[at + 3], 2) == 1, table[at + 3], terms)]
-        empty += range(terms, scratch[0].shape[1] // width)
-        for u in range(unroll):
-            lhs, rhs, _ = scratch[3 * u : 3 * u + 3]
-            for one in empty:
-                lanes = pl.ds(pl.multiple_of(one * width, width), width)
-                lhs[:, lanes] = jnp.zeros((lhs.shape[0], width), lhs.dtype)
-                rhs[lanes] = jnp.zeros((width, rhs.shape[1]), rhs.dtype)
-
+    results = [
+        sector(table, count, terms, deep, *inputs[4 * u : 4 * u + 4], *scratch[3 * u : 3 * u + 3])
+        for u in range(unroll)
+    ]
     for u in range(unroll):
-        sector(table, count, terms, *inputs[4 * u : 4 * u + 4], *scratch[3 * u : 3 * u + 3])
-    if terms % 2 == 0:
-
-        @pl.when(table[at + 2] > terms // 2)
-        def _():
-            for u in range(unroll):
-                add_pair(table, at, terms // 2, *scratch[3 * u : 3 * u + 3])
-
-    for u in range(unroll):
-        kept_ref[u * height : (u + 1) * height] = scratch[3 * u + 2][height:]
+        kept_ref[u * height : (u + 1) * height] = results[u][:, width:]
     for ref, begin, end in zip(moved_refs, starts, starts[1:]):
         for u in range(unroll):
-            to = step * unroll + u - begin
-
-            @pl.when((to >= 0) & (to < end - begin))
-            def _(ref=ref, u=u, to=to):
-                into = pl.ds(pl.multiple_of(to * height, height), height)
-                ref[into] = scratch[3 * u + 2][:height]
+            at = step * unroll + u - begin
+
+            @pl.when((at >= 0) & (at < end - begin))
+            def _(ref=ref, u=u, at=at):
+                ref[pl.ds(pl.multiple_of(at * height, height), height)] = results[u][:, :width]
 
 
 def place_of(i, pieces):
@@ -232,10 +214,10 @@
         in_specs.append(ANY)
         args.append(kept)
         aliases = {len(args): len(pieces)}
-    deep = (terms + 2 - terms % 2) * width
+    deep = terms * width
     shapes = [(size * height + TAG * tagged, width) for (_, size), tagged in zip(pieces, tags)]
     out = pl.pallas_call(
-        functools.partial(sector_kernel, count, terms, unroll, starts, tags),
+        functools.partial(sector_kernel, count, terms, unroll, origin is not None, starts, tags),
         out_shape=[
             jax.ShapeDtypeStruct(shape, jnp.float32)
             for shape in shapes + [(count * height, width)]
@@ -254,7 +236,7 @@
             scratch_shapes=[
                 pltpu.VMEM((2 * height, deep), jnp.bfloat16),
                 pltpu.VMEM((deep, 2 * width), jnp.bfloat16),
-                pltpu.VMEM((2 * height, width), jnp.float32),
+                pltpu.VMEM((deep, 2 * width), jnp.bfloat16),
             ]
             * unroll,
         ),
@@ -505,20 +487,13 @@
     table = make_table(partner, term_kind, vector)
     diag = left_diag[:, :, None] + right_diag[:, None, :]
 
-    staying = (0, 0, per)
-    pairs = [
-        [(c, c * per, per), (devices - c, (devices - c) * per, per)]
-        for c in range(1, (devices + 1) // 2)
-    ]
-    opposite = []
+    staying, moving = (0, 0, per), []
+    for c in range(1, (devices + 1) // 2):
+        moving += [(c, c * per, per), (devices - c, (devices - c) * per, per)]
     if devices % 2 == 0:
-        c = devices // 2
-        cuts = [(0, per // 2), (per // 2, per - per // 2)] if per > 1 else [(0, per)]
-        opposite = [(c, c * per + start, size) for start, size in cuts]
-    moving = [piece for pair in pairs for piece in pair] + opposite
+        moving.append((devices // 2, devices // 2 * per, per))
     groups = [[piece] for piece in [staying] + moving]
     batches = [moving[:1], moving[1:] + [staying]]
-    late = len(opposite) == 2 and len(pairs) > 0
 
     def spans(pieces):
         return [piece[1:] for piece in pieces]
@@ -529,7 +504,7 @@
     def swap(value):
         return lax.ppermute(value, "sub", [(0, 1), (1, 0)])
 
-    def partials(own, second, between):
+    def partials(own, second):
         if second:
             early = (ahead, swap(ahead))
             other = swap(after(own, early[1])[0])
@@ -551,7 +526,7 @@
                 roots,
             )
             outgoing.update(zip(batch, parts))
-        arrived, sums, inners, done = {}, [], [], ()
+        arrived, sums, inners = {}, [], []
         for at, piece in enumerate(moving):
             value = outgoing[piece]
             if at >= 1:
@@ -559,13 +534,9 @@
             arrived[piece] = relay(value, piece[0])
         arrived[staying] = after(outgoing[staying], arrived[moving[0]])[0]
         for group in groups:
-            if late and group == groups[-1] and between:
-                piece = group[0]
-                arrived[piece], *done = after(arrived[piece], *between(sums, arrived, other))
             first, *others = [arrived[piece] for piece in group]
             if sums:
                 first = after(first, sums[-2])[0]
-            last = group == groups[-1] and len(groups) > 1
             mine, inner = combine(
                 table,
                 spans(group),
@@ -578,17 +549,13 @@
                 not second,
                 (),
             )
-            if last:
-                mine = after(mine, *sums[1::2][-2:])[0]
-            elif len(sums) >= 4:
-                mine = after(mine, sums[-3])[0]
+            if len(sums) >= 4:
+                mine = after(mine, sums[-1])[0]
             sums += add_over_term(mine)
             inners.append(inner)
-        if between and not late:
-            done = between(sums, arrived, other)
-        return sums, inners, done
-
-    sums, inners, _ = partials(vector, False, None)
+        return sums, inners, arrived, other
+
+    sums, inners, _, _ = partials(vector, False)
     inner = small_sum(small_sum(sum(inners[1:], inners[0]), "sub"), "blk")
     inner = small_sum(after(inner, sums[-1])[0], "term")
     first = spans(batches[0])[0]
@@ -596,23 +563,18 @@
         table, [spans(group) for group in groups], first, inner, vector, diag, sums
     )
 
-    def add_finished(sigma, scale, sums, at):
-        return finish(
-            table, spans(groups[at]), scale, sums[2 * at], sums[2 * at + 1], sigma, slots, rows
+    sums, _, arrived, other = partials(raw, True)
+    squares = raw[-TAG:] + other[-TAG:]
+    for piece in moving:
+        squares = squares + arrived[piece][-TAG:]
+    scale = lax.rsqrt(jnp.sum(squares, axis=1, keepdims=True) / elements + 1e-06)
+    scale = jnp.broadcast_to(scale, squares.shape)
+    correction = scaled(table, scale, raw, slots, rows)
+    sigma = None
+    for at, group in enumerate(groups):
+        sigma = finish(
+            table, spans(group), scale, sums[2 * at], sums[2 * at + 1], sigma, slots, rows
         )
-
-    def correction_and_more(sums, arrived, other):
-        squares = raw[-TAG:] + other[-TAG:]
-        first_of = {piece[0]: piece for piece in reversed(moving)}
-        for c in sorted(first_of):
-            squares = squares + arrived[first_of[c]][-TAG:]
-        scale = lax.rsqrt(jnp.sum(squares, axis=1, keepdims=True) / elements + 1e-06)
-        scale = jnp.broadcast_to(scale, squares.shape)
-        return scaled(table, scale, raw, slots, rows), scale, add_finished(None, scale, sums, 0)
-
-    sums, _, (correction, scale, sigma) = partials(raw, True, correction_and_more)
-    for at in range(1, len(groups)):
-        sigma = add_finished(sigma, scale, sums, at)
     return tuple(
         jnp.transpose(value.reshape(slots, roots, rows, width), (0, 2, 1, 3))
         for value in (sigma, correction)

time: 146 us -> 143 us (0.979)
  waiting for transfers between devices: 50.9 us -> 58 us
  starting transfers between devices: 36.1 us -> 29.8 us
  Pallas kernels: 54.8 us -> 51.5 us
    ppermute x8 -> x6, waiting for transfers between devices: 28 us -> 41 us  [relay(): lax.ppermute(value, 'blk', [(p, (p + c) % devices) for p in range(devices)])]
    ppermute x14 -> x12, starting transfers between devices: 22.9 us -> 14.2 us  [flip(): return lax.ppermute(value, axis, [(i, i ^ bit) for i in range(size)])]
    ppermute x14 -> x12, waiting for transfers between devices: 21.2 us -> 15.2 us  [flip(): return lax.ppermute(value, axis, [(i, i ^ bit) for i in range(size)])]
    ppermute x8 -> x6, starting transfers between devices: 12.5 us -> 14.8 us  [relay(): lax.ppermute(value, 'blk', [(p, (p + c) % devices) for p in range(devices)])]
    pallas_call x5 -> x4, Pallas kernels: 6.47 us -> 5.33 us  [finish(): pl.pallas_call(functools.partial(finish_kernel, count, rows, places), out...]
    pallas_call x10 -> x8, Pallas kernels: 7.14 us -> 6.02 us  [combine(): pl.pallas_call(functools.partial(combine_kernel, share, starts[:-1], with...]
  transfers between devices with their start and end apart: 25 -> 21, of which waited for: 18 -> 14; matrix products, arithmetic and copies ran while one was open for 0% -> 0% of each run, Pallas kernels for 32% -> 30%
where the time goes in v8:
time: 143 us
  waiting for transfers between devices  58 us (41%)
  Pallas kernels  51.5 us (36%)
  starting transfers between devices  29.8 us (21%)
  local copies, waits for them, and re-layouts  2.81 us (2%)
    ppermute x6, waiting for transfers between devices, relay(): lax.ppermute(value, 'blk', [(p, (p + c) % devices) for p in range(devices)])  41 us
    pallas_call x4, Pallas kernels, sectors(): pl.pallas_call(functools.partial(sector_kernel, count, terms, unroll, ori...  35.6 us
    ppermute x12, waiting for transfers between devices, flip(): return lax.ppermute(value, axis, [(i, i ^ bit) for i in range(size)])  15.2 us
    ppermute x6, starting transfers between devices, relay(): lax.ppermute(value, 'blk', [(p, (p + c) % devices) for p in range(devices)])  14.8 us
    ppermute x12, starting transfers between devices, flip(): return lax.ppermute(value, axis, [(i, i ^ bit) for i in range(size)])  14.2 us
    pallas_call x8, Pallas kernels, combine(): pl.pallas_call(functools.partial(combine_kernel, share, starts[:-1], with...  6.02 us
    pallas_call x4, Pallas kernels, finish(): pl.pallas_call(functools.partial(finish_kernel, count, rows, places), out...  5.33 us
  transfers between devices with their start and end apart: 21, of which 14 were waited for; matrix products, arithmetic and copies ran while one was open for 0% of the time, Pallas kernels for 30%

profile of v8, /device:TPU:0, one launch (start us, length us, event | category | flops | bytes accessed | tf_op | source)
XLA Modules:
  0.0 143.2 jit_solution(8727672073000608701)
XLA Ops:
  1.1 1.4 copy-done
  2.6 0.7 copy-done.2
  3.2 0.7 copy-done.3
  3.9 1.5 %table.1 = s32[57]{0:T(128)S(1)} custom-call(s32[16]{0:T(128)S(1)} %copy-done.2, s32[8]{0:T(128)S(1)} %copy-done.3, f32[3072,128]{1,0:T(8,128)S(1)} %bitcast.10), custom_call_target="tpu_custom_call" | custom-call | tf_op jit(solution)/shard_map/table/pallas_call | solution.py:72
  5.4 5.4 %sectors.4 = (f32[768,128]{1,0:T(8,128)S(1)}, f32[3072,128]{1,0:T(8,128)S(1)}) custom-call(s32[57]{0:T(128)S(1)} %table.1, f32[8,16,64,128]{3,2,1,0:T(8,128)} %refs_4_.7, f32[8,16,128,128]{3,2,1,0:T(8,128)} %refs_5_.7, f32[3072,128]{1,0:T(8,128)S(1)} %bitcast.11, f32[3072,128]{1,0:T(8,128)S(1)} %collective-permute-done.refs_3_.refs_7_, ...), custom_call_target="tpu_custom_call" | custom-call | tf_op jit(solution)/shard_map/sectors/pallas_call | solution.py:219
  10.8 2.6 %collective-permute-start.1 = (f32[768,128]{1,0:T(8,128)S(1)}, f32[768,128]{1,0:T(8,128)S(1)}, u32[]{:S(2)}, u32[]{:S(2)}) collective-permute-start(f32[768,128]{1,0:T(8,128)S(1)} %get-tuple-element.45), channel_id=1, source_target_pairs={{0,4},{4,8},{8,12},{12,0},{1,5},{5,9},{9,13},{13,1},{2,6},{6,10},{... | collective-permute-start | bytes 1179656 | tf_op jit(solution)/shard_map/ppermute | solution.py:502
  13.6 12.4 %sectors.5 = (f32[768,128]{1,0:T(8,128)S(1)}, f32[768,128]{1,0:T(8,128)S(1)}, f32[768,128]{1,0:T(8,128)S(1)}, f32[3072,128]{1,0:T(8,128)S(1)}) custom-call(s32[57]{0:T(128)S(1)} %table.1, f32[8,16,64,128]{3,2,1,0:T(8,128)} %refs_4_.7, f32[8,16,128,128]{3,2,1,0:T(8,128)} %refs_5_.7, f32[3072,128]{1,0:T(8,128)S(1)} %bitcast.13, ...), custom_call_target="tpu_custom_call", output_to_operand_aliasing={{3}: (9, {})} | custom-call | tf_op jit(solution)/shard_map/sectors/pallas_call | solution.py:219
  26.0 2.1 %collective-permute-start.2 = (f32[768,128]{1,0:T(8,128)S(1)}, f32[768,128]{1,0:T(8,128)S(1)}, u32[]{:S(2)}, u32[]{:S(2)}) collective-permute-start(f32[768,128]{1,0:T(8,128)S(1)} %get-tuple-element.52), channel_id=1, source_target_pairs={{0,12},{4,0},{8,4},{12,8},{1,13},{5,1},{9,5},{13,9},{2,14},{6,2},{... | collective-permute-start | bytes 1179656 | tf_op jit(solution)/shard_map/ppermute | solution.py:502
  28.2 0.8 combine.8
  29.0 0.8 combine.9
  29.8 1.7 %collective-permute-start.4 = (f32[768,128]{1,0:T(8,128)S(1)}, f32[768,128]{1,0:T(8,128)S(1)}, u32[]{:S(2)}, u32[]{:S(2)}) collective-permute-start(f32[768,128]{1,0:T(8,128)S(1)} %get-tuple-element.53.rest_2_), channel_id=1, source_target_pairs={{0,2},{2,0},{1,3},{3,1},{4,6},{6,4},{5,7},{7,5},{8,10},{10,8},{9,1... | collective-permute-start | bytes 1179656 | tf_op jit(solution)/shard_map/ppermute | solution.py:25
  31.5 5.8 %collective-permute-done.2.refs_0_ = f32[768,128]{1,0:T(8,128)S(1)} collective-permute-done((f32[768,128]{1,0:T(8,128)S(1)}, f32[768,128]{1,0:T(8,128)S(1)}, u32[]{:S(2)}, u32[]{:S(2)}) %collective-permute-start.2) | collective-permute-done | bytes 393248 | tf_op jit(solution)/shard_map/ppermute | solution.py:502
  37.4 2.6 %collective-permute-start.3 = (f32[768,128]{1,0:T(8,128)S(1)}, f32[768,128]{1,0:T(8,128)S(1)}, u32[]{:S(2)}, u32[]{:S(2)}) collective-permute-start(f32[768,128]{1,0:T(8,128)S(1)} %get-tuple-element.57), channel_id=1, source_target_pairs={{0,8},{4,12},{8,0},{12,4},{1,9},{5,13},{9,1},{13,5},{2,10},{6,14},... | collective-permute-start | bytes 1179656 | tf_op jit(solution)/shard_map/ppermute | solution.py:502
  39.9 0.8 combine.10
  41.1 1.5 %collective-permute-start.8 = (f32[768,128]{1,0:T(8,128)S(1)}, f32[768,128]{1,0:T(8,128)S(1)}, u32[]{:S(2)}, u32[]{:S(2)}) collective-permute-start(f32[768,128]{1,0:T(8,128)S(1)} %get-tuple-element.59.rest_4_), channel_id=1, source_target_pairs={{0,2},{2,0},{1,3},{3,1},{4,6},{6,4},{5,7},{7,5},{8,10},{10,8},{9,1... | collective-permute-start | bytes 1179656 | tf_op jit(solution)/shard_map/ppermute | solution.py:25
  42.6 14.7 %collective-permute-done.3.refs_0_ = f32[768,128]{1,0:T(8,128)S(1)} collective-permute-done((f32[768,128]{1,0:T(8,128)S(1)}, f32[768,128]{1,0:T(8,128)S(1)}, u32[]{:S(2)}, u32[]{:S(2)}) %collective-permute-start.3) | collective-permute-done | bytes 393248 | tf_op jit(solution)/shard_map/ppermute | solution.py:502
  57.3 0.8 combine.11
  58.1 1.4 collective-permute-start.9
  59.5 0.7 collective-permute-start.11
  60.2 1.2 collective-permute-done.5
  61.8 3.1 %collective-permute-done.6 = f32[8,128]{1,0:T(8,128)S(1)} collective-permute-done((f32[8,128]{1,0:T(8,128)S(1)}, f32[8,128]{1,0:T(8,128)S(1)}, u32[]{:S(2)}, u32[]{:S(2)}) %collective-permute-start.6) | collective-permute-done | bytes 4128 | tf_op jit(solution)/shard_map/ppermute | solution.py:25
  65.0 1.8 %collective-permute-start.7 = (f32[8,128]{1,0:T(8,128)S(1)}, f32[8,128]{1,0:T(8,128)S(1)}, u32[]{:S(2)}, u32[]{:S(2)}) collective-permute-start(f32[8,128]{1,0:T(8,128)S(1)} %add.61), channel_id=1, source_target_pairs={{0,8},{4,12},{8,0},{12,4},{1,9},{5,13},{9,1},{13,5},{2,10},{6,14},... | collective-permute-start | bytes 12296 | tf_op jit(solution)/shard_map/ppermute | solution.py:25
  66.8 2.7 %collective-permute-done.7 = f32[8,128]{1,0:T(8,128)S(1)} collective-permute-done((f32[8,128]{1,0:T(8,128)S(1)}, f32[8,128]{1,0:T(8,128)S(1)}, u32[]{:S(2)}, u32[]{:S(2)}) %collective-permute-start.7) | collective-permute-done | bytes 4128 | tf_op jit(solution)/shard_map/ppermute | solution.py:25
  69.5 0.7 collective-permute-done.9.rest_7_
  70.2 1.3 collective-permute-start.10
  71.5 4.8 %collective-permute-done.10 = f32[8,128]{1,0:T(8,128)S(1)} collective-permute-done((f32[8,128]{1,0:T(8,128)S(1)}, f32[8,128]{1,0:T(8,128)S(1)}, u32[]{:S(2)}, u32[]{:S(2)}) %collective-permute-start.10) | collective-permute-done | bytes 4128 | tf_op jit(solution)/shard_map/ppermute | solution.py:25
  76.3 1.3 correct.1
  77.7 1.7 %collective-permute-done.12.refs_3_.refs_7_.refs_9_ = f32[776,128]{1,0:T(8,128)S(1)} collective-permute-done((f32[776,128]{1,0:T(8,128)S(1)}, f32[776,128]{1,0:T(8,128)S(1)}, u32[]{:S(2)}, u32[]{:S(2)}) %collective-permute-start.12) | collective-permute-done | bytes 397344 | tf_op jit(solution)/shard_map/ppermute | solution.py:505
  79.5 5.4 %sectors.6 = (f32[776,128]{1,0:T(8,128)S(1)}, f32[3072,128]{1,0:T(8,128)S(1)}) custom-call(s32[57]{0:T(128)S(1)} %table.1, f32[8,16,64,128]{3,2,1,0:T(8,128)} %refs_4_.7, f32[8,16,128,128]{3,2,1,0:T(8,128)} %refs_5_.7, f32[776,128]{1,0:T(8,128)S(1)} %get-tuple-element.66.refs_2_.refs_6_.refs_8_, ...), custom_call_target="tpu_custom_call" | custom-call | tf_op jit(solution)/shard_map/sectors/pallas_call | solution.py:219
  84.9 1.9 %collective-permute-start.14 = (f32[776,128]{1,0:T(8,128)S(1)}, f32[776,128]{1,0:T(8,128)S(1)}, u32[]{:S(2)}, u32[]{:S(2)}) collective-permute-start(f32[776,128]{1,0:T(8,128)S(1)} %get-tuple-element.68), channel_id=1, source_target_pairs={{0,4},{4,8},{8,12},{12,0},{1,5},{5,9},{9,13},{13,1},{2,6},{6,10},{... | collective-permute-start | bytes 1191944 | tf_op jit(solution)/shard_map/ppermute | solution.py:502
  86.9 12.4 %sectors.7 = (f32[776,128]{1,0:T(8,128)S(1)}, f32[776,128]{1,0:T(8,128)S(1)}, f32[768,128]{1,0:T(8,128)S(1)}, f32[3072,128]{1,0:T(8,128)S(1)}) custom-call(s32[57]{0:T(128)S(1)} %table.1, f32[8,16,64,128]{3,2,1,0:T(8,128)} %refs_4_.7, f32[8,16,128,128]{3,2,1,0:T(8,128)} %refs_5_.7, ...), custom_call_target="tpu_custom_call", output_to_operand_aliasing={{3}: (11, {})} | custom-call | tf_op jit(solution)/shard_map/sectors/pallas_call | solution.py:219
  99.4 2.8 %collective-permute-start.15 = (f32[776,128]{1,0:T(8,128)S(1)}, f32[776,128]{1,0:T(8,128)S(1)}, u32[]{:S(2)}, u32[]{:S(2)}) collective-permute-start(f32[776,128]{1,0:T(8,128)S(1)} %get-tuple-element.71), channel_id=1, source_target_pairs={{0,12},{4,0},{8,4},{12,8},{1,13},{5,1},{9,5},{13,9},{2,14},{6,2},{... | collective-permute-start | bytes 1191944 | tf_op jit(solution)/shard_map/ppermute | solution.py:502
  102.2 0.7 combine.12.mine_ref
  102.9 0.7 combine.13.mine_ref
  103.6 1.6 %collective-permute-start.17 = (f32[768,128]{1,0:T(8,128)S(1)}, f32[768,128]{1,0:T(8,128)S(1)}, u32[]{:S(2)}, u32[]{:S(2)}) collective-permute-start(f32[768,128]{1,0:T(8,128)S(1)} %combine.13.mine_ref), channel_id=1, source_target_pairs={{0,2},{2,0},{1,3},{3,1},{4,6},{6,4},{5,7},{7,5},{8,10},{10,8},{9,1... | collective-permute-start | bytes 1179656 | tf_op jit(solution)/shard_map/ppermute | solution.py:25
  105.3 6.0 %collective-permute-done.15.refs_0_ = f32[776,128]{1,0:T(8,128)S(1)} collective-permute-done((f32[776,128]{1,0:T(8,128)S(1)}, f32[776,128]{1,0:T(8,128)S(1)}, u32[]{:S(2)}, u32[]{:S(2)}) %collective-permute-start.15) | collective-permute-done | bytes 397344 | tf_op jit(solution)/shard_map/ppermute | solution.py:502
  111.2 2.7 %collective-permute-start.16 = (f32[776,128]{1,0:T(8,128)S(1)}, f32[776,128]{1,0:T(8,128)S(1)}, u32[]{:S(2)}, u32[]{:S(2)}) collective-permute-start(f32[776,128]{1,0:T(8,128)S(1)} %get-tuple-element.73), channel_id=1, source_target_pairs={{0,8},{4,12},{8,0},{12,4},{1,9},{5,13},{9,1},{13,5},{2,10},{6,14},... | collective-permute-start | bytes 1191944 | tf_op jit(solution)/shard_map/ppermute | solution.py:502
  113.9 0.7 combine.14.mine_ref
  114.8 1.5 %collective-permute-start.18 = (f32[768,128]{1,0:T(8,128)S(1)}, f32[768,128]{1,0:T(8,128)S(1)}, u32[]{:S(2)}, u32[]{:S(2)}) collective-permute-start(f32[768,128]{1,0:T(8,128)S(1)} %combine.14.mine_ref), channel_id=1, source_target_pairs={{0,2},{2,0},{1,3},{3,1},{4,6},{6,4},{5,7},{7,5},{8,10},{10,8},{9,1... | collective-permute-start | bytes 1179656 | tf_op jit(solution)/shard_map/ppermute | solution.py:25
  116.8 14.4 %collective-permute-done.16.refs_0_ = f32[776,128]{1,0:T(8,128)S(1)} collective-permute-done((f32[776,128]{1,0:T(8,128)S(1)}, f32[776,128]{1,0:T(8,128)S(1)}, u32[]{:S(2)}, u32[]{:S(2)}) %collective-permute-start.16) | collective-permute-done | bytes 397344 | tf_op jit(solution)/shard_map/ppermute | solution.py:502
  131.3 0.7 combine.15.mine_ref
  132.0 1.6 %collective-permute-start.19 = (f32[768,128]{1,0:T(8,128)S(1)}, f32[768,128]{1,0:T(8,128)S(1)}, u32[]{:S(2)}, u32[]{:S(2)}) collective-permute-start(f32[768,128]{1,0:T(8,128)S(1)} %combine.15.mine_ref), channel_id=1, source_target_pairs={{0,2},{2,0},{1,3},{3,1},{4,6},{6,4},{5,7},{7,5},{8,10},{10,8},{9,1... | collective-permute-start | bytes 1179656 | tf_op jit(solution)/shard_map/ppermute | solution.py:25
  133.8 1.8 %scaled.1 = f32[3072,128]{1,0:T(8,128)} custom-call(s32[57]{0:T(128)S(1)} %table.1, f32[8,128]{1,0:T(8,128)S(1)} %broadcast_in_dim.2.scale_ref, f32[3080,128]{1,0:T(8,128)S(1)} %get-tuple-element.67.refs_2_.refs_6_.refs_8_.vector_ref.raw_ref), custom_call_target="tpu_custom_call" | custom-call | tf_op jit(solution)/shard_map/scaled/pallas_call | solution.py:413
  135.6 1.3 finish.4.rest_0_
  137.0 1.3 finish.5.rest_0_
  138.3 1.3 finish.6.rest_0_
  139.7 2.3 %collective-permute-done.19.theirs_ref = f32[768,128]{1,0:T(8,128)S(1)} collective-permute-done((f32[768,128]{1,0:T(8,128)S(1)}, f32[768,128]{1,0:T(8,128)S(1)}, u32[]{:S(2)}, u32[]{:S(2)}) %collective-permute-start.19) | collective-permute-done | bytes 393248 | tf_op jit(solution)/shard_map/ppermute | solution.py:25
  141.9 1.3 finish.7
  (34 shorter events, 2.8 us)
Async XLA Ops:
  0.6 4.7 %collective-permute-start = (f32[3072,128]{1,0:T(8,128)}, f32[3072,128]{1,0:T(8,128)S(1)}, u32[]{:S(2)}, u32[]{:S(2)}) collective-permute-start(f32[3072,128]{1,0:T(8,128)} %bitcast.9), channel_id=1, source_target_pairs={{0,1},{1,0},{2,3},{3,2},{4,5},{5,4},{6,7},{7,6},{8,9},{9,8},{10,11... | collective-permute-start | bytes 4718600 | tf_op jit(solution)/shard_map/ppermute | solution.py:505
  1.1 1.4 copy-start
  2.6 0.7 copy-start.2
  3.2 0.7 copy-start.3
  3.9 1.5 %copy-start.1 = (f32[16,64,3,128]{3,1,2,0:T(8,128)S(1)}, f32[16,64,3,128]{3,1,2,0:T(8,128)}, u32[]{:S(2)}) copy-start(f32[16,64,3,128]{3,1,2,0:T(8,128)} %param.7) | copy-start | bytes 4718596
  5.3 8.1 %copy-start.4 = (f32[16,128]{1,0:T(8,128)S(1)}, f32[16,128]{1,0:T(8,128)}, u32[]{:S(2)}) copy-start(f32[16,128]{1,0:T(8,128)} %param.13) | copy-start | bytes 24580
  5.4 8.1 %copy-start.5 = (f32[16,64]{1,0:T(8,128)S(1)}, f32[16,64]{1,0:T(8,128)}, u32[]{:S(2)}) copy-start(f32[16,64]{1,0:T(8,128)} %param.12) | copy-start | bytes 12292
  10.8 15.2 %collective-permute-start.1 = (f32[768,128]{1,0:T(8,128)S(1)}, f32[768,128]{1,0:T(8,128)S(1)}, u32[]{:S(2)}, u32[]{:S(2)}) collective-permute-start(f32[768,128]{1,0:T(8,128)S(1)} %get-tuple-element.45), channel_id=1, source_target_pairs={{0,4},{4,8},{8,12},{12,0},{1,5},{5,9},{9,13},{13,1},{2,6},{6,10},{... | collective-permute-start | bytes 1179656 | tf_op jit(solution)/shard_map/ppermute | solution.py:502
  26.0 11.3 %collective-permute-start.2 = (f32[768,128]{1,0:T(8,128)S(1)}, f32[768,128]{1,0:T(8,128)S(1)}, u32[]{:S(2)}, u32[]{:S(2)}) collective-permute-start(f32[768,128]{1,0:T(8,128)S(1)} %get-tuple-element.52), channel_id=1, source_target_pairs={{0,12},{4,0},{8,4},{12,8},{1,13},{5,1},{9,5},{13,9},{2,14},{6,2},{... | collective-permute-start | bytes 1179656 | tf_op jit(solution)/shard_map/ppermute | solution.py:502
  29.8 11.3 %collective-permute-start.4 = (f32[768,128]{1,0:T(8,128)S(1)}, f32[768,128]{1,0:T(8,128)S(1)}, u32[]{:S(2)}, u32[]{:S(2)}) collective-permute-start(f32[768,128]{1,0:T(8,128)S(1)} %get-tuple-element.53.rest_2_), channel_id=1, source_target_pairs={{0,2},{2,0},{1,3},{3,1},{4,6},{6,4},{5,7},{7,5},{8,10},{10,8},{9,1... | collective-permute-start | bytes 1179656 | tf_op jit(solution)/shard_map/ppermute | solution.py:25
  37.4 19.9 %collective-permute-start.3 = (f32[768,128]{1,0:T(8,128)S(1)}, f32[768,128]{1,0:T(8,128)S(1)}, u32[]{:S(2)}, u32[]{:S(2)}) collective-permute-start(f32[768,128]{1,0:T(8,128)S(1)} %get-tuple-element.57), channel_id=1, source_target_pairs={{0,8},{4,12},{8,0},{12,4},{1,9},{5,13},{9,1},{13,5},{2,10},{6,14},... | collective-permute-start | bytes 1179656 | tf_op jit(solution)/shard_map/ppermute | solution.py:502
  41.1 17.0 %collective-permute-start.8 = (f32[768,128]{1,0:T(8,128)S(1)}, f32[768,128]{1,0:T(8,128)S(1)}, u32[]{:S(2)}, u32[]{:S(2)}) collective-permute-start(f32[768,128]{1,0:T(8,128)S(1)} %get-tuple-element.59.rest_4_), channel_id=1, source_target_pairs={{0,2},{2,0},{1,3},{3,1},{4,6},{6,4},{5,7},{7,5},{8,10},{10,8},{9,1... | collective-permute-start | bytes 1179656 | tf_op jit(solution)/shard_map/ppermute | solution.py:25
  58.1 12.1 %collective-permute-start.9 = (f32[768,128]{1,0:T(8,128)S(1)}, f32[768,128]{1,0:T(8,128)S(1)}, u32[]{:S(2)}, u32[]{:S(2)}) collective-permute-start(f32[768,128]{1,0:T(8,128)S(1)} %get-tuple-element.63.rest_6_), channel_id=1, source_target_pairs={{0,2},{2,0},{1,3},{3,1},{4,6},{6,4},{5,7},{7,5},{8,10},{10,8},{9,1... | collective-permute-start | bytes 1179656 | tf_op jit(solution)/shard_map/ppermute | solution.py:25
  59.5 16.8 %collective-permute-start.11 = (f32[768,128]{1,0:T(8,128)S(1)}, f32[768,128]{1,0:T(8,128)S(1)}, u32[]{:S(2)}, u32[]{:S(2)}) collective-permute-start(f32[768,128]{1,0:T(8,128)S(1)} %get-tuple-element.48.rest_0_), channel_id=1, source_target_pairs={{0,2},{2,0},{1,3},{3,1},{4,6},{6,4},{5,7},{7,5},{8,10},{10,8},{9,1... | collective-permute-start | bytes 1179656 | tf_op jit(solution)/shard_map/ppermute | solution.py:25
  60.2 1.2 collective-permute-start.5
  61.4 3.6 %collective-permute-start.6 = (f32[8,128]{1,0:T(8,128)S(1)}, f32[8,128]{1,0:T(8,128)S(1)}, u32[]{:S(2)}, u32[]{:S(2)}) collective-permute-start(f32[8,128]{1,0:T(8,128)S(1)} %add.60), channel_id=1, source_target_pairs={{0,4},{4,0},{8,12},{12,8},{1,5},{5,1},{9,13},{13,9},{2,6},{6,2},{1... | collective-permute-start | bytes 12296 | tf_op jit(solution)/shard_map/ppermute | solution.py:25
  65.0 4.5 %collective-permute-start.7 = (f32[8,128]{1,0:T(8,128)S(1)}, f32[8,128]{1,0:T(8,128)S(1)}, u32[]{:S(2)}, u32[]{:S(2)}) collective-permute-start(f32[8,128]{1,0:T(8,128)S(1)} %add.61), channel_id=1, source_target_pairs={{0,8},{4,12},{8,0},{12,4},{1,9},{5,13},{9,1},{13,5},{2,10},{6,14},... | collective-permute-start | bytes 12296 | tf_op jit(solution)/shard_map/ppermute | solution.py:25
  70.2 6.1 %collective-permute-start.10 = (f32[8,128]{1,0:T(8,128)S(1)}, f32[8,128]{1,0:T(8,128)S(1)}, u32[]{:S(2)}, u32[]{:S(2)}) collective-permute-start(f32[8,128]{1,0:T(8,128)S(1)} %add.62), channel_id=1, source_target_pairs={{0,2},{2,0},{1,3},{3,1},{4,6},{6,4},{5,7},{7,5},{8,10},{10,8},{9,1... | collective-permute-start | bytes 12296 | tf_op jit(solution)/shard_map/ppermute | solution.py:25
  77.6 1.8 %collective-permute-start.12 = (f32[776,128]{1,0:T(8,128)S(1)}, f32[776,128]{1,0:T(8,128)S(1)}, u32[]{:S(2)}, u32[]{:S(2)}) collective-permute-start(f32[776,128]{1,0:T(8,128)S(1)} %get-tuple-element.66.refs_2_.refs_6_.refs_8_), channel_id=1, source_target_pairs={{0,1},{1,0},{2,3},{3,2},{4,5},{5,4},{6,7},{7,6},{8,9},{9,8},{10,11... | collective-permute-start | bytes 1191944 | tf_op jit(solution)/shard_map/ppermute | solution.py:505
  79.4 7.5 %collective-permute-start.13 = (f32[3080,128]{1,0:T(8,128)S(1)}, f32[3080,128]{1,0:T(8,128)S(1)}, u32[]{:S(2)}, u32[]{:S(2)}) collective-permute-start(f32[3080,128]{1,0:T(8,128)S(1)} %get-tuple-element.67.refs_2_.refs_6_.refs_8_.vector_ref.raw_ref), channel_id=1, source_target_pairs={{0,1},{1,0},{2,3},{3,2},{4,5},{5,4},{6,7},{7,6},{8,9},{9,8},{10,11... | collective-permute-start | bytes 4730888 | tf_op jit(solution)/shard_map/ppermute | solution.py:505
  84.9 14.5 %collective-permute-start.14 = (f32[776,128]{1,0:T(8,128)S(1)}, f32[776,128]{1,0:T(8,128)S(1)}, u32[]{:S(2)}, u32[]{:S(2)}) collective-permute-start(f32[776,128]{1,0:T(8,128)S(1)} %get-tuple-element.68), channel_id=1, source_target_pairs={{0,4},{4,8},{8,12},{12,0},{1,5},{5,9},{9,13},{13,1},{2,6},{6,10},{... | collective-permute-start | bytes 1191944 | tf_op jit(solution)/shard_map/ppermute | solution.py:502
  99.4 11.8 %collective-permute-start.15 = (f32[776,128]{1,0:T(8,128)S(1)}, f32[776,128]{1,0:T(8,128)S(1)}, u32[]{:S(2)}, u32[]{:S(2)}) collective-permute-start(f32[776,128]{1,0:T(8,128)S(1)} %get-tuple-element.71), channel_id=1, source_target_pairs={{0,12},{4,0},{8,4},{12,8},{1,13},{5,1},{9,5},{13,9},{2,14},{6,2},{... | collective-permute-start | bytes 1191944 | tf_op jit(solution)/shard_map/ppermute | solution.py:502
  103.6 11.2 %collective-permute-start.17 = (f32[768,128]{1,0:T(8,128)S(1)}, f32[768,128]{1,0:T(8,128)S(1)}, u32[]{:S(2)}, u32[]{:S(2)}) collective-permute-start(f32[768,128]{1,0:T(8,128)S(1)} %combine.13.mine_ref), channel_id=1, source_target_pairs={{0,2},{2,0},{1,3},{3,1},{4,6},{6,4},{5,7},{7,5},{8,10},{10,8},{9,1... | collective-permute-start | bytes 1179656 | tf_op jit(solution)/shard_map/ppermute | solution.py:25
  111.2 20.1 %collective-permute-start.16 = (f32[776,128]{1,0:T(8,128)S(1)}, f32[776,128]{1,0:T(8,128)S(1)}, u32[]{:S(2)}, u32[]{:S(2)}) collective-permute-start(f32[776,128]{1,0:T(8,128)S(1)} %get-tuple-element.73), channel_id=1, source_target_pairs={{0,8},{4,12},{8,0},{12,4},{1,9},{5,13},{9,1},{13,5},{2,10},{6,14},... | collective-permute-start | bytes 1191944 | tf_op jit(solution)/shard_map/ppermute | solution.py:502
  114.8 17.2 %collective-permute-start.18 = (f32[768,128]{1,0:T(8,128)S(1)}, f32[768,128]{1,0:T(8,128)S(1)}, u32[]{:S(2)}, u32[]{:S(2)}) collective-permute-start(f32[768,128]{1,0:T(8,128)S(1)} %combine.14.mine_ref), channel_id=1, source_target_pairs={{0,2},{2,0},{1,3},{3,1},{4,6},{6,4},{5,7},{7,5},{8,10},{10,8},{9,1... | collective-permute-start | bytes 1179656 | tf_op jit(solution)/shard_map/ppermute | solution.py:25
  116.3 19.3 %collective-permute-start.20 = (f32[768,128]{1,0:T(8,128)S(1)}, f32[768,128]{1,0:T(8,128)S(1)}, u32[]{:S(2)}, u32[]{:S(2)}) collective-permute-start(f32[768,128]{1,0:T(8,128)S(1)} %combine.12.mine_ref), channel_id=1, source_target_pairs={{0,2},{2,0},{1,3},{3,1},{4,6},{6,4},{5,7},{7,5},{8,10},{10,8},{9,1... | collective-permute-start | bytes 1179656 | tf_op jit(solution)/shard_map/ppermute | solution.py:25
  132.0 9.9 %collective-permute-start.19 = (f32[768,128]{1,0:T(8,128)S(1)}, f32[768,128]{1,0:T(8,128)S(1)}, u32[]{:S(2)}, u32[]{:S(2)}) collective-permute-start(f32[768,128]{1,0:T(8,128)S(1)} %combine.15.mine_ref), channel_id=1, source_target_pairs={{0,2},{2,0},{1,3},{3,1},{4,6},{6,4},{5,7},{7,5},{8,10},{10,8},{9,1... | collective-permute-start | bytes 1179656 | tf_op jit(solution)/shard_map/ppermute | solution.py:25

commit v9 on v8

--- a/solution.py
+++ b/solution.py
@@ -80,7 +80,7 @@
     )(partner, term_kind, vector)
 
 
-def sector(table, count, terms, deep, l_ref, r_ref, own_ref, other_ref, lhs, high_rhs, low_rhs):
+def sector(table, count, terms, l_ref, r_ref, own_ref, other_ref, lhs, high_rhs, low_rhs):
     rows, width = l_ref.shape[2], r_ref.shape[3]
     height = own_ref.shape[0]
     roots = height // rows
@@ -88,26 +88,18 @@
     own, other = own_ref[...], other_ref[...]
     top = jnp.where(first, own, other)
     bottom = jnp.where(first, other, own)
-    vector = jnp.concatenate(
-        [
-            jnp.concatenate([half[r * rows : (r + 1) * rows] for r in range(roots)], axis=1)
-            for half in (top, bottom)
-        ],
-        axis=0,
-    )
-    high, low = halves(vector)
     left = l_ref[:, 0].reshape(terms * rows, 2 * rows)
-    left = jnp.concatenate(halves(left) * 2, axis=1)
-    middle = jnp.dot(
-        left,
-        jnp.concatenate([high, high, low, low], axis=0),
-        preferred_element_type=jnp.float32,
-    )
-    high, low = halves(middle)
-    for k in range(terms):
-        lanes = slice(k * width, (k + 1) * width)
-        for r in range(roots):
-            part = (slice(k * rows, (k + 1) * rows), slice(r * width, (r + 1) * width))
+    left = jnp.concatenate(halves(left), axis=1)
+    for r in range(roots):
+        at = slice(r * rows, (r + 1) * rows)
+        wide = jnp.concatenate(halves(jnp.concatenate([top[at], bottom[at]], axis=0)), axis=1)
+        both = jnp.dot(
+            left, jnp.concatenate([wide, wide], axis=0), preferred_element_type=jnp.float32
+        )
+        high, low = halves(both[:, :width] + both[:, width:])
+        for k in range(terms):
+            lanes = slice(k * width, (k + 1) * width)
+            part = slice(k * rows, (k + 1) * rows)
             lhs[r * rows : (r + 1) * rows, lanes] = high[part]
             lhs[(roots + r) * rows : (roots + r + 1) * rows, lanes] = low[part]
     for k in range(terms):
@@ -117,19 +109,15 @@
         high, low = halves(r_ref[k, 0].T)
         high_rhs[lanes, used] = high
         low_rhs[lanes, used] = low
-    if deep:
-        high, low = lhs[:height], lhs[height:]
-        return jnp.dot(
-            jnp.concatenate([high, low, high], axis=1),
-            jnp.concatenate([high_rhs[...], high_rhs[...], low_rhs[...]], axis=0),
-            preferred_element_type=jnp.float32,
-        )
-    tall = jnp.dot(lhs[...], high_rhs[...], preferred_element_type=jnp.float32)
-    short = jnp.dot(lhs[:height], low_rhs[...], preferred_element_type=jnp.float32)
-    return tall[:height] + tall[height:] + short
-
-
-def sector_kernel(count, terms, unroll, deep, starts, tags, table, *refs):
+    high, low = lhs[:height], lhs[height:]
+    return jnp.dot(
+        jnp.concatenate([high, low, high], axis=1),
+        jnp.concatenate([high_rhs[...], high_rhs[...], low_rhs[...]], axis=0),
+        preferred_element_type=jnp.float32,
+    )
+
+
+def sector_kernel(count, terms, unroll, starts, tags, table, *refs):
     inputs, scratch = refs[: 4 * unroll], refs[-3 * unroll :]
     outputs = refs[-3 * unroll - len(starts) : -3 * unroll]
     tag_refs = refs[4 * unroll : 4 * unroll + 2]
@@ -150,7 +138,7 @@
                     ref[(end - begin) * height :] = tag
 
     results = [
-        sector(table, count, terms, deep, *inputs[4 * u : 4 * u + 4], *scratch[3 * u : 3 * u + 3])
+        sector(table, count, terms, *inputs[4 * u : 4 * u + 4], *scratch[3 * u : 3 * u + 3])
         for u in range(unroll)
     ]
     for u in range(unroll):
@@ -217,7 +205,7 @@
     deep = terms * width
     shapes = [(size * height + TAG * tagged, width) for (_, size), tagged in zip(pieces, tags)]
     out = pl.pallas_call(
-        functools.partial(sector_kernel, count, terms, unroll, origin is not None, starts, tags),
+        functools.partial(sector_kernel, count, terms, unroll, starts, tags),
         out_shape=[
             jax.ShapeDtypeStruct(shape, jnp.float32)
             for shape in shapes + [(count * height, width)]
@@ -487,11 +475,9 @@
     table = make_table(partner, term_kind, vector)
     diag = left_diag[:, :, None] + right_diag[:, None, :]
 
-    staying, moving = (0, 0, per), []
-    for c in range(1, (devices + 1) // 2):
-        moving += [(c, c * per, per), (devices - c, (devices - c) * per, per)]
-    if devices % 2 == 0:
-        moving.append((devices // 2, devices // 2 * per, per))
+    staying = (0, 0, per)
+    moving = sorted(range(1, devices), key=lambda c: (-min(c, devices - c), c))
+    moving = [(c, c * per, per) for c in moving]
     groups = [[piece] for piece in [staying] + moving]
     batches = [moving[:1], moving[1:] + [staying]]
 
@@ -532,7 +518,7 @@
             if at >= 1:
                 value = after(value, arrived[moving[at - 1]])[0]
             arrived[piece] = relay(value, piece[0])
-        arrived[staying] = after(outgoing[staying], arrived[moving[0]])[0]
+        arrived[staying] = outgoing[staying]
         for group in groups:
             first, *others = [arrived[piece] for piece in group]
             if sums:
@@ -549,7 +535,7 @@
                 not second,
                 (),
             )
-            if len(sums) >= 4:
+            if sums:
                 mine = after(mine, sums[-1])[0]
             sums += add_over_term(mine)
             inners.append(inner)

time: 143 us -> 135 us (0.944)
  starting transfers between devices: 29.8 us -> 20.5 us
  waiting for transfers between devices: 58 us -> 61.1 us
  Pallas kernels: 51.5 us -> 49.7 us
    ppermute x6, starting transfers between devices: 14.8 us -> 6.58 us  [relay(): lax.ppermute(value, 'blk', [(p, (p + c) % devices) for p in range(devices)])]
    ppermute x12, waiting for transfers between devices: 15.2 us -> 22.1 us  [flip(): return lax.ppermute(value, axis, [(i, i ^ bit) for i in range(size)])]
    ppermute x6, waiting for transfers between devices: 41 us -> 37.3 us  [relay(): lax.ppermute(value, 'blk', [(p, (p + c) % devices) for p in range(devices)])]
    pallas_call x4, Pallas kernels: 35.6 us -> 33.8 us  [sectors(): pl.pallas_call(functools.partial(sector_kernel, count, terms, unroll, sta...]
  transfers between devices with their start and end apart: 21 -> 21, of which waited for: 14 -> 18; matrix products, arithmetic and copies ran while one was open for 0% -> 0% of each run, Pallas kernels for 30% -> 31%
where the time goes in v9:
time: 135 us
  waiting for transfers between devices  61.1 us (45%)
  Pallas kernels  49.7 us (37%)
  starting transfers between devices  20.5 us (15%)
  local copies, waits for them, and re-layouts  2.81 us (2%)
    ppermute x6, waiting for transfers between devices, relay(): lax.ppermute(value, 'blk', [(p, (p + c) % devices) for p in range(devices)])  37.3 us
    pallas_call x4, Pallas kernels, sectors(): pl.pallas_call(functools.partial(sector_kernel, count, terms, unroll, sta...  33.8 us
    ppermute x12, waiting for transfers between devices, flip(): return lax.ppermute(value, axis, [(i, i ^ bit) for i in range(size)])  22.1 us
    ppermute x12, starting transfers between devices, flip(): return lax.ppermute(value, axis, [(i, i ^ bit) for i in range(size)])  13.1 us
    ppermute x6, starting transfers between devices, relay(): lax.ppermute(value, 'blk', [(p, (p + c) % devices) for p in range(devices)])  6.58 us
    pallas_call x8, Pallas kernels, combine(): pl.pallas_call(functools.partial(combine_kernel, share, starts[:-1], with...  6.02 us
    pallas_call x4, Pallas kernels, finish(): pl.pallas_call(functools.partial(finish_kernel, count, rows, places), out...  5.33 us
    unnamed x12, local copies, waits for them, and re-layouts  2.73 us
  transfers between devices with their start and end apart: 21, of which 18 were waited for; matrix products, arithmetic and copies ran while one was open for 0% of the time, Pallas kernels for 31%

profile of v9, /device:TPU:0, one launch (start us, length us, event | category | flops | bytes accessed | tf_op | source)
XLA Modules:
  0.0 135.2 jit_solution(4782748814803016709)
XLA Ops:
  1.1 1.4 %copy-done = f32[16,64,3,128]{3,1,2,0:T(8,128)S(1)} copy-done((f32[16,64,3,128]{3,1,2,0:T(8,128)S(1)}, f32[16,64,3,128]{3,1,2,0:T(8,128)}, u32[]{:S(2)}) %copy-start) | copy-done | bytes 1572888
  3.9 1.5 %table.1 = s32[57]{0:T(128)S(1)} custom-call(s32[16]{0:T(128)S(1)} %copy-done.2, s32[8]{0:T(128)S(1)} %copy-done.3, f32[3072,128]{1,0:T(8,128)S(1)} %bitcast.10), custom_call_target="tpu_custom_call" | custom-call | tf_op jit(solution)/shard_map/table/pallas_call | solution.py:72
  5.4 5.2 %sectors.4 = (f32[768,128]{1,0:T(8,128)S(1)}, f32[3072,128]{1,0:T(8,128)S(1)}) custom-call(s32[57]{0:T(128)S(1)} %table.1, f32[8,16,64,128]{3,2,1,0:T(8,128)} %refs_4_.7, f32[8,16,128,128]{3,2,1,0:T(8,128)} %refs_5_.7, f32[3072,128]{1,0:T(8,128)S(1)} %bitcast.11, f32[3072,128]{1,0:T(8,128)S(1)} %collective-permute-done.refs_3_.refs_7_, ...), custom_call_target="tpu_custom_call" | custom-call | tf_op jit(solution)/shard_map/sectors/pallas_call | solution.py:207
  10.6 3.7 %collective-permute-start.1 = (f32[768,128]{1,0:T(8,128)S(1)}, f32[768,128]{1,0:T(8,128)S(1)}, u32[]{:S(2)}, u32[]{:S(2)}) collective-permute-start(f32[768,128]{1,0:T(8,128)S(1)} %get-tuple-element.46), channel_id=1, source_target_pairs={{0,8},{4,12},{8,0},{12,4},{1,9},{5,13},{9,1},{13,5},{2,10},{6,14},... | collective-permute-start | bytes 1179656 | tf_op jit(solution)/shard_map/ppermute | solution.py:488
  14.4 11.7 %sectors.5 = (f32[768,128]{1,0:T(8,128)S(1)}, f32[768,128]{1,0:T(8,128)S(1)}, f32[768,128]{1,0:T(8,128)S(1)}, f32[3072,128]{1,0:T(8,128)S(1)}) custom-call(s32[57]{0:T(128)S(1)} %table.1, f32[8,16,64,128]{3,2,1,0:T(8,128)} %refs_4_.7, f32[8,16,128,128]{3,2,1,0:T(8,128)} %refs_5_.7, f32[3072,128]{1,0:T(8,128)S(1)} %bitcast.13, ...), custom_call_target="tpu_custom_call", output_to_operand_aliasing={{3}: (9, {})} | custom-call | tf_op jit(solution)/shard_map/sectors/pallas_call | solution.py:207
  26.2 0.8 combine.8
  27.0 1.6 %collective-permute-start.3 = (f32[768,128]{1,0:T(8,128)S(1)}, f32[768,128]{1,0:T(8,128)S(1)}, u32[]{:S(2)}, u32[]{:S(2)}) collective-permute-start(f32[768,128]{1,0:T(8,128)S(1)} %get-tuple-element.47.rest_0_), channel_id=1, source_target_pairs={{0,2},{2,0},{1,3},{3,1},{4,6},{6,4},{5,7},{7,5},{8,10},{10,8},{9,1... | collective-permute-start | bytes 1179656 | tf_op jit(solution)/shard_map/ppermute | solution.py:25
  28.6 3.9 %collective-permute-done.1.refs_0_ = f32[768,128]{1,0:T(8,128)S(1)} collective-permute-done((f32[768,128]{1,0:T(8,128)S(1)}, f32[768,128]{1,0:T(8,128)S(1)}, u32[]{:S(2)}, u32[]{:S(2)}) %collective-permute-start.1) | collective-permute-done | bytes 393248 | tf_op jit(solution)/shard_map/ppermute | solution.py:488
  32.4 0.7 collective-permute-start.2
  33.2 0.8 combine.9
  34.0 4.3 %collective-permute-done.3.rest_1_ = f32[768,128]{1,0:T(8,128)S(1)} collective-permute-done((f32[768,128]{1,0:T(8,128)S(1)}, f32[768,128]{1,0:T(8,128)S(1)}, u32[]{:S(2)}, u32[]{:S(2)}) %collective-permute-start.3) | collective-permute-done | bytes 393248 | tf_op jit(solution)/shard_map/ppermute | solution.py:25
  38.3 1.5 %collective-permute-start.5 = (f32[768,128]{1,0:T(8,128)S(1)}, f32[768,128]{1,0:T(8,128)S(1)}, u32[]{:S(2)}, u32[]{:S(2)}) collective-permute-start(f32[768,128]{1,0:T(8,128)S(1)} %get-tuple-element.53.rest_2_), channel_id=1, source_target_pairs={{0,2},{2,0},{1,3},{3,1},{4,6},{6,4},{5,7},{7,5},{8,10},{10,8},{9,1... | collective-permute-start | bytes 1179656 | tf_op jit(solution)/shard_map/ppermute | solution.py:25
  39.8 5.5 %collective-permute-done.2.refs_0_ = f32[768,128]{1,0:T(8,128)S(1)} collective-permute-done((f32[768,128]{1,0:T(8,128)S(1)}, f32[768,128]{1,0:T(8,128)S(1)}, u32[]{:S(2)}, u32[]{:S(2)}) %collective-permute-start.2) | collective-permute-done | bytes 393248 | tf_op jit(solution)/shard_map/ppermute | solution.py:488
  45.3 1.7 %collective-permute-start.4 = (f32[768,128]{1,0:T(8,128)S(1)}, f32[768,128]{1,0:T(8,128)S(1)}, u32[]{:S(2)}, u32[]{:S(2)}) collective-permute-start(f32[768,128]{1,0:T(8,128)S(1)} %get-tuple-element.57), channel_id=1, source_target_pairs={{0,12},{4,0},{8,4},{12,8},{1,13},{5,1},{9,5},{13,9},{2,14},{6,2},{... | collective-permute-start | bytes 1179656 | tf_op jit(solution)/shard_map/ppermute | solution.py:488
  47.1 0.8 combine.10
  47.9 0.8 collective-permute-done.5.rest_3_
  48.7 1.5 %collective-permute-start.9 = (f32[768,128]{1,0:T(8,128)S(1)}, f32[768,128]{1,0:T(8,128)S(1)}, u32[]{:S(2)}, u32[]{:S(2)}) collective-permute-start(f32[768,128]{1,0:T(8,128)S(1)} %get-tuple-element.59.rest_4_), channel_id=1, source_target_pairs={{0,2},{2,0},{1,3},{3,1},{4,6},{6,4},{5,7},{7,5},{8,10},{10,8},{9,1... | collective-permute-start | bytes 1179656 | tf_op jit(solution)/shard_map/ppermute | solution.py:25
  50.2 5.4 %collective-permute-done.4.refs_0_ = f32[768,128]{1,0:T(8,128)S(1)} collective-permute-done((f32[768,128]{1,0:T(8,128)S(1)}, f32[768,128]{1,0:T(8,128)S(1)}, u32[]{:S(2)}, u32[]{:S(2)}) %collective-permute-start.4) | collective-permute-done | bytes 393248 | tf_op jit(solution)/shard_map/ppermute | solution.py:488
  55.6 0.8 combine.11
  56.4 1.8 %collective-permute-done.9.rest_5_ = f32[768,128]{1,0:T(8,128)S(1)} collective-permute-done((f32[768,128]{1,0:T(8,128)S(1)}, f32[768,128]{1,0:T(8,128)S(1)}, u32[]{:S(2)}, u32[]{:S(2)}) %collective-permute-start.9) | collective-permute-done | bytes 393248 | tf_op jit(solution)/shard_map/ppermute | solution.py:25
  58.2 1.5 %collective-permute-start.10 = (f32[768,128]{1,0:T(8,128)S(1)}, f32[768,128]{1,0:T(8,128)S(1)}, u32[]{:S(2)}, u32[]{:S(2)}) collective-permute-start(f32[768,128]{1,0:T(8,128)S(1)} %get-tuple-element.63.rest_6_), channel_id=1, source_target_pairs={{0,2},{2,0},{1,3},{3,1},{4,6},{6,4},{5,7},{7,5},{8,10},{10,8},{9,1... | collective-permute-start | bytes 1179656 | tf_op jit(solution)/shard_map/ppermute | solution.py:25
  59.7 1.2 collective-permute-done.6
  60.8 1.6 %collective-permute-start.7 = (f32[8,128]{1,0:T(8,128)S(1)}, f32[8,128]{1,0:T(8,128)S(1)}, u32[]{:S(2)}, u32[]{:S(2)}) collective-permute-start(f32[8,128]{1,0:T(8,128)S(1)} %add.60), channel_id=1, source_target_pairs={{0,4},{4,0},{8,12},{12,8},{1,5},{5,1},{9,13},{13,9},{2,6},{6,2},{1... | collective-permute-start | bytes 12296 | tf_op jit(solution)/shard_map/ppermute | solution.py:25
  62.4 2.0 %collective-permute-done.7 = f32[8,128]{1,0:T(8,128)S(1)} collective-permute-done((f32[8,128]{1,0:T(8,128)S(1)}, f32[8,128]{1,0:T(8,128)S(1)}, u32[]{:S(2)}, u32[]{:S(2)}) %collective-permute-start.7) | collective-permute-done | bytes 4128 | tf_op jit(solution)/shard_map/ppermute | solution.py:25
  64.8 4.1 %collective-permute-done.8 = f32[8,128]{1,0:T(8,128)S(1)} collective-permute-done((f32[8,128]{1,0:T(8,128)S(1)}, f32[8,128]{1,0:T(8,128)S(1)}, u32[]{:S(2)}, u32[]{:S(2)}) %collective-permute-start.8) | collective-permute-done | bytes 4128 | tf_op jit(solution)/shard_map/ppermute | solution.py:25
  69.5 3.1 %collective-permute-done.11 = f32[8,128]{1,0:T(8,128)S(1)} collective-permute-done((f32[8,128]{1,0:T(8,128)S(1)}, f32[8,128]{1,0:T(8,128)S(1)}, u32[]{:S(2)}, u32[]{:S(2)}) %collective-permute-start.11) | collective-permute-done | bytes 4128 | tf_op jit(solution)/shard_map/ppermute | solution.py:25
  72.6 1.3 correct.1
  73.9 1.7 %collective-permute-done.12.refs_3_.refs_7_.refs_9_ = f32[776,128]{1,0:T(8,128)S(1)} collective-permute-done((f32[776,128]{1,0:T(8,128)S(1)}, f32[776,128]{1,0:T(8,128)S(1)}, u32[]{:S(2)}, u32[]{:S(2)}) %collective-permute-start.12) | collective-permute-done | bytes 397344 | tf_op jit(solution)/shard_map/ppermute | solution.py:491
  75.8 5.2 %sectors.6 = (f32[776,128]{1,0:T(8,128)S(1)}, f32[3072,128]{1,0:T(8,128)S(1)}) custom-call(s32[57]{0:T(128)S(1)} %table.1, f32[8,16,64,128]{3,2,1,0:T(8,128)} %refs_4_.7, f32[8,16,128,128]{3,2,1,0:T(8,128)} %refs_5_.7, f32[776,128]{1,0:T(8,128)S(1)} %get-tuple-element.66.refs_2_.refs_6_.refs_8_, ...), custom_call_target="tpu_custom_call" | custom-call | tf_op jit(solution)/shard_map/sectors/pallas_call | solution.py:207
  81.4 11.7 %sectors.7 = (f32[776,128]{1,0:T(8,128)S(1)}, f32[776,128]{1,0:T(8,128)S(1)}, f32[768,128]{1,0:T(8,128)S(1)}, f32[3072,128]{1,0:T(8,128)S(1)}) custom-call(s32[57]{0:T(128)S(1)} %table.1, f32[8,16,64,128]{3,2,1,0:T(8,128)} %refs_4_.7, f32[8,16,128,128]{3,2,1,0:T(8,128)} %refs_5_.7, ...), custom_call_target="tpu_custom_call", output_to_operand_aliasing={{3}: (11, {})} | custom-call | tf_op jit(solution)/shard_map/sectors/pallas_call | solution.py:207
  93.1 0.7 combine.12.mine_ref
  93.8 1.3 collective-permute-start.17
  95.1 6.8 %collective-permute-done.14.refs_0_ = f32[776,128]{1,0:T(8,128)S(1)} collective-permute-done((f32[776,128]{1,0:T(8,128)S(1)}, f32[776,128]{1,0:T(8,128)S(1)}, u32[]{:S(2)}, u32[]{:S(2)}) %collective-permute-start.14) | collective-permute-done | bytes 397344 | tf_op jit(solution)/shard_map/ppermute | solution.py:488
  101.9 0.7 combine.13.mine_ref
  102.6 2.4 %collective-permute-done.17.theirs_ref = f32[768,128]{1,0:T(8,128)S(1)} collective-permute-done((f32[768,128]{1,0:T(8,128)S(1)}, f32[768,128]{1,0:T(8,128)S(1)}, u32[]{:S(2)}, u32[]{:S(2)}) %collective-permute-start.17) | collective-permute-done | bytes 393248 | tf_op jit(solution)/shard_map/ppermute | solution.py:25
  105.0 1.2 collective-permute-start.18
  106.2 8.2 %collective-permute-done.15.refs_0_ = f32[776,128]{1,0:T(8,128)S(1)} collective-permute-done((f32[776,128]{1,0:T(8,128)S(1)}, f32[776,128]{1,0:T(8,128)S(1)}, u32[]{:S(2)}, u32[]{:S(2)}) %collective-permute-start.15) | collective-permute-done | bytes 397344 | tf_op jit(solution)/shard_map/ppermute | solution.py:488
  114.4 0.7 combine.14.mine_ref
  115.3 1.2 collective-permute-start.19
  116.5 7.6 %collective-permute-done.16.refs_0_ = f32[776,128]{1,0:T(8,128)S(1)} collective-permute-done((f32[776,128]{1,0:T(8,128)S(1)}, f32[776,128]{1,0:T(8,128)S(1)}, u32[]{:S(2)}, u32[]{:S(2)}) %collective-permute-start.16) | collective-permute-done | bytes 397344 | tf_op jit(solution)/shard_map/ppermute | solution.py:488
  124.1 0.7 combine.15.mine_ref
  125.1 0.9 collective-permute-start.20
  126.1 1.8 %scaled.1 = f32[3072,128]{1,0:T(8,128)} custom-call(s32[57]{0:T(128)S(1)} %table.1, f32[8,128]{1,0:T(8,128)S(1)} %broadcast_in_dim.2.scale_ref, f32[3080,128]{1,0:T(8,128)S(1)} %get-tuple-element.67.refs_2_.refs_6_.refs_8_.vector_ref.raw_ref), custom_call_target="tpu_custom_call" | custom-call | tf_op jit(solution)/shard_map/scaled/pallas_call | solution.py:401
  127.9 1.3 finish.4.rest_0_
  129.3 1.3 finish.5.rest_0_
  130.6 1.3 finish.6.rest_0_
  132.0 1.9 %collective-permute-done.20.theirs_ref = f32[768,128]{1,0:T(8,128)S(1)} collective-permute-done((f32[768,128]{1,0:T(8,128)S(1)}, f32[768,128]{1,0:T(8,128)S(1)}, u32[]{:S(2)}, u32[]{:S(2)}) %collective-permute-start.20) | collective-permute-done | bytes 393248 | tf_op jit(solution)/shard_map/ppermute | solution.py:25
  133.9 1.3 finish.7
  (34 shorter events, 4.2 us)
Async XLA Ops:
  0.6 4.7 %collective-permute-start = (f32[3072,128]{1,0:T(8,128)}, f32[3072,128]{1,0:T(8,128)S(1)}, u32[]{:S(2)}, u32[]{:S(2)}) collective-permute-start(f32[3072,128]{1,0:T(8,128)} %bitcast.9), channel_id=1, source_target_pairs={{0,1},{1,0},{2,3},{3,2},{4,5},{5,4},{6,7},{7,6},{8,9},{9,8},{10,11... | collective-permute-start | bytes 4718600 | tf_op jit(solution)/shard_map/ppermute | solution.py:491
  1.1 1.4 %copy-start = (f32[16,64,3,128]{3,1,2,0:T(8,128)S(1)}, f32[16,64,3,128]{3,1,2,0:T(8,128)}, u32[]{:S(2)}) copy-start(f32[16,64,3,128]{3,1,2,0:T(8,128)} %param.7) | copy-start | bytes 4718596
  2.6 0.7 copy-start.2
  3.2 0.7 copy-start.3
  3.9 1.5 %copy-start.1 = (f32[16,64,3,128]{3,1,2,0:T(8,128)S(1)}, f32[16,64,3,128]{3,1,2,0:T(8,128)}, u32[]{:S(2)}) copy-start(f32[16,64,3,128]{3,1,2,0:T(8,128)} %param.7) | copy-start | bytes 4718596
  5.3 8.9 %copy-start.4 = (f32[16,128]{1,0:T(8,128)S(1)}, f32[16,128]{1,0:T(8,128)}, u32[]{:S(2)}) copy-start(f32[16,128]{1,0:T(8,128)} %param.13) | copy-start | bytes 24580
  5.4 8.9 %copy-start.5 = (f32[16,64]{1,0:T(8,128)S(1)}, f32[16,64]{1,0:T(8,128)}, u32[]{:S(2)}) copy-start(f32[16,64]{1,0:T(8,128)} %param.12) | copy-start | bytes 12292
  10.6 21.9 %collective-permute-start.1 = (f32[768,128]{1,0:T(8,128)S(1)}, f32[768,128]{1,0:T(8,128)S(1)}, u32[]{:S(2)}, u32[]{:S(2)}) collective-permute-start(f32[768,128]{1,0:T(8,128)S(1)} %get-tuple-element.46), channel_id=1, source_target_pairs={{0,8},{4,12},{8,0},{12,4},{1,9},{5,13},{9,1},{13,5},{2,10},{6,14},... | collective-permute-start | bytes 1179656 | tf_op jit(solution)/shard_map/ppermute | solution.py:488
  27.0 11.3 %collective-permute-start.3 = (f32[768,128]{1,0:T(8,128)S(1)}, f32[768,128]{1,0:T(8,128)S(1)}, u32[]{:S(2)}, u32[]{:S(2)}) collective-permute-start(f32[768,128]{1,0:T(8,128)S(1)} %get-tuple-element.47.rest_0_), channel_id=1, source_target_pairs={{0,2},{2,0},{1,3},{3,1},{4,6},{6,4},{5,7},{7,5},{8,10},{10,8},{9,1... | collective-permute-start | bytes 1179656 | tf_op jit(solution)/shard_map/ppermute | solution.py:25
  32.4 12.9 %collective-permute-start.2 = (f32[768,128]{1,0:T(8,128)S(1)}, f32[768,128]{1,0:T(8,128)S(1)}, u32[]{:S(2)}, u32[]{:S(2)}) collective-permute-start(f32[768,128]{1,0:T(8,128)S(1)} %get-tuple-element.51), channel_id=1, source_target_pairs={{0,4},{4,8},{8,12},{12,0},{1,5},{5,9},{9,13},{13,1},{2,6},{6,10},{... | collective-permute-start | bytes 1179656 | tf_op jit(solution)/shard_map/ppermute | solution.py:488
  38.3 10.4 %collective-permute-start.5 = (f32[768,128]{1,0:T(8,128)S(1)}, f32[768,128]{1,0:T(8,128)S(1)}, u32[]{:S(2)}, u32[]{:S(2)}) collective-permute-start(f32[768,128]{1,0:T(8,128)S(1)} %get-tuple-element.53.rest_2_), channel_id=1, source_target_pairs={{0,2},{2,0},{1,3},{3,1},{4,6},{6,4},{5,7},{7,5},{8,10},{10,8},{9,1... | collective-permute-start | bytes 1179656 | tf_op jit(solution)/shard_map/ppermute | solution.py:25
  45.3 10.2 %collective-permute-start.4 = (f32[768,128]{1,0:T(8,128)S(1)}, f32[768,128]{1,0:T(8,128)S(1)}, u32[]{:S(2)}, u32[]{:S(2)}) collective-permute-start(f32[768,128]{1,0:T(8,128)S(1)} %get-tuple-element.57), channel_id=1, source_target_pairs={{0,12},{4,0},{8,4},{12,8},{1,13},{5,1},{9,5},{13,9},{2,14},{6,2},{... | collective-permute-start | bytes 1179656 | tf_op jit(solution)/shard_map/ppermute | solution.py:488
  48.7 9.5 %collective-permute-start.9 = (f32[768,128]{1,0:T(8,128)S(1)}, f32[768,128]{1,0:T(8,128)S(1)}, u32[]{:S(2)}, u32[]{:S(2)}) collective-permute-start(f32[768,128]{1,0:T(8,128)S(1)} %get-tuple-element.59.rest_4_), channel_id=1, source_target_pairs={{0,2},{2,0},{1,3},{3,1},{4,6},{6,4},{5,7},{7,5},{8,10},{10,8},{9,1... | collective-permute-start | bytes 1179656 | tf_op jit(solution)/shard_map/ppermute | solution.py:25
  58.2 10.8 %collective-permute-start.10 = (f32[768,128]{1,0:T(8,128)S(1)}, f32[768,128]{1,0:T(8,128)S(1)}, u32[]{:S(2)}, u32[]{:S(2)}) collective-permute-start(f32[768,128]{1,0:T(8,128)S(1)} %get-tuple-element.63.rest_6_), channel_id=1, source_target_pairs={{0,2},{2,0},{1,3},{3,1},{4,6},{6,4},{5,7},{7,5},{8,10},{10,8},{9,1... | collective-permute-start | bytes 1179656 | tf_op jit(solution)/shard_map/ppermute | solution.py:25
  59.7 1.2 collective-permute-start.6
  60.8 3.6 %collective-permute-start.7 = (f32[8,128]{1,0:T(8,128)S(1)}, f32[8,128]{1,0:T(8,128)S(1)}, u32[]{:S(2)}, u32[]{:S(2)}) collective-permute-start(f32[8,128]{1,0:T(8,128)S(1)} %add.60), channel_id=1, source_target_pairs={{0,4},{4,0},{8,12},{12,8},{1,5},{5,1},{9,13},{13,9},{2,6},{6,2},{1... | collective-permute-start | bytes 12296 | tf_op jit(solution)/shard_map/ppermute | solution.py:25
  64.4 4.5 %collective-permute-start.8 = (f32[8,128]{1,0:T(8,128)S(1)}, f32[8,128]{1,0:T(8,128)S(1)}, u32[]{:S(2)}, u32[]{:S(2)}) collective-permute-start(f32[8,128]{1,0:T(8,128)S(1)} %add.61), channel_id=1, source_target_pairs={{0,8},{4,12},{8,0},{12,4},{1,9},{5,13},{9,1},{13,5},{2,10},{6,14},... | collective-permute-start | bytes 12296 | tf_op jit(solution)/shard_map/ppermute | solution.py:25
  69.0 3.6 %collective-permute-start.11 = (f32[8,128]{1,0:T(8,128)S(1)}, f32[8,128]{1,0:T(8,128)S(1)}, u32[]{:S(2)}, u32[]{:S(2)}) collective-permute-start(f32[8,128]{1,0:T(8,128)S(1)} %add.62), channel_id=1, source_target_pairs={{0,2},{2,0},{1,3},{3,1},{4,6},{6,4},{5,7},{7,5},{8,10},{10,8},{9,1... | collective-permute-start | bytes 12296 | tf_op jit(solution)/shard_map/ppermute | solution.py:25
  73.8 1.8 %collective-permute-start.12 = (f32[776,128]{1,0:T(8,128)S(1)}, f32[776,128]{1,0:T(8,128)S(1)}, u32[]{:S(2)}, u32[]{:S(2)}) collective-permute-start(f32[776,128]{1,0:T(8,128)S(1)} %get-tuple-element.66.refs_2_.refs_6_.refs_8_), channel_id=1, source_target_pairs={{0,1},{1,0},{2,3},{3,2},{4,5},{5,4},{6,7},{7,6},{8,9},{9,8},{10,11... | collective-permute-start | bytes 1191944 | tf_op jit(solution)/shard_map/ppermute | solution.py:491
  75.6 5.7 %collective-permute-start.13 = (f32[3080,128]{1,0:T(8,128)S(1)}, f32[3080,128]{1,0:T(8,128)S(1)}, u32[]{:S(2)}, u32[]{:S(2)}) collective-permute-start(f32[3080,128]{1,0:T(8,128)S(1)} %get-tuple-element.67.refs_2_.refs_6_.refs_8_.vector_ref.raw_ref), channel_id=1, source_target_pairs={{0,1},{1,0},{2,3},{3,2},{4,5},{5,4},{6,7},{7,6},{8,9},{9,8},{10,11... | collective-permute-start | bytes 4730888 | tf_op jit(solution)/shard_map/ppermute | solution.py:491
  80.9 21.0 %collective-permute-start.14 = (f32[776,128]{1,0:T(8,128)S(1)}, f32[776,128]{1,0:T(8,128)S(1)}, u32[]{:S(2)}, u32[]{:S(2)}) collective-permute-start(f32[776,128]{1,0:T(8,128)S(1)} %get-tuple-element.68), channel_id=1, source_target_pairs={{0,8},{4,12},{8,0},{12,4},{1,9},{5,13},{9,1},{13,5},{2,10},{6,14},... | collective-permute-start | bytes 1191944 | tf_op jit(solution)/shard_map/ppermute | solution.py:488
  93.8 11.2 %collective-permute-start.17 = (f32[768,128]{1,0:T(8,128)S(1)}, f32[768,128]{1,0:T(8,128)S(1)}, u32[]{:S(2)}, u32[]{:S(2)}) collective-permute-start(f32[768,128]{1,0:T(8,128)S(1)} %combine.12.mine_ref), channel_id=1, source_target_pairs={{0,2},{2,0},{1,3},{3,1},{4,6},{6,4},{5,7},{7,5},{8,10},{10,8},{9,1... | collective-permute-start | bytes 1179656 | tf_op jit(solution)/shard_map/ppermute | solution.py:25
  101.9 12.5 %collective-permute-start.15 = (f32[776,128]{1,0:T(8,128)S(1)}, f32[776,128]{1,0:T(8,128)S(1)}, u32[]{:S(2)}, u32[]{:S(2)}) collective-permute-start(f32[776,128]{1,0:T(8,128)S(1)} %get-tuple-element.71), channel_id=1, source_target_pairs={{0,4},{4,8},{8,12},{12,0},{1,5},{5,9},{9,13},{13,1},{2,6},{6,10},{... | collective-permute-start | bytes 1191944 | tf_op jit(solution)/shard_map/ppermute | solution.py:488
  105.0 10.3 %collective-permute-start.18 = (f32[768,128]{1,0:T(8,128)S(1)}, f32[768,128]{1,0:T(8,128)S(1)}, u32[]{:S(2)}, u32[]{:S(2)}) collective-permute-start(f32[768,128]{1,0:T(8,128)S(1)} %combine.13.mine_ref), channel_id=1, source_target_pairs={{0,2},{2,0},{1,3},{3,1},{4,6},{6,4},{5,7},{7,5},{8,10},{10,8},{9,1... | collective-permute-start | bytes 1179656 | tf_op jit(solution)/shard_map/ppermute | solution.py:25
  114.4 9.7 %collective-permute-start.16 = (f32[776,128]{1,0:T(8,128)S(1)}, f32[776,128]{1,0:T(8,128)S(1)}, u32[]{:S(2)}, u32[]{:S(2)}) collective-permute-start(f32[776,128]{1,0:T(8,128)S(1)} %get-tuple-element.73), channel_id=1, source_target_pairs={{0,12},{4,0},{8,4},{12,8},{1,13},{5,1},{9,5},{13,9},{2,14},{6,2},{... | collective-permute-start | bytes 1191944 | tf_op jit(solution)/shard_map/ppermute | solution.py:488
  115.3 9.8 %collective-permute-start.19 = (f32[768,128]{1,0:T(8,128)S(1)}, f32[768,128]{1,0:T(8,128)S(1)}, u32[]{:S(2)}, u32[]{:S(2)}) collective-permute-start(f32[768,128]{1,0:T(8,128)S(1)} %combine.14.mine_ref), channel_id=1, source_target_pairs={{0,2},{2,0},{1,3},{3,1},{4,6},{6,4},{5,7},{7,5},{8,10},{10,8},{9,1... | collective-permute-start | bytes 1179656 | tf_op jit(solution)/shard_map/ppermute | solution.py:25
  125.1 8.9 %collective-permute-start.20 = (f32[768,128]{1,0:T(8,128)S(1)}, f32[768,128]{1,0:T(8,128)S(1)}, u32[]{:S(2)}, u32[]{:S(2)}) collective-permute-start(f32[768,128]{1,0:T(8,128)S(1)} %combine.15.mine_ref), channel_id=1, source_target_pairs={{0,2},{2,0},{1,3},{3,1},{4,6},{6,4},{5,7},{7,5},{8,10},{10,8},{9,1... | collective-permute-start | bytes 1179656 | tf_op jit(solution)/shard_map/ppermute | solution.py:25

commit v10 on v9

--- a/solution.py
+++ b/solution.py
@@ -29,6 +29,9 @@
     size = lax.axis_size(axis)
     if not power_of_two(size):
         return lax.psum(value, axis)
+    if size == 4:
+        one, two, three = (flip(value, axis, bit) for bit in (1, 2, 3))
+        return (value + one) + (two + three)
     bit = 1
     while bit < size:
         value = value + flip(value, axis, bit)
@@ -42,7 +45,15 @@
     return high, low
 
 
-def table_kernel(devices, partner_ref, kind_ref, _, table_ref, used):
+def table_kernel(devices, partner_hbm, kind_hbm, _, table_ref, used, partner_ref, kind_ref, sems):
+    copies = [
+        pltpu.make_async_copy(partner_hbm, partner_ref, sems.at[0]),
+        pltpu.make_async_copy(kind_hbm, kind_ref, sems.at[1]),
+    ]
+    for copy in copies:
+        copy.start()
+    for copy in copies:
+        copy.wait()
     count, terms = partner_ref.shape[0], kind_ref.shape[0]
     per = count // devices
     me = lax.axis_index("blk")
@@ -72,9 +83,14 @@
     return pl.pallas_call(
         functools.partial(table_kernel, devices),
         out_shape=jax.ShapeDtypeStruct((length,), jnp.int32),
-        in_specs=[SCALARS, SCALARS, WHOLE],
+        in_specs=[ANY, ANY, WHOLE],
         out_specs=SCALARS,
-        scratch_shapes=[pltpu.SMEM((devices,), jnp.int32)],
+        scratch_shapes=[
+            pltpu.SMEM((devices,), jnp.int32),
+            pltpu.SMEM(partner.shape, jnp.int32),
+            pltpu.SMEM(term_kind.shape, jnp.int32),
+            pltpu.SemaphoreType.DMA((2,)),
+        ],
         compiler_params=pltpu.CompilerParams(vmem_limit_bytes=SMALL),
         name="table",
     )(partner, term_kind, vector)
@@ -236,50 +252,36 @@
     return out[:-1], out[-1]
 
 
-def combine_kernel(share, starts, with_inner, table, kept_ref, vector_ref, diag_ref, *refs):
-    arrived_refs, sum_ref = refs[: len(starts)], refs[-2 if with_inner else -1]
-    height = vector_ref.shape[0]
-    before = refs[len(starts) : -2] if with_inner else ()
+def combine_kernel(share, with_inner, table, kept_ref, arrived_ref, vector_ref, diag_ref, sum_ref, *refs):
     rows = diag_ref.shape[1]
     roots = vector_ref.shape[0] // rows
-    step = pl.program_id(0)
-    arrived = arrived_refs[0][...]
-    for ref, begin in zip(arrived_refs[1:], starts[1:]):
-        arrived = jnp.where(step >= begin, ref[...], arrived)
     diag = share * diag_ref[0]
     if with_inner:
-        inner_ref = refs[-1]
-
-        @pl.when(step == 0)
+        inner_ref = refs[0]
+
+        @pl.when(pl.program_id(0) == 0)
         def _():
-            inner_ref[...] = sum((ref[...] for ref in before), jnp.zeros_like(inner_ref))
+            inner_ref[...] = jnp.zeros_like(inner_ref)
 
     for r in range(roots):
         at = slice(r * rows, (r + 1) * rows)
         vector = vector_ref[at]
-        total = kept_ref[at] + arrived[at] + diag * vector
-        if before:
-            sum_ref[pl.ds(pl.multiple_of(step * height + r * rows, rows), rows)] = total
-        else:
-            sum_ref[at] = total
+        total = kept_ref[at] + arrived_ref[at] + diag * vector
+        sum_ref[at] = total
         if with_inner:
             inner_ref[r : r + 1] += jnp.sum(vector * total, axis=0, keepdims=True)
             inner_ref[roots + r : roots + r + 1] += share * jnp.sum(
                 vector * vector, axis=0, keepdims=True
             )
-    if before:
-        sum_ref[sum_ref.shape[0] - TAG :] = inner_ref[...]
-
-
-def combine(table, pieces, kept, arrived, vector, diag, share, ordered, with_inner, before):
+
+
+def combine(table, part, kept, arrived, vector, diag, share, ordered, with_inner):
     count, rows, width = diag.shape
-    height = kept.shape[0] // count
-    starts = [0]
-    for _, size in pieces:
-        starts.append(starts[-1] + size)
+    base, size, skip = part
+    block = (kept.shape[0] // count, width)
 
     def slot(i, table):
-        return table[count + place_of(i, pieces)]
+        return table[count + base + i]
 
     def place(i, table):
         return table[2 * count + slot(i, table)]
@@ -287,35 +289,29 @@
     def held(i, table):
         return (place(i, table) if ordered else slot(i, table), 0)
 
-    def arrived_spec(begin, end):
-        return pl.BlockSpec((height, width), lambda i, t: (jnp.clip(i - begin, 0, end - begin - 1), 0))
-
-    block = (height, width)
-    whole = (starts[-1] * height + TAG * bool(before), width)
-    out_shape = [jax.ShapeDtypeStruct(whole, jnp.float32)]
-    out_specs = [pl.BlockSpec(whole if before else block, lambda i, t: (0 if before else i, 0))]
+    out_shape = [jax.ShapeDtypeStruct((size * block[0], width), jnp.float32)]
+    out_specs = [pl.BlockSpec(block, lambda i, t: (i, 0))]
     if with_inner:
         out_shape.append(jax.ShapeDtypeStruct((TAG, width), jnp.float32))
         out_specs.append(pl.BlockSpec((TAG, width), lambda i, t: (0, 0)))
     out = pl.pallas_call(
-        functools.partial(combine_kernel, share, starts[:-1], with_inner),
+        functools.partial(combine_kernel, share, with_inner),
         out_shape=out_shape,
         grid_spec=pltpu.PrefetchScalarGridSpec(
             num_scalar_prefetch=1,
-            grid=(starts[-1],),
+            grid=(size,),
             in_specs=[
                 pl.BlockSpec(block, lambda i, t: (place(i, t), 0)),
+                pl.BlockSpec(block, lambda i, t: (skip + i, 0)),
                 pl.BlockSpec(block, held),
                 pl.BlockSpec((1, rows, width), lambda i, t: (slot(i, t), 0, 0)),
-            ]
-            + [arrived_spec(begin, end) for begin, end in zip(starts, starts[1:])]
-            + [pl.BlockSpec((TAG, width), lambda i, t: (0, 0))] * len(before),
+            ],
             out_specs=out_specs,
         ),
         compiler_params=pltpu.CompilerParams(vmem_limit_bytes=SMALL),
         cost_estimate=FREE,
         name="combine",
-    )(table, kept, vector, diag, *arrived, *before)
+    )(table, kept, arrived, vector, diag)
     return out if with_inner else (out[0], None)
 
 
@@ -413,35 +409,39 @@
     )(table, scale, raw)
 
 
-def finish_kernel(count, rows, places, table, scale_ref, mine_ref, theirs_ref, *rest):
-    out_ref, held, sems = rest[-3:]
+def finish_kernel(count, rows, sizes, places, table, scale_ref, *refs):
+    parts, (out_ref, held, sems) = refs[: 2 * len(sizes)], refs[-3:]
     height = held.shape[0] // len(places)
-
-    def make(place, at):
+    sources = [(part, i) for part, size in enumerate(sizes) for i in range(size)]
+
+    def make(source, place, at):
+        part, i = source
+        mine, theirs = parts[2 * part], parts[2 * part + 1]
         for r in range(height // rows):
-            part = slice(at.start + r * rows, at.start + (r + 1) * rows)
-            held[part] = (mine_ref[part] + theirs_ref[part]) * scale_ref[r : r + 1]
+            row = i * height + r * rows
+            total = mine[row : row + rows] + theirs[row : row + rows]
+            held[at.start + r * rows : at.start + (r + 1) * rows] = total * scale_ref[r : r + 1]
         return table[count + place] * height
 
-    scatter(held, out_ref, sems, [functools.partial(make, place) for place in places])
-
-
-def finish(table, pieces, scale, mine, theirs, out, count, rows):
-    places = [base + i for base, size in pieces for i in range(size)]
-    height, width = mine.shape[0] // len(places), mine.shape[1]
-    in_specs = [SCALARS, WHOLE, WHOLE, WHOLE]
-    args, aliases = [table, scale, mine, theirs], {}
+    scatter(held, out_ref, sems, [functools.partial(make, *one) for one in zip(sources, places)])
+
+
+def finish(table, spans, scale, parts, out, count, rows):
+    places = [base + i for base, size in spans for i in range(size)]
+    height, width = parts[0].shape[0] // spans[0][1], parts[0].shape[1]
+    in_specs = [SCALARS] + [WHOLE] * (1 + len(parts))
+    args, aliases = [table, scale, *parts], {}
     if out is not None:
         in_specs.append(ANY)
+        aliases = {len(args): 0}
         args.append(out)
-        aliases = {4: 0}
     return pl.pallas_call(
-        functools.partial(finish_kernel, count, rows, places),
+        functools.partial(finish_kernel, count, rows, [size for _, size in spans], places),
         out_shape=jax.ShapeDtypeStruct((count * height, width), jnp.float32),
         in_specs=in_specs,
         out_specs=ANY,
         scratch_shapes=[
-            pltpu.VMEM(mine.shape, jnp.float32),
+            pltpu.VMEM((len(places) * height, width), jnp.float32),
             pltpu.SemaphoreType.DMA((len(places),)),
         ],
         input_output_aliases=aliases,
@@ -478,7 +478,11 @@
     staying = (0, 0, per)
     moving = sorted(range(1, devices), key=lambda c: (-min(c, devices - c), c))
     moving = [(c, c * per, per) for c in moving]
-    groups = [[piece] for piece in [staying] + moving]
+    cuts = [(0, per // 2), (per // 2, per - per // 2)] if per > 1 else [(0, per)]
+    shares = [
+        (piece, piece[1] + start, size, start) for piece in [staying] + moving for start, size in cuts
+    ]
+    lasting = len(shares) - len(cuts)
     batches = [moving[:1], moving[1:] + [staying]]
 
     def spans(pieces):
@@ -515,28 +519,24 @@
         arrived, sums, inners = {}, [], []
         for at, piece in enumerate(moving):
             value = outgoing[piece]
-            if at >= 1:
-                value = after(value, arrived[moving[at - 1]])[0]
+            if at >= 2:
+                value = after(value, arrived[moving[at - 2]])[0]
             arrived[piece] = relay(value, piece[0])
         arrived[staying] = outgoing[staying]
-        for group in groups:
-            first, *others = [arrived[piece] for piece in group]
-            if sums:
-                first = after(first, sums[-2])[0]
+        for piece, *part in shares:
             mine, inner = combine(
                 table,
-                spans(group),
+                part,
                 kept,
-                [first] + others,
+                arrived[piece],
                 own,
                 diag,
                 1.0 / terms_over,
                 second,
                 not second,
-                (),
             )
-            if sums:
-                mine = after(mine, sums[-1])[0]
+            if len(sums) >= 2 * len(cuts):
+                mine = after(mine, sums[1 - 2 * len(cuts)])[0]
             sums += add_over_term(mine)
             inners.append(inner)
         return sums, inners, arrived, other
@@ -546,7 +546,7 @@
     inner = small_sum(after(inner, sums[-1])[0], "term")
     first = spans(batches[0])[0]
     raw, ahead = correct(
-        table, [spans(group) for group in groups], first, inner, vector, diag, sums
+        table, [[part[1:3]] for part in shares], first, inner, vector, diag, sums
     )
 
     sums, _, arrived, other = partials(raw, True)
@@ -557,10 +557,11 @@
     scale = jnp.broadcast_to(scale, squares.shape)
     correction = scaled(table, scale, raw, slots, rows)
     sigma = None
-    for at, group in enumerate(groups):
-        sigma = finish(
-            table, spans(group), scale, sums[2 * at], sums[2 * at + 1], sigma, slots, rows
-        )
+    for some in (slice(0, lasting), slice(lasting, None)):
+        parts = [one for pair in list(zip(sums[::2], sums[1::2]))[some] for one in pair]
+        if parts:
+            spans_of = [part[1:3] for part in shares[some]]
+            sigma = finish(table, spans_of, scale, parts, sigma, slots, rows)
     return tuple(
         jnp.transpose(value.reshape(slots, roots, rows, width), (0, 2, 1, 3))
         for value in (sigma, correction)

time: 135 us -> 141 us (1.044)
  starting transfers between devices: 20.5 us -> 34.5 us
  waiting for transfers between devices: 61.1 us -> 50.6 us
  Pallas kernels: 49.7 us -> 51.8 us
    ppermute x6, waiting for transfers between devices: 37.3 us -> 13.9 us  [relay(): lax.ppermute(value, 'blk', [(p, (p + c) % devices) for p in range(devices)])]
    ppermute x12 -> x21, waiting for transfers between devices: 22.1 us -> 35 us  [flip(): return lax.ppermute(value, axis, [(i, i ^ bit) for i in range(size)])]
    ppermute x12 -> x21, starting transfers between devices: 13.1 us -> 23.3 us  [flip(): return lax.ppermute(value, axis, [(i, i ^ bit) for i in range(size)])]
    ppermute x6, starting transfers between devices: 6.58 us -> 10.5 us  [relay(): lax.ppermute(value, 'blk', [(p, (p + c) % devices) for p in range(devices)])]
    pallas_call x12 -> x18, Pallas kernels: 11.3 us -> 13.4 us  [the longest x16 10.4 us: combine(): pl.pallas_call(functools.partial(combine_kernel, share, with_inner), out_...]
  transfers between devices with their start and end apart: 21 -> 30, of which waited for: 18 -> 15; matrix products, arithmetic and copies ran while one was open for 0% -> 0% of each run, Pallas kernels for 31% -> 31%
where the time goes in v10:
time: 141 us
  Pallas kernels  51.8 us (37%)
  waiting for transfers between devices  50.6 us (36%)
  starting transfers between devices  34.5 us (24%)
  local copies, waits for them, and re-layouts  2.81 us (2%)
    ppermute x21, waiting for transfers between devices, flip(): return lax.ppermute(value, axis, [(i, i ^ bit) for i in range(size)])  35 us
    pallas_call x4, Pallas kernels, sectors(): pl.pallas_call(functools.partial(sector_kernel, count, terms, unroll, sta...  33.8 us
    ppermute x21, starting transfers between devices, flip(): return lax.ppermute(value, axis, [(i, i ^ bit) for i in range(size)])  23.3 us
    ppermute x6, waiting for transfers between devices, relay(): lax.ppermute(value, 'blk', [(p, (p + c) % devices) for p in range(devices)])  13.9 us
    ppermute x6, starting transfers between devices, relay(): lax.ppermute(value, 'blk', [(p, (p + c) % devices) for p in range(devices)])  10.5 us
    pallas_call x16, Pallas kernels, combine(): pl.pallas_call(functools.partial(combine_kernel, share, with_inner), out_...  10.4 us
    pallas_call x2, Pallas kernels, finish(): pl.pallas_call(functools.partial(finish_kernel, count, rows, [size for _,...  2.99 us
  transfers between devices with their start and end apart: 30, of which 15 were waited for; matrix products, arithmetic and copies ran while one was open for 0% of the time, Pallas kernels for 31%

profile of v10, /device:TPU:0, one launch (start us, length us, event | category | flops | bytes accessed | tf_op | source)
XLA Modules:
  0.0 140.9 jit_solution(2111200813253162349)
XLA Ops:
  1.1 1.4 copy-done
  2.6 0.7 copy-done.2
  3.2 0.7 copy-done.3
  3.9 1.5 %table.1 = s32[57]{0:T(128)S(1)} custom-call(s32[16]{0:T(128)S(1)} %copy-done.2, s32[8]{0:T(128)S(1)} %copy-done.3, f32[3072,128]{1,0:T(8,128)S(1)} %bitcast.10), custom_call_target="tpu_custom_call" | custom-call | tf_op jit(solution)/shard_map/table/pallas_call | solution.py:83
  5.4 5.2 %sectors.4 = (f32[768,128]{1,0:T(8,128)S(1)}, f32[3072,128]{1,0:T(8,128)S(1)}) custom-call(s32[57]{0:T(128)S(1)} %table.1, f32[8,16,64,128]{3,2,1,0:T(8,128)} %refs_4_.7, f32[8,16,128,128]{3,2,1,0:T(8,128)} %refs_5_.7, f32[3072,128]{1,0:T(8,128)S(1)} %bitcast.11, f32[3072,128]{1,0:T(8,128)S(1)} %collective-permute-done.refs_3_.refs_7_, ...), custom_call_target="tpu_custom_call" | custom-call | tf_op jit(solution)/shard_map/sectors/pallas_call | solution.py:223
  10.6 3.7 %collective-permute-start.1 = (f32[768,128]{1,0:T(8,128)S(1)}, f32[768,128]{1,0:T(8,128)S(1)}, u32[]{:S(2)}, u32[]{:S(2)}) collective-permute-start(f32[768,128]{1,0:T(8,128)S(1)} %get-tuple-element.53), channel_id=1, source_target_pairs={{0,8},{4,12},{8,0},{12,4},{1,9},{5,13},{9,1},{13,5},{2,10},{6,14},... | collective-permute-start | bytes 1179656 | tf_op jit(solution)/shard_map/ppermute | solution.py:492
  14.5 11.7 %sectors.5 = (f32[768,128]{1,0:T(8,128)S(1)}, f32[768,128]{1,0:T(8,128)S(1)}, f32[768,128]{1,0:T(8,128)S(1)}, f32[3072,128]{1,0:T(8,128)S(1)}) custom-call(s32[57]{0:T(128)S(1)} %table.1, f32[8,16,64,128]{3,2,1,0:T(8,128)} %refs_4_.7, f32[8,16,128,128]{3,2,1,0:T(8,128)} %refs_5_.7, f32[3072,128]{1,0:T(8,128)S(1)} %bitcast.13, ...), custom_call_target="tpu_custom_call", output_to_operand_aliasing={{3}: (9, {})} | custom-call | tf_op jit(solution)/shard_map/sectors/pallas_call | solution.py:223
  26.2 0.7 combine.17
  26.9 1.5 %collective-permute-start.8 = (f32[384,128]{1,0:T(8,128)S(1)}, f32[384,128]{1,0:T(8,128)S(1)}, u32[]{:S(2)}, u32[]{:S(2)}) collective-permute-start(f32[384,128]{1,0:T(8,128)S(1)} %get-tuple-element.66.rest_2_), channel_id=1, source_target_pairs={{0,2},{2,0},{1,3},{3,1},{4,6},{6,4},{5,7},{7,5},{8,10},{10,8},{9,1... | collective-permute-start | bytes 589832 | tf_op jit(solution)/shard_map/ppermute | solution.py:25
  28.4 1.6 %collective-permute-start.2 = (f32[768,128]{1,0:T(8,128)S(1)}, f32[768,128]{1,0:T(8,128)S(1)}, u32[]{:S(2)}, u32[]{:S(2)}) collective-permute-start(f32[768,128]{1,0:T(8,128)S(1)} %get-tuple-element.56), channel_id=1, source_target_pairs={{0,4},{4,8},{8,12},{12,0},{1,5},{5,9},{9,13},{13,1},{2,6},{6,10},{... | collective-permute-start | bytes 1179656 | tf_op jit(solution)/shard_map/ppermute | solution.py:492
  30.0 0.7 combine.16
  31.3 1.2 collective-permute-done.1.arrived_ref
  32.5 3.6 %collective-permute-start.3 = (f32[768,128]{1,0:T(8,128)S(1)}, f32[768,128]{1,0:T(8,128)S(1)}, u32[]{:S(2)}, u32[]{:S(2)}) collective-permute-start(f32[768,128]{1,0:T(8,128)S(1)} %get-tuple-element.60), channel_id=1, source_target_pairs={{0,12},{4,0},{8,4},{12,8},{1,13},{5,1},{9,5},{13,9},{2,14},{6,2},{... | collective-permute-start | bytes 1179656 | tf_op jit(solution)/shard_map/ppermute | solution.py:492
  36.1 0.7 combine.19
  36.8 6.8 %collective-permute-start.9 = (f32[384,128]{1,0:T(8,128)S(1)}, f32[384,128]{1,0:T(8,128)S(1)}, u32[]{:S(2)}, u32[]{:S(2)}) collective-permute-start(f32[384,128]{1,0:T(8,128)S(1)} %get-tuple-element.67.rest_6_), channel_id=1, source_target_pairs={{0,2},{2,0},{1,3},{3,1},{4,6},{6,4},{5,7},{7,5},{8,10},{10,8},{9,1... | collective-permute-start | bytes 589832 | tf_op jit(solution)/shard_map/ppermute | solution.py:25
  43.6 0.7 combine.18
  44.4 0.7 combine.21
  45.0 0.7 combine.20
  45.7 3.5 %collective-permute-done.9.rest_7_ = f32[384,128]{1,0:T(8,128)S(1)} collective-permute-done((f32[384,128]{1,0:T(8,128)S(1)}, f32[384,128]{1,0:T(8,128)S(1)}, u32[]{:S(2)}, u32[]{:S(2)}) %collective-permute-start.9) | collective-permute-done | bytes 196640 | tf_op jit(solution)/shard_map/ppermute | solution.py:25
  49.2 2.2 %collective-permute-start.10 = (f32[384,128]{1,0:T(8,128)S(1)}, f32[384,128]{1,0:T(8,128)S(1)}, u32[]{:S(2)}, u32[]{:S(2)}) collective-permute-start(f32[384,128]{1,0:T(8,128)S(1)} %get-tuple-element.68.rest_10_), channel_id=1, source_target_pairs={{0,2},{2,0},{1,3},{3,1},{4,6},{6,4},{5,7},{7,5},{8,10},{10,8},{9,1... | collective-permute-start | bytes 589832 | tf_op jit(solution)/shard_map/ppermute | solution.py:25
  51.4 2.0 %collective-permute-done.14.rest_5_ = f32[384,128]{1,0:T(8,128)S(1)} collective-permute-done((f32[384,128]{1,0:T(8,128)S(1)}, f32[384,128]{1,0:T(8,128)S(1)}, u32[]{:S(2)}, u32[]{:S(2)}) %collective-permute-start.14) | collective-permute-done | bytes 196640 | tf_op jit(solution)/shard_map/ppermute | solution.py:25
  53.5 2.2 %collective-permute-start.15 = (f32[384,128]{1,0:T(8,128)S(1)}, f32[384,128]{1,0:T(8,128)S(1)}, u32[]{:S(2)}, u32[]{:S(2)}) collective-permute-start(f32[384,128]{1,0:T(8,128)S(1)} %get-tuple-element.75.rest_8_), channel_id=1, source_target_pairs={{0,2},{2,0},{1,3},{3,1},{4,6},{6,4},{5,7},{7,5},{8,10},{10,8},{9,1... | collective-permute-start | bytes 589832 | tf_op jit(solution)/shard_map/ppermute | solution.py:25
  55.6 0.7 combine.23
  56.3 0.7 combine.22
  57.1 1.2 collective-permute-done.4
  58.2 2.1 %collective-permute-start.7 = (f32[8,128]{1,0:T(8,128)S(1)}, f32[8,128]{1,0:T(8,128)S(1)}, u32[]{:S(2)}, u32[]{:S(2)}) collective-permute-start(f32[8,128]{1,0:T(8,128)S(1)} %add.79), channel_id=1, source_target_pairs={{0,12},{4,8},{8,4},{12,0},{1,13},{5,9},{9,5},{13,1},{2,14},{6,10},... | collective-permute-start | bytes 12296 | tf_op jit(solution)/shard_map/ppermute | solution.py:25
  60.3 1.4 %collective-permute-start.5 = (f32[8,128]{1,0:T(8,128)S(1)}, f32[8,128]{1,0:T(8,128)S(1)}, u32[]{:S(2)}, u32[]{:S(2)}) collective-permute-start(f32[8,128]{1,0:T(8,128)S(1)} %add.79), channel_id=1, source_target_pairs={{0,4},{4,0},{8,12},{12,8},{1,5},{5,1},{9,13},{13,9},{2,6},{6,2},{1... | collective-permute-start | bytes 12296 | tf_op jit(solution)/shard_map/ppermute | solution.py:25
  61.7 2.0 %collective-permute-start.16 = (f32[384,128]{1,0:T(8,128)S(1)}, f32[384,128]{1,0:T(8,128)S(1)}, u32[]{:S(2)}, u32[]{:S(2)}) collective-permute-start(f32[384,128]{1,0:T(8,128)S(1)} %get-tuple-element.77.rest_12_), channel_id=1, source_target_pairs={{0,2},{2,0},{1,3},{3,1},{4,6},{6,4},{5,7},{7,5},{8,10},{10,8},{9,1... | collective-permute-start | bytes 589832 | tf_op jit(solution)/shard_map/ppermute | solution.py:25
  63.9 5.6 %collective-permute-done.11.rest_15_ = f32[384,128]{1,0:T(8,128)S(1)} collective-permute-done((f32[384,128]{1,0:T(8,128)S(1)}, f32[384,128]{1,0:T(8,128)S(1)}, u32[]{:S(2)}, u32[]{:S(2)}) %collective-permute-start.11) | collective-permute-done | bytes 196640 | tf_op jit(solution)/shard_map/ppermute | solution.py:25
  69.6 3.6 %collective-permute-done.12 = f32[8,128]{1,0:T(8,128)S(1)} collective-permute-done((f32[8,128]{1,0:T(8,128)S(1)}, f32[8,128]{1,0:T(8,128)S(1)}, u32[]{:S(2)}, u32[]{:S(2)}) %collective-permute-start.12) | collective-permute-done | bytes 4128 | tf_op jit(solution)/shard_map/ppermute | solution.py:25
  73.2 1.3 correct.1
  74.5 1.7 %collective-permute-done.17.refs_3_.refs_7_.refs_9_ = f32[776,128]{1,0:T(8,128)S(1)} collective-permute-done((f32[776,128]{1,0:T(8,128)S(1)}, f32[776,128]{1,0:T(8,128)S(1)}, u32[]{:S(2)}, u32[]{:S(2)}) %collective-permute-start.17) | collective-permute-done | bytes 397344 | tf_op jit(solution)/shard_map/ppermute | solution.py:495
  76.4 5.2 %sectors.6 = (f32[776,128]{1,0:T(8,128)S(1)}, f32[3072,128]{1,0:T(8,128)S(1)}) custom-call(s32[57]{0:T(128)S(1)} %table.1, f32[8,16,64,128]{3,2,1,0:T(8,128)} %refs_4_.7, f32[8,16,128,128]{3,2,1,0:T(8,128)} %refs_5_.7, f32[776,128]{1,0:T(8,128)S(1)} %get-tuple-element.79.refs_2_.refs_6_.refs_8_, ...), custom_call_target="tpu_custom_call" | custom-call | tf_op jit(solution)/shard_map/sectors/pallas_call | solution.py:223
  81.6 1.0 collective-permute-start.19
  82.5 11.7 %sectors.7 = (f32[776,128]{1,0:T(8,128)S(1)}, f32[776,128]{1,0:T(8,128)S(1)}, f32[768,128]{1,0:T(8,128)S(1)}, f32[3072,128]{1,0:T(8,128)S(1)}) custom-call(s32[57]{0:T(128)S(1)} %table.1, f32[8,16,64,128]{3,2,1,0:T(8,128)} %refs_4_.7, f32[8,16,128,128]{3,2,1,0:T(8,128)} %refs_5_.7, ...), custom_call_target="tpu_custom_call", output_to_operand_aliasing={{3}: (11, {})} | custom-call | tf_op jit(solution)/shard_map/sectors/pallas_call | solution.py:223
  96.3 2.0 %collective-permute-start.26 = (f32[384,128]{1,0:T(8,128)S(1)}, f32[384,128]{1,0:T(8,128)S(1)}, u32[]{:S(2)}, u32[]{:S(2)}) collective-permute-start(f32[384,128]{1,0:T(8,128)S(1)} %combine.31.refs_2_), channel_id=1, source_target_pairs={{0,2},{2,0},{1,3},{3,1},{4,6},{6,4},{5,7},{7,5},{8,10},{10,8},{9,1... | collective-permute-start | bytes 589832 | tf_op jit(solution)/shard_map/ppermute | solution.py:25
  98.3 12.7 %collective-permute-done.19.arrived_ref = f32[776,128]{1,0:T(8,128)S(1)} collective-permute-done((f32[776,128]{1,0:T(8,128)S(1)}, f32[776,128]{1,0:T(8,128)S(1)}, u32[]{:S(2)}, u32[]{:S(2)}) %collective-permute-start.19) | collective-permute-done | bytes 397344 | tf_op jit(solution)/shard_map/ppermute | solution.py:492
  112.4 2.1 %collective-permute-start.27 = (f32[384,128]{1,0:T(8,128)S(1)}, f32[384,128]{1,0:T(8,128)S(1)}, u32[]{:S(2)}, u32[]{:S(2)}) collective-permute-start(f32[384,128]{1,0:T(8,128)S(1)} %combine.30.refs_6_), channel_id=1, source_target_pairs={{0,2},{2,0},{1,3},{3,1},{4,6},{6,4},{5,7},{7,5},{8,10},{10,8},{9,1... | collective-permute-start | bytes 589832 | tf_op jit(solution)/shard_map/ppermute | solution.py:25
  115.1 4.4 %collective-permute-done.23.refs_5_ = f32[384,128]{1,0:T(8,128)S(1)} collective-permute-done((f32[384,128]{1,0:T(8,128)S(1)}, f32[384,128]{1,0:T(8,128)S(1)}, u32[]{:S(2)}, u32[]{:S(2)}) %collective-permute-start.23) | collective-permute-done | bytes 196640 | tf_op jit(solution)/shard_map/ppermute | solution.py:25
  120.2 3.6 %collective-permute-done.27.refs_7_ = f32[384,128]{1,0:T(8,128)S(1)} collective-permute-done((f32[384,128]{1,0:T(8,128)S(1)}, f32[384,128]{1,0:T(8,128)S(1)}, u32[]{:S(2)}, u32[]{:S(2)}) %collective-permute-start.27) | collective-permute-done | bytes 196640 | tf_op jit(solution)/shard_map/ppermute | solution.py:25
  124.4 0.6 combine.28.refs_2_
  125.1 2.8 %collective-permute-done.24.refs_9_ = f32[384,128]{1,0:T(8,128)S(1)} collective-permute-done((f32[384,128]{1,0:T(8,128)S(1)}, f32[384,128]{1,0:T(8,128)S(1)}, u32[]{:S(2)}, u32[]{:S(2)}) %collective-permute-start.24) | collective-permute-done | bytes 196640 | tf_op jit(solution)/shard_map/ppermute | solution.py:25
  128.0 4.2 %collective-permute-done.28.refs_11_ = f32[384,128]{1,0:T(8,128)S(1)} collective-permute-done((f32[384,128]{1,0:T(8,128)S(1)}, f32[384,128]{1,0:T(8,128)S(1)}, u32[]{:S(2)}, u32[]{:S(2)}) %collective-permute-start.28) | collective-permute-done | bytes 196640 | tf_op jit(solution)/shard_map/ppermute | solution.py:25
  132.2 1.8 %scaled.1 = f32[3072,128]{1,0:T(8,128)} custom-call(s32[57]{0:T(128)S(1)} %table.1, f32[8,128]{1,0:T(8,128)S(1)} %broadcast_in_dim.2.scale_ref, f32[3080,128]{1,0:T(8,128)S(1)} %get-tuple-element.80.refs_2_.refs_6_.refs_8_.vector_ref.raw_ref), custom_call_target="tpu_custom_call" | custom-call | tf_op jit(solution)/shard_map/scaled/pallas_call | solution.py:397
  134.1 1.7 %finish.2.refs_4_ = f32[3072,128]{1,0:T(8,128)} custom-call(s32[57]{0:T(128)S(1)} %table.1, f32[8,128]{1,0:T(8,128)S(1)} %broadcast_in_dim.2.scale_ref, f32[384,128]{1,0:T(8,128)S(1)} %combine.27.refs_0_, f32[384,128]{1,0:T(8,128)S(1)} %collective-permute-done.22.refs_1_, f32[384,128]{1,0:T(8,128)S(1)} %combine.31.refs_2_, ...), custom_call_target="tpu_custom_call" | custom-call | tf_op jit(solution)/shard_map/finish/pallas_call | solution.py:438
  135.7 0.6 collective-permute-done.25.refs_1_
  136.4 3.2 %collective-permute-done.29.refs_3_ = f32[384,128]{1,0:T(8,128)S(1)} collective-permute-done((f32[384,128]{1,0:T(8,128)S(1)}, f32[384,128]{1,0:T(8,128)S(1)}, u32[]{:S(2)}, u32[]{:S(2)}) %collective-permute-start.29) | collective-permute-done | bytes 196640 | tf_op jit(solution)/shard_map/ppermute | solution.py:25
  139.6 1.3 finish.3
  (57 shorter events, 7.3 us)
Async XLA Ops:
  0.6 4.8 %collective-permute-start = (f32[3072,128]{1,0:T(8,128)}, f32[3072,128]{1,0:T(8,128)S(1)}, u32[]{:S(2)}, u32[]{:S(2)}) collective-permute-start(f32[3072,128]{1,0:T(8,128)} %bitcast.9), channel_id=1, source_target_pairs={{0,1},{1,0},{2,3},{3,2},{4,5},{5,4},{6,7},{7,6},{8,9},{9,8},{10,11... | collective-permute-start | bytes 4718600 | tf_op jit(solution)/shard_map/ppermute | solution.py:495
  1.1 1.4 copy-start
  2.6 0.7 copy-start.2
  3.2 0.7 copy-start.3
  3.9 1.5 %copy-start.1 = (f32[16,64,3,128]{3,1,2,0:T(8,128)S(1)}, f32[16,64,3,128]{3,1,2,0:T(8,128)}, u32[]{:S(2)}) copy-start(f32[16,64,3,128]{3,1,2,0:T(8,128)} %param.7) | copy-start | bytes 4718596
  5.4 8.9 %copy-start.4 = (f32[16,128]{1,0:T(8,128)S(1)}, f32[16,128]{1,0:T(8,128)}, u32[]{:S(2)}) copy-start(f32[16,128]{1,0:T(8,128)} %param.13) | copy-start | bytes 24580
  5.4 8.9 %copy-start.5 = (f32[16,64]{1,0:T(8,128)S(1)}, f32[16,64]{1,0:T(8,128)}, u32[]{:S(2)}) copy-start(f32[16,64]{1,0:T(8,128)} %param.12) | copy-start | bytes 12292
  10.6 21.9 %collective-permute-start.1 = (f32[768,128]{1,0:T(8,128)S(1)}, f32[768,128]{1,0:T(8,128)S(1)}, u32[]{:S(2)}, u32[]{:S(2)}) collective-permute-start(f32[768,128]{1,0:T(8,128)S(1)} %get-tuple-element.53), channel_id=1, source_target_pairs={{0,8},{4,12},{8,0},{12,4},{1,9},{5,13},{9,1},{13,5},{2,10},{6,14},... | collective-permute-start | bytes 1179656 | tf_op jit(solution)/shard_map/ppermute | solution.py:492
  26.9 9.9 %collective-permute-start.8 = (f32[384,128]{1,0:T(8,128)S(1)}, f32[384,128]{1,0:T(8,128)S(1)}, u32[]{:S(2)}, u32[]{:S(2)}) collective-permute-start(f32[384,128]{1,0:T(8,128)S(1)} %get-tuple-element.66.rest_2_), channel_id=1, source_target_pairs={{0,2},{2,0},{1,3},{3,1},{4,6},{6,4},{5,7},{7,5},{8,10},{10,8},{9,1... | collective-permute-start | bytes 589832 | tf_op jit(solution)/shard_map/ppermute | solution.py:25
  28.4 15.9 %collective-permute-start.2 = (f32[768,128]{1,0:T(8,128)S(1)}, f32[768,128]{1,0:T(8,128)S(1)}, u32[]{:S(2)}, u32[]{:S(2)}) collective-permute-start(f32[768,128]{1,0:T(8,128)S(1)} %get-tuple-element.56), channel_id=1, source_target_pairs={{0,4},{4,8},{8,12},{12,0},{1,5},{5,9},{9,13},{13,1},{2,6},{6,10},{... | collective-permute-start | bytes 1179656 | tf_op jit(solution)/shard_map/ppermute | solution.py:492
  30.7 13.6 %collective-permute-start.13 = (f32[384,128]{1,0:T(8,128)S(1)}, f32[384,128]{1,0:T(8,128)S(1)}, u32[]{:S(2)}, u32[]{:S(2)}) collective-permute-start(f32[384,128]{1,0:T(8,128)S(1)} %get-tuple-element.71.rest_0_), channel_id=1, source_target_pairs={{0,2},{2,0},{1,3},{3,1},{4,6},{6,4},{5,7},{7,5},{8,10},{10,8},{9,1... | collective-permute-start | bytes 589832 | tf_op jit(solution)/shard_map/ppermute | solution.py:25
  32.5 23.2 %collective-permute-start.3 = (f32[768,128]{1,0:T(8,128)S(1)}, f32[768,128]{1,0:T(8,128)S(1)}, u32[]{:S(2)}, u32[]{:S(2)}) collective-permute-start(f32[768,128]{1,0:T(8,128)S(1)} %get-tuple-element.60), channel_id=1, source_target_pairs={{0,12},{4,0},{8,4},{12,8},{1,13},{5,1},{9,5},{13,9},{2,14},{6,2},{... | collective-permute-start | bytes 1179656 | tf_op jit(solution)/shard_map/ppermute | solution.py:492
  36.8 12.5 %collective-permute-start.9 = (f32[384,128]{1,0:T(8,128)S(1)}, f32[384,128]{1,0:T(8,128)S(1)}, u32[]{:S(2)}, u32[]{:S(2)}) collective-permute-start(f32[384,128]{1,0:T(8,128)S(1)} %get-tuple-element.67.rest_6_), channel_id=1, source_target_pairs={{0,2},{2,0},{1,3},{3,1},{4,6},{6,4},{5,7},{7,5},{8,10},{10,8},{9,1... | collective-permute-start | bytes 589832 | tf_op jit(solution)/shard_map/ppermute | solution.py:25
  44.3 9.2 %collective-permute-start.14 = (f32[384,128]{1,0:T(8,128)S(1)}, f32[384,128]{1,0:T(8,128)S(1)}, u32[]{:S(2)}, u32[]{:S(2)}) collective-permute-start(f32[384,128]{1,0:T(8,128)S(1)} %get-tuple-element.73.rest_4_), channel_id=1, source_target_pairs={{0,2},{2,0},{1,3},{3,1},{4,6},{6,4},{5,7},{7,5},{8,10},{10,8},{9,1... | collective-permute-start | bytes 589832 | tf_op jit(solution)/shard_map/ppermute | solution.py:25
  49.2 12.5 %collective-permute-start.10 = (f32[384,128]{1,0:T(8,128)S(1)}, f32[384,128]{1,0:T(8,128)S(1)}, u32[]{:S(2)}, u32[]{:S(2)}) collective-permute-start(f32[384,128]{1,0:T(8,128)S(1)} %get-tuple-element.68.rest_10_), channel_id=1, source_target_pairs={{0,2},{2,0},{1,3},{3,1},{4,6},{6,4},{5,7},{7,5},{8,10},{10,8},{9,1... | collective-permute-start | bytes 589832 | tf_op jit(solution)/shard_map/ppermute | solution.py:25
  53.5 8.3 %collective-permute-start.15 = (f32[384,128]{1,0:T(8,128)S(1)}, f32[384,128]{1,0:T(8,128)S(1)}, u32[]{:S(2)}, u32[]{:S(2)}) collective-permute-start(f32[384,128]{1,0:T(8,128)S(1)} %get-tuple-element.75.rest_8_), channel_id=1, source_target_pairs={{0,2},{2,0},{1,3},{3,1},{4,6},{6,4},{5,7},{7,5},{8,10},{10,8},{9,1... | collective-permute-start | bytes 589832 | tf_op jit(solution)/shard_map/ppermute | solution.py:25
  57.0 1.2 collective-permute-start.4
  58.2 5.5 %collective-permute-start.6 = (f32[8,128]{1,0:T(8,128)S(1)}, f32[8,128]{1,0:T(8,128)S(1)}, u32[]{:S(2)}, u32[]{:S(2)}) collective-permute-start(f32[8,128]{1,0:T(8,128)S(1)} %add.79), channel_id=1, source_target_pairs={{0,8},{4,12},{8,0},{12,4},{1,9},{5,13},{9,1},{13,5},{2,10},{6,14},... | collective-permute-start | bytes 12296 | tf_op jit(solution)/shard_map/ppermute | solution.py:25
  58.2 5.5 %collective-permute-start.7 = (f32[8,128]{1,0:T(8,128)S(1)}, f32[8,128]{1,0:T(8,128)S(1)}, u32[]{:S(2)}, u32[]{:S(2)}) collective-permute-start(f32[8,128]{1,0:T(8,128)S(1)} %add.79), channel_id=1, source_target_pairs={{0,12},{4,8},{8,4},{12,0},{1,13},{5,9},{9,5},{13,1},{2,14},{6,10},... | collective-permute-start | bytes 12296 | tf_op jit(solution)/shard_map/ppermute | solution.py:25
  60.3 3.6 %collective-permute-start.5 = (f32[8,128]{1,0:T(8,128)S(1)}, f32[8,128]{1,0:T(8,128)S(1)}, u32[]{:S(2)}, u32[]{:S(2)}) collective-permute-start(f32[8,128]{1,0:T(8,128)S(1)} %add.79), channel_id=1, source_target_pairs={{0,4},{4,0},{8,12},{12,8},{1,5},{5,1},{9,13},{13,9},{2,6},{6,2},{1... | collective-permute-start | bytes 12296 | tf_op jit(solution)/shard_map/ppermute | solution.py:25
  61.7 7.8 %collective-permute-start.11 = (f32[384,128]{1,0:T(8,128)S(1)}, f32[384,128]{1,0:T(8,128)S(1)}, u32[]{:S(2)}, u32[]{:S(2)}) collective-permute-start(f32[384,128]{1,0:T(8,128)S(1)} %get-tuple-element.69.rest_14_), channel_id=1, source_target_pairs={{0,2},{2,0},{1,3},{3,1},{4,6},{6,4},{5,7},{7,5},{8,10},{10,8},{9,1... | collective-permute-start | bytes 589832 | tf_op jit(solution)/shard_map/ppermute | solution.py:25
  61.7 11.4 %collective-permute-start.16 = (f32[384,128]{1,0:T(8,128)S(1)}, f32[384,128]{1,0:T(8,128)S(1)}, u32[]{:S(2)}, u32[]{:S(2)}) collective-permute-start(f32[384,128]{1,0:T(8,128)S(1)} %get-tuple-element.77.rest_12_), channel_id=1, source_target_pairs={{0,2},{2,0},{1,3},{3,1},{4,6},{6,4},{5,7},{7,5},{8,10},{10,8},{9,1... | collective-permute-start | bytes 589832 | tf_op jit(solution)/shard_map/ppermute | solution.py:25
  69.6 3.6 %collective-permute-start.12 = (f32[8,128]{1,0:T(8,128)S(1)}, f32[8,128]{1,0:T(8,128)S(1)}, u32[]{:S(2)}, u32[]{:S(2)}) collective-permute-start(f32[8,128]{1,0:T(8,128)S(1)} %add_add_fusion), channel_id=1, source_target_pairs={{0,2},{2,0},{1,3},{3,1},{4,6},{6,4},{5,7},{7,5},{8,10},{10,8},{9,1... | collective-permute-start | bytes 12296 | tf_op jit(solution)/shard_map/ppermute | solution.py:25
  74.5 1.8 %collective-permute-start.17 = (f32[776,128]{1,0:T(8,128)S(1)}, f32[776,128]{1,0:T(8,128)S(1)}, u32[]{:S(2)}, u32[]{:S(2)}) collective-permute-start(f32[776,128]{1,0:T(8,128)S(1)} %get-tuple-element.79.refs_2_.refs_6_.refs_8_), channel_id=1, source_target_pairs={{0,1},{1,0},{2,3},{3,2},{4,5},{5,4},{6,7},{7,6},{8,9},{9,8},{10,11... | collective-permute-start | bytes 1191944 | tf_op jit(solution)/shard_map/ppermute | solution.py:495
  76.3 6.3 %collective-permute-start.18 = (f32[3080,128]{1,0:T(8,128)S(1)}, f32[3080,128]{1,0:T(8,128)S(1)}, u32[]{:S(2)}, u32[]{:S(2)}) collective-permute-start(f32[3080,128]{1,0:T(8,128)S(1)} %get-tuple-element.80.refs_2_.refs_6_.refs_8_.vector_ref.raw_ref), channel_id=1, source_target_pairs={{0,1},{1,0},{2,3},{3,2},{4,5},{5,4},{6,7},{7,6},{8,9},{9,8},{10,11... | collective-permute-start | bytes 4730888 | tf_op jit(solution)/shard_map/ppermute | solution.py:495
  81.6 29.5 %collective-permute-start.19 = (f32[776,128]{1,0:T(8,128)S(1)}, f32[776,128]{1,0:T(8,128)S(1)}, u32[]{:S(2)}, u32[]{:S(2)}) collective-permute-start(f32[776,128]{1,0:T(8,128)S(1)} %get-tuple-element.81), channel_id=1, source_target_pairs={{0,8},{4,12},{8,0},{12,4},{1,9},{5,13},{9,1},{13,5},{2,10},{6,14},... | collective-permute-start | bytes 1191944 | tf_op jit(solution)/shard_map/ppermute | solution.py:492
  94.3 20.2 %collective-permute-start.20 = (f32[776,128]{1,0:T(8,128)S(1)}, f32[776,128]{1,0:T(8,128)S(1)}, u32[]{:S(2)}, u32[]{:S(2)}) collective-permute-start(f32[776,128]{1,0:T(8,128)S(1)} %get-tuple-element.83), channel_id=1, source_target_pairs={{0,4},{4,8},{8,12},{12,0},{1,5},{5,9},{9,13},{13,1},{2,6},{6,10},{... | collective-permute-start | bytes 1191944 | tf_op jit(solution)/shard_map/ppermute | solution.py:492
  95.5 16.1 %collective-permute-start.22 = (f32[384,128]{1,0:T(8,128)S(1)}, f32[384,128]{1,0:T(8,128)S(1)}, u32[]{:S(2)}, u32[]{:S(2)}) collective-permute-start(f32[384,128]{1,0:T(8,128)S(1)} %combine.27.refs_0_), channel_id=1, source_target_pairs={{0,2},{2,0},{1,3},{3,1},{4,6},{6,4},{5,7},{7,5},{8,10},{10,8},{9,1... | collective-permute-start | bytes 589832 | tf_op jit(solution)/shard_map/ppermute | solution.py:25
  96.3 16.1 %collective-permute-start.26 = (f32[384,128]{1,0:T(8,128)S(1)}, f32[384,128]{1,0:T(8,128)S(1)}, u32[]{:S(2)}, u32[]{:S(2)}) collective-permute-start(f32[384,128]{1,0:T(8,128)S(1)} %combine.31.refs_2_), channel_id=1, source_target_pairs={{0,2},{2,0},{1,3},{3,1},{4,6},{6,4},{5,7},{7,5},{8,10},{10,8},{9,1... | collective-permute-start | bytes 589832 | tf_op jit(solution)/shard_map/ppermute | solution.py:25
  111.0 12.7 %collective-permute-start.21 = (f32[776,128]{1,0:T(8,128)S(1)}, f32[776,128]{1,0:T(8,128)S(1)}, u32[]{:S(2)}, u32[]{:S(2)}) collective-permute-start(f32[776,128]{1,0:T(8,128)S(1)} %get-tuple-element.85), channel_id=1, source_target_pairs={{0,12},{4,0},{8,4},{12,8},{1,13},{5,1},{9,5},{13,9},{2,14},{6,2},{... | collective-permute-start | bytes 1191944 | tf_op jit(solution)/shard_map/ppermute | solution.py:492
  111.7 7.8 %collective-permute-start.23 = (f32[384,128]{1,0:T(8,128)S(1)}, f32[384,128]{1,0:T(8,128)S(1)}, u32[]{:S(2)}, u32[]{:S(2)}) collective-permute-start(f32[384,128]{1,0:T(8,128)S(1)} %combine.26.refs_4_), channel_id=1, source_target_pairs={{0,2},{2,0},{1,3},{3,1},{4,6},{6,4},{5,7},{7,5},{8,10},{10,8},{9,1... | collective-permute-start | bytes 589832 | tf_op jit(solution)/shard_map/ppermute | solution.py:25
  112.4 11.3 %collective-permute-start.27 = (f32[384,128]{1,0:T(8,128)S(1)}, f32[384,128]{1,0:T(8,128)S(1)}, u32[]{:S(2)}, u32[]{:S(2)}) collective-permute-start(f32[384,128]{1,0:T(8,128)S(1)} %combine.30.refs_6_), channel_id=1, source_target_pairs={{0,2},{2,0},{1,3},{3,1},{4,6},{6,4},{5,7},{7,5},{8,10},{10,8},{9,1... | collective-permute-start | bytes 589832 | tf_op jit(solution)/shard_map/ppermute | solution.py:25
  119.5 8.4 %collective-permute-start.24 = (f32[384,128]{1,0:T(8,128)S(1)}, f32[384,128]{1,0:T(8,128)S(1)}, u32[]{:S(2)}, u32[]{:S(2)}) collective-permute-start(f32[384,128]{1,0:T(8,128)S(1)} %combine.25.refs_8_), channel_id=1, source_target_pairs={{0,2},{2,0},{1,3},{3,1},{4,6},{6,4},{5,7},{7,5},{8,10},{10,8},{9,1... | collective-permute-start | bytes 589832 | tf_op jit(solution)/shard_map/ppermute | solution.py:25
  123.7 8.4 %collective-permute-start.28 = (f32[384,128]{1,0:T(8,128)S(1)}, f32[384,128]{1,0:T(8,128)S(1)}, u32[]{:S(2)}, u32[]{:S(2)}) collective-permute-start(f32[384,128]{1,0:T(8,128)S(1)} %combine.29.refs_10_), channel_id=1, source_target_pairs={{0,2},{2,0},{1,3},{3,1},{4,6},{6,4},{5,7},{7,5},{8,10},{10,8},{9,1... | collective-permute-start | bytes 589832 | tf_op jit(solution)/shard_map/ppermute | solution.py:25
  127.9 8.4 %collective-permute-start.25 = (f32[384,128]{1,0:T(8,128)S(1)}, f32[384,128]{1,0:T(8,128)S(1)}, u32[]{:S(2)}, u32[]{:S(2)}) collective-permute-start(f32[384,128]{1,0:T(8,128)S(1)} %combine.24.refs_0_), channel_id=1, source_target_pairs={{0,2},{2,0},{1,3},{3,1},{4,6},{6,4},{5,7},{7,5},{8,10},{10,8},{9,1... | collective-permute-start | bytes 589832 | tf_op jit(solution)/shard_map/ppermute | solution.py:25
  132.2 7.4 %collective-permute-start.29 = (f32[384,128]{1,0:T(8,128)S(1)}, f32[384,128]{1,0:T(8,128)S(1)}, u32[]{:S(2)}, u32[]{:S(2)}) collective-permute-start(f32[384,128]{1,0:T(8,128)S(1)} %combine.28.refs_2_), channel_id=1, source_target_pairs={{0,2},{2,0},{1,3},{3,1},{4,6},{6,4},{5,7},{7,5},{8,10},{10,8},{9,1... | collective-permute-start | bytes 589832 | tf_op jit(solution)/shard_map/ppermute | solution.py:25

commit v11 on v10

--- a/solution.py
+++ b/solution.py
@@ -275,9 +275,9 @@
             )
 
 
-def combine(table, part, kept, arrived, vector, diag, share, ordered, with_inner):
+def combine(table, piece, kept, arrived, vector, diag, share, ordered, with_inner):
     count, rows, width = diag.shape
-    base, size, skip = part
+    base, size = piece
     block = (kept.shape[0] // count, width)
 
     def slot(i, table):
@@ -302,7 +302,7 @@
             grid=(size,),
             in_specs=[
                 pl.BlockSpec(block, lambda i, t: (place(i, t), 0)),
-                pl.BlockSpec(block, lambda i, t: (skip + i, 0)),
+                pl.BlockSpec(block, lambda i, t: (i, 0)),
                 pl.BlockSpec(block, held),
                 pl.BlockSpec((1, rows, width), lambda i, t: (slot(i, t), 0, 0)),
             ],
@@ -475,15 +475,14 @@
     table = make_table(partner, term_kind, vector)
     diag = left_diag[:, :, None] + right_diag[:, None, :]
 
-    staying = (0, 0, per)
-    moving = sorted(range(1, devices), key=lambda c: (-min(c, devices - c), c))
-    moving = [(c, c * per, per) for c in moving]
     cuts = [(0, per // 2), (per // 2, per - per // 2)] if per > 1 else [(0, per)]
-    shares = [
-        (piece, piece[1] + start, size, start) for piece in [staying] + moving for start, size in cuts
-    ]
-    lasting = len(shares) - len(cuts)
-    batches = [moving[:1], moving[1:] + [staying]]
+    offsets = sorted(range(1, devices), key=lambda c: (-min(c, devices - c), c))
+    moving = [(c, c * per + start, size) for c in offsets for start, size in cuts]
+    staying = [(0, start, size) for start, size in cuts]
+    pieces = staying + moving
+    ahead_of = len(cuts)
+    lasting = len(pieces) - ahead_of
+    batches = [moving[:ahead_of], moving[ahead_of:] + staying]
 
     def spans(pieces):
         return [piece[1:] for piece in pieces]
@@ -519,24 +518,23 @@
         arrived, sums, inners = {}, [], []
         for at, piece in enumerate(moving):
             value = outgoing[piece]
-            if at >= 2:
-                value = after(value, arrived[moving[at - 2]])[0]
+            if at >= ahead_of:
+                value = after(value, arrived[moving[at - ahead_of]])[0]
             arrived[piece] = relay(value, piece[0])
-        arrived[staying] = outgoing[staying]
-        for piece, *part in shares:
+        for piece in pieces:
             mine, inner = combine(
                 table,
-                part,
+                piece[1:],
                 kept,
-                arrived[piece],
+                arrived[piece] if piece[0] else outgoing[piece],
                 own,
                 diag,
                 1.0 / terms_over,
                 second,
                 not second,
             )
-            if len(sums) >= 2 * len(cuts):
-                mine = after(mine, sums[1 - 2 * len(cuts)])[0]
+            if len(sums) >= 2 * ahead_of:
+                mine = after(mine, sums[1 - 2 * ahead_of])[0]
             sums += add_over_term(mine)
             inners.append(inner)
         return sums, inners, arrived, other
@@ -544,14 +542,14 @@
     sums, inners, _, _ = partials(vector, False)
     inner = small_sum(small_sum(sum(inners[1:], inners[0]), "sub"), "blk")
     inner = small_sum(after(inner, sums[-1])[0], "term")
-    first = spans(batches[0])[0]
+    first = (batches[0][0][1], sum(size for _, _, size in batches[0]))
     raw, ahead = correct(
-        table, [[part[1:3]] for part in shares], first, inner, vector, diag, sums
+        table, [[piece[1:]] for piece in pieces], first, inner, vector, diag, sums
     )
 
     sums, _, arrived, other = partials(raw, True)
     squares = raw[-TAG:] + other[-TAG:]
-    for piece in moving:
+    for piece in moving[::ahead_of]:
         squares = squares + arrived[piece][-TAG:]
     scale = lax.rsqrt(jnp.sum(squares, axis=1, keepdims=True) / elements + 1e-06)
     scale = jnp.broadcast_to(scale, squares.shape)
@@ -560,8 +558,7 @@
     for some in (slice(0, lasting), slice(lasting, None)):
         parts = [one for pair in list(zip(sums[::2], sums[1::2]))[some] for one in pair]
         if parts:
-            spans_of = [part[1:3] for part in shares[some]]
-            sigma = finish(table, spans_of, scale, parts, sigma, slots, rows)
+            sigma = finish(table, spans(pieces[some]), scale, parts, sigma, slots, rows)
     return tuple(
         jnp.transpose(value.reshape(slots, roots, rows, width), (0, 2, 1, 3))
         for value in (sigma, correction)

time: 141 us -> 131 us (0.929)
  waiting for transfers between devices: 50.6 us -> 33.1 us
  starting transfers between devices: 34.5 us -> 41.1 us
    ppermute x21, waiting for transfers between devices: 35 us -> 25.8 us  [flip(): return lax.ppermute(value, axis, [(i, i ^ bit) for i in range(size)])]
    ppermute x6 -> x12, waiting for transfers between devices: 13.9 us -> 5.52 us  [relay(): lax.ppermute(value, 'blk', [(p, (p + c) % devices) for p in range(devices)])]
    ppermute x6 -> x12, starting transfers between devices: 10.5 us -> 18.5 us  [relay(): lax.ppermute(value, 'blk', [(p, (p + c) % devices) for p in range(devices)])]
  transfers between devices with their start and end apart: 30 -> 36, of which waited for: 15 -> 21; matrix products, arithmetic and copies ran while one was open for 0% -> 0% of each run, Pallas kernels for 31% -> 34%
where the time goes in v11:
time: 131 us
  Pallas kernels  52.4 us (40%)
  starting transfers between devices  41.1 us (31%)
  waiting for transfers between devices  33.1 us (25%)
  local copies, waits for them, and re-layouts  2.81 us (2%)
    pallas_call x4, Pallas kernels, sectors(): pl.pallas_call(functools.partial(sector_kernel, count, terms, unroll, sta...  34.5 us
    ppermute x21, waiting for transfers between devices, flip(): return lax.ppermute(value, axis, [(i, i ^ bit) for i in range(size)])  25.8 us
    ppermute x21, starting transfers between devices, flip(): return lax.ppermute(value, axis, [(i, i ^ bit) for i in range(size)])  21.9 us
    ppermute x12, starting transfers between devices, relay(): lax.ppermute(value, 'blk', [(p, (p + c) % devices) for p in range(devices)])  18.5 us
    pallas_call x16, Pallas kernels, combine(): pl.pallas_call(functools.partial(combine_kernel, share, with_inner), out_...  10.4 us
    ppermute x12, waiting for transfers between devices, relay(): lax.ppermute(value, 'blk', [(p, (p + c) % devices) for p in range(devices)])  5.52 us
    pallas_call x2, Pallas kernels, finish(): pl.pallas_call(functools.partial(finish_kernel, count, rows, [size for _,...  2.99 us
    unnamed x12, local copies, waits for them, and re-layouts  2.73 us
  transfers between devices with their start and end apart: 36, of which 21 were waited for; matrix products, arithmetic and copies ran while one was open for 0% of the time, Pallas kernels for 34%

profile of v11, /device:TPU:0, one launch (start us, length us, event | category | flops | bytes accessed | tf_op | source)
XLA Modules:
  0.0 130.8 jit_solution(17361041735511057465)
XLA Ops:
  1.1 1.4 %copy-done = f32[16,64,3,128]{3,1,2,0:T(8,128)S(1)} copy-done((f32[16,64,3,128]{3,1,2,0:T(8,128)S(1)}, f32[16,64,3,128]{3,1,2,0:T(8,128)}, u32[]{:S(2)}) %copy-start) | copy-done | bytes 1572888
  3.9 1.5 %table.1 = s32[57]{0:T(128)S(1)} custom-call(s32[16]{0:T(128)S(1)} %copy-done.2, s32[8]{0:T(128)S(1)} %copy-done.3, f32[3072,128]{1,0:T(8,128)S(1)} %bitcast.10), custom_call_target="tpu_custom_call" | custom-call | tf_op jit(solution)/shard_map/table/pallas_call | solution.py:83
  5.4 5.2 %sectors.4 = (f32[384,128]{1,0:T(8,128)S(1)}, f32[384,128]{1,0:T(8,128)S(1)}, f32[3072,128]{1,0:T(8,128)S(1)}) custom-call(s32[57]{0:T(128)S(1)} %table.1, f32[8,16,64,128]{3,2,1,0:T(8,128)} %refs_4_.7, f32[8,16,128,128]{3,2,1,0:T(8,128)} %refs_5_.7, f32[3072,128]{1,0:T(8,128)S(1)} %bitcast.11, f32[3072,128]{1,0:T(8,128)S(1)} %collective-permute-done.refs_3_.refs_7_, ...), custom_call_target="tpu_custom_call" | custom-call | tf_op jit(solution)/shard_map/sectors/pallas_call | solution.py:223
  10.6 3.7 %collective-permute-start.2 = (f32[384,128]{1,0:T(8,128)S(1)}, f32[384,128]{1,0:T(8,128)S(1)}, u32[]{:S(2)}, u32[]{:S(2)}) collective-permute-start(f32[384,128]{1,0:T(8,128)S(1)} %get-tuple-element.70), channel_id=1, source_target_pairs={{0,8},{4,12},{8,0},{12,4},{1,9},{5,13},{9,1},{13,5},{2,10},{6,14},... | collective-permute-start | bytes 589832 | tf_op jit(solution)/shard_map/ppermute | solution.py:491
  14.6 12.1 %sectors.5 = (f32[384,128]{1,0:T(8,128)S(1)}, f32[384,128]{1,0:T(8,128)S(1)}, f32[384,128]{1,0:T(8,128)S(1)}, f32[384,128]{1,0:T(8,128)S(1)}, f32[384,128]{1,0:T...) custom-call(s32[57]{0:T(128)S(1)} %table.1, ...), custom_call_target="tpu_custom_call", output_to_operand_aliasing={{6}: (9, {})} | custom-call | tf_op jit(solution)/shard_map/sectors/pallas_call | solution.py:223
  27.3 1.7 %collective-permute-start.11 = (f32[384,128]{1,0:T(8,128)S(1)}, f32[384,128]{1,0:T(8,128)S(1)}, u32[]{:S(2)}, u32[]{:S(2)}) collective-permute-start(f32[384,128]{1,0:T(8,128)S(1)} %get-tuple-element.87.rest_2_), channel_id=1, source_target_pairs={{0,2},{2,0},{1,3},{3,1},{4,6},{6,4},{5,7},{7,5},{8,10},{10,8},{9,1... | collective-permute-start | bytes 589832 | tf_op jit(solution)/shard_map/ppermute | solution.py:25
  30.2 1.8 %collective-permute-start.4 = (f32[384,128]{1,0:T(8,128)S(1)}, f32[384,128]{1,0:T(8,128)S(1)}, u32[]{:S(2)}, u32[]{:S(2)}) collective-permute-start(f32[384,128]{1,0:T(8,128)S(1)} %get-tuple-element.76), channel_id=1, source_target_pairs={{0,4},{4,8},{8,12},{12,0},{1,5},{5,9},{9,13},{13,1},{2,6},{6,10},{... | collective-permute-start | bytes 589832 | tf_op jit(solution)/shard_map/ppermute | solution.py:491
  32.5 1.0 collective-permute-start.3
  34.2 0.9 collective-permute-done.11.rest_3_
  35.1 1.7 %collective-permute-start.12 = (f32[384,128]{1,0:T(8,128)S(1)}, f32[384,128]{1,0:T(8,128)S(1)}, u32[]{:S(2)}, u32[]{:S(2)}) collective-permute-start(f32[384,128]{1,0:T(8,128)S(1)} %get-tuple-element.88.rest_6_), channel_id=1, source_target_pairs={{0,2},{2,0},{1,3},{3,1},{4,6},{6,4},{5,7},{7,5},{8,10},{10,8},{9,1... | collective-permute-start | bytes 589832 | tf_op jit(solution)/shard_map/ppermute | solution.py:25
  37.5 1.8 %collective-permute-done.16.rest_1_ = f32[384,128]{1,0:T(8,128)S(1)} collective-permute-done((f32[384,128]{1,0:T(8,128)S(1)}, f32[384,128]{1,0:T(8,128)S(1)}, u32[]{:S(2)}, u32[]{:S(2)}) %collective-permute-start.16) | collective-permute-done | bytes 196640 | tf_op jit(solution)/shard_map/ppermute | solution.py:25
  39.3 1.7 %collective-permute-start.17 = (f32[384,128]{1,0:T(8,128)S(1)}, f32[384,128]{1,0:T(8,128)S(1)}, u32[]{:S(2)}, u32[]{:S(2)}) collective-permute-start(f32[384,128]{1,0:T(8,128)S(1)} %get-tuple-element.94.rest_4_), channel_id=1, source_target_pairs={{0,2},{2,0},{1,3},{3,1},{4,6},{6,4},{5,7},{7,5},{8,10},{10,8},{9,1... | collective-permute-start | bytes 589832 | tf_op jit(solution)/shard_map/ppermute | solution.py:25
  41.1 3.6 %collective-permute-start.6 = (f32[384,128]{1,0:T(8,128)S(1)}, f32[384,128]{1,0:T(8,128)S(1)}, u32[]{:S(2)}, u32[]{:S(2)}) collective-permute-start(f32[384,128]{1,0:T(8,128)S(1)} %get-tuple-element.82), channel_id=1, source_target_pairs={{0,12},{4,0},{8,4},{12,8},{1,13},{5,1},{9,5},{13,9},{2,14},{6,2},{... | collective-permute-start | bytes 589832 | tf_op jit(solution)/shard_map/ppermute | solution.py:491
  45.8 0.9 collective-permute-start.13
  47.8 1.5 %collective-permute-start.18 = (f32[384,128]{1,0:T(8,128)S(1)}, f32[384,128]{1,0:T(8,128)S(1)}, u32[]{:S(2)}, u32[]{:S(2)}) collective-permute-start(f32[384,128]{1,0:T(8,128)S(1)} %get-tuple-element.96.rest_8_), channel_id=1, source_target_pairs={{0,2},{2,0},{1,3},{3,1},{4,6},{6,4},{5,7},{7,5},{8,10},{10,8},{9,1... | collective-permute-start | bytes 589832 | tf_op jit(solution)/shard_map/ppermute | solution.py:25
  50.0 1.1 collective-permute-done.5.arrived_ref
  51.9 1.2 collective-permute-done.7
  53.0 1.7 %collective-permute-start.9 = (f32[8,128]{1,0:T(8,128)S(1)}, f32[8,128]{1,0:T(8,128)S(1)}, u32[]{:S(2)}, u32[]{:S(2)}) collective-permute-start(f32[8,128]{1,0:T(8,128)S(1)} %add.79), channel_id=1, source_target_pairs={{0,8},{4,12},{8,0},{12,4},{1,9},{5,13},{9,1},{13,5},{2,10},{6,14},... | collective-permute-start | bytes 12296 | tf_op jit(solution)/shard_map/ppermute | solution.py:25
  54.7 2.5 %collective-permute-start.10 = (f32[8,128]{1,0:T(8,128)S(1)}, f32[8,128]{1,0:T(8,128)S(1)}, u32[]{:S(2)}, u32[]{:S(2)}) collective-permute-start(f32[8,128]{1,0:T(8,128)S(1)} %add.79), channel_id=1, source_target_pairs={{0,12},{4,8},{8,4},{12,0},{1,13},{5,9},{9,5},{13,1},{2,14},{6,10},... | collective-permute-start | bytes 12296 | tf_op jit(solution)/shard_map/ppermute | solution.py:25
  57.7 0.7 collective-permute-start.14
  58.4 1.3 %collective-permute-start.19 = (f32[384,128]{1,0:T(8,128)S(1)}, f32[384,128]{1,0:T(8,128)S(1)}, u32[]{:S(2)}, u32[]{:S(2)}) collective-permute-start(f32[384,128]{1,0:T(8,128)S(1)} %get-tuple-element.98.rest_12_), channel_id=1, source_target_pairs={{0,2},{2,0},{1,3},{3,1},{4,6},{6,4},{5,7},{7,5},{8,10},{10,8},{9,1... | collective-permute-start | bytes 589832 | tf_op jit(solution)/shard_map/ppermute | solution.py:25
  60.8 4.8 %collective-permute-done.14.rest_15_ = f32[384,128]{1,0:T(8,128)S(1)} collective-permute-done((f32[384,128]{1,0:T(8,128)S(1)}, f32[384,128]{1,0:T(8,128)S(1)}, u32[]{:S(2)}, u32[]{:S(2)}) %collective-permute-start.14) | collective-permute-done | bytes 196640 | tf_op jit(solution)/shard_map/ppermute | solution.py:25
  65.6 0.7 collective-permute-start.15
  66.2 2.9 %collective-permute-done.15 = f32[8,128]{1,0:T(8,128)S(1)} collective-permute-done((f32[8,128]{1,0:T(8,128)S(1)}, f32[8,128]{1,0:T(8,128)S(1)}, u32[]{:S(2)}, u32[]{:S(2)}) %collective-permute-start.15) | collective-permute-done | bytes 4128 | tf_op jit(solution)/shard_map/ppermute | solution.py:25
  69.2 1.3 correct.1
  70.5 1.7 %collective-permute-done.20.refs_3_.refs_7_.refs_9_ = f32[776,128]{1,0:T(8,128)S(1)} collective-permute-done((f32[776,128]{1,0:T(8,128)S(1)}, f32[776,128]{1,0:T(8,128)S(1)}, u32[]{:S(2)}, u32[]{:S(2)}) %collective-permute-start.20) | collective-permute-done | bytes 397344 | tf_op jit(solution)/shard_map/ppermute | solution.py:494
  72.4 5.2 %sectors.6 = (f32[392,128]{1,0:T(8,128)S(1)}, f32[392,128]{1,0:T(8,128)S(1)}, f32[3072,128]{1,0:T(8,128)S(1)}) custom-call(s32[57]{0:T(128)S(1)} %table.1, f32[8,16,64,128]{3,2,1,0:T(8,128)} %refs_4_.7, f32[8,16,128,128]{3,2,1,0:T(8,128)} %refs_5_.7, f32[776,128]{1,0:T(8,128)S(1)} %get-tuple-element.100.refs_2_.refs_6_.refs_8_, ...), custom_call_target="tpu_custom_call" | custom-call | tf_op jit(solution)/shard_map/sectors/pallas_call | solution.py:223
  77.6 1.5 %collective-permute-start.22 = (f32[392,128]{1,0:T(8,128)S(1)}, f32[392,128]{1,0:T(8,128)S(1)}, u32[]{:S(2)}, u32[]{:S(2)}) collective-permute-start(f32[392,128]{1,0:T(8,128)S(1)} %get-tuple-element.102), channel_id=1, source_target_pairs={{0,8},{4,12},{8,0},{12,4},{1,9},{5,13},{9,1},{13,5},{2,10},{6,14},... | collective-permute-start | bytes 602120 | tf_op jit(solution)/shard_map/ppermute | solution.py:491
  79.1 1.5 %collective-permute-start.29 = (f32[392,128]{1,0:T(8,128)S(1)}, f32[392,128]{1,0:T(8,128)S(1)}, u32[]{:S(2)}, u32[]{:S(2)}) collective-permute-start(f32[392,128]{1,0:T(8,128)S(1)} %get-tuple-element.115), channel_id=1, source_target_pairs={{0,8},{4,12},{8,0},{12,4},{1,9},{5,13},{9,1},{13,5},{2,10},{6,14},... | collective-permute-start | bytes 602120 | tf_op jit(solution)/shard_map/ppermute | solution.py:491
  80.6 12.1 %sectors.7 = (f32[392,128]{1,0:T(8,128)S(1)}, f32[392,128]{1,0:T(8,128)S(1)}, f32[392,128]{1,0:T(8,128)S(1)}, f32[392,128]{1,0:T(8,128)S(1)}, f32[384,128]{1,0:T...) custom-call(s32[57]{0:T(128)S(1)} %table.1, ...), custom_call_target="tpu_custom_call", output_to_operand_aliasing={{6}: (11, {})} | custom-call | tf_op jit(solution)/shard_map/sectors/pallas_call | solution.py:223
  93.3 0.7 collective-permute-start.25
  94.6 1.5 %collective-permute-start.32 = (f32[384,128]{1,0:T(8,128)S(1)}, f32[384,128]{1,0:T(8,128)S(1)}, u32[]{:S(2)}, u32[]{:S(2)}) collective-permute-start(f32[384,128]{1,0:T(8,128)S(1)} %combine.31.refs_2_), channel_id=1, source_target_pairs={{0,2},{2,0},{1,3},{3,1},{4,6},{6,4},{5,7},{7,5},{8,10},{10,8},{9,1... | collective-permute-start | bytes 589832 | tf_op jit(solution)/shard_map/ppermute | solution.py:25
  96.1 1.5 %collective-permute-start.23 = (f32[392,128]{1,0:T(8,128)S(1)}, f32[392,128]{1,0:T(8,128)S(1)}, u32[]{:S(2)}, u32[]{:S(2)}) collective-permute-start(f32[392,128]{1,0:T(8,128)S(1)} %get-tuple-element.105), channel_id=1, source_target_pairs={{0,4},{4,8},{8,12},{12,0},{1,5},{5,9},{9,13},{13,1},{2,6},{6,10},{... | collective-permute-start | bytes 602120 | tf_op jit(solution)/shard_map/ppermute | solution.py:491
  97.5 1.2 collective-permute-done.29.arrived_ref
  100.0 1.2 collective-permute-done.25.refs_1_
  101.8 3.6 %collective-permute-done.32.refs_3_ = f32[384,128]{1,0:T(8,128)S(1)} collective-permute-done((f32[384,128]{1,0:T(8,128)S(1)}, f32[384,128]{1,0:T(8,128)S(1)}, u32[]{:S(2)}, u32[]{:S(2)}) %collective-permute-start.32) | collective-permute-done | bytes 196640 | tf_op jit(solution)/shard_map/ppermute | solution.py:25
  106.0 3.0 %collective-permute-start.24 = (f32[392,128]{1,0:T(8,128)S(1)}, f32[392,128]{1,0:T(8,128)S(1)}, u32[]{:S(2)}, u32[]{:S(2)}) collective-permute-start(f32[392,128]{1,0:T(8,128)S(1)} %get-tuple-element.107), channel_id=1, source_target_pairs={{0,12},{4,0},{8,4},{12,8},{1,13},{5,1},{9,5},{13,9},{2,14},{6,2},{... | collective-permute-start | bytes 602120 | tf_op jit(solution)/shard_map/ppermute | solution.py:491
  111.0 0.8 collective-permute-start.27
  111.7 1.5 %collective-permute-done.33.refs_7_ = f32[384,128]{1,0:T(8,128)S(1)} collective-permute-done((f32[384,128]{1,0:T(8,128)S(1)}, f32[384,128]{1,0:T(8,128)S(1)}, u32[]{:S(2)}, u32[]{:S(2)}) %collective-permute-start.33) | collective-permute-done | bytes 196640 | tf_op jit(solution)/shard_map/ppermute | solution.py:25
  114.6 2.3 %collective-permute-done.31.arrived_ref = f32[392,128]{1,0:T(8,128)S(1)} collective-permute-done((f32[392,128]{1,0:T(8,128)S(1)}, f32[392,128]{1,0:T(8,128)S(1)}, u32[]{:S(2)}, u32[]{:S(2)}) %collective-permute-start.31) | collective-permute-done | bytes 200736 | tf_op jit(solution)/shard_map/ppermute | solution.py:491
  117.6 1.2 collective-permute-done.27.refs_9_
  118.9 0.7 collective-permute-start.28
  119.6 3.3 %collective-permute-done.34.refs_11_ = f32[384,128]{1,0:T(8,128)S(1)} collective-permute-done((f32[384,128]{1,0:T(8,128)S(1)}, f32[384,128]{1,0:T(8,128)S(1)}, u32[]{:S(2)}, u32[]{:S(2)}) %collective-permute-start.34) | collective-permute-done | bytes 196640 | tf_op jit(solution)/shard_map/ppermute | solution.py:25
  122.8 0.9 collective-permute-start.35
  123.8 1.8 %scaled.1 = f32[3072,128]{1,0:T(8,128)} custom-call(s32[57]{0:T(128)S(1)} %table.1, f32[8,128]{1,0:T(8,128)S(1)} %broadcast_in_dim.2.scale_ref, f32[3080,128]{1,0:T(8,128)S(1)} %get-tuple-element.101.refs_2_.refs_6_.refs_8_.vector_ref.raw_ref), custom_call_target="tpu_custom_call" | custom-call | tf_op jit(solution)/shard_map/scaled/pallas_call | solution.py:397
  125.7 1.7 %finish.2.refs_4_ = f32[3072,128]{1,0:T(8,128)} custom-call(s32[57]{0:T(128)S(1)} %table.1, f32[8,128]{1,0:T(8,128)S(1)} %broadcast_in_dim.2.scale_ref, f32[384,128]{1,0:T(8,128)S(1)} %combine.27.refs_0_, f32[384,128]{1,0:T(8,128)S(1)} %collective-permute-done.25.refs_1_, f32[384,128]{1,0:T(8,128)S(1)} %combine.31.refs_2_, ...), custom_call_target="tpu_custom_call" | custom-call | tf_op jit(solution)/shard_map/finish/pallas_call | solution.py:438
  127.4 2.1 %collective-permute-done.35.refs_3_ = f32[384,128]{1,0:T(8,128)S(1)} collective-permute-done((f32[384,128]{1,0:T(8,128)S(1)}, f32[384,128]{1,0:T(8,128)S(1)}, u32[]{:S(2)}, u32[]{:S(2)}) %collective-permute-start.35) | collective-permute-done | bytes 196640 | tf_op jit(solution)/shard_map/ppermute | solution.py:25
  129.4 1.3 %finish.3 = f32[3072,128]{1,0:T(8,128)} custom-call(s32[57]{0:T(128)S(1)} %table.1, f32[8,128]{1,0:T(8,128)S(1)} %broadcast_in_dim.2.scale_ref, f32[384,128]{1,0:T(8,128)S(1)} %combine.24.refs_0_, f32[384,128]{1,0:T(8,128)S(1)} %collective-permute-done.28.refs_1_, f32[384,128]{1,0:T(8,128)S(1)} %combine.28.refs_2_, ...), custom_call_target="tpu_custom_call", output_to_operand_aliasing={{}: (6, {})} | custom-call | tf_op jit(solution)/shard_map/finish/pallas_call | solution.py:438
  (69 shorter events, 19.1 us)
Async XLA Ops:
  0.6 4.8 %collective-permute-start = (f32[3072,128]{1,0:T(8,128)}, f32[3072,128]{1,0:T(8,128)S(1)}, u32[]{:S(2)}, u32[]{:S(2)}) collective-permute-start(f32[3072,128]{1,0:T(8,128)} %bitcast.9), channel_id=1, source_target_pairs={{0,1},{1,0},{2,3},{3,2},{4,5},{5,4},{6,7},{7,6},{8,9},{9,8},{10,11... | collective-permute-start | bytes 4718600 | tf_op jit(solution)/shard_map/ppermute | solution.py:494
  1.1 1.4 %copy-start = (f32[16,64,3,128]{3,1,2,0:T(8,128)S(1)}, f32[16,64,3,128]{3,1,2,0:T(8,128)}, u32[]{:S(2)}) copy-start(f32[16,64,3,128]{3,1,2,0:T(8,128)} %param.7) | copy-start | bytes 4718596
  2.6 0.7 copy-start.2
  3.2 0.7 copy-start.3
  3.9 1.5 %copy-start.1 = (f32[16,64,3,128]{3,1,2,0:T(8,128)S(1)}, f32[16,64,3,128]{3,1,2,0:T(8,128)}, u32[]{:S(2)}) copy-start(f32[16,64,3,128]{3,1,2,0:T(8,128)} %param.7) | copy-start | bytes 4718596
  5.4 9.0 %copy-start.4 = (f32[16,128]{1,0:T(8,128)S(1)}, f32[16,128]{1,0:T(8,128)}, u32[]{:S(2)}) copy-start(f32[16,128]{1,0:T(8,128)} %param.13) | copy-start | bytes 24580
  5.4 9.0 %copy-start.5 = (f32[16,64]{1,0:T(8,128)S(1)}, f32[16,64]{1,0:T(8,128)}, u32[]{:S(2)}) copy-start(f32[16,64]{1,0:T(8,128)} %param.12) | copy-start | bytes 12292
  10.6 19.5 %collective-permute-start.2 = (f32[384,128]{1,0:T(8,128)S(1)}, f32[384,128]{1,0:T(8,128)S(1)}, u32[]{:S(2)}, u32[]{:S(2)}) collective-permute-start(f32[384,128]{1,0:T(8,128)S(1)} %get-tuple-element.70), channel_id=1, source_target_pairs={{0,8},{4,12},{8,0},{12,4},{1,9},{5,13},{9,1},{13,5},{2,10},{6,14},... | collective-permute-start | bytes 589832 | tf_op jit(solution)/shard_map/ppermute | solution.py:491
  14.3 18.2 %collective-permute-start.1 = (f32[384,128]{1,0:T(8,128)S(1)}, f32[384,128]{1,0:T(8,128)S(1)}, u32[]{:S(2)}, u32[]{:S(2)}) collective-permute-start(f32[384,128]{1,0:T(8,128)S(1)} %get-tuple-element.68), channel_id=1, source_target_pairs={{0,8},{4,12},{8,0},{12,4},{1,9},{5,13},{9,1},{13,5},{2,10},{6,14},... | collective-permute-start | bytes 589832 | tf_op jit(solution)/shard_map/ppermute | solution.py:491
  27.3 7.8 %collective-permute-start.11 = (f32[384,128]{1,0:T(8,128)S(1)}, f32[384,128]{1,0:T(8,128)S(1)}, u32[]{:S(2)}, u32[]{:S(2)}) collective-permute-start(f32[384,128]{1,0:T(8,128)S(1)} %get-tuple-element.87.rest_2_), channel_id=1, source_target_pairs={{0,2},{2,0},{1,3},{3,1},{4,6},{6,4},{5,7},{7,5},{8,10},{10,8},{9,1... | collective-permute-start | bytes 589832 | tf_op jit(solution)/shard_map/ppermute | solution.py:25
  29.7 9.6 %collective-permute-start.16 = (f32[384,128]{1,0:T(8,128)S(1)}, f32[384,128]{1,0:T(8,128)S(1)}, u32[]{:S(2)}, u32[]{:S(2)}) collective-permute-start(f32[384,128]{1,0:T(8,128)S(1)} %get-tuple-element.92.rest_0_), channel_id=1, source_target_pairs={{0,2},{2,0},{1,3},{3,1},{4,6},{6,4},{5,7},{7,5},{8,10},{10,8},{9,1... | collective-permute-start | bytes 589832 | tf_op jit(solution)/shard_map/ppermute | solution.py:25
  30.2 10.9 %collective-permute-start.4 = (f32[384,128]{1,0:T(8,128)S(1)}, f32[384,128]{1,0:T(8,128)S(1)}, u32[]{:S(2)}, u32[]{:S(2)}) collective-permute-start(f32[384,128]{1,0:T(8,128)S(1)} %get-tuple-element.76), channel_id=1, source_target_pairs={{0,4},{4,8},{8,12},{12,0},{1,5},{5,9},{9,13},{13,1},{2,6},{6,10},{... | collective-permute-start | bytes 589832 | tf_op jit(solution)/shard_map/ppermute | solution.py:491
  32.5 12.2 %collective-permute-start.3 = (f32[384,128]{1,0:T(8,128)S(1)}, f32[384,128]{1,0:T(8,128)S(1)}, u32[]{:S(2)}, u32[]{:S(2)}) collective-permute-start(f32[384,128]{1,0:T(8,128)S(1)} %get-tuple-element.73), channel_id=1, source_target_pairs={{0,4},{4,8},{8,12},{12,0},{1,5},{5,9},{9,13},{13,1},{2,6},{6,10},{... | collective-permute-start | bytes 589832 | tf_op jit(solution)/shard_map/ppermute | solution.py:491
  35.1 10.7 %collective-permute-start.12 = (f32[384,128]{1,0:T(8,128)S(1)}, f32[384,128]{1,0:T(8,128)S(1)}, u32[]{:S(2)}, u32[]{:S(2)}) collective-permute-start(f32[384,128]{1,0:T(8,128)S(1)} %get-tuple-element.88.rest_6_), channel_id=1, source_target_pairs={{0,2},{2,0},{1,3},{3,1},{4,6},{6,4},{5,7},{7,5},{8,10},{10,8},{9,1... | collective-permute-start | bytes 589832 | tf_op jit(solution)/shard_map/ppermute | solution.py:25
  39.3 8.4 %collective-permute-start.17 = (f32[384,128]{1,0:T(8,128)S(1)}, f32[384,128]{1,0:T(8,128)S(1)}, u32[]{:S(2)}, u32[]{:S(2)}) collective-permute-start(f32[384,128]{1,0:T(8,128)S(1)} %get-tuple-element.94.rest_4_), channel_id=1, source_target_pairs={{0,2},{2,0},{1,3},{3,1},{4,6},{6,4},{5,7},{7,5},{8,10},{10,8},{9,1... | collective-permute-start | bytes 589832 | tf_op jit(solution)/shard_map/ppermute | solution.py:25
  41.1 8.3 %collective-permute-start.6 = (f32[384,128]{1,0:T(8,128)S(1)}, f32[384,128]{1,0:T(8,128)S(1)}, u32[]{:S(2)}, u32[]{:S(2)}) collective-permute-start(f32[384,128]{1,0:T(8,128)S(1)} %get-tuple-element.82), channel_id=1, source_target_pairs={{0,12},{4,0},{8,4},{12,8},{1,13},{5,1},{9,5},{13,9},{2,14},{6,2},{... | collective-permute-start | bytes 589832 | tf_op jit(solution)/shard_map/ppermute | solution.py:491
  44.7 6.4 %collective-permute-start.5 = (f32[384,128]{1,0:T(8,128)S(1)}, f32[384,128]{1,0:T(8,128)S(1)}, u32[]{:S(2)}, u32[]{:S(2)}) collective-permute-start(f32[384,128]{1,0:T(8,128)S(1)} %get-tuple-element.79), channel_id=1, source_target_pairs={{0,12},{4,0},{8,4},{12,8},{1,13},{5,1},{9,5},{13,9},{2,14},{6,2},{... | collective-permute-start | bytes 589832 | tf_op jit(solution)/shard_map/ppermute | solution.py:491
  45.8 11.9 %collective-permute-start.13 = (f32[384,128]{1,0:T(8,128)S(1)}, f32[384,128]{1,0:T(8,128)S(1)}, u32[]{:S(2)}, u32[]{:S(2)}) collective-permute-start(f32[384,128]{1,0:T(8,128)S(1)} %get-tuple-element.89.rest_10_), channel_id=1, source_target_pairs={{0,2},{2,0},{1,3},{3,1},{4,6},{6,4},{5,7},{7,5},{8,10},{10,8},{9,1... | collective-permute-start | bytes 589832 | tf_op jit(solution)/shard_map/ppermute | solution.py:25
  47.8 10.7 %collective-permute-start.18 = (f32[384,128]{1,0:T(8,128)S(1)}, f32[384,128]{1,0:T(8,128)S(1)}, u32[]{:S(2)}, u32[]{:S(2)}) collective-permute-start(f32[384,128]{1,0:T(8,128)S(1)} %get-tuple-element.96.rest_8_), channel_id=1, source_target_pairs={{0,2},{2,0},{1,3},{3,1},{4,6},{6,4},{5,7},{7,5},{8,10},{10,8},{9,1... | collective-permute-start | bytes 589832 | tf_op jit(solution)/shard_map/ppermute | solution.py:25
  51.8 1.2 collective-permute-start.7
  53.0 6.7 %collective-permute-start.9 = (f32[8,128]{1,0:T(8,128)S(1)}, f32[8,128]{1,0:T(8,128)S(1)}, u32[]{:S(2)}, u32[]{:S(2)}) collective-permute-start(f32[8,128]{1,0:T(8,128)S(1)} %add.79), channel_id=1, source_target_pairs={{0,8},{4,12},{8,0},{12,4},{1,9},{5,13},{9,1},{13,5},{2,10},{6,14},... | collective-permute-start | bytes 12296 | tf_op jit(solution)/shard_map/ppermute | solution.py:25
  54.7 5.4 %collective-permute-start.10 = (f32[8,128]{1,0:T(8,128)S(1)}, f32[8,128]{1,0:T(8,128)S(1)}, u32[]{:S(2)}, u32[]{:S(2)}) collective-permute-start(f32[8,128]{1,0:T(8,128)S(1)} %add.79), channel_id=1, source_target_pairs={{0,12},{4,8},{8,4},{12,0},{1,13},{5,9},{9,5},{13,1},{2,14},{6,10},... | collective-permute-start | bytes 12296 | tf_op jit(solution)/shard_map/ppermute | solution.py:25
  57.2 3.6 %collective-permute-start.8 = (f32[8,128]{1,0:T(8,128)S(1)}, f32[8,128]{1,0:T(8,128)S(1)}, u32[]{:S(2)}, u32[]{:S(2)}) collective-permute-start(f32[8,128]{1,0:T(8,128)S(1)} %add.79), channel_id=1, source_target_pairs={{0,4},{4,0},{8,12},{12,8},{1,5},{5,1},{9,13},{13,9},{2,6},{6,2},{1... | collective-permute-start | bytes 12296 | tf_op jit(solution)/shard_map/ppermute | solution.py:25
  57.7 7.8 %collective-permute-start.14 = (f32[384,128]{1,0:T(8,128)S(1)}, f32[384,128]{1,0:T(8,128)S(1)}, u32[]{:S(2)}, u32[]{:S(2)}) collective-permute-start(f32[384,128]{1,0:T(8,128)S(1)} %get-tuple-element.90.rest_14_), channel_id=1, source_target_pairs={{0,2},{2,0},{1,3},{3,1},{4,6},{6,4},{5,7},{7,5},{8,10},{10,8},{9,1... | collective-permute-start | bytes 589832 | tf_op jit(solution)/shard_map/ppermute | solution.py:25
  58.4 10.8 %collective-permute-start.19 = (f32[384,128]{1,0:T(8,128)S(1)}, f32[384,128]{1,0:T(8,128)S(1)}, u32[]{:S(2)}, u32[]{:S(2)}) collective-permute-start(f32[384,128]{1,0:T(8,128)S(1)} %get-tuple-element.98.rest_12_), channel_id=1, source_target_pairs={{0,2},{2,0},{1,3},{3,1},{4,6},{6,4},{5,7},{7,5},{8,10},{10,8},{9,1... | collective-permute-start | bytes 589832 | tf_op jit(solution)/shard_map/ppermute | solution.py:25
  65.6 3.6 %collective-permute-start.15 = (f32[8,128]{1,0:T(8,128)S(1)}, f32[8,128]{1,0:T(8,128)S(1)}, u32[]{:S(2)}, u32[]{:S(2)}) collective-permute-start(f32[8,128]{1,0:T(8,128)S(1)} %add_add_fusion), channel_id=1, source_target_pairs={{0,2},{2,0},{1,3},{3,1},{4,6},{6,4},{5,7},{7,5},{8,10},{10,8},{9,1... | collective-permute-start | bytes 12296 | tf_op jit(solution)/shard_map/ppermute | solution.py:25
  70.4 1.8 %collective-permute-start.20 = (f32[776,128]{1,0:T(8,128)S(1)}, f32[776,128]{1,0:T(8,128)S(1)}, u32[]{:S(2)}, u32[]{:S(2)}) collective-permute-start(f32[776,128]{1,0:T(8,128)S(1)} %get-tuple-element.100.refs_2_.refs_6_.refs_8_), channel_id=1, source_target_pairs={{0,1},{1,0},{2,3},{3,2},{4,5},{5,4},{6,7},{7,6},{8,9},{9,8},{10,11... | collective-permute-start | bytes 1191944 | tf_op jit(solution)/shard_map/ppermute | solution.py:494
  72.2 8.3 %collective-permute-start.21 = (f32[3080,128]{1,0:T(8,128)S(1)}, f32[3080,128]{1,0:T(8,128)S(1)}, u32[]{:S(2)}, u32[]{:S(2)}) collective-permute-start(f32[3080,128]{1,0:T(8,128)S(1)} %get-tuple-element.101.refs_2_.refs_6_.refs_8_.vector_ref.raw_ref), channel_id=1, source_target_pairs={{0,1},{1,0},{2,3},{3,2},{4,5},{5,4},{6,7},{7,6},{8,9},{9,8},{10,11... | collective-permute-start | bytes 4730888 | tf_op jit(solution)/shard_map/ppermute | solution.py:494
  77.6 18.5 %collective-permute-start.22 = (f32[392,128]{1,0:T(8,128)S(1)}, f32[392,128]{1,0:T(8,128)S(1)}, u32[]{:S(2)}, u32[]{:S(2)}) collective-permute-start(f32[392,128]{1,0:T(8,128)S(1)} %get-tuple-element.102), channel_id=1, source_target_pairs={{0,8},{4,12},{8,0},{12,4},{1,9},{5,13},{9,1},{13,5},{2,10},{6,14},... | collective-permute-start | bytes 602120 | tf_op jit(solution)/shard_map/ppermute | solution.py:491
  79.1 19.6 %collective-permute-start.29 = (f32[392,128]{1,0:T(8,128)S(1)}, f32[392,128]{1,0:T(8,128)S(1)}, u32[]{:S(2)}, u32[]{:S(2)}) collective-permute-start(f32[392,128]{1,0:T(8,128)S(1)} %get-tuple-element.115), channel_id=1, source_target_pairs={{0,8},{4,12},{8,0},{12,4},{1,9},{5,13},{9,1},{13,5},{2,10},{6,14},... | collective-permute-start | bytes 602120 | tf_op jit(solution)/shard_map/ppermute | solution.py:491
  93.3 7.9 %collective-permute-start.25 = (f32[384,128]{1,0:T(8,128)S(1)}, f32[384,128]{1,0:T(8,128)S(1)}, u32[]{:S(2)}, u32[]{:S(2)}) collective-permute-start(f32[384,128]{1,0:T(8,128)S(1)} %combine.27.refs_0_), channel_id=1, source_target_pairs={{0,2},{2,0},{1,3},{3,1},{4,6},{6,4},{5,7},{7,5},{8,10},{10,8},{9,1... | collective-permute-start | bytes 589832 | tf_op jit(solution)/shard_map/ppermute | solution.py:25
  94.6 10.7 %collective-permute-start.32 = (f32[384,128]{1,0:T(8,128)S(1)}, f32[384,128]{1,0:T(8,128)S(1)}, u32[]{:S(2)}, u32[]{:S(2)}) collective-permute-start(f32[384,128]{1,0:T(8,128)S(1)} %combine.31.refs_2_), channel_id=1, source_target_pairs={{0,2},{2,0},{1,3},{3,1},{4,6},{6,4},{5,7},{7,5},{8,10},{10,8},{9,1... | collective-permute-start | bytes 589832 | tf_op jit(solution)/shard_map/ppermute | solution.py:25
  96.1 9.9 %collective-permute-start.23 = (f32[392,128]{1,0:T(8,128)S(1)}, f32[392,128]{1,0:T(8,128)S(1)}, u32[]{:S(2)}, u32[]{:S(2)}) collective-permute-start(f32[392,128]{1,0:T(8,128)S(1)} %get-tuple-element.105), channel_id=1, source_target_pairs={{0,4},{4,8},{8,12},{12,0},{1,5},{5,9},{9,13},{13,1},{2,6},{6,10},{... | collective-permute-start | bytes 602120 | tf_op jit(solution)/shard_map/ppermute | solution.py:491
  98.7 10.5 %collective-permute-start.30 = (f32[392,128]{1,0:T(8,128)S(1)}, f32[392,128]{1,0:T(8,128)S(1)}, u32[]{:S(2)}, u32[]{:S(2)}) collective-permute-start(f32[392,128]{1,0:T(8,128)S(1)} %get-tuple-element.116), channel_id=1, source_target_pairs={{0,4},{4,8},{8,12},{12,0},{1,5},{5,9},{9,13},{13,1},{2,6},{6,10},{... | collective-permute-start | bytes 602120 | tf_op jit(solution)/shard_map/ppermute | solution.py:491
  101.1 9.8 %collective-permute-start.26 = (f32[384,128]{1,0:T(8,128)S(1)}, f32[384,128]{1,0:T(8,128)S(1)}, u32[]{:S(2)}, u32[]{:S(2)}) collective-permute-start(f32[384,128]{1,0:T(8,128)S(1)} %combine.26.refs_4_), channel_id=1, source_target_pairs={{0,2},{2,0},{1,3},{3,1},{4,6},{6,4},{5,7},{7,5},{8,10},{10,8},{9,1... | collective-permute-start | bytes 589832 | tf_op jit(solution)/shard_map/ppermute | solution.py:25
  105.3 7.8 %collective-permute-start.33 = (f32[384,128]{1,0:T(8,128)S(1)}, f32[384,128]{1,0:T(8,128)S(1)}, u32[]{:S(2)}, u32[]{:S(2)}) collective-permute-start(f32[384,128]{1,0:T(8,128)S(1)} %combine.30.refs_6_), channel_id=1, source_target_pairs={{0,2},{2,0},{1,3},{3,1},{4,6},{6,4},{5,7},{7,5},{8,10},{10,8},{9,1... | collective-permute-start | bytes 589832 | tf_op jit(solution)/shard_map/ppermute | solution.py:25
  106.0 7.9 %collective-permute-start.24 = (f32[392,128]{1,0:T(8,128)S(1)}, f32[392,128]{1,0:T(8,128)S(1)}, u32[]{:S(2)}, u32[]{:S(2)}) collective-permute-start(f32[392,128]{1,0:T(8,128)S(1)} %get-tuple-element.107), channel_id=1, source_target_pairs={{0,12},{4,0},{8,4},{12,8},{1,13},{5,1},{9,5},{13,9},{2,14},{6,2},{... | collective-permute-start | bytes 602120 | tf_op jit(solution)/shard_map/ppermute | solution.py:491
  109.2 7.7 %collective-permute-start.31 = (f32[392,128]{1,0:T(8,128)S(1)}, f32[392,128]{1,0:T(8,128)S(1)}, u32[]{:S(2)}, u32[]{:S(2)}) collective-permute-start(f32[392,128]{1,0:T(8,128)S(1)} %get-tuple-element.117), channel_id=1, source_target_pairs={{0,12},{4,0},{8,4},{12,8},{1,13},{5,1},{9,5},{13,9},{2,14},{6,2},{... | collective-permute-start | bytes 602120 | tf_op jit(solution)/shard_map/ppermute | solution.py:491
  111.0 7.9 %collective-permute-start.27 = (f32[384,128]{1,0:T(8,128)S(1)}, f32[384,128]{1,0:T(8,128)S(1)}, u32[]{:S(2)}, u32[]{:S(2)}) collective-permute-start(f32[384,128]{1,0:T(8,128)S(1)} %combine.25.refs_8_), channel_id=1, source_target_pairs={{0,2},{2,0},{1,3},{3,1},{4,6},{6,4},{5,7},{7,5},{8,10},{10,8},{9,1... | collective-permute-start | bytes 589832 | tf_op jit(solution)/shard_map/ppermute | solution.py:25
  113.2 9.6 %collective-permute-start.34 = (f32[384,128]{1,0:T(8,128)S(1)}, f32[384,128]{1,0:T(8,128)S(1)}, u32[]{:S(2)}, u32[]{:S(2)}) collective-permute-start(f32[384,128]{1,0:T(8,128)S(1)} %combine.29.refs_10_), channel_id=1, source_target_pairs={{0,2},{2,0},{1,3},{3,1},{4,6},{6,4},{5,7},{7,5},{8,10},{10,8},{9,1... | collective-permute-start | bytes 589832 | tf_op jit(solution)/shard_map/ppermute | solution.py:25
  118.9 8.5 %collective-permute-start.28 = (f32[384,128]{1,0:T(8,128)S(1)}, f32[384,128]{1,0:T(8,128)S(1)}, u32[]{:S(2)}, u32[]{:S(2)}) collective-permute-start(f32[384,128]{1,0:T(8,128)S(1)} %combine.24.refs_0_), channel_id=1, source_target_pairs={{0,2},{2,0},{1,3},{3,1},{4,6},{6,4},{5,7},{7,5},{8,10},{10,8},{9,1... | collective-permute-start | bytes 589832 | tf_op jit(solution)/shard_map/ppermute | solution.py:25
  122.8 6.6 %collective-permute-start.35 = (f32[384,128]{1,0:T(8,128)S(1)}, f32[384,128]{1,0:T(8,128)S(1)}, u32[]{:S(2)}, u32[]{:S(2)}) collective-permute-start(f32[384,128]{1,0:T(8,128)S(1)} %combine.28.refs_2_), channel_id=1, source_target_pairs={{0,2},{2,0},{1,3},{3,1},{4,6},{6,4},{5,7},{7,5},{8,10},{10,8},{9,1... | collective-permute-start | bytes 589832 | tf_op jit(solution)/shard_map/ppermute | solution.py:25

commit v12 on v11

--- a/solution.py
+++ b/solution.py
@@ -45,23 +45,17 @@
     return high, low
 
 
-def table_kernel(devices, partner_hbm, kind_hbm, _, table_ref, used, partner_ref, kind_ref, sems):
-    copies = [
-        pltpu.make_async_copy(partner_hbm, partner_ref, sems.at[0]),
-        pltpu.make_async_copy(kind_hbm, kind_ref, sems.at[1]),
-    ]
-    for copy in copies:
-        copy.start()
-    for copy in copies:
-        copy.wait()
-    count, terms = partner_ref.shape[0], kind_ref.shape[0]
+def table_kernel(devices, count, terms, given_hbm, _, table_ref, used, given_ref, sem):
+    copy = pltpu.make_async_copy(given_hbm, given_ref, sem)
+    copy.start()
+    copy.wait()
     per = count // devices
     me = lax.axis_index("blk")
     for c in range(devices):
         used[c] = 0
 
     def place(j, carry):
-        where_to = partner_ref[j]
+        where_to = given_ref[j]
         owner = lax.div(where_to, count)
         offset = lax.rem(owner - me + devices, devices)
         at = offset * per + used[offset]
@@ -73,35 +67,34 @@
 
     lax.fori_loop(0, count, place, 0)
     for k in range(terms):
-        table_ref[3 * count + k] = kind_ref[k]
+        table_ref[3 * count + k] = given_ref[count + k]
     table_ref[3 * count + terms] = lax.axis_index("sub")
 
 
 def make_table(partner, term_kind, vector):
     devices = lax.axis_size("blk")
-    length = 3 * partner.shape[0] + term_kind.shape[0] + 1
+    count, terms = partner.shape[0], term_kind.shape[0]
+    given = jnp.concatenate([partner, term_kind])
     return pl.pallas_call(
-        functools.partial(table_kernel, devices),
-        out_shape=jax.ShapeDtypeStruct((length,), jnp.int32),
-        in_specs=[ANY, ANY, WHOLE],
+        functools.partial(table_kernel, devices, count, terms),
+        out_shape=jax.ShapeDtypeStruct((3 * count + terms + 1,), jnp.int32),
+        in_specs=[ANY, WHOLE],
         out_specs=SCALARS,
         scratch_shapes=[
             pltpu.SMEM((devices,), jnp.int32),
-            pltpu.SMEM(partner.shape, jnp.int32),
-            pltpu.SMEM(term_kind.shape, jnp.int32),
-            pltpu.SemaphoreType.DMA((2,)),
+            pltpu.SMEM(given.shape, jnp.int32),
+            pltpu.SemaphoreType.DMA,
         ],
         compiler_params=pltpu.CompilerParams(vmem_limit_bytes=SMALL),
         name="table",
-    )(partner, term_kind, vector)
-
-
-def sector(table, count, terms, l_ref, r_ref, own_ref, other_ref, lhs, high_rhs, low_rhs):
+    )(given, vector)
+
+
+def sector(table, count, terms, height, held, own_ref, other_ref, l_ref, r_ref, lhs, high_rhs, low_rhs):
     rows, width = l_ref.shape[2], r_ref.shape[3]
-    height = own_ref.shape[0]
     roots = height // rows
     first = table[3 * count + terms] == 0
-    own, other = own_ref[...], other_ref[...]
+    own, other = own_ref[held], other_ref[held]
     top = jnp.where(first, own, other)
     bottom = jnp.where(first, other, own)
     left = l_ref[:, 0].reshape(terms * rows, 2 * rows)
@@ -133,39 +126,54 @@
     )
 
 
-def sector_kernel(count, terms, unroll, starts, tags, table, *refs):
-    inputs, scratch = refs[: 4 * unroll], refs[-3 * unroll :]
+def sector_kernel(count, terms, unroll, height, pieces, origin, starts, tags, table, own_ref, other_ref, *refs):
+    inputs, scratch = refs[: 2 * unroll], refs[-3 * unroll :]
     outputs = refs[-3 * unroll - len(starts) : -3 * unroll]
-    tag_refs = refs[4 * unroll : 4 * unroll + 2]
     moved_refs, kept_ref = outputs[:-1], outputs[-1]
     width = kept_ref.shape[1]
-    height = kept_ref.shape[0] // unroll
     step = pl.program_id(0)
+
+    def sector_at(at):
+        return pl.ds(pl.multiple_of(at * height, height), height)
 
     @pl.when(step == 0)
     def _():
-        for at, ref in enumerate(scratch):
-            if at % 3:
-                ref[...] = jnp.zeros_like(ref)
+        for k in range(terms):
+            kind = table[3 * count + k]
+            unused = pl.ds(pl.multiple_of(kind * width, width), width)
+            for at, ref in enumerate(scratch):
+                if at % 3:
+                    ref[k * width : (k + 1) * width, unused] = jnp.zeros((width, width), ref.dtype)
         if any(tags):
-            tag = tag_refs[0][...] + tag_refs[1][...]
+            tag = own_ref[own_ref.shape[0] - TAG :] + other_ref[other_ref.shape[0] - TAG :]
             for ref, begin, end, tagged in zip(moved_refs, starts, starts[1:], tags):
                 if tagged:
                     ref[(end - begin) * height :] = tag
 
+    places = [place_of(step * unroll + u, pieces) for u in range(unroll)]
     results = [
-        sector(table, count, terms, *inputs[4 * u : 4 * u + 4], *scratch[3 * u : 3 * u + 3])
-        for u in range(unroll)
+        sector(
+            table,
+            count,
+            terms,
+            height,
+            sector_at(table[place] if origin is None else place - origin),
+            own_ref,
+            other_ref,
+            *inputs[2 * u : 2 * u + 2],
+            *scratch[3 * u : 3 * u + 3],
+        )
+        for u, place in enumerate(places)
     ]
-    for u in range(unroll):
-        kept_ref[u * height : (u + 1) * height] = results[u][:, width:]
+    for u, place in enumerate(places):
+        kept_ref[sector_at(place)] = results[u][:, width:]
     for ref, begin, end in zip(moved_refs, starts, starts[1:]):
         for u in range(unroll):
             at = step * unroll + u - begin
 
             @pl.when((at >= 0) & (at < end - begin))
             def _(ref=ref, u=u, at=at):
-                ref[pl.ds(pl.multiple_of(at * height, height), height)] = results[u][:, :width]
+                ref[sector_at(at)] = results[u][:, :width]
 
 
 def place_of(i, pieces):
@@ -184,44 +192,30 @@
         starts.append(starts[-1] + size)
     places = [base + i for base, size in pieces for i in range(size)]
 
-    def fits(unroll):
-        return len(places) % unroll == 0 and all(
-            places[i] % unroll == 0
-            and places[i : i + unroll] == list(range(places[i], places[i] + unroll))
-            for i in range(0, len(places), unroll)
-        )
-
-    unroll = next(unroll for unroll in (2, 1) if fits(unroll))
+    unroll = 2 if len(places) % 2 == 0 else 1
 
     def specs(u):
         def source(i, table):
             return table[place_of(unroll * i + u, pieces)]
 
-        def held(i, table):
-            at = source(i, table) if origin is None else place_of(unroll * i + u, pieces) - origin
-            return (at, 0)
-
         return [
             pl.BlockSpec((terms, 1, rows, width), lambda i, t: (0, source(i, t), 0, 0)),
             pl.BlockSpec((terms, 1, width, width), lambda i, t: (0, source(i, t), 0, 0)),
-            pl.BlockSpec((height, width), held),
-            pl.BlockSpec((height, width), held),
         ]
 
-    in_specs = [spec for u in range(unroll) for spec in specs(u)]
-    args = [left, right, own, other] * unroll
-    if any(tags):
-        in_specs += [pl.BlockSpec((TAG, width), lambda i, t: (own.shape[0] // TAG - 1, 0))] * 2
-        args += [own, other]
+    in_specs = [WHOLE, WHOLE] + [spec for u in range(unroll) for spec in specs(u)]
+    args = [own, other] + [left, right] * unroll
     aliases = {}
     if kept is not None:
-        in_specs.append(ANY)
+        in_specs.append(WHOLE)
         args.append(kept)
         aliases = {len(args): len(pieces)}
     deep = terms * width
     shapes = [(size * height + TAG * tagged, width) for (_, size), tagged in zip(pieces, tags)]
     out = pl.pallas_call(
-        functools.partial(sector_kernel, count, terms, unroll, starts, tags),
+        functools.partial(
+            sector_kernel, count, terms, unroll, height, pieces, origin, starts, tags
+        ),
         out_shape=[
             jax.ShapeDtypeStruct(shape, jnp.float32)
             for shape in shapes + [(count * height, width)]
@@ -230,13 +224,7 @@
             num_scalar_prefetch=1,
             grid=(starts[-1] // unroll,),
             in_specs=in_specs,
-            out_specs=[pl.BlockSpec(shape, lambda i, t: (0, 0)) for shape in shapes]
-            + [
-                pl.BlockSpec(
-                    (unroll * height, width),
-                    lambda i, t: (lax.div(place_of(unroll * i, pieces), unroll), 0),
-                )
-            ],
+            out_specs=[WHOLE] * (len(shapes) + 1),
             scratch_shapes=[
                 pltpu.VMEM((2 * height, deep), jnp.bfloat16),
                 pltpu.VMEM((deep, 2 * width), jnp.bfloat16),
@@ -252,62 +240,46 @@
     return out[:-1], out[-1]
 
 
-def combine_kernel(share, with_inner, table, kept_ref, arrived_ref, vector_ref, diag_ref, sum_ref, *refs):
-    rows = diag_ref.shape[1]
-    roots = vector_ref.shape[0] // rows
-    diag = share * diag_ref[0]
+def combine_kernel(share, piece, ordered, with_inner, table, kept_ref, arrived_ref, vector_ref, diag_ref, sum_ref, *refs):
+    count, rows, width = diag_ref.shape
+    height = kept_ref.shape[0] // count
+    roots = height // rows
+    base, size = piece
+    inner = [jnp.zeros((1, width), jnp.float32) for _ in range(2 * roots)]
+    for i in range(size):
+        slot = table[count + base + i]
+        place = table[2 * count + slot]
+        held = place if ordered else slot
+        diag = share * diag_ref[slot]
+        for r in range(roots):
+
+            def at(sector):
+                return pl.ds(pl.multiple_of(sector * height + r * rows, rows), rows)
+
+            here = slice(i * height + r * rows, i * height + (r + 1) * rows)
+            vector = vector_ref[at(held)]
+            total = kept_ref[at(place)] + arrived_ref[here] + diag * vector
+            sum_ref[here] = total
+            if with_inner:
+                inner[r] = inner[r] + jnp.sum(vector * total, axis=0, keepdims=True)
+                inner[roots + r] = inner[roots + r] + share * jnp.sum(
+                    vector * vector, axis=0, keepdims=True
+                )
     if with_inner:
-        inner_ref = refs[0]
-
-        @pl.when(pl.program_id(0) == 0)
-        def _():
-            inner_ref[...] = jnp.zeros_like(inner_ref)
-
-    for r in range(roots):
-        at = slice(r * rows, (r + 1) * rows)
-        vector = vector_ref[at]
-        total = kept_ref[at] + arrived_ref[at] + diag * vector
-        sum_ref[at] = total
-        if with_inner:
-            inner_ref[r : r + 1] += jnp.sum(vector * total, axis=0, keepdims=True)
-            inner_ref[roots + r : roots + r + 1] += share * jnp.sum(
-                vector * vector, axis=0, keepdims=True
-            )
+        rest = jnp.zeros((TAG - 2 * roots, width), jnp.float32)
+        refs[0][...] = jnp.concatenate(inner + [rest], axis=0)
 
 
 def combine(table, piece, kept, arrived, vector, diag, share, ordered, with_inner):
-    count, rows, width = diag.shape
-    base, size = piece
-    block = (kept.shape[0] // count, width)
-
-    def slot(i, table):
-        return table[count + base + i]
-
-    def place(i, table):
-        return table[2 * count + slot(i, table)]
-
-    def held(i, table):
-        return (place(i, table) if ordered else slot(i, table), 0)
-
-    out_shape = [jax.ShapeDtypeStruct((size * block[0], width), jnp.float32)]
-    out_specs = [pl.BlockSpec(block, lambda i, t: (i, 0))]
+    height, width = kept.shape[0] // diag.shape[0], kept.shape[1]
+    out_shape = [jax.ShapeDtypeStruct((piece[1] * height, width), jnp.float32)]
     if with_inner:
         out_shape.append(jax.ShapeDtypeStruct((TAG, width), jnp.float32))
-        out_specs.append(pl.BlockSpec((TAG, width), lambda i, t: (0, 0)))
     out = pl.pallas_call(
-        functools.partial(combine_kernel, share, with_inner),
+        functools.partial(combine_kernel, share, piece, ordered, with_inner),
         out_shape=out_shape,
-        grid_spec=pltpu.PrefetchScalarGridSpec(
-            num_scalar_prefetch=1,
-            grid=(size,),
-            in_specs=[
-                pl.BlockSpec(block, lambda i, t: (place(i, t), 0)),
-                pl.BlockSpec(block, lambda i, t: (i, 0)),
-                pl.BlockSpec(block, held),
-                pl.BlockSpec((1, rows, width), lambda i, t: (slot(i, t), 0, 0)),
-            ],
-            out_specs=out_specs,
-        ),
+        in_specs=[SCALARS] + [WHOLE] * 4,
+        out_specs=[WHOLE] * len(out_shape),
         compiler_params=pltpu.CompilerParams(vmem_limit_bytes=SMALL),
         cost_estimate=FREE,
         name="combine",

time: 131 us -> 130 us (level)
  starting transfers between devices: 41.1 us -> 42.7 us
  Pallas kernels: 52.4 us -> 51 us
  local copies, waits for them, and re-layouts: 2.81 us -> 1.5 us
    ppermute x21, waiting for transfers between devices: 25.8 us -> 23.2 us  [flip(): return lax.ppermute(value, axis, [(i, i ^ bit) for i in range(size)])]
    ppermute x12, waiting for transfers between devices: 5.52 us -> 7.31 us  [relay(): lax.ppermute(value, 'blk', [(p, (p + c) % devices) for p in range(devices)])]
    ppermute x21, starting transfers between devices: 21.9 us -> 23.4 us  [flip(): return lax.ppermute(value, axis, [(i, i ^ bit) for i in range(size)])]
    pallas_call x21, Pallas kernels: 46.4 us -> 44.9 us  [the longest x4 33.8 us: sectors(): pl.pallas_call(functools.partial(sector_kernel, count, terms, unroll, hei...]
    unnamed x12 -> x8, local copies, waits for them, and re-layouts: 2.73 us -> 1.42 us
  transfers between devices with their start and end apart: 36 -> 36, of which waited for: 21 -> 20; matrix products, arithmetic and copies ran while one was open for 0% -> 1% of each run, Pallas kernels for 34% -> 33%
where the time goes in v12:
time: 130 us; the launch traced here: 129 us
  Pallas kernels  51 us (39%)
  starting transfers between devices  42.7 us (33%)
  waiting for transfers between devices  32.2 us (25%)
  local copies, waits for them, and re-layouts  1.5 us (1%)
    pallas_call x4, Pallas kernels, sectors(): pl.pallas_call(functools.partial(sector_kernel, count, terms, unroll, hei...  33.8 us
    ppermute x21, starting transfers between devices, flip(): return lax.ppermute(value, axis, [(i, i ^ bit) for i in range(size)])  23.4 us
    ppermute x21, waiting for transfers between devices, flip(): return lax.ppermute(value, axis, [(i, i ^ bit) for i in range(size)])  23.2 us
    ppermute x12, starting transfers between devices, relay(): lax.ppermute(value, 'blk', [(p, (p + c) % devices) for p in range(devices)])  18.5 us
    pallas_call x16, Pallas kernels, combine(): pl.pallas_call(functools.partial(combine_kernel, share, piece, ordered, w...  9.64 us
    ppermute x12, waiting for transfers between devices, relay(): lax.ppermute(value, 'blk', [(p, (p + c) % devices) for p in range(devices)])  7.31 us
    pallas_call x2, Pallas kernels, finish(): pl.pallas_call(functools.partial(finish_kernel, count, rows, [size for _,...  2.99 us
  transfers between devices with their start and end apart: 36, of which 20 were waited for; matrix products, arithmetic and copies ran while one was open for 1% of the time, Pallas kernels for 33%

profile of v12, /device:TPU:0, one launch (start us, length us, event | category | flops | bytes accessed | tf_op | source)
XLA Modules:
  0.0 129.4 jit_solution(12931427529827480782)
XLA Ops:
  1.9 1.4 %copy-done = f32[16,64,3,128]{3,1,2,0:T(8,128)S(1)} copy-done((f32[16,64,3,128]{3,1,2,0:T(8,128)S(1)}, f32[16,64,3,128]{3,1,2,0:T(8,128)}, u32[]{:S(2)}) %copy-start) | copy-done | bytes 1572888
  3.3 1.5 %table.1 = s32[57]{0:T(128)S(1)} custom-call(s32[24]{0:T(128)S(1)} %pad_add_fusion.given_hbm, f32[3072,128]{1,0:T(8,128)S(1)} %bitcast.10), custom_call_target="tpu_custom_call" | custom-call | tf_op jit(solution)/shard_map/table/pallas_call | solution.py:78
  4.8 5.2 %sectors.4 = (f32[384,128]{1,0:T(8,128)S(1)}, f32[384,128]{1,0:T(8,128)S(1)}, f32[3072,128]{1,0:T(8,128)S(1)}) custom-call(s32[57]{0:T(128)S(1)} %table.1, f32[3072,128]{1,0:T(8,128)S(1)} %bitcast.11, f32[3072,128]{1,0:T(8,128)S(1)} %collective-permute-done.other_ref, f32[8,16,64,128]{3,2,1,0:T(8,128)} %refs_2_.7, f32[8,16,128,128]{3,2,1,0:T(8,128)} %refs_3_.7, ...), custom_call_target="tpu_custom_call" | custom-call | tf_op jit(solution)/shard_map/sectors/pallas_call | solution.py:215
  10.0 3.7 %collective-permute-start.2 = (f32[384,128]{1,0:T(8,128)S(1)}, f32[384,128]{1,0:T(8,128)S(1)}, u32[]{:S(2)}, u32[]{:S(2)}) collective-permute-start(f32[384,128]{1,0:T(8,128)S(1)} %get-tuple-element.70), channel_id=1, source_target_pairs={{0,8},{4,12},{8,0},{12,4},{1,9},{5,13},{9,1},{13,5},{2,10},{6,14},... | collective-permute-start | bytes 589832 | tf_op jit(solution)/shard_map/ppermute | solution.py:463
  14.0 11.6 %sectors.5 = (f32[384,128]{1,0:T(8,128)S(1)}, f32[384,128]{1,0:T(8,128)S(1)}, f32[384,128]{1,0:T(8,128)S(1)}, f32[384,128]{1,0:T(8,128)S(1)}, f32[384,128]{1,0:T...) custom-call(s32[57]{0:T(128)S(1)} %table.1, ...), custom_call_target="tpu_custom_call", output_to_operand_aliasing={{6}: (7, {})} | custom-call | tf_op jit(solution)/shard_map/sectors/pallas_call | solution.py:215
  26.2 1.8 %collective-permute-start.11 = (f32[384,128]{1,0:T(8,128)S(1)}, f32[384,128]{1,0:T(8,128)S(1)}, u32[]{:S(2)}, u32[]{:S(2)}) collective-permute-start(f32[384,128]{1,0:T(8,128)S(1)} %get-tuple-element.87.rest_2_), channel_id=1, source_target_pairs={{0,2},{2,0},{1,3},{3,1},{4,6},{6,4},{5,7},{7,5},{8,10},{10,8},{9,1... | collective-permute-start | bytes 589832 | tf_op jit(solution)/shard_map/ppermute | solution.py:25
  29.0 1.8 %collective-permute-start.4 = (f32[384,128]{1,0:T(8,128)S(1)}, f32[384,128]{1,0:T(8,128)S(1)}, u32[]{:S(2)}, u32[]{:S(2)}) collective-permute-start(f32[384,128]{1,0:T(8,128)S(1)} %get-tuple-element.76), channel_id=1, source_target_pairs={{0,4},{4,8},{8,12},{12,0},{1,5},{5,9},{9,13},{13,1},{2,6},{6,10},{... | collective-permute-start | bytes 589832 | tf_op jit(solution)/shard_map/ppermute | solution.py:463
  30.8 1.0 collective-permute-done.1.arrived_ref
  34.0 1.8 %collective-permute-start.12 = (f32[384,128]{1,0:T(8,128)S(1)}, f32[384,128]{1,0:T(8,128)S(1)}, u32[]{:S(2)}, u32[]{:S(2)}) collective-permute-start(f32[384,128]{1,0:T(8,128)S(1)} %get-tuple-element.88.rest_6_), channel_id=1, source_target_pairs={{0,2},{2,0},{1,3},{3,1},{4,6},{6,4},{5,7},{7,5},{8,10},{10,8},{9,1... | collective-permute-start | bytes 589832 | tf_op jit(solution)/shard_map/ppermute | solution.py:25
  36.4 1.8 %collective-permute-done.16.rest_1_ = f32[384,128]{1,0:T(8,128)S(1)} collective-permute-done((f32[384,128]{1,0:T(8,128)S(1)}, f32[384,128]{1,0:T(8,128)S(1)}, u32[]{:S(2)}, u32[]{:S(2)}) %collective-permute-start.16) | collective-permute-done | bytes 196640 | tf_op jit(solution)/shard_map/ppermute | solution.py:25
  38.2 1.8 %collective-permute-start.17 = (f32[384,128]{1,0:T(8,128)S(1)}, f32[384,128]{1,0:T(8,128)S(1)}, u32[]{:S(2)}, u32[]{:S(2)}) collective-permute-start(f32[384,128]{1,0:T(8,128)S(1)} %get-tuple-element.94.rest_4_), channel_id=1, source_target_pairs={{0,2},{2,0},{1,3},{3,1},{4,6},{6,4},{5,7},{7,5},{8,10},{10,8},{9,1... | collective-permute-start | bytes 589832 | tf_op jit(solution)/shard_map/ppermute | solution.py:25
  40.0 3.6 %collective-permute-start.6 = (f32[384,128]{1,0:T(8,128)S(1)}, f32[384,128]{1,0:T(8,128)S(1)}, u32[]{:S(2)}, u32[]{:S(2)}) collective-permute-start(f32[384,128]{1,0:T(8,128)S(1)} %get-tuple-element.82), channel_id=1, source_target_pairs={{0,12},{4,0},{8,4},{12,8},{1,13},{5,1},{9,5},{13,9},{2,14},{6,2},{... | collective-permute-start | bytes 589832 | tf_op jit(solution)/shard_map/ppermute | solution.py:463
  44.6 1.4 %collective-permute-start.13 = (f32[384,128]{1,0:T(8,128)S(1)}, f32[384,128]{1,0:T(8,128)S(1)}, u32[]{:S(2)}, u32[]{:S(2)}) collective-permute-start(f32[384,128]{1,0:T(8,128)S(1)} %get-tuple-element.89.rest_10_), channel_id=1, source_target_pairs={{0,2},{2,0},{1,3},{3,1},{4,6},{6,4},{5,7},{7,5},{8,10},{10,8},{9,1... | collective-permute-start | bytes 589832 | tf_op jit(solution)/shard_map/ppermute | solution.py:25
  48.4 1.5 %collective-permute-done.5.arrived_ref = f32[384,128]{1,0:T(8,128)S(1)} collective-permute-done((f32[384,128]{1,0:T(8,128)S(1)}, f32[384,128]{1,0:T(8,128)S(1)}, u32[]{:S(2)}, u32[]{:S(2)}) %collective-permute-start.5) | collective-permute-done | bytes 196640 | tf_op jit(solution)/shard_map/ppermute | solution.py:463
  50.7 1.2 collective-permute-done.7
  51.8 1.6 %collective-permute-start.9 = (f32[8,128]{1,0:T(8,128)S(1)}, f32[8,128]{1,0:T(8,128)S(1)}, u32[]{:S(2)}, u32[]{:S(2)}) collective-permute-start(f32[8,128]{1,0:T(8,128)S(1)} %add.79), channel_id=1, source_target_pairs={{0,8},{4,12},{8,0},{12,4},{1,9},{5,13},{9,1},{13,5},{2,10},{6,14},... | collective-permute-start | bytes 12296 | tf_op jit(solution)/shard_map/ppermute | solution.py:25
  53.4 2.6 %collective-permute-start.10 = (f32[8,128]{1,0:T(8,128)S(1)}, f32[8,128]{1,0:T(8,128)S(1)}, u32[]{:S(2)}, u32[]{:S(2)}) collective-permute-start(f32[8,128]{1,0:T(8,128)S(1)} %add.79), channel_id=1, source_target_pairs={{0,12},{4,8},{8,4},{12,0},{1,13},{5,9},{9,5},{13,1},{2,14},{6,10},... | collective-permute-start | bytes 12296 | tf_op jit(solution)/shard_map/ppermute | solution.py:25
  56.6 0.9 collective-permute-start.14
  57.5 1.1 collective-permute-start.19
  59.7 4.8 %collective-permute-done.14.rest_15_ = f32[384,128]{1,0:T(8,128)S(1)} collective-permute-done((f32[384,128]{1,0:T(8,128)S(1)}, f32[384,128]{1,0:T(8,128)S(1)}, u32[]{:S(2)}, u32[]{:S(2)}) %collective-permute-start.14) | collective-permute-done | bytes 196640 | tf_op jit(solution)/shard_map/ppermute | solution.py:25
  64.4 0.9 collective-permute-start.15
  65.3 2.7 %collective-permute-done.15 = f32[8,128]{1,0:T(8,128)S(1)} collective-permute-done((f32[8,128]{1,0:T(8,128)S(1)}, f32[8,128]{1,0:T(8,128)S(1)}, u32[]{:S(2)}, u32[]{:S(2)}) %collective-permute-start.15) | collective-permute-done | bytes 4128 | tf_op jit(solution)/shard_map/ppermute | solution.py:25
  68.1 1.3 correct.1
  69.4 1.7 %collective-permute-done.20.other_ref = f32[776,128]{1,0:T(8,128)S(1)} collective-permute-done((f32[776,128]{1,0:T(8,128)S(1)}, f32[776,128]{1,0:T(8,128)S(1)}, u32[]{:S(2)}, u32[]{:S(2)}) %collective-permute-start.20) | collective-permute-done | bytes 397344 | tf_op jit(solution)/shard_map/ppermute | solution.py:466
  71.3 5.3 %sectors.6 = (f32[392,128]{1,0:T(8,128)S(1)}, f32[392,128]{1,0:T(8,128)S(1)}, f32[3072,128]{1,0:T(8,128)S(1)}) custom-call(s32[57]{0:T(128)S(1)} %table.1, f32[776,128]{1,0:T(8,128)S(1)} %get-tuple-element.100.own_ref, f32[776,128]{1,0:T(8,128)S(1)} %collective-permute-done.20.other_ref, f32[8,16,64,128]{3,2,1,0:T(8,128)} %refs_2_.7, ...), custom_call_target="tpu_custom_call" | custom-call | tf_op jit(solution)/shard_map/sectors/pallas_call | solution.py:215
  76.5 1.5 %collective-permute-start.22 = (f32[392,128]{1,0:T(8,128)S(1)}, f32[392,128]{1,0:T(8,128)S(1)}, u32[]{:S(2)}, u32[]{:S(2)}) collective-permute-start(f32[392,128]{1,0:T(8,128)S(1)} %get-tuple-element.102), channel_id=1, source_target_pairs={{0,8},{4,12},{8,0},{12,4},{1,9},{5,13},{9,1},{13,5},{2,10},{6,14},... | collective-permute-start | bytes 602120 | tf_op jit(solution)/shard_map/ppermute | solution.py:463
  78.1 1.5 %collective-permute-start.29 = (f32[392,128]{1,0:T(8,128)S(1)}, f32[392,128]{1,0:T(8,128)S(1)}, u32[]{:S(2)}, u32[]{:S(2)}) collective-permute-start(f32[392,128]{1,0:T(8,128)S(1)} %get-tuple-element.115), channel_id=1, source_target_pairs={{0,8},{4,12},{8,0},{12,4},{1,9},{5,13},{9,1},{13,5},{2,10},{6,14},... | collective-permute-start | bytes 602120 | tf_op jit(solution)/shard_map/ppermute | solution.py:463
  79.5 11.8 %sectors.7 = (f32[392,128]{1,0:T(8,128)S(1)}, f32[392,128]{1,0:T(8,128)S(1)}, f32[392,128]{1,0:T(8,128)S(1)}, f32[392,128]{1,0:T(8,128)S(1)}, f32[384,128]{1,0:T...) custom-call(s32[57]{0:T(128)S(1)} %table.1, ...), custom_call_target="tpu_custom_call", output_to_operand_aliasing={{6}: (7, {})} | custom-call | tf_op jit(solution)/shard_map/sectors/pallas_call | solution.py:215
  91.9 1.0 collective-permute-start.25
  93.4 1.2 collective-permute-start.32
  94.6 1.5 %collective-permute-start.23 = (f32[392,128]{1,0:T(8,128)S(1)}, f32[392,128]{1,0:T(8,128)S(1)}, u32[]{:S(2)}, u32[]{:S(2)}) collective-permute-start(f32[392,128]{1,0:T(8,128)S(1)} %get-tuple-element.105), channel_id=1, source_target_pairs={{0,4},{4,8},{8,12},{12,0},{1,5},{5,9},{9,13},{13,1},{2,6},{6,10},{... | collective-permute-start | bytes 602120 | tf_op jit(solution)/shard_map/ppermute | solution.py:463
  96.1 1.6 %collective-permute-done.29.arrived_ref = f32[392,128]{1,0:T(8,128)S(1)} collective-permute-done((f32[392,128]{1,0:T(8,128)S(1)}, f32[392,128]{1,0:T(8,128)S(1)}, u32[]{:S(2)}, u32[]{:S(2)}) %collective-permute-start.29) | collective-permute-done | bytes 200736 | tf_op jit(solution)/shard_map/ppermute | solution.py:463
  98.8 0.9 collective-permute-done.25.refs_1_
  100.6 3.3 %collective-permute-done.32.refs_3_ = f32[384,128]{1,0:T(8,128)S(1)} collective-permute-done((f32[384,128]{1,0:T(8,128)S(1)}, f32[384,128]{1,0:T(8,128)S(1)}, u32[]{:S(2)}, u32[]{:S(2)}) %collective-permute-start.32) | collective-permute-done | bytes 196640 | tf_op jit(solution)/shard_map/ppermute | solution.py:25
  103.9 0.9 collective-permute-start.33
  104.8 2.8 %collective-permute-start.24 = (f32[392,128]{1,0:T(8,128)S(1)}, f32[392,128]{1,0:T(8,128)S(1)}, u32[]{:S(2)}, u32[]{:S(2)}) collective-permute-start(f32[392,128]{1,0:T(8,128)S(1)} %get-tuple-element.107), channel_id=1, source_target_pairs={{0,12},{4,0},{8,4},{12,8},{1,13},{5,1},{9,5},{13,9},{2,14},{6,2},{... | collective-permute-start | bytes 602120 | tf_op jit(solution)/shard_map/ppermute | solution.py:463
  107.6 1.0 collective-permute-start.31
  109.8 1.0 collective-permute-start.27
  111.2 0.9 collective-permute-start.34
  113.4 2.1 %collective-permute-done.31.arrived_ref = f32[392,128]{1,0:T(8,128)S(1)} collective-permute-done((f32[392,128]{1,0:T(8,128)S(1)}, f32[392,128]{1,0:T(8,128)S(1)}, u32[]{:S(2)}, u32[]{:S(2)}) %collective-permute-start.31) | collective-permute-done | bytes 200736 | tf_op jit(solution)/shard_map/ppermute | solution.py:463
  116.2 1.5 %collective-permute-done.27.refs_9_ = f32[384,128]{1,0:T(8,128)S(1)} collective-permute-done((f32[384,128]{1,0:T(8,128)S(1)}, f32[384,128]{1,0:T(8,128)S(1)}, u32[]{:S(2)}, u32[]{:S(2)}) %collective-permute-start.27) | collective-permute-done | bytes 196640 | tf_op jit(solution)/shard_map/ppermute | solution.py:25
  117.6 1.0 collective-permute-start.28
  118.6 3.2 %collective-permute-done.34.refs_11_ = f32[384,128]{1,0:T(8,128)S(1)} collective-permute-done((f32[384,128]{1,0:T(8,128)S(1)}, f32[384,128]{1,0:T(8,128)S(1)}, u32[]{:S(2)}, u32[]{:S(2)}) %collective-permute-start.34) | collective-permute-done | bytes 196640 | tf_op jit(solution)/shard_map/ppermute | solution.py:25
  121.8 1.0 collective-permute-start.35
  122.9 1.8 %scaled.1 = f32[3072,128]{1,0:T(8,128)} custom-call(s32[57]{0:T(128)S(1)} %table.1, f32[8,128]{1,0:T(8,128)S(1)} %broadcast_in_dim.2.scale_ref, f32[3080,128]{1,0:T(8,128)S(1)} %get-tuple-element.101.own_ref.vector_ref.raw_ref), custom_call_target="tpu_custom_call" | custom-call | tf_op jit(solution)/shard_map/scaled/pallas_call | solution.py:369
  124.7 1.7 %finish.2.refs_4_ = f32[3072,128]{1,0:T(8,128)} custom-call(s32[57]{0:T(128)S(1)} %table.1, f32[8,128]{1,0:T(8,128)S(1)} %broadcast_in_dim.2.scale_ref, f32[384,128]{1,0:T(8,128)S(1)} %combine.27.refs_0_, f32[384,128]{1,0:T(8,128)S(1)} %collective-permute-done.25.refs_1_, f32[384,128]{1,0:T(8,128)S(1)} %combine.31.refs_2_, ...), custom_call_target="tpu_custom_call" | custom-call | tf_op jit(solution)/shard_map/finish/pallas_call | solution.py:410
  126.4 1.6 %collective-permute-done.35.refs_3_ = f32[384,128]{1,0:T(8,128)S(1)} collective-permute-done((f32[384,128]{1,0:T(8,128)S(1)}, f32[384,128]{1,0:T(8,128)S(1)}, u32[]{:S(2)}, u32[]{:S(2)}) %collective-permute-start.35) | collective-permute-done | bytes 196640 | tf_op jit(solution)/shard_map/ppermute | solution.py:25
  128.0 1.3 %finish.3 = f32[3072,128]{1,0:T(8,128)} custom-call(s32[57]{0:T(128)S(1)} %table.1, f32[8,128]{1,0:T(8,128)S(1)} %broadcast_in_dim.2.scale_ref, f32[384,128]{1,0:T(8,128)S(1)} %combine.24.refs_0_, f32[384,128]{1,0:T(8,128)S(1)} %collective-permute-done.28.refs_1_, f32[384,128]{1,0:T(8,128)S(1)} %combine.28.refs_2_, ...), custom_call_target="tpu_custom_call", output_to_operand_aliasing={{}: (6, {})} | custom-call | tf_op jit(solution)/shard_map/finish/pallas_call | solution.py:410
  (66 shorter events, 18.7 us)
Async XLA Ops:
  0.6 4.2 %collective-permute-start = (f32[3072,128]{1,0:T(8,128)}, f32[3072,128]{1,0:T(8,128)S(1)}, u32[]{:S(2)}, u32[]{:S(2)}) collective-permute-start(f32[3072,128]{1,0:T(8,128)} %bitcast.9), channel_id=1, source_target_pairs={{0,1},{1,0},{2,3},{3,2},{4,5},{5,4},{6,7},{7,6},{8,9},{9,8},{10,11... | collective-permute-start | bytes 4718600 | tf_op jit(solution)/shard_map/ppermute | solution.py:466
  1.9 1.4 %copy-start = (f32[16,64,3,128]{3,1,2,0:T(8,128)S(1)}, f32[16,64,3,128]{3,1,2,0:T(8,128)}, u32[]{:S(2)}) copy-start(f32[16,64,3,128]{3,1,2,0:T(8,128)} %param.7) | copy-start | bytes 4718596
  3.3 1.5 %copy-start.1 = (f32[16,64,3,128]{3,1,2,0:T(8,128)S(1)}, f32[16,64,3,128]{3,1,2,0:T(8,128)}, u32[]{:S(2)}) copy-start(f32[16,64,3,128]{3,1,2,0:T(8,128)} %param.7) | copy-start | bytes 4718596
  4.8 9.0 %copy-start.2 = (f32[16,128]{1,0:T(8,128)S(1)}, f32[16,128]{1,0:T(8,128)}, u32[]{:S(2)}) copy-start(f32[16,128]{1,0:T(8,128)} %param.13) | copy-start | bytes 24580
  4.8 9.0 %copy-start.3 = (f32[16,64]{1,0:T(8,128)S(1)}, f32[16,64]{1,0:T(8,128)}, u32[]{:S(2)}) copy-start(f32[16,64]{1,0:T(8,128)} %param.12) | copy-start | bytes 12292
  10.0 19.0 %collective-permute-start.2 = (f32[384,128]{1,0:T(8,128)S(1)}, f32[384,128]{1,0:T(8,128)S(1)}, u32[]{:S(2)}, u32[]{:S(2)}) collective-permute-start(f32[384,128]{1,0:T(8,128)S(1)} %get-tuple-element.70), channel_id=1, source_target_pairs={{0,8},{4,12},{8,0},{12,4},{1,9},{5,13},{9,1},{13,5},{2,10},{6,14},... | collective-permute-start | bytes 589832 | tf_op jit(solution)/shard_map/ppermute | solution.py:463
  13.7 18.2 %collective-permute-start.1 = (f32[384,128]{1,0:T(8,128)S(1)}, f32[384,128]{1,0:T(8,128)S(1)}, u32[]{:S(2)}, u32[]{:S(2)}) collective-permute-start(f32[384,128]{1,0:T(8,128)S(1)} %get-tuple-element.68), channel_id=1, source_target_pairs={{0,8},{4,12},{8,0},{12,4},{1,9},{5,13},{9,1},{13,5},{2,10},{6,14},... | collective-permute-start | bytes 589832 | tf_op jit(solution)/shard_map/ppermute | solution.py:463
  26.2 7.8 %collective-permute-start.11 = (f32[384,128]{1,0:T(8,128)S(1)}, f32[384,128]{1,0:T(8,128)S(1)}, u32[]{:S(2)}, u32[]{:S(2)}) collective-permute-start(f32[384,128]{1,0:T(8,128)S(1)} %get-tuple-element.87.rest_2_), channel_id=1, source_target_pairs={{0,2},{2,0},{1,3},{3,1},{4,6},{6,4},{5,7},{7,5},{8,10},{10,8},{9,1... | collective-permute-start | bytes 589832 | tf_op jit(solution)/shard_map/ppermute | solution.py:25
  28.6 9.6 %collective-permute-start.16 = (f32[384,128]{1,0:T(8,128)S(1)}, f32[384,128]{1,0:T(8,128)S(1)}, u32[]{:S(2)}, u32[]{:S(2)}) collective-permute-start(f32[384,128]{1,0:T(8,128)S(1)} %get-tuple-element.92.rest_0_), channel_id=1, source_target_pairs={{0,2},{2,0},{1,3},{3,1},{4,6},{6,4},{5,7},{7,5},{8,10},{10,8},{9,1... | collective-permute-start | bytes 589832 | tf_op jit(solution)/shard_map/ppermute | solution.py:25
  29.0 11.0 %collective-permute-start.4 = (f32[384,128]{1,0:T(8,128)S(1)}, f32[384,128]{1,0:T(8,128)S(1)}, u32[]{:S(2)}, u32[]{:S(2)}) collective-permute-start(f32[384,128]{1,0:T(8,128)S(1)} %get-tuple-element.76), channel_id=1, source_target_pairs={{0,4},{4,8},{8,12},{12,0},{1,5},{5,9},{9,13},{13,1},{2,6},{6,10},{... | collective-permute-start | bytes 589832 | tf_op jit(solution)/shard_map/ppermute | solution.py:463
  31.9 11.8 %collective-permute-start.3 = (f32[384,128]{1,0:T(8,128)S(1)}, f32[384,128]{1,0:T(8,128)S(1)}, u32[]{:S(2)}, u32[]{:S(2)}) collective-permute-start(f32[384,128]{1,0:T(8,128)S(1)} %get-tuple-element.73), channel_id=1, source_target_pairs={{0,4},{4,8},{8,12},{12,0},{1,5},{5,9},{9,13},{13,1},{2,6},{6,10},{... | collective-permute-start | bytes 589832 | tf_op jit(solution)/shard_map/ppermute | solution.py:463
  34.0 10.6 %collective-permute-start.12 = (f32[384,128]{1,0:T(8,128)S(1)}, f32[384,128]{1,0:T(8,128)S(1)}, u32[]{:S(2)}, u32[]{:S(2)}) collective-permute-start(f32[384,128]{1,0:T(8,128)S(1)} %get-tuple-element.88.rest_6_), channel_id=1, source_target_pairs={{0,2},{2,0},{1,3},{3,1},{4,6},{6,4},{5,7},{7,5},{8,10},{10,8},{9,1... | collective-permute-start | bytes 589832 | tf_op jit(solution)/shard_map/ppermute | solution.py:25
  38.2 8.4 %collective-permute-start.17 = (f32[384,128]{1,0:T(8,128)S(1)}, f32[384,128]{1,0:T(8,128)S(1)}, u32[]{:S(2)}, u32[]{:S(2)}) collective-permute-start(f32[384,128]{1,0:T(8,128)S(1)} %get-tuple-element.94.rest_4_), channel_id=1, source_target_pairs={{0,2},{2,0},{1,3},{3,1},{4,6},{6,4},{5,7},{7,5},{8,10},{10,8},{9,1... | collective-permute-start | bytes 589832 | tf_op jit(solution)/shard_map/ppermute | solution.py:25
  40.0 7.8 %collective-permute-start.6 = (f32[384,128]{1,0:T(8,128)S(1)}, f32[384,128]{1,0:T(8,128)S(1)}, u32[]{:S(2)}, u32[]{:S(2)}) collective-permute-start(f32[384,128]{1,0:T(8,128)S(1)} %get-tuple-element.82), channel_id=1, source_target_pairs={{0,12},{4,0},{8,4},{12,8},{1,13},{5,1},{9,5},{13,9},{2,14},{6,2},{... | collective-permute-start | bytes 589832 | tf_op jit(solution)/shard_map/ppermute | solution.py:463
  43.6 6.3 %collective-permute-start.5 = (f32[384,128]{1,0:T(8,128)S(1)}, f32[384,128]{1,0:T(8,128)S(1)}, u32[]{:S(2)}, u32[]{:S(2)}) collective-permute-start(f32[384,128]{1,0:T(8,128)S(1)} %get-tuple-element.79), channel_id=1, source_target_pairs={{0,12},{4,0},{8,4},{12,8},{1,13},{5,1},{9,5},{13,9},{2,14},{6,2},{... | collective-permute-start | bytes 589832 | tf_op jit(solution)/shard_map/ppermute | solution.py:463
  44.6 12.0 %collective-permute-start.13 = (f32[384,128]{1,0:T(8,128)S(1)}, f32[384,128]{1,0:T(8,128)S(1)}, u32[]{:S(2)}, u32[]{:S(2)}) collective-permute-start(f32[384,128]{1,0:T(8,128)S(1)} %get-tuple-element.89.rest_10_), channel_id=1, source_target_pairs={{0,2},{2,0},{1,3},{3,1},{4,6},{6,4},{5,7},{7,5},{8,10},{10,8},{9,1... | collective-permute-start | bytes 589832 | tf_op jit(solution)/shard_map/ppermute | solution.py:25
  46.6 10.9 %collective-permute-start.18 = (f32[384,128]{1,0:T(8,128)S(1)}, f32[384,128]{1,0:T(8,128)S(1)}, u32[]{:S(2)}, u32[]{:S(2)}) collective-permute-start(f32[384,128]{1,0:T(8,128)S(1)} %get-tuple-element.96.rest_8_), channel_id=1, source_target_pairs={{0,2},{2,0},{1,3},{3,1},{4,6},{6,4},{5,7},{7,5},{8,10},{10,8},{9,1... | collective-permute-start | bytes 589832 | tf_op jit(solution)/shard_map/ppermute | solution.py:25
  50.6 1.2 collective-permute-start.7
  51.8 6.8 %collective-permute-start.9 = (f32[8,128]{1,0:T(8,128)S(1)}, f32[8,128]{1,0:T(8,128)S(1)}, u32[]{:S(2)}, u32[]{:S(2)}) collective-permute-start(f32[8,128]{1,0:T(8,128)S(1)} %add.79), channel_id=1, source_target_pairs={{0,8},{4,12},{8,0},{12,4},{1,9},{5,13},{9,1},{13,5},{2,10},{6,14},... | collective-permute-start | bytes 12296 | tf_op jit(solution)/shard_map/ppermute | solution.py:25
  53.4 5.4 %collective-permute-start.10 = (f32[8,128]{1,0:T(8,128)S(1)}, f32[8,128]{1,0:T(8,128)S(1)}, u32[]{:S(2)}, u32[]{:S(2)}) collective-permute-start(f32[8,128]{1,0:T(8,128)S(1)} %add.79), channel_id=1, source_target_pairs={{0,12},{4,8},{8,4},{12,0},{1,13},{5,9},{9,5},{13,1},{2,14},{6,10},... | collective-permute-start | bytes 12296 | tf_op jit(solution)/shard_map/ppermute | solution.py:25
  56.0 3.6 %collective-permute-start.8 = (f32[8,128]{1,0:T(8,128)S(1)}, f32[8,128]{1,0:T(8,128)S(1)}, u32[]{:S(2)}, u32[]{:S(2)}) collective-permute-start(f32[8,128]{1,0:T(8,128)S(1)} %add.79), channel_id=1, source_target_pairs={{0,4},{4,0},{8,12},{12,8},{1,5},{5,1},{9,13},{13,9},{2,6},{6,2},{1... | collective-permute-start | bytes 12296 | tf_op jit(solution)/shard_map/ppermute | solution.py:25
  56.6 7.8 %collective-permute-start.14 = (f32[384,128]{1,0:T(8,128)S(1)}, f32[384,128]{1,0:T(8,128)S(1)}, u32[]{:S(2)}, u32[]{:S(2)}) collective-permute-start(f32[384,128]{1,0:T(8,128)S(1)} %get-tuple-element.90.rest_14_), channel_id=1, source_target_pairs={{0,2},{2,0},{1,3},{3,1},{4,6},{6,4},{5,7},{7,5},{8,10},{10,8},{9,1... | collective-permute-start | bytes 589832 | tf_op jit(solution)/shard_map/ppermute | solution.py:25
  57.5 10.5 %collective-permute-start.19 = (f32[384,128]{1,0:T(8,128)S(1)}, f32[384,128]{1,0:T(8,128)S(1)}, u32[]{:S(2)}, u32[]{:S(2)}) collective-permute-start(f32[384,128]{1,0:T(8,128)S(1)} %get-tuple-element.98.rest_12_), channel_id=1, source_target_pairs={{0,2},{2,0},{1,3},{3,1},{4,6},{6,4},{5,7},{7,5},{8,10},{10,8},{9,1... | collective-permute-start | bytes 589832 | tf_op jit(solution)/shard_map/ppermute | solution.py:25
  64.4 3.6 %collective-permute-start.15 = (f32[8,128]{1,0:T(8,128)S(1)}, f32[8,128]{1,0:T(8,128)S(1)}, u32[]{:S(2)}, u32[]{:S(2)}) collective-permute-start(f32[8,128]{1,0:T(8,128)S(1)} %add_add_fusion), channel_id=1, source_target_pairs={{0,2},{2,0},{1,3},{3,1},{4,6},{6,4},{5,7},{7,5},{8,10},{10,8},{9,1... | collective-permute-start | bytes 12296 | tf_op jit(solution)/shard_map/ppermute | solution.py:25
  69.3 1.8 %collective-permute-start.20 = (f32[776,128]{1,0:T(8,128)S(1)}, f32[776,128]{1,0:T(8,128)S(1)}, u32[]{:S(2)}, u32[]{:S(2)}) collective-permute-start(f32[776,128]{1,0:T(8,128)S(1)} %get-tuple-element.100.own_ref), channel_id=1, source_target_pairs={{0,1},{1,0},{2,3},{3,2},{4,5},{5,4},{6,7},{7,6},{8,9},{9,8},{10,11... | collective-permute-start | bytes 1191944 | tf_op jit(solution)/shard_map/ppermute | solution.py:466
  71.1 8.4 %collective-permute-start.21 = (f32[3080,128]{1,0:T(8,128)S(1)}, f32[3080,128]{1,0:T(8,128)S(1)}, u32[]{:S(2)}, u32[]{:S(2)}) collective-permute-start(f32[3080,128]{1,0:T(8,128)S(1)} %get-tuple-element.101.own_ref.vector_ref.raw_ref), channel_id=1, source_target_pairs={{0,1},{1,0},{2,3},{3,2},{4,5},{5,4},{6,7},{7,6},{8,9},{9,8},{10,11... | collective-permute-start | bytes 4730888 | tf_op jit(solution)/shard_map/ppermute | solution.py:466
  76.5 18.1 %collective-permute-start.22 = (f32[392,128]{1,0:T(8,128)S(1)}, f32[392,128]{1,0:T(8,128)S(1)}, u32[]{:S(2)}, u32[]{:S(2)}) collective-permute-start(f32[392,128]{1,0:T(8,128)S(1)} %get-tuple-element.102), channel_id=1, source_target_pairs={{0,8},{4,12},{8,0},{12,4},{1,9},{5,13},{9,1},{13,5},{2,10},{6,14},... | collective-permute-start | bytes 602120 | tf_op jit(solution)/shard_map/ppermute | solution.py:463
  78.1 19.6 %collective-permute-start.29 = (f32[392,128]{1,0:T(8,128)S(1)}, f32[392,128]{1,0:T(8,128)S(1)}, u32[]{:S(2)}, u32[]{:S(2)}) collective-permute-start(f32[392,128]{1,0:T(8,128)S(1)} %get-tuple-element.115), channel_id=1, source_target_pairs={{0,8},{4,12},{8,0},{12,4},{1,9},{5,13},{9,1},{13,5},{2,10},{6,14},... | collective-permute-start | bytes 602120 | tf_op jit(solution)/shard_map/ppermute | solution.py:463
  91.9 7.9 %collective-permute-start.25 = (f32[384,128]{1,0:T(8,128)S(1)}, f32[384,128]{1,0:T(8,128)S(1)}, u32[]{:S(2)}, u32[]{:S(2)}) collective-permute-start(f32[384,128]{1,0:T(8,128)S(1)} %combine.27.refs_0_), channel_id=1, source_target_pairs={{0,2},{2,0},{1,3},{3,1},{4,6},{6,4},{5,7},{7,5},{8,10},{10,8},{9,1... | collective-permute-start | bytes 589832 | tf_op jit(solution)/shard_map/ppermute | solution.py:25
  93.4 10.5 %collective-permute-start.32 = (f32[384,128]{1,0:T(8,128)S(1)}, f32[384,128]{1,0:T(8,128)S(1)}, u32[]{:S(2)}, u32[]{:S(2)}) collective-permute-start(f32[384,128]{1,0:T(8,128)S(1)} %combine.31.refs_2_), channel_id=1, source_target_pairs={{0,2},{2,0},{1,3},{3,1},{4,6},{6,4},{5,7},{7,5},{8,10},{10,8},{9,1... | collective-permute-start | bytes 589832 | tf_op jit(solution)/shard_map/ppermute | solution.py:25
  94.6 10.2 %collective-permute-start.23 = (f32[392,128]{1,0:T(8,128)S(1)}, f32[392,128]{1,0:T(8,128)S(1)}, u32[]{:S(2)}, u32[]{:S(2)}) collective-permute-start(f32[392,128]{1,0:T(8,128)S(1)} %get-tuple-element.105), channel_id=1, source_target_pairs={{0,4},{4,8},{8,12},{12,0},{1,5},{5,9},{9,13},{13,1},{2,6},{6,10},{... | collective-permute-start | bytes 602120 | tf_op jit(solution)/shard_map/ppermute | solution.py:463
  97.6 10.0 %collective-permute-start.30 = (f32[392,128]{1,0:T(8,128)S(1)}, f32[392,128]{1,0:T(8,128)S(1)}, u32[]{:S(2)}, u32[]{:S(2)}) collective-permute-start(f32[392,128]{1,0:T(8,128)S(1)} %get-tuple-element.116), channel_id=1, source_target_pairs={{0,4},{4,8},{8,12},{12,0},{1,5},{5,9},{9,13},{13,1},{2,6},{6,10},{... | collective-permute-start | bytes 602120 | tf_op jit(solution)/shard_map/ppermute | solution.py:463
  99.7 10.1 %collective-permute-start.26 = (f32[384,128]{1,0:T(8,128)S(1)}, f32[384,128]{1,0:T(8,128)S(1)}, u32[]{:S(2)}, u32[]{:S(2)}) collective-permute-start(f32[384,128]{1,0:T(8,128)S(1)} %combine.26.refs_4_), channel_id=1, source_target_pairs={{0,2},{2,0},{1,3},{3,1},{4,6},{6,4},{5,7},{7,5},{8,10},{10,8},{9,1... | collective-permute-start | bytes 589832 | tf_op jit(solution)/shard_map/ppermute | solution.py:25
  103.9 7.2 %collective-permute-start.33 = (f32[384,128]{1,0:T(8,128)S(1)}, f32[384,128]{1,0:T(8,128)S(1)}, u32[]{:S(2)}, u32[]{:S(2)}) collective-permute-start(f32[384,128]{1,0:T(8,128)S(1)} %combine.30.refs_6_), channel_id=1, source_target_pairs={{0,2},{2,0},{1,3},{3,1},{4,6},{6,4},{5,7},{7,5},{8,10},{10,8},{9,1... | collective-permute-start | bytes 589832 | tf_op jit(solution)/shard_map/ppermute | solution.py:25
  104.8 7.9 %collective-permute-start.24 = (f32[392,128]{1,0:T(8,128)S(1)}, f32[392,128]{1,0:T(8,128)S(1)}, u32[]{:S(2)}, u32[]{:S(2)}) collective-permute-start(f32[392,128]{1,0:T(8,128)S(1)} %get-tuple-element.107), channel_id=1, source_target_pairs={{0,12},{4,0},{8,4},{12,8},{1,13},{5,1},{9,5},{13,9},{2,14},{6,2},{... | collective-permute-start | bytes 602120 | tf_op jit(solution)/shard_map/ppermute | solution.py:463
  107.6 7.8 %collective-permute-start.31 = (f32[392,128]{1,0:T(8,128)S(1)}, f32[392,128]{1,0:T(8,128)S(1)}, u32[]{:S(2)}, u32[]{:S(2)}) collective-permute-start(f32[392,128]{1,0:T(8,128)S(1)} %get-tuple-element.117), channel_id=1, source_target_pairs={{0,12},{4,0},{8,4},{12,8},{1,13},{5,1},{9,5},{13,9},{2,14},{6,2},{... | collective-permute-start | bytes 602120 | tf_op jit(solution)/shard_map/ppermute | solution.py:463
  109.8 7.8 %collective-permute-start.27 = (f32[384,128]{1,0:T(8,128)S(1)}, f32[384,128]{1,0:T(8,128)S(1)}, u32[]{:S(2)}, u32[]{:S(2)}) collective-permute-start(f32[384,128]{1,0:T(8,128)S(1)} %combine.25.refs_8_), channel_id=1, source_target_pairs={{0,2},{2,0},{1,3},{3,1},{4,6},{6,4},{5,7},{7,5},{8,10},{10,8},{9,1... | collective-permute-start | bytes 589832 | tf_op jit(solution)/shard_map/ppermute | solution.py:25
  111.2 10.7 %collective-permute-start.34 = (f32[384,128]{1,0:T(8,128)S(1)}, f32[384,128]{1,0:T(8,128)S(1)}, u32[]{:S(2)}, u32[]{:S(2)}) collective-permute-start(f32[384,128]{1,0:T(8,128)S(1)} %combine.29.refs_10_), channel_id=1, source_target_pairs={{0,2},{2,0},{1,3},{3,1},{4,6},{6,4},{5,7},{7,5},{8,10},{10,8},{9,1... | collective-permute-start | bytes 589832 | tf_op jit(solution)/shard_map/ppermute | solution.py:25
  117.6 8.8 %collective-permute-start.28 = (f32[384,128]{1,0:T(8,128)S(1)}, f32[384,128]{1,0:T(8,128)S(1)}, u32[]{:S(2)}, u32[]{:S(2)}) collective-permute-start(f32[384,128]{1,0:T(8,128)S(1)} %combine.24.refs_0_), channel_id=1, source_target_pairs={{0,2},{2,0},{1,3},{3,1},{4,6},{6,4},{5,7},{7,5},{8,10},{10,8},{9,1... | collective-permute-start | bytes 589832 | tf_op jit(solution)/shard_map/ppermute | solution.py:25
  121.8 6.2 %collective-permute-start.35 = (f32[384,128]{1,0:T(8,128)S(1)}, f32[384,128]{1,0:T(8,128)S(1)}, u32[]{:S(2)}, u32[]{:S(2)}) collective-permute-start(f32[384,128]{1,0:T(8,128)S(1)} %combine.28.refs_2_), channel_id=1, source_target_pairs={{0,2},{2,0},{1,3},{3,1},{4,6},{6,4},{5,7},{7,5},{8,10},{10,8},{9,1... | collective-permute-start | bytes 589832 | tf_op jit(solution)/shard_map/ppermute | solution.py:25

commit v13 on v12

--- a/solution.py
+++ b/solution.py
@@ -69,6 +69,35 @@
     for k in range(terms):
         table_ref[3 * count + k] = given_ref[count + k]
     table_ref[3 * count + terms] = lax.axis_index("sub")
+    order = 3 * count + terms + 1
+    far = devices // 2 * per
+    for at in range(count):
+        used[at] = 0
+    for i in range(per):
+        table_ref[order + i] = far + i
+        used[far + i] = 1
+    done = per
+    if devices > 1:
+        for i in range(per):
+            table_ref[order + per + i] = i
+            used[i] = 1
+        done = 2 * per
+    done = jnp.int32(done)
+
+    def add(at, done):
+        new = 1 - used[at]
+
+        @pl.when(new == 1)
+        def _():
+            table_ref[order + done] = at
+
+        used[at] = 1
+        return done + new
+
+    done = lax.fori_loop(
+        0, per, lambda i, done: add(table_ref[2 * count + table_ref[count + i]], done), done
+    )
+    lax.fori_loop(0, count, add, done)
 
 
 def make_table(partner, term_kind, vector):
@@ -77,11 +106,11 @@
     given = jnp.concatenate([partner, term_kind])
     return pl.pallas_call(
         functools.partial(table_kernel, devices, count, terms),
-        out_shape=jax.ShapeDtypeStruct((3 * count + terms + 1,), jnp.int32),
+        out_shape=jax.ShapeDtypeStruct((4 * count + terms + 1,), jnp.int32),
         in_specs=[ANY, WHOLE],
         out_specs=SCALARS,
         scratch_shapes=[
-            pltpu.SMEM((devices,), jnp.int32),
+            pltpu.SMEM((max(devices, count),), jnp.int32),
             pltpu.SMEM(given.shape, jnp.int32),
             pltpu.SemaphoreType.DMA,
         ],
@@ -126,9 +155,9 @@
     )
 
 
-def sector_kernel(count, terms, unroll, height, pieces, origin, starts, tags, table, own_ref, other_ref, *refs):
+def sector_kernel(count, terms, unroll, height, begin, pieces, origin, tags, table, own_ref, other_ref, *refs):
     inputs, scratch = refs[: 2 * unroll], refs[-3 * unroll :]
-    outputs = refs[-3 * unroll - len(starts) : -3 * unroll]
+    outputs = refs[-3 * unroll - len(pieces) - 1 : -3 * unroll]
     moved_refs, kept_ref = outputs[:-1], outputs[-1]
     width = kept_ref.shape[1]
     step = pl.program_id(0)
@@ -146,11 +175,11 @@
                     ref[k * width : (k + 1) * width, unused] = jnp.zeros((width, width), ref.dtype)
         if any(tags):
             tag = own_ref[own_ref.shape[0] - TAG :] + other_ref[other_ref.shape[0] - TAG :]
-            for ref, begin, end, tagged in zip(moved_refs, starts, starts[1:], tags):
+            for ref, (_, size), tagged in zip(moved_refs, pieces, tags):
                 if tagged:
-                    ref[(end - begin) * height :] = tag
-
-    places = [place_of(step * unroll + u, pieces) for u in range(unroll)]
+                    ref[size * height :] = tag
+
+    places = [table[3 * count + terms + 1 + begin + step * unroll + u] for u in range(unroll)]
     results = [
         sector(
             table,
@@ -167,36 +196,23 @@
     ]
     for u, place in enumerate(places):
         kept_ref[sector_at(place)] = results[u][:, width:]
-    for ref, begin, end in zip(moved_refs, starts, starts[1:]):
-        for u in range(unroll):
-            at = step * unroll + u - begin
-
-            @pl.when((at >= 0) & (at < end - begin))
-            def _(ref=ref, u=u, at=at):
+    for ref, (base, size) in zip(moved_refs, pieces):
+        for u, place in enumerate(places):
+
+            @pl.when((place >= base) & (place < base + size))
+            def _(ref=ref, u=u, at=place - base):
                 ref[sector_at(at)] = results[u][:, :width]
 
 
-def place_of(i, pieces):
-    at, begin = pieces[0][0] + i, 0
-    for (_, size), (base, _) in zip(pieces, pieces[1:]):
-        begin += size
-        at = jnp.where(i >= begin, base + i - begin, at)
-    return at
-
-
-def sectors(table, pieces, tags, left, right, own, other, kept, origin, roots):
+def sectors(table, begin, size, pieces, tags, moved, kept, left, right, own, other, origin, roots):
     terms, count, rows, width = left.shape
     height = roots * rows
-    starts = [0]
-    for _, size in pieces:
-        starts.append(starts[-1] + size)
-    places = [base + i for base, size in pieces for i in range(size)]
-
-    unroll = 2 if len(places) % 2 == 0 else 1
+    unroll = 2 if size % 2 == 0 else 1
+    first = 3 * count + terms + 1 + begin
 
     def specs(u):
         def source(i, table):
-            return table[place_of(unroll * i + u, pieces)]
+            return table[table[first + unroll * i + u]]
 
         return [
             pl.BlockSpec((terms, 1, rows, width), lambda i, t: (0, source(i, t), 0, 0)),
@@ -206,15 +222,24 @@
     in_specs = [WHOLE, WHOLE] + [spec for u in range(unroll) for spec in specs(u)]
     args = [own, other] + [left, right] * unroll
     aliases = {}
-    if kept is not None:
-        in_specs.append(WHOLE)
-        args.append(kept)
-        aliases = {len(args): len(pieces)}
+    for at, earlier in enumerate(moved + [kept]):
+        if earlier is not None:
+            in_specs.append(WHOLE)
+            args.append(earlier)
+            aliases[len(args)] = at
     deep = terms * width
     shapes = [(size * height + TAG * tagged, width) for (_, size), tagged in zip(pieces, tags)]
     out = pl.pallas_call(
         functools.partial(
-            sector_kernel, count, terms, unroll, height, pieces, origin, starts, tags
+            sector_kernel,
+            count,
+            terms,
+            unroll,
+            height,
+            begin,
+            pieces,
+            origin,
+            [tagged and earlier is None for tagged, earlier in zip(tags, moved)],
         ),
         out_shape=[
             jax.ShapeDtypeStruct(shape, jnp.float32)
@@ -222,7 +247,7 @@
         ],
         grid_spec=pltpu.PrefetchScalarGridSpec(
             num_scalar_prefetch=1,
-            grid=(starts[-1] // unroll,),
+            grid=(size // unroll,),
             in_specs=in_specs,
             out_specs=[WHOLE] * (len(shapes) + 1),
             scratch_shapes=[
@@ -454,7 +479,8 @@
     pieces = staying + moving
     ahead_of = len(cuts)
     lasting = len(pieces) - ahead_of
-    batches = [moving[:ahead_of], moving[ahead_of:] + staying]
+    far, others = moving[:ahead_of], moving[ahead_of:]
+    calls = [(0, per), (per, min(2 * per, slots - per)), (3 * per, slots - 3 * per)]
 
     def spans(pieces):
         return [piece[1:] for piece in pieces]
@@ -472,29 +498,27 @@
         else:
             other = swap(own)
         kept, outgoing = None, {}
-        for batch in batches:
-            early_now = second and batch is batches[0]
-            pair = early if early_now else (own, other)
+
+        def compute(call, some, kept):
+            ahead_now = second and call == calls[0]
             parts, kept = sectors(
                 table,
-                spans(batch),
-                [second and piece[0] > 0 for piece in batch],
+                *call,
+                spans(some),
+                [second and piece[0] > 0 for piece in some],
+                [outgoing.get(piece) for piece in some],
+                kept,
                 left,
                 right,
-                *pair,
-                kept,
-                (batch[0][1] if early_now else 0) if second else None,
+                *(early if ahead_now else (own, other)),
+                (far[0][1] if ahead_now else 0) if second else None,
                 roots,
             )
-            outgoing.update(zip(batch, parts))
-        arrived, sums, inners = {}, [], []
-        for at, piece in enumerate(moving):
-            value = outgoing[piece]
-            if at >= ahead_of:
-                value = after(value, arrived[moving[at - ahead_of]])[0]
-            arrived[piece] = relay(value, piece[0])
-        for piece in pieces:
-            mine, inner = combine(
+            outgoing.update(zip(some, parts))
+            return kept
+
+        def add_up(piece, kept):
+            return combine(
                 table,
                 piece[1:],
                 kept,
@@ -505,6 +529,21 @@
                 second,
                 not second,
             )
+
+        arrived, sums, inners = {}, [], []
+        kept = compute(calls[0], far, kept)
+        kept = compute(calls[1], staying + others, kept)
+        totals = {piece: add_up(piece, kept) for piece in staying}
+        if calls[2][1] > 0:
+            kept = after(kept, *[totals[piece][0] for piece in staying])[0]
+            kept = compute(calls[2], others, kept)
+        for at, piece in enumerate(moving):
+            value = outgoing[piece]
+            if at >= ahead_of:
+                value = after(value, arrived[moving[at - ahead_of]])[0]
+            arrived[piece] = relay(value, piece[0])
+        for piece in pieces:
+            mine, inner = totals[piece] if piece in totals else add_up(piece, kept)
             if len(sums) >= 2 * ahead_of:
                 mine = after(mine, sums[1 - 2 * ahead_of])[0]
             sums += add_over_term(mine)
@@ -514,7 +553,7 @@
     sums, inners, _, _ = partials(vector, False)
     inner = small_sum(small_sum(sum(inners[1:], inners[0]), "sub"), "blk")
     inner = small_sum(after(inner, sums[-1])[0], "term")
-    first = (batches[0][0][1], sum(size for _, _, size in batches[0]))
+    first = (far[0][1], per)
     raw, ahead = correct(
         table, [[piece[1:]] for piece in pieces], first, inner, vector, diag, sums
     )

time: 130 us -> 139 us (1.069)
  starting transfers between devices: 42.7 us -> 48.6 us
  Pallas kernels: 51 us -> 55.2 us
    ppermute x21, waiting for transfers between devices: 23.2 us -> 14.4 us  [flip(): return lax.ppermute(value, axis, [(i, i ^ bit) for i in range(size)])]
    ppermute x12, waiting for transfers between devices: 7.31 us -> 14.8 us  [relay(): lax.ppermute(value, 'blk', [(p, (p + c) % devices) for p in range(devices)])]
    ppermute x12, starting transfers between devices: 18.5 us -> 24.2 us  [relay(): lax.ppermute(value, 'blk', [(p, (p + c) % devices) for p in range(devices)])]
    pallas_call x4 -> x6, Pallas kernels: 33.8 us -> 37.8 us  [sectors(): pl.pallas_call(functools.partial(sector_kernel, count, terms, unroll, hei...]
  transfers between devices with their start and end apart: 36 -> 36, of which waited for: 20 -> 14; matrix products, arithmetic and copies ran while one was open for 1% -> 1% of each run, Pallas kernels for 33% -> 34%
where the time goes in v13:
time: 139 us; the launch traced here: 138 us
  Pallas kernels  55.2 us (40%)
  starting transfers between devices  48.6 us (35%)
  waiting for transfers between devices  30.9 us (22%)
  local copies, waits for them, and re-layouts  1.5 us (1%)
    pallas_call x6, Pallas kernels, sectors(): pl.pallas_call(functools.partial(sector_kernel, count, terms, unroll, hei...  37.8 us
    ppermute x12, starting transfers between devices, relay(): lax.ppermute(value, 'blk', [(p, (p + c) % devices) for p in range(devices)])  24.2 us
    ppermute x21, starting transfers between devices, flip(): return lax.ppermute(value, axis, [(i, i ^ bit) for i in range(size)])  23.6 us
    ppermute x12, waiting for transfers between devices, relay(): lax.ppermute(value, 'blk', [(p, (p + c) % devices) for p in range(devices)])  14.8 us
    ppermute x21, waiting for transfers between devices, flip(): return lax.ppermute(value, axis, [(i, i ^ bit) for i in range(size)])  14.4 us
    pallas_call x16, Pallas kernels, combine(): pl.pallas_call(functools.partial(combine_kernel, share, piece, ordered, w...  9.66 us
    pallas_call x2, Pallas kernels, finish(): pl.pallas_call(functools.partial(finish_kernel, count, rows, [size for _,...  2.99 us
  transfers between devices with their start and end apart: 36, of which 14 were waited for; matrix products, arithmetic and copies ran while one was open for 1% of the time, Pallas kernels for 34%

profile of v13, /device:TPU:0, one launch (start us, length us, event | category | flops | bytes accessed | tf_op | source)
XLA Modules:
  0.0 138.3 jit_solution(18336310768986531305)
XLA Ops:
  1.9 1.4 %copy-done = f32[16,64,3,128]{3,1,2,0:T(8,128)S(1)} copy-done((f32[16,64,3,128]{3,1,2,0:T(8,128)S(1)}, f32[16,64,3,128]{3,1,2,0:T(8,128)}, u32[]{:S(2)}) %copy-start) | copy-done | bytes 1572888
  3.3 1.7 %table.1 = s32[73]{0:T(128)S(1)} custom-call(s32[24]{0:T(128)S(1)} %pad_add_fusion.given_hbm, f32[3072,128]{1,0:T(8,128)S(1)} %bitcast.10), custom_call_target="tpu_custom_call" | custom-call | tf_op jit(solution)/shard_map/table/pallas_call | solution.py:107
  5.1 5.1 %sectors.6 = (f32[384,128]{1,0:T(8,128)S(1)}, f32[384,128]{1,0:T(8,128)S(1)}, f32[3072,128]{1,0:T(8,128)S(1)}) custom-call(s32[73]{0:T(128)S(1)} %table.1, f32[3072,128]{1,0:T(8,128)S(1)} %bitcast.11, f32[3072,128]{1,0:T(8,128)S(1)} %collective-permute-done.other_ref, f32[8,16,64,128]{3,2,1,0:T(8,128)} %refs_2_.11, f32[8,16,128,128]{3,2,1,0:T(8,128)} %refs_3_.11, ...), custom_call_target="tpu_custom_call" | custom-call | tf_op jit(solution)/shard_map/sectors/pallas_call | solution.py:232
  10.2 3.7 %collective-permute-start.1 = (f32[384,128]{1,0:T(8,128)S(1)}, f32[384,128]{1,0:T(8,128)S(1)}, u32[]{:S(2)}, u32[]{:S(2)}) collective-permute-start(f32[384,128]{1,0:T(8,128)S(1)} %get-tuple-element.88), channel_id=1, source_target_pairs={{0,8},{4,12},{8,0},{12,4},{1,9},{5,13},{9,1},{13,5},{2,10},{6,14},... | collective-permute-start | bytes 589832 | tf_op jit(solution)/shard_map/ppermute | solution.py:489
  14.2 8.5 %sectors.7 = (f32[384,128]{1,0:T(8,128)S(1)}, f32[384,128]{1,0:T(8,128)S(1)}, f32[384,128]{1,0:T(8,128)S(1)}, f32[384,128]{1,0:T(8,128)S(1)}, f32[384,128]{1,0:T...) custom-call(s32[73]{0:T(128)S(1)} %table.1, ...), custom_call_target="tpu_custom_call", output_to_operand_aliasing={{6}: (7, {})} | custom-call | tf_op jit(solution)/shard_map/sectors/pallas_call | solution.py:232
  23.9 1.8 %collective-permute-start.11 = (f32[384,128]{1,0:T(8,128)S(1)}, f32[384,128]{1,0:T(8,128)S(1)}, u32[]{:S(2)}, u32[]{:S(2)}) collective-permute-start(f32[384,128]{1,0:T(8,128)S(1)} %get-tuple-element.85.rest_2_), channel_id=1, source_target_pairs={{0,2},{2,0},{1,3},{3,1},{4,6},{6,4},{5,7},{7,5},{8,10},{10,8},{9,1... | collective-permute-start | bytes 589832 | tf_op jit(solution)/shard_map/ppermute | solution.py:25
  26.0 5.2 %sectors.8 = (f32[384,128]{1,0:T(8,128)S(1)}, f32[384,128]{1,0:T(8,128)S(1)}, f32[384,128]{1,0:T(8,128)S(1)}, f32[384,128]{1,0:T(8,128)S(1)}, f32[3072,128]{1,0:T(8,128)S(1)}) custom-call(s32[73]{0:T(128)S(1)} %table.1, f32[3072,128]{1,0:T(8,128)S(1)} %bitcast.15, ...), custom_call_target="tpu_custom_call", output_to_operand_aliasing={{0}: (7, {}), {1}: (8, {}), {2}: (9, {}), {3}: (10, {}), {4... | custom-call | tf_op jit(solution)/shard_map/sectors/pallas_call | solution.py:232
  32.1 1.0 collective-permute-start.4
  33.1 1.6 %collective-permute-start.3 = (f32[384,128]{1,0:T(8,128)S(1)}, f32[384,128]{1,0:T(8,128)S(1)}, u32[]{:S(2)}, u32[]{:S(2)}) collective-permute-start(f32[384,128]{1,0:T(8,128)S(1)} %get-tuple-element.93), channel_id=1, source_target_pairs={{0,4},{4,8},{8,12},{12,0},{1,5},{5,9},{9,13},{13,1},{2,6},{6,10},{... | collective-permute-start | bytes 589832 | tf_op jit(solution)/shard_map/ppermute | solution.py:489
  35.3 1.5 %collective-permute-start.12 = (f32[384,128]{1,0:T(8,128)S(1)}, f32[384,128]{1,0:T(8,128)S(1)}, u32[]{:S(2)}, u32[]{:S(2)}) collective-permute-start(f32[384,128]{1,0:T(8,128)S(1)} %get-tuple-element.107.rest_6_), channel_id=1, source_target_pairs={{0,2},{2,0},{1,3},{3,1},{4,6},{6,4},{5,7},{7,5},{8,10},{10,8},{9,1... | collective-permute-start | bytes 589832 | tf_op jit(solution)/shard_map/ppermute | solution.py:25
  38.1 3.6 %collective-permute-done.4.arrived_ref = f32[384,128]{1,0:T(8,128)S(1)} collective-permute-done((f32[384,128]{1,0:T(8,128)S(1)}, f32[384,128]{1,0:T(8,128)S(1)}, u32[]{:S(2)}, u32[]{:S(2)}) %collective-permute-start.4) | collective-permute-done | bytes 196640 | tf_op jit(solution)/shard_map/ppermute | solution.py:489
  41.7 1.7 %collective-permute-start.6 = (f32[384,128]{1,0:T(8,128)S(1)}, f32[384,128]{1,0:T(8,128)S(1)}, u32[]{:S(2)}, u32[]{:S(2)}) collective-permute-start(f32[384,128]{1,0:T(8,128)S(1)} %get-tuple-element.102), channel_id=1, source_target_pairs={{0,12},{4,0},{8,4},{12,8},{1,13},{5,1},{9,5},{13,9},{2,14},{6,2},{... | collective-permute-start | bytes 589832 | tf_op jit(solution)/shard_map/ppermute | solution.py:489
  43.4 2.5 %collective-permute-done.3.arrived_ref = f32[384,128]{1,0:T(8,128)S(1)} collective-permute-done((f32[384,128]{1,0:T(8,128)S(1)}, f32[384,128]{1,0:T(8,128)S(1)}, u32[]{:S(2)}, u32[]{:S(2)}) %collective-permute-start.3) | collective-permute-done | bytes 196640 | tf_op jit(solution)/shard_map/ppermute | solution.py:489
  45.9 7.2 %collective-permute-start.5 = (f32[384,128]{1,0:T(8,128)S(1)}, f32[384,128]{1,0:T(8,128)S(1)}, u32[]{:S(2)}, u32[]{:S(2)}) collective-permute-start(f32[384,128]{1,0:T(8,128)S(1)} %get-tuple-element.99), channel_id=1, source_target_pairs={{0,12},{4,0},{8,4},{12,8},{1,13},{5,1},{9,5},{13,9},{2,14},{6,2},{... | collective-permute-start | bytes 589832 | tf_op jit(solution)/shard_map/ppermute | solution.py:489
  53.7 1.5 %collective-permute-start.13 = (f32[384,128]{1,0:T(8,128)S(1)}, f32[384,128]{1,0:T(8,128)S(1)}, u32[]{:S(2)}, u32[]{:S(2)}) collective-permute-start(f32[384,128]{1,0:T(8,128)S(1)} %get-tuple-element.108.rest_10_), channel_id=1, source_target_pairs={{0,2},{2,0},{1,3},{3,1},{4,6},{6,4},{5,7},{7,5},{8,10},{10,8},{9,1... | collective-permute-start | bytes 589832 | tf_op jit(solution)/shard_map/ppermute | solution.py:25
  57.8 1.2 collective-permute-done.7
  59.0 3.4 %collective-permute-start.10 = (f32[8,128]{1,0:T(8,128)S(1)}, f32[8,128]{1,0:T(8,128)S(1)}, u32[]{:S(2)}, u32[]{:S(2)}) collective-permute-start(f32[8,128]{1,0:T(8,128)S(1)} %add.79), channel_id=1, source_target_pairs={{0,12},{4,8},{8,4},{12,0},{1,13},{5,9},{9,5},{13,1},{2,14},{6,10},... | collective-permute-start | bytes 12296 | tf_op jit(solution)/shard_map/ppermute | solution.py:25
  62.4 1.0 collective-permute-start.8
  63.4 1.5 %collective-permute-start.14 = (f32[384,128]{1,0:T(8,128)S(1)}, f32[384,128]{1,0:T(8,128)S(1)}, u32[]{:S(2)}, u32[]{:S(2)}) collective-permute-start(f32[384,128]{1,0:T(8,128)S(1)} %get-tuple-element.109.rest_14_), channel_id=1, source_target_pairs={{0,2},{2,0},{1,3},{3,1},{4,6},{6,4},{5,7},{7,5},{8,10},{10,8},{9,1... | collective-permute-start | bytes 589832 | tf_op jit(solution)/shard_map/ppermute | solution.py:25
  65.4 1.5 %collective-permute-done.9 = f32[8,128]{1,0:T(8,128)S(1)} collective-permute-done((f32[8,128]{1,0:T(8,128)S(1)}, f32[8,128]{1,0:T(8,128)S(1)}, u32[]{:S(2)}, u32[]{:S(2)}) %collective-permute-start.9) | collective-permute-done | bytes 4128 | tf_op jit(solution)/shard_map/ppermute | solution.py:25
  66.9 4.3 %collective-permute-done.14.rest_15_ = f32[384,128]{1,0:T(8,128)S(1)} collective-permute-done((f32[384,128]{1,0:T(8,128)S(1)}, f32[384,128]{1,0:T(8,128)S(1)}, u32[]{:S(2)}, u32[]{:S(2)}) %collective-permute-start.14) | collective-permute-done | bytes 196640 | tf_op jit(solution)/shard_map/ppermute | solution.py:25
  71.2 1.5 %collective-permute-start.15 = (f32[8,128]{1,0:T(8,128)S(1)}, f32[8,128]{1,0:T(8,128)S(1)}, u32[]{:S(2)}, u32[]{:S(2)}) collective-permute-start(f32[8,128]{1,0:T(8,128)S(1)} %add_add_fusion), channel_id=1, source_target_pairs={{0,2},{2,0},{1,3},{3,1},{4,6},{6,4},{5,7},{7,5},{8,10},{10,8},{9,1... | collective-permute-start | bytes 12296 | tf_op jit(solution)/shard_map/ppermute | solution.py:25
  72.7 2.1 %collective-permute-done.15 = f32[8,128]{1,0:T(8,128)S(1)} collective-permute-done((f32[8,128]{1,0:T(8,128)S(1)}, f32[8,128]{1,0:T(8,128)S(1)}, u32[]{:S(2)}, u32[]{:S(2)}) %collective-permute-start.15) | collective-permute-done | bytes 4128 | tf_op jit(solution)/shard_map/ppermute | solution.py:25
  74.8 1.3 correct.1
  76.2 1.7 %collective-permute-done.20.other_ref = f32[776,128]{1,0:T(8,128)S(1)} collective-permute-done((f32[776,128]{1,0:T(8,128)S(1)}, f32[776,128]{1,0:T(8,128)S(1)}, u32[]{:S(2)}, u32[]{:S(2)}) %collective-permute-start.20) | collective-permute-done | bytes 397344 | tf_op jit(solution)/shard_map/ppermute | solution.py:492
  78.0 5.1 %sectors.9 = (f32[392,128]{1,0:T(8,128)S(1)}, f32[392,128]{1,0:T(8,128)S(1)}, f32[3072,128]{1,0:T(8,128)S(1)}) custom-call(s32[73]{0:T(128)S(1)} %table.1, f32[776,128]{1,0:T(8,128)S(1)} %get-tuple-element.118.own_ref, f32[776,128]{1,0:T(8,128)S(1)} %collective-permute-done.20.other_ref, f32[8,16,64,128]{3,2,1,0:T(8,128)} %refs_2_.11, ...), custom_call_target="tpu_custom_call" | custom-call | tf_op jit(solution)/shard_map/sectors/pallas_call | solution.py:232
  83.1 2.0 %collective-permute-start.29 = (f32[392,128]{1,0:T(8,128)S(1)}, f32[392,128]{1,0:T(8,128)S(1)}, u32[]{:S(2)}, u32[]{:S(2)}) collective-permute-start(f32[392,128]{1,0:T(8,128)S(1)} %get-tuple-element.140), channel_id=1, source_target_pairs={{0,8},{4,12},{8,0},{12,4},{1,9},{5,13},{9,1},{13,5},{2,10},{6,14},... | collective-permute-start | bytes 602120 | tf_op jit(solution)/shard_map/ppermute | solution.py:489
  85.2 1.0 collective-permute-start.22
  86.2 8.6 %sectors.10 = (f32[384,128]{1,0:T(8,128)S(1)}, f32[384,128]{1,0:T(8,128)S(1)}, f32[392,128]{1,0:T(8,128)S(1)}, f32[392,128]{1,0:T(8,128)S(1)}, f32[392,128]{1,0:...) custom-call(s32[73]{0:T(128)S(1)} %table.1, ...), custom_call_target="tpu_custom_call", output_to_operand_aliasing={{6}: (7, {})} | custom-call | tf_op jit(solution)/shard_map/sectors/pallas_call | solution.py:232
  95.4 1.5 %collective-permute-start.32 = (f32[384,128]{1,0:T(8,128)S(1)}, f32[384,128]{1,0:T(8,128)S(1)}, u32[]{:S(2)}, u32[]{:S(2)}) collective-permute-start(f32[384,128]{1,0:T(8,128)S(1)} %combine.25.refs_2_), channel_id=1, source_target_pairs={{0,2},{2,0},{1,3},{3,1},{4,6},{6,4},{5,7},{7,5},{8,10},{10,8},{9,1... | collective-permute-start | bytes 589832 | tf_op jit(solution)/shard_map/ppermute | solution.py:25
  98.1 5.2 %sectors.11 = (f32[392,128]{1,0:T(8,128)S(1)}, f32[392,128]{1,0:T(8,128)S(1)}, f32[392,128]{1,0:T(8,128)S(1)}, f32[392,128]{1,0:T(8,128)S(1)}, f32[3072,128]{1,0:T(8,128)S(1)}) custom-call(s32[73]{0:T(128)S(1)} %table.1, ...), custom_call_target="tpu_custom_call", output_to_operand_aliasing={{0}: (7, {}), {1}: (8, {}), {2}: (9, {}), {3}: (10, {}), {4... | custom-call | tf_op jit(solution)/shard_map/sectors/pallas_call | solution.py:232
  103.3 1.2 collective-permute-start.30
  104.5 1.4 collective-permute-start.23
  107.1 1.5 %collective-permute-start.33 = (f32[384,128]{1,0:T(8,128)S(1)}, f32[384,128]{1,0:T(8,128)S(1)}, u32[]{:S(2)}, u32[]{:S(2)}) collective-permute-start(f32[384,128]{1,0:T(8,128)S(1)} %combine.31.refs_6_), channel_id=1, source_target_pairs={{0,2},{2,0},{1,3},{3,1},{4,6},{6,4},{5,7},{7,5},{8,10},{10,8},{9,1... | collective-permute-start | bytes 589832 | tf_op jit(solution)/shard_map/ppermute | solution.py:25
  109.2 4.1 %collective-permute-done.30.arrived_ref = f32[392,128]{1,0:T(8,128)S(1)} collective-permute-done((f32[392,128]{1,0:T(8,128)S(1)}, f32[392,128]{1,0:T(8,128)S(1)}, u32[]{:S(2)}, u32[]{:S(2)}) %collective-permute-start.30) | collective-permute-done | bytes 200736 | tf_op jit(solution)/shard_map/ppermute | solution.py:489
  113.3 1.5 %collective-permute-start.31 = (f32[392,128]{1,0:T(8,128)S(1)}, f32[392,128]{1,0:T(8,128)S(1)}, u32[]{:S(2)}, u32[]{:S(2)}) collective-permute-start(f32[392,128]{1,0:T(8,128)S(1)} %get-tuple-element.142), channel_id=1, source_target_pairs={{0,12},{4,0},{8,4},{12,8},{1,13},{5,1},{9,5},{13,9},{2,14},{6,2},{... | collective-permute-start | bytes 602120 | tf_op jit(solution)/shard_map/ppermute | solution.py:489
  114.7 2.7 %collective-permute-done.23.arrived_ref = f32[392,128]{1,0:T(8,128)S(1)} collective-permute-done((f32[392,128]{1,0:T(8,128)S(1)}, f32[392,128]{1,0:T(8,128)S(1)}, u32[]{:S(2)}, u32[]{:S(2)}) %collective-permute-start.23) | collective-permute-done | bytes 200736 | tf_op jit(solution)/shard_map/ppermute | solution.py:489
  117.5 1.9 %collective-permute-start.24 = (f32[392,128]{1,0:T(8,128)S(1)}, f32[392,128]{1,0:T(8,128)S(1)}, u32[]{:S(2)}, u32[]{:S(2)}) collective-permute-start(f32[392,128]{1,0:T(8,128)S(1)} %get-tuple-element.133), channel_id=1, source_target_pairs={{0,12},{4,0},{8,4},{12,8},{1,13},{5,1},{9,5},{13,9},{2,14},{6,2},{... | collective-permute-start | bytes 602120 | tf_op jit(solution)/shard_map/ppermute | solution.py:489
  120.6 1.5 %collective-permute-start.34 = (f32[384,128]{1,0:T(8,128)S(1)}, f32[384,128]{1,0:T(8,128)S(1)}, u32[]{:S(2)}, u32[]{:S(2)}) collective-permute-start(f32[384,128]{1,0:T(8,128)S(1)} %combine.30.refs_10_), channel_id=1, source_target_pairs={{0,2},{2,0},{1,3},{3,1},{4,6},{6,4},{5,7},{7,5},{8,10},{10,8},{9,1... | collective-permute-start | bytes 589832 | tf_op jit(solution)/shard_map/ppermute | solution.py:25
  123.3 1.0 collective-permute-done.24.arrived_ref
  125.0 1.3 collective-permute-done.34.refs_11_
  126.3 1.5 %collective-permute-start.35 = (f32[384,128]{1,0:T(8,128)S(1)}, f32[384,128]{1,0:T(8,128)S(1)}, u32[]{:S(2)}, u32[]{:S(2)}) collective-permute-start(f32[384,128]{1,0:T(8,128)S(1)} %combine.29.refs_2_), channel_id=1, source_target_pairs={{0,2},{2,0},{1,3},{3,1},{4,6},{6,4},{5,7},{7,5},{8,10},{10,8},{9,1... | collective-permute-start | bytes 589832 | tf_op jit(solution)/shard_map/ppermute | solution.py:25
  127.8 2.7 %collective-permute-done.27.refs_9_ = f32[384,128]{1,0:T(8,128)S(1)} collective-permute-done((f32[384,128]{1,0:T(8,128)S(1)}, f32[384,128]{1,0:T(8,128)S(1)}, u32[]{:S(2)}, u32[]{:S(2)}) %collective-permute-start.27) | collective-permute-done | bytes 196640 | tf_op jit(solution)/shard_map/ppermute | solution.py:25
  130.5 1.5 %collective-permute-start.28 = (f32[384,128]{1,0:T(8,128)S(1)}, f32[384,128]{1,0:T(8,128)S(1)}, u32[]{:S(2)}, u32[]{:S(2)}) collective-permute-start(f32[384,128]{1,0:T(8,128)S(1)} %combine.26.refs_0_), channel_id=1, source_target_pairs={{0,2},{2,0},{1,3},{3,1},{4,6},{6,4},{5,7},{7,5},{8,10},{10,8},{9,1... | collective-permute-start | bytes 589832 | tf_op jit(solution)/shard_map/ppermute | solution.py:25
  132.1 1.8 %scaled.1 = f32[3072,128]{1,0:T(8,128)} custom-call(s32[73]{0:T(128)S(1)} %table.1, f32[8,128]{1,0:T(8,128)S(1)} %broadcast_in_dim.2.scale_ref, f32[3080,128]{1,0:T(8,128)S(1)} %get-tuple-element.119.own_ref.vector_ref.raw_ref), custom_call_target="tpu_custom_call" | custom-call | tf_op jit(solution)/shard_map/scaled/pallas_call | solution.py:394
  133.9 1.7 %finish.2.refs_4_ = f32[3072,128]{1,0:T(8,128)} custom-call(s32[73]{0:T(128)S(1)} %table.1, f32[8,128]{1,0:T(8,128)S(1)} %broadcast_in_dim.2.scale_ref, f32[384,128]{1,0:T(8,128)S(1)} %combine.24.refs_0_, f32[384,128]{1,0:T(8,128)S(1)} %collective-permute-done.25.refs_1_, f32[384,128]{1,0:T(8,128)S(1)} %combine.25.refs_2_, ...), custom_call_target="tpu_custom_call" | custom-call | tf_op jit(solution)/shard_map/finish/pallas_call | solution.py:435
  135.6 1.3 collective-permute-done.28.refs_1_
  136.8 1.3 finish.3
  (68 shorter events, 16.5 us)
Async XLA Ops:
  0.6 4.4 %collective-permute-start = (f32[3072,128]{1,0:T(8,128)}, f32[3072,128]{1,0:T(8,128)S(1)}, u32[]{:S(2)}, u32[]{:S(2)}) collective-permute-start(f32[3072,128]{1,0:T(8,128)} %bitcast.9), channel_id=1, source_target_pairs={{0,1},{1,0},{2,3},{3,2},{4,5},{5,4},{6,7},{7,6},{8,9},{9,8},{10,11... | collective-permute-start | bytes 4718600 | tf_op jit(solution)/shard_map/ppermute | solution.py:492
  1.9 1.4 %copy-start = (f32[16,64,3,128]{3,1,2,0:T(8,128)S(1)}, f32[16,64,3,128]{3,1,2,0:T(8,128)}, u32[]{:S(2)}) copy-start(f32[16,64,3,128]{3,1,2,0:T(8,128)} %param.7) | copy-start | bytes 4718596
  3.3 1.7 %copy-start.1 = (f32[16,64,3,128]{3,1,2,0:T(8,128)S(1)}, f32[16,64,3,128]{3,1,2,0:T(8,128)}, u32[]{:S(2)}) copy-start(f32[16,64,3,128]{3,1,2,0:T(8,128)} %param.7) | copy-start | bytes 4718596
  5.0 8.9 %copy-start.2 = (f32[16,128]{1,0:T(8,128)S(1)}, f32[16,128]{1,0:T(8,128)}, u32[]{:S(2)}) copy-start(f32[16,128]{1,0:T(8,128)} %param.13) | copy-start | bytes 24580
  5.0 8.9 %copy-start.3 = (f32[16,64]{1,0:T(8,128)S(1)}, f32[16,64]{1,0:T(8,128)}, u32[]{:S(2)}) copy-start(f32[16,64]{1,0:T(8,128)} %param.12) | copy-start | bytes 12292
  10.2 22.9 %collective-permute-start.1 = (f32[384,128]{1,0:T(8,128)S(1)}, f32[384,128]{1,0:T(8,128)S(1)}, u32[]{:S(2)}, u32[]{:S(2)}) collective-permute-start(f32[384,128]{1,0:T(8,128)S(1)} %get-tuple-element.88), channel_id=1, source_target_pairs={{0,8},{4,12},{8,0},{12,4},{1,9},{5,13},{9,1},{13,5},{2,10},{6,14},... | collective-permute-start | bytes 589832 | tf_op jit(solution)/shard_map/ppermute | solution.py:489
  13.9 18.2 %collective-permute-start.2 = (f32[384,128]{1,0:T(8,128)S(1)}, f32[384,128]{1,0:T(8,128)S(1)}, u32[]{:S(2)}, u32[]{:S(2)}) collective-permute-start(f32[384,128]{1,0:T(8,128)S(1)} %get-tuple-element.90), channel_id=1, source_target_pairs={{0,8},{4,12},{8,0},{12,4},{1,9},{5,13},{9,1},{13,5},{2,10},{6,14},... | collective-permute-start | bytes 589832 | tf_op jit(solution)/shard_map/ppermute | solution.py:489
  23.9 11.4 %collective-permute-start.11 = (f32[384,128]{1,0:T(8,128)S(1)}, f32[384,128]{1,0:T(8,128)S(1)}, u32[]{:S(2)}, u32[]{:S(2)}) collective-permute-start(f32[384,128]{1,0:T(8,128)S(1)} %get-tuple-element.85.rest_2_), channel_id=1, source_target_pairs={{0,2},{2,0},{1,3},{3,1},{4,6},{6,4},{5,7},{7,5},{8,10},{10,8},{9,1... | collective-permute-start | bytes 589832 | tf_op jit(solution)/shard_map/ppermute | solution.py:25
  25.7 11.8 %collective-permute-start.16 = (f32[384,128]{1,0:T(8,128)S(1)}, f32[384,128]{1,0:T(8,128)S(1)}, u32[]{:S(2)}, u32[]{:S(2)}) collective-permute-start(f32[384,128]{1,0:T(8,128)S(1)} %get-tuple-element.84.rest_0_), channel_id=1, source_target_pairs={{0,2},{2,0},{1,3},{3,1},{4,6},{6,4},{5,7},{7,5},{8,10},{10,8},{9,1... | collective-permute-start | bytes 589832 | tf_op jit(solution)/shard_map/ppermute | solution.py:25
  32.1 9.6 %collective-permute-start.4 = (f32[384,128]{1,0:T(8,128)S(1)}, f32[384,128]{1,0:T(8,128)S(1)}, u32[]{:S(2)}, u32[]{:S(2)}) collective-permute-start(f32[384,128]{1,0:T(8,128)S(1)} %get-tuple-element.96), channel_id=1, source_target_pairs={{0,4},{4,8},{8,12},{12,0},{1,5},{5,9},{9,13},{13,1},{2,6},{6,10},{... | collective-permute-start | bytes 589832 | tf_op jit(solution)/shard_map/ppermute | solution.py:489
  33.1 12.8 %collective-permute-start.3 = (f32[384,128]{1,0:T(8,128)S(1)}, f32[384,128]{1,0:T(8,128)S(1)}, u32[]{:S(2)}, u32[]{:S(2)}) collective-permute-start(f32[384,128]{1,0:T(8,128)S(1)} %get-tuple-element.93), channel_id=1, source_target_pairs={{0,4},{4,8},{8,12},{12,0},{1,5},{5,9},{9,13},{13,1},{2,6},{6,10},{... | collective-permute-start | bytes 589832 | tf_op jit(solution)/shard_map/ppermute | solution.py:489
  35.3 18.3 %collective-permute-start.12 = (f32[384,128]{1,0:T(8,128)S(1)}, f32[384,128]{1,0:T(8,128)S(1)}, u32[]{:S(2)}, u32[]{:S(2)}) collective-permute-start(f32[384,128]{1,0:T(8,128)S(1)} %get-tuple-element.107.rest_6_), channel_id=1, source_target_pairs={{0,2},{2,0},{1,3},{3,1},{4,6},{6,4},{5,7},{7,5},{8,10},{10,8},{9,1... | collective-permute-start | bytes 589832 | tf_op jit(solution)/shard_map/ppermute | solution.py:25
  37.5 18.3 %collective-permute-start.17 = (f32[384,128]{1,0:T(8,128)S(1)}, f32[384,128]{1,0:T(8,128)S(1)}, u32[]{:S(2)}, u32[]{:S(2)}) collective-permute-start(f32[384,128]{1,0:T(8,128)S(1)} %get-tuple-element.112.rest_4_), channel_id=1, source_target_pairs={{0,2},{2,0},{1,3},{3,1},{4,6},{6,4},{5,7},{7,5},{8,10},{10,8},{9,1... | collective-permute-start | bytes 589832 | tf_op jit(solution)/shard_map/ppermute | solution.py:25
  41.7 14.8 %collective-permute-start.6 = (f32[384,128]{1,0:T(8,128)S(1)}, f32[384,128]{1,0:T(8,128)S(1)}, u32[]{:S(2)}, u32[]{:S(2)}) collective-permute-start(f32[384,128]{1,0:T(8,128)S(1)} %get-tuple-element.102), channel_id=1, source_target_pairs={{0,12},{4,0},{8,4},{12,8},{1,13},{5,1},{9,5},{13,9},{2,14},{6,2},{... | collective-permute-start | bytes 589832 | tf_op jit(solution)/shard_map/ppermute | solution.py:489
  45.9 11.2 %collective-permute-start.5 = (f32[384,128]{1,0:T(8,128)S(1)}, f32[384,128]{1,0:T(8,128)S(1)}, u32[]{:S(2)}, u32[]{:S(2)}) collective-permute-start(f32[384,128]{1,0:T(8,128)S(1)} %get-tuple-element.99), channel_id=1, source_target_pairs={{0,12},{4,0},{8,4},{12,8},{1,13},{5,1},{9,5},{13,9},{2,14},{6,2},{... | collective-permute-start | bytes 589832 | tf_op jit(solution)/shard_map/ppermute | solution.py:489
  53.7 9.7 %collective-permute-start.13 = (f32[384,128]{1,0:T(8,128)S(1)}, f32[384,128]{1,0:T(8,128)S(1)}, u32[]{:S(2)}, u32[]{:S(2)}) collective-permute-start(f32[384,128]{1,0:T(8,128)S(1)} %get-tuple-element.108.rest_10_), channel_id=1, source_target_pairs={{0,2},{2,0},{1,3},{3,1},{4,6},{6,4},{5,7},{7,5},{8,10},{10,8},{9,1... | collective-permute-start | bytes 589832 | tf_op jit(solution)/shard_map/ppermute | solution.py:25
  55.8 9.0 %collective-permute-start.18 = (f32[384,128]{1,0:T(8,128)S(1)}, f32[384,128]{1,0:T(8,128)S(1)}, u32[]{:S(2)}, u32[]{:S(2)}) collective-permute-start(f32[384,128]{1,0:T(8,128)S(1)} %get-tuple-element.114.rest_8_), channel_id=1, source_target_pairs={{0,2},{2,0},{1,3},{3,1},{4,6},{6,4},{5,7},{7,5},{8,10},{10,8},{9,1... | collective-permute-start | bytes 589832 | tf_op jit(solution)/shard_map/ppermute | solution.py:25
  57.7 1.2 collective-permute-start.7
  59.0 6.4 %collective-permute-start.10 = (f32[8,128]{1,0:T(8,128)S(1)}, f32[8,128]{1,0:T(8,128)S(1)}, u32[]{:S(2)}, u32[]{:S(2)}) collective-permute-start(f32[8,128]{1,0:T(8,128)S(1)} %add.79), channel_id=1, source_target_pairs={{0,12},{4,8},{8,4},{12,0},{1,13},{5,9},{9,5},{13,1},{2,14},{6,10},... | collective-permute-start | bytes 12296 | tf_op jit(solution)/shard_map/ppermute | solution.py:25
  62.4 4.5 %collective-permute-start.9 = (f32[8,128]{1,0:T(8,128)S(1)}, f32[8,128]{1,0:T(8,128)S(1)}, u32[]{:S(2)}, u32[]{:S(2)}) collective-permute-start(f32[8,128]{1,0:T(8,128)S(1)} %add.79), channel_id=1, source_target_pairs={{0,8},{4,12},{8,0},{12,4},{1,9},{5,13},{9,1},{13,5},{2,10},{6,14},... | collective-permute-start | bytes 12296 | tf_op jit(solution)/shard_map/ppermute | solution.py:25
  62.4 4.5 %collective-permute-start.8 = (f32[8,128]{1,0:T(8,128)S(1)}, f32[8,128]{1,0:T(8,128)S(1)}, u32[]{:S(2)}, u32[]{:S(2)}) collective-permute-start(f32[8,128]{1,0:T(8,128)S(1)} %add.79), channel_id=1, source_target_pairs={{0,4},{4,0},{8,12},{12,8},{1,5},{5,1},{9,13},{13,9},{2,6},{6,2},{1... | collective-permute-start | bytes 12296 | tf_op jit(solution)/shard_map/ppermute | solution.py:25
  63.4 7.8 %collective-permute-start.14 = (f32[384,128]{1,0:T(8,128)S(1)}, f32[384,128]{1,0:T(8,128)S(1)}, u32[]{:S(2)}, u32[]{:S(2)}) collective-permute-start(f32[384,128]{1,0:T(8,128)S(1)} %get-tuple-element.109.rest_14_), channel_id=1, source_target_pairs={{0,2},{2,0},{1,3},{3,1},{4,6},{6,4},{5,7},{7,5},{8,10},{10,8},{9,1... | collective-permute-start | bytes 589832 | tf_op jit(solution)/shard_map/ppermute | solution.py:25
  64.8 10.0 %collective-permute-start.19 = (f32[384,128]{1,0:T(8,128)S(1)}, f32[384,128]{1,0:T(8,128)S(1)}, u32[]{:S(2)}, u32[]{:S(2)}) collective-permute-start(f32[384,128]{1,0:T(8,128)S(1)} %get-tuple-element.116.rest_12_), channel_id=1, source_target_pairs={{0,2},{2,0},{1,3},{3,1},{4,6},{6,4},{5,7},{7,5},{8,10},{10,8},{9,1... | collective-permute-start | bytes 589832 | tf_op jit(solution)/shard_map/ppermute | solution.py:25
  71.2 3.6 %collective-permute-start.15 = (f32[8,128]{1,0:T(8,128)S(1)}, f32[8,128]{1,0:T(8,128)S(1)}, u32[]{:S(2)}, u32[]{:S(2)}) collective-permute-start(f32[8,128]{1,0:T(8,128)S(1)} %add_add_fusion), channel_id=1, source_target_pairs={{0,2},{2,0},{1,3},{3,1},{4,6},{6,4},{5,7},{7,5},{8,10},{10,8},{9,1... | collective-permute-start | bytes 12296 | tf_op jit(solution)/shard_map/ppermute | solution.py:25
  76.1 1.8 %collective-permute-start.20 = (f32[776,128]{1,0:T(8,128)S(1)}, f32[776,128]{1,0:T(8,128)S(1)}, u32[]{:S(2)}, u32[]{:S(2)}) collective-permute-start(f32[776,128]{1,0:T(8,128)S(1)} %get-tuple-element.118.own_ref), channel_id=1, source_target_pairs={{0,1},{1,0},{2,3},{3,2},{4,5},{5,4},{6,7},{7,6},{8,9},{9,8},{10,11... | collective-permute-start | bytes 1191944 | tf_op jit(solution)/shard_map/ppermute | solution.py:492
  77.9 8.3 %collective-permute-start.21 = (f32[3080,128]{1,0:T(8,128)S(1)}, f32[3080,128]{1,0:T(8,128)S(1)}, u32[]{:S(2)}, u32[]{:S(2)}) collective-permute-start(f32[3080,128]{1,0:T(8,128)S(1)} %get-tuple-element.119.own_ref.vector_ref.raw_ref), channel_id=1, source_target_pairs={{0,1},{1,0},{2,3},{3,2},{4,5},{5,4},{6,7},{7,6},{8,9},{9,8},{10,11... | collective-permute-start | bytes 4730888 | tf_op jit(solution)/shard_map/ppermute | solution.py:492
  83.1 20.2 %collective-permute-start.29 = (f32[392,128]{1,0:T(8,128)S(1)}, f32[392,128]{1,0:T(8,128)S(1)}, u32[]{:S(2)}, u32[]{:S(2)}) collective-permute-start(f32[392,128]{1,0:T(8,128)S(1)} %get-tuple-element.140), channel_id=1, source_target_pairs={{0,8},{4,12},{8,0},{12,4},{1,9},{5,13},{9,1},{13,5},{2,10},{6,14},... | collective-permute-start | bytes 602120 | tf_op jit(solution)/shard_map/ppermute | solution.py:489
  85.2 19.3 %collective-permute-start.22 = (f32[392,128]{1,0:T(8,128)S(1)}, f32[392,128]{1,0:T(8,128)S(1)}, u32[]{:S(2)}, u32[]{:S(2)}) collective-permute-start(f32[392,128]{1,0:T(8,128)S(1)} %get-tuple-element.120), channel_id=1, source_target_pairs={{0,8},{4,12},{8,0},{12,4},{1,9},{5,13},{9,1},{13,5},{2,10},{6,14},... | collective-permute-start | bytes 602120 | tf_op jit(solution)/shard_map/ppermute | solution.py:489
  95.4 11.7 %collective-permute-start.32 = (f32[384,128]{1,0:T(8,128)S(1)}, f32[384,128]{1,0:T(8,128)S(1)}, u32[]{:S(2)}, u32[]{:S(2)}) collective-permute-start(f32[384,128]{1,0:T(8,128)S(1)} %combine.25.refs_2_), channel_id=1, source_target_pairs={{0,2},{2,0},{1,3},{3,1},{4,6},{6,4},{5,7},{7,5},{8,10},{10,8},{9,1... | collective-permute-start | bytes 589832 | tf_op jit(solution)/shard_map/ppermute | solution.py:25
  97.5 11.1 %collective-permute-start.25 = (f32[384,128]{1,0:T(8,128)S(1)}, f32[384,128]{1,0:T(8,128)S(1)}, u32[]{:S(2)}, u32[]{:S(2)}) collective-permute-start(f32[384,128]{1,0:T(8,128)S(1)} %combine.24.refs_0_), channel_id=1, source_target_pairs={{0,2},{2,0},{1,3},{3,1},{4,6},{6,4},{5,7},{7,5},{8,10},{10,8},{9,1... | collective-permute-start | bytes 589832 | tf_op jit(solution)/shard_map/ppermute | solution.py:25
  103.3 9.9 %collective-permute-start.30 = (f32[392,128]{1,0:T(8,128)S(1)}, f32[392,128]{1,0:T(8,128)S(1)}, u32[]{:S(2)}, u32[]{:S(2)}) collective-permute-start(f32[392,128]{1,0:T(8,128)S(1)} %get-tuple-element.141), channel_id=1, source_target_pairs={{0,4},{4,8},{8,12},{12,0},{1,5},{5,9},{9,13},{13,1},{2,6},{6,10},{... | collective-permute-start | bytes 602120 | tf_op jit(solution)/shard_map/ppermute | solution.py:489
  104.5 12.9 %collective-permute-start.23 = (f32[392,128]{1,0:T(8,128)S(1)}, f32[392,128]{1,0:T(8,128)S(1)}, u32[]{:S(2)}, u32[]{:S(2)}) collective-permute-start(f32[392,128]{1,0:T(8,128)S(1)} %get-tuple-element.131), channel_id=1, source_target_pairs={{0,4},{4,8},{8,12},{12,0},{1,5},{5,9},{9,13},{13,1},{2,6},{6,10},{... | collective-permute-start | bytes 602120 | tf_op jit(solution)/shard_map/ppermute | solution.py:489
  107.1 13.5 %collective-permute-start.33 = (f32[384,128]{1,0:T(8,128)S(1)}, f32[384,128]{1,0:T(8,128)S(1)}, u32[]{:S(2)}, u32[]{:S(2)}) collective-permute-start(f32[384,128]{1,0:T(8,128)S(1)} %combine.31.refs_6_), channel_id=1, source_target_pairs={{0,2},{2,0},{1,3},{3,1},{4,6},{6,4},{5,7},{7,5},{8,10},{10,8},{9,1... | collective-permute-start | bytes 589832 | tf_op jit(solution)/shard_map/ppermute | solution.py:25
  108.6 13.5 %collective-permute-start.26 = (f32[384,128]{1,0:T(8,128)S(1)}, f32[384,128]{1,0:T(8,128)S(1)}, u32[]{:S(2)}, u32[]{:S(2)}) collective-permute-start(f32[384,128]{1,0:T(8,128)S(1)} %combine.28.refs_4_), channel_id=1, source_target_pairs={{0,2},{2,0},{1,3},{3,1},{4,6},{6,4},{5,7},{7,5},{8,10},{10,8},{9,1... | collective-permute-start | bytes 589832 | tf_op jit(solution)/shard_map/ppermute | solution.py:25
  113.3 9.4 %collective-permute-start.31 = (f32[392,128]{1,0:T(8,128)S(1)}, f32[392,128]{1,0:T(8,128)S(1)}, u32[]{:S(2)}, u32[]{:S(2)}) collective-permute-start(f32[392,128]{1,0:T(8,128)S(1)} %get-tuple-element.142), channel_id=1, source_target_pairs={{0,12},{4,0},{8,4},{12,8},{1,13},{5,1},{9,5},{13,9},{2,14},{6,2},{... | collective-permute-start | bytes 602120 | tf_op jit(solution)/shard_map/ppermute | solution.py:489
  117.5 6.8 %collective-permute-start.24 = (f32[392,128]{1,0:T(8,128)S(1)}, f32[392,128]{1,0:T(8,128)S(1)}, u32[]{:S(2)}, u32[]{:S(2)}) collective-permute-start(f32[392,128]{1,0:T(8,128)S(1)} %get-tuple-element.133), channel_id=1, source_target_pairs={{0,12},{4,0},{8,4},{12,8},{1,13},{5,1},{9,5},{13,9},{2,14},{6,2},{... | collective-permute-start | bytes 602120 | tf_op jit(solution)/shard_map/ppermute | solution.py:489
  120.6 5.7 %collective-permute-start.34 = (f32[384,128]{1,0:T(8,128)S(1)}, f32[384,128]{1,0:T(8,128)S(1)}, u32[]{:S(2)}, u32[]{:S(2)}) collective-permute-start(f32[384,128]{1,0:T(8,128)S(1)} %combine.30.refs_10_), channel_id=1, source_target_pairs={{0,2},{2,0},{1,3},{3,1},{4,6},{6,4},{5,7},{7,5},{8,10},{10,8},{9,1... | collective-permute-start | bytes 589832 | tf_op jit(solution)/shard_map/ppermute | solution.py:25
  122.1 8.4 %collective-permute-start.27 = (f32[384,128]{1,0:T(8,128)S(1)}, f32[384,128]{1,0:T(8,128)S(1)}, u32[]{:S(2)}, u32[]{:S(2)}) collective-permute-start(f32[384,128]{1,0:T(8,128)S(1)} %combine.27.refs_8_), channel_id=1, source_target_pairs={{0,2},{2,0},{1,3},{3,1},{4,6},{6,4},{5,7},{7,5},{8,10},{10,8},{9,1... | collective-permute-start | bytes 589832 | tf_op jit(solution)/shard_map/ppermute | solution.py:25
  126.3 9.3 %collective-permute-start.35 = (f32[384,128]{1,0:T(8,128)S(1)}, f32[384,128]{1,0:T(8,128)S(1)}, u32[]{:S(2)}, u32[]{:S(2)}) collective-permute-start(f32[384,128]{1,0:T(8,128)S(1)} %combine.29.refs_2_), channel_id=1, source_target_pairs={{0,2},{2,0},{1,3},{3,1},{4,6},{6,4},{5,7},{7,5},{8,10},{10,8},{9,1... | collective-permute-start | bytes 589832 | tf_op jit(solution)/shard_map/ppermute | solution.py:25
  130.5 6.3 %collective-permute-start.28 = (f32[384,128]{1,0:T(8,128)S(1)}, f32[384,128]{1,0:T(8,128)S(1)}, u32[]{:S(2)}, u32[]{:S(2)}) collective-permute-start(f32[384,128]{1,0:T(8,128)S(1)} %combine.26.refs_0_), channel_id=1, source_target_pairs={{0,2},{2,0},{1,3},{3,1},{4,6},{6,4},{5,7},{7,5},{8,10},{10,8},{9,1... | collective-permute-start | bytes 589832 | tf_op jit(solution)/shard_map/ppermute | solution.py:25

commit v14 on v12

--- a/solution.py
+++ b/solution.py
@@ -240,14 +240,15 @@
     return out[:-1], out[-1]
 
 
-def combine_kernel(share, piece, ordered, with_inner, table, kept_ref, arrived_ref, vector_ref, diag_ref, sum_ref, *refs):
+def combine_kernel(share, pieces, ordered, with_inner, table, kept_ref, vector_ref, diag_ref, *refs):
+    arrived_refs, sum_ref, refs = refs[: len(pieces)], refs[len(pieces)], refs[len(pieces) + 1 :]
     count, rows, width = diag_ref.shape
     height = kept_ref.shape[0] // count
     roots = height // rows
-    base, size = piece
     inner = [jnp.zeros((1, width), jnp.float32) for _ in range(2 * roots)]
-    for i in range(size):
-        slot = table[count + base + i]
+    every = [(ref, base + i, i) for ref, (base, size) in zip(arrived_refs, pieces) for i in range(size)]
+    for i, (arrived_ref, at_place, of_piece) in enumerate(every):
+        slot = table[count + at_place]
         place = table[2 * count + slot]
         held = place if ordered else slot
         diag = share * diag_ref[slot]
@@ -257,8 +258,9 @@
                 return pl.ds(pl.multiple_of(sector * height + r * rows, rows), rows)
 
             here = slice(i * height + r * rows, i * height + (r + 1) * rows)
+            there = slice(of_piece * height + r * rows, of_piece * height + (r + 1) * rows)
             vector = vector_ref[at(held)]
-            total = kept_ref[at(place)] + arrived_ref[here] + diag * vector
+            total = kept_ref[at(place)] + arrived_ref[there] + diag * vector
             sum_ref[here] = total
             if with_inner:
                 inner[r] = inner[r] + jnp.sum(vector * total, axis=0, keepdims=True)
@@ -270,20 +272,21 @@
         refs[0][...] = jnp.concatenate(inner + [rest], axis=0)
 
 
-def combine(table, piece, kept, arrived, vector, diag, share, ordered, with_inner):
+def combine(table, pieces, kept, arrived, vector, diag, share, ordered, with_inner):
     height, width = kept.shape[0] // diag.shape[0], kept.shape[1]
-    out_shape = [jax.ShapeDtypeStruct((piece[1] * height, width), jnp.float32)]
+    size = sum(size for _, size in pieces)
+    out_shape = [jax.ShapeDtypeStruct((size * height, width), jnp.float32)]
     if with_inner:
         out_shape.append(jax.ShapeDtypeStruct((TAG, width), jnp.float32))
     out = pl.pallas_call(
-        functools.partial(combine_kernel, share, piece, ordered, with_inner),
+        functools.partial(combine_kernel, share, pieces, ordered, with_inner),
         out_shape=out_shape,
-        in_specs=[SCALARS] + [WHOLE] * 4,
+        in_specs=[SCALARS] + [WHOLE] * (3 + len(arrived)),
         out_specs=[WHOLE] * len(out_shape),
         compiler_params=pltpu.CompilerParams(vmem_limit_bytes=SMALL),
         cost_estimate=FREE,
         name="combine",
-    )(table, kept, arrived, vector, diag)
+    )(table, kept, vector, diag, *arrived)
     return out if with_inner else (out[0], None)
 
 
@@ -453,7 +456,8 @@
     staying = [(0, start, size) for start, size in cuts]
     pieces = staying + moving
     ahead_of = len(cuts)
-    lasting = len(pieces) - ahead_of
+    whole = [pieces[i : i + ahead_of] for i in range(0, len(pieces), ahead_of)]
+    single = [[piece] for piece in pieces]
     batches = [moving[:ahead_of], moving[ahead_of:] + staying]
 
     def spans(pieces):
@@ -493,30 +497,30 @@
             if at >= ahead_of:
                 value = after(value, arrived[moving[at - ahead_of]])[0]
             arrived[piece] = relay(value, piece[0])
-        for piece in pieces:
+        for group in single if second else whole:
             mine, inner = combine(
                 table,
-                piece[1:],
+                spans(group),
                 kept,
-                arrived[piece] if piece[0] else outgoing[piece],
+                [arrived[piece] if piece[0] else outgoing[piece] for piece in group],
                 own,
                 diag,
                 1.0 / terms_over,
                 second,
                 not second,
             )
-            if len(sums) >= 2 * ahead_of:
-                mine = after(mine, sums[1 - 2 * ahead_of])[0]
+            if len(sums) >= 2 * 2:
+                mine = after(mine, sums[1 - 2 * 2])[0]
             sums += add_over_term(mine)
             inners.append(inner)
         return sums, inners, arrived, other
 
     sums, inners, _, _ = partials(vector, False)
     inner = small_sum(small_sum(sum(inners[1:], inners[0]), "sub"), "blk")
-    inner = small_sum(after(inner, sums[-1])[0], "term")
+    inner = small_sum(after(inner, sums[-3])[0], "term")
     first = (batches[0][0][1], sum(size for _, _, size in batches[0]))
     raw, ahead = correct(
-        table, [[piece[1:]] for piece in pieces], first, inner, vector, diag, sums
+        table, [spans(group) for group in whole], first, inner, vector, diag, sums
     )
 
     sums, _, arrived, other = partials(raw, True)
@@ -527,7 +531,7 @@
     scale = jnp.broadcast_to(scale, squares.shape)
     correction = scaled(table, scale, raw, slots, rows)
     sigma = None
-    for some in (slice(0, lasting), slice(lasting, None)):
+    for some in (slice(0, -ahead_of), slice(-ahead_of, None)):
         parts = [one for pair in list(zip(sums[::2], sums[1::2]))[some] for one in pair]
         if parts:
             sigma = finish(table, spans(pieces[some]), scale, parts, sigma, slots, rows)

time: 130 us -> 126 us (0.969)
  Pallas kernels: 51 us -> 48.7 us
    ppermute x21 -> x17, waiting for transfers between devices: 23.2 us -> 17.7 us  [flip(): return lax.ppermute(value, axis, [(i, i ^ bit) for i in range(size)])]
    ppermute x12, waiting for transfers between devices: 7.31 us -> 12.5 us  [relay(): lax.ppermute(value, 'blk', [(p, (p + c) % devices) for p in range(devices)])]
    pallas_call x16 -> x12, Pallas kernels: 9.64 us -> 7.4 us  [combine(): pl.pallas_call(functools.partial(combine_kernel, share, pieces, ordered,...]
    ppermute x21 -> x17, starting transfers between devices: 23.4 us -> 21.6 us  [flip(): return lax.ppermute(value, axis, [(i, i ^ bit) for i in range(size)])]
  transfers between devices with their start and end apart: 36 -> 32, of which waited for: 20 -> 18; matrix products, arithmetic and copies ran while one was open for 1% -> 1% of each run, Pallas kernels for 33% -> 33%
where the time goes in v14:
time: 126 us
  Pallas kernels  48.7 us (39%)
  starting transfers between devices  41.8 us (33%)
  waiting for transfers between devices  31.9 us (25%)
  local copies, waits for them, and re-layouts  1.5 us (1%)
    pallas_call x4, Pallas kernels, sectors(): pl.pallas_call(functools.partial(sector_kernel, count, terms, unroll, hei...  33.8 us
    ppermute x17, starting transfers between devices, flip(): return lax.ppermute(value, axis, [(i, i ^ bit) for i in range(size)])  21.6 us
    ppermute x12, starting transfers between devices, relay(): lax.ppermute(value, 'blk', [(p, (p + c) % devices) for p in range(devices)])  19.5 us
    ppermute x17, waiting for transfers between devices, flip(): return lax.ppermute(value, axis, [(i, i ^ bit) for i in range(size)])  17.7 us
    ppermute x12, waiting for transfers between devices, relay(): lax.ppermute(value, 'blk', [(p, (p + c) % devices) for p in range(devices)])  12.5 us
    pallas_call x12, Pallas kernels, combine(): pl.pallas_call(functools.partial(combine_kernel, share, pieces, ordered,...  7.4 us
    pallas_call x2, Pallas kernels, finish(): pl.pallas_call(functools.partial(finish_kernel, count, rows, [size for _,...  2.99 us
  transfers between devices with their start and end apart: 32, of which 18 were waited for; matrix products, arithmetic and copies ran while one was open for 1% of the time, Pallas kernels for 33%

profile of v14, /device:TPU:0, one launch (start us, length us, event | category | flops | bytes accessed | tf_op | source)
XLA Modules:
  0.0 125.8 jit_solution(10747150814989501580)
XLA Ops:
  1.9 1.4 %copy-done = f32[16,64,3,128]{3,1,2,0:T(8,128)S(1)} copy-done((f32[16,64,3,128]{3,1,2,0:T(8,128)S(1)}, f32[16,64,3,128]{3,1,2,0:T(8,128)}, u32[]{:S(2)}) %copy-start) | copy-done | bytes 1572888
  3.3 1.5 %table.1 = s32[57]{0:T(128)S(1)} custom-call(s32[24]{0:T(128)S(1)} %pad_add_fusion.given_hbm, f32[3072,128]{1,0:T(8,128)S(1)} %bitcast.10), custom_call_target="tpu_custom_call" | custom-call | tf_op jit(solution)/shard_map/table/pallas_call | solution.py:78
  4.8 5.2 %sectors.4 = (f32[384,128]{1,0:T(8,128)S(1)}, f32[384,128]{1,0:T(8,128)S(1)}, f32[3072,128]{1,0:T(8,128)S(1)}) custom-call(s32[57]{0:T(128)S(1)} %table.1, f32[3072,128]{1,0:T(8,128)S(1)} %bitcast.11, f32[3072,128]{1,0:T(8,128)S(1)} %collective-permute-done.other_ref, f32[8,16,64,128]{3,2,1,0:T(8,128)} %refs_2_.7, f32[8,16,128,128]{3,2,1,0:T(8,128)} %refs_3_.7, ...), custom_call_target="tpu_custom_call" | custom-call | tf_op jit(solution)/shard_map/sectors/pallas_call | solution.py:215
  10.0 3.7 %collective-permute-start.1 = (f32[384,128]{1,0:T(8,128)S(1)}, f32[384,128]{1,0:T(8,128)S(1)}, u32[]{:S(2)}, u32[]{:S(2)}) collective-permute-start(f32[384,128]{1,0:T(8,128)S(1)} %get-tuple-element.55), channel_id=1, source_target_pairs={{0,8},{4,12},{8,0},{12,4},{1,9},{5,13},{9,1},{13,5},{2,10},{6,14},... | collective-permute-start | bytes 589832 | tf_op jit(solution)/shard_map/ppermute | solution.py:467
  14.0 11.6 %sectors.5 = (f32[384,128]{1,0:T(8,128)S(1)}, f32[384,128]{1,0:T(8,128)S(1)}, f32[384,128]{1,0:T(8,128)S(1)}, f32[384,128]{1,0:T(8,128)S(1)}, f32[384,128]{1,0:T...) custom-call(s32[57]{0:T(128)S(1)} %table.1, ...), custom_call_target="tpu_custom_call", output_to_operand_aliasing={{6}: (7, {})} | custom-call | tf_op jit(solution)/shard_map/sectors/pallas_call | solution.py:215
  26.3 1.8 %collective-permute-start.11 = (f32[768,128]{1,0:T(8,128)S(1)}, f32[768,128]{1,0:T(8,128)S(1)}, u32[]{:S(2)}, u32[]{:S(2)}) collective-permute-start(f32[768,128]{1,0:T(8,128)S(1)} %get-tuple-element.69.rest_0_), channel_id=1, source_target_pairs={{0,2},{2,0},{1,3},{3,1},{4,6},{6,4},{5,7},{7,5},{8,10},{10,8},{9,1... | collective-permute-start | bytes 1179656 | tf_op jit(solution)/shard_map/ppermute | solution.py:25
  28.1 1.6 %collective-permute-start.3 = (f32[384,128]{1,0:T(8,128)S(1)}, f32[384,128]{1,0:T(8,128)S(1)}, u32[]{:S(2)}, u32[]{:S(2)}) collective-permute-start(f32[384,128]{1,0:T(8,128)S(1)} %get-tuple-element.59), channel_id=1, source_target_pairs={{0,4},{4,8},{8,12},{12,0},{1,5},{5,9},{9,13},{13,1},{2,6},{6,10},{... | collective-permute-start | bytes 589832 | tf_op jit(solution)/shard_map/ppermute | solution.py:467
  29.7 2.2 %collective-permute-done.2.refs_1_ = f32[384,128]{1,0:T(8,128)S(1)} collective-permute-done((f32[384,128]{1,0:T(8,128)S(1)}, f32[384,128]{1,0:T(8,128)S(1)}, u32[]{:S(2)}, u32[]{:S(2)}) %collective-permute-start.2) | collective-permute-done | bytes 196640 | tf_op jit(solution)/shard_map/ppermute | solution.py:467
  31.9 0.8 collective-permute-start.4
  33.3 1.6 %collective-permute-start.14 = (f32[768,128]{1,0:T(8,128)S(1)}, f32[768,128]{1,0:T(8,128)S(1)}, u32[]{:S(2)}, u32[]{:S(2)}) collective-permute-start(f32[768,128]{1,0:T(8,128)S(1)} %get-tuple-element.72.rest_2_), channel_id=1, source_target_pairs={{0,2},{2,0},{1,3},{3,1},{4,6},{6,4},{5,7},{7,5},{8,10},{10,8},{9,1... | collective-permute-start | bytes 1179656 | tf_op jit(solution)/shard_map/ppermute | solution.py:25
  34.9 1.6 %collective-permute-done.3.refs_0_ = f32[384,128]{1,0:T(8,128)S(1)} collective-permute-done((f32[384,128]{1,0:T(8,128)S(1)}, f32[384,128]{1,0:T(8,128)S(1)}, u32[]{:S(2)}, u32[]{:S(2)}) %collective-permute-start.3) | collective-permute-done | bytes 196640 | tf_op jit(solution)/shard_map/ppermute | solution.py:467
  36.5 3.3 %collective-permute-start.5 = (f32[384,128]{1,0:T(8,128)S(1)}, f32[384,128]{1,0:T(8,128)S(1)}, u32[]{:S(2)}, u32[]{:S(2)}) collective-permute-start(f32[384,128]{1,0:T(8,128)S(1)} %get-tuple-element.64), channel_id=1, source_target_pairs={{0,12},{4,0},{8,4},{12,8},{1,13},{5,1},{9,5},{13,9},{2,14},{6,2},{... | collective-permute-start | bytes 589832 | tf_op jit(solution)/shard_map/ppermute | solution.py:467
  39.7 1.1 collective-permute-done.4.refs_1_
  40.8 3.0 %collective-permute-start.6 = (f32[384,128]{1,0:T(8,128)S(1)}, f32[384,128]{1,0:T(8,128)S(1)}, u32[]{:S(2)}, u32[]{:S(2)}) collective-permute-start(f32[384,128]{1,0:T(8,128)S(1)} %get-tuple-element.66), channel_id=1, source_target_pairs={{0,12},{4,0},{8,4},{12,8},{1,13},{5,1},{9,5},{13,9},{2,14},{6,2},{... | collective-permute-start | bytes 589832 | tf_op jit(solution)/shard_map/ppermute | solution.py:467
  44.5 1.5 %collective-permute-start.12 = (f32[768,128]{1,0:T(8,128)S(1)}, f32[768,128]{1,0:T(8,128)S(1)}, u32[]{:S(2)}, u32[]{:S(2)}) collective-permute-start(f32[768,128]{1,0:T(8,128)S(1)} %get-tuple-element.70.rest_4_), channel_id=1, source_target_pairs={{0,2},{2,0},{1,3},{3,1},{4,6},{6,4},{5,7},{7,5},{8,10},{10,8},{9,1... | collective-permute-start | bytes 1179656 | tf_op jit(solution)/shard_map/ppermute | solution.py:25
  46.1 3.0 %collective-permute-done.6.refs_1_ = f32[384,128]{1,0:T(8,128)S(1)} collective-permute-done((f32[384,128]{1,0:T(8,128)S(1)}, f32[384,128]{1,0:T(8,128)S(1)}, u32[]{:S(2)}, u32[]{:S(2)}) %collective-permute-start.6) | collective-permute-done | bytes 196640 | tf_op jit(solution)/shard_map/ppermute | solution.py:467
  49.8 1.4 %collective-permute-start.15 = (f32[768,128]{1,0:T(8,128)S(1)}, f32[768,128]{1,0:T(8,128)S(1)}, u32[]{:S(2)}, u32[]{:S(2)}) collective-permute-start(f32[768,128]{1,0:T(8,128)S(1)} %get-tuple-element.74.rest_6_), channel_id=1, source_target_pairs={{0,2},{2,0},{1,3},{3,1},{4,6},{6,4},{5,7},{7,5},{8,10},{10,8},{9,1... | collective-permute-start | bytes 1179656 | tf_op jit(solution)/shard_map/ppermute | solution.py:25
  51.2 1.2 collective-permute-done.7
  52.4 0.8 collective-permute-start.9
  53.2 2.6 %collective-permute-start.10 = (f32[8,128]{1,0:T(8,128)S(1)}, f32[8,128]{1,0:T(8,128)S(1)}, u32[]{:S(2)}, u32[]{:S(2)}) collective-permute-start(f32[8,128]{1,0:T(8,128)S(1)} %add.63), channel_id=1, source_target_pairs={{0,12},{4,8},{8,4},{12,0},{1,13},{5,9},{9,5},{13,1},{2,14},{6,10},... | collective-permute-start | bytes 12296 | tf_op jit(solution)/shard_map/ppermute | solution.py:25
  56.9 1.7 %collective-permute-done.10 = f32[8,128]{1,0:T(8,128)S(1)} collective-permute-done((f32[8,128]{1,0:T(8,128)S(1)}, f32[8,128]{1,0:T(8,128)S(1)}, u32[]{:S(2)}, u32[]{:S(2)}) %collective-permute-start.10) | collective-permute-done | bytes 4128 | tf_op jit(solution)/shard_map/ppermute | solution.py:25
  58.6 0.8 collective-permute-done.8
  60.1 3.8 %collective-permute-done.13 = f32[8,128]{1,0:T(8,128)S(1)} collective-permute-done((f32[8,128]{1,0:T(8,128)S(1)}, f32[8,128]{1,0:T(8,128)S(1)}, u32[]{:S(2)}, u32[]{:S(2)}) %collective-permute-start.13) | collective-permute-done | bytes 4128 | tf_op jit(solution)/shard_map/ppermute | solution.py:25
  63.9 1.3 %correct.1 = (f32[3080,128]{1,0:T(8,128)S(1)}, f32[776,128]{1,0:T(8,128)S(1)}) custom-call(s32[57]{0:T(128)S(1)} %table.1, f32[8,128]{1,0:T(8,128)S(1)} %add.67.inner_ref, f32[3072,128]{1,0:T(8,128)S(1)} %bitcast.17, f32[16,64,128]{2,1,0:T(8,128)S(1)} %broadcast_add_fusion.diag_ref, f32[768,128]{1,0:T(8,128)S(1)} %get-tuple-element.69.rest_0_, ...), custom_call_target="tpu_custom_call" | custom-call | tf_op jit(solution)/shard_map/correct/pallas_call | solution.py:327
  65.2 1.7 %collective-permute-done.16.other_ref = f32[776,128]{1,0:T(8,128)S(1)} collective-permute-done((f32[776,128]{1,0:T(8,128)S(1)}, f32[776,128]{1,0:T(8,128)S(1)}, u32[]{:S(2)}, u32[]{:S(2)}) %collective-permute-start.16) | collective-permute-done | bytes 397344 | tf_op jit(solution)/shard_map/ppermute | solution.py:470
  67.1 5.2 %sectors.6 = (f32[392,128]{1,0:T(8,128)S(1)}, f32[392,128]{1,0:T(8,128)S(1)}, f32[3072,128]{1,0:T(8,128)S(1)}) custom-call(s32[57]{0:T(128)S(1)} %table.1, f32[776,128]{1,0:T(8,128)S(1)} %get-tuple-element.76.own_ref, f32[776,128]{1,0:T(8,128)S(1)} %collective-permute-done.16.other_ref, f32[8,16,64,128]{3,2,1,0:T(8,128)} %refs_2_.7, ...), custom_call_target="tpu_custom_call" | custom-call | tf_op jit(solution)/shard_map/sectors/pallas_call | solution.py:215
  72.3 1.8 %collective-permute-start.18 = (f32[392,128]{1,0:T(8,128)S(1)}, f32[392,128]{1,0:T(8,128)S(1)}, u32[]{:S(2)}, u32[]{:S(2)}) collective-permute-start(f32[392,128]{1,0:T(8,128)S(1)} %get-tuple-element.78), channel_id=1, source_target_pairs={{0,8},{4,12},{8,0},{12,4},{1,9},{5,13},{9,1},{13,5},{2,10},{6,14},... | collective-permute-start | bytes 602120 | tf_op jit(solution)/shard_map/ppermute | solution.py:467
  74.1 1.3 collective-permute-start.25
  75.3 11.7 %sectors.7 = (f32[392,128]{1,0:T(8,128)S(1)}, f32[392,128]{1,0:T(8,128)S(1)}, f32[392,128]{1,0:T(8,128)S(1)}, f32[392,128]{1,0:T(8,128)S(1)}, f32[384,128]{1,0:T...) custom-call(s32[57]{0:T(128)S(1)} %table.1, ...), custom_call_target="tpu_custom_call", output_to_operand_aliasing={{6}: (7, {})} | custom-call | tf_op jit(solution)/shard_map/sectors/pallas_call | solution.py:215
  87.7 1.5 %collective-permute-start.21 = (f32[384,128]{1,0:T(8,128)S(1)}, f32[384,128]{1,0:T(8,128)S(1)}, u32[]{:S(2)}, u32[]{:S(2)}) collective-permute-start(f32[384,128]{1,0:T(8,128)S(1)} %combine.19.refs_0_), channel_id=1, source_target_pairs={{0,2},{2,0},{1,3},{3,1},{4,6},{6,4},{5,7},{7,5},{8,10},{10,8},{9,1... | collective-permute-start | bytes 589832 | tf_op jit(solution)/shard_map/ppermute | solution.py:25
  91.1 2.4 %collective-permute-done.25.refs_0_ = f32[392,128]{1,0:T(8,128)S(1)} collective-permute-done((f32[392,128]{1,0:T(8,128)S(1)}, f32[392,128]{1,0:T(8,128)S(1)}, u32[]{:S(2)}, u32[]{:S(2)}) %collective-permute-start.25) | collective-permute-done | bytes 200736 | tf_op jit(solution)/shard_map/ppermute | solution.py:467
  94.6 0.9 collective-permute-done.21.refs_1_
  95.5 1.4 %collective-permute-start.22 = (f32[384,128]{1,0:T(8,128)S(1)}, f32[384,128]{1,0:T(8,128)S(1)}, u32[]{:S(2)}, u32[]{:S(2)}) collective-permute-start(f32[384,128]{1,0:T(8,128)S(1)} %combine.18.refs_4_), channel_id=1, source_target_pairs={{0,2},{2,0},{1,3},{3,1},{4,6},{6,4},{5,7},{7,5},{8,10},{10,8},{9,1... | collective-permute-start | bytes 589832 | tf_op jit(solution)/shard_map/ppermute | solution.py:25
  97.0 2.8 %collective-permute-done.28.refs_3_ = f32[384,128]{1,0:T(8,128)S(1)} collective-permute-done((f32[384,128]{1,0:T(8,128)S(1)}, f32[384,128]{1,0:T(8,128)S(1)}, u32[]{:S(2)}, u32[]{:S(2)}) %collective-permute-start.28) | collective-permute-done | bytes 196640 | tf_op jit(solution)/shard_map/ppermute | solution.py:25
  99.8 1.4 %collective-permute-start.29 = (f32[384,128]{1,0:T(8,128)S(1)}, f32[384,128]{1,0:T(8,128)S(1)}, u32[]{:S(2)}, u32[]{:S(2)}) collective-permute-start(f32[384,128]{1,0:T(8,128)S(1)} %combine.22.refs_6_), channel_id=1, source_target_pairs={{0,2},{2,0},{1,3},{3,1},{4,6},{6,4},{5,7},{7,5},{8,10},{10,8},{9,1... | collective-permute-start | bytes 589832 | tf_op jit(solution)/shard_map/ppermute | solution.py:25
  101.2 1.9 %collective-permute-start.20 = (f32[392,128]{1,0:T(8,128)S(1)}, f32[392,128]{1,0:T(8,128)S(1)}, u32[]{:S(2)}, u32[]{:S(2)}) collective-permute-start(f32[392,128]{1,0:T(8,128)S(1)} %get-tuple-element.83), channel_id=1, source_target_pairs={{0,12},{4,0},{8,4},{12,8},{1,13},{5,1},{9,5},{13,9},{2,14},{6,2},{... | collective-permute-start | bytes 602120 | tf_op jit(solution)/shard_map/ppermute | solution.py:467
  103.1 1.6 %collective-permute-start.27 = (f32[392,128]{1,0:T(8,128)S(1)}, f32[392,128]{1,0:T(8,128)S(1)}, u32[]{:S(2)}, u32[]{:S(2)}) collective-permute-start(f32[392,128]{1,0:T(8,128)S(1)} %get-tuple-element.93), channel_id=1, source_target_pairs={{0,12},{4,0},{8,4},{12,8},{1,13},{5,1},{9,5},{13,9},{2,14},{6,2},{... | collective-permute-start | bytes 602120 | tf_op jit(solution)/shard_map/ppermute | solution.py:467
  105.8 1.5 %collective-permute-start.23 = (f32[384,128]{1,0:T(8,128)S(1)}, f32[384,128]{1,0:T(8,128)S(1)}, u32[]{:S(2)}, u32[]{:S(2)}) collective-permute-start(f32[384,128]{1,0:T(8,128)S(1)} %combine.17.refs_8_), channel_id=1, source_target_pairs={{0,2},{2,0},{1,3},{3,1},{4,6},{6,4},{5,7},{7,5},{8,10},{10,8},{9,1... | collective-permute-start | bytes 589832 | tf_op jit(solution)/shard_map/ppermute | solution.py:25
  107.4 1.1 collective-permute-start.30
  109.6 1.6 %collective-permute-done.27.refs_0_ = f32[392,128]{1,0:T(8,128)S(1)} collective-permute-done((f32[392,128]{1,0:T(8,128)S(1)}, f32[392,128]{1,0:T(8,128)S(1)}, u32[]{:S(2)}, u32[]{:S(2)}) %collective-permute-start.27) | collective-permute-done | bytes 200736 | tf_op jit(solution)/shard_map/ppermute | solution.py:467
  111.9 1.8 %collective-permute-done.23.refs_9_ = f32[384,128]{1,0:T(8,128)S(1)} collective-permute-done((f32[384,128]{1,0:T(8,128)S(1)}, f32[384,128]{1,0:T(8,128)S(1)}, u32[]{:S(2)}, u32[]{:S(2)}) %collective-permute-start.23) | collective-permute-done | bytes 196640 | tf_op jit(solution)/shard_map/ppermute | solution.py:25
  113.7 1.5 %collective-permute-start.24 = (f32[384,128]{1,0:T(8,128)S(1)}, f32[384,128]{1,0:T(8,128)S(1)}, u32[]{:S(2)}, u32[]{:S(2)}) collective-permute-start(f32[384,128]{1,0:T(8,128)S(1)} %combine.16.refs_0_), channel_id=1, source_target_pairs={{0,2},{2,0},{1,3},{3,1},{4,6},{6,4},{5,7},{7,5},{8,10},{10,8},{9,1... | collective-permute-start | bytes 589832 | tf_op jit(solution)/shard_map/ppermute | solution.py:25
  115.2 2.8 %collective-permute-done.30.refs_11_ = f32[384,128]{1,0:T(8,128)S(1)} collective-permute-done((f32[384,128]{1,0:T(8,128)S(1)}, f32[384,128]{1,0:T(8,128)S(1)}, u32[]{:S(2)}, u32[]{:S(2)}) %collective-permute-start.30) | collective-permute-done | bytes 196640 | tf_op jit(solution)/shard_map/ppermute | solution.py:25
  118.0 1.5 %collective-permute-start.31 = (f32[384,128]{1,0:T(8,128)S(1)}, f32[384,128]{1,0:T(8,128)S(1)}, u32[]{:S(2)}, u32[]{:S(2)}) collective-permute-start(f32[384,128]{1,0:T(8,128)S(1)} %combine.20.refs_2_), channel_id=1, source_target_pairs={{0,2},{2,0},{1,3},{3,1},{4,6},{6,4},{5,7},{7,5},{8,10},{10,8},{9,1... | collective-permute-start | bytes 589832 | tf_op jit(solution)/shard_map/ppermute | solution.py:25
  119.5 1.8 %scaled.1 = f32[3072,128]{1,0:T(8,128)} custom-call(s32[57]{0:T(128)S(1)} %table.1, f32[8,128]{1,0:T(8,128)S(1)} %broadcast_in_dim.2.scale_ref, f32[3080,128]{1,0:T(8,128)S(1)} %get-tuple-element.77.own_ref.vector_ref.raw_ref), custom_call_target="tpu_custom_call" | custom-call | tf_op jit(solution)/shard_map/scaled/pallas_call | solution.py:372
  121.3 1.7 %finish.2.refs_4_ = f32[3072,128]{1,0:T(8,128)} custom-call(s32[57]{0:T(128)S(1)} %table.1, f32[8,128]{1,0:T(8,128)S(1)} %broadcast_in_dim.2.scale_ref, f32[384,128]{1,0:T(8,128)S(1)} %combine.19.refs_0_, f32[384,128]{1,0:T(8,128)S(1)} %collective-permute-done.21.refs_1_, f32[384,128]{1,0:T(8,128)S(1)} %combine.23.refs_2_, ...), custom_call_target="tpu_custom_call" | custom-call | tf_op jit(solution)/shard_map/finish/pallas_call | solution.py:413
  123.0 1.5 %collective-permute-done.31.refs_3_ = f32[384,128]{1,0:T(8,128)S(1)} collective-permute-done((f32[384,128]{1,0:T(8,128)S(1)}, f32[384,128]{1,0:T(8,128)S(1)}, u32[]{:S(2)}, u32[]{:S(2)}) %collective-permute-start.31) | collective-permute-done | bytes 196640 | tf_op jit(solution)/shard_map/ppermute | solution.py:25
  124.5 1.3 %finish.3 = f32[3072,128]{1,0:T(8,128)} custom-call(s32[57]{0:T(128)S(1)} %table.1, f32[8,128]{1,0:T(8,128)S(1)} %broadcast_in_dim.2.scale_ref, f32[384,128]{1,0:T(8,128)S(1)} %combine.16.refs_0_, f32[384,128]{1,0:T(8,128)S(1)} %collective-permute-done.24.refs_1_, f32[384,128]{1,0:T(8,128)S(1)} %combine.20.refs_2_, ...), custom_call_target="tpu_custom_call", output_to_operand_aliasing={{}: (6, {})} | custom-call | tf_op jit(solution)/shard_map/finish/pallas_call | solution.py:413
  (54 shorter events, 12.9 us)
Async XLA Ops:
  0.6 4.2 %collective-permute-start = (f32[3072,128]{1,0:T(8,128)}, f32[3072,128]{1,0:T(8,128)S(1)}, u32[]{:S(2)}, u32[]{:S(2)}) collective-permute-start(f32[3072,128]{1,0:T(8,128)} %bitcast.9), channel_id=1, source_target_pairs={{0,1},{1,0},{2,3},{3,2},{4,5},{5,4},{6,7},{7,6},{8,9},{9,8},{10,11... | collective-permute-start | bytes 4718600 | tf_op jit(solution)/shard_map/ppermute | solution.py:470
  1.9 1.4 %copy-start = (f32[16,64,3,128]{3,1,2,0:T(8,128)S(1)}, f32[16,64,3,128]{3,1,2,0:T(8,128)}, u32[]{:S(2)}) copy-start(f32[16,64,3,128]{3,1,2,0:T(8,128)} %param.7) | copy-start | bytes 4718596
  3.3 1.5 %copy-start.1 = (f32[16,64,3,128]{3,1,2,0:T(8,128)S(1)}, f32[16,64,3,128]{3,1,2,0:T(8,128)}, u32[]{:S(2)}) copy-start(f32[16,64,3,128]{3,1,2,0:T(8,128)} %param.7) | copy-start | bytes 4718596
  4.8 9.0 %copy-start.2 = (f32[16,128]{1,0:T(8,128)S(1)}, f32[16,128]{1,0:T(8,128)}, u32[]{:S(2)}) copy-start(f32[16,128]{1,0:T(8,128)} %param.13) | copy-start | bytes 24580
  4.8 8.9 %copy-start.3 = (f32[16,64]{1,0:T(8,128)S(1)}, f32[16,64]{1,0:T(8,128)}, u32[]{:S(2)}) copy-start(f32[16,64]{1,0:T(8,128)} %param.12) | copy-start | bytes 12292
  10.0 18.1 %collective-permute-start.1 = (f32[384,128]{1,0:T(8,128)S(1)}, f32[384,128]{1,0:T(8,128)S(1)}, u32[]{:S(2)}, u32[]{:S(2)}) collective-permute-start(f32[384,128]{1,0:T(8,128)S(1)} %get-tuple-element.55), channel_id=1, source_target_pairs={{0,8},{4,12},{8,0},{12,4},{1,9},{5,13},{9,1},{13,5},{2,10},{6,14},... | collective-permute-start | bytes 589832 | tf_op jit(solution)/shard_map/ppermute | solution.py:467
  13.7 18.2 %collective-permute-start.2 = (f32[384,128]{1,0:T(8,128)S(1)}, f32[384,128]{1,0:T(8,128)S(1)}, u32[]{:S(2)}, u32[]{:S(2)}) collective-permute-start(f32[384,128]{1,0:T(8,128)S(1)} %get-tuple-element.56), channel_id=1, source_target_pairs={{0,8},{4,12},{8,0},{12,4},{1,9},{5,13},{9,1},{13,5},{2,10},{6,14},... | collective-permute-start | bytes 589832 | tf_op jit(solution)/shard_map/ppermute | solution.py:467
  26.3 18.2 %collective-permute-start.11 = (f32[768,128]{1,0:T(8,128)S(1)}, f32[768,128]{1,0:T(8,128)S(1)}, u32[]{:S(2)}, u32[]{:S(2)}) collective-permute-start(f32[768,128]{1,0:T(8,128)S(1)} %get-tuple-element.69.rest_0_), channel_id=1, source_target_pairs={{0,2},{2,0},{1,3},{3,1},{4,6},{6,4},{5,7},{7,5},{8,10},{10,8},{9,1... | collective-permute-start | bytes 1179656 | tf_op jit(solution)/shard_map/ppermute | solution.py:25
  28.1 8.3 %collective-permute-start.3 = (f32[384,128]{1,0:T(8,128)S(1)}, f32[384,128]{1,0:T(8,128)S(1)}, u32[]{:S(2)}, u32[]{:S(2)}) collective-permute-start(f32[384,128]{1,0:T(8,128)S(1)} %get-tuple-element.59), channel_id=1, source_target_pairs={{0,4},{4,8},{8,12},{12,0},{1,5},{5,9},{9,13},{13,1},{2,6},{6,10},{... | collective-permute-start | bytes 589832 | tf_op jit(solution)/shard_map/ppermute | solution.py:467
  31.9 9.0 %collective-permute-start.4 = (f32[384,128]{1,0:T(8,128)S(1)}, f32[384,128]{1,0:T(8,128)S(1)}, u32[]{:S(2)}, u32[]{:S(2)}) collective-permute-start(f32[384,128]{1,0:T(8,128)S(1)} %get-tuple-element.61), channel_id=1, source_target_pairs={{0,4},{4,8},{8,12},{12,0},{1,5},{5,9},{9,13},{13,1},{2,6},{6,10},{... | collective-permute-start | bytes 589832 | tf_op jit(solution)/shard_map/ppermute | solution.py:467
  33.3 16.4 %collective-permute-start.14 = (f32[768,128]{1,0:T(8,128)S(1)}, f32[768,128]{1,0:T(8,128)S(1)}, u32[]{:S(2)}, u32[]{:S(2)}) collective-permute-start(f32[768,128]{1,0:T(8,128)S(1)} %get-tuple-element.72.rest_2_), channel_id=1, source_target_pairs={{0,2},{2,0},{1,3},{3,1},{4,6},{6,4},{5,7},{7,5},{8,10},{10,8},{9,1... | collective-permute-start | bytes 1179656 | tf_op jit(solution)/shard_map/ppermute | solution.py:25
  36.5 9.6 %collective-permute-start.5 = (f32[384,128]{1,0:T(8,128)S(1)}, f32[384,128]{1,0:T(8,128)S(1)}, u32[]{:S(2)}, u32[]{:S(2)}) collective-permute-start(f32[384,128]{1,0:T(8,128)S(1)} %get-tuple-element.64), channel_id=1, source_target_pairs={{0,12},{4,0},{8,4},{12,8},{1,13},{5,1},{9,5},{13,9},{2,14},{6,2},{... | collective-permute-start | bytes 589832 | tf_op jit(solution)/shard_map/ppermute | solution.py:467
  40.8 8.2 %collective-permute-start.6 = (f32[384,128]{1,0:T(8,128)S(1)}, f32[384,128]{1,0:T(8,128)S(1)}, u32[]{:S(2)}, u32[]{:S(2)}) collective-permute-start(f32[384,128]{1,0:T(8,128)S(1)} %get-tuple-element.66), channel_id=1, source_target_pairs={{0,12},{4,0},{8,4},{12,8},{1,13},{5,1},{9,5},{13,9},{2,14},{6,2},{... | collective-permute-start | bytes 589832 | tf_op jit(solution)/shard_map/ppermute | solution.py:467
  44.5 15.0 %collective-permute-start.12 = (f32[768,128]{1,0:T(8,128)S(1)}, f32[768,128]{1,0:T(8,128)S(1)}, u32[]{:S(2)}, u32[]{:S(2)}) collective-permute-start(f32[768,128]{1,0:T(8,128)S(1)} %get-tuple-element.70.rest_4_), channel_id=1, source_target_pairs={{0,2},{2,0},{1,3},{3,1},{4,6},{6,4},{5,7},{7,5},{8,10},{10,8},{9,1... | collective-permute-start | bytes 1179656 | tf_op jit(solution)/shard_map/ppermute | solution.py:25
  49.8 14.1 %collective-permute-start.15 = (f32[768,128]{1,0:T(8,128)S(1)}, f32[768,128]{1,0:T(8,128)S(1)}, u32[]{:S(2)}, u32[]{:S(2)}) collective-permute-start(f32[768,128]{1,0:T(8,128)S(1)} %get-tuple-element.74.rest_6_), channel_id=1, source_target_pairs={{0,2},{2,0},{1,3},{3,1},{4,6},{6,4},{5,7},{7,5},{8,10},{10,8},{9,1... | collective-permute-start | bytes 1179656 | tf_op jit(solution)/shard_map/ppermute | solution.py:25
  51.2 1.2 collective-permute-start.7
  52.4 4.5 %collective-permute-start.9 = (f32[8,128]{1,0:T(8,128)S(1)}, f32[8,128]{1,0:T(8,128)S(1)}, u32[]{:S(2)}, u32[]{:S(2)}) collective-permute-start(f32[8,128]{1,0:T(8,128)S(1)} %add.63), channel_id=1, source_target_pairs={{0,8},{4,12},{8,0},{12,4},{1,9},{5,13},{9,1},{13,5},{2,10},{6,14},... | collective-permute-start | bytes 12296 | tf_op jit(solution)/shard_map/ppermute | solution.py:25
  53.2 5.4 %collective-permute-start.10 = (f32[8,128]{1,0:T(8,128)S(1)}, f32[8,128]{1,0:T(8,128)S(1)}, u32[]{:S(2)}, u32[]{:S(2)}) collective-permute-start(f32[8,128]{1,0:T(8,128)S(1)} %add.63), channel_id=1, source_target_pairs={{0,12},{4,8},{8,4},{12,0},{1,13},{5,9},{9,5},{13,1},{2,14},{6,10},... | collective-permute-start | bytes 12296 | tf_op jit(solution)/shard_map/ppermute | solution.py:25
  55.9 3.6 %collective-permute-start.8 = (f32[8,128]{1,0:T(8,128)S(1)}, f32[8,128]{1,0:T(8,128)S(1)}, u32[]{:S(2)}, u32[]{:S(2)}) collective-permute-start(f32[8,128]{1,0:T(8,128)S(1)} %add.63), channel_id=1, source_target_pairs={{0,4},{4,0},{8,12},{12,8},{1,5},{5,1},{9,13},{13,9},{2,6},{6,2},{1... | collective-permute-start | bytes 12296 | tf_op jit(solution)/shard_map/ppermute | solution.py:25
  59.5 4.4 %collective-permute-start.13 = (f32[8,128]{1,0:T(8,128)S(1)}, f32[8,128]{1,0:T(8,128)S(1)}, u32[]{:S(2)}, u32[]{:S(2)}) collective-permute-start(f32[8,128]{1,0:T(8,128)S(1)} %add_add_fusion), channel_id=1, source_target_pairs={{0,2},{2,0},{1,3},{3,1},{4,6},{6,4},{5,7},{7,5},{8,10},{10,8},{9,1... | collective-permute-start | bytes 12296 | tf_op jit(solution)/shard_map/ppermute | solution.py:25
  65.2 1.8 %collective-permute-start.16 = (f32[776,128]{1,0:T(8,128)S(1)}, f32[776,128]{1,0:T(8,128)S(1)}, u32[]{:S(2)}, u32[]{:S(2)}) collective-permute-start(f32[776,128]{1,0:T(8,128)S(1)} %get-tuple-element.76.own_ref), channel_id=1, source_target_pairs={{0,1},{1,0},{2,3},{3,2},{4,5},{5,4},{6,7},{7,6},{8,9},{9,8},{10,11... | collective-permute-start | bytes 1191944 | tf_op jit(solution)/shard_map/ppermute | solution.py:470
  66.9 8.4 %collective-permute-start.17 = (f32[3080,128]{1,0:T(8,128)S(1)}, f32[3080,128]{1,0:T(8,128)S(1)}, u32[]{:S(2)}, u32[]{:S(2)}) collective-permute-start(f32[3080,128]{1,0:T(8,128)S(1)} %get-tuple-element.77.own_ref.vector_ref.raw_ref), channel_id=1, source_target_pairs={{0,1},{1,0},{2,3},{3,2},{4,5},{5,4},{6,7},{7,6},{8,9},{9,8},{10,11... | collective-permute-start | bytes 4730888 | tf_op jit(solution)/shard_map/ppermute | solution.py:470
  72.3 18.1 %collective-permute-start.18 = (f32[392,128]{1,0:T(8,128)S(1)}, f32[392,128]{1,0:T(8,128)S(1)}, u32[]{:S(2)}, u32[]{:S(2)}) collective-permute-start(f32[392,128]{1,0:T(8,128)S(1)} %get-tuple-element.78), channel_id=1, source_target_pairs={{0,8},{4,12},{8,0},{12,4},{1,9},{5,13},{9,1},{13,5},{2,10},{6,14},... | collective-permute-start | bytes 602120 | tf_op jit(solution)/shard_map/ppermute | solution.py:467
  74.1 19.4 %collective-permute-start.25 = (f32[392,128]{1,0:T(8,128)S(1)}, f32[392,128]{1,0:T(8,128)S(1)}, u32[]{:S(2)}, u32[]{:S(2)}) collective-permute-start(f32[392,128]{1,0:T(8,128)S(1)} %get-tuple-element.91), channel_id=1, source_target_pairs={{0,8},{4,12},{8,0},{12,4},{1,9},{5,13},{9,1},{13,5},{2,10},{6,14},... | collective-permute-start | bytes 602120 | tf_op jit(solution)/shard_map/ppermute | solution.py:467
  87.7 7.9 %collective-permute-start.21 = (f32[384,128]{1,0:T(8,128)S(1)}, f32[384,128]{1,0:T(8,128)S(1)}, u32[]{:S(2)}, u32[]{:S(2)}) collective-permute-start(f32[384,128]{1,0:T(8,128)S(1)} %combine.19.refs_0_), channel_id=1, source_target_pairs={{0,2},{2,0},{1,3},{3,1},{4,6},{6,4},{5,7},{7,5},{8,10},{10,8},{9,1... | collective-permute-start | bytes 589832 | tf_op jit(solution)/shard_map/ppermute | solution.py:25
  89.8 10.0 %collective-permute-start.28 = (f32[384,128]{1,0:T(8,128)S(1)}, f32[384,128]{1,0:T(8,128)S(1)}, u32[]{:S(2)}, u32[]{:S(2)}) collective-permute-start(f32[384,128]{1,0:T(8,128)S(1)} %combine.23.refs_2_), channel_id=1, source_target_pairs={{0,2},{2,0},{1,3},{3,1},{4,6},{6,4},{5,7},{7,5},{8,10},{10,8},{9,1... | collective-permute-start | bytes 589832 | tf_op jit(solution)/shard_map/ppermute | solution.py:25
  90.4 10.8 %collective-permute-start.19 = (f32[392,128]{1,0:T(8,128)S(1)}, f32[392,128]{1,0:T(8,128)S(1)}, u32[]{:S(2)}, u32[]{:S(2)}) collective-permute-start(f32[392,128]{1,0:T(8,128)S(1)} %get-tuple-element.81), channel_id=1, source_target_pairs={{0,4},{4,8},{8,12},{12,0},{1,5},{5,9},{9,13},{13,1},{2,6},{6,10},{... | collective-permute-start | bytes 602120 | tf_op jit(solution)/shard_map/ppermute | solution.py:467
  93.5 9.6 %collective-permute-start.26 = (f32[392,128]{1,0:T(8,128)S(1)}, f32[392,128]{1,0:T(8,128)S(1)}, u32[]{:S(2)}, u32[]{:S(2)}) collective-permute-start(f32[392,128]{1,0:T(8,128)S(1)} %get-tuple-element.92), channel_id=1, source_target_pairs={{0,4},{4,8},{8,12},{12,0},{1,5},{5,9},{9,13},{13,1},{2,6},{6,10},{... | collective-permute-start | bytes 602120 | tf_op jit(solution)/shard_map/ppermute | solution.py:467
  95.5 10.3 %collective-permute-start.22 = (f32[384,128]{1,0:T(8,128)S(1)}, f32[384,128]{1,0:T(8,128)S(1)}, u32[]{:S(2)}, u32[]{:S(2)}) collective-permute-start(f32[384,128]{1,0:T(8,128)S(1)} %combine.18.refs_4_), channel_id=1, source_target_pairs={{0,2},{2,0},{1,3},{3,1},{4,6},{6,4},{5,7},{7,5},{8,10},{10,8},{9,1... | collective-permute-start | bytes 589832 | tf_op jit(solution)/shard_map/ppermute | solution.py:25
  99.8 7.6 %collective-permute-start.29 = (f32[384,128]{1,0:T(8,128)S(1)}, f32[384,128]{1,0:T(8,128)S(1)}, u32[]{:S(2)}, u32[]{:S(2)}) collective-permute-start(f32[384,128]{1,0:T(8,128)S(1)} %combine.22.refs_6_), channel_id=1, source_target_pairs={{0,2},{2,0},{1,3},{3,1},{4,6},{6,4},{5,7},{7,5},{8,10},{10,8},{9,1... | collective-permute-start | bytes 589832 | tf_op jit(solution)/shard_map/ppermute | solution.py:25
  101.2 7.8 %collective-permute-start.20 = (f32[392,128]{1,0:T(8,128)S(1)}, f32[392,128]{1,0:T(8,128)S(1)}, u32[]{:S(2)}, u32[]{:S(2)}) collective-permute-start(f32[392,128]{1,0:T(8,128)S(1)} %get-tuple-element.83), channel_id=1, source_target_pairs={{0,12},{4,0},{8,4},{12,8},{1,13},{5,1},{9,5},{13,9},{2,14},{6,2},{... | collective-permute-start | bytes 602120 | tf_op jit(solution)/shard_map/ppermute | solution.py:467
  103.1 8.2 %collective-permute-start.27 = (f32[392,128]{1,0:T(8,128)S(1)}, f32[392,128]{1,0:T(8,128)S(1)}, u32[]{:S(2)}, u32[]{:S(2)}) collective-permute-start(f32[392,128]{1,0:T(8,128)S(1)} %get-tuple-element.93), channel_id=1, source_target_pairs={{0,12},{4,0},{8,4},{12,8},{1,13},{5,1},{9,5},{13,9},{2,14},{6,2},{... | collective-permute-start | bytes 602120 | tf_op jit(solution)/shard_map/ppermute | solution.py:467
  105.8 7.9 %collective-permute-start.23 = (f32[384,128]{1,0:T(8,128)S(1)}, f32[384,128]{1,0:T(8,128)S(1)}, u32[]{:S(2)}, u32[]{:S(2)}) collective-permute-start(f32[384,128]{1,0:T(8,128)S(1)} %combine.17.refs_8_), channel_id=1, source_target_pairs={{0,2},{2,0},{1,3},{3,1},{4,6},{6,4},{5,7},{7,5},{8,10},{10,8},{9,1... | collective-permute-start | bytes 589832 | tf_op jit(solution)/shard_map/ppermute | solution.py:25
  107.4 10.6 %collective-permute-start.30 = (f32[384,128]{1,0:T(8,128)S(1)}, f32[384,128]{1,0:T(8,128)S(1)}, u32[]{:S(2)}, u32[]{:S(2)}) collective-permute-start(f32[384,128]{1,0:T(8,128)S(1)} %combine.21.refs_10_), channel_id=1, source_target_pairs={{0,2},{2,0},{1,3},{3,1},{4,6},{6,4},{5,7},{7,5},{8,10},{10,8},{9,1... | collective-permute-start | bytes 589832 | tf_op jit(solution)/shard_map/ppermute | solution.py:25
  113.7 9.2 %collective-permute-start.24 = (f32[384,128]{1,0:T(8,128)S(1)}, f32[384,128]{1,0:T(8,128)S(1)}, u32[]{:S(2)}, u32[]{:S(2)}) collective-permute-start(f32[384,128]{1,0:T(8,128)S(1)} %combine.16.refs_0_), channel_id=1, source_target_pairs={{0,2},{2,0},{1,3},{3,1},{4,6},{6,4},{5,7},{7,5},{8,10},{10,8},{9,1... | collective-permute-start | bytes 589832 | tf_op jit(solution)/shard_map/ppermute | solution.py:25
  118.0 6.5 %collective-permute-start.31 = (f32[384,128]{1,0:T(8,128)S(1)}, f32[384,128]{1,0:T(8,128)S(1)}, u32[]{:S(2)}, u32[]{:S(2)}) collective-permute-start(f32[384,128]{1,0:T(8,128)S(1)} %combine.20.refs_2_), channel_id=1, source_target_pairs={{0,2},{2,0},{1,3},{3,1},{4,6},{6,4},{5,7},{7,5},{8,10},{10,8},{9,1... | collective-permute-start | bytes 589832 | tf_op jit(solution)/shard_map/ppermute | solution.py:25

commit v15 on v14

--- a/solution.py
+++ b/solution.py
@@ -90,14 +90,14 @@
     )(given, vector)
 
 
-def sector(table, count, terms, height, held, own_ref, other_ref, l_ref, r_ref, lhs, high_rhs, low_rhs):
+def sector(table, count, terms, height, source, held, own_ref, other_ref, l_ref, r_ref, lhs, high_rhs, low_rhs):
     rows, width = l_ref.shape[2], r_ref.shape[3]
     roots = height // rows
     first = table[3 * count + terms] == 0
     own, other = own_ref[held], other_ref[held]
     top = jnp.where(first, own, other)
     bottom = jnp.where(first, other, own)
-    left = l_ref[:, 0].reshape(terms * rows, 2 * rows)
+    left = l_ref[:, source].reshape(terms * rows, 2 * rows)
     left = jnp.concatenate(halves(left), axis=1)
     for r in range(roots):
         at = slice(r * rows, (r + 1) * rows)
@@ -115,7 +115,7 @@
         lanes = slice(k * width, (k + 1) * width)
         kind = table[3 * count + k]
         used = pl.ds(pl.multiple_of((1 - kind) * width, width), width)
-        high, low = halves(r_ref[k, 0].T)
+        high, low = halves(r_ref[k, source].T)
         high_rhs[lanes, used] = high
         low_rhs[lanes, used] = low
     high, low = lhs[:height], lhs[height:]
@@ -127,7 +127,8 @@
 
 
 def sector_kernel(count, terms, unroll, height, pieces, origin, starts, tags, table, own_ref, other_ref, *refs):
-    inputs, scratch = refs[: 2 * unroll], refs[-3 * unroll :]
+    streamed = origin is None
+    inputs, scratch = refs[: 2 * unroll if streamed else 2], refs[-3 * unroll :]
     outputs = refs[-3 * unroll - len(starts) : -3 * unroll]
     moved_refs, kept_ref = outputs[:-1], outputs[-1]
     width = kept_ref.shape[1]
@@ -157,10 +158,11 @@
             count,
             terms,
             height,
-            sector_at(table[place] if origin is None else place - origin),
+            0 if streamed else table[place],
+            sector_at(table[place] if streamed else place - origin),
             own_ref,
             other_ref,
-            *inputs[2 * u : 2 * u + 2],
+            *(inputs[2 * u : 2 * u + 2] if streamed else inputs),
             *scratch[3 * u : 3 * u + 3],
         )
         for u, place in enumerate(places)
@@ -203,8 +205,12 @@
             pl.BlockSpec((terms, 1, width, width), lambda i, t: (0, source(i, t), 0, 0)),
         ]
 
-    in_specs = [WHOLE, WHOLE] + [spec for u in range(unroll) for spec in specs(u)]
-    args = [own, other] + [left, right] * unroll
+    if origin is None:
+        in_specs = [WHOLE, WHOLE] + [spec for u in range(unroll) for spec in specs(u)]
+        args = [own, other] + [left, right] * unroll
+    else:
+        in_specs = [WHOLE] * 4
+        args = [own, other, left, right]
     aliases = {}
     if kept is not None:
         in_specs.append(WHOLE)
@@ -233,7 +239,7 @@
             * unroll,
         ),
         input_output_aliases=aliases,
-        compiler_params=pltpu.CompilerParams(vmem_limit_bytes=LIMIT),
+        compiler_params=pltpu.CompilerParams(vmem_limit_bytes=LIMIT if origin is None else SMALL),
         cost_estimate=FREE,
         name="sectors",
     )(table, *args)

time: 126 us -> 125 us (level)
  Pallas kernels: 48.7 us -> 45.6 us
  waiting for transfers between devices: 31.9 us -> 33.6 us
    ppermute x12, waiting for transfers between devices: 12.5 us -> 16 us  [relay(): lax.ppermute(value, 'blk', [(p, (p + c) % devices) for p in range(devices)])]
    pallas_call x4, Pallas kernels: 33.8 us -> 30.7 us  [sectors(): pl.pallas_call(functools.partial(sector_kernel, count, terms, unroll, hei...]
    ppermute x17, waiting for transfers between devices: 17.7 us -> 15.9 us  [flip(): return lax.ppermute(value, axis, [(i, i ^ bit) for i in range(size)])]
  transfers between devices with their start and end apart: 32 -> 32, of which waited for: 18 -> 18; matrix products, arithmetic and copies ran while one was open for 1% -> 1% of each run, Pallas kernels for 33% -> 30%
where the time goes in v15:
time: 125 us
  Pallas kernels  45.6 us (36%)
  starting transfers between devices  42.2 us (34%)
  waiting for transfers between devices  33.6 us (27%)
  local copies, waits for them, and re-layouts  1.51 us (1%)
    pallas_call x4, Pallas kernels, sectors(): pl.pallas_call(functools.partial(sector_kernel, count, terms, unroll, hei...  30.7 us
    ppermute x17, starting transfers between devices, flip(): return lax.ppermute(value, axis, [(i, i ^ bit) for i in range(size)])  21.3 us
    ppermute x12, starting transfers between devices, relay(): lax.ppermute(value, 'blk', [(p, (p + c) % devices) for p in range(devices)])  20.2 us
    ppermute x12, waiting for transfers between devices, relay(): lax.ppermute(value, 'blk', [(p, (p + c) % devices) for p in range(devices)])  16 us
    ppermute x17, waiting for transfers between devices, flip(): return lax.ppermute(value, axis, [(i, i ^ bit) for i in range(size)])  15.9 us
    pallas_call x12, Pallas kernels, combine(): pl.pallas_call(functools.partial(combine_kernel, share, pieces, ordered,...  7.36 us
    pallas_call x2, Pallas kernels, finish(): pl.pallas_call(functools.partial(finish_kernel, count, rows, [size for _,...  2.99 us
  transfers between devices with their start and end apart: 32, of which 18 were waited for; matrix products, arithmetic and copies ran while one was open for 1% of the time, Pallas kernels for 30%

profile of v15, /device:TPU:0, one launch (start us, length us, event | category | flops | bytes accessed | tf_op | source)
XLA Modules:
  0.0 124.9 jit_solution(14351633782749854088)
XLA Ops:
  1.1 0.7 pad_add_fusion.given_hbm
  1.9 1.4 %copy-done.1 = f32[16,64,3,128]{3,1,2,0:T(8,128)S(1)} copy-done((f32[16,64,3,128]{3,1,2,0:T(8,128)S(1)}, f32[16,64,3,128]{3,1,2,0:T(8,128)}, u32[]{:S(2)}) %copy-start.1) | copy-done | bytes 1572888
  3.3 1.5 %table.1 = s32[57]{0:T(128)S(1)} custom-call(s32[24]{0:T(128)S(1)} %pad_add_fusion.given_hbm, f32[3072,128]{1,0:T(8,128)S(1)} %bitcast.12), custom_call_target="tpu_custom_call" | custom-call | tf_op jit(solution)/shard_map/table/pallas_call | solution.py:78
  4.8 5.2 %sectors.4 = (f32[384,128]{1,0:T(8,128)S(1)}, f32[384,128]{1,0:T(8,128)S(1)}, f32[3072,128]{1,0:T(8,128)S(1)}) custom-call(s32[57]{0:T(128)S(1)} %table.1, f32[3072,128]{1,0:T(8,128)S(1)} %bitcast.13, f32[3072,128]{1,0:T(8,128)S(1)} %collective-permute-done.other_ref, f32[8,16,64,128]{3,2,1,0:T(8,128)} %refs_0_.7, f32[8,16,128,128]{3,2,1,0:T(8,128)} %refs_1_.7, ...), custom_call_target="tpu_custom_call" | custom-call | tf_op jit(solution)/shard_map/sectors/pallas_call | solution.py:221
  10.0 3.7 %collective-permute-start.1 = (f32[384,128]{1,0:T(8,128)S(1)}, f32[384,128]{1,0:T(8,128)S(1)}, u32[]{:S(2)}, u32[]{:S(2)}) collective-permute-start(f32[384,128]{1,0:T(8,128)S(1)} %get-tuple-element.55), channel_id=1, source_target_pairs={{0,8},{4,12},{8,0},{12,4},{1,9},{5,13},{9,1},{13,5},{2,10},{6,14},... | collective-permute-start | bytes 589832 | tf_op jit(solution)/shard_map/ppermute | solution.py:473
  13.9 11.6 %sectors.5 = (f32[384,128]{1,0:T(8,128)S(1)}, f32[384,128]{1,0:T(8,128)S(1)}, f32[384,128]{1,0:T(8,128)S(1)}, f32[384,128]{1,0:T(8,128)S(1)}, f32[384,128]{1,0:T...) custom-call(s32[57]{0:T(128)S(1)} %table.1, ...), custom_call_target="tpu_custom_call", output_to_operand_aliasing={{6}: (7, {})} | custom-call | tf_op jit(solution)/shard_map/sectors/pallas_call | solution.py:221
  26.2 1.8 %collective-permute-start.11 = (f32[768,128]{1,0:T(8,128)S(1)}, f32[768,128]{1,0:T(8,128)S(1)}, u32[]{:S(2)}, u32[]{:S(2)}) collective-permute-start(f32[768,128]{1,0:T(8,128)S(1)} %get-tuple-element.69.rest_0_), channel_id=1, source_target_pairs={{0,2},{2,0},{1,3},{3,1},{4,6},{6,4},{5,7},{7,5},{8,10},{10,8},{9,1... | collective-permute-start | bytes 1179656 | tf_op jit(solution)/shard_map/ppermute | solution.py:25
  28.1 1.6 %collective-permute-start.3 = (f32[384,128]{1,0:T(8,128)S(1)}, f32[384,128]{1,0:T(8,128)S(1)}, u32[]{:S(2)}, u32[]{:S(2)}) collective-permute-start(f32[384,128]{1,0:T(8,128)S(1)} %get-tuple-element.59), channel_id=1, source_target_pairs={{0,4},{4,8},{8,12},{12,0},{1,5},{5,9},{9,13},{13,1},{2,6},{6,10},{... | collective-permute-start | bytes 589832 | tf_op jit(solution)/shard_map/ppermute | solution.py:473
  29.6 2.2 %collective-permute-done.2.refs_1_ = f32[384,128]{1,0:T(8,128)S(1)} collective-permute-done((f32[384,128]{1,0:T(8,128)S(1)}, f32[384,128]{1,0:T(8,128)S(1)}, u32[]{:S(2)}, u32[]{:S(2)}) %collective-permute-start.2) | collective-permute-done | bytes 196640 | tf_op jit(solution)/shard_map/ppermute | solution.py:473
  31.9 0.8 collective-permute-start.4
  33.3 1.5 %collective-permute-start.14 = (f32[768,128]{1,0:T(8,128)S(1)}, f32[768,128]{1,0:T(8,128)S(1)}, u32[]{:S(2)}, u32[]{:S(2)}) collective-permute-start(f32[768,128]{1,0:T(8,128)S(1)} %get-tuple-element.72.rest_2_), channel_id=1, source_target_pairs={{0,2},{2,0},{1,3},{3,1},{4,6},{6,4},{5,7},{7,5},{8,10},{10,8},{9,1... | collective-permute-start | bytes 1179656 | tf_op jit(solution)/shard_map/ppermute | solution.py:25
  34.9 1.5 %collective-permute-done.3.refs_0_ = f32[384,128]{1,0:T(8,128)S(1)} collective-permute-done((f32[384,128]{1,0:T(8,128)S(1)}, f32[384,128]{1,0:T(8,128)S(1)}, u32[]{:S(2)}, u32[]{:S(2)}) %collective-permute-start.3) | collective-permute-done | bytes 196640 | tf_op jit(solution)/shard_map/ppermute | solution.py:473
  36.4 3.3 %collective-permute-start.5 = (f32[384,128]{1,0:T(8,128)S(1)}, f32[384,128]{1,0:T(8,128)S(1)}, u32[]{:S(2)}, u32[]{:S(2)}) collective-permute-start(f32[384,128]{1,0:T(8,128)S(1)} %get-tuple-element.64), channel_id=1, source_target_pairs={{0,12},{4,0},{8,4},{12,8},{1,13},{5,1},{9,5},{13,9},{2,14},{6,2},{... | collective-permute-start | bytes 589832 | tf_op jit(solution)/shard_map/ppermute | solution.py:473
  39.7 1.1 collective-permute-done.4.refs_1_
  40.8 3.1 %collective-permute-start.6 = (f32[384,128]{1,0:T(8,128)S(1)}, f32[384,128]{1,0:T(8,128)S(1)}, u32[]{:S(2)}, u32[]{:S(2)}) collective-permute-start(f32[384,128]{1,0:T(8,128)S(1)} %get-tuple-element.66), channel_id=1, source_target_pairs={{0,12},{4,0},{8,4},{12,8},{1,13},{5,1},{9,5},{13,9},{2,14},{6,2},{... | collective-permute-start | bytes 589832 | tf_op jit(solution)/shard_map/ppermute | solution.py:473
  44.5 1.5 %collective-permute-start.12 = (f32[768,128]{1,0:T(8,128)S(1)}, f32[768,128]{1,0:T(8,128)S(1)}, u32[]{:S(2)}, u32[]{:S(2)}) collective-permute-start(f32[768,128]{1,0:T(8,128)S(1)} %get-tuple-element.70.rest_4_), channel_id=1, source_target_pairs={{0,2},{2,0},{1,3},{3,1},{4,6},{6,4},{5,7},{7,5},{8,10},{10,8},{9,1... | collective-permute-start | bytes 1179656 | tf_op jit(solution)/shard_map/ppermute | solution.py:25
  46.1 2.9 %collective-permute-done.6.refs_1_ = f32[384,128]{1,0:T(8,128)S(1)} collective-permute-done((f32[384,128]{1,0:T(8,128)S(1)}, f32[384,128]{1,0:T(8,128)S(1)}, u32[]{:S(2)}, u32[]{:S(2)}) %collective-permute-start.6) | collective-permute-done | bytes 196640 | tf_op jit(solution)/shard_map/ppermute | solution.py:473
  49.7 1.5 %collective-permute-start.15 = (f32[768,128]{1,0:T(8,128)S(1)}, f32[768,128]{1,0:T(8,128)S(1)}, u32[]{:S(2)}, u32[]{:S(2)}) collective-permute-start(f32[768,128]{1,0:T(8,128)S(1)} %get-tuple-element.74.rest_6_), channel_id=1, source_target_pairs={{0,2},{2,0},{1,3},{3,1},{4,6},{6,4},{5,7},{7,5},{8,10},{10,8},{9,1... | collective-permute-start | bytes 1179656 | tf_op jit(solution)/shard_map/ppermute | solution.py:25
  51.2 1.2 collective-permute-done.7
  52.4 0.8 collective-permute-start.9
  53.2 2.6 %collective-permute-start.10 = (f32[8,128]{1,0:T(8,128)S(1)}, f32[8,128]{1,0:T(8,128)S(1)}, u32[]{:S(2)}, u32[]{:S(2)}) collective-permute-start(f32[8,128]{1,0:T(8,128)S(1)} %add.63), channel_id=1, source_target_pairs={{0,12},{4,8},{8,4},{12,0},{1,13},{5,9},{9,5},{13,1},{2,14},{6,10},... | collective-permute-start | bytes 12296 | tf_op jit(solution)/shard_map/ppermute | solution.py:25
  56.9 1.7 %collective-permute-done.10 = f32[8,128]{1,0:T(8,128)S(1)} collective-permute-done((f32[8,128]{1,0:T(8,128)S(1)}, f32[8,128]{1,0:T(8,128)S(1)}, u32[]{:S(2)}, u32[]{:S(2)}) %collective-permute-start.10) | collective-permute-done | bytes 4128 | tf_op jit(solution)/shard_map/ppermute | solution.py:25
  58.6 0.8 collective-permute-done.8
  60.1 3.8 %collective-permute-done.13 = f32[8,128]{1,0:T(8,128)S(1)} collective-permute-done((f32[8,128]{1,0:T(8,128)S(1)}, f32[8,128]{1,0:T(8,128)S(1)}, u32[]{:S(2)}, u32[]{:S(2)}) %collective-permute-start.13) | collective-permute-done | bytes 4128 | tf_op jit(solution)/shard_map/ppermute | solution.py:25
  63.9 1.3 %correct.1 = (f32[3080,128]{1,0:T(8,128)S(1)}, f32[776,128]{1,0:T(8,128)S(1)}) custom-call(s32[57]{0:T(128)S(1)} %table.1, f32[8,128]{1,0:T(8,128)S(1)} %add.67.inner_ref, f32[3072,128]{1,0:T(8,128)S(1)} %bitcast.19, f32[16,64,128]{2,1,0:T(8,128)S(1)} %broadcast_add_fusion.diag_ref, f32[768,128]{1,0:T(8,128)S(1)} %get-tuple-element.69.rest_0_, ...), custom_call_target="tpu_custom_call" | custom-call | tf_op jit(solution)/shard_map/correct/pallas_call | solution.py:333
  65.2 1.7 %collective-permute-done.16.other_ref = f32[776,128]{1,0:T(8,128)S(1)} collective-permute-done((f32[776,128]{1,0:T(8,128)S(1)}, f32[776,128]{1,0:T(8,128)S(1)}, u32[]{:S(2)}, u32[]{:S(2)}) %collective-permute-start.16) | collective-permute-done | bytes 397344 | tf_op jit(solution)/shard_map/ppermute | solution.py:476
  67.1 3.7 %sectors.6 = (f32[392,128]{1,0:T(8,128)S(1)}, f32[392,128]{1,0:T(8,128)S(1)}, f32[3072,128]{1,0:T(8,128)S(1)}) custom-call(s32[57]{0:T(128)S(1)} %table.1, f32[776,128]{1,0:T(8,128)S(1)} %get-tuple-element.76.own_ref, f32[776,128]{1,0:T(8,128)S(1)} %collective-permute-done.16.other_ref, f32[8,16,64,128]{3,2,1,0:T(8,128)S(1)} %copy-done, ...), custom_call_target="tpu_custom_call" | custom-call | tf_op jit(solution)/shard_map/sectors/pallas_call | solution.py:221
  70.8 1.7 %collective-permute-start.18 = (f32[392,128]{1,0:T(8,128)S(1)}, f32[392,128]{1,0:T(8,128)S(1)}, u32[]{:S(2)}, u32[]{:S(2)}) collective-permute-start(f32[392,128]{1,0:T(8,128)S(1)} %get-tuple-element.78), channel_id=1, source_target_pairs={{0,8},{4,12},{8,0},{12,4},{1,9},{5,13},{9,1},{13,5},{2,10},{6,14},... | collective-permute-start | bytes 602120 | tf_op jit(solution)/shard_map/ppermute | solution.py:473
  72.5 1.3 %collective-permute-start.25 = (f32[392,128]{1,0:T(8,128)S(1)}, f32[392,128]{1,0:T(8,128)S(1)}, u32[]{:S(2)}, u32[]{:S(2)}) collective-permute-start(f32[392,128]{1,0:T(8,128)S(1)} %get-tuple-element.91), channel_id=1, source_target_pairs={{0,8},{4,12},{8,0},{12,4},{1,9},{5,13},{9,1},{13,5},{2,10},{6,14},... | collective-permute-start | bytes 602120 | tf_op jit(solution)/shard_map/ppermute | solution.py:473
  73.8 10.2 %sectors.7 = (f32[392,128]{1,0:T(8,128)S(1)}, f32[392,128]{1,0:T(8,128)S(1)}, f32[392,128]{1,0:T(8,128)S(1)}, f32[392,128]{1,0:T(8,128)S(1)}, f32[384,128]{1,0:T...) custom-call(s32[57]{0:T(128)S(1)} %table.1, ...), custom_call_target="tpu_custom_call", output_to_operand_aliasing={{6}: (5, {})} | custom-call | tf_op jit(solution)/shard_map/sectors/pallas_call | solution.py:221
  84.6 1.5 %collective-permute-start.21 = (f32[384,128]{1,0:T(8,128)S(1)}, f32[384,128]{1,0:T(8,128)S(1)}, u32[]{:S(2)}, u32[]{:S(2)}) collective-permute-start(f32[384,128]{1,0:T(8,128)S(1)} %combine.19.refs_0_), channel_id=1, source_target_pairs={{0,2},{2,0},{1,3},{3,1},{4,6},{6,4},{5,7},{7,5},{8,10},{10,8},{9,1... | collective-permute-start | bytes 589832 | tf_op jit(solution)/shard_map/ppermute | solution.py:25
  88.0 4.0 %collective-permute-done.25.refs_0_ = f32[392,128]{1,0:T(8,128)S(1)} collective-permute-done((f32[392,128]{1,0:T(8,128)S(1)}, f32[392,128]{1,0:T(8,128)S(1)}, u32[]{:S(2)}, u32[]{:S(2)}) %collective-permute-start.25) | collective-permute-done | bytes 200736 | tf_op jit(solution)/shard_map/ppermute | solution.py:473
  93.2 1.5 %collective-permute-start.22 = (f32[384,128]{1,0:T(8,128)S(1)}, f32[384,128]{1,0:T(8,128)S(1)}, u32[]{:S(2)}, u32[]{:S(2)}) collective-permute-start(f32[384,128]{1,0:T(8,128)S(1)} %combine.18.refs_4_), channel_id=1, source_target_pairs={{0,2},{2,0},{1,3},{3,1},{4,6},{6,4},{5,7},{7,5},{8,10},{10,8},{9,1... | collective-permute-start | bytes 589832 | tf_op jit(solution)/shard_map/ppermute | solution.py:25
  94.7 0.8 collective-permute-done.28.refs_3_
  95.5 1.5 %collective-permute-start.29 = (f32[384,128]{1,0:T(8,128)S(1)}, f32[384,128]{1,0:T(8,128)S(1)}, u32[]{:S(2)}, u32[]{:S(2)}) collective-permute-start(f32[384,128]{1,0:T(8,128)S(1)} %combine.22.refs_6_), channel_id=1, source_target_pairs={{0,2},{2,0},{1,3},{3,1},{4,6},{6,4},{5,7},{7,5},{8,10},{10,8},{9,1... | collective-permute-start | bytes 589832 | tf_op jit(solution)/shard_map/ppermute | solution.py:25
  97.0 2.6 %collective-permute-start.20 = (f32[392,128]{1,0:T(8,128)S(1)}, f32[392,128]{1,0:T(8,128)S(1)}, u32[]{:S(2)}, u32[]{:S(2)}) collective-permute-start(f32[392,128]{1,0:T(8,128)S(1)} %get-tuple-element.83), channel_id=1, source_target_pairs={{0,12},{4,0},{8,4},{12,8},{1,13},{5,1},{9,5},{13,9},{2,14},{6,2},{... | collective-permute-start | bytes 602120 | tf_op jit(solution)/shard_map/ppermute | solution.py:473
  99.6 1.6 %collective-permute-done.26.refs_0_ = f32[392,128]{1,0:T(8,128)S(1)} collective-permute-done((f32[392,128]{1,0:T(8,128)S(1)}, f32[392,128]{1,0:T(8,128)S(1)}, u32[]{:S(2)}, u32[]{:S(2)}) %collective-permute-start.26) | collective-permute-done | bytes 200736 | tf_op jit(solution)/shard_map/ppermute | solution.py:473
  101.2 1.9 %collective-permute-start.27 = (f32[392,128]{1,0:T(8,128)S(1)}, f32[392,128]{1,0:T(8,128)S(1)}, u32[]{:S(2)}, u32[]{:S(2)}) collective-permute-start(f32[392,128]{1,0:T(8,128)S(1)} %get-tuple-element.93), channel_id=1, source_target_pairs={{0,12},{4,0},{8,4},{12,8},{1,13},{5,1},{9,5},{13,9},{2,14},{6,2},{... | collective-permute-start | bytes 602120 | tf_op jit(solution)/shard_map/ppermute | solution.py:473
  104.3 1.5 %collective-permute-start.23 = (f32[384,128]{1,0:T(8,128)S(1)}, f32[384,128]{1,0:T(8,128)S(1)}, u32[]{:S(2)}, u32[]{:S(2)}) collective-permute-start(f32[384,128]{1,0:T(8,128)S(1)} %combine.17.refs_8_), channel_id=1, source_target_pairs={{0,2},{2,0},{1,3},{3,1},{4,6},{6,4},{5,7},{7,5},{8,10},{10,8},{9,1... | collective-permute-start | bytes 589832 | tf_op jit(solution)/shard_map/ppermute | solution.py:25
  107.0 2.3 %collective-permute-done.27.refs_0_ = f32[392,128]{1,0:T(8,128)S(1)} collective-permute-done((f32[392,128]{1,0:T(8,128)S(1)}, f32[392,128]{1,0:T(8,128)S(1)}, u32[]{:S(2)}, u32[]{:S(2)}) %collective-permute-start.27) | collective-permute-done | bytes 200736 | tf_op jit(solution)/shard_map/ppermute | solution.py:473
  109.9 2.2 %collective-permute-done.23.refs_9_ = f32[384,128]{1,0:T(8,128)S(1)} collective-permute-done((f32[384,128]{1,0:T(8,128)S(1)}, f32[384,128]{1,0:T(8,128)S(1)}, u32[]{:S(2)}, u32[]{:S(2)}) %collective-permute-start.23) | collective-permute-done | bytes 196640 | tf_op jit(solution)/shard_map/ppermute | solution.py:25
  112.1 1.5 %collective-permute-start.24 = (f32[384,128]{1,0:T(8,128)S(1)}, f32[384,128]{1,0:T(8,128)S(1)}, u32[]{:S(2)}, u32[]{:S(2)}) collective-permute-start(f32[384,128]{1,0:T(8,128)S(1)} %combine.16.refs_0_), channel_id=1, source_target_pairs={{0,2},{2,0},{1,3},{3,1},{4,6},{6,4},{5,7},{7,5},{8,10},{10,8},{9,1... | collective-permute-start | bytes 589832 | tf_op jit(solution)/shard_map/ppermute | solution.py:25
  113.6 2.7 %collective-permute-done.30.refs_11_ = f32[384,128]{1,0:T(8,128)S(1)} collective-permute-done((f32[384,128]{1,0:T(8,128)S(1)}, f32[384,128]{1,0:T(8,128)S(1)}, u32[]{:S(2)}, u32[]{:S(2)}) %collective-permute-start.30) | collective-permute-done | bytes 196640 | tf_op jit(solution)/shard_map/ppermute | solution.py:25
  116.3 1.5 %collective-permute-start.31 = (f32[384,128]{1,0:T(8,128)S(1)}, f32[384,128]{1,0:T(8,128)S(1)}, u32[]{:S(2)}, u32[]{:S(2)}) collective-permute-start(f32[384,128]{1,0:T(8,128)S(1)} %combine.20.refs_2_), channel_id=1, source_target_pairs={{0,2},{2,0},{1,3},{3,1},{4,6},{6,4},{5,7},{7,5},{8,10},{10,8},{9,1... | collective-permute-start | bytes 589832 | tf_op jit(solution)/shard_map/ppermute | solution.py:25
  117.9 1.8 %scaled.1 = f32[3072,128]{1,0:T(8,128)} custom-call(s32[57]{0:T(128)S(1)} %table.1, f32[8,128]{1,0:T(8,128)S(1)} %broadcast_in_dim.2.scale_ref, f32[3080,128]{1,0:T(8,128)S(1)} %get-tuple-element.77.own_ref.vector_ref.raw_ref), custom_call_target="tpu_custom_call" | custom-call | tf_op jit(solution)/shard_map/scaled/pallas_call | solution.py:378
  119.7 1.7 %finish.2.refs_4_ = f32[3072,128]{1,0:T(8,128)} custom-call(s32[57]{0:T(128)S(1)} %table.1, f32[8,128]{1,0:T(8,128)S(1)} %broadcast_in_dim.2.scale_ref, f32[384,128]{1,0:T(8,128)S(1)} %combine.19.refs_0_, f32[384,128]{1,0:T(8,128)S(1)} %collective-permute-done.21.refs_1_, f32[384,128]{1,0:T(8,128)S(1)} %combine.23.refs_2_, ...), custom_call_target="tpu_custom_call" | custom-call | tf_op jit(solution)/shard_map/finish/pallas_call | solution.py:419
  121.4 2.1 %collective-permute-done.31.refs_3_ = f32[384,128]{1,0:T(8,128)S(1)} collective-permute-done((f32[384,128]{1,0:T(8,128)S(1)}, f32[384,128]{1,0:T(8,128)S(1)}, u32[]{:S(2)}, u32[]{:S(2)}) %collective-permute-start.31) | collective-permute-done | bytes 196640 | tf_op jit(solution)/shard_map/ppermute | solution.py:25
  123.5 1.3 %finish.3 = f32[3072,128]{1,0:T(8,128)} custom-call(s32[57]{0:T(128)S(1)} %table.1, f32[8,128]{1,0:T(8,128)S(1)} %broadcast_in_dim.2.scale_ref, f32[384,128]{1,0:T(8,128)S(1)} %combine.16.refs_0_, f32[384,128]{1,0:T(8,128)S(1)} %collective-permute-done.24.refs_1_, f32[384,128]{1,0:T(8,128)S(1)} %combine.20.refs_2_, ...), custom_call_target="tpu_custom_call", output_to_operand_aliasing={{}: (6, {})} | custom-call | tf_op jit(solution)/shard_map/finish/pallas_call | solution.py:419
  (61 shorter events, 12.1 us)
Async XLA Ops:
  0.6 4.2 %collective-permute-start = (f32[3072,128]{1,0:T(8,128)}, f32[3072,128]{1,0:T(8,128)S(1)}, u32[]{:S(2)}, u32[]{:S(2)}) collective-permute-start(f32[3072,128]{1,0:T(8,128)} %bitcast.11), channel_id=1, source_target_pairs={{0,1},{1,0},{2,3},{3,2},{4,5},{5,4},{6,7},{7,6},{8,9},{9,8},{10,11... | collective-permute-start | bytes 4718600 | tf_op jit(solution)/shard_map/ppermute | solution.py:476
  1.9 1.4 %copy-start.1 = (f32[16,64,3,128]{3,1,2,0:T(8,128)S(1)}, f32[16,64,3,128]{3,1,2,0:T(8,128)}, u32[]{:S(2)}) copy-start(f32[16,64,3,128]{3,1,2,0:T(8,128)} %param.7) | copy-start | bytes 4718596
  3.3 1.5 %copy-start.2 = (f32[16,64,3,128]{3,1,2,0:T(8,128)S(1)}, f32[16,64,3,128]{3,1,2,0:T(8,128)}, u32[]{:S(2)}) copy-start(f32[16,64,3,128]{3,1,2,0:T(8,128)} %param.7) | copy-start | bytes 4718596
  4.8 9.0 %copy-start.3 = (f32[16,128]{1,0:T(8,128)S(1)}, f32[16,128]{1,0:T(8,128)}, u32[]{:S(2)}) copy-start(f32[16,128]{1,0:T(8,128)} %param.13) | copy-start | bytes 24580
  4.8 8.9 %copy-start.4 = (f32[16,64]{1,0:T(8,128)S(1)}, f32[16,64]{1,0:T(8,128)}, u32[]{:S(2)}) copy-start(f32[16,64]{1,0:T(8,128)} %param.12) | copy-start | bytes 12292
  10.0 18.1 %collective-permute-start.1 = (f32[384,128]{1,0:T(8,128)S(1)}, f32[384,128]{1,0:T(8,128)S(1)}, u32[]{:S(2)}, u32[]{:S(2)}) collective-permute-start(f32[384,128]{1,0:T(8,128)S(1)} %get-tuple-element.55), channel_id=1, source_target_pairs={{0,8},{4,12},{8,0},{12,4},{1,9},{5,13},{9,1},{13,5},{2,10},{6,14},... | collective-permute-start | bytes 589832 | tf_op jit(solution)/shard_map/ppermute | solution.py:473
  13.7 18.2 %collective-permute-start.2 = (f32[384,128]{1,0:T(8,128)S(1)}, f32[384,128]{1,0:T(8,128)S(1)}, u32[]{:S(2)}, u32[]{:S(2)}) collective-permute-start(f32[384,128]{1,0:T(8,128)S(1)} %get-tuple-element.56), channel_id=1, source_target_pairs={{0,8},{4,12},{8,0},{12,4},{1,9},{5,13},{9,1},{13,5},{2,10},{6,14},... | collective-permute-start | bytes 589832 | tf_op jit(solution)/shard_map/ppermute | solution.py:473
  26.2 18.3 %collective-permute-start.11 = (f32[768,128]{1,0:T(8,128)S(1)}, f32[768,128]{1,0:T(8,128)S(1)}, u32[]{:S(2)}, u32[]{:S(2)}) collective-permute-start(f32[768,128]{1,0:T(8,128)S(1)} %get-tuple-element.69.rest_0_), channel_id=1, source_target_pairs={{0,2},{2,0},{1,3},{3,1},{4,6},{6,4},{5,7},{7,5},{8,10},{10,8},{9,1... | collective-permute-start | bytes 1179656 | tf_op jit(solution)/shard_map/ppermute | solution.py:25
  28.1 8.3 %collective-permute-start.3 = (f32[384,128]{1,0:T(8,128)S(1)}, f32[384,128]{1,0:T(8,128)S(1)}, u32[]{:S(2)}, u32[]{:S(2)}) collective-permute-start(f32[384,128]{1,0:T(8,128)S(1)} %get-tuple-element.59), channel_id=1, source_target_pairs={{0,4},{4,8},{8,12},{12,0},{1,5},{5,9},{9,13},{13,1},{2,6},{6,10},{... | collective-permute-start | bytes 589832 | tf_op jit(solution)/shard_map/ppermute | solution.py:473
  31.9 8.9 %collective-permute-start.4 = (f32[384,128]{1,0:T(8,128)S(1)}, f32[384,128]{1,0:T(8,128)S(1)}, u32[]{:S(2)}, u32[]{:S(2)}) collective-permute-start(f32[384,128]{1,0:T(8,128)S(1)} %get-tuple-element.61), channel_id=1, source_target_pairs={{0,4},{4,8},{8,12},{12,0},{1,5},{5,9},{9,13},{13,1},{2,6},{6,10},{... | collective-permute-start | bytes 589832 | tf_op jit(solution)/shard_map/ppermute | solution.py:473
  32.6 34.4 %slice-start = ((s8[8388608]{0:T(1024)(128)(4,1)}), s8[4194304]{0:T(1024)(128)(4,1)S(1)}, s32[]{:S(2)}) async-start(s8[8388608]{0:T(1024)(128)(4,1)} %bitcast.9), calls=%async_computation | async-start | bytes 8388608
  33.3 16.4 %collective-permute-start.14 = (f32[768,128]{1,0:T(8,128)S(1)}, f32[768,128]{1,0:T(8,128)S(1)}, u32[]{:S(2)}, u32[]{:S(2)}) collective-permute-start(f32[768,128]{1,0:T(8,128)S(1)} %get-tuple-element.72.rest_2_), channel_id=1, source_target_pairs={{0,2},{2,0},{1,3},{3,1},{4,6},{6,4},{5,7},{7,5},{8,10},{10,8},{9,1... | collective-permute-start | bytes 1179656 | tf_op jit(solution)/shard_map/ppermute | solution.py:25
  36.4 9.7 %collective-permute-start.5 = (f32[384,128]{1,0:T(8,128)S(1)}, f32[384,128]{1,0:T(8,128)S(1)}, u32[]{:S(2)}, u32[]{:S(2)}) collective-permute-start(f32[384,128]{1,0:T(8,128)S(1)} %get-tuple-element.64), channel_id=1, source_target_pairs={{0,12},{4,0},{8,4},{12,8},{1,13},{5,1},{9,5},{13,9},{2,14},{6,2},{... | collective-permute-start | bytes 589832 | tf_op jit(solution)/shard_map/ppermute | solution.py:473
  40.8 8.2 %collective-permute-start.6 = (f32[384,128]{1,0:T(8,128)S(1)}, f32[384,128]{1,0:T(8,128)S(1)}, u32[]{:S(2)}, u32[]{:S(2)}) collective-permute-start(f32[384,128]{1,0:T(8,128)S(1)} %get-tuple-element.66), channel_id=1, source_target_pairs={{0,12},{4,0},{8,4},{12,8},{1,13},{5,1},{9,5},{13,9},{2,14},{6,2},{... | collective-permute-start | bytes 589832 | tf_op jit(solution)/shard_map/ppermute | solution.py:473
  44.5 22.6 %slice-start.1 = ((s8[8388608]{0:T(1024)(128)(4,1)}), s8[4194304]{0:T(1024)(128)(4,1)S(1)}, s32[]{:S(2)}) async-start(s8[8388608]{0:T(1024)(128)(4,1)} %bitcast.9), calls=%async_computation.1 | async-start | bytes 8388608
  44.5 14.9 %collective-permute-start.12 = (f32[768,128]{1,0:T(8,128)S(1)}, f32[768,128]{1,0:T(8,128)S(1)}, u32[]{:S(2)}, u32[]{:S(2)}) collective-permute-start(f32[768,128]{1,0:T(8,128)S(1)} %get-tuple-element.70.rest_4_), channel_id=1, source_target_pairs={{0,2},{2,0},{1,3},{3,1},{4,6},{6,4},{5,7},{7,5},{8,10},{10,8},{9,1... | collective-permute-start | bytes 1179656 | tf_op jit(solution)/shard_map/ppermute | solution.py:25
  49.7 14.2 %collective-permute-start.15 = (f32[768,128]{1,0:T(8,128)S(1)}, f32[768,128]{1,0:T(8,128)S(1)}, u32[]{:S(2)}, u32[]{:S(2)}) collective-permute-start(f32[768,128]{1,0:T(8,128)S(1)} %get-tuple-element.74.rest_6_), channel_id=1, source_target_pairs={{0,2},{2,0},{1,3},{3,1},{4,6},{6,4},{5,7},{7,5},{8,10},{10,8},{9,1... | collective-permute-start | bytes 1179656 | tf_op jit(solution)/shard_map/ppermute | solution.py:25
  51.2 1.2 collective-permute-start.7
  52.4 4.5 %collective-permute-start.9 = (f32[8,128]{1,0:T(8,128)S(1)}, f32[8,128]{1,0:T(8,128)S(1)}, u32[]{:S(2)}, u32[]{:S(2)}) collective-permute-start(f32[8,128]{1,0:T(8,128)S(1)} %add.63), channel_id=1, source_target_pairs={{0,8},{4,12},{8,0},{12,4},{1,9},{5,13},{9,1},{13,5},{2,10},{6,14},... | collective-permute-start | bytes 12296 | tf_op jit(solution)/shard_map/ppermute | solution.py:25
  53.2 5.4 %collective-permute-start.10 = (f32[8,128]{1,0:T(8,128)S(1)}, f32[8,128]{1,0:T(8,128)S(1)}, u32[]{:S(2)}, u32[]{:S(2)}) collective-permute-start(f32[8,128]{1,0:T(8,128)S(1)} %add.63), channel_id=1, source_target_pairs={{0,12},{4,8},{8,4},{12,0},{1,13},{5,9},{9,5},{13,1},{2,14},{6,10},... | collective-permute-start | bytes 12296 | tf_op jit(solution)/shard_map/ppermute | solution.py:25
  55.9 3.6 %collective-permute-start.8 = (f32[8,128]{1,0:T(8,128)S(1)}, f32[8,128]{1,0:T(8,128)S(1)}, u32[]{:S(2)}, u32[]{:S(2)}) collective-permute-start(f32[8,128]{1,0:T(8,128)S(1)} %add.63), channel_id=1, source_target_pairs={{0,4},{4,0},{8,12},{12,8},{1,5},{5,1},{9,13},{13,9},{2,6},{6,2},{1... | collective-permute-start | bytes 12296 | tf_op jit(solution)/shard_map/ppermute | solution.py:25
  59.5 4.4 %collective-permute-start.13 = (f32[8,128]{1,0:T(8,128)S(1)}, f32[8,128]{1,0:T(8,128)S(1)}, u32[]{:S(2)}, u32[]{:S(2)}) collective-permute-start(f32[8,128]{1,0:T(8,128)S(1)} %add_add_fusion), channel_id=1, source_target_pairs={{0,2},{2,0},{1,3},{3,1},{4,6},{6,4},{5,7},{7,5},{8,10},{10,8},{9,1... | collective-permute-start | bytes 12296 | tf_op jit(solution)/shard_map/ppermute | solution.py:25
  63.9 3.2 %copy-start = (f32[8,16,64,128]{3,2,1,0:T(8,128)S(1)}, f32[8,16,64,128]{3,2,1,0:T(8,128)}, u32[]{:S(2)}) copy-start(f32[8,16,64,128]{3,2,1,0:T(8,128)} %refs_0_.7) | copy-start | bytes 12582916
  65.1 1.8 %collective-permute-start.16 = (f32[776,128]{1,0:T(8,128)S(1)}, f32[776,128]{1,0:T(8,128)S(1)}, u32[]{:S(2)}, u32[]{:S(2)}) collective-permute-start(f32[776,128]{1,0:T(8,128)S(1)} %get-tuple-element.76.own_ref), channel_id=1, source_target_pairs={{0,1},{1,0},{2,3},{3,2},{4,5},{5,4},{6,7},{7,6},{8,9},{9,8},{10,11... | collective-permute-start | bytes 1191944 | tf_op jit(solution)/shard_map/ppermute | solution.py:476
  66.9 6.9 %collective-permute-start.17 = (f32[3080,128]{1,0:T(8,128)S(1)}, f32[3080,128]{1,0:T(8,128)S(1)}, u32[]{:S(2)}, u32[]{:S(2)}) collective-permute-start(f32[3080,128]{1,0:T(8,128)S(1)} %get-tuple-element.77.own_ref.vector_ref.raw_ref), channel_id=1, source_target_pairs={{0,1},{1,0},{2,3},{3,2},{4,5},{5,4},{6,7},{7,6},{8,9},{9,8},{10,11... | collective-permute-start | bytes 4730888 | tf_op jit(solution)/shard_map/ppermute | solution.py:476
  70.8 17.0 %collective-permute-start.18 = (f32[392,128]{1,0:T(8,128)S(1)}, f32[392,128]{1,0:T(8,128)S(1)}, u32[]{:S(2)}, u32[]{:S(2)}) collective-permute-start(f32[392,128]{1,0:T(8,128)S(1)} %get-tuple-element.78), channel_id=1, source_target_pairs={{0,8},{4,12},{8,0},{12,4},{1,9},{5,13},{9,1},{13,5},{2,10},{6,14},... | collective-permute-start | bytes 602120 | tf_op jit(solution)/shard_map/ppermute | solution.py:473
  72.5 19.4 %collective-permute-start.25 = (f32[392,128]{1,0:T(8,128)S(1)}, f32[392,128]{1,0:T(8,128)S(1)}, u32[]{:S(2)}, u32[]{:S(2)}) collective-permute-start(f32[392,128]{1,0:T(8,128)S(1)} %get-tuple-element.91), channel_id=1, source_target_pairs={{0,8},{4,12},{8,0},{12,4},{1,9},{5,13},{9,1},{13,5},{2,10},{6,14},... | collective-permute-start | bytes 602120 | tf_op jit(solution)/shard_map/ppermute | solution.py:473
  84.6 8.5 %collective-permute-start.21 = (f32[384,128]{1,0:T(8,128)S(1)}, f32[384,128]{1,0:T(8,128)S(1)}, u32[]{:S(2)}, u32[]{:S(2)}) collective-permute-start(f32[384,128]{1,0:T(8,128)S(1)} %combine.19.refs_0_), channel_id=1, source_target_pairs={{0,2},{2,0},{1,3},{3,1},{4,6},{6,4},{5,7},{7,5},{8,10},{10,8},{9,1... | collective-permute-start | bytes 589832 | tf_op jit(solution)/shard_map/ppermute | solution.py:25
  86.8 8.8 %collective-permute-start.28 = (f32[384,128]{1,0:T(8,128)S(1)}, f32[384,128]{1,0:T(8,128)S(1)}, u32[]{:S(2)}, u32[]{:S(2)}) collective-permute-start(f32[384,128]{1,0:T(8,128)S(1)} %combine.23.refs_2_), channel_id=1, source_target_pairs={{0,2},{2,0},{1,3},{3,1},{4,6},{6,4},{5,7},{7,5},{8,10},{10,8},{9,1... | collective-permute-start | bytes 589832 | tf_op jit(solution)/shard_map/ppermute | solution.py:25
  87.8 9.2 %collective-permute-start.19 = (f32[392,128]{1,0:T(8,128)S(1)}, f32[392,128]{1,0:T(8,128)S(1)}, u32[]{:S(2)}, u32[]{:S(2)}) collective-permute-start(f32[392,128]{1,0:T(8,128)S(1)} %get-tuple-element.81), channel_id=1, source_target_pairs={{0,4},{4,8},{8,12},{12,0},{1,5},{5,9},{9,13},{13,1},{2,6},{6,10},{... | collective-permute-start | bytes 602120 | tf_op jit(solution)/shard_map/ppermute | solution.py:473
  92.0 9.2 %collective-permute-start.26 = (f32[392,128]{1,0:T(8,128)S(1)}, f32[392,128]{1,0:T(8,128)S(1)}, u32[]{:S(2)}, u32[]{:S(2)}) collective-permute-start(f32[392,128]{1,0:T(8,128)S(1)} %get-tuple-element.92), channel_id=1, source_target_pairs={{0,4},{4,8},{8,12},{12,0},{1,5},{5,9},{9,13},{13,1},{2,6},{6,10},{... | collective-permute-start | bytes 602120 | tf_op jit(solution)/shard_map/ppermute | solution.py:473
  93.2 11.1 %collective-permute-start.22 = (f32[384,128]{1,0:T(8,128)S(1)}, f32[384,128]{1,0:T(8,128)S(1)}, u32[]{:S(2)}, u32[]{:S(2)}) collective-permute-start(f32[384,128]{1,0:T(8,128)S(1)} %combine.18.refs_4_), channel_id=1, source_target_pairs={{0,2},{2,0},{1,3},{3,1},{4,6},{6,4},{5,7},{7,5},{8,10},{10,8},{9,1... | collective-permute-start | bytes 589832 | tf_op jit(solution)/shard_map/ppermute | solution.py:25
  95.5 10.3 %collective-permute-start.29 = (f32[384,128]{1,0:T(8,128)S(1)}, f32[384,128]{1,0:T(8,128)S(1)}, u32[]{:S(2)}, u32[]{:S(2)}) collective-permute-start(f32[384,128]{1,0:T(8,128)S(1)} %combine.22.refs_6_), channel_id=1, source_target_pairs={{0,2},{2,0},{1,3},{3,1},{4,6},{6,4},{5,7},{7,5},{8,10},{10,8},{9,1... | collective-permute-start | bytes 589832 | tf_op jit(solution)/shard_map/ppermute | solution.py:25
  97.0 9.4 %collective-permute-start.20 = (f32[392,128]{1,0:T(8,128)S(1)}, f32[392,128]{1,0:T(8,128)S(1)}, u32[]{:S(2)}, u32[]{:S(2)}) collective-permute-start(f32[392,128]{1,0:T(8,128)S(1)} %get-tuple-element.83), channel_id=1, source_target_pairs={{0,12},{4,0},{8,4},{12,8},{1,13},{5,1},{9,5},{13,9},{2,14},{6,2},{... | collective-permute-start | bytes 602120 | tf_op jit(solution)/shard_map/ppermute | solution.py:473
  101.2 8.0 %collective-permute-start.27 = (f32[392,128]{1,0:T(8,128)S(1)}, f32[392,128]{1,0:T(8,128)S(1)}, u32[]{:S(2)}, u32[]{:S(2)}) collective-permute-start(f32[392,128]{1,0:T(8,128)S(1)} %get-tuple-element.93), channel_id=1, source_target_pairs={{0,12},{4,0},{8,4},{12,8},{1,13},{5,1},{9,5},{13,9},{2,14},{6,2},{... | collective-permute-start | bytes 602120 | tf_op jit(solution)/shard_map/ppermute | solution.py:473
  104.3 7.9 %collective-permute-start.23 = (f32[384,128]{1,0:T(8,128)S(1)}, f32[384,128]{1,0:T(8,128)S(1)}, u32[]{:S(2)}, u32[]{:S(2)}) collective-permute-start(f32[384,128]{1,0:T(8,128)S(1)} %combine.17.refs_8_), channel_id=1, source_target_pairs={{0,2},{2,0},{1,3},{3,1},{4,6},{6,4},{5,7},{7,5},{8,10},{10,8},{9,1... | collective-permute-start | bytes 589832 | tf_op jit(solution)/shard_map/ppermute | solution.py:25
  105.8 10.5 %collective-permute-start.30 = (f32[384,128]{1,0:T(8,128)S(1)}, f32[384,128]{1,0:T(8,128)S(1)}, u32[]{:S(2)}, u32[]{:S(2)}) collective-permute-start(f32[384,128]{1,0:T(8,128)S(1)} %combine.21.refs_10_), channel_id=1, source_target_pairs={{0,2},{2,0},{1,3},{3,1},{4,6},{6,4},{5,7},{7,5},{8,10},{10,8},{9,1... | collective-permute-start | bytes 589832 | tf_op jit(solution)/shard_map/ppermute | solution.py:25
  112.1 9.3 %collective-permute-start.24 = (f32[384,128]{1,0:T(8,128)S(1)}, f32[384,128]{1,0:T(8,128)S(1)}, u32[]{:S(2)}, u32[]{:S(2)}) collective-permute-start(f32[384,128]{1,0:T(8,128)S(1)} %combine.16.refs_0_), channel_id=1, source_target_pairs={{0,2},{2,0},{1,3},{3,1},{4,6},{6,4},{5,7},{7,5},{8,10},{10,8},{9,1... | collective-permute-start | bytes 589832 | tf_op jit(solution)/shard_map/ppermute | solution.py:25
  116.3 7.2 %collective-permute-start.31 = (f32[384,128]{1,0:T(8,128)S(1)}, f32[384,128]{1,0:T(8,128)S(1)}, u32[]{:S(2)}, u32[]{:S(2)}) collective-permute-start(f32[384,128]{1,0:T(8,128)S(1)} %combine.20.refs_2_), channel_id=1, source_target_pairs={{0,2},{2,0},{1,3},{3,1},{4,6},{6,4},{5,7},{7,5},{8,10},{10,8},{9,1... | collective-permute-start | bytes 589832 | tf_op jit(solution)/shard_map/ppermute | solution.py:25

commit v16 on v15

--- a/solution.py
+++ b/solution.py
@@ -463,7 +463,7 @@
     pieces = staying + moving
     ahead_of = len(cuts)
     whole = [pieces[i : i + ahead_of] for i in range(0, len(pieces), ahead_of)]
-    single = [[piece] for piece in pieces]
+    mixed = [[piece] for piece in staying] + whole[1:]
     batches = [moving[:ahead_of], moving[ahead_of:] + staying]
 
     def spans(pieces):
@@ -503,7 +503,7 @@
             if at >= ahead_of:
                 value = after(value, arrived[moving[at - ahead_of]])[0]
             arrived[piece] = relay(value, piece[0])
-        for group in single if second else whole:
+        for group in mixed if second else whole:
             mine, inner = combine(
                 table,
                 spans(group),
@@ -515,8 +515,10 @@
                 second,
                 not second,
             )
-            if len(sums) >= 2 * 2:
-                mine = after(mine, sums[1 - 2 * 2])[0]
+            if second and len(sums) == 2 * ahead_of and ahead_of > 1:
+                mine = after(mine, sums[-1], sums[-3])[0]
+            elif len(sums) >= 4:
+                mine = after(mine, sums[-3])[0]
             sums += add_over_term(mine)
             inners.append(inner)
         return sums, inners, arrived, other
@@ -537,10 +539,11 @@
     scale = jnp.broadcast_to(scale, squares.shape)
     correction = scaled(table, scale, raw, slots, rows)
     sigma = None
-    for some in (slice(0, -ahead_of), slice(-ahead_of, None)):
+    for some in (slice(0, -1), slice(-1, None)):
         parts = [one for pair in list(zip(sums[::2], sums[1::2]))[some] for one in pair]
         if parts:
-            sigma = finish(table, spans(pieces[some]), scale, parts, sigma, slots, rows)
+            spans_of = [(group[0][1], sum(one[2] for one in group)) for group in mixed[some]]
+            sigma = finish(table, spans_of, scale, parts, sigma, slots, rows)
     return tuple(
         jnp.transpose(value.reshape(slots, roots, rows, width), (0, 2, 1, 3))
         for value in (sigma, correction)

time: 125 us -> 125 us (level)
  waiting for transfers between devices: 33.6 us -> 38.5 us
  starting transfers between devices: 42.2 us -> 38.5 us
  Pallas kernels: 45.6 us -> 44 us
    ppermute x17 -> x14, starting transfers between devices: 21.3 us -> 17.6 us  [flip(): return lax.ppermute(value, axis, [(i, i ^ bit) for i in range(size)])]
    ppermute x17 -> x14, waiting for transfers between devices: 15.9 us -> 19.2 us  [flip(): return lax.ppermute(value, axis, [(i, i ^ bit) for i in range(size)])]
    ppermute x12, waiting for transfers between devices: 16 us -> 17.6 us  [relay(): lax.ppermute(value, 'blk', [(p, (p + c) % devices) for p in range(devices)])]
    pallas_call x12 -> x9, Pallas kernels: 7.36 us -> 5.71 us  [combine(): pl.pallas_call(functools.partial(combine_kernel, share, pieces, ordered,...]
  transfers between devices with their start and end apart: 32 -> 29, of which waited for: 18 -> 18; matrix products, arithmetic and copies ran while one was open for 1% -> 1% of each run, Pallas kernels for 30% -> 29%
where the time goes in v16:
time: 125 us; the launch traced here: 124 us
  Pallas kernels  44 us (35%)
  starting transfers between devices  38.5 us (31%)
  waiting for transfers between devices  38.5 us (31%)
  local copies, waits for them, and re-layouts  1.51 us (1%)
    pallas_call x4, Pallas kernels, sectors(): pl.pallas_call(functools.partial(sector_kernel, count, terms, unroll, hei...  30.7 us
    ppermute x12, starting transfers between devices, relay(): lax.ppermute(value, 'blk', [(p, (p + c) % devices) for p in range(devices)])  20.1 us
    ppermute x14, waiting for transfers between devices, flip(): return lax.ppermute(value, axis, [(i, i ^ bit) for i in range(size)])  19.2 us
    ppermute x14, starting transfers between devices, flip(): return lax.ppermute(value, axis, [(i, i ^ bit) for i in range(size)])  17.6 us
    ppermute x12, waiting for transfers between devices, relay(): lax.ppermute(value, 'blk', [(p, (p + c) % devices) for p in range(devices)])  17.6 us
    pallas_call x9, Pallas kernels, combine(): pl.pallas_call(functools.partial(combine_kernel, share, pieces, ordered,...  5.71 us
    pallas_call x2, Pallas kernels, finish(): pl.pallas_call(functools.partial(finish_kernel, count, rows, [size for _,...  2.99 us
  transfers between devices with their start and end apart: 29, of which 18 were waited for; matrix products, arithmetic and copies ran while one was open for 1% of the time, Pallas kernels for 29%

profile of v16, /device:TPU:0, one launch (start us, length us, event | category | flops | bytes accessed | tf_op | source)
XLA Modules:
  0.0 124.4 jit_solution(990502673899543652)
XLA Ops:
  1.1 0.7 pad_add_fusion.given_hbm
  1.9 1.4 %copy-done.1 = f32[16,64,3,128]{3,1,2,0:T(8,128)S(1)} copy-done((f32[16,64,3,128]{3,1,2,0:T(8,128)S(1)}, f32[16,64,3,128]{3,1,2,0:T(8,128)}, u32[]{:S(2)}) %copy-start.1) | copy-done | bytes 1572888
  3.3 1.5 %table.1 = s32[57]{0:T(128)S(1)} custom-call(s32[24]{0:T(128)S(1)} %pad_add_fusion.given_hbm, f32[3072,128]{1,0:T(8,128)S(1)} %bitcast.12), custom_call_target="tpu_custom_call" | custom-call | tf_op jit(solution)/shard_map/table/pallas_call | solution.py:78
  4.8 5.1 %sectors.4 = (f32[384,128]{1,0:T(8,128)S(1)}, f32[384,128]{1,0:T(8,128)S(1)}, f32[3072,128]{1,0:T(8,128)S(1)}) custom-call(s32[57]{0:T(128)S(1)} %table.1, f32[3072,128]{1,0:T(8,128)S(1)} %bitcast.13, f32[3072,128]{1,0:T(8,128)S(1)} %collective-permute-done.other_ref, f32[8,16,64,128]{3,2,1,0:T(8,128)} %refs_0_.7, f32[8,16,128,128]{3,2,1,0:T(8,128)} %refs_1_.7, ...), custom_call_target="tpu_custom_call" | custom-call | tf_op jit(solution)/shard_map/sectors/pallas_call | solution.py:221
  10.0 3.7 %collective-permute-start.1 = (f32[384,128]{1,0:T(8,128)S(1)}, f32[384,128]{1,0:T(8,128)S(1)}, u32[]{:S(2)}, u32[]{:S(2)}) collective-permute-start(f32[384,128]{1,0:T(8,128)S(1)} %get-tuple-element.52), channel_id=1, source_target_pairs={{0,8},{4,12},{8,0},{12,4},{1,9},{5,13},{9,1},{13,5},{2,10},{6,14},... | collective-permute-start | bytes 589832 | tf_op jit(solution)/shard_map/ppermute | solution.py:473
  13.9 11.6 %sectors.5 = (f32[384,128]{1,0:T(8,128)S(1)}, f32[384,128]{1,0:T(8,128)S(1)}, f32[384,128]{1,0:T(8,128)S(1)}, f32[384,128]{1,0:T(8,128)S(1)}, f32[384,128]{1,0:T...) custom-call(s32[57]{0:T(128)S(1)} %table.1, ...), custom_call_target="tpu_custom_call", output_to_operand_aliasing={{6}: (7, {})} | custom-call | tf_op jit(solution)/shard_map/sectors/pallas_call | solution.py:221
  25.6 0.7 combine.9
  26.2 1.8 %collective-permute-start.11 = (f32[768,128]{1,0:T(8,128)S(1)}, f32[768,128]{1,0:T(8,128)S(1)}, u32[]{:S(2)}, u32[]{:S(2)}) collective-permute-start(f32[768,128]{1,0:T(8,128)S(1)} %get-tuple-element.66.rest_0_), channel_id=1, source_target_pairs={{0,2},{2,0},{1,3},{3,1},{4,6},{6,4},{5,7},{7,5},{8,10},{10,8},{9,1... | collective-permute-start | bytes 1179656 | tf_op jit(solution)/shard_map/ppermute | solution.py:25
  28.1 1.6 %collective-permute-start.3 = (f32[384,128]{1,0:T(8,128)S(1)}, f32[384,128]{1,0:T(8,128)S(1)}, u32[]{:S(2)}, u32[]{:S(2)}) collective-permute-start(f32[384,128]{1,0:T(8,128)S(1)} %get-tuple-element.56), channel_id=1, source_target_pairs={{0,4},{4,8},{8,12},{12,0},{1,5},{5,9},{9,13},{13,1},{2,6},{6,10},{... | collective-permute-start | bytes 589832 | tf_op jit(solution)/shard_map/ppermute | solution.py:473
  29.6 2.2 %collective-permute-done.2.refs_1_ = f32[384,128]{1,0:T(8,128)S(1)} collective-permute-done((f32[384,128]{1,0:T(8,128)S(1)}, f32[384,128]{1,0:T(8,128)S(1)}, u32[]{:S(2)}, u32[]{:S(2)}) %collective-permute-start.2) | collective-permute-done | bytes 196640 | tf_op jit(solution)/shard_map/ppermute | solution.py:473
  31.9 0.8 collective-permute-start.4
  33.3 1.6 %collective-permute-start.14 = (f32[768,128]{1,0:T(8,128)S(1)}, f32[768,128]{1,0:T(8,128)S(1)}, u32[]{:S(2)}, u32[]{:S(2)}) collective-permute-start(f32[768,128]{1,0:T(8,128)S(1)} %get-tuple-element.69.rest_2_), channel_id=1, source_target_pairs={{0,2},{2,0},{1,3},{3,1},{4,6},{6,4},{5,7},{7,5},{8,10},{10,8},{9,1... | collective-permute-start | bytes 1179656 | tf_op jit(solution)/shard_map/ppermute | solution.py:25
  34.9 1.5 %collective-permute-done.3.refs_0_ = f32[384,128]{1,0:T(8,128)S(1)} collective-permute-done((f32[384,128]{1,0:T(8,128)S(1)}, f32[384,128]{1,0:T(8,128)S(1)}, u32[]{:S(2)}, u32[]{:S(2)}) %collective-permute-start.3) | collective-permute-done | bytes 196640 | tf_op jit(solution)/shard_map/ppermute | solution.py:473
  36.4 3.3 %collective-permute-start.5 = (f32[384,128]{1,0:T(8,128)S(1)}, f32[384,128]{1,0:T(8,128)S(1)}, u32[]{:S(2)}, u32[]{:S(2)}) collective-permute-start(f32[384,128]{1,0:T(8,128)S(1)} %get-tuple-element.61), channel_id=1, source_target_pairs={{0,12},{4,0},{8,4},{12,8},{1,13},{5,1},{9,5},{13,9},{2,14},{6,2},{... | collective-permute-start | bytes 589832 | tf_op jit(solution)/shard_map/ppermute | solution.py:473
  39.7 1.1 collective-permute-done.4.refs_1_
  40.8 3.1 %collective-permute-start.6 = (f32[384,128]{1,0:T(8,128)S(1)}, f32[384,128]{1,0:T(8,128)S(1)}, u32[]{:S(2)}, u32[]{:S(2)}) collective-permute-start(f32[384,128]{1,0:T(8,128)S(1)} %get-tuple-element.63), channel_id=1, source_target_pairs={{0,12},{4,0},{8,4},{12,8},{1,13},{5,1},{9,5},{13,9},{2,14},{6,2},{... | collective-permute-start | bytes 589832 | tf_op jit(solution)/shard_map/ppermute | solution.py:473
  44.5 1.5 %collective-permute-start.12 = (f32[768,128]{1,0:T(8,128)S(1)}, f32[768,128]{1,0:T(8,128)S(1)}, u32[]{:S(2)}, u32[]{:S(2)}) collective-permute-start(f32[768,128]{1,0:T(8,128)S(1)} %get-tuple-element.67.rest_4_), channel_id=1, source_target_pairs={{0,2},{2,0},{1,3},{3,1},{4,6},{6,4},{5,7},{7,5},{8,10},{10,8},{9,1... | collective-permute-start | bytes 1179656 | tf_op jit(solution)/shard_map/ppermute | solution.py:25
  46.1 2.9 %collective-permute-done.6.refs_1_ = f32[384,128]{1,0:T(8,128)S(1)} collective-permute-done((f32[384,128]{1,0:T(8,128)S(1)}, f32[384,128]{1,0:T(8,128)S(1)}, u32[]{:S(2)}, u32[]{:S(2)}) %collective-permute-start.6) | collective-permute-done | bytes 196640 | tf_op jit(solution)/shard_map/ppermute | solution.py:473
  49.0 0.7 combine.12
  49.7 1.5 %collective-permute-start.15 = (f32[768,128]{1,0:T(8,128)S(1)}, f32[768,128]{1,0:T(8,128)S(1)}, u32[]{:S(2)}, u32[]{:S(2)}) collective-permute-start(f32[768,128]{1,0:T(8,128)S(1)} %get-tuple-element.71.rest_6_), channel_id=1, source_target_pairs={{0,2},{2,0},{1,3},{3,1},{4,6},{6,4},{5,7},{7,5},{8,10},{10,8},{9,1... | collective-permute-start | bytes 1179656 | tf_op jit(solution)/shard_map/ppermute | solution.py:25
  51.2 1.2 collective-permute-done.7
  52.4 3.5 %collective-permute-start.10 = (f32[8,128]{1,0:T(8,128)S(1)}, f32[8,128]{1,0:T(8,128)S(1)}, u32[]{:S(2)}, u32[]{:S(2)}) collective-permute-start(f32[8,128]{1,0:T(8,128)S(1)} %add.63), channel_id=1, source_target_pairs={{0,12},{4,8},{8,4},{12,0},{1,13},{5,9},{9,5},{13,1},{2,14},{6,10},... | collective-permute-start | bytes 12296 | tf_op jit(solution)/shard_map/ppermute | solution.py:25
  55.9 0.9 collective-permute-start.8
  56.8 1.0 collective-permute-done.10
  57.8 2.6 %collective-permute-done.9 = f32[8,128]{1,0:T(8,128)S(1)} collective-permute-done((f32[8,128]{1,0:T(8,128)S(1)}, f32[8,128]{1,0:T(8,128)S(1)}, u32[]{:S(2)}, u32[]{:S(2)}) %collective-permute-start.9) | collective-permute-done | bytes 4128 | tf_op jit(solution)/shard_map/ppermute | solution.py:25
  61.0 3.1 %collective-permute-done.13 = f32[8,128]{1,0:T(8,128)S(1)} collective-permute-done((f32[8,128]{1,0:T(8,128)S(1)}, f32[8,128]{1,0:T(8,128)S(1)}, u32[]{:S(2)}, u32[]{:S(2)}) %collective-permute-start.13) | collective-permute-done | bytes 4128 | tf_op jit(solution)/shard_map/ppermute | solution.py:25
  64.1 1.3 %correct.1 = (f32[3080,128]{1,0:T(8,128)S(1)}, f32[776,128]{1,0:T(8,128)S(1)}) custom-call(s32[57]{0:T(128)S(1)} %table.1, f32[8,128]{1,0:T(8,128)S(1)} %add.67.inner_ref, f32[3072,128]{1,0:T(8,128)S(1)} %bitcast.19, f32[16,64,128]{2,1,0:T(8,128)S(1)} %broadcast_add_fusion.diag_ref, f32[768,128]{1,0:T(8,128)S(1)} %get-tuple-element.66.rest_0_, ...), custom_call_target="tpu_custom_call" | custom-call | tf_op jit(solution)/shard_map/correct/pallas_call | solution.py:333
  65.4 1.7 %collective-permute-done.16.other_ref = f32[776,128]{1,0:T(8,128)S(1)} collective-permute-done((f32[776,128]{1,0:T(8,128)S(1)}, f32[776,128]{1,0:T(8,128)S(1)}, u32[]{:S(2)}, u32[]{:S(2)}) %collective-permute-start.16) | collective-permute-done | bytes 397344 | tf_op jit(solution)/shard_map/ppermute | solution.py:476
  67.3 3.8 %sectors.6 = (f32[392,128]{1,0:T(8,128)S(1)}, f32[392,128]{1,0:T(8,128)S(1)}, f32[3072,128]{1,0:T(8,128)S(1)}) custom-call(s32[57]{0:T(128)S(1)} %table.1, f32[776,128]{1,0:T(8,128)S(1)} %get-tuple-element.73.own_ref, f32[776,128]{1,0:T(8,128)S(1)} %collective-permute-done.16.other_ref, f32[8,16,64,128]{3,2,1,0:T(8,128)S(1)} %copy-done, ...), custom_call_target="tpu_custom_call" | custom-call | tf_op jit(solution)/shard_map/sectors/pallas_call | solution.py:221
  71.0 2.1 %collective-permute-start.21 = (f32[392,128]{1,0:T(8,128)S(1)}, f32[392,128]{1,0:T(8,128)S(1)}, u32[]{:S(2)}, u32[]{:S(2)}) collective-permute-start(f32[392,128]{1,0:T(8,128)S(1)} %get-tuple-element.84), channel_id=1, source_target_pairs={{0,8},{4,12},{8,0},{12,4},{1,9},{5,13},{9,1},{13,5},{2,10},{6,14},... | collective-permute-start | bytes 602120 | tf_op jit(solution)/shard_map/ppermute | solution.py:473
  73.1 0.9 collective-permute-start.18
  74.0 10.2 %sectors.7 = (f32[392,128]{1,0:T(8,128)S(1)}, f32[392,128]{1,0:T(8,128)S(1)}, f32[392,128]{1,0:T(8,128)S(1)}, f32[392,128]{1,0:T(8,128)S(1)}, f32[384,128]{1,0:T...) custom-call(s32[57]{0:T(128)S(1)} %table.1, ...), custom_call_target="tpu_custom_call", output_to_operand_aliasing={{6}: (5, {})} | custom-call | tf_op jit(solution)/shard_map/sectors/pallas_call | solution.py:221
  85.4 1.3 %collective-permute-start.25 = (f32[384,128]{1,0:T(8,128)S(1)}, f32[384,128]{1,0:T(8,128)S(1)}, u32[]{:S(2)}, u32[]{:S(2)}) collective-permute-start(f32[384,128]{1,0:T(8,128)S(1)} %combine.16.refs_0_), channel_id=1, source_target_pairs={{0,2},{2,0},{1,3},{3,1},{4,6},{6,4},{5,7},{7,5},{8,10},{10,8},{9,1... | collective-permute-start | bytes 589832 | tf_op jit(solution)/shard_map/ppermute | solution.py:25
  86.8 0.8 collective-permute-start.24
  88.0 4.0 %collective-permute-done.18.refs_0_ = f32[392,128]{1,0:T(8,128)S(1)} collective-permute-done((f32[392,128]{1,0:T(8,128)S(1)}, f32[392,128]{1,0:T(8,128)S(1)}, u32[]{:S(2)}, u32[]{:S(2)}) %collective-permute-start.18) | collective-permute-done | bytes 200736 | tf_op jit(solution)/shard_map/ppermute | solution.py:473
  93.3 3.0 %collective-permute-done.24.refs_3_ = f32[384,128]{1,0:T(8,128)S(1)} collective-permute-done((f32[384,128]{1,0:T(8,128)S(1)}, f32[384,128]{1,0:T(8,128)S(1)}, u32[]{:S(2)}, u32[]{:S(2)}) %collective-permute-start.24) | collective-permute-done | bytes 196640 | tf_op jit(solution)/shard_map/ppermute | solution.py:25
  96.3 1.3 %collective-permute-start.26 = (f32[768,128]{1,0:T(8,128)S(1)}, f32[768,128]{1,0:T(8,128)S(1)}, u32[]{:S(2)}, u32[]{:S(2)}) collective-permute-start(f32[768,128]{1,0:T(8,128)S(1)} %combine.14.refs_4_), channel_id=1, source_target_pairs={{0,2},{2,0},{1,3},{3,1},{4,6},{6,4},{5,7},{7,5},{8,10},{10,8},{9,1... | collective-permute-start | bytes 1179656 | tf_op jit(solution)/shard_map/ppermute | solution.py:25
  97.6 2.6 %collective-permute-start.23 = (f32[392,128]{1,0:T(8,128)S(1)}, f32[392,128]{1,0:T(8,128)S(1)}, u32[]{:S(2)}, u32[]{:S(2)}) collective-permute-start(f32[392,128]{1,0:T(8,128)S(1)} %get-tuple-element.86), channel_id=1, source_target_pairs={{0,12},{4,0},{8,4},{12,8},{1,13},{5,1},{9,5},{13,9},{2,14},{6,2},{... | collective-permute-start | bytes 602120 | tf_op jit(solution)/shard_map/ppermute | solution.py:473
  100.2 1.5 %collective-permute-done.19.refs_0_ = f32[392,128]{1,0:T(8,128)S(1)} collective-permute-done((f32[392,128]{1,0:T(8,128)S(1)}, f32[392,128]{1,0:T(8,128)S(1)}, u32[]{:S(2)}, u32[]{:S(2)}) %collective-permute-start.19) | collective-permute-done | bytes 200736 | tf_op jit(solution)/shard_map/ppermute | solution.py:473
  101.7 1.5 %collective-permute-start.20 = (f32[392,128]{1,0:T(8,128)S(1)}, f32[392,128]{1,0:T(8,128)S(1)}, u32[]{:S(2)}, u32[]{:S(2)}) collective-permute-start(f32[392,128]{1,0:T(8,128)S(1)} %get-tuple-element.80), channel_id=1, source_target_pairs={{0,12},{4,0},{8,4},{12,8},{1,13},{5,1},{9,5},{13,9},{2,14},{6,2},{... | collective-permute-start | bytes 602120 | tf_op jit(solution)/shard_map/ppermute | solution.py:473
  103.8 1.4 %collective-permute-start.28 = (f32[768,128]{1,0:T(8,128)S(1)}, f32[768,128]{1,0:T(8,128)S(1)}, u32[]{:S(2)}, u32[]{:S(2)}) collective-permute-start(f32[768,128]{1,0:T(8,128)S(1)} %combine.17.refs_6_), channel_id=1, source_target_pairs={{0,2},{2,0},{1,3},{3,1},{4,6},{6,4},{5,7},{7,5},{8,10},{10,8},{9,1... | collective-permute-start | bytes 1179656 | tf_op jit(solution)/shard_map/ppermute | solution.py:25
  105.8 3.6 %collective-permute-done.20.refs_0_ = f32[392,128]{1,0:T(8,128)S(1)} collective-permute-done((f32[392,128]{1,0:T(8,128)S(1)}, f32[392,128]{1,0:T(8,128)S(1)}, u32[]{:S(2)}, u32[]{:S(2)}) %collective-permute-start.20) | collective-permute-done | bytes 200736 | tf_op jit(solution)/shard_map/ppermute | solution.py:473
  110.0 1.4 %collective-permute-start.27 = (f32[768,128]{1,0:T(8,128)S(1)}, f32[768,128]{1,0:T(8,128)S(1)}, u32[]{:S(2)}, u32[]{:S(2)}) collective-permute-start(f32[768,128]{1,0:T(8,128)S(1)} %combine.13.refs_0_), channel_id=1, source_target_pairs={{0,2},{2,0},{1,3},{3,1},{4,6},{6,4},{5,7},{7,5},{8,10},{10,8},{9,1... | collective-permute-start | bytes 1179656 | tf_op jit(solution)/shard_map/ppermute | solution.py:25
  111.6 1.8 %scaled.1 = f32[3072,128]{1,0:T(8,128)} custom-call(s32[57]{0:T(128)S(1)} %table.1, f32[8,128]{1,0:T(8,128)S(1)} %broadcast_in_dim.2.scale_ref, f32[3080,128]{1,0:T(8,128)S(1)} %get-tuple-element.74.own_ref.vector_ref.raw_ref), custom_call_target="tpu_custom_call" | custom-call | tf_op jit(solution)/shard_map/scaled/pallas_call | solution.py:378
  113.5 2.5 %collective-permute-done.28.refs_7_ = f32[768,128]{1,0:T(8,128)S(1)} collective-permute-done((f32[768,128]{1,0:T(8,128)S(1)}, f32[768,128]{1,0:T(8,128)S(1)}, u32[]{:S(2)}, u32[]{:S(2)}) %collective-permute-start.28) | collective-permute-done | bytes 393248 | tf_op jit(solution)/shard_map/ppermute | solution.py:25
  115.9 1.7 %finish.2.refs_2_ = f32[3072,128]{1,0:T(8,128)} custom-call(s32[57]{0:T(128)S(1)} %table.1, f32[8,128]{1,0:T(8,128)S(1)} %broadcast_in_dim.2.scale_ref, f32[384,128]{1,0:T(8,128)S(1)} %combine.16.refs_0_, f32[384,128]{1,0:T(8,128)S(1)} %collective-permute-done.25.refs_1_, f32[384,128]{1,0:T(8,128)S(1)} %combine.15.refs_2_, ...), custom_call_target="tpu_custom_call" | custom-call | tf_op jit(solution)/shard_map/finish/pallas_call | solution.py:419
  117.6 5.5 %collective-permute-done.27.refs_1_ = f32[768,128]{1,0:T(8,128)S(1)} collective-permute-done((f32[768,128]{1,0:T(8,128)S(1)}, f32[768,128]{1,0:T(8,128)S(1)}, u32[]{:S(2)}, u32[]{:S(2)}) %collective-permute-start.27) | collective-permute-done | bytes 393248 | tf_op jit(solution)/shard_map/ppermute | solution.py:25
  123.1 1.3 %finish.3 = f32[3072,128]{1,0:T(8,128)} custom-call(s32[57]{0:T(128)S(1)} %table.1, f32[8,128]{1,0:T(8,128)S(1)} %broadcast_in_dim.2.scale_ref, f32[768,128]{1,0:T(8,128)S(1)} %combine.13.refs_0_, f32[768,128]{1,0:T(8,128)S(1)} %collective-permute-done.27.refs_1_, f32[3072,128]{1,0:T(8,128)} %finish.2.refs_2_), custom_call_target="tpu_custom_call", output_to_operand_aliasing={{}: (4, {})} | custom-call | tf_op jit(solution)/shard_map/finish/pallas_call | solution.py:419
  (52 shorter events, 7.9 us)
Async XLA Ops:
  0.6 4.2 %collective-permute-start = (f32[3072,128]{1,0:T(8,128)}, f32[3072,128]{1,0:T(8,128)S(1)}, u32[]{:S(2)}, u32[]{:S(2)}) collective-permute-start(f32[3072,128]{1,0:T(8,128)} %bitcast.11), channel_id=1, source_target_pairs={{0,1},{1,0},{2,3},{3,2},{4,5},{5,4},{6,7},{7,6},{8,9},{9,8},{10,11... | collective-permute-start | bytes 4718600 | tf_op jit(solution)/shard_map/ppermute | solution.py:476
  1.9 1.4 %copy-start.1 = (f32[16,64,3,128]{3,1,2,0:T(8,128)S(1)}, f32[16,64,3,128]{3,1,2,0:T(8,128)}, u32[]{:S(2)}) copy-start(f32[16,64,3,128]{3,1,2,0:T(8,128)} %param.7) | copy-start | bytes 4718596
  3.3 1.5 %copy-start.2 = (f32[16,64,3,128]{3,1,2,0:T(8,128)S(1)}, f32[16,64,3,128]{3,1,2,0:T(8,128)}, u32[]{:S(2)}) copy-start(f32[16,64,3,128]{3,1,2,0:T(8,128)} %param.7) | copy-start | bytes 4718596
  4.8 8.9 %copy-start.3 = (f32[16,128]{1,0:T(8,128)S(1)}, f32[16,128]{1,0:T(8,128)}, u32[]{:S(2)}) copy-start(f32[16,128]{1,0:T(8,128)} %param.13) | copy-start | bytes 24580
  4.8 8.9 %copy-start.4 = (f32[16,64]{1,0:T(8,128)S(1)}, f32[16,64]{1,0:T(8,128)}, u32[]{:S(2)}) copy-start(f32[16,64]{1,0:T(8,128)} %param.12) | copy-start | bytes 12292
  10.0 18.1 %collective-permute-start.1 = (f32[384,128]{1,0:T(8,128)S(1)}, f32[384,128]{1,0:T(8,128)S(1)}, u32[]{:S(2)}, u32[]{:S(2)}) collective-permute-start(f32[384,128]{1,0:T(8,128)S(1)} %get-tuple-element.52), channel_id=1, source_target_pairs={{0,8},{4,12},{8,0},{12,4},{1,9},{5,13},{9,1},{13,5},{2,10},{6,14},... | collective-permute-start | bytes 589832 | tf_op jit(solution)/shard_map/ppermute | solution.py:473
  13.7 18.2 %collective-permute-start.2 = (f32[384,128]{1,0:T(8,128)S(1)}, f32[384,128]{1,0:T(8,128)S(1)}, u32[]{:S(2)}, u32[]{:S(2)}) collective-permute-start(f32[384,128]{1,0:T(8,128)S(1)} %get-tuple-element.53), channel_id=1, source_target_pairs={{0,8},{4,12},{8,0},{12,4},{1,9},{5,13},{9,1},{13,5},{2,10},{6,14},... | collective-permute-start | bytes 589832 | tf_op jit(solution)/shard_map/ppermute | solution.py:473
  26.2 18.3 %collective-permute-start.11 = (f32[768,128]{1,0:T(8,128)S(1)}, f32[768,128]{1,0:T(8,128)S(1)}, u32[]{:S(2)}, u32[]{:S(2)}) collective-permute-start(f32[768,128]{1,0:T(8,128)S(1)} %get-tuple-element.66.rest_0_), channel_id=1, source_target_pairs={{0,2},{2,0},{1,3},{3,1},{4,6},{6,4},{5,7},{7,5},{8,10},{10,8},{9,1... | collective-permute-start | bytes 1179656 | tf_op jit(solution)/shard_map/ppermute | solution.py:25
  28.1 8.3 %collective-permute-start.3 = (f32[384,128]{1,0:T(8,128)S(1)}, f32[384,128]{1,0:T(8,128)S(1)}, u32[]{:S(2)}, u32[]{:S(2)}) collective-permute-start(f32[384,128]{1,0:T(8,128)S(1)} %get-tuple-element.56), channel_id=1, source_target_pairs={{0,4},{4,8},{8,12},{12,0},{1,5},{5,9},{9,13},{13,1},{2,6},{6,10},{... | collective-permute-start | bytes 589832 | tf_op jit(solution)/shard_map/ppermute | solution.py:473
  31.9 8.9 %collective-permute-start.4 = (f32[384,128]{1,0:T(8,128)S(1)}, f32[384,128]{1,0:T(8,128)S(1)}, u32[]{:S(2)}, u32[]{:S(2)}) collective-permute-start(f32[384,128]{1,0:T(8,128)S(1)} %get-tuple-element.58), channel_id=1, source_target_pairs={{0,4},{4,8},{8,12},{12,0},{1,5},{5,9},{9,13},{13,1},{2,6},{6,10},{... | collective-permute-start | bytes 589832 | tf_op jit(solution)/shard_map/ppermute | solution.py:473
  32.6 34.6 %slice-start = ((s8[8388608]{0:T(1024)(128)(4,1)}), s8[4194304]{0:T(1024)(128)(4,1)S(1)}, s32[]{:S(2)}) async-start(s8[8388608]{0:T(1024)(128)(4,1)} %bitcast.9), calls=%async_computation | async-start | bytes 8388608
  33.3 16.4 %collective-permute-start.14 = (f32[768,128]{1,0:T(8,128)S(1)}, f32[768,128]{1,0:T(8,128)S(1)}, u32[]{:S(2)}, u32[]{:S(2)}) collective-permute-start(f32[768,128]{1,0:T(8,128)S(1)} %get-tuple-element.69.rest_2_), channel_id=1, source_target_pairs={{0,2},{2,0},{1,3},{3,1},{4,6},{6,4},{5,7},{7,5},{8,10},{10,8},{9,1... | collective-permute-start | bytes 1179656 | tf_op jit(solution)/shard_map/ppermute | solution.py:25
  36.4 9.7 %collective-permute-start.5 = (f32[384,128]{1,0:T(8,128)S(1)}, f32[384,128]{1,0:T(8,128)S(1)}, u32[]{:S(2)}, u32[]{:S(2)}) collective-permute-start(f32[384,128]{1,0:T(8,128)S(1)} %get-tuple-element.61), channel_id=1, source_target_pairs={{0,12},{4,0},{8,4},{12,8},{1,13},{5,1},{9,5},{13,9},{2,14},{6,2},{... | collective-permute-start | bytes 589832 | tf_op jit(solution)/shard_map/ppermute | solution.py:473
  40.8 8.2 %collective-permute-start.6 = (f32[384,128]{1,0:T(8,128)S(1)}, f32[384,128]{1,0:T(8,128)S(1)}, u32[]{:S(2)}, u32[]{:S(2)}) collective-permute-start(f32[384,128]{1,0:T(8,128)S(1)} %get-tuple-element.63), channel_id=1, source_target_pairs={{0,12},{4,0},{8,4},{12,8},{1,13},{5,1},{9,5},{13,9},{2,14},{6,2},{... | collective-permute-start | bytes 589832 | tf_op jit(solution)/shard_map/ppermute | solution.py:473
  44.5 22.8 %slice-start.1 = ((s8[8388608]{0:T(1024)(128)(4,1)}), s8[4194304]{0:T(1024)(128)(4,1)S(1)}, s32[]{:S(2)}) async-start(s8[8388608]{0:T(1024)(128)(4,1)} %bitcast.9), calls=%async_computation.1 | async-start | bytes 8388608
  44.5 15.9 %collective-permute-start.12 = (f32[768,128]{1,0:T(8,128)S(1)}, f32[768,128]{1,0:T(8,128)S(1)}, u32[]{:S(2)}, u32[]{:S(2)}) collective-permute-start(f32[768,128]{1,0:T(8,128)S(1)} %get-tuple-element.67.rest_4_), channel_id=1, source_target_pairs={{0,2},{2,0},{1,3},{3,1},{4,6},{6,4},{5,7},{7,5},{8,10},{10,8},{9,1... | collective-permute-start | bytes 1179656 | tf_op jit(solution)/shard_map/ppermute | solution.py:25
  49.7 14.4 %collective-permute-start.15 = (f32[768,128]{1,0:T(8,128)S(1)}, f32[768,128]{1,0:T(8,128)S(1)}, u32[]{:S(2)}, u32[]{:S(2)}) collective-permute-start(f32[768,128]{1,0:T(8,128)S(1)} %get-tuple-element.71.rest_6_), channel_id=1, source_target_pairs={{0,2},{2,0},{1,3},{3,1},{4,6},{6,4},{5,7},{7,5},{8,10},{10,8},{9,1... | collective-permute-start | bytes 1179656 | tf_op jit(solution)/shard_map/ppermute | solution.py:25
  51.2 1.2 collective-permute-start.7
  52.4 5.4 %collective-permute-start.10 = (f32[8,128]{1,0:T(8,128)S(1)}, f32[8,128]{1,0:T(8,128)S(1)}, u32[]{:S(2)}, u32[]{:S(2)}) collective-permute-start(f32[8,128]{1,0:T(8,128)S(1)} %add.63), channel_id=1, source_target_pairs={{0,12},{4,8},{8,4},{12,0},{1,13},{5,9},{9,5},{13,1},{2,14},{6,10},... | collective-permute-start | bytes 12296 | tf_op jit(solution)/shard_map/ppermute | solution.py:25
  55.9 4.5 %collective-permute-start.9 = (f32[8,128]{1,0:T(8,128)S(1)}, f32[8,128]{1,0:T(8,128)S(1)}, u32[]{:S(2)}, u32[]{:S(2)}) collective-permute-start(f32[8,128]{1,0:T(8,128)S(1)} %add.63), channel_id=1, source_target_pairs={{0,8},{4,12},{8,0},{12,4},{1,9},{5,13},{9,1},{13,5},{2,10},{6,14},... | collective-permute-start | bytes 12296 | tf_op jit(solution)/shard_map/ppermute | solution.py:25
  55.9 4.5 %collective-permute-start.8 = (f32[8,128]{1,0:T(8,128)S(1)}, f32[8,128]{1,0:T(8,128)S(1)}, u32[]{:S(2)}, u32[]{:S(2)}) collective-permute-start(f32[8,128]{1,0:T(8,128)S(1)} %add.63), channel_id=1, source_target_pairs={{0,4},{4,0},{8,12},{12,8},{1,5},{5,1},{9,13},{13,9},{2,6},{6,2},{1... | collective-permute-start | bytes 12296 | tf_op jit(solution)/shard_map/ppermute | solution.py:25
  60.4 3.7 %collective-permute-start.13 = (f32[8,128]{1,0:T(8,128)S(1)}, f32[8,128]{1,0:T(8,128)S(1)}, u32[]{:S(2)}, u32[]{:S(2)}) collective-permute-start(f32[8,128]{1,0:T(8,128)S(1)} %add_add_fusion), channel_id=1, source_target_pairs={{0,2},{2,0},{1,3},{3,1},{4,6},{6,4},{5,7},{7,5},{8,10},{10,8},{9,1... | collective-permute-start | bytes 12296 | tf_op jit(solution)/shard_map/ppermute | solution.py:25
  64.1 3.2 %copy-start = (f32[8,16,64,128]{3,2,1,0:T(8,128)S(1)}, f32[8,16,64,128]{3,2,1,0:T(8,128)}, u32[]{:S(2)}) copy-start(f32[8,16,64,128]{3,2,1,0:T(8,128)} %refs_0_.7) | copy-start | bytes 12582916
  65.3 1.8 %collective-permute-start.16 = (f32[776,128]{1,0:T(8,128)S(1)}, f32[776,128]{1,0:T(8,128)S(1)}, u32[]{:S(2)}, u32[]{:S(2)}) collective-permute-start(f32[776,128]{1,0:T(8,128)S(1)} %get-tuple-element.73.own_ref), channel_id=1, source_target_pairs={{0,1},{1,0},{2,3},{3,2},{4,5},{5,4},{6,7},{7,6},{8,9},{9,8},{10,11... | collective-permute-start | bytes 1191944 | tf_op jit(solution)/shard_map/ppermute | solution.py:476
  67.1 6.9 %collective-permute-start.17 = (f32[3080,128]{1,0:T(8,128)S(1)}, f32[3080,128]{1,0:T(8,128)S(1)}, u32[]{:S(2)}, u32[]{:S(2)}) collective-permute-start(f32[3080,128]{1,0:T(8,128)S(1)} %get-tuple-element.74.own_ref.vector_ref.raw_ref), channel_id=1, source_target_pairs={{0,1},{1,0},{2,3},{3,2},{4,5},{5,4},{6,7},{7,6},{8,9},{9,8},{10,11... | collective-permute-start | bytes 4730888 | tf_op jit(solution)/shard_map/ppermute | solution.py:476
  71.0 16.7 %collective-permute-start.21 = (f32[392,128]{1,0:T(8,128)S(1)}, f32[392,128]{1,0:T(8,128)S(1)}, u32[]{:S(2)}, u32[]{:S(2)}) collective-permute-start(f32[392,128]{1,0:T(8,128)S(1)} %get-tuple-element.84), channel_id=1, source_target_pairs={{0,8},{4,12},{8,0},{12,4},{1,9},{5,13},{9,1},{13,5},{2,10},{6,14},... | collective-permute-start | bytes 602120 | tf_op jit(solution)/shard_map/ppermute | solution.py:473
  73.1 18.9 %collective-permute-start.18 = (f32[392,128]{1,0:T(8,128)S(1)}, f32[392,128]{1,0:T(8,128)S(1)}, u32[]{:S(2)}, u32[]{:S(2)}) collective-permute-start(f32[392,128]{1,0:T(8,128)S(1)} %get-tuple-element.75), channel_id=1, source_target_pairs={{0,8},{4,12},{8,0},{12,4},{1,9},{5,13},{9,1},{13,5},{2,10},{6,14},... | collective-permute-start | bytes 602120 | tf_op jit(solution)/shard_map/ppermute | solution.py:473
  85.4 7.9 %collective-permute-start.25 = (f32[384,128]{1,0:T(8,128)S(1)}, f32[384,128]{1,0:T(8,128)S(1)}, u32[]{:S(2)}, u32[]{:S(2)}) collective-permute-start(f32[384,128]{1,0:T(8,128)S(1)} %combine.16.refs_0_), channel_id=1, source_target_pairs={{0,2},{2,0},{1,3},{3,1},{4,6},{6,4},{5,7},{7,5},{8,10},{10,8},{9,1... | collective-permute-start | bytes 589832 | tf_op jit(solution)/shard_map/ppermute | solution.py:25
  86.8 9.5 %collective-permute-start.24 = (f32[384,128]{1,0:T(8,128)S(1)}, f32[384,128]{1,0:T(8,128)S(1)}, u32[]{:S(2)}, u32[]{:S(2)}) collective-permute-start(f32[384,128]{1,0:T(8,128)S(1)} %combine.15.refs_2_), channel_id=1, source_target_pairs={{0,2},{2,0},{1,3},{3,1},{4,6},{6,4},{5,7},{7,5},{8,10},{10,8},{9,1... | collective-permute-start | bytes 589832 | tf_op jit(solution)/shard_map/ppermute | solution.py:25
  87.8 9.8 %collective-permute-start.22 = (f32[392,128]{1,0:T(8,128)S(1)}, f32[392,128]{1,0:T(8,128)S(1)}, u32[]{:S(2)}, u32[]{:S(2)}) collective-permute-start(f32[392,128]{1,0:T(8,128)S(1)} %get-tuple-element.85), channel_id=1, source_target_pairs={{0,4},{4,8},{8,12},{12,0},{1,5},{5,9},{9,13},{13,1},{2,6},{6,10},{... | collective-permute-start | bytes 602120 | tf_op jit(solution)/shard_map/ppermute | solution.py:473
  92.0 9.6 %collective-permute-start.19 = (f32[392,128]{1,0:T(8,128)S(1)}, f32[392,128]{1,0:T(8,128)S(1)}, u32[]{:S(2)}, u32[]{:S(2)}) collective-permute-start(f32[392,128]{1,0:T(8,128)S(1)} %get-tuple-element.78), channel_id=1, source_target_pairs={{0,4},{4,8},{8,12},{12,0},{1,5},{5,9},{9,13},{13,1},{2,6},{6,10},{... | collective-permute-start | bytes 602120 | tf_op jit(solution)/shard_map/ppermute | solution.py:473
  96.3 13.7 %collective-permute-start.26 = (f32[768,128]{1,0:T(8,128)S(1)}, f32[768,128]{1,0:T(8,128)S(1)}, u32[]{:S(2)}, u32[]{:S(2)}) collective-permute-start(f32[768,128]{1,0:T(8,128)S(1)} %combine.14.refs_4_), channel_id=1, source_target_pairs={{0,2},{2,0},{1,3},{3,1},{4,6},{6,4},{5,7},{7,5},{8,10},{10,8},{9,1... | collective-permute-start | bytes 1179656 | tf_op jit(solution)/shard_map/ppermute | solution.py:25
  97.6 8.2 %collective-permute-start.23 = (f32[392,128]{1,0:T(8,128)S(1)}, f32[392,128]{1,0:T(8,128)S(1)}, u32[]{:S(2)}, u32[]{:S(2)}) collective-permute-start(f32[392,128]{1,0:T(8,128)S(1)} %get-tuple-element.86), channel_id=1, source_target_pairs={{0,12},{4,0},{8,4},{12,8},{1,13},{5,1},{9,5},{13,9},{2,14},{6,2},{... | collective-permute-start | bytes 602120 | tf_op jit(solution)/shard_map/ppermute | solution.py:473
  101.7 7.7 %collective-permute-start.20 = (f32[392,128]{1,0:T(8,128)S(1)}, f32[392,128]{1,0:T(8,128)S(1)}, u32[]{:S(2)}, u32[]{:S(2)}) collective-permute-start(f32[392,128]{1,0:T(8,128)S(1)} %get-tuple-element.80), channel_id=1, source_target_pairs={{0,12},{4,0},{8,4},{12,8},{1,13},{5,1},{9,5},{13,9},{2,14},{6,2},{... | collective-permute-start | bytes 602120 | tf_op jit(solution)/shard_map/ppermute | solution.py:473
  103.8 12.1 %collective-permute-start.28 = (f32[768,128]{1,0:T(8,128)S(1)}, f32[768,128]{1,0:T(8,128)S(1)}, u32[]{:S(2)}, u32[]{:S(2)}) collective-permute-start(f32[768,128]{1,0:T(8,128)S(1)} %combine.17.refs_6_), channel_id=1, source_target_pairs={{0,2},{2,0},{1,3},{3,1},{4,6},{6,4},{5,7},{7,5},{8,10},{10,8},{9,1... | collective-permute-start | bytes 1179656 | tf_op jit(solution)/shard_map/ppermute | solution.py:25
  110.0 13.1 %collective-permute-start.27 = (f32[768,128]{1,0:T(8,128)S(1)}, f32[768,128]{1,0:T(8,128)S(1)}, u32[]{:S(2)}, u32[]{:S(2)}) collective-permute-start(f32[768,128]{1,0:T(8,128)S(1)} %combine.13.refs_0_), channel_id=1, source_target_pairs={{0,2},{2,0},{1,3},{3,1},{4,6},{6,4},{5,7},{7,5},{8,10},{10,8},{9,1... | collective-permute-start | bytes 1179656 | tf_op jit(solution)/shard_map/ppermute | solution.py:25

commit v17 on v16

--- a/solution.py
+++ b/solution.py
@@ -247,13 +247,17 @@
 
 
 def combine_kernel(share, pieces, ordered, with_inner, table, kept_ref, vector_ref, diag_ref, *refs):
-    arrived_refs, sum_ref, refs = refs[: len(pieces)], refs[len(pieces)], refs[len(pieces) + 1 :]
+    arrived_refs, refs = refs[: len(pieces)], refs[len(pieces) :]
+    sum_refs, refs = refs[: len(refs) - with_inner], refs[len(refs) - with_inner :]
     count, rows, width = diag_ref.shape
     height = kept_ref.shape[0] // count
     roots = height // rows
     inner = [jnp.zeros((1, width), jnp.float32) for _ in range(2 * roots)]
-    every = [(ref, base + i, i) for ref, (base, size) in zip(arrived_refs, pieces) for i in range(size)]
-    for i, (arrived_ref, at_place, of_piece) in enumerate(every):
+    every = [
+        (at, base + i, i) for at, (base, size) in enumerate(pieces) for i in range(size)
+    ]
+    for i, (of_group, at_place, of_piece) in enumerate(every):
+        arrived_ref = arrived_refs[of_group]
         slot = table[count + at_place]
         place = table[2 * count + slot]
         held = place if ordered else slot
@@ -267,7 +271,10 @@
             there = slice(of_piece * height + r * rows, of_piece * height + (r + 1) * rows)
             vector = vector_ref[at(held)]
             total = kept_ref[at(place)] + arrived_ref[there] + diag * vector
-            sum_ref[here] = total
+            if len(sum_refs) == 1:
+                sum_refs[0][here] = total
+            else:
+                sum_refs[of_group][there] = total
             if with_inner:
                 inner[r] = inner[r] + jnp.sum(vector * total, axis=0, keepdims=True)
                 inner[roots + r] = inner[roots + r] + share * jnp.sum(
@@ -278,10 +285,13 @@
         refs[0][...] = jnp.concatenate(inner + [rest], axis=0)
 
 
-def combine(table, pieces, kept, arrived, vector, diag, share, ordered, with_inner):
+def combine(table, pieces, kept, arrived, vector, diag, share, ordered, with_inner, apart=False):
     height, width = kept.shape[0] // diag.shape[0], kept.shape[1]
-    size = sum(size for _, size in pieces)
-    out_shape = [jax.ShapeDtypeStruct((size * height, width), jnp.float32)]
+    sizes = [size for _, size in pieces]
+    out_shape = [
+        jax.ShapeDtypeStruct((size * height, width), jnp.float32)
+        for size in (sizes if apart else [sum(sizes)])
+    ]
     if with_inner:
         out_shape.append(jax.ShapeDtypeStruct((TAG, width), jnp.float32))
     out = pl.pallas_call(
@@ -293,7 +303,7 @@
         cost_estimate=FREE,
         name="combine",
     )(table, kept, vector, diag, *arrived)
-    return out if with_inner else (out[0], None)
+    return out if with_inner or apart else (out[0], None)
 
 
 def correct_kernel(groups, ahead, table, inner_ref, vector_ref, diag_ref, *rest):
@@ -503,18 +513,35 @@
             if at >= ahead_of:
                 value = after(value, arrived[moving[at - ahead_of]])[0]
             arrived[piece] = relay(value, piece[0])
-        for group in mixed if second else whole:
-            mine, inner = combine(
+        stays = []
+        if second:
+            stays = combine(
                 table,
-                spans(group),
+                spans(staying),
                 kept,
-                [arrived[piece] if piece[0] else outgoing[piece] for piece in group],
+                [outgoing[piece] for piece in staying],
                 own,
                 diag,
                 1.0 / terms_over,
-                second,
-                not second,
+                True,
+                False,
+                True,
             )
+        for at, group in enumerate(mixed if second else whole):
+            if at < len(stays):
+                mine, inner = stays[at], None
+            else:
+                mine, inner = combine(
+                    table,
+                    spans(group),
+                    kept,
+                    [arrived[piece] if piece[0] else outgoing[piece] for piece in group],
+                    own,
+                    diag,
+                    1.0 / terms_over,
+                    second,
+                    not second,
+                )
             if second and len(sums) == 2 * ahead_of and ahead_of > 1:
                 mine = after(mine, sums[-1], sums[-3])[0]
             elif len(sums) >= 4:

time: 125 us -> 125 us (level)
    pallas_call x9 -> x8, Pallas kernels: 5.71 us -> 5.17 us  [combine(): pl.pallas_call(functools.partial(combine_kernel, share, pieces, ordered,...]
  transfers between devices with their start and end apart: 29 -> 29, of which waited for: 18 -> 17; matrix products, arithmetic and copies ran while one was open for 1% -> 1% of each run, Pallas kernels for 29% -> 29%
where the time goes in v17:
time: 125 us; the launch traced here: 124 us
  Pallas kernels  43.5 us (35%)
  waiting for transfers between devices  39 us (31%)
  starting transfers between devices  38.5 us (31%)
  local copies, waits for them, and re-layouts  1.51 us (1%)
    pallas_call x4, Pallas kernels, sectors(): pl.pallas_call(functools.partial(sector_kernel, count, terms, unroll, hei...  30.7 us
    ppermute x12, starting transfers between devices, relay(): lax.ppermute(value, 'blk', [(p, (p + c) % devices) for p in range(devices)])  20.1 us
    ppermute x12, waiting for transfers between devices, relay(): lax.ppermute(value, 'blk', [(p, (p + c) % devices) for p in range(devices)])  18.6 us
    ppermute x14, waiting for transfers between devices, flip(): return lax.ppermute(value, axis, [(i, i ^ bit) for i in range(size)])  18.6 us
    ppermute x14, starting transfers between devices, flip(): return lax.ppermute(value, axis, [(i, i ^ bit) for i in range(size)])  17.6 us
    pallas_call x8, Pallas kernels, combine(): pl.pallas_call(functools.partial(combine_kernel, share, pieces, ordered,...  5.17 us
    pallas_call x2, Pallas kernels, finish(): pl.pallas_call(functools.partial(finish_kernel, count, rows, [size for _,...  2.98 us
  transfers between devices with their start and end apart: 29, of which 17 were waited for; matrix products, arithmetic and copies ran while one was open for 1% of the time, Pallas kernels for 29%

profile of v17, /device:TPU:0, one launch (start us, length us, event | category | flops | bytes accessed | tf_op | source)
XLA Modules:
  0.0 124.3 jit_solution(615807569493706083)
XLA Ops:
  1.1 0.7 pad_add_fusion.given_hbm
  1.9 1.4 %copy-done.1 = f32[16,64,3,128]{3,1,2,0:T(8,128)S(1)} copy-done((f32[16,64,3,128]{3,1,2,0:T(8,128)S(1)}, f32[16,64,3,128]{3,1,2,0:T(8,128)}, u32[]{:S(2)}) %copy-start.1) | copy-done | bytes 1572888
  3.3 1.5 %table.1 = s32[57]{0:T(128)S(1)} custom-call(s32[24]{0:T(128)S(1)} %pad_add_fusion.given_hbm, f32[3072,128]{1,0:T(8,128)S(1)} %bitcast.12), custom_call_target="tpu_custom_call" | custom-call | tf_op jit(solution)/shard_map/table/pallas_call | solution.py:78
  4.8 5.2 %sectors.4 = (f32[384,128]{1,0:T(8,128)S(1)}, f32[384,128]{1,0:T(8,128)S(1)}, f32[3072,128]{1,0:T(8,128)S(1)}) custom-call(s32[57]{0:T(128)S(1)} %table.1, f32[3072,128]{1,0:T(8,128)S(1)} %bitcast.13, f32[3072,128]{1,0:T(8,128)S(1)} %collective-permute-done.other_ref, f32[8,16,64,128]{3,2,1,0:T(8,128)} %refs_0_.7, f32[8,16,128,128]{3,2,1,0:T(8,128)} %refs_1_.7, ...), custom_call_target="tpu_custom_call" | custom-call | tf_op jit(solution)/shard_map/sectors/pallas_call | solution.py:221
  10.0 3.7 %collective-permute-start.1 = (f32[384,128]{1,0:T(8,128)S(1)}, f32[384,128]{1,0:T(8,128)S(1)}, u32[]{:S(2)}, u32[]{:S(2)}) collective-permute-start(f32[384,128]{1,0:T(8,128)S(1)} %get-tuple-element.54), channel_id=1, source_target_pairs={{0,8},{4,12},{8,0},{12,4},{1,9},{5,13},{9,1},{13,5},{2,10},{6,14},... | collective-permute-start | bytes 589832 | tf_op jit(solution)/shard_map/ppermute | solution.py:483
  13.9 11.6 %sectors.5 = (f32[384,128]{1,0:T(8,128)S(1)}, f32[384,128]{1,0:T(8,128)S(1)}, f32[384,128]{1,0:T(8,128)S(1)}, f32[384,128]{1,0:T(8,128)S(1)}, f32[384,128]{1,0:T...) custom-call(s32[57]{0:T(128)S(1)} %table.1, ...), custom_call_target="tpu_custom_call", output_to_operand_aliasing={{6}: (7, {})} | custom-call | tf_op jit(solution)/shard_map/sectors/pallas_call | solution.py:221
  25.6 0.7 combine.8
  26.2 1.8 %collective-permute-start.11 = (f32[768,128]{1,0:T(8,128)S(1)}, f32[768,128]{1,0:T(8,128)S(1)}, u32[]{:S(2)}, u32[]{:S(2)}) collective-permute-start(f32[768,128]{1,0:T(8,128)S(1)} %get-tuple-element.68.rest_0_), channel_id=1, source_target_pairs={{0,2},{2,0},{1,3},{3,1},{4,6},{6,4},{5,7},{7,5},{8,10},{10,8},{9,1... | collective-permute-start | bytes 1179656 | tf_op jit(solution)/shard_map/ppermute | solution.py:25
  28.1 1.6 %collective-permute-start.3 = (f32[384,128]{1,0:T(8,128)S(1)}, f32[384,128]{1,0:T(8,128)S(1)}, u32[]{:S(2)}, u32[]{:S(2)}) collective-permute-start(f32[384,128]{1,0:T(8,128)S(1)} %get-tuple-element.58), channel_id=1, source_target_pairs={{0,4},{4,8},{8,12},{12,0},{1,5},{5,9},{9,13},{13,1},{2,6},{6,10},{... | collective-permute-start | bytes 589832 | tf_op jit(solution)/shard_map/ppermute | solution.py:483
  29.6 2.2 %collective-permute-done.2.refs_1_ = f32[384,128]{1,0:T(8,128)S(1)} collective-permute-done((f32[384,128]{1,0:T(8,128)S(1)}, f32[384,128]{1,0:T(8,128)S(1)}, u32[]{:S(2)}, u32[]{:S(2)}) %collective-permute-start.2) | collective-permute-done | bytes 196640 | tf_op jit(solution)/shard_map/ppermute | solution.py:483
  31.9 0.8 collective-permute-start.4
  33.3 1.6 %collective-permute-start.14 = (f32[768,128]{1,0:T(8,128)S(1)}, f32[768,128]{1,0:T(8,128)S(1)}, u32[]{:S(2)}, u32[]{:S(2)}) collective-permute-start(f32[768,128]{1,0:T(8,128)S(1)} %get-tuple-element.71.rest_2_), channel_id=1, source_target_pairs={{0,2},{2,0},{1,3},{3,1},{4,6},{6,4},{5,7},{7,5},{8,10},{10,8},{9,1... | collective-permute-start | bytes 1179656 | tf_op jit(solution)/shard_map/ppermute | solution.py:25
  34.9 1.5 %collective-permute-done.3.refs_0_ = f32[384,128]{1,0:T(8,128)S(1)} collective-permute-done((f32[384,128]{1,0:T(8,128)S(1)}, f32[384,128]{1,0:T(8,128)S(1)}, u32[]{:S(2)}, u32[]{:S(2)}) %collective-permute-start.3) | collective-permute-done | bytes 196640 | tf_op jit(solution)/shard_map/ppermute | solution.py:483
  36.4 3.3 %collective-permute-start.5 = (f32[384,128]{1,0:T(8,128)S(1)}, f32[384,128]{1,0:T(8,128)S(1)}, u32[]{:S(2)}, u32[]{:S(2)}) collective-permute-start(f32[384,128]{1,0:T(8,128)S(1)} %get-tuple-element.63), channel_id=1, source_target_pairs={{0,12},{4,0},{8,4},{12,8},{1,13},{5,1},{9,5},{13,9},{2,14},{6,2},{... | collective-permute-start | bytes 589832 | tf_op jit(solution)/shard_map/ppermute | solution.py:483
  39.7 1.1 collective-permute-done.4.refs_1_
  40.8 3.1 %collective-permute-start.6 = (f32[384,128]{1,0:T(8,128)S(1)}, f32[384,128]{1,0:T(8,128)S(1)}, u32[]{:S(2)}, u32[]{:S(2)}) collective-permute-start(f32[384,128]{1,0:T(8,128)S(1)} %get-tuple-element.65), channel_id=1, source_target_pairs={{0,12},{4,0},{8,4},{12,8},{1,13},{5,1},{9,5},{13,9},{2,14},{6,2},{... | collective-permute-start | bytes 589832 | tf_op jit(solution)/shard_map/ppermute | solution.py:483
  44.5 1.5 %collective-permute-start.12 = (f32[768,128]{1,0:T(8,128)S(1)}, f32[768,128]{1,0:T(8,128)S(1)}, u32[]{:S(2)}, u32[]{:S(2)}) collective-permute-start(f32[768,128]{1,0:T(8,128)S(1)} %get-tuple-element.69.rest_4_), channel_id=1, source_target_pairs={{0,2},{2,0},{1,3},{3,1},{4,6},{6,4},{5,7},{7,5},{8,10},{10,8},{9,1... | collective-permute-start | bytes 1179656 | tf_op jit(solution)/shard_map/ppermute | solution.py:25
  46.1 2.9 %collective-permute-done.6.refs_1_ = f32[384,128]{1,0:T(8,128)S(1)} collective-permute-done((f32[384,128]{1,0:T(8,128)S(1)}, f32[384,128]{1,0:T(8,128)S(1)}, u32[]{:S(2)}, u32[]{:S(2)}) %collective-permute-start.6) | collective-permute-done | bytes 196640 | tf_op jit(solution)/shard_map/ppermute | solution.py:483
  49.7 1.5 %collective-permute-start.15 = (f32[768,128]{1,0:T(8,128)S(1)}, f32[768,128]{1,0:T(8,128)S(1)}, u32[]{:S(2)}, u32[]{:S(2)}) collective-permute-start(f32[768,128]{1,0:T(8,128)S(1)} %get-tuple-element.73.rest_6_), channel_id=1, source_target_pairs={{0,2},{2,0},{1,3},{3,1},{4,6},{6,4},{5,7},{7,5},{8,10},{10,8},{9,1... | collective-permute-start | bytes 1179656 | tf_op jit(solution)/shard_map/ppermute | solution.py:25
  51.2 1.2 collective-permute-done.7
  52.4 3.5 %collective-permute-start.10 = (f32[8,128]{1,0:T(8,128)S(1)}, f32[8,128]{1,0:T(8,128)S(1)}, u32[]{:S(2)}, u32[]{:S(2)}) collective-permute-start(f32[8,128]{1,0:T(8,128)S(1)} %add.63), channel_id=1, source_target_pairs={{0,12},{4,8},{8,4},{12,0},{1,13},{5,9},{9,5},{13,1},{2,14},{6,10},... | collective-permute-start | bytes 12296 | tf_op jit(solution)/shard_map/ppermute | solution.py:25
  55.9 0.9 collective-permute-start.8
  56.8 1.0 collective-permute-done.10
  57.8 2.6 %collective-permute-done.9 = f32[8,128]{1,0:T(8,128)S(1)} collective-permute-done((f32[8,128]{1,0:T(8,128)S(1)}, f32[8,128]{1,0:T(8,128)S(1)}, u32[]{:S(2)}, u32[]{:S(2)}) %collective-permute-start.9) | collective-permute-done | bytes 4128 | tf_op jit(solution)/shard_map/ppermute | solution.py:25
  61.0 3.1 %collective-permute-done.13 = f32[8,128]{1,0:T(8,128)S(1)} collective-permute-done((f32[8,128]{1,0:T(8,128)S(1)}, f32[8,128]{1,0:T(8,128)S(1)}, u32[]{:S(2)}, u32[]{:S(2)}) %collective-permute-start.13) | collective-permute-done | bytes 4128 | tf_op jit(solution)/shard_map/ppermute | solution.py:25
  64.1 1.3 %correct.1 = (f32[3080,128]{1,0:T(8,128)S(1)}, f32[776,128]{1,0:T(8,128)S(1)}) custom-call(s32[57]{0:T(128)S(1)} %table.1, f32[8,128]{1,0:T(8,128)S(1)} %add.67.inner_ref, f32[3072,128]{1,0:T(8,128)S(1)} %bitcast.19, f32[16,64,128]{2,1,0:T(8,128)S(1)} %broadcast_add_fusion.diag_ref, f32[768,128]{1,0:T(8,128)S(1)} %get-tuple-element.68.rest_0_, ...), custom_call_target="tpu_custom_call" | custom-call | tf_op jit(solution)/shard_map/correct/pallas_call | solution.py:343
  65.4 1.7 %collective-permute-done.16.other_ref = f32[776,128]{1,0:T(8,128)S(1)} collective-permute-done((f32[776,128]{1,0:T(8,128)S(1)}, f32[776,128]{1,0:T(8,128)S(1)}, u32[]{:S(2)}, u32[]{:S(2)}) %collective-permute-start.16) | collective-permute-done | bytes 397344 | tf_op jit(solution)/shard_map/ppermute | solution.py:486
  67.3 3.7 %sectors.6 = (f32[392,128]{1,0:T(8,128)S(1)}, f32[392,128]{1,0:T(8,128)S(1)}, f32[3072,128]{1,0:T(8,128)S(1)}) custom-call(s32[57]{0:T(128)S(1)} %table.1, f32[776,128]{1,0:T(8,128)S(1)} %get-tuple-element.75.own_ref, f32[776,128]{1,0:T(8,128)S(1)} %collective-permute-done.16.other_ref, f32[8,16,64,128]{3,2,1,0:T(8,128)S(1)} %copy-done, ...), custom_call_target="tpu_custom_call" | custom-call | tf_op jit(solution)/shard_map/sectors/pallas_call | solution.py:221
  71.0 2.1 %collective-permute-start.21 = (f32[392,128]{1,0:T(8,128)S(1)}, f32[392,128]{1,0:T(8,128)S(1)}, u32[]{:S(2)}, u32[]{:S(2)}) collective-permute-start(f32[392,128]{1,0:T(8,128)S(1)} %get-tuple-element.86), channel_id=1, source_target_pairs={{0,8},{4,12},{8,0},{12,4},{1,9},{5,13},{9,1},{13,5},{2,10},{6,14},... | collective-permute-start | bytes 602120 | tf_op jit(solution)/shard_map/ppermute | solution.py:483
  73.1 0.9 collective-permute-start.18
  74.0 10.2 %sectors.7 = (f32[392,128]{1,0:T(8,128)S(1)}, f32[392,128]{1,0:T(8,128)S(1)}, f32[392,128]{1,0:T(8,128)S(1)}, f32[392,128]{1,0:T(8,128)S(1)}, f32[384,128]{1,0:T...) custom-call(s32[57]{0:T(128)S(1)} %table.1, ...), custom_call_target="tpu_custom_call", output_to_operand_aliasing={{6}: (5, {})} | custom-call | tf_op jit(solution)/shard_map/sectors/pallas_call | solution.py:221
  84.9 1.3 %collective-permute-start.24 = (f32[384,128]{1,0:T(8,128)S(1)}, f32[384,128]{1,0:T(8,128)S(1)}, u32[]{:S(2)}, u32[]{:S(2)}) collective-permute-start(f32[384,128]{1,0:T(8,128)S(1)} %get-tuple-element.91.refs_2_), channel_id=1, source_target_pairs={{0,2},{2,0},{1,3},{3,1},{4,6},{6,4},{5,7},{7,5},{8,10},{10,8},{9,1... | collective-permute-start | bytes 589832 | tf_op jit(solution)/shard_map/ppermute | solution.py:25
  86.2 0.8 collective-permute-start.25
  87.0 0.8 collective-permute-done.21.refs_1_
  88.0 4.0 %collective-permute-done.18.refs_0_ = f32[392,128]{1,0:T(8,128)S(1)} collective-permute-done((f32[392,128]{1,0:T(8,128)S(1)}, f32[392,128]{1,0:T(8,128)S(1)}, u32[]{:S(2)}, u32[]{:S(2)}) %collective-permute-start.18) | collective-permute-done | bytes 200736 | tf_op jit(solution)/shard_map/ppermute | solution.py:483
  93.0 2.8 %collective-permute-done.25.refs_1_ = f32[384,128]{1,0:T(8,128)S(1)} collective-permute-done((f32[384,128]{1,0:T(8,128)S(1)}, f32[384,128]{1,0:T(8,128)S(1)}, u32[]{:S(2)}, u32[]{:S(2)}) %collective-permute-start.25) | collective-permute-done | bytes 196640 | tf_op jit(solution)/shard_map/ppermute | solution.py:25
  95.8 1.3 %collective-permute-start.26 = (f32[768,128]{1,0:T(8,128)S(1)}, f32[768,128]{1,0:T(8,128)S(1)}, u32[]{:S(2)}, u32[]{:S(2)}) collective-permute-start(f32[768,128]{1,0:T(8,128)S(1)} %combine.13.refs_4_), channel_id=1, source_target_pairs={{0,2},{2,0},{1,3},{3,1},{4,6},{6,4},{5,7},{7,5},{8,10},{10,8},{9,1... | collective-permute-start | bytes 1179656 | tf_op jit(solution)/shard_map/ppermute | solution.py:25
  97.1 2.6 %collective-permute-start.23 = (f32[392,128]{1,0:T(8,128)S(1)}, f32[392,128]{1,0:T(8,128)S(1)}, u32[]{:S(2)}, u32[]{:S(2)}) collective-permute-start(f32[392,128]{1,0:T(8,128)S(1)} %get-tuple-element.88), channel_id=1, source_target_pairs={{0,12},{4,0},{8,4},{12,8},{1,13},{5,1},{9,5},{13,9},{2,14},{6,2},{... | collective-permute-start | bytes 602120 | tf_op jit(solution)/shard_map/ppermute | solution.py:483
  99.7 2.0 %collective-permute-done.19.refs_0_ = f32[392,128]{1,0:T(8,128)S(1)} collective-permute-done((f32[392,128]{1,0:T(8,128)S(1)}, f32[392,128]{1,0:T(8,128)S(1)}, u32[]{:S(2)}, u32[]{:S(2)}) %collective-permute-start.19) | collective-permute-done | bytes 200736 | tf_op jit(solution)/shard_map/ppermute | solution.py:483
  101.7 1.5 %collective-permute-start.20 = (f32[392,128]{1,0:T(8,128)S(1)}, f32[392,128]{1,0:T(8,128)S(1)}, u32[]{:S(2)}, u32[]{:S(2)}) collective-permute-start(f32[392,128]{1,0:T(8,128)S(1)} %get-tuple-element.82), channel_id=1, source_target_pairs={{0,12},{4,0},{8,4},{12,8},{1,13},{5,1},{9,5},{13,9},{2,14},{6,2},{... | collective-permute-start | bytes 602120 | tf_op jit(solution)/shard_map/ppermute | solution.py:483
  103.8 1.4 %collective-permute-start.28 = (f32[768,128]{1,0:T(8,128)S(1)}, f32[768,128]{1,0:T(8,128)S(1)}, u32[]{:S(2)}, u32[]{:S(2)}) collective-permute-start(f32[768,128]{1,0:T(8,128)S(1)} %combine.15.refs_6_), channel_id=1, source_target_pairs={{0,2},{2,0},{1,3},{3,1},{4,6},{6,4},{5,7},{7,5},{8,10},{10,8},{9,1... | collective-permute-start | bytes 1179656 | tf_op jit(solution)/shard_map/ppermute | solution.py:25
  105.5 3.9 %collective-permute-done.20.refs_0_ = f32[392,128]{1,0:T(8,128)S(1)} collective-permute-done((f32[392,128]{1,0:T(8,128)S(1)}, f32[392,128]{1,0:T(8,128)S(1)}, u32[]{:S(2)}, u32[]{:S(2)}) %collective-permute-start.20) | collective-permute-done | bytes 200736 | tf_op jit(solution)/shard_map/ppermute | solution.py:483
  110.0 1.4 %collective-permute-start.27 = (f32[768,128]{1,0:T(8,128)S(1)}, f32[768,128]{1,0:T(8,128)S(1)}, u32[]{:S(2)}, u32[]{:S(2)}) collective-permute-start(f32[768,128]{1,0:T(8,128)S(1)} %combine.12.refs_0_), channel_id=1, source_target_pairs={{0,2},{2,0},{1,3},{3,1},{4,6},{6,4},{5,7},{7,5},{8,10},{10,8},{9,1... | collective-permute-start | bytes 1179656 | tf_op jit(solution)/shard_map/ppermute | solution.py:25
  111.6 1.8 %scaled.1 = f32[3072,128]{1,0:T(8,128)} custom-call(s32[57]{0:T(128)S(1)} %table.1, f32[8,128]{1,0:T(8,128)S(1)} %broadcast_in_dim.2.scale_ref, f32[3080,128]{1,0:T(8,128)S(1)} %get-tuple-element.76.own_ref.vector_ref.raw_ref), custom_call_target="tpu_custom_call" | custom-call | tf_op jit(solution)/shard_map/scaled/pallas_call | solution.py:388
  113.4 2.5 %collective-permute-done.28.refs_7_ = f32[768,128]{1,0:T(8,128)S(1)} collective-permute-done((f32[768,128]{1,0:T(8,128)S(1)}, f32[768,128]{1,0:T(8,128)S(1)}, u32[]{:S(2)}, u32[]{:S(2)}) %collective-permute-start.28) | collective-permute-done | bytes 393248 | tf_op jit(solution)/shard_map/ppermute | solution.py:25
  115.9 1.7 %finish.2.refs_2_ = f32[3072,128]{1,0:T(8,128)} custom-call(s32[57]{0:T(128)S(1)} %table.1, f32[8,128]{1,0:T(8,128)S(1)} %broadcast_in_dim.2.scale_ref, f32[384,128]{1,0:T(8,128)S(1)} %get-tuple-element.92.refs_0_, f32[384,128]{1,0:T(8,128)S(1)} %collective-permute-done.25.refs_1_, f32[384,128]{1,0:T(8,128)S(1)} %get-tuple-element.91.refs_2_, ...), custom_call_target="tpu_custom_call" | custom-call | tf_op jit(solution)/shard_map/finish/pallas_call | solution.py:429
  117.6 5.4 %collective-permute-done.27.refs_1_ = f32[768,128]{1,0:T(8,128)S(1)} collective-permute-done((f32[768,128]{1,0:T(8,128)S(1)}, f32[768,128]{1,0:T(8,128)S(1)}, u32[]{:S(2)}, u32[]{:S(2)}) %collective-permute-start.27) | collective-permute-done | bytes 393248 | tf_op jit(solution)/shard_map/ppermute | solution.py:25
  123.0 1.3 %finish.3 = f32[3072,128]{1,0:T(8,128)} custom-call(s32[57]{0:T(128)S(1)} %table.1, f32[8,128]{1,0:T(8,128)S(1)} %broadcast_in_dim.2.scale_ref, f32[768,128]{1,0:T(8,128)S(1)} %combine.12.refs_0_, f32[768,128]{1,0:T(8,128)S(1)} %collective-permute-done.27.refs_1_, f32[3072,128]{1,0:T(8,128)} %finish.2.refs_2_), custom_call_target="tpu_custom_call", output_to_operand_aliasing={{}: (4, {})} | custom-call | tf_op jit(solution)/shard_map/finish/pallas_call | solution.py:429
  (51 shorter events, 7.2 us)
Async XLA Ops:
  0.6 4.2 %collective-permute-start = (f32[3072,128]{1,0:T(8,128)}, f32[3072,128]{1,0:T(8,128)S(1)}, u32[]{:S(2)}, u32[]{:S(2)}) collective-permute-start(f32[3072,128]{1,0:T(8,128)} %bitcast.11), channel_id=1, source_target_pairs={{0,1},{1,0},{2,3},{3,2},{4,5},{5,4},{6,7},{7,6},{8,9},{9,8},{10,11... | collective-permute-start | bytes 4718600 | tf_op jit(solution)/shard_map/ppermute | solution.py:486
  1.9 1.4 %copy-start.1 = (f32[16,64,3,128]{3,1,2,0:T(8,128)S(1)}, f32[16,64,3,128]{3,1,2,0:T(8,128)}, u32[]{:S(2)}) copy-start(f32[16,64,3,128]{3,1,2,0:T(8,128)} %param.7) | copy-start | bytes 4718596
  3.3 1.5 %copy-start.2 = (f32[16,64,3,128]{3,1,2,0:T(8,128)S(1)}, f32[16,64,3,128]{3,1,2,0:T(8,128)}, u32[]{:S(2)}) copy-start(f32[16,64,3,128]{3,1,2,0:T(8,128)} %param.7) | copy-start | bytes 4718596
  4.8 9.0 %copy-start.3 = (f32[16,128]{1,0:T(8,128)S(1)}, f32[16,128]{1,0:T(8,128)}, u32[]{:S(2)}) copy-start(f32[16,128]{1,0:T(8,128)} %param.13) | copy-start | bytes 24580
  4.8 8.9 %copy-start.4 = (f32[16,64]{1,0:T(8,128)S(1)}, f32[16,64]{1,0:T(8,128)}, u32[]{:S(2)}) copy-start(f32[16,64]{1,0:T(8,128)} %param.12) | copy-start | bytes 12292
  10.0 18.1 %collective-permute-start.1 = (f32[384,128]{1,0:T(8,128)S(1)}, f32[384,128]{1,0:T(8,128)S(1)}, u32[]{:S(2)}, u32[]{:S(2)}) collective-permute-start(f32[384,128]{1,0:T(8,128)S(1)} %get-tuple-element.54), channel_id=1, source_target_pairs={{0,8},{4,12},{8,0},{12,4},{1,9},{5,13},{9,1},{13,5},{2,10},{6,14},... | collective-permute-start | bytes 589832 | tf_op jit(solution)/shard_map/ppermute | solution.py:483
  13.7 18.2 %collective-permute-start.2 = (f32[384,128]{1,0:T(8,128)S(1)}, f32[384,128]{1,0:T(8,128)S(1)}, u32[]{:S(2)}, u32[]{:S(2)}) collective-permute-start(f32[384,128]{1,0:T(8,128)S(1)} %get-tuple-element.55), channel_id=1, source_target_pairs={{0,8},{4,12},{8,0},{12,4},{1,9},{5,13},{9,1},{13,5},{2,10},{6,14},... | collective-permute-start | bytes 589832 | tf_op jit(solution)/shard_map/ppermute | solution.py:483
  26.2 18.3 %collective-permute-start.11 = (f32[768,128]{1,0:T(8,128)S(1)}, f32[768,128]{1,0:T(8,128)S(1)}, u32[]{:S(2)}, u32[]{:S(2)}) collective-permute-start(f32[768,128]{1,0:T(8,128)S(1)} %get-tuple-element.68.rest_0_), channel_id=1, source_target_pairs={{0,2},{2,0},{1,3},{3,1},{4,6},{6,4},{5,7},{7,5},{8,10},{10,8},{9,1... | collective-permute-start | bytes 1179656 | tf_op jit(solution)/shard_map/ppermute | solution.py:25
  28.1 8.3 %collective-permute-start.3 = (f32[384,128]{1,0:T(8,128)S(1)}, f32[384,128]{1,0:T(8,128)S(1)}, u32[]{:S(2)}, u32[]{:S(2)}) collective-permute-start(f32[384,128]{1,0:T(8,128)S(1)} %get-tuple-element.58), channel_id=1, source_target_pairs={{0,4},{4,8},{8,12},{12,0},{1,5},{5,9},{9,13},{13,1},{2,6},{6,10},{... | collective-permute-start | bytes 589832 | tf_op jit(solution)/shard_map/ppermute | solution.py:483
  31.9 8.9 %collective-permute-start.4 = (f32[384,128]{1,0:T(8,128)S(1)}, f32[384,128]{1,0:T(8,128)S(1)}, u32[]{:S(2)}, u32[]{:S(2)}) collective-permute-start(f32[384,128]{1,0:T(8,128)S(1)} %get-tuple-element.60), channel_id=1, source_target_pairs={{0,4},{4,8},{8,12},{12,0},{1,5},{5,9},{9,13},{13,1},{2,6},{6,10},{... | collective-permute-start | bytes 589832 | tf_op jit(solution)/shard_map/ppermute | solution.py:483
  32.6 34.6 %slice-start = ((s8[8388608]{0:T(1024)(128)(4,1)}), s8[4194304]{0:T(1024)(128)(4,1)S(1)}, s32[]{:S(2)}) async-start(s8[8388608]{0:T(1024)(128)(4,1)} %bitcast.9), calls=%async_computation | async-start | bytes 8388608
  33.3 16.4 %collective-permute-start.14 = (f32[768,128]{1,0:T(8,128)S(1)}, f32[768,128]{1,0:T(8,128)S(1)}, u32[]{:S(2)}, u32[]{:S(2)}) collective-permute-start(f32[768,128]{1,0:T(8,128)S(1)} %get-tuple-element.71.rest_2_), channel_id=1, source_target_pairs={{0,2},{2,0},{1,3},{3,1},{4,6},{6,4},{5,7},{7,5},{8,10},{10,8},{9,1... | collective-permute-start | bytes 1179656 | tf_op jit(solution)/shard_map/ppermute | solution.py:25
  36.4 9.7 %collective-permute-start.5 = (f32[384,128]{1,0:T(8,128)S(1)}, f32[384,128]{1,0:T(8,128)S(1)}, u32[]{:S(2)}, u32[]{:S(2)}) collective-permute-start(f32[384,128]{1,0:T(8,128)S(1)} %get-tuple-element.63), channel_id=1, source_target_pairs={{0,12},{4,0},{8,4},{12,8},{1,13},{5,1},{9,5},{13,9},{2,14},{6,2},{... | collective-permute-start | bytes 589832 | tf_op jit(solution)/shard_map/ppermute | solution.py:483
  40.8 8.2 %collective-permute-start.6 = (f32[384,128]{1,0:T(8,128)S(1)}, f32[384,128]{1,0:T(8,128)S(1)}, u32[]{:S(2)}, u32[]{:S(2)}) collective-permute-start(f32[384,128]{1,0:T(8,128)S(1)} %get-tuple-element.65), channel_id=1, source_target_pairs={{0,12},{4,0},{8,4},{12,8},{1,13},{5,1},{9,5},{13,9},{2,14},{6,2},{... | collective-permute-start | bytes 589832 | tf_op jit(solution)/shard_map/ppermute | solution.py:483
  44.5 22.8 %slice-start.1 = ((s8[8388608]{0:T(1024)(128)(4,1)}), s8[4194304]{0:T(1024)(128)(4,1)S(1)}, s32[]{:S(2)}) async-start(s8[8388608]{0:T(1024)(128)(4,1)} %bitcast.9), calls=%async_computation.1 | async-start | bytes 8388608
  44.5 15.8 %collective-permute-start.12 = (f32[768,128]{1,0:T(8,128)S(1)}, f32[768,128]{1,0:T(8,128)S(1)}, u32[]{:S(2)}, u32[]{:S(2)}) collective-permute-start(f32[768,128]{1,0:T(8,128)S(1)} %get-tuple-element.69.rest_4_), channel_id=1, source_target_pairs={{0,2},{2,0},{1,3},{3,1},{4,6},{6,4},{5,7},{7,5},{8,10},{10,8},{9,1... | collective-permute-start | bytes 1179656 | tf_op jit(solution)/shard_map/ppermute | solution.py:25
  49.7 14.4 %collective-permute-start.15 = (f32[768,128]{1,0:T(8,128)S(1)}, f32[768,128]{1,0:T(8,128)S(1)}, u32[]{:S(2)}, u32[]{:S(2)}) collective-permute-start(f32[768,128]{1,0:T(8,128)S(1)} %get-tuple-element.73.rest_6_), channel_id=1, source_target_pairs={{0,2},{2,0},{1,3},{3,1},{4,6},{6,4},{5,7},{7,5},{8,10},{10,8},{9,1... | collective-permute-start | bytes 1179656 | tf_op jit(solution)/shard_map/ppermute | solution.py:25
  51.2 1.2 collective-permute-start.7
  52.4 5.4 %collective-permute-start.10 = (f32[8,128]{1,0:T(8,128)S(1)}, f32[8,128]{1,0:T(8,128)S(1)}, u32[]{:S(2)}, u32[]{:S(2)}) collective-permute-start(f32[8,128]{1,0:T(8,128)S(1)} %add.63), channel_id=1, source_target_pairs={{0,12},{4,8},{8,4},{12,0},{1,13},{5,9},{9,5},{13,1},{2,14},{6,10},... | collective-permute-start | bytes 12296 | tf_op jit(solution)/shard_map/ppermute | solution.py:25
  55.9 4.5 %collective-permute-start.9 = (f32[8,128]{1,0:T(8,128)S(1)}, f32[8,128]{1,0:T(8,128)S(1)}, u32[]{:S(2)}, u32[]{:S(2)}) collective-permute-start(f32[8,128]{1,0:T(8,128)S(1)} %add.63), channel_id=1, source_target_pairs={{0,8},{4,12},{8,0},{12,4},{1,9},{5,13},{9,1},{13,5},{2,10},{6,14},... | collective-permute-start | bytes 12296 | tf_op jit(solution)/shard_map/ppermute | solution.py:25
  55.9 4.5 %collective-permute-start.8 = (f32[8,128]{1,0:T(8,128)S(1)}, f32[8,128]{1,0:T(8,128)S(1)}, u32[]{:S(2)}, u32[]{:S(2)}) collective-permute-start(f32[8,128]{1,0:T(8,128)S(1)} %add.63), channel_id=1, source_target_pairs={{0,4},{4,0},{8,12},{12,8},{1,5},{5,1},{9,13},{13,9},{2,6},{6,2},{1... | collective-permute-start | bytes 12296 | tf_op jit(solution)/shard_map/ppermute | solution.py:25
  60.4 3.7 %collective-permute-start.13 = (f32[8,128]{1,0:T(8,128)S(1)}, f32[8,128]{1,0:T(8,128)S(1)}, u32[]{:S(2)}, u32[]{:S(2)}) collective-permute-start(f32[8,128]{1,0:T(8,128)S(1)} %add_add_fusion), channel_id=1, source_target_pairs={{0,2},{2,0},{1,3},{3,1},{4,6},{6,4},{5,7},{7,5},{8,10},{10,8},{9,1... | collective-permute-start | bytes 12296 | tf_op jit(solution)/shard_map/ppermute | solution.py:25
  64.1 3.2 %copy-start = (f32[8,16,64,128]{3,2,1,0:T(8,128)S(1)}, f32[8,16,64,128]{3,2,1,0:T(8,128)}, u32[]{:S(2)}) copy-start(f32[8,16,64,128]{3,2,1,0:T(8,128)} %refs_0_.7) | copy-start | bytes 12582916
  65.3 1.8 %collective-permute-start.16 = (f32[776,128]{1,0:T(8,128)S(1)}, f32[776,128]{1,0:T(8,128)S(1)}, u32[]{:S(2)}, u32[]{:S(2)}) collective-permute-start(f32[776,128]{1,0:T(8,128)S(1)} %get-tuple-element.75.own_ref), channel_id=1, source_target_pairs={{0,1},{1,0},{2,3},{3,2},{4,5},{5,4},{6,7},{7,6},{8,9},{9,8},{10,11... | collective-permute-start | bytes 1191944 | tf_op jit(solution)/shard_map/ppermute | solution.py:486
  67.1 6.9 %collective-permute-start.17 = (f32[3080,128]{1,0:T(8,128)S(1)}, f32[3080,128]{1,0:T(8,128)S(1)}, u32[]{:S(2)}, u32[]{:S(2)}) collective-permute-start(f32[3080,128]{1,0:T(8,128)S(1)} %get-tuple-element.76.own_ref.vector_ref.raw_ref), channel_id=1, source_target_pairs={{0,1},{1,0},{2,3},{3,2},{4,5},{5,4},{6,7},{7,6},{8,9},{9,8},{10,11... | collective-permute-start | bytes 4730888 | tf_op jit(solution)/shard_map/ppermute | solution.py:486
  71.0 16.8 %collective-permute-start.21 = (f32[392,128]{1,0:T(8,128)S(1)}, f32[392,128]{1,0:T(8,128)S(1)}, u32[]{:S(2)}, u32[]{:S(2)}) collective-permute-start(f32[392,128]{1,0:T(8,128)S(1)} %get-tuple-element.86), channel_id=1, source_target_pairs={{0,8},{4,12},{8,0},{12,4},{1,9},{5,13},{9,1},{13,5},{2,10},{6,14},... | collective-permute-start | bytes 602120 | tf_op jit(solution)/shard_map/ppermute | solution.py:483
  73.1 18.9 %collective-permute-start.18 = (f32[392,128]{1,0:T(8,128)S(1)}, f32[392,128]{1,0:T(8,128)S(1)}, u32[]{:S(2)}, u32[]{:S(2)}) collective-permute-start(f32[392,128]{1,0:T(8,128)S(1)} %get-tuple-element.77), channel_id=1, source_target_pairs={{0,8},{4,12},{8,0},{12,4},{1,9},{5,13},{9,1},{13,5},{2,10},{6,14},... | collective-permute-start | bytes 602120 | tf_op jit(solution)/shard_map/ppermute | solution.py:483
  84.9 8.0 %collective-permute-start.24 = (f32[384,128]{1,0:T(8,128)S(1)}, f32[384,128]{1,0:T(8,128)S(1)}, u32[]{:S(2)}, u32[]{:S(2)}) collective-permute-start(f32[384,128]{1,0:T(8,128)S(1)} %get-tuple-element.91.refs_2_), channel_id=1, source_target_pairs={{0,2},{2,0},{1,3},{3,1},{4,6},{6,4},{5,7},{7,5},{8,10},{10,8},{9,1... | collective-permute-start | bytes 589832 | tf_op jit(solution)/shard_map/ppermute | solution.py:25
  86.2 9.6 %collective-permute-start.25 = (f32[384,128]{1,0:T(8,128)S(1)}, f32[384,128]{1,0:T(8,128)S(1)}, u32[]{:S(2)}, u32[]{:S(2)}) collective-permute-start(f32[384,128]{1,0:T(8,128)S(1)} %get-tuple-element.92.refs_0_), channel_id=1, source_target_pairs={{0,2},{2,0},{1,3},{3,1},{4,6},{6,4},{5,7},{7,5},{8,10},{10,8},{9,1... | collective-permute-start | bytes 589832 | tf_op jit(solution)/shard_map/ppermute | solution.py:25
  87.8 9.3 %collective-permute-start.22 = (f32[392,128]{1,0:T(8,128)S(1)}, f32[392,128]{1,0:T(8,128)S(1)}, u32[]{:S(2)}, u32[]{:S(2)}) collective-permute-start(f32[392,128]{1,0:T(8,128)S(1)} %get-tuple-element.87), channel_id=1, source_target_pairs={{0,4},{4,8},{8,12},{12,0},{1,5},{5,9},{9,13},{13,1},{2,6},{6,10},{... | collective-permute-start | bytes 602120 | tf_op jit(solution)/shard_map/ppermute | solution.py:483
  92.0 9.6 %collective-permute-start.19 = (f32[392,128]{1,0:T(8,128)S(1)}, f32[392,128]{1,0:T(8,128)S(1)}, u32[]{:S(2)}, u32[]{:S(2)}) collective-permute-start(f32[392,128]{1,0:T(8,128)S(1)} %get-tuple-element.80), channel_id=1, source_target_pairs={{0,4},{4,8},{8,12},{12,0},{1,5},{5,9},{9,13},{13,1},{2,6},{6,10},{... | collective-permute-start | bytes 602120 | tf_op jit(solution)/shard_map/ppermute | solution.py:483
  95.8 14.2 %collective-permute-start.26 = (f32[768,128]{1,0:T(8,128)S(1)}, f32[768,128]{1,0:T(8,128)S(1)}, u32[]{:S(2)}, u32[]{:S(2)}) collective-permute-start(f32[768,128]{1,0:T(8,128)S(1)} %combine.13.refs_4_), channel_id=1, source_target_pairs={{0,2},{2,0},{1,3},{3,1},{4,6},{6,4},{5,7},{7,5},{8,10},{10,8},{9,1... | collective-permute-start | bytes 1179656 | tf_op jit(solution)/shard_map/ppermute | solution.py:25
  97.1 8.4 %collective-permute-start.23 = (f32[392,128]{1,0:T(8,128)S(1)}, f32[392,128]{1,0:T(8,128)S(1)}, u32[]{:S(2)}, u32[]{:S(2)}) collective-permute-start(f32[392,128]{1,0:T(8,128)S(1)} %get-tuple-element.88), channel_id=1, source_target_pairs={{0,12},{4,0},{8,4},{12,8},{1,13},{5,1},{9,5},{13,9},{2,14},{6,2},{... | collective-permute-start | bytes 602120 | tf_op jit(solution)/shard_map/ppermute | solution.py:483
  101.7 7.7 %collective-permute-start.20 = (f32[392,128]{1,0:T(8,128)S(1)}, f32[392,128]{1,0:T(8,128)S(1)}, u32[]{:S(2)}, u32[]{:S(2)}) collective-permute-start(f32[392,128]{1,0:T(8,128)S(1)} %get-tuple-element.82), channel_id=1, source_target_pairs={{0,12},{4,0},{8,4},{12,8},{1,13},{5,1},{9,5},{13,9},{2,14},{6,2},{... | collective-permute-start | bytes 602120 | tf_op jit(solution)/shard_map/ppermute | solution.py:483
  103.8 12.1 %collective-permute-start.28 = (f32[768,128]{1,0:T(8,128)S(1)}, f32[768,128]{1,0:T(8,128)S(1)}, u32[]{:S(2)}, u32[]{:S(2)}) collective-permute-start(f32[768,128]{1,0:T(8,128)S(1)} %combine.15.refs_6_), channel_id=1, source_target_pairs={{0,2},{2,0},{1,3},{3,1},{4,6},{6,4},{5,7},{7,5},{8,10},{10,8},{9,1... | collective-permute-start | bytes 1179656 | tf_op jit(solution)/shard_map/ppermute | solution.py:25
  110.0 13.0 %collective-permute-start.27 = (f32[768,128]{1,0:T(8,128)S(1)}, f32[768,128]{1,0:T(8,128)S(1)}, u32[]{:S(2)}, u32[]{:S(2)}) collective-permute-start(f32[768,128]{1,0:T(8,128)S(1)} %combine.12.refs_0_), channel_id=1, source_target_pairs={{0,2},{2,0},{1,3},{3,1},{4,6},{6,4},{5,7},{7,5},{8,10},{10,8},{9,1... | collective-permute-start | bytes 1179656 | tf_op jit(solution)/shard_map/ppermute | solution.py:25

commit v18 on v17

--- a/solution.py
+++ b/solution.py
@@ -194,7 +194,8 @@
         starts.append(starts[-1] + size)
     places = [base + i for base, size in pieces for i in range(size)]
 
-    unroll = 2 if len(places) % 2 == 0 else 1
+    most = 2 if origin is None else 4
+    unroll = next(unroll for unroll in (4, 2, 1) if unroll <= most and len(places) % unroll == 0)
 
     def specs(u):
         def source(i, table):

time: 125 us -> 125 us (level)
  transfers between devices with their start and end apart: 29 -> 29, of which waited for: 17 -> 16; matrix products, arithmetic and copies ran while one was open for 1% -> 1% of each run, Pallas kernels for 29% -> 28%
where the time goes in v18:
time: 125 us; the launch traced here: 124 us
  Pallas kernels  42.7 us (34%)
  waiting for transfers between devices  39.6 us (32%)
  starting transfers between devices  38.4 us (31%)
  local copies, waits for them, and re-layouts  1.51 us (1%)
    pallas_call x4, Pallas kernels, sectors(): pl.pallas_call(functools.partial(sector_kernel, count, terms, unroll, hei...  30 us
    ppermute x12, starting transfers between devices, relay(): lax.ppermute(value, 'blk', [(p, (p + c) % devices) for p in range(devices)])  20.1 us
    ppermute x12, waiting for transfers between devices, relay(): lax.ppermute(value, 'blk', [(p, (p + c) % devices) for p in range(devices)])  19.8 us
    ppermute x14, waiting for transfers between devices, flip(): return lax.ppermute(value, axis, [(i, i ^ bit) for i in range(size)])  18.1 us
    ppermute x14, starting transfers between devices, flip(): return lax.ppermute(value, axis, [(i, i ^ bit) for i in range(size)])  17.6 us
    pallas_call x8, Pallas kernels, combine(): pl.pallas_call(functools.partial(combine_kernel, share, pieces, ordered,...  5.17 us
    pallas_call x2, Pallas kernels, finish(): pl.pallas_call(functools.partial(finish_kernel, count, rows, [size for _,...  2.98 us
  transfers between devices with their start and end apart: 29, of which 16 were waited for; matrix products, arithmetic and copies ran while one was open for 1% of the time, Pallas kernels for 28%

profile of v18, /device:TPU:0, one launch (start us, length us, event | category | flops | bytes accessed | tf_op | source)
XLA Modules:
  0.0 124.3 jit_solution(4241792380186517752)
XLA Ops:
  1.1 0.7 pad_add_fusion.given_hbm
  1.9 1.4 %copy-done.1 = f32[16,64,3,128]{3,1,2,0:T(8,128)S(1)} copy-done((f32[16,64,3,128]{3,1,2,0:T(8,128)S(1)}, f32[16,64,3,128]{3,1,2,0:T(8,128)}, u32[]{:S(2)}) %copy-start.1) | copy-done | bytes 1572888
  3.3 1.5 %table.1 = s32[57]{0:T(128)S(1)} custom-call(s32[24]{0:T(128)S(1)} %pad_add_fusion.given_hbm, f32[3072,128]{1,0:T(8,128)S(1)} %bitcast.12), custom_call_target="tpu_custom_call" | custom-call | tf_op jit(solution)/shard_map/table/pallas_call | solution.py:78
  4.8 5.1 %sectors.4 = (f32[384,128]{1,0:T(8,128)S(1)}, f32[384,128]{1,0:T(8,128)S(1)}, f32[3072,128]{1,0:T(8,128)S(1)}) custom-call(s32[57]{0:T(128)S(1)} %table.1, f32[3072,128]{1,0:T(8,128)S(1)} %bitcast.13, f32[3072,128]{1,0:T(8,128)S(1)} %collective-permute-done.other_ref, f32[8,16,64,128]{3,2,1,0:T(8,128)} %refs_0_.7, f32[8,16,128,128]{3,2,1,0:T(8,128)} %refs_1_.7, ...), custom_call_target="tpu_custom_call" | custom-call | tf_op jit(solution)/shard_map/sectors/pallas_call | solution.py:222
  10.0 3.7 %collective-permute-start.1 = (f32[384,128]{1,0:T(8,128)S(1)}, f32[384,128]{1,0:T(8,128)S(1)}, u32[]{:S(2)}, u32[]{:S(2)}) collective-permute-start(f32[384,128]{1,0:T(8,128)S(1)} %get-tuple-element.54), channel_id=1, source_target_pairs={{0,8},{4,12},{8,0},{12,4},{1,9},{5,13},{9,1},{13,5},{2,10},{6,14},... | collective-permute-start | bytes 589832 | tf_op jit(solution)/shard_map/ppermute | solution.py:484
  13.9 11.6 %sectors.5 = (f32[384,128]{1,0:T(8,128)S(1)}, f32[384,128]{1,0:T(8,128)S(1)}, f32[384,128]{1,0:T(8,128)S(1)}, f32[384,128]{1,0:T(8,128)S(1)}, f32[384,128]{1,0:T...) custom-call(s32[57]{0:T(128)S(1)} %table.1, ...), custom_call_target="tpu_custom_call", output_to_operand_aliasing={{6}: (7, {})} | custom-call | tf_op jit(solution)/shard_map/sectors/pallas_call | solution.py:222
  25.6 0.7 combine.8
  26.2 1.8 %collective-permute-start.11 = (f32[768,128]{1,0:T(8,128)S(1)}, f32[768,128]{1,0:T(8,128)S(1)}, u32[]{:S(2)}, u32[]{:S(2)}) collective-permute-start(f32[768,128]{1,0:T(8,128)S(1)} %get-tuple-element.68.rest_0_), channel_id=1, source_target_pairs={{0,2},{2,0},{1,3},{3,1},{4,6},{6,4},{5,7},{7,5},{8,10},{10,8},{9,1... | collective-permute-start | bytes 1179656 | tf_op jit(solution)/shard_map/ppermute | solution.py:25
  28.1 1.6 %collective-permute-start.3 = (f32[384,128]{1,0:T(8,128)S(1)}, f32[384,128]{1,0:T(8,128)S(1)}, u32[]{:S(2)}, u32[]{:S(2)}) collective-permute-start(f32[384,128]{1,0:T(8,128)S(1)} %get-tuple-element.58), channel_id=1, source_target_pairs={{0,4},{4,8},{8,12},{12,0},{1,5},{5,9},{9,13},{13,1},{2,6},{6,10},{... | collective-permute-start | bytes 589832 | tf_op jit(solution)/shard_map/ppermute | solution.py:484
  29.6 2.2 %collective-permute-done.2.refs_1_ = f32[384,128]{1,0:T(8,128)S(1)} collective-permute-done((f32[384,128]{1,0:T(8,128)S(1)}, f32[384,128]{1,0:T(8,128)S(1)}, u32[]{:S(2)}, u32[]{:S(2)}) %collective-permute-start.2) | collective-permute-done | bytes 196640 | tf_op jit(solution)/shard_map/ppermute | solution.py:484
  31.9 0.8 collective-permute-start.4
  33.3 1.5 %collective-permute-start.14 = (f32[768,128]{1,0:T(8,128)S(1)}, f32[768,128]{1,0:T(8,128)S(1)}, u32[]{:S(2)}, u32[]{:S(2)}) collective-permute-start(f32[768,128]{1,0:T(8,128)S(1)} %get-tuple-element.71.rest_2_), channel_id=1, source_target_pairs={{0,2},{2,0},{1,3},{3,1},{4,6},{6,4},{5,7},{7,5},{8,10},{10,8},{9,1... | collective-permute-start | bytes 1179656 | tf_op jit(solution)/shard_map/ppermute | solution.py:25
  34.9 1.6 %collective-permute-done.3.refs_0_ = f32[384,128]{1,0:T(8,128)S(1)} collective-permute-done((f32[384,128]{1,0:T(8,128)S(1)}, f32[384,128]{1,0:T(8,128)S(1)}, u32[]{:S(2)}, u32[]{:S(2)}) %collective-permute-start.3) | collective-permute-done | bytes 196640 | tf_op jit(solution)/shard_map/ppermute | solution.py:484
  36.4 3.3 %collective-permute-start.5 = (f32[384,128]{1,0:T(8,128)S(1)}, f32[384,128]{1,0:T(8,128)S(1)}, u32[]{:S(2)}, u32[]{:S(2)}) collective-permute-start(f32[384,128]{1,0:T(8,128)S(1)} %get-tuple-element.63), channel_id=1, source_target_pairs={{0,12},{4,0},{8,4},{12,8},{1,13},{5,1},{9,5},{13,9},{2,14},{6,2},{... | collective-permute-start | bytes 589832 | tf_op jit(solution)/shard_map/ppermute | solution.py:484
  39.7 1.1 collective-permute-done.4.refs_1_
  40.8 3.0 %collective-permute-start.6 = (f32[384,128]{1,0:T(8,128)S(1)}, f32[384,128]{1,0:T(8,128)S(1)}, u32[]{:S(2)}, u32[]{:S(2)}) collective-permute-start(f32[384,128]{1,0:T(8,128)S(1)} %get-tuple-element.65), channel_id=1, source_target_pairs={{0,12},{4,0},{8,4},{12,8},{1,13},{5,1},{9,5},{13,9},{2,14},{6,2},{... | collective-permute-start | bytes 589832 | tf_op jit(solution)/shard_map/ppermute | solution.py:484
  44.5 1.5 %collective-permute-start.12 = (f32[768,128]{1,0:T(8,128)S(1)}, f32[768,128]{1,0:T(8,128)S(1)}, u32[]{:S(2)}, u32[]{:S(2)}) collective-permute-start(f32[768,128]{1,0:T(8,128)S(1)} %get-tuple-element.69.rest_4_), channel_id=1, source_target_pairs={{0,2},{2,0},{1,3},{3,1},{4,6},{6,4},{5,7},{7,5},{8,10},{10,8},{9,1... | collective-permute-start | bytes 1179656 | tf_op jit(solution)/shard_map/ppermute | solution.py:25
  46.1 3.0 %collective-permute-done.6.refs_1_ = f32[384,128]{1,0:T(8,128)S(1)} collective-permute-done((f32[384,128]{1,0:T(8,128)S(1)}, f32[384,128]{1,0:T(8,128)S(1)}, u32[]{:S(2)}, u32[]{:S(2)}) %collective-permute-start.6) | collective-permute-done | bytes 196640 | tf_op jit(solution)/shard_map/ppermute | solution.py:484
  49.7 1.5 %collective-permute-start.15 = (f32[768,128]{1,0:T(8,128)S(1)}, f32[768,128]{1,0:T(8,128)S(1)}, u32[]{:S(2)}, u32[]{:S(2)}) collective-permute-start(f32[768,128]{1,0:T(8,128)S(1)} %get-tuple-element.73.rest_6_), channel_id=1, source_target_pairs={{0,2},{2,0},{1,3},{3,1},{4,6},{6,4},{5,7},{7,5},{8,10},{10,8},{9,1... | collective-permute-start | bytes 1179656 | tf_op jit(solution)/shard_map/ppermute | solution.py:25
  51.2 1.2 collective-permute-done.7
  52.4 3.5 %collective-permute-start.10 = (f32[8,128]{1,0:T(8,128)S(1)}, f32[8,128]{1,0:T(8,128)S(1)}, u32[]{:S(2)}, u32[]{:S(2)}) collective-permute-start(f32[8,128]{1,0:T(8,128)S(1)} %add.63), channel_id=1, source_target_pairs={{0,12},{4,8},{8,4},{12,0},{1,13},{5,9},{9,5},{13,1},{2,14},{6,10},... | collective-permute-start | bytes 12296 | tf_op jit(solution)/shard_map/ppermute | solution.py:25
  55.9 0.9 collective-permute-start.8
  56.8 1.0 collective-permute-done.10
  57.8 2.6 %collective-permute-done.9 = f32[8,128]{1,0:T(8,128)S(1)} collective-permute-done((f32[8,128]{1,0:T(8,128)S(1)}, f32[8,128]{1,0:T(8,128)S(1)}, u32[]{:S(2)}, u32[]{:S(2)}) %collective-permute-start.9) | collective-permute-done | bytes 4128 | tf_op jit(solution)/shard_map/ppermute | solution.py:25
  61.0 3.1 %collective-permute-done.13 = f32[8,128]{1,0:T(8,128)S(1)} collective-permute-done((f32[8,128]{1,0:T(8,128)S(1)}, f32[8,128]{1,0:T(8,128)S(1)}, u32[]{:S(2)}, u32[]{:S(2)}) %collective-permute-start.13) | collective-permute-done | bytes 4128 | tf_op jit(solution)/shard_map/ppermute | solution.py:25
  64.1 1.3 %correct.1 = (f32[3080,128]{1,0:T(8,128)S(1)}, f32[776,128]{1,0:T(8,128)S(1)}) custom-call(s32[57]{0:T(128)S(1)} %table.1, f32[8,128]{1,0:T(8,128)S(1)} %add.67.inner_ref, f32[3072,128]{1,0:T(8,128)S(1)} %bitcast.19, f32[16,64,128]{2,1,0:T(8,128)S(1)} %broadcast_add_fusion.diag_ref, f32[768,128]{1,0:T(8,128)S(1)} %get-tuple-element.68.rest_0_, ...), custom_call_target="tpu_custom_call" | custom-call | tf_op jit(solution)/shard_map/correct/pallas_call | solution.py:344
  65.4 1.7 %collective-permute-done.16.other_ref = f32[776,128]{1,0:T(8,128)S(1)} collective-permute-done((f32[776,128]{1,0:T(8,128)S(1)}, f32[776,128]{1,0:T(8,128)S(1)}, u32[]{:S(2)}, u32[]{:S(2)}) %collective-permute-start.16) | collective-permute-done | bytes 397344 | tf_op jit(solution)/shard_map/ppermute | solution.py:487
  67.3 3.6 %sectors.6 = (f32[392,128]{1,0:T(8,128)S(1)}, f32[392,128]{1,0:T(8,128)S(1)}, f32[3072,128]{1,0:T(8,128)S(1)}) custom-call(s32[57]{0:T(128)S(1)} %table.1, f32[776,128]{1,0:T(8,128)S(1)} %get-tuple-element.75.own_ref, f32[776,128]{1,0:T(8,128)S(1)} %collective-permute-done.16.other_ref, f32[8,16,64,128]{3,2,1,0:T(8,128)S(1)} %copy-done, ...), custom_call_target="tpu_custom_call" | custom-call | tf_op jit(solution)/shard_map/sectors/pallas_call | solution.py:222
  70.9 2.1 %collective-permute-start.21 = (f32[392,128]{1,0:T(8,128)S(1)}, f32[392,128]{1,0:T(8,128)S(1)}, u32[]{:S(2)}, u32[]{:S(2)}) collective-permute-start(f32[392,128]{1,0:T(8,128)S(1)} %get-tuple-element.86), channel_id=1, source_target_pairs={{0,8},{4,12},{8,0},{12,4},{1,9},{5,13},{9,1},{13,5},{2,10},{6,14},... | collective-permute-start | bytes 602120 | tf_op jit(solution)/shard_map/ppermute | solution.py:484
  73.0 0.9 collective-permute-start.18
  73.9 9.7 %sectors.7 = (f32[392,128]{1,0:T(8,128)S(1)}, f32[392,128]{1,0:T(8,128)S(1)}, f32[392,128]{1,0:T(8,128)S(1)}, f32[392,128]{1,0:T(8,128)S(1)}, f32[384,128]{1,0:T...) custom-call(s32[57]{0:T(128)S(1)} %table.1, ...), custom_call_target="tpu_custom_call", output_to_operand_aliasing={{6}: (5, {})} | custom-call | tf_op jit(solution)/shard_map/sectors/pallas_call | solution.py:222
  84.2 1.4 %collective-permute-start.24 = (f32[384,128]{1,0:T(8,128)S(1)}, f32[384,128]{1,0:T(8,128)S(1)}, u32[]{:S(2)}, u32[]{:S(2)}) collective-permute-start(f32[384,128]{1,0:T(8,128)S(1)} %get-tuple-element.91.refs_2_), channel_id=1, source_target_pairs={{0,2},{2,0},{1,3},{3,1},{4,6},{6,4},{5,7},{7,5},{8,10},{10,8},{9,1... | collective-permute-start | bytes 589832 | tf_op jit(solution)/shard_map/ppermute | solution.py:25
  85.6 0.7 collective-permute-start.25
  86.3 1.3 %collective-permute-done.21.refs_1_ = f32[392,128]{1,0:T(8,128)S(1)} collective-permute-done((f32[392,128]{1,0:T(8,128)S(1)}, f32[392,128]{1,0:T(8,128)S(1)}, u32[]{:S(2)}, u32[]{:S(2)}) %collective-permute-start.21) | collective-permute-done | bytes 200736 | tf_op jit(solution)/shard_map/ppermute | solution.py:484
  87.8 4.0 %collective-permute-done.18.refs_0_ = f32[392,128]{1,0:T(8,128)S(1)} collective-permute-done((f32[392,128]{1,0:T(8,128)S(1)}, f32[392,128]{1,0:T(8,128)S(1)}, u32[]{:S(2)}, u32[]{:S(2)}) %collective-permute-start.18) | collective-permute-done | bytes 200736 | tf_op jit(solution)/shard_map/ppermute | solution.py:484
  92.8 2.3 %collective-permute-done.25.refs_1_ = f32[384,128]{1,0:T(8,128)S(1)} collective-permute-done((f32[384,128]{1,0:T(8,128)S(1)}, f32[384,128]{1,0:T(8,128)S(1)}, u32[]{:S(2)}, u32[]{:S(2)}) %collective-permute-start.25) | collective-permute-done | bytes 196640 | tf_op jit(solution)/shard_map/ppermute | solution.py:25
  95.1 1.3 %collective-permute-start.26 = (f32[768,128]{1,0:T(8,128)S(1)}, f32[768,128]{1,0:T(8,128)S(1)}, u32[]{:S(2)}, u32[]{:S(2)}) collective-permute-start(f32[768,128]{1,0:T(8,128)S(1)} %combine.13.refs_4_), channel_id=1, source_target_pairs={{0,2},{2,0},{1,3},{3,1},{4,6},{6,4},{5,7},{7,5},{8,10},{10,8},{9,1... | collective-permute-start | bytes 1179656 | tf_op jit(solution)/shard_map/ppermute | solution.py:25
  96.4 2.7 %collective-permute-start.23 = (f32[392,128]{1,0:T(8,128)S(1)}, f32[392,128]{1,0:T(8,128)S(1)}, u32[]{:S(2)}, u32[]{:S(2)}) collective-permute-start(f32[392,128]{1,0:T(8,128)S(1)} %get-tuple-element.88), channel_id=1, source_target_pairs={{0,12},{4,0},{8,4},{12,8},{1,13},{5,1},{9,5},{13,9},{2,14},{6,2},{... | collective-permute-start | bytes 602120 | tf_op jit(solution)/shard_map/ppermute | solution.py:484
  99.0 2.5 %collective-permute-done.19.refs_0_ = f32[392,128]{1,0:T(8,128)S(1)} collective-permute-done((f32[392,128]{1,0:T(8,128)S(1)}, f32[392,128]{1,0:T(8,128)S(1)}, u32[]{:S(2)}, u32[]{:S(2)}) %collective-permute-start.19) | collective-permute-done | bytes 200736 | tf_op jit(solution)/shard_map/ppermute | solution.py:484
  101.5 1.5 %collective-permute-start.20 = (f32[392,128]{1,0:T(8,128)S(1)}, f32[392,128]{1,0:T(8,128)S(1)}, u32[]{:S(2)}, u32[]{:S(2)}) collective-permute-start(f32[392,128]{1,0:T(8,128)S(1)} %get-tuple-element.82), channel_id=1, source_target_pairs={{0,12},{4,0},{8,4},{12,8},{1,13},{5,1},{9,5},{13,9},{2,14},{6,2},{... | collective-permute-start | bytes 602120 | tf_op jit(solution)/shard_map/ppermute | solution.py:484
  103.7 1.5 %collective-permute-start.28 = (f32[768,128]{1,0:T(8,128)S(1)}, f32[768,128]{1,0:T(8,128)S(1)}, u32[]{:S(2)}, u32[]{:S(2)}) collective-permute-start(f32[768,128]{1,0:T(8,128)S(1)} %combine.15.refs_6_), channel_id=1, source_target_pairs={{0,2},{2,0},{1,3},{3,1},{4,6},{6,4},{5,7},{7,5},{8,10},{10,8},{9,1... | collective-permute-start | bytes 1179656 | tf_op jit(solution)/shard_map/ppermute | solution.py:25
  105.1 4.1 %collective-permute-done.20.refs_0_ = f32[392,128]{1,0:T(8,128)S(1)} collective-permute-done((f32[392,128]{1,0:T(8,128)S(1)}, f32[392,128]{1,0:T(8,128)S(1)}, u32[]{:S(2)}, u32[]{:S(2)}) %collective-permute-start.20) | collective-permute-done | bytes 200736 | tf_op jit(solution)/shard_map/ppermute | solution.py:484
  109.9 1.4 %collective-permute-start.27 = (f32[768,128]{1,0:T(8,128)S(1)}, f32[768,128]{1,0:T(8,128)S(1)}, u32[]{:S(2)}, u32[]{:S(2)}) collective-permute-start(f32[768,128]{1,0:T(8,128)S(1)} %combine.12.refs_0_), channel_id=1, source_target_pairs={{0,2},{2,0},{1,3},{3,1},{4,6},{6,4},{5,7},{7,5},{8,10},{10,8},{9,1... | collective-permute-start | bytes 1179656 | tf_op jit(solution)/shard_map/ppermute | solution.py:25
  111.4 1.8 %scaled.1 = f32[3072,128]{1,0:T(8,128)} custom-call(s32[57]{0:T(128)S(1)} %table.1, f32[8,128]{1,0:T(8,128)S(1)} %broadcast_in_dim.2.scale_ref, f32[3080,128]{1,0:T(8,128)S(1)} %get-tuple-element.76.own_ref.vector_ref.raw_ref), custom_call_target="tpu_custom_call" | custom-call | tf_op jit(solution)/shard_map/scaled/pallas_call | solution.py:389
  113.2 2.5 %collective-permute-done.28.refs_7_ = f32[768,128]{1,0:T(8,128)S(1)} collective-permute-done((f32[768,128]{1,0:T(8,128)S(1)}, f32[768,128]{1,0:T(8,128)S(1)}, u32[]{:S(2)}, u32[]{:S(2)}) %collective-permute-start.28) | collective-permute-done | bytes 393248 | tf_op jit(solution)/shard_map/ppermute | solution.py:25
  115.8 1.7 %finish.2.refs_2_ = f32[3072,128]{1,0:T(8,128)} custom-call(s32[57]{0:T(128)S(1)} %table.1, f32[8,128]{1,0:T(8,128)S(1)} %broadcast_in_dim.2.scale_ref, f32[384,128]{1,0:T(8,128)S(1)} %get-tuple-element.92.refs_0_, f32[384,128]{1,0:T(8,128)S(1)} %collective-permute-done.25.refs_1_, f32[384,128]{1,0:T(8,128)S(1)} %get-tuple-element.91.refs_2_, ...), custom_call_target="tpu_custom_call" | custom-call | tf_op jit(solution)/shard_map/finish/pallas_call | solution.py:430
  117.4 5.4 %collective-permute-done.27.refs_1_ = f32[768,128]{1,0:T(8,128)S(1)} collective-permute-done((f32[768,128]{1,0:T(8,128)S(1)}, f32[768,128]{1,0:T(8,128)S(1)}, u32[]{:S(2)}, u32[]{:S(2)}) %collective-permute-start.27) | collective-permute-done | bytes 393248 | tf_op jit(solution)/shard_map/ppermute | solution.py:25
  122.9 1.3 %finish.3 = f32[3072,128]{1,0:T(8,128)} custom-call(s32[57]{0:T(128)S(1)} %table.1, f32[8,128]{1,0:T(8,128)S(1)} %broadcast_in_dim.2.scale_ref, f32[768,128]{1,0:T(8,128)S(1)} %combine.12.refs_0_, f32[768,128]{1,0:T(8,128)S(1)} %collective-permute-done.27.refs_1_, f32[3072,128]{1,0:T(8,128)} %finish.2.refs_2_), custom_call_target="tpu_custom_call", output_to_operand_aliasing={{}: (4, {})} | custom-call | tf_op jit(solution)/shard_map/finish/pallas_call | solution.py:430
  (51 shorter events, 6.9 us)
Async XLA Ops:
  0.6 4.2 %collective-permute-start = (f32[3072,128]{1,0:T(8,128)}, f32[3072,128]{1,0:T(8,128)S(1)}, u32[]{:S(2)}, u32[]{:S(2)}) collective-permute-start(f32[3072,128]{1,0:T(8,128)} %bitcast.11), channel_id=1, source_target_pairs={{0,1},{1,0},{2,3},{3,2},{4,5},{5,4},{6,7},{7,6},{8,9},{9,8},{10,11... | collective-permute-start | bytes 4718600 | tf_op jit(solution)/shard_map/ppermute | solution.py:487
  1.9 1.4 %copy-start.1 = (f32[16,64,3,128]{3,1,2,0:T(8,128)S(1)}, f32[16,64,3,128]{3,1,2,0:T(8,128)}, u32[]{:S(2)}) copy-start(f32[16,64,3,128]{3,1,2,0:T(8,128)} %param.7) | copy-start | bytes 4718596
  3.3 1.5 %copy-start.2 = (f32[16,64,3,128]{3,1,2,0:T(8,128)S(1)}, f32[16,64,3,128]{3,1,2,0:T(8,128)}, u32[]{:S(2)}) copy-start(f32[16,64,3,128]{3,1,2,0:T(8,128)} %param.7) | copy-start | bytes 4718596
  4.8 8.9 %copy-start.3 = (f32[16,128]{1,0:T(8,128)S(1)}, f32[16,128]{1,0:T(8,128)}, u32[]{:S(2)}) copy-start(f32[16,128]{1,0:T(8,128)} %param.13) | copy-start | bytes 24580
  4.8 8.9 %copy-start.4 = (f32[16,64]{1,0:T(8,128)S(1)}, f32[16,64]{1,0:T(8,128)}, u32[]{:S(2)}) copy-start(f32[16,64]{1,0:T(8,128)} %param.12) | copy-start | bytes 12292
  10.0 18.1 %collective-permute-start.1 = (f32[384,128]{1,0:T(8,128)S(1)}, f32[384,128]{1,0:T(8,128)S(1)}, u32[]{:S(2)}, u32[]{:S(2)}) collective-permute-start(f32[384,128]{1,0:T(8,128)S(1)} %get-tuple-element.54), channel_id=1, source_target_pairs={{0,8},{4,12},{8,0},{12,4},{1,9},{5,13},{9,1},{13,5},{2,10},{6,14},... | collective-permute-start | bytes 589832 | tf_op jit(solution)/shard_map/ppermute | solution.py:484
  13.7 18.2 %collective-permute-start.2 = (f32[384,128]{1,0:T(8,128)S(1)}, f32[384,128]{1,0:T(8,128)S(1)}, u32[]{:S(2)}, u32[]{:S(2)}) collective-permute-start(f32[384,128]{1,0:T(8,128)S(1)} %get-tuple-element.55), channel_id=1, source_target_pairs={{0,8},{4,12},{8,0},{12,4},{1,9},{5,13},{9,1},{13,5},{2,10},{6,14},... | collective-permute-start | bytes 589832 | tf_op jit(solution)/shard_map/ppermute | solution.py:484
  26.2 18.3 %collective-permute-start.11 = (f32[768,128]{1,0:T(8,128)S(1)}, f32[768,128]{1,0:T(8,128)S(1)}, u32[]{:S(2)}, u32[]{:S(2)}) collective-permute-start(f32[768,128]{1,0:T(8,128)S(1)} %get-tuple-element.68.rest_0_), channel_id=1, source_target_pairs={{0,2},{2,0},{1,3},{3,1},{4,6},{6,4},{5,7},{7,5},{8,10},{10,8},{9,1... | collective-permute-start | bytes 1179656 | tf_op jit(solution)/shard_map/ppermute | solution.py:25
  28.1 8.3 %collective-permute-start.3 = (f32[384,128]{1,0:T(8,128)S(1)}, f32[384,128]{1,0:T(8,128)S(1)}, u32[]{:S(2)}, u32[]{:S(2)}) collective-permute-start(f32[384,128]{1,0:T(8,128)S(1)} %get-tuple-element.58), channel_id=1, source_target_pairs={{0,4},{4,8},{8,12},{12,0},{1,5},{5,9},{9,13},{13,1},{2,6},{6,10},{... | collective-permute-start | bytes 589832 | tf_op jit(solution)/shard_map/ppermute | solution.py:484
  31.9 8.9 %collective-permute-start.4 = (f32[384,128]{1,0:T(8,128)S(1)}, f32[384,128]{1,0:T(8,128)S(1)}, u32[]{:S(2)}, u32[]{:S(2)}) collective-permute-start(f32[384,128]{1,0:T(8,128)S(1)} %get-tuple-element.60), channel_id=1, source_target_pairs={{0,4},{4,8},{8,12},{12,0},{1,5},{5,9},{9,13},{13,1},{2,6},{6,10},{... | collective-permute-start | bytes 589832 | tf_op jit(solution)/shard_map/ppermute | solution.py:484
  32.6 34.6 %slice-start = ((s8[8388608]{0:T(1024)(128)(4,1)}), s8[4194304]{0:T(1024)(128)(4,1)S(1)}, s32[]{:S(2)}) async-start(s8[8388608]{0:T(1024)(128)(4,1)} %bitcast.9), calls=%async_computation | async-start | bytes 8388608
  33.3 16.4 %collective-permute-start.14 = (f32[768,128]{1,0:T(8,128)S(1)}, f32[768,128]{1,0:T(8,128)S(1)}, u32[]{:S(2)}, u32[]{:S(2)}) collective-permute-start(f32[768,128]{1,0:T(8,128)S(1)} %get-tuple-element.71.rest_2_), channel_id=1, source_target_pairs={{0,2},{2,0},{1,3},{3,1},{4,6},{6,4},{5,7},{7,5},{8,10},{10,8},{9,1... | collective-permute-start | bytes 1179656 | tf_op jit(solution)/shard_map/ppermute | solution.py:25
  36.4 9.7 %collective-permute-start.5 = (f32[384,128]{1,0:T(8,128)S(1)}, f32[384,128]{1,0:T(8,128)S(1)}, u32[]{:S(2)}, u32[]{:S(2)}) collective-permute-start(f32[384,128]{1,0:T(8,128)S(1)} %get-tuple-element.63), channel_id=1, source_target_pairs={{0,12},{4,0},{8,4},{12,8},{1,13},{5,1},{9,5},{13,9},{2,14},{6,2},{... | collective-permute-start | bytes 589832 | tf_op jit(solution)/shard_map/ppermute | solution.py:484
  40.8 8.2 %collective-permute-start.6 = (f32[384,128]{1,0:T(8,128)S(1)}, f32[384,128]{1,0:T(8,128)S(1)}, u32[]{:S(2)}, u32[]{:S(2)}) collective-permute-start(f32[384,128]{1,0:T(8,128)S(1)} %get-tuple-element.65), channel_id=1, source_target_pairs={{0,12},{4,0},{8,4},{12,8},{1,13},{5,1},{9,5},{13,9},{2,14},{6,2},{... | collective-permute-start | bytes 589832 | tf_op jit(solution)/shard_map/ppermute | solution.py:484
  44.5 22.8 %slice-start.1 = ((s8[8388608]{0:T(1024)(128)(4,1)}), s8[4194304]{0:T(1024)(128)(4,1)S(1)}, s32[]{:S(2)}) async-start(s8[8388608]{0:T(1024)(128)(4,1)} %bitcast.9), calls=%async_computation.1 | async-start | bytes 8388608
  44.5 15.8 %collective-permute-start.12 = (f32[768,128]{1,0:T(8,128)S(1)}, f32[768,128]{1,0:T(8,128)S(1)}, u32[]{:S(2)}, u32[]{:S(2)}) collective-permute-start(f32[768,128]{1,0:T(8,128)S(1)} %get-tuple-element.69.rest_4_), channel_id=1, source_target_pairs={{0,2},{2,0},{1,3},{3,1},{4,6},{6,4},{5,7},{7,5},{8,10},{10,8},{9,1... | collective-permute-start | bytes 1179656 | tf_op jit(solution)/shard_map/ppermute | solution.py:25
  49.7 14.3 %collective-permute-start.15 = (f32[768,128]{1,0:T(8,128)S(1)}, f32[768,128]{1,0:T(8,128)S(1)}, u32[]{:S(2)}, u32[]{:S(2)}) collective-permute-start(f32[768,128]{1,0:T(8,128)S(1)} %get-tuple-element.73.rest_6_), channel_id=1, source_target_pairs={{0,2},{2,0},{1,3},{3,1},{4,6},{6,4},{5,7},{7,5},{8,10},{10,8},{9,1... | collective-permute-start | bytes 1179656 | tf_op jit(solution)/shard_map/ppermute | solution.py:25
  51.2 1.2 collective-permute-start.7
  52.4 5.4 %collective-permute-start.10 = (f32[8,128]{1,0:T(8,128)S(1)}, f32[8,128]{1,0:T(8,128)S(1)}, u32[]{:S(2)}, u32[]{:S(2)}) collective-permute-start(f32[8,128]{1,0:T(8,128)S(1)} %add.63), channel_id=1, source_target_pairs={{0,12},{4,8},{8,4},{12,0},{1,13},{5,9},{9,5},{13,1},{2,14},{6,10},... | collective-permute-start | bytes 12296 | tf_op jit(solution)/shard_map/ppermute | solution.py:25
  55.9 4.5 %collective-permute-start.9 = (f32[8,128]{1,0:T(8,128)S(1)}, f32[8,128]{1,0:T(8,128)S(1)}, u32[]{:S(2)}, u32[]{:S(2)}) collective-permute-start(f32[8,128]{1,0:T(8,128)S(1)} %add.63), channel_id=1, source_target_pairs={{0,8},{4,12},{8,0},{12,4},{1,9},{5,13},{9,1},{13,5},{2,10},{6,14},... | collective-permute-start | bytes 12296 | tf_op jit(solution)/shard_map/ppermute | solution.py:25
  55.9 4.5 %collective-permute-start.8 = (f32[8,128]{1,0:T(8,128)S(1)}, f32[8,128]{1,0:T(8,128)S(1)}, u32[]{:S(2)}, u32[]{:S(2)}) collective-permute-start(f32[8,128]{1,0:T(8,128)S(1)} %add.63), channel_id=1, source_target_pairs={{0,4},{4,0},{8,12},{12,8},{1,5},{5,1},{9,13},{13,9},{2,6},{6,2},{1... | collective-permute-start | bytes 12296 | tf_op jit(solution)/shard_map/ppermute | solution.py:25
  60.4 3.7 %collective-permute-start.13 = (f32[8,128]{1,0:T(8,128)S(1)}, f32[8,128]{1,0:T(8,128)S(1)}, u32[]{:S(2)}, u32[]{:S(2)}) collective-permute-start(f32[8,128]{1,0:T(8,128)S(1)} %add_add_fusion), channel_id=1, source_target_pairs={{0,2},{2,0},{1,3},{3,1},{4,6},{6,4},{5,7},{7,5},{8,10},{10,8},{9,1... | collective-permute-start | bytes 12296 | tf_op jit(solution)/shard_map/ppermute | solution.py:25
  64.1 3.2 %copy-start = (f32[8,16,64,128]{3,2,1,0:T(8,128)S(1)}, f32[8,16,64,128]{3,2,1,0:T(8,128)}, u32[]{:S(2)}) copy-start(f32[8,16,64,128]{3,2,1,0:T(8,128)} %refs_0_.7) | copy-start | bytes 12582916
  65.3 1.8 %collective-permute-start.16 = (f32[776,128]{1,0:T(8,128)S(1)}, f32[776,128]{1,0:T(8,128)S(1)}, u32[]{:S(2)}, u32[]{:S(2)}) collective-permute-start(f32[776,128]{1,0:T(8,128)S(1)} %get-tuple-element.75.own_ref), channel_id=1, source_target_pairs={{0,1},{1,0},{2,3},{3,2},{4,5},{5,4},{6,7},{7,6},{8,9},{9,8},{10,11... | collective-permute-start | bytes 1191944 | tf_op jit(solution)/shard_map/ppermute | solution.py:487
  67.1 6.8 %collective-permute-start.17 = (f32[3080,128]{1,0:T(8,128)S(1)}, f32[3080,128]{1,0:T(8,128)S(1)}, u32[]{:S(2)}, u32[]{:S(2)}) collective-permute-start(f32[3080,128]{1,0:T(8,128)S(1)} %get-tuple-element.76.own_ref.vector_ref.raw_ref), channel_id=1, source_target_pairs={{0,1},{1,0},{2,3},{3,2},{4,5},{5,4},{6,7},{7,6},{8,9},{9,8},{10,11... | collective-permute-start | bytes 4730888 | tf_op jit(solution)/shard_map/ppermute | solution.py:487
  70.9 16.8 %collective-permute-start.21 = (f32[392,128]{1,0:T(8,128)S(1)}, f32[392,128]{1,0:T(8,128)S(1)}, u32[]{:S(2)}, u32[]{:S(2)}) collective-permute-start(f32[392,128]{1,0:T(8,128)S(1)} %get-tuple-element.86), channel_id=1, source_target_pairs={{0,8},{4,12},{8,0},{12,4},{1,9},{5,13},{9,1},{13,5},{2,10},{6,14},... | collective-permute-start | bytes 602120 | tf_op jit(solution)/shard_map/ppermute | solution.py:484
  73.0 18.9 %collective-permute-start.18 = (f32[392,128]{1,0:T(8,128)S(1)}, f32[392,128]{1,0:T(8,128)S(1)}, u32[]{:S(2)}, u32[]{:S(2)}) collective-permute-start(f32[392,128]{1,0:T(8,128)S(1)} %get-tuple-element.77), channel_id=1, source_target_pairs={{0,8},{4,12},{8,0},{12,4},{1,9},{5,13},{9,1},{13,5},{2,10},{6,14},... | collective-permute-start | bytes 602120 | tf_op jit(solution)/shard_map/ppermute | solution.py:484
  84.2 8.6 %collective-permute-start.24 = (f32[384,128]{1,0:T(8,128)S(1)}, f32[384,128]{1,0:T(8,128)S(1)}, u32[]{:S(2)}, u32[]{:S(2)}) collective-permute-start(f32[384,128]{1,0:T(8,128)S(1)} %get-tuple-element.91.refs_2_), channel_id=1, source_target_pairs={{0,2},{2,0},{1,3},{3,1},{4,6},{6,4},{5,7},{7,5},{8,10},{10,8},{9,1... | collective-permute-start | bytes 589832 | tf_op jit(solution)/shard_map/ppermute | solution.py:25
  85.6 9.5 %collective-permute-start.25 = (f32[384,128]{1,0:T(8,128)S(1)}, f32[384,128]{1,0:T(8,128)S(1)}, u32[]{:S(2)}, u32[]{:S(2)}) collective-permute-start(f32[384,128]{1,0:T(8,128)S(1)} %get-tuple-element.92.refs_0_), channel_id=1, source_target_pairs={{0,2},{2,0},{1,3},{3,1},{4,6},{6,4},{5,7},{7,5},{8,10},{10,8},{9,1... | collective-permute-start | bytes 589832 | tf_op jit(solution)/shard_map/ppermute | solution.py:25
  87.6 8.7 %collective-permute-start.22 = (f32[392,128]{1,0:T(8,128)S(1)}, f32[392,128]{1,0:T(8,128)S(1)}, u32[]{:S(2)}, u32[]{:S(2)}) collective-permute-start(f32[392,128]{1,0:T(8,128)S(1)} %get-tuple-element.87), channel_id=1, source_target_pairs={{0,4},{4,8},{8,12},{12,0},{1,5},{5,9},{9,13},{13,1},{2,6},{6,10},{... | collective-permute-start | bytes 602120 | tf_op jit(solution)/shard_map/ppermute | solution.py:484
  91.9 9.6 %collective-permute-start.19 = (f32[392,128]{1,0:T(8,128)S(1)}, f32[392,128]{1,0:T(8,128)S(1)}, u32[]{:S(2)}, u32[]{:S(2)}) collective-permute-start(f32[392,128]{1,0:T(8,128)S(1)} %get-tuple-element.80), channel_id=1, source_target_pairs={{0,4},{4,8},{8,12},{12,0},{1,5},{5,9},{9,13},{13,1},{2,6},{6,10},{... | collective-permute-start | bytes 602120 | tf_op jit(solution)/shard_map/ppermute | solution.py:484
  95.1 14.8 %collective-permute-start.26 = (f32[768,128]{1,0:T(8,128)S(1)}, f32[768,128]{1,0:T(8,128)S(1)}, u32[]{:S(2)}, u32[]{:S(2)}) collective-permute-start(f32[768,128]{1,0:T(8,128)S(1)} %combine.13.refs_4_), channel_id=1, source_target_pairs={{0,2},{2,0},{1,3},{3,1},{4,6},{6,4},{5,7},{7,5},{8,10},{10,8},{9,1... | collective-permute-start | bytes 1179656 | tf_op jit(solution)/shard_map/ppermute | solution.py:25
  96.4 8.7 %collective-permute-start.23 = (f32[392,128]{1,0:T(8,128)S(1)}, f32[392,128]{1,0:T(8,128)S(1)}, u32[]{:S(2)}, u32[]{:S(2)}) collective-permute-start(f32[392,128]{1,0:T(8,128)S(1)} %get-tuple-element.88), channel_id=1, source_target_pairs={{0,12},{4,0},{8,4},{12,8},{1,13},{5,1},{9,5},{13,9},{2,14},{6,2},{... | collective-permute-start | bytes 602120 | tf_op jit(solution)/shard_map/ppermute | solution.py:484
  101.5 7.7 %collective-permute-start.20 = (f32[392,128]{1,0:T(8,128)S(1)}, f32[392,128]{1,0:T(8,128)S(1)}, u32[]{:S(2)}, u32[]{:S(2)}) collective-permute-start(f32[392,128]{1,0:T(8,128)S(1)} %get-tuple-element.82), channel_id=1, source_target_pairs={{0,12},{4,0},{8,4},{12,8},{1,13},{5,1},{9,5},{13,9},{2,14},{6,2},{... | collective-permute-start | bytes 602120 | tf_op jit(solution)/shard_map/ppermute | solution.py:484
  103.7 12.1 %collective-permute-start.28 = (f32[768,128]{1,0:T(8,128)S(1)}, f32[768,128]{1,0:T(8,128)S(1)}, u32[]{:S(2)}, u32[]{:S(2)}) collective-permute-start(f32[768,128]{1,0:T(8,128)S(1)} %combine.15.refs_6_), channel_id=1, source_target_pairs={{0,2},{2,0},{1,3},{3,1},{4,6},{6,4},{5,7},{7,5},{8,10},{10,8},{9,1... | collective-permute-start | bytes 1179656 | tf_op jit(solution)/shard_map/ppermute | solution.py:25
  109.9 13.0 %collective-permute-start.27 = (f32[768,128]{1,0:T(8,128)S(1)}, f32[768,128]{1,0:T(8,128)S(1)}, u32[]{:S(2)}, u32[]{:S(2)}) collective-permute-start(f32[768,128]{1,0:T(8,128)S(1)} %combine.12.refs_0_), channel_id=1, source_target_pairs={{0,2},{2,0},{1,3},{3,1},{4,6},{6,4},{5,7},{7,5},{8,10},{10,8},{9,1... | collective-permute-start | bytes 1179656 | tf_op jit(solution)/shard_map/ppermute | solution.py:25
